TPU v7x, 32 devices: a whole 2x2x4 slice. The times are simulated.
32 devices in a mesh: groups: 2 (over x), vir: 16 (over z, y, core).
Axes of the slice: x: 2, y: 2, z: 4, core: 2. Of those that a mesh axis runs over, the one named last changes fastest.
Arguments:
- amplitudes: bfloat16 [256, 64, 384], P(('groups', 'vir')), parts along dimension 0, may hold values from -12 to 12
- ij_counts: int32 [16], P('groups'), parts along dimension 0, may hold values from 1 to 32, 128 in all
- integrals: bfloat16 [1024, 64, 384], P(('groups', 'vir')), parts along dimension 0, may hold values from -1 to 1
- ab_irrep: int32 [1024], P(('groups', 'vir')), parts along dimension 0, may hold values from 0 to 7, as said below
Outputs:
- residual: bfloat16 [1024, 64, 2048], P(('groups', 'vir')), parts along dimension 0
- norms: float32 [16], P('groups'), parts along dimension 0
There are 2 independent parts, one for each index of `groups`. A program takes and returns all parts, laid end to end along the dimension named above; each array names one. Nothing has to cross between parts.
Inputs may be any that keep to these rules, and one draw needn't show every extreme that they name: `ij_counts`: every symmetry holds at least one occupied-pair tile and at most 32; some symmetry holds exactly 32. The counts sum to 128. `ab_irrep`: every symmetry holds at least one ab tile.
All inputs are finite; a program needn't handle non-finite values.
Results may differ from a plain program's by a relative error of at most 0.001.
Values may be sent and summed in bfloat16 or wider, within the bound.
No kernel may reach another device: no remote copies, remote signals or barrier semaphores. Data moves between devices by JAX's collectives and lax.ppermute only.
A program may use at most 128 MiB of HBM per device.

v0:
```python
import jax
import jax.numpy as jnp
from jax import lax
from jax.sharding import PartitionSpec as P


def build_stacks(padded, ij_counts, capacity):
    offsets = jnp.cumsum(ij_counts) - ij_counts
    position = jnp.arange(capacity, dtype=jnp.int32)
    blocks = []
    for irrep in range(ij_counts.shape[0]):
        block = lax.dynamic_slice_in_dim(padded, offsets[irrep], capacity, 0)
        keep = position < ij_counts[irrep]
        blocks.append(jnp.where(keep[:, None, None], block, jnp.zeros_like(block)))
    stacked = jnp.stack(blocks, axis=0)
    return stacked.reshape(ij_counts.shape[0], capacity * padded.shape[1], padded.shape[2])


def per_device(amplitudes, ij_counts, integrals, ab_irrep):
    tile_rows = amplitudes.shape[1]
    pair_width = amplitudes.shape[2]
    irreps = ij_counts.shape[0]
    all_tiles = amplitudes.shape[0] * lax.axis_size("vir")
    capacity = all_tiles // 4
    gathered = lax.all_gather(amplitudes, "vir", axis=0, tiled=True)
    padded = jnp.concatenate(
        [gathered, jnp.zeros((capacity, tile_rows, pair_width), jnp.bfloat16)], axis=0
    )
    stacks = build_stacks(padded, ij_counts, capacity)
    own_tiles = integrals.shape[0]

    def one_group(group):
        tile_block, irrep_group = group
        results = []
        for member in range(tile_block.shape[0]):
            chosen = lax.dynamic_index_in_dim(stacks, irrep_group[member], 0, keepdims=False)
            results.append(
                lax.dot_general(
                    tile_block[member],
                    chosen,
                    (((1,), (1,)), ((), ())),
                    preferred_element_type=jnp.float32,
                )
            )
        products = jnp.stack(results, axis=0)
        return (products.astype(jnp.bfloat16), jnp.sum(products * products, axis=(1, 2)))

    residual, squares = lax.map(
        one_group,
        (
            integrals.reshape(own_tiles // 8, 8, tile_rows, pair_width),
            ab_irrep.reshape(own_tiles // 8, 8),
        ),
    )
    match = ab_irrep[:, None] == jnp.arange(irreps, dtype=jnp.int32)[None, :]
    partial_sums = jnp.sum(jnp.where(match, squares.reshape(-1)[:, None], jnp.float32(0.0)), axis=0)
    local_counts = jnp.sum(match.astype(jnp.float32), axis=0)
    irrep_sums, ab_counts = lax.psum((partial_sums, local_counts), "vir")
    entries = ab_counts * ij_counts.astype(jnp.float32) * float(tile_rows * tile_rows)
    norms = jnp.sqrt(irrep_sums / entries + 1e-06)
    return (residual.reshape(own_tiles, tile_rows, capacity * tile_rows), norms)


def solution(mesh):
    in_specs = (
        P(("groups", "vir"), None, None),
        P("groups"),
        P(("groups", "vir"), None, None),
        P(("groups", "vir")),
    )
    out_specs = (P(("groups", "vir"), None, None), P("groups"))
    return jax.shard_map(
        per_device, mesh=mesh, in_specs=in_specs, out_specs=out_specs, check_vma=False
    )
```

profile of v0, /device:TPU:0, one launch (start us, length us, event | category | flops | bytes accessed | tf_op | source)
XLA Modules:
  0.0 300.9 jit_solution(12012121934619938479)
XLA Ops:
  25.7 1.6 fusion.41
  31.0 1.3 iota_compare_fusion.2
  32.3 42.6 %all-gather.2.cloned.1.call-done = bf16[128,64,384]{2,1,0:T(8,128)(2,1)} async-done(((bf16[8,64,384]{2,1,0:T(8,128)(2,1)}), bf16[128,64,384]{2,1,0:T(8,128)(2,1)}) %all-gather.2.cloned.1.call-update) | async-done | bytes 6291472 | tf_op jit(solution)/shard_map/all_gather | solution.py:25
  74.9 2.9 fusion.38
  78.7 2.9 fusion.39
  83.9 4.5 %copy-done = bf16[8,2048,384]{2,1,0:T(8,128)(2,1)} copy-done((bf16[8,2048,384]{2,1,0:T(8,128)(2,1)}, bf16[8,2048,384]{2,1,0:T(8,128)(2,1)S(1)}, u32[]{:S(2)}) %copy-start) | copy-done | bytes 12582936
  88.4 173.6 %while.12 = (s32[]{:T(128)}, bf16[4,8,64,2048]{3,2,1,0:T(8,128)(2,1)}, f32[4,8]{1,0:T(4,128)S(1)}, bf16[4,8,64,384]{3,2,1,0:T(8,128)(2,1)}, s32[4,8]{1,0:T(4,128...) while((s32[]{:T(128)}, ...), condition=%wide.region_3.4_spmd, body=%wide.region_1.3_spmd.sunk | while | flops 808452096 | bytes 36050204 | solution.py:48
  91.0 2.0 bitcast_dynamic-update-slice_fusion.40
  95.1 2.1 bitcast_dynamic-update-slice_fusion.41
  101.0 2.1 bitcast_dynamic-update-slice_fusion.42
  105.5 2.1 bitcast_dynamic-update-slice_fusion.43
  110.1 2.1 bitcast_dynamic-update-slice_fusion.44
  115.0 2.1 bitcast_dynamic-update-slice_fusion.45
  119.8 2.1 bitcast_dynamic-update-slice_fusion.46
  124.6 2.1 bitcast_dynamic-update-slice_fusion.47
  127.5 2.6 multiply_reduce_fusion.2
  130.2 1.6 constant_dynamic-update-slice_fusion.2
  134.4 2.1 bitcast_dynamic-update-slice_fusion.40
  138.5 2.1 bitcast_dynamic-update-slice_fusion.41
  144.3 2.1 bitcast_dynamic-update-slice_fusion.42
  148.9 2.1 bitcast_dynamic-update-slice_fusion.43
  153.5 2.1 bitcast_dynamic-update-slice_fusion.44
  158.4 2.1 bitcast_dynamic-update-slice_fusion.45
  163.2 2.1 bitcast_dynamic-update-slice_fusion.46
  168.0 2.1 bitcast_dynamic-update-slice_fusion.47
  170.9 2.6 multiply_reduce_fusion.2
  173.6 1.6 constant_dynamic-update-slice_fusion.2
  177.8 2.1 bitcast_dynamic-update-slice_fusion.40
  181.9 2.1 bitcast_dynamic-update-slice_fusion.41
  187.7 2.1 bitcast_dynamic-update-slice_fusion.42
  192.3 2.1 bitcast_dynamic-update-slice_fusion.43
  196.9 2.1 bitcast_dynamic-update-slice_fusion.44
  201.8 2.1 bitcast_dynamic-update-slice_fusion.45
  206.6 2.1 bitcast_dynamic-update-slice_fusion.46
  211.4 2.1 bitcast_dynamic-update-slice_fusion.47
  214.3 2.6 multiply_reduce_fusion.2
  217.0 1.6 constant_dynamic-update-slice_fusion.2
  221.2 2.1 bitcast_dynamic-update-slice_fusion.40
  225.3 2.1 bitcast_dynamic-update-slice_fusion.41
  231.1 2.1 bitcast_dynamic-update-slice_fusion.42
  235.7 2.1 bitcast_dynamic-update-slice_fusion.43
  240.3 2.1 bitcast_dynamic-update-slice_fusion.44
  245.2 2.1 bitcast_dynamic-update-slice_fusion.45
  250.0 2.1 bitcast_dynamic-update-slice_fusion.46
  254.8 2.1 bitcast_dynamic-update-slice_fusion.47
  257.7 2.6 multiply_reduce_fusion.2
  260.4 1.6 constant_dynamic-update-slice_fusion.2
  262.2 31.3 %all-reduce.1 = (f32[8]{0:T(128)S(1)}, f32[8]{0:T(128)S(1)}) all-reduce(f32[8]{0:T(128)S(1)} %get-tuple-element.38, f32[8]{0:T(128)S(1)} %get-tuple-element.37), channel_id=1, replica_groups=mesh['groups'=2,'vir'=16] {'vir'}, use_global_device_ids=true, to_apply=%region_5.6 | all-reduce | flops 16 | bytes 128 | tf_op jit(solution)/shard_map/psum | solution.py:58
  (76 shorter events, 41.3 us)
Async XLA Ops:
  7.2 67.7 %all-gather.2.cloned.1.call-start = ((), (), s32[]{:S(2)}) async-start(), calls=%async_computation | async-start | bytes 6684672 | tf_op jit(solution)/shard_map/all_gather | solution.py:25
  74.9 3.1 %slice-start = ((s8[6291456]{0:T(1024)(128)(4,1)}), s8[4194304]{0:T(1024)(128)(4,1)S(1)}, s32[]{:S(2)}) async-start(s8[6291456]{0:T(1024)(128)(4,1)} %bitcast.248), calls=%async_computation.1 | async-start | bytes 8388608
  74.9 3.8 %slice-start.1 = ((s8[6291456]{0:T(1024)(128)(4,1)}), s8[2097152]{0:T(1024)(128)(4,1)S(1)}, s32[]{:S(2)}) async-start(s8[6291456]{0:T(1024)(128)(4,1)} %bitcast.248), calls=%async_computation.2 | async-start | bytes 4194304
  83.8 4.5 %copy-start = (bf16[8,2048,384]{2,1,0:T(8,128)(2,1)}, bf16[8,2048,384]{2,1,0:T(8,128)(2,1)S(1)}, u32[]{:S(2)}) copy-start(bf16[8,2048,384]{2,1,0:T(8,128)(2,1)S(1)} %bitcast_dynamic-update-slice_fusion.16) | copy-start | bytes 37748740
  88.4 173.7 %copy-start.2 = (s32[32]{0:T(128)S(1)}, s32[32]{0:T(128)}, u32[]{:S(2)}) copy-start(s32[32]{0:T(128)} %param.9) | copy-start | bytes 388
  88.4 205.1 %copy-start.1 = (s32[8]{0:T(128)S(1)}, s32[8]{0:T(128)}, u32[]{:S(2)}) copy-start(s32[8]{0:T(128)} %param.7) | copy-start | bytes 100
Sparse Core Ops, SparseCore 0:
  10.3 64.5 all-gather.1
where the time goes:
time: 303 us; the launch traced here: 301 us
  matrix products  65.7 us (22%)
  loops' own time  61 us (20%)
  local copies, waits for them, and re-layouts  47.1 us (16%)
  waiting for transfers between devices  43.2 us (14%)
  blocking collectives  31.3 us (10%)
  between operations  29.1 us (10%)
  other arithmetic  23.4 us (8%)
    dot_general x32, matrix products, one_group(): lax.dot_general(tile_block[member], chosen, (((1,), (1,)), ((), ())), pre...  65.7 us
    another operation x1, loops' own time, per_device(): lax.map(one_group, (integrals.reshape(own_tiles // 8, 8, tile_rows, pair_...  61 us
    all_gather x1, waiting for transfers between devices, per_device(): gathered = lax.all_gather(amplitudes, 'vir', axis=0, tiled=True)  42.6 us
    psum x1, blocking collectives, per_device(): irrep_sums, ab_counts = lax.psum((partial_sums, local_counts), 'vir')  31.3 us
    while x28, local copies, waits for them, and re-layouts  23.7 us
    reduce_sum x4, other arithmetic, one_group(): jnp.sum(products * products, axis=(1, 2))  10.5 us
    unnamed x17, local copies, waits for them, and re-layouts  7.36 us
    dynamic_update_slice x8, local copies, waits for them, and re-layouts, per_device(): lax.map(one_group, (integrals.reshape(own_tiles // 8, 8, tile_rows, pair_...  6.4 us
  transfers between devices with their start and end apart: 1, of which 1 were waited for; matrix products, arithmetic and copies ran while one was open for 3% of the time, Pallas kernels for 0%

commit v1 on v0

v1 whole, which is shorter than its diff:
```python
import functools

import jax
import jax.numpy as jnp
from jax import lax
from jax.experimental import pallas as pl
from jax.experimental.pallas import tpu as pltpu
from jax.sharding import PartitionSpec as P

BATCH = 4
VMEM_BYTES = 56 * 1024 * 1024


def ladder_kernel(
    capacity, shard_tiles, n_sources,
    counts_ref, irrep_ref, dest_ref, v_hbm, *refs,
):
    sources = refs[:n_sources]
    res_hbm, stats_ref = refs[n_sources:n_sources + 2]
    a_buf, v_buf, o_buf, acc_ref, size_ref, first_ref, next_ref, offset_ref, order_ref = (
        refs[n_sources + 2:n_sources + 11]
    )
    a_sem, v_sem, o_sem = refs[n_sources + 11:]
    own_tiles, rows, width = v_hbm.shape
    irreps = counts_ref.shape[0]
    all_tiles = sum(source.shape[0] for source in sources)

    piece = 0
    for source in sources:
        for start in range(0, source.shape[0], shard_tiles):
            pltpu.make_async_copy(
                source.at[pl.ds(start, shard_tiles)],
                a_buf.at[pl.ds(dest_ref[piece], shard_tiles)],
                a_sem,
            ).start()
            piece += 1

    for s in range(irreps):
        size_ref[s] = 0

    def count(l, carry):
        s = irrep_ref[l]
        size_ref[s] = size_ref[s] + 1
        return carry

    lax.fori_loop(0, own_tiles, count, 0)
    first, offset = jnp.int32(0), jnp.int32(0)
    for s in range(irreps):
        first_ref[s] = first
        next_ref[s] = first
        offset_ref[s] = offset
        first = first + size_ref[s]
        offset = offset + counts_ref[s]

    def place(l, carry):
        s = irrep_ref[l]
        slot = next_ref[s]
        next_ref[s] = slot + 1
        order_ref[slot] = l
        pltpu.make_async_copy(v_hbm.at[l], v_buf.at[slot], v_sem).start()
        return carry

    lax.fori_loop(0, own_tiles, place, 0)
    pltpu.make_async_copy(v_hbm, v_buf.at[pl.ds(0, own_tiles)], v_sem).wait()
    whole = a_buf.at[pl.ds(0, all_tiles)]
    pltpu.make_async_copy(whole, whole, a_sem).wait()

    side = BATCH * rows
    row_at = lax.broadcasted_iota(jnp.int32, (side, side), 0)
    col_at = lax.broadcasted_iota(jnp.int32, (side, side), 1)

    def symmetry(s, carry):
        size, slot0 = size_ref[s], first_ref[s]
        tiles, offset = counts_ref[s], offset_ref[s]
        blocks = (tiles + BATCH - 1) // BATCH

        def member_batch(i, total):
            slot = slot0 + i * BATCH
            rows_left = (size - i * BATCH) * rows

            def column_block(j, total):
                left = v_buf[pl.ds(slot, BATCH)].reshape(side, width)
                right = a_buf[pl.ds(offset + j * BATCH, BATCH)].reshape(side, width)
                product = lax.dot_general(
                    left, right, (((1,), (1,)), ((), ())),
                    preferred_element_type=jnp.float32,
                )
                keep = (row_at < rows_left) & (col_at < (tiles - j * BATCH) * rows)
                product = jnp.where(keep, product, 0.0)
                o_buf[pl.ds(slot, BATCH), :, pl.ds(pl.multiple_of(j * side, side), side)] = (
                    product.astype(jnp.bfloat16).reshape(BATCH, rows, side)
                )
                squares = (product * product).reshape(side // 8, 8, side)
                return total + jnp.sum(squares, axis=0)

            def blank_block(j, inner):
                o_buf[pl.ds(slot, BATCH), :, pl.ds(pl.multiple_of(j * side, side), side)] = (
                    jnp.zeros((BATCH, rows, side), jnp.bfloat16)
                )
                return inner

            total = lax.fori_loop(0, blocks, column_block, total)
            lax.fori_loop(blocks, capacity // BATCH, blank_block, 0)
            for t in range(BATCH):
                @pl.when(i * BATCH + t < size)
                def _():
                    pltpu.make_async_copy(
                        o_buf.at[slot + t], res_hbm.at[order_ref[slot + t]], o_sem
                    ).start()
            return total

        acc_ref[s] = lax.fori_loop(
            0, (size + BATCH - 1) // BATCH, member_batch, jnp.zeros((8, side), jnp.float32)
        )
        return carry

    lax.fori_loop(0, irreps, symmetry, 0)
    sums = jnp.sum(acc_ref[...], axis=1)
    sums = sum(sums[:, k:k + 128] for k in range(0, side, 128))
    stats_ref[0] = sums
    at_row = lax.broadcasted_iota(jnp.int32, sums.shape, 0)
    at_lane = lax.broadcasted_iota(jnp.int32, sums.shape, 1)
    sizes = jnp.zeros(sums.shape, jnp.int32)
    for s in range(irreps):
        sizes = jnp.where((at_row == s) & (at_lane == 0), size_ref[s], sizes)
    stats_ref[1] = sizes.astype(jnp.float32)
    pltpu.make_async_copy(o_buf.at[pl.ds(0, own_tiles)], res_hbm, o_sem).wait()


def ladder(counts, irrep, dest, integrals, sources, shard_tiles, capacity):
    own_tiles, rows, width = integrals.shape
    irreps = counts.shape[0]
    all_tiles = sum(source.shape[0] for source in sources)
    smem = pl.BlockSpec(memory_space=pltpu.SMEM)
    anywhere = pl.BlockSpec(memory_space=pl.ANY)
    return pl.pallas_call(
        functools.partial(ladder_kernel, capacity, shard_tiles, len(sources)),
        out_shape=(
            jax.ShapeDtypeStruct((own_tiles, rows, capacity * rows), jnp.bfloat16),
            jax.ShapeDtypeStruct((2, irreps, 128), jnp.float32),
        ),
        in_specs=[smem, smem, smem] + [anywhere] * (1 + len(sources)),
        out_specs=(anywhere, pl.BlockSpec(memory_space=pltpu.VMEM)),
        scratch_shapes=[
            pltpu.VMEM((all_tiles + BATCH, rows, width), jnp.bfloat16),
            pltpu.VMEM((own_tiles + BATCH, rows, width), jnp.bfloat16),
            pltpu.VMEM((own_tiles + BATCH, rows, capacity * rows), jnp.bfloat16),
            pltpu.VMEM((irreps, 8, BATCH * rows), jnp.float32),
            pltpu.SMEM((irreps,), jnp.int32),
            pltpu.SMEM((irreps,), jnp.int32),
            pltpu.SMEM((irreps,), jnp.int32),
            pltpu.SMEM((irreps,), jnp.int32),
            pltpu.SMEM((own_tiles,), jnp.int32),
            pltpu.SemaphoreType.DMA,
            pltpu.SemaphoreType.DMA,
            pltpu.SemaphoreType.DMA,
        ],
        compiler_params=pltpu.CompilerParams(vmem_limit_bytes=VMEM_BYTES),
        name="ladder",
    )(counts, irrep, dest, integrals, *sources)


def per_device(amplitudes, ij_counts, integrals, ab_irrep):
    shard_tiles, rows, _ = amplitudes.shape
    devices = lax.axis_size("vir")
    me = lax.axis_index("vir")
    capacity = shard_tiles * devices // 4
    same_core = [list(range(core, devices, 2)) for core in range(2)]
    swap_core = [(d, d ^ 1) for d in range(devices)]

    mine = lax.all_gather(amplitudes, "vir", axis=0, tiled=True, axis_index_groups=same_core)
    other = lax.ppermute(mine, "vir", swap_core)
    core = me % 2
    half = jnp.arange(devices // 2, dtype=jnp.int32) * 2
    dest = jnp.concatenate([half + core, half + 1 - core]) * shard_tiles

    residual, stats = ladder(ij_counts, ab_irrep, dest, integrals, [mine, other], shard_tiles, capacity)

    step = 1
    while step < devices:
        stats = stats + lax.ppermute(stats, "vir", [(d, d ^ step) for d in range(devices)])
        step *= 2
    irrep_sums, ab_counts = jnp.sum(stats, axis=2)
    entries = ab_counts * ij_counts.astype(jnp.float32) * float(rows * rows)
    return residual, jnp.sqrt(irrep_sums / entries + 1e-06)


def solution(mesh):
    in_specs = (
        P(("groups", "vir"), None, None),
        P("groups"),
        P(("groups", "vir"), None, None),
        P(("groups", "vir")),
    )
    out_specs = (P(("groups", "vir"), None, None), P("groups"))
    return jax.shard_map(
        per_device, mesh=mesh, in_specs=in_specs, out_specs=out_specs, check_vma=False
    )
```

time: 303 us -> 123 us (0.41)
  matrix products: 65.7 us -> 0 us
  loops' own time: 61 us -> 0 us
  local copies, waits for them, and re-layouts: 47.1 us -> 1.69 us
  waiting for transfers between devices: 43.2 us -> 79.3 us
  blocking collectives: 31.3 us -> 0 us
  other arithmetic: 23.4 us -> 1.92 us
  Pallas kernels: 0 us -> 17.9 us
  between operations: 29.1 us -> 14.1 us
  starting transfers between devices: 0.04 us -> 6.58 us
    dot_general x32 -> x0, matrix products: 65.7 us -> none  [one_group(): lax.dot_general(tile_block[member], chosen, (((1,), (1,)), ((), ())), pre...]
    another operation x1 -> x0, loops' own time: 61 us -> none  [per_device(): lax.map(one_group, (integrals.reshape(own_tiles // 8, 8, tile_rows, pair_...]
    psum x1 -> x0, blocking collectives: 31.3 us -> none  [per_device(): irrep_sums, ab_counts = lax.psum((partial_sums, local_counts), 'vir')]
    while x28 -> x0, local copies, waits for them, and re-layouts: 23.7 us -> none
    all_gather x1, waiting for transfers between devices: 42.6 us -> 65.5 us  [per_device(): lax.all_gather(amplitudes, 'vir', axis=0, tiled=True, axis_index_groups=s...]
    pallas_call x0 -> x1, Pallas kernels: none -> 17.9 us  [ladder(): pl.pallas_call(functools.partial(ladder_kernel, capacity, shard_tiles, le...]
    ppermute x0 -> x5, waiting for transfers between devices: none -> 13.2 us  [the longest x4 7.9 us: per_device(): lax.ppermute(stats, 'vir', [(d, d ^ step) for d in range(devices)])]
    reduce_sum x5 -> x1, other arithmetic: 10.7 us -> 0.09 us  [per_device(): irrep_sums, ab_counts = jnp.sum(stats, axis=2)]
  transfers between devices with their start and end apart: 1 -> 6, of which waited for: 1 -> 6; matrix products, arithmetic and copies ran while one was open for 3% -> 0% of each run, Pallas kernels for 0% -> 0%
where the time goes in v1:
time: 123 us; the launch traced here: 121 us
  waiting for transfers between devices  79.3 us (64%)
  Pallas kernels  17.9 us (15%)
  between operations  14.1 us (11%)
  starting transfers between devices  6.58 us (5%)
  other arithmetic  1.92 us (2%)
  local copies, waits for them, and re-layouts  1.69 us (1%)
    all_gather x1, waiting for transfers between devices, per_device(): lax.all_gather(amplitudes, 'vir', axis=0, tiled=True, axis_index_groups=s...  65.5 us
    pallas_call x1, Pallas kernels, ladder(): pl.pallas_call(functools.partial(ladder_kernel, capacity, shard_tiles, le...  17.9 us
    ppermute x4, waiting for transfers between devices, per_device(): lax.ppermute(stats, 'vir', [(d, d ^ step) for d in range(devices)])  7.9 us
    ppermute x4, starting transfers between devices, per_device(): lax.ppermute(stats, 'vir', [(d, d ^ step) for d in range(devices)])  6.54 us
    ppermute x1, waiting for transfers between devices, per_device(): other = lax.ppermute(mine, 'vir', swap_core)  5.27 us
  transfers between devices with their start and end apart: 6, of which 6 were waited for; matrix products, arithmetic and copies ran while one was open for 0% of the time, Pallas kernels for 0%

profile of v1, /device:TPU:0, one launch (start us, length us, event | category | flops | bytes accessed | tf_op | source)
XLA Modules:
  0.0 121.4 jit_solution(8385084824051457503)
XLA Ops:
  7.2 0.0 all-gather.2.cloned.1.call-start
  7.2 0.7 all-gather.2.cloned.1.call-update
  7.9 65.5 %all-gather.2.cloned.1.call-done.refs_0_ = bf16[64,64,384]{2,1,0:T(8,128)(2,1)} async-done(((bf16[8,64,384]{2,1,0:T(8,128)(2,1)}), bf16[64,64,384]{2,1,0:T(8,128)(2,1)}) %all-gather.2.cloned.1.call-update) | async-done | bytes 3145744 | tf_op jit(solution)/shard_map/all_gather | solution.py:171
  73.4 0.0 collective-permute-start
  73.4 0.6 add_multiply_fusion.dest_ref
  74.0 0.0 copy-start.1
  74.0 5.3 %collective-permute-done.refs_1_ = bf16[64,64,384]{2,1,0:T(8,128)(2,1)S(1)} collective-permute-done((bf16[64,64,384]{2,1,0:T(8,128)(2,1)}, bf16[64,64,384]{2,1,0:T(8,128)(2,1)S(1)}, u32[]{:S(2)}, u32[]{:S(2)}) %collective-permute-start) | collective-permute-done | bytes 3145760 | tf_op jit(solution)/shard_map/ppermute | solution.py:172
  79.2 0.0 copy-start
  79.2 1.7 %copy-done = bf16[64,64,384]{2,1,0:T(8,128)(2,1)} copy-done((bf16[64,64,384]{2,1,0:T(8,128)(2,1)}, bf16[64,64,384]{2,1,0:T(8,128)(2,1)S(1)}, u32[]{:S(2)}) %copy-start) | copy-done | bytes 3145752
  80.9 17.9 %ladder.1 = (bf16[32,64,2048]{2,1,0:T(8,128)(2,1)}, f32[2,8,128]{2,1,0:T(8,128)}) custom-call(s32[8]{0:T(128)} %counts_ref.1, s32[32]{0:T(128)} %irrep_ref.1, s32[16]{0:T(128)} %add_multiply_fusion.dest_ref, bf16[32,64,384]{2,1,0:T(8,128)(2,1)} %v_hbm.1, bf16[64,64,384]{2,1,0:T(8,128)(2,1)} %all-gather.2.cloned.1.call-done.refs_0_, bf16[64,64,384]{2,1,0:T(8,128)(2,1)} %copy-done), custom_call_target="tpu_custom_call" | custom-call | tf_op jit(solution)/shard_map/ladder/pallas_call | solution.py:136
  98.8 0.1 collective-permute-start.1
  98.9 1.4 %collective-permute-done.1 = f32[2,8,128]{2,1,0:T(8,128)S(1)} collective-permute-done((f32[2,8,128]{2,1,0:T(8,128)}, f32[2,8,128]{2,1,0:T(8,128)S(1)}, u32[]{:S(2)}, u32[]{:S(2)}) %collective-permute-start.1) | collective-permute-done | bytes 8224 | tf_op jit(solution)/shard_map/ppermute | solution.py:181
  100.3 0.7 add.32
  101.0 1.5 %collective-permute-start.2 = (f32[2,8,128]{2,1,0:T(8,128)S(1)}, f32[2,8,128]{2,1,0:T(8,128)S(1)}, u32[]{:S(2)}, u32[]{:S(2)}) collective-permute-start(f32[2,8,128]{2,1,0:T(8,128)S(1)} %add.32), channel_id=1, source_target_pairs={{0,2},{1,3},{2,0},{3,1},{4,6},{5,7},{6,4},{7,5},{8,10},{9,11},{10,... | collective-permute-start | bytes 24584 | tf_op jit(solution)/shard_map/ppermute | solution.py:181
  102.5 2.1 %collective-permute-done.2 = f32[2,8,128]{2,1,0:T(8,128)S(1)} collective-permute-done((f32[2,8,128]{2,1,0:T(8,128)S(1)}, f32[2,8,128]{2,1,0:T(8,128)S(1)}, u32[]{:S(2)}, u32[]{:S(2)}) %collective-permute-start.2) | collective-permute-done | bytes 8224 | tf_op jit(solution)/shard_map/ppermute | solution.py:181
  104.6 3.2 %collective-permute-start.3 = (f32[2,8,128]{2,1,0:T(8,128)S(1)}, f32[2,8,128]{2,1,0:T(8,128)S(1)}, u32[]{:S(2)}, u32[]{:S(2)}) collective-permute-start(f32[2,8,128]{2,1,0:T(8,128)S(1)} %add.33), channel_id=1, source_target_pairs={{0,4},{1,5},{2,6},{3,7},{4,0},{5,1},{6,2},{7,3},{8,12},{9,13},{10,... | collective-permute-start | bytes 24584 | tf_op jit(solution)/shard_map/ppermute | solution.py:181
  107.8 1.6 %collective-permute-done.3 = f32[2,8,128]{2,1,0:T(8,128)S(1)} collective-permute-done((f32[2,8,128]{2,1,0:T(8,128)S(1)}, f32[2,8,128]{2,1,0:T(8,128)S(1)}, u32[]{:S(2)}, u32[]{:S(2)}) %collective-permute-start.3) | collective-permute-done | bytes 8224 | tf_op jit(solution)/shard_map/ppermute | solution.py:181
  109.4 1.8 %collective-permute-start.4 = (f32[2,8,128]{2,1,0:T(8,128)S(1)}, f32[2,8,128]{2,1,0:T(8,128)S(1)}, u32[]{:S(2)}, u32[]{:S(2)}) collective-permute-start(f32[2,8,128]{2,1,0:T(8,128)S(1)} %add.34), channel_id=1, source_target_pairs={{0,8},{1,9},{2,10},{3,11},{4,12},{5,13},{6,14},{7,15},{8,0},{9,1},... | collective-permute-start | bytes 24584 | tf_op jit(solution)/shard_map/ppermute | solution.py:181
  111.2 2.8 %collective-permute-done.4 = f32[2,8,128]{2,1,0:T(8,128)S(1)} collective-permute-done((f32[2,8,128]{2,1,0:T(8,128)S(1)}, f32[2,8,128]{2,1,0:T(8,128)S(1)}, u32[]{:S(2)}, u32[]{:S(2)}) %collective-permute-start.4) | collective-permute-done | bytes 8224 | tf_op jit(solution)/shard_map/ppermute | solution.py:181
  114.0 0.1 add_reduce_fusion
  114.1 0.0 copy-done.1
  114.1 0.5 add_sqrt_fusion
  (3 shorter events, 0.0 us)
Async XLA Ops:
  7.2 66.2 %all-gather.2.cloned.1.call-start = ((), (), s32[]{:S(2)}) async-start(), calls=%async_computation | async-start | bytes 3538944 | tf_op jit(solution)/shard_map/all_gather | solution.py:171
  73.4 5.9 %collective-permute-start = (bf16[64,64,384]{2,1,0:T(8,128)(2,1)}, bf16[64,64,384]{2,1,0:T(8,128)(2,1)S(1)}, u32[]{:S(2)}, u32[]{:S(2)}) collective-permute-start(bf16[64,64,384]{2,1,0:T(8,128)(2,1)} %all-gather.2.cloned.1.call-done.refs_0_), channel_id=1, source_target_pairs={{0,1},{1,0},{2,3},{3,2},{4,5},{5,4},{6,7},{7,6},{8,9},{9,8},{10,11... | collective-permute-start | bytes 9437192 | tf_op jit(solution)/shard_map/ppermute | solution.py:172
  74.0 40.1 %copy-start.1 = (s32[8]{0:T(128)S(1)}, s32[8]{0:T(128)}, u32[]{:S(2)}) copy-start(s32[8]{0:T(128)} %counts_ref.1) | copy-start | bytes 100
  79.2 1.7 %copy-start = (bf16[64,64,384]{2,1,0:T(8,128)(2,1)}, bf16[64,64,384]{2,1,0:T(8,128)(2,1)S(1)}, u32[]{:S(2)}) copy-start(bf16[64,64,384]{2,1,0:T(8,128)(2,1)S(1)} %collective-permute-done.refs_1_) | copy-start | bytes 9437188
  98.8 1.4 %collective-permute-start.1 = (f32[2,8,128]{2,1,0:T(8,128)}, f32[2,8,128]{2,1,0:T(8,128)S(1)}, u32[]{:S(2)}, u32[]{:S(2)}) collective-permute-start(f32[2,8,128]{2,1,0:T(8,128)} %get-tuple-element.5), channel_id=1, source_target_pairs={{0,1},{1,0},{2,3},{3,2},{4,5},{5,4},{6,7},{7,6},{8,9},{9,8},{10,11... | collective-permute-start | bytes 24584 | tf_op jit(solution)/shard_map/ppermute | solution.py:181
  101.0 3.7 %collective-permute-start.2 = (f32[2,8,128]{2,1,0:T(8,128)S(1)}, f32[2,8,128]{2,1,0:T(8,128)S(1)}, u32[]{:S(2)}, u32[]{:S(2)}) collective-permute-start(f32[2,8,128]{2,1,0:T(8,128)S(1)} %add.32), channel_id=1, source_target_pairs={{0,2},{1,3},{2,0},{3,1},{4,6},{5,7},{6,4},{7,5},{8,10},{9,11},{10,... | collective-permute-start | bytes 24584 | tf_op jit(solution)/shard_map/ppermute | solution.py:181
  104.6 4.8 %collective-permute-start.3 = (f32[2,8,128]{2,1,0:T(8,128)S(1)}, f32[2,8,128]{2,1,0:T(8,128)S(1)}, u32[]{:S(2)}, u32[]{:S(2)}) collective-permute-start(f32[2,8,128]{2,1,0:T(8,128)S(1)} %add.33), channel_id=1, source_target_pairs={{0,4},{1,5},{2,6},{3,7},{4,0},{5,1},{6,2},{7,3},{8,12},{9,13},{10,... | collective-permute-start | bytes 24584 | tf_op jit(solution)/shard_map/ppermute | solution.py:181
  109.4 4.5 %collective-permute-start.4 = (f32[2,8,128]{2,1,0:T(8,128)S(1)}, f32[2,8,128]{2,1,0:T(8,128)S(1)}, u32[]{:S(2)}, u32[]{:S(2)}) collective-permute-start(f32[2,8,128]{2,1,0:T(8,128)S(1)} %add.34), channel_id=1, source_target_pairs={{0,8},{1,9},{2,10},{3,11},{4,12},{5,13},{6,14},{7,15},{8,0},{9,1},... | collective-permute-start | bytes 24584 | tf_op jit(solution)/shard_map/ppermute | solution.py:181
Sparse Core Ops, SparseCore 0:
  10.2 63.1 all-gather.1

commit v2 on v1

--- a/solution.py
+++ b/solution.py
@@ -163,23 +163,33 @@
 def per_device(amplitudes, ij_counts, integrals, ab_irrep):
     shard_tiles, rows, _ = amplitudes.shape
     devices = lax.axis_size("vir")
+    depth = devices // 4
     me = lax.axis_index("vir")
+    z, y, core = me // 4, me // 2 % 2, me % 2
     capacity = shard_tiles * devices // 4
-    same_core = [list(range(core, devices, 2)) for core in range(2)]
-    swap_core = [(d, d ^ 1) for d in range(devices)]
-
-    mine = lax.all_gather(amplitudes, "vir", axis=0, tiled=True, axis_index_groups=same_core)
-    other = lax.ppermute(mine, "vir", swap_core)
-    core = me % 2
-    half = jnp.arange(devices // 2, dtype=jnp.int32) * 2
-    dest = jnp.concatenate([half + core, half + 1 - core]) * shard_tiles
-
-    residual, stats = ladder(ij_counts, ab_irrep, dest, integrals, [mine, other], shard_tiles, capacity)
-
-    step = 1
-    while step < devices:
-        stats = stats + lax.ppermute(stats, "vir", [(d, d ^ step) for d in range(devices)])
-        step *= 2
+
+    def shift_z(x, by):
+        return lax.ppermute(x, "vir", [(d, (d + 4 * by) % devices) for d in range(devices)])
+
+    def swap(x, bit):
+        return lax.ppermute(x, "vir", [(d, d ^ bit) for d in range(devices)])
+
+    sources, dest = [], []
+    here = amplitudes
+    for k in range(depth):
+        there = swap(here, 2)
+        sources += [here, there, swap(here, 1), swap(there, 1)]
+        at = (z + depth - k) % depth
+        for other_y, other_core in ((0, 0), (1, 0), (0, 1), (1, 1)):
+            dest.append((at * 2 + (y ^ other_y)) * 2 + (core ^ other_core))
+        if k < depth - 1:
+            here = shift_z(here, 1)
+    dest = jnp.stack(dest) * shard_tiles
+
+    residual, stats = ladder(ij_counts, ab_irrep, dest, integrals, sources, shard_tiles, capacity)
+
+    stats = sum([shift_z(stats, by) for by in range(1, depth)], stats)
+    stats = sum([swap(stats, bits) for bits in (1, 2, 3)], stats)
     irrep_sums, ab_counts = jnp.sum(stats, axis=2)
     entries = ab_counts * ij_counts.astype(jnp.float32) * float(rows * rows)
     return residual, jnp.sqrt(irrep_sums / entries + 1e-06)

time: 123 us -> 93.4 us (0.76)
  waiting for transfers between devices: 79.3 us -> 54.6 us
  between operations: 14.1 us -> 0.77 us
  starting transfers between devices: 6.58 us -> 16 us
  local copies, waits for them, and re-layouts: 1.69 us -> 0.12 us
    all_gather x1 -> x0, waiting for transfers between devices: 65.5 us -> none  [per_device(): lax.all_gather(amplitudes, 'vir', axis=0, tiled=True, axis_index_groups=s...]
    ppermute x5 -> x21, waiting for transfers between devices: 13.2 us -> 54.6 us  [the longest x6 35.8 us: shift_z(): lax.ppermute(x, 'vir', [(d, (d + 4 * by) % devices) for d in range(device...]
    ppermute x5 -> x21, starting transfers between devices: 6.54 us -> 16 us  [the longest x15 8.5 us: swap(): return lax.ppermute(x, 'vir', [(d, d ^ bit) for d in range(devices)])]
    unnamed x4 -> x18, local copies, waits for them, and re-layouts: 1.69 us -> 0.03 us
  transfers between devices with their start and end apart: 6 -> 21, of which waited for: 6 -> 10; matrix products, arithmetic and copies ran while one was open for 0% -> 1% of each run, Pallas kernels for 0% -> 0%
where the time goes in v2:
time: 93.4 us; the launch traced here: 91.7 us
  waiting for transfers between devices  54.6 us (58%)
  Pallas kernels  17.7 us (19%)
  starting transfers between devices  16 us (17%)
  other arithmetic  2.5 us (3%)
    ppermute x6, waiting for transfers between devices, shift_z(): lax.ppermute(x, 'vir', [(d, (d + 4 * by) % devices) for d in range(device...  35.8 us
    ppermute x15, waiting for transfers between devices, swap(): return lax.ppermute(x, 'vir', [(d, d ^ bit) for d in range(devices)])  18.8 us
    pallas_call x1, Pallas kernels, ladder(): pl.pallas_call(functools.partial(ladder_kernel, capacity, shard_tiles, le...  17.7 us
    ppermute x15, starting transfers between devices, swap(): return lax.ppermute(x, 'vir', [(d, d ^ bit) for d in range(devices)])  8.5 us
    ppermute x6, starting transfers between devices, shift_z(): lax.ppermute(x, 'vir', [(d, (d + 4 * by) % devices) for d in range(device...  7.48 us
  transfers between devices with their start and end apart: 21, of which 10 were waited for; matrix products, arithmetic and copies ran while one was open for 1% of the time, Pallas kernels for 0%

profile of v2, /device:TPU:0, one launch (start us, length us, event | category | flops | bytes accessed | tf_op | source)
XLA Modules:
  0.0 91.7 jit_solution(13616291385540121389)
XLA Ops:
  0.6 3.1 %collective-permute-start.3 = (bf16[8,64,384]{2,1,0:T(8,128)(2,1)}, bf16[8,64,384]{2,1,0:T(8,128)(2,1)S(1)}, u32[]{:S(2)}, u32[]{:S(2)}) collective-permute-start(bf16[8,64,384]{2,1,0:T(8,128)(2,1)} %refs_0_.1), channel_id=1, source_target_pairs={{0,4},{1,5},{2,6},{3,7},{4,8},{5,9},{6,10},{7,11},{8,12},{9,13},{1... | collective-permute-start | bytes 1179656 | tf_op jit(solution)/shard_map/ppermute | solution.py:172
  3.7 11.4 %collective-permute-done.3.refs_4_ = bf16[8,64,384]{2,1,0:T(8,128)(2,1)S(1)} collective-permute-done((bf16[8,64,384]{2,1,0:T(8,128)(2,1)}, bf16[8,64,384]{2,1,0:T(8,128)(2,1)S(1)}, u32[]{:S(2)}, u32[]{:S(2)}) %collective-permute-start.3) | collective-permute-done | bytes 393248 | tf_op jit(solution)/shard_map/ppermute | solution.py:172
  15.1 0.0 collective-permute-start.7
  15.1 1.5 %collective-permute-start = (bf16[8,64,384]{2,1,0:T(8,128)(2,1)}, bf16[8,64,384]{2,1,0:T(8,128)(2,1)S(1)}, u32[]{:S(2)}, u32[]{:S(2)}) collective-permute-start(bf16[8,64,384]{2,1,0:T(8,128)(2,1)} %refs_0_.1), channel_id=1, source_target_pairs={{0,2},{1,3},{2,0},{3,1},{4,6},{5,7},{6,4},{7,5},{8,10},{9,11},{10,... | collective-permute-start | bytes 1179656 | tf_op jit(solution)/shard_map/ppermute | solution.py:175
  16.6 0.0 collective-permute-start.1
  16.6 10.6 %collective-permute-done.7.refs_8_ = bf16[8,64,384]{2,1,0:T(8,128)(2,1)S(1)} collective-permute-done((bf16[8,64,384]{2,1,0:T(8,128)(2,1)S(1)}, bf16[8,64,384]{2,1,0:T(8,128)(2,1)S(1)}, u32[]{:S(2)}, u32[]{:S(2)}) %collective-permute-start.7) | collective-permute-done | bytes 393248 | tf_op jit(solution)/shard_map/ppermute | solution.py:172
  27.2 0.0 collective-permute-start.11
  27.2 0.0 collective-permute-done.refs_1_
  27.2 0.1 collective-permute-start.2
  27.3 1.3 %collective-permute-start.4 = (bf16[8,64,384]{2,1,0:T(8,128)(2,1)S(1)}, bf16[8,64,384]{2,1,0:T(8,128)(2,1)S(1)}, u32[]{:S(2)}, u32[]{:S(2)}) collective-permute-start(bf16[8,64,384]{2,1,0:T(8,128)(2,1)S(1)} %collective-permute-done.3.refs_4_), channel_id=1, source_target_pairs={{0,2},{1,3},{2,0},{3,1},{4,6},{5,7},{6,4},{7,5},{8,10},{9,11},{10,... | collective-permute-start | bytes 1179656 | tf_op jit(solution)/shard_map/ppermute | solution.py:175
  28.6 0.2 collective-permute-start.5
  28.8 0.0 collective-permute-done.1.refs_2_
  28.8 0.7 collective-permute-start.8
  29.5 8.8 %collective-permute-done.11.refs_12_ = bf16[8,64,384]{2,1,0:T(8,128)(2,1)S(1)} collective-permute-done((bf16[8,64,384]{2,1,0:T(8,128)(2,1)S(1)}, bf16[8,64,384]{2,1,0:T(8,128)(2,1)S(1)}, u32[]{:S(2)}, u32[]{:S(2)}) %collective-permute-start.11) | collective-permute-done | bytes 393248 | tf_op jit(solution)/shard_map/ppermute | solution.py:172
  38.3 1.0 %collective-permute-start.12 = (bf16[8,64,384]{2,1,0:T(8,128)(2,1)S(1)}, bf16[8,64,384]{2,1,0:T(8,128)(2,1)}, u32[]{:S(2)}, u32[]{:S(2)}) collective-permute-start(bf16[8,64,384]{2,1,0:T(8,128)(2,1)S(1)} %collective-permute-done.11.refs_12_), channel_id=1, source_target_pairs={{0,2},{1,3},{2,0},{3,1},{4,6},{5,7},{6,4},{7,5},{8,10},{9,11},{10,... | collective-permute-start | bytes 1179656 | tf_op jit(solution)/shard_map/ppermute | solution.py:175
  39.4 0.0 collective-permute-done.2.refs_3_
  39.4 0.0 collective-permute-start.9
  39.4 0.0 collective-permute-done.4.refs_5_
  39.4 0.5 collective-permute-start.6
  39.9 0.0 collective-permute-done.5.refs_6_
  39.9 0.1 collective-permute-start.13
  40.0 7.7 %collective-permute-done.8.refs_9_ = bf16[8,64,384]{2,1,0:T(8,128)(2,1)S(1)} collective-permute-done((bf16[8,64,384]{2,1,0:T(8,128)(2,1)S(1)}, bf16[8,64,384]{2,1,0:T(8,128)(2,1)S(1)}, u32[]{:S(2)}, u32[]{:S(2)}) %collective-permute-start.8) | collective-permute-done | bytes 393248 | tf_op jit(solution)/shard_map/ppermute | solution.py:175
  47.7 0.0 collective-permute-start.10
  47.7 8.1 %collective-permute-done.12.refs_13_ = bf16[8,64,384]{2,1,0:T(8,128)(2,1)} collective-permute-done((bf16[8,64,384]{2,1,0:T(8,128)(2,1)S(1)}, bf16[8,64,384]{2,1,0:T(8,128)(2,1)}, u32[]{:S(2)}, u32[]{:S(2)}) %collective-permute-start.12) | collective-permute-done | bytes 393248 | tf_op jit(solution)/shard_map/ppermute | solution.py:175
  55.8 0.0 collective-permute-start.14
  55.8 0.1 stack.67
  55.8 0.5 broadcast_multiply_fusion.dest_ref
  56.4 0.0 collective-permute-done.9.refs_10_
  56.4 0.0 collective-permute-done.6.refs_7_
  56.4 0.0 collective-permute-done.13.refs_14_
  56.4 0.0 collective-permute-done.10.refs_11_
  56.4 1.4 %collective-permute-done.14.refs_15_ = bf16[8,64,384]{2,1,0:T(8,128)(2,1)} collective-permute-done((bf16[8,64,384]{2,1,0:T(8,128)(2,1)}, bf16[8,64,384]{2,1,0:T(8,128)(2,1)}, u32[]{:S(2)}, u32[]{:S(2)}) %collective-permute-start.14) | collective-permute-done | bytes 393248 | tf_op jit(solution)/shard_map/ppermute | solution.py:175
  57.9 17.7 %ladder.1 = (bf16[32,64,2048]{2,1,0:T(8,128)(2,1)}, f32[2,8,128]{2,1,0:T(8,128)}) custom-call(s32[8]{0:T(128)} %counts_ref.1, s32[32]{0:T(128)} %irrep_ref.1, s32[16]{0:T(128)} %broadcast_multiply_fusion.dest_ref, bf16[32,64,384]{2,1,0:T(8,128)(2,1)} %v_hbm.1, bf16[8,64,384]{2,1,0:T(8,128)(2,1)} %refs_0_.1, bf16[8,64,384]{2,1,0:T(8,128)(2,1)} %copy-done.2, ...), custom_call_target="tpu_custom_call" | custom-call | tf_op jit(solution)/shard_map/ladder/pallas_call | solution.py:136
  75.6 3.8 %collective-permute-start.17 = (f32[2,8,128]{2,1,0:T(8,128)}, f32[2,8,128]{2,1,0:T(8,128)S(1)}, u32[]{:S(2)}, u32[]{:S(2)}) collective-permute-start(f32[2,8,128]{2,1,0:T(8,128)} %get-tuple-element.5), channel_id=1, source_target_pairs={{0,12},{1,13},{2,14},{3,15},{4,0},{5,1},{6,2},{7,3},{8,4},{9,5},{1... | collective-permute-start | bytes 24584 | tf_op jit(solution)/shard_map/ppermute | solution.py:172
  79.4 0.0 collective-permute-start.16
  79.4 0.6 collective-permute-start.15
  80.0 0.9 %collective-permute-done.17 = f32[2,8,128]{2,1,0:T(8,128)S(1)} collective-permute-done((f32[2,8,128]{2,1,0:T(8,128)}, f32[2,8,128]{2,1,0:T(8,128)S(1)}, u32[]{:S(2)}, u32[]{:S(2)}) %collective-permute-start.17) | collective-permute-done | bytes 8224 | tf_op jit(solution)/shard_map/ppermute | solution.py:172
  81.0 3.2 %collective-permute-done.16 = f32[2,8,128]{2,1,0:T(8,128)S(1)} collective-permute-done((f32[2,8,128]{2,1,0:T(8,128)}, f32[2,8,128]{2,1,0:T(8,128)S(1)}, u32[]{:S(2)}, u32[]{:S(2)}) %collective-permute-start.16) | collective-permute-done | bytes 8224 | tf_op jit(solution)/shard_map/ppermute | solution.py:172
  84.2 0.9 collective-permute-done.15
  85.1 0.7 add_add_fusion
  85.8 0.0 collective-permute-start.20
  85.8 2.9 %collective-permute-start.19 = (f32[2,8,128]{2,1,0:T(8,128)S(1)}, f32[2,8,128]{2,1,0:T(8,128)S(1)}, u32[]{:S(2)}, u32[]{:S(2)}) collective-permute-start(f32[2,8,128]{2,1,0:T(8,128)S(1)} %add_add_fusion), channel_id=1, source_target_pairs={{0,2},{1,3},{2,0},{3,1},{4,6},{5,7},{6,4},{7,5},{8,10},{9,11},{10,... | collective-permute-start | bytes 24584 | tf_op jit(solution)/shard_map/ppermute | solution.py:175
  88.7 0.1 collective-permute-start.18
  88.8 0.0 collective-permute-done.20
  88.8 1.6 %collective-permute-done.19 = f32[2,8,128]{2,1,0:T(8,128)S(1)} collective-permute-done((f32[2,8,128]{2,1,0:T(8,128)S(1)}, f32[2,8,128]{2,1,0:T(8,128)S(1)}, u32[]{:S(2)}, u32[]{:S(2)}) %collective-permute-start.19) | collective-permute-done | bytes 8224 | tf_op jit(solution)/shard_map/ppermute | solution.py:175
  90.4 0.0 collective-permute-done.18
  90.4 0.1 add_reduce_fusion
  90.5 1.2 %add_sqrt_fusion = f32[8]{0:T(128)} fusion(s32[8]{0:T(128)} %counts_ref.1, f32[2,8]{1,0:T(2,128)S(1)} %add_reduce_fusion), kind=kLoop, calls=%fused_computation.5 | loop fusion | flops 40 | bytes 128 | tf_op jit(solution)/shard_map/sqrt | solution.py:195
  (18 shorter events, 0.0 us)
Async XLA Ops:
  0.6 14.4 %collective-permute-start.3 = (bf16[8,64,384]{2,1,0:T(8,128)(2,1)}, bf16[8,64,384]{2,1,0:T(8,128)(2,1)S(1)}, u32[]{:S(2)}, u32[]{:S(2)}) collective-permute-start(bf16[8,64,384]{2,1,0:T(8,128)(2,1)} %refs_0_.1), channel_id=1, source_target_pairs={{0,4},{1,5},{2,6},{3,7},{4,8},{5,9},{6,10},{7,11},{8,12},{9,13},{1... | collective-permute-start | bytes 1179656 | tf_op jit(solution)/shard_map/ppermute | solution.py:172
  15.1 42.8 %copy-start = (bf16[8,64,384]{2,1,0:T(8,128)(2,1)}, bf16[8,64,384]{2,1,0:T(8,128)(2,1)S(1)}, u32[]{:S(2)}) copy-start(bf16[8,64,384]{2,1,0:T(8,128)(2,1)S(1)} %collective-permute-done.3.refs_4_) | copy-start | bytes 1179652
  15.1 12.1 %collective-permute-start.7 = (bf16[8,64,384]{2,1,0:T(8,128)(2,1)S(1)}, bf16[8,64,384]{2,1,0:T(8,128)(2,1)S(1)}, u32[]{:S(2)}, u32[]{:S(2)}) collective-permute-start(bf16[8,64,384]{2,1,0:T(8,128)(2,1)S(1)} %collective-permute-done.3.refs_4_), channel_id=1, source_target_pairs={{0,4},{1,5},{2,6},{3,7},{4,8},{5,9},{6,10},{7,11},{8,12},{9,13},{1... | collective-permute-start | bytes 1179656 | tf_op jit(solution)/shard_map/ppermute | solution.py:172
  15.1 12.1 %collective-permute-start = (bf16[8,64,384]{2,1,0:T(8,128)(2,1)}, bf16[8,64,384]{2,1,0:T(8,128)(2,1)S(1)}, u32[]{:S(2)}, u32[]{:S(2)}) collective-permute-start(bf16[8,64,384]{2,1,0:T(8,128)(2,1)} %refs_0_.1), channel_id=1, source_target_pairs={{0,2},{1,3},{2,0},{3,1},{4,6},{5,7},{6,4},{7,5},{8,10},{9,11},{10,... | collective-permute-start | bytes 1179656 | tf_op jit(solution)/shard_map/ppermute | solution.py:175
  16.6 12.2 %collective-permute-start.1 = (bf16[8,64,384]{2,1,0:T(8,128)(2,1)}, bf16[8,64,384]{2,1,0:T(8,128)(2,1)S(1)}, u32[]{:S(2)}, u32[]{:S(2)}) collective-permute-start(bf16[8,64,384]{2,1,0:T(8,128)(2,1)} %refs_0_.1), channel_id=1, source_target_pairs={{0,1},{1,0},{2,3},{3,2},{4,5},{5,4},{6,7},{7,6},{8,9},{9,8},{10,11... | collective-permute-start | bytes 1179656 | tf_op jit(solution)/shard_map/ppermute | solution.py:175
  27.2 30.7 %copy-start.1 = (bf16[8,64,384]{2,1,0:T(8,128)(2,1)}, bf16[8,64,384]{2,1,0:T(8,128)(2,1)S(1)}, u32[]{:S(2)}) copy-start(bf16[8,64,384]{2,1,0:T(8,128)(2,1)S(1)} %collective-permute-done.7.refs_8_) | copy-start | bytes 1179652
  27.2 11.2 %collective-permute-start.11 = (bf16[8,64,384]{2,1,0:T(8,128)(2,1)S(1)}, bf16[8,64,384]{2,1,0:T(8,128)(2,1)S(1)}, u32[]{:S(2)}, u32[]{:S(2)}) collective-permute-start(bf16[8,64,384]{2,1,0:T(8,128)(2,1)S(1)} %collective-permute-done.7.refs_8_), channel_id=1, source_target_pairs={{0,4},{1,5},{2,6},{3,7},{4,8},{5,9},{6,10},{7,11},{8,12},{9,13},{1... | collective-permute-start | bytes 1179656 | tf_op jit(solution)/shard_map/ppermute | solution.py:172
  27.2 30.7 %copy-start.2 = (bf16[8,64,384]{2,1,0:T(8,128)(2,1)}, bf16[8,64,384]{2,1,0:T(8,128)(2,1)S(1)}, u32[]{:S(2)}) copy-start(bf16[8,64,384]{2,1,0:T(8,128)(2,1)S(1)} %collective-permute-done.refs_1_) | copy-start | bytes 1179652
  27.2 12.2 %collective-permute-start.2 = (bf16[8,64,384]{2,1,0:T(8,128)(2,1)S(1)}, bf16[8,64,384]{2,1,0:T(8,128)(2,1)S(1)}, u32[]{:S(2)}, u32[]{:S(2)}) collective-permute-start(bf16[8,64,384]{2,1,0:T(8,128)(2,1)S(1)} %collective-permute-done.refs_1_), channel_id=1, source_target_pairs={{0,1},{1,0},{2,3},{3,2},{4,5},{5,4},{6,7},{7,6},{8,9},{9,8},{10,11... | collective-permute-start | bytes 1179656 | tf_op jit(solution)/shard_map/ppermute | solution.py:175
  27.3 12.1 %collective-permute-start.4 = (bf16[8,64,384]{2,1,0:T(8,128)(2,1)S(1)}, bf16[8,64,384]{2,1,0:T(8,128)(2,1)S(1)}, u32[]{:S(2)}, u32[]{:S(2)}) collective-permute-start(bf16[8,64,384]{2,1,0:T(8,128)(2,1)S(1)} %collective-permute-done.3.refs_4_), channel_id=1, source_target_pairs={{0,2},{1,3},{2,0},{3,1},{4,6},{5,7},{6,4},{7,5},{8,10},{9,11},{10,... | collective-permute-start | bytes 1179656 | tf_op jit(solution)/shard_map/ppermute | solution.py:175
  28.6 11.3 %collective-permute-start.5 = (bf16[8,64,384]{2,1,0:T(8,128)(2,1)S(1)}, bf16[8,64,384]{2,1,0:T(8,128)(2,1)S(1)}, u32[]{:S(2)}, u32[]{:S(2)}) collective-permute-start(bf16[8,64,384]{2,1,0:T(8,128)(2,1)S(1)} %collective-permute-done.3.refs_4_), channel_id=1, source_target_pairs={{0,1},{1,0},{2,3},{3,2},{4,5},{5,4},{6,7},{7,6},{8,9},{9,8},{10,11... | collective-permute-start | bytes 1179656 | tf_op jit(solution)/shard_map/ppermute | solution.py:175
  28.8 29.1 %copy-start.3 = (bf16[8,64,384]{2,1,0:T(8,128)(2,1)}, bf16[8,64,384]{2,1,0:T(8,128)(2,1)S(1)}, u32[]{:S(2)}) copy-start(bf16[8,64,384]{2,1,0:T(8,128)(2,1)S(1)} %collective-permute-done.1.refs_2_) | copy-start | bytes 1179652
  28.8 18.9 %collective-permute-start.8 = (bf16[8,64,384]{2,1,0:T(8,128)(2,1)S(1)}, bf16[8,64,384]{2,1,0:T(8,128)(2,1)S(1)}, u32[]{:S(2)}, u32[]{:S(2)}) collective-permute-start(bf16[8,64,384]{2,1,0:T(8,128)(2,1)S(1)} %collective-permute-done.7.refs_8_), channel_id=1, source_target_pairs={{0,2},{1,3},{2,0},{3,1},{4,6},{5,7},{6,4},{7,5},{8,10},{9,11},{10,... | collective-permute-start | bytes 1179656 | tf_op jit(solution)/shard_map/ppermute | solution.py:175
  38.3 19.5 %copy-start.4 = (bf16[8,64,384]{2,1,0:T(8,128)(2,1)}, bf16[8,64,384]{2,1,0:T(8,128)(2,1)S(1)}, u32[]{:S(2)}) copy-start(bf16[8,64,384]{2,1,0:T(8,128)(2,1)S(1)} %collective-permute-done.11.refs_12_) | copy-start | bytes 1179652
  38.3 17.4 %collective-permute-start.12 = (bf16[8,64,384]{2,1,0:T(8,128)(2,1)S(1)}, bf16[8,64,384]{2,1,0:T(8,128)(2,1)}, u32[]{:S(2)}, u32[]{:S(2)}) collective-permute-start(bf16[8,64,384]{2,1,0:T(8,128)(2,1)S(1)} %collective-permute-done.11.refs_12_), channel_id=1, source_target_pairs={{0,2},{1,3},{2,0},{3,1},{4,6},{5,7},{6,4},{7,5},{8,10},{9,11},{10,... | collective-permute-start | bytes 1179656 | tf_op jit(solution)/shard_map/ppermute | solution.py:175
  39.4 18.5 %copy-start.5 = (bf16[8,64,384]{2,1,0:T(8,128)(2,1)}, bf16[8,64,384]{2,1,0:T(8,128)(2,1)S(1)}, u32[]{:S(2)}) copy-start(bf16[8,64,384]{2,1,0:T(8,128)(2,1)S(1)} %collective-permute-done.2.refs_3_) | copy-start | bytes 1179652
  39.4 17.0 %collective-permute-start.9 = (bf16[8,64,384]{2,1,0:T(8,128)(2,1)S(1)}, bf16[8,64,384]{2,1,0:T(8,128)(2,1)}, u32[]{:S(2)}, u32[]{:S(2)}) collective-permute-start(bf16[8,64,384]{2,1,0:T(8,128)(2,1)S(1)} %collective-permute-done.7.refs_8_), channel_id=1, source_target_pairs={{0,1},{1,0},{2,3},{3,2},{4,5},{5,4},{6,7},{7,6},{8,9},{9,8},{10,11... | collective-permute-start | bytes 1179656 | tf_op jit(solution)/shard_map/ppermute | solution.py:175
  39.4 18.5 %copy-start.6 = (bf16[8,64,384]{2,1,0:T(8,128)(2,1)}, bf16[8,64,384]{2,1,0:T(8,128)(2,1)S(1)}, u32[]{:S(2)}) copy-start(bf16[8,64,384]{2,1,0:T(8,128)(2,1)S(1)} %collective-permute-done.4.refs_5_) | copy-start | bytes 1179652
  39.4 17.0 %collective-permute-start.6 = (bf16[8,64,384]{2,1,0:T(8,128)(2,1)S(1)}, bf16[8,64,384]{2,1,0:T(8,128)(2,1)}, u32[]{:S(2)}, u32[]{:S(2)}) collective-permute-start(bf16[8,64,384]{2,1,0:T(8,128)(2,1)S(1)} %collective-permute-done.4.refs_5_), channel_id=1, source_target_pairs={{0,1},{1,0},{2,3},{3,2},{4,5},{5,4},{6,7},{7,6},{8,9},{9,8},{10,11... | collective-permute-start | bytes 1179656 | tf_op jit(solution)/shard_map/ppermute | solution.py:175
  39.9 18.0 %copy-start.7 = (bf16[8,64,384]{2,1,0:T(8,128)(2,1)}, bf16[8,64,384]{2,1,0:T(8,128)(2,1)S(1)}, u32[]{:S(2)}) copy-start(bf16[8,64,384]{2,1,0:T(8,128)(2,1)S(1)} %collective-permute-done.5.refs_6_) | copy-start | bytes 1179652
  39.9 16.5 %collective-permute-start.13 = (bf16[8,64,384]{2,1,0:T(8,128)(2,1)S(1)}, bf16[8,64,384]{2,1,0:T(8,128)(2,1)}, u32[]{:S(2)}, u32[]{:S(2)}) collective-permute-start(bf16[8,64,384]{2,1,0:T(8,128)(2,1)S(1)} %collective-permute-done.11.refs_12_), channel_id=1, source_target_pairs={{0,1},{1,0},{2,3},{3,2},{4,5},{5,4},{6,7},{7,6},{8,9},{9,8},{10,11... | collective-permute-start | bytes 1179656 | tf_op jit(solution)/shard_map/ppermute | solution.py:175
  47.7 10.2 %copy-start.8 = (bf16[8,64,384]{2,1,0:T(8,128)(2,1)}, bf16[8,64,384]{2,1,0:T(8,128)(2,1)S(1)}, u32[]{:S(2)}) copy-start(bf16[8,64,384]{2,1,0:T(8,128)(2,1)S(1)} %collective-permute-done.8.refs_9_) | copy-start | bytes 1179652
  47.7 8.7 %collective-permute-start.10 = (bf16[8,64,384]{2,1,0:T(8,128)(2,1)S(1)}, bf16[8,64,384]{2,1,0:T(8,128)(2,1)}, u32[]{:S(2)}, u32[]{:S(2)}) collective-permute-start(bf16[8,64,384]{2,1,0:T(8,128)(2,1)S(1)} %collective-permute-done.8.refs_9_), channel_id=1, source_target_pairs={{0,1},{1,0},{2,3},{3,2},{4,5},{5,4},{6,7},{7,6},{8,9},{9,8},{10,11... | collective-permute-start | bytes 1179656 | tf_op jit(solution)/shard_map/ppermute | solution.py:175
  55.8 2.1 %collective-permute-start.14 = (bf16[8,64,384]{2,1,0:T(8,128)(2,1)}, bf16[8,64,384]{2,1,0:T(8,128)(2,1)}, u32[]{:S(2)}, u32[]{:S(2)}) collective-permute-start(bf16[8,64,384]{2,1,0:T(8,128)(2,1)} %collective-permute-done.12.refs_13_), channel_id=1, source_target_pairs={{0,1},{1,0},{2,3},{3,2},{4,5},{5,4},{6,7},{7,6},{8,9},{9,8},{10,11... | collective-permute-start | bytes 1179656 | tf_op jit(solution)/shard_map/ppermute | solution.py:175
  75.6 5.3 %collective-permute-start.17 = (f32[2,8,128]{2,1,0:T(8,128)}, f32[2,8,128]{2,1,0:T(8,128)S(1)}, u32[]{:S(2)}, u32[]{:S(2)}) collective-permute-start(f32[2,8,128]{2,1,0:T(8,128)} %get-tuple-element.5), channel_id=1, source_target_pairs={{0,12},{1,13},{2,14},{3,15},{4,0},{5,1},{6,2},{7,3},{8,4},{9,5},{1... | collective-permute-start | bytes 24584 | tf_op jit(solution)/shard_map/ppermute | solution.py:172
  79.4 4.8 %collective-permute-start.16 = (f32[2,8,128]{2,1,0:T(8,128)}, f32[2,8,128]{2,1,0:T(8,128)S(1)}, u32[]{:S(2)}, u32[]{:S(2)}) collective-permute-start(f32[2,8,128]{2,1,0:T(8,128)} %get-tuple-element.5), channel_id=1, source_target_pairs={{0,8},{1,9},{2,10},{3,11},{4,12},{5,13},{6,14},{7,15},{8,0},{9,1},... | collective-permute-start | bytes 24584 | tf_op jit(solution)/shard_map/ppermute | solution.py:172
  79.4 5.7 %collective-permute-start.15 = (f32[2,8,128]{2,1,0:T(8,128)}, f32[2,8,128]{2,1,0:T(8,128)S(1)}, u32[]{:S(2)}, u32[]{:S(2)}) collective-permute-start(f32[2,8,128]{2,1,0:T(8,128)} %get-tuple-element.5), channel_id=1, source_target_pairs={{0,4},{1,5},{2,6},{3,7},{4,8},{5,9},{6,10},{7,11},{8,12},{9,13},{1... | collective-permute-start | bytes 24584 | tf_op jit(solution)/shard_map/ppermute | solution.py:172
  85.8 3.1 %collective-permute-start.20 = (f32[2,8,128]{2,1,0:T(8,128)S(1)}, f32[2,8,128]{2,1,0:T(8,128)S(1)}, u32[]{:S(2)}, u32[]{:S(2)}) collective-permute-start(f32[2,8,128]{2,1,0:T(8,128)S(1)} %add_add_fusion), channel_id=1, source_target_pairs={{0,3},{1,2},{2,1},{3,0},{4,7},{5,6},{6,5},{7,4},{8,11},{9,10},{10,... | collective-permute-start | bytes 24584 | tf_op jit(solution)/shard_map/ppermute | solution.py:175
  85.8 4.6 %collective-permute-start.19 = (f32[2,8,128]{2,1,0:T(8,128)S(1)}, f32[2,8,128]{2,1,0:T(8,128)S(1)}, u32[]{:S(2)}, u32[]{:S(2)}) collective-permute-start(f32[2,8,128]{2,1,0:T(8,128)S(1)} %add_add_fusion), channel_id=1, source_target_pairs={{0,2},{1,3},{2,0},{3,1},{4,6},{5,7},{6,4},{7,5},{8,10},{9,11},{10,... | collective-permute-start | bytes 24584 | tf_op jit(solution)/shard_map/ppermute | solution.py:175
  88.7 1.7 %collective-permute-start.18 = (f32[2,8,128]{2,1,0:T(8,128)S(1)}, f32[2,8,128]{2,1,0:T(8,128)S(1)}, u32[]{:S(2)}, u32[]{:S(2)}) collective-permute-start(f32[2,8,128]{2,1,0:T(8,128)S(1)} %add_add_fusion), channel_id=1, source_target_pairs={{0,1},{1,0},{2,3},{3,2},{4,5},{5,4},{6,7},{7,6},{8,9},{9,8},{10,11... | collective-permute-start | bytes 24584 | tf_op jit(solution)/shard_map/ppermute | solution.py:175

commit v3 on v2

--- a/solution.py
+++ b/solution.py
@@ -174,19 +174,36 @@
     def swap(x, bit):
         return lax.ppermute(x, "vir", [(d, d ^ bit) for d in range(devices)])
 
+    def after(x, *earlier):
+        return lax.optimization_barrier((x, *earlier))[0]
+
+    half = shard_tiles // 2
+    a = {(0, h): amplitudes[h * half:(h + 1) * half] for h in range(2)}
+    b = {}
+    z_done, y_done = [], []
+    last = 2 * depth - 2
+    for i in range(last + 1):
+        k, h = i // 2, i % 2
+        y_in = a[k, h]
+        if i >= 2:
+            y_in = after(y_in, y_done[i - 2])
+        b[k, h] = swap(y_in, 2)
+        y_done.append(b[k, h])
+        if i < last:
+            a[k + 1, h] = shift_z(a[k, h], 1)
+            z_done.append(a[k + 1, h])
+        else:
+            b[k, 1] = shift_z(after(b[k - 1, 1], z_done[i - 2]), 1)
     sources, dest = [], []
-    here = amplitudes
     for k in range(depth):
-        there = swap(here, 2)
-        sources += [here, there, swap(here, 1), swap(there, 1)]
         at = (z + depth - k) % depth
-        for other_y, other_core in ((0, 0), (1, 0), (0, 1), (1, 1)):
-            dest.append((at * 2 + (y ^ other_y)) * 2 + (core ^ other_core))
-        if k < depth - 1:
-            here = shift_z(here, 1)
-    dest = jnp.stack(dest) * shard_tiles
-
-    residual, stats = ladder(ij_counts, ab_irrep, dest, integrals, sources, shard_tiles, capacity)
+        for h in range(2):
+            sources += [a[k, h], b[k, h], swap(a[k, h], 1), swap(b[k, h], 1)]
+            for other_y, other_core in ((0, 0), (1, 0), (0, 1), (1, 1)):
+                dest.append((((at * 2 + (y ^ other_y)) * 2 + (core ^ other_core)) * 2 + h))
+    dest = jnp.stack(dest) * half
+
+    residual, stats = ladder(ij_counts, ab_irrep, dest, integrals, sources, half, capacity)
 
     stats = sum([shift_z(stats, by) for by in range(1, depth)], stats)
     stats = sum([swap(stats, bits) for bits in (1, 2, 3)], stats)

time: 93.4 us -> 85 us (0.910); the launches traced: 91.7 us -> 84.5 us
  waiting for transfers between devices: 54.6 us -> 34.8 us
  starting transfers between devices: 16 us -> 24 us
  Pallas kernels: 17.7 us -> 20.8 us
  local copies, waits for them, and re-layouts: 0.12 us -> 2.18 us
    ppermute x15 -> x26, waiting for transfers between devices: 18.8 us -> 8.64 us  [swap(): return lax.ppermute(x, 'vir', [(d, d ^ bit) for d in range(devices)])]
    ppermute x6 -> x10, waiting for transfers between devices: 35.8 us -> 26.1 us  [shift_z(): lax.ppermute(x, 'vir', [(d, (d + 4 * by) % devices) for d in range(device...]
    ppermute x15 -> x26, starting transfers between devices: 8.5 us -> 13.5 us  [swap(): return lax.ppermute(x, 'vir', [(d, d ^ bit) for d in range(devices)])]
    pallas_call x1, Pallas kernels: 17.7 us -> 20.8 us  [ladder(): pl.pallas_call(functools.partial(ladder_kernel, capacity, shard_tiles, le...]
    ppermute x6 -> x10, starting transfers between devices: 7.48 us -> 10.5 us  [shift_z(): lax.ppermute(x, 'vir', [(d, (d + 4 * by) % devices) for d in range(device...]
    slice x0 -> x1, local copies, waits for them, and re-layouts: none -> 1.07 us  [per_device(): a = {(0, h): amplitudes[h * half:(h + 1) * half] for h in range(2)}]
    unnamed x18 -> x54, local copies, waits for them, and re-layouts: 0.03 us -> 1 us
  transfers between devices with their start and end apart: 21 -> 36, of which waited for: 10 -> 18; matrix products, arithmetic and copies ran while one was open for 1% -> 1% of each run, Pallas kernels for 0% -> 0%
where the time goes in v3:
time: 85 us; the launch traced here: 84.5 us
  waiting for transfers between devices  34.8 us (41%)
  starting transfers between devices  24 us (28%)
  Pallas kernels  20.8 us (24%)
  local copies, waits for them, and re-layouts  2.18 us (3%)
  other arithmetic  1.84 us (2%)
  between operations  0.99 us (1%)
    ppermute x10, waiting for transfers between devices, shift_z(): lax.ppermute(x, 'vir', [(d, (d + 4 * by) % devices) for d in range(device...  26.1 us
    pallas_call x1, Pallas kernels, ladder(): pl.pallas_call(functools.partial(ladder_kernel, capacity, shard_tiles, le...  20.8 us
    ppermute x26, starting transfers between devices, swap(): return lax.ppermute(x, 'vir', [(d, d ^ bit) for d in range(devices)])  13.5 us
    ppermute x10, starting transfers between devices, shift_z(): lax.ppermute(x, 'vir', [(d, (d + 4 * by) % devices) for d in range(device...  10.5 us
    ppermute x26, waiting for transfers between devices, swap(): return lax.ppermute(x, 'vir', [(d, d ^ bit) for d in range(devices)])  8.64 us
  transfers between devices with their start and end apart: 36, of which 18 were waited for; matrix products, arithmetic and copies ran while one was open for 1% of the time, Pallas kernels for 0%

profile of v3, /device:TPU:0, one launch (start us, length us, event | category | flops | bytes accessed | tf_op | source)
XLA Modules:
  0.0 84.5 jit_solution(7141376252168778512)
XLA Ops:
  0.6 1.1 %fusion.2 = (bf16[4,64,384]{2,1,0:T(8,128)(2,1)S(1)}, bf16[4,64,384]{2,1,0:T(8,128)(2,1)S(1)}) fusion(bf16[8,64,384]{2,1,0:T(8,128)(2,1)} %param.4), kind=kLoop, calls=%fused_computation.7 | loop fusion | bytes 786432 | tf_op jit(solution)/shard_map/slice | solution.py:181
  1.7 3.1 %collective-permute-start.10 = (bf16[4,64,384]{2,1,0:T(8,128)(2,1)S(1)}, bf16[4,64,384]{2,1,0:T(8,128)(2,1)S(1)}, u32[]{:S(2)}, u32[]{:S(2)}) collective-permute-start(bf16[4,64,384]{2,1,0:T(8,128)(2,1)S(1)} %get-tuple-element.18.refs_4_), channel_id=1, source_target_pairs={{0,4},{1,5},{2,6},{3,7},{4,8},{5,9},{6,10},{7,11},{8,12},{9,13},{1... | collective-permute-start | bytes 589832 | tf_op jit(solution)/shard_map/ppermute | solution.py:172
  4.8 1.5 %collective-permute-start.3 = (bf16[4,64,384]{2,1,0:T(8,128)(2,1)S(1)}, bf16[4,64,384]{2,1,0:T(8,128)(2,1)S(1)}, u32[]{:S(2)}, u32[]{:S(2)}) collective-permute-start(bf16[4,64,384]{2,1,0:T(8,128)(2,1)S(1)} %get-tuple-element.18.refs_4_), channel_id=1, source_target_pairs={{0,2},{1,3},{2,0},{3,1},{4,6},{5,7},{6,4},{7,5},{8,10},{9,11},{10,... | collective-permute-start | bytes 589832 | tf_op jit(solution)/shard_map/ppermute | solution.py:175
  6.3 1.6 %collective-permute-start.6 = (bf16[4,64,384]{2,1,0:T(8,128)(2,1)S(1)}, bf16[4,64,384]{2,1,0:T(8,128)(2,1)S(1)}, u32[]{:S(2)}, u32[]{:S(2)}) collective-permute-start(bf16[4,64,384]{2,1,0:T(8,128)(2,1)S(1)} %get-tuple-element.19.refs_0_), channel_id=1, source_target_pairs={{0,4},{1,5},{2,6},{3,7},{4,8},{5,9},{6,10},{7,11},{8,12},{9,13},{1... | collective-permute-start | bytes 589832 | tf_op jit(solution)/shard_map/ppermute | solution.py:172
  7.9 0.5 collective-permute-start
  8.4 4.2 %collective-permute-done.10.refs_12_ = bf16[4,64,384]{2,1,0:T(8,128)(2,1)S(1)} collective-permute-done((bf16[4,64,384]{2,1,0:T(8,128)(2,1)S(1)}, bf16[4,64,384]{2,1,0:T(8,128)(2,1)S(1)}, u32[]{:S(2)}, u32[]{:S(2)}) %collective-permute-start.10) | collective-permute-done | bytes 196640 | tf_op jit(solution)/shard_map/ppermute | solution.py:172
  12.6 1.8 %collective-permute-start.11 = (bf16[4,64,384]{2,1,0:T(8,128)(2,1)S(1)}, bf16[4,64,384]{2,1,0:T(8,128)(2,1)S(1)}, u32[]{:S(2)}, u32[]{:S(2)}) collective-permute-start(bf16[4,64,384]{2,1,0:T(8,128)(2,1)S(1)} %collective-permute-done.10.refs_12_), channel_id=1, source_target_pairs={{0,2},{1,3},{2,0},{3,1},{4,6},{5,7},{6,4},{7,5},{8,10},{9,11},{10,... | collective-permute-start | bytes 589832 | tf_op jit(solution)/shard_map/ppermute | solution.py:175
  14.4 2.0 %collective-permute-done.6.refs_8_ = bf16[4,64,384]{2,1,0:T(8,128)(2,1)S(1)} collective-permute-done((bf16[4,64,384]{2,1,0:T(8,128)(2,1)S(1)}, bf16[4,64,384]{2,1,0:T(8,128)(2,1)S(1)}, u32[]{:S(2)}, u32[]{:S(2)}) %collective-permute-start.6) | collective-permute-done | bytes 196640 | tf_op jit(solution)/shard_map/ppermute | solution.py:172
  16.4 0.4 collective-permute-done.refs_1_
  16.9 1.6 %collective-permute-start.14 = (bf16[4,64,384]{2,1,0:T(8,128)(2,1)S(1)}, bf16[4,64,384]{2,1,0:T(8,128)(2,1)S(1)}, u32[]{:S(2)}, u32[]{:S(2)}) collective-permute-start(bf16[4,64,384]{2,1,0:T(8,128)(2,1)S(1)} %collective-permute-done.6.refs_8_), channel_id=1, source_target_pairs={{0,4},{1,5},{2,6},{3,7},{4,8},{5,9},{6,10},{7,11},{8,12},{9,13},{1... | collective-permute-start | bytes 589832 | tf_op jit(solution)/shard_map/ppermute | solution.py:172
  18.4 1.5 %collective-permute-start.7 = (bf16[4,64,384]{2,1,0:T(8,128)(2,1)S(1)}, bf16[4,64,384]{2,1,0:T(8,128)(2,1)S(1)}, u32[]{:S(2)}, u32[]{:S(2)}) collective-permute-start(bf16[4,64,384]{2,1,0:T(8,128)(2,1)S(1)} %collective-permute-done.6.refs_8_), channel_id=1, source_target_pairs={{0,2},{1,3},{2,0},{3,1},{4,6},{5,7},{6,4},{7,5},{8,10},{9,11},{10,... | collective-permute-start | bytes 589832 | tf_op jit(solution)/shard_map/ppermute | solution.py:175
  20.0 0.6 collective-permute-done.18.refs_20_
  20.6 0.5 collective-permute-done.11.refs_13_
  21.1 3.3 %collective-permute-done.14.refs_16_ = bf16[4,64,384]{2,1,0:T(8,128)(2,1)S(1)} collective-permute-done((bf16[4,64,384]{2,1,0:T(8,128)(2,1)S(1)}, bf16[4,64,384]{2,1,0:T(8,128)(2,1)S(1)}, u32[]{:S(2)}, u32[]{:S(2)}) %collective-permute-start.14) | collective-permute-done | bytes 196640 | tf_op jit(solution)/shard_map/ppermute | solution.py:172
  24.4 1.7 %collective-permute-start.19 = (bf16[4,64,384]{2,1,0:T(8,128)(2,1)S(1)}, bf16[4,64,384]{2,1,0:T(8,128)(2,1)S(1)}, u32[]{:S(2)}, u32[]{:S(2)}) collective-permute-start(bf16[4,64,384]{2,1,0:T(8,128)(2,1)S(1)} %collective-permute-done.18.refs_20_), channel_id=1, source_target_pairs={{0,2},{1,3},{2,0},{3,1},{4,6},{5,7},{6,4},{7,5},{8,10},{9,11},{10,... | collective-permute-start | bytes 589832 | tf_op jit(solution)/shard_map/ppermute | solution.py:175
  26.1 1.1 %collective-permute-start.22 = (bf16[4,64,384]{2,1,0:T(8,128)(2,1)S(1)}, bf16[4,64,384]{2,1,0:T(8,128)(2,1)S(1)}, u32[]{:S(2)}, u32[]{:S(2)}) collective-permute-start(bf16[4,64,384]{2,1,0:T(8,128)(2,1)S(1)} %collective-permute-done.14.refs_16_), channel_id=1, source_target_pairs={{0,4},{1,5},{2,6},{3,7},{4,8},{5,9},{6,10},{7,11},{8,12},{9,13},{1... | collective-permute-start | bytes 589832 | tf_op jit(solution)/shard_map/ppermute | solution.py:172
  27.2 0.5 collective-permute-start.15
  27.7 0.5 collective-permute-start.2
  28.2 3.9 %collective-permute-done.19.refs_21_ = bf16[4,64,384]{2,1,0:T(8,128)(2,1)S(1)} collective-permute-done((bf16[4,64,384]{2,1,0:T(8,128)(2,1)S(1)}, bf16[4,64,384]{2,1,0:T(8,128)(2,1)S(1)}, u32[]{:S(2)}, u32[]{:S(2)}) %collective-permute-start.19) | collective-permute-done | bytes 196640 | tf_op jit(solution)/shard_map/ppermute | solution.py:175
  32.2 1.0 %collective-permute-start.26 = (bf16[4,64,384]{2,1,0:T(8,128)(2,1)S(1)}, bf16[4,64,384]{2,1,0:T(8,128)(2,1)}, u32[]{:S(2)}, u32[]{:S(2)}) collective-permute-start(bf16[4,64,384]{2,1,0:T(8,128)(2,1)S(1)} %collective-permute-done.18.refs_20_), channel_id=1, source_target_pairs={{0,4},{1,5},{2,6},{3,7},{4,8},{5,9},{6,10},{7,11},{8,12},{9,13},{1... | collective-permute-start | bytes 589832 | tf_op jit(solution)/shard_map/ppermute | solution.py:172
  33.2 1.7 %collective-permute-done.22.refs_24_ = bf16[4,64,384]{2,1,0:T(8,128)(2,1)S(1)} collective-permute-done((bf16[4,64,384]{2,1,0:T(8,128)(2,1)S(1)}, bf16[4,64,384]{2,1,0:T(8,128)(2,1)S(1)}, u32[]{:S(2)}, u32[]{:S(2)}) %collective-permute-start.22) | collective-permute-done | bytes 196640 | tf_op jit(solution)/shard_map/ppermute | solution.py:172
  34.9 1.0 %collective-permute-done.15.refs_17_ = bf16[4,64,384]{2,1,0:T(8,128)(2,1)S(1)} collective-permute-done((bf16[4,64,384]{2,1,0:T(8,128)(2,1)S(1)}, bf16[4,64,384]{2,1,0:T(8,128)(2,1)S(1)}, u32[]{:S(2)}, u32[]{:S(2)}) %collective-permute-start.15) | collective-permute-done | bytes 196640 | tf_op jit(solution)/shard_map/ppermute | solution.py:175
  35.9 0.5 collective-permute-start.16
  36.5 3.5 %collective-permute-done.26.refs_28_ = bf16[4,64,384]{2,1,0:T(8,128)(2,1)} collective-permute-done((bf16[4,64,384]{2,1,0:T(8,128)(2,1)S(1)}, bf16[4,64,384]{2,1,0:T(8,128)(2,1)}, u32[]{:S(2)}, u32[]{:S(2)}) %collective-permute-start.26) | collective-permute-done | bytes 196640 | tf_op jit(solution)/shard_map/ppermute | solution.py:172
  40.2 1.7 %collective-permute-start.23 = (bf16[4,64,384]{2,1,0:T(8,128)(2,1)S(1)}, bf16[4,64,384]{2,1,0:T(8,128)(2,1)}, u32[]{:S(2)}, u32[]{:S(2)}) collective-permute-start(bf16[4,64,384]{2,1,0:T(8,128)(2,1)S(1)} %collective-permute-done.22.refs_24_), channel_id=1, source_target_pairs={{0,2},{1,3},{2,0},{3,1},{4,6},{5,7},{6,4},{7,5},{8,10},{9,11},{10,... | collective-permute-start | bytes 589832 | tf_op jit(solution)/shard_map/ppermute | solution.py:175
  41.9 0.1 stack.131
  42.0 0.2 collective-permute-start.21
  42.3 0.3 collective-permute-start.24
  42.6 0.2 collective-permute-start.17
  42.8 6.5 %collective-permute-done.27.refs_29_ = bf16[4,64,384]{2,1,0:T(8,128)(2,1)} collective-permute-done((bf16[4,64,384]{2,1,0:T(8,128)(2,1)S(1)}, bf16[4,64,384]{2,1,0:T(8,128)(2,1)}, u32[]{:S(2)}, u32[]{:S(2)}) %collective-permute-start.27) | collective-permute-done | bytes 196640 | tf_op jit(solution)/shard_map/ppermute | solution.py:172
  49.3 0.5 collective-permute-start.25
  49.8 0.5 broadcast_multiply_fusion.dest_ref
  50.4 0.6 collective-permute-done.29.refs_31_
  51.0 0.3 collective-permute-done.25.refs_27_
  51.4 0.2 copy-done.24
  51.7 0.7 copy-done.25
  52.3 20.8 %ladder.1 = (bf16[32,64,2048]{2,1,0:T(8,128)(2,1)}, f32[2,8,128]{2,1,0:T(8,128)}) custom-call(s32[8]{0:T(128)} %counts_ref.1, s32[32]{0:T(128)} %irrep_ref.1, s32[32]{0:T(128)} %broadcast_multiply_fusion.dest_ref, bf16[32,64,384]{2,1,0:T(8,128)(2,1)} %v_hbm.1, bf16[4,64,384]{2,1,0:T(8,128)(2,1)} %copy-done.1, bf16[4,64,384]{2,1,0:T(8,128)(2,1)} %copy-done.5, ...), custom_call_target="tpu_custom_call" | custom-call | tf_op jit(solution)/shard_map/ladder/pallas_call | solution.py:136
  73.3 1.9 %collective-permute-start.30 = (f32[2,8,128]{2,1,0:T(8,128)}, f32[2,8,128]{2,1,0:T(8,128)S(1)}, u32[]{:S(2)}, u32[]{:S(2)}) collective-permute-start(f32[2,8,128]{2,1,0:T(8,128)} %get-tuple-element.17), channel_id=1, source_target_pairs={{0,4},{1,5},{2,6},{3,7},{4,8},{5,9},{6,10},{7,11},{8,12},{9,13},{1... | collective-permute-start | bytes 24584 | tf_op jit(solution)/shard_map/ppermute | solution.py:172
  75.2 1.8 %collective-permute-done.32 = f32[2,8,128]{2,1,0:T(8,128)S(1)} collective-permute-done((f32[2,8,128]{2,1,0:T(8,128)}, f32[2,8,128]{2,1,0:T(8,128)S(1)}, u32[]{:S(2)}, u32[]{:S(2)}) %collective-permute-start.32) | collective-permute-done | bytes 8224 | tf_op jit(solution)/shard_map/ppermute | solution.py:172
  77.1 1.0 %collective-permute-done.31 = f32[2,8,128]{2,1,0:T(8,128)S(1)} collective-permute-done((f32[2,8,128]{2,1,0:T(8,128)}, f32[2,8,128]{2,1,0:T(8,128)S(1)}, u32[]{:S(2)}, u32[]{:S(2)}) %collective-permute-start.31) | collective-permute-done | bytes 8224 | tf_op jit(solution)/shard_map/ppermute | solution.py:172
  78.0 1.5 %collective-permute-done.30 = f32[2,8,128]{2,1,0:T(8,128)S(1)} collective-permute-done((f32[2,8,128]{2,1,0:T(8,128)}, f32[2,8,128]{2,1,0:T(8,128)S(1)}, u32[]{:S(2)}, u32[]{:S(2)}) %collective-permute-start.30) | collective-permute-done | bytes 8224 | tf_op jit(solution)/shard_map/ppermute | solution.py:172
  79.5 0.7 add_add_fusion
  80.2 0.7 collective-permute-start.34
  80.9 1.1 %collective-permute-start.33 = (f32[2,8,128]{2,1,0:T(8,128)S(1)}, f32[2,8,128]{2,1,0:T(8,128)S(1)}, u32[]{:S(2)}, u32[]{:S(2)}) collective-permute-start(f32[2,8,128]{2,1,0:T(8,128)S(1)} %add_add_fusion), channel_id=1, source_target_pairs={{0,1},{1,0},{2,3},{3,2},{4,5},{5,4},{6,7},{7,6},{8,9},{9,8},{10,11... | collective-permute-start | bytes 24584 | tf_op jit(solution)/shard_map/ppermute | solution.py:175
  82.1 1.2 %collective-permute-done.35 = f32[2,8,128]{2,1,0:T(8,128)S(1)} collective-permute-done((f32[2,8,128]{2,1,0:T(8,128)S(1)}, f32[2,8,128]{2,1,0:T(8,128)S(1)}, u32[]{:S(2)}, u32[]{:S(2)}) %collective-permute-start.35) | collective-permute-done | bytes 8224 | tf_op jit(solution)/shard_map/ppermute | solution.py:175
  83.3 0.6 collective-permute-done.34
  83.9 0.1 add_reduce_fusion
  84.0 0.5 add_sqrt_fusion
  (85 shorter events, 0.5 us)
Async XLA Ops:
  0.6 83.4 %copy-start.26 = (s32[8]{0:T(128)S(1)}, s32[8]{0:T(128)}, u32[]{:S(2)}) copy-start(s32[8]{0:T(128)} %counts_ref.1) | copy-start | bytes 100
  1.7 49.5 %copy-start = (bf16[4,64,384]{2,1,0:T(8,128)(2,1)}, bf16[4,64,384]{2,1,0:T(8,128)(2,1)S(1)}, u32[]{:S(2)}) copy-start(bf16[4,64,384]{2,1,0:T(8,128)(2,1)S(1)} %get-tuple-element.18.refs_4_) | copy-start | bytes 589828
  1.7 49.5 %copy-start.1 = (bf16[4,64,384]{2,1,0:T(8,128)(2,1)}, bf16[4,64,384]{2,1,0:T(8,128)(2,1)S(1)}, u32[]{:S(2)}) copy-start(bf16[4,64,384]{2,1,0:T(8,128)(2,1)S(1)} %get-tuple-element.19.refs_0_) | copy-start | bytes 589828
  1.7 10.8 %collective-permute-start.10 = (bf16[4,64,384]{2,1,0:T(8,128)(2,1)S(1)}, bf16[4,64,384]{2,1,0:T(8,128)(2,1)S(1)}, u32[]{:S(2)}, u32[]{:S(2)}) collective-permute-start(bf16[4,64,384]{2,1,0:T(8,128)(2,1)S(1)} %get-tuple-element.18.refs_4_), channel_id=1, source_target_pairs={{0,4},{1,5},{2,6},{3,7},{4,8},{5,9},{6,10},{7,11},{8,12},{9,13},{1... | collective-permute-start | bytes 589832 | tf_op jit(solution)/shard_map/ppermute | solution.py:172
  4.8 7.8 %collective-permute-start.3 = (bf16[4,64,384]{2,1,0:T(8,128)(2,1)S(1)}, bf16[4,64,384]{2,1,0:T(8,128)(2,1)S(1)}, u32[]{:S(2)}, u32[]{:S(2)}) collective-permute-start(bf16[4,64,384]{2,1,0:T(8,128)(2,1)S(1)} %get-tuple-element.18.refs_4_), channel_id=1, source_target_pairs={{0,2},{1,3},{2,0},{3,1},{4,6},{5,7},{6,4},{7,5},{8,10},{9,11},{10,... | collective-permute-start | bytes 589832 | tf_op jit(solution)/shard_map/ppermute | solution.py:175
  6.3 10.1 %collective-permute-start.6 = (bf16[4,64,384]{2,1,0:T(8,128)(2,1)S(1)}, bf16[4,64,384]{2,1,0:T(8,128)(2,1)S(1)}, u32[]{:S(2)}, u32[]{:S(2)}) collective-permute-start(bf16[4,64,384]{2,1,0:T(8,128)(2,1)S(1)} %get-tuple-element.19.refs_0_), channel_id=1, source_target_pairs={{0,4},{1,5},{2,6},{3,7},{4,8},{5,9},{6,10},{7,11},{8,12},{9,13},{1... | collective-permute-start | bytes 589832 | tf_op jit(solution)/shard_map/ppermute | solution.py:172
  7.9 8.9 %collective-permute-start = (bf16[4,64,384]{2,1,0:T(8,128)(2,1)S(1)}, bf16[4,64,384]{2,1,0:T(8,128)(2,1)S(1)}, u32[]{:S(2)}, u32[]{:S(2)}) collective-permute-start(bf16[4,64,384]{2,1,0:T(8,128)(2,1)S(1)} %get-tuple-element.19.refs_0_), channel_id=1, source_target_pairs={{0,2},{1,3},{2,0},{3,1},{4,6},{5,7},{6,4},{7,5},{8,10},{9,11},{10,... | collective-permute-start | bytes 589832 | tf_op jit(solution)/shard_map/ppermute | solution.py:175
  12.6 38.7 %copy-start.2 = (bf16[4,64,384]{2,1,0:T(8,128)(2,1)}, bf16[4,64,384]{2,1,0:T(8,128)(2,1)S(1)}, u32[]{:S(2)}) copy-start(bf16[4,64,384]{2,1,0:T(8,128)(2,1)S(1)} %collective-permute-done.10.refs_12_) | copy-start | bytes 589828
  12.6 8.0 %collective-permute-start.18 = (bf16[4,64,384]{2,1,0:T(8,128)(2,1)S(1)}, bf16[4,64,384]{2,1,0:T(8,128)(2,1)S(1)}, u32[]{:S(2)}, u32[]{:S(2)}) collective-permute-start(bf16[4,64,384]{2,1,0:T(8,128)(2,1)S(1)} %collective-permute-done.10.refs_12_), channel_id=1, source_target_pairs={{0,4},{1,5},{2,6},{3,7},{4,8},{5,9},{6,10},{7,11},{8,12},{9,13},{1... | collective-permute-start | bytes 589832 | tf_op jit(solution)/shard_map/ppermute | solution.py:172
  12.6 38.6 %copy-start.3 = (bf16[4,64,384]{2,1,0:T(8,128)(2,1)}, bf16[4,64,384]{2,1,0:T(8,128)(2,1)S(1)}, u32[]{:S(2)}) copy-start(bf16[4,64,384]{2,1,0:T(8,128)(2,1)S(1)} %collective-permute-done.3.refs_5_) | copy-start | bytes 589828
  12.6 8.4 %collective-permute-start.11 = (bf16[4,64,384]{2,1,0:T(8,128)(2,1)S(1)}, bf16[4,64,384]{2,1,0:T(8,128)(2,1)S(1)}, u32[]{:S(2)}, u32[]{:S(2)}) collective-permute-start(bf16[4,64,384]{2,1,0:T(8,128)(2,1)S(1)} %collective-permute-done.10.refs_12_), channel_id=1, source_target_pairs={{0,2},{1,3},{2,0},{3,1},{4,6},{5,7},{6,4},{7,5},{8,10},{9,11},{10,... | collective-permute-start | bytes 589832 | tf_op jit(solution)/shard_map/ppermute | solution.py:175
  16.4 34.9 %copy-start.4 = (bf16[4,64,384]{2,1,0:T(8,128)(2,1)}, bf16[4,64,384]{2,1,0:T(8,128)(2,1)S(1)}, u32[]{:S(2)}) copy-start(bf16[4,64,384]{2,1,0:T(8,128)(2,1)S(1)} %collective-permute-done.6.refs_8_) | copy-start | bytes 589828
  16.8 34.4 %copy-start.5 = (bf16[4,64,384]{2,1,0:T(8,128)(2,1)}, bf16[4,64,384]{2,1,0:T(8,128)(2,1)S(1)}, u32[]{:S(2)}) copy-start(bf16[4,64,384]{2,1,0:T(8,128)(2,1)S(1)} %collective-permute-done.refs_1_) | copy-start | bytes 589828
  16.9 7.5 %collective-permute-start.14 = (bf16[4,64,384]{2,1,0:T(8,128)(2,1)S(1)}, bf16[4,64,384]{2,1,0:T(8,128)(2,1)S(1)}, u32[]{:S(2)}, u32[]{:S(2)}) collective-permute-start(bf16[4,64,384]{2,1,0:T(8,128)(2,1)S(1)} %collective-permute-done.6.refs_8_), channel_id=1, source_target_pairs={{0,4},{1,5},{2,6},{3,7},{4,8},{5,9},{6,10},{7,11},{8,12},{9,13},{1... | collective-permute-start | bytes 589832 | tf_op jit(solution)/shard_map/ppermute | solution.py:172
  18.4 6.0 %collective-permute-start.7 = (bf16[4,64,384]{2,1,0:T(8,128)(2,1)S(1)}, bf16[4,64,384]{2,1,0:T(8,128)(2,1)S(1)}, u32[]{:S(2)}, u32[]{:S(2)}) collective-permute-start(bf16[4,64,384]{2,1,0:T(8,128)(2,1)S(1)} %collective-permute-done.6.refs_8_), channel_id=1, source_target_pairs={{0,2},{1,3},{2,0},{3,1},{4,6},{5,7},{6,4},{7,5},{8,10},{9,11},{10,... | collective-permute-start | bytes 589832 | tf_op jit(solution)/shard_map/ppermute | solution.py:175
  19.9 6.2 %collective-permute-start.4 = (bf16[4,64,384]{2,1,0:T(8,128)(2,1)S(1)}, bf16[4,64,384]{2,1,0:T(8,128)(2,1)S(1)}, u32[]{:S(2)}, u32[]{:S(2)}) collective-permute-start(bf16[4,64,384]{2,1,0:T(8,128)(2,1)S(1)} %get-tuple-element.18.refs_4_), channel_id=1, source_target_pairs={{0,1},{1,0},{2,3},{3,2},{4,5},{5,4},{6,7},{7,6},{8,9},{9,8},{10,11... | collective-permute-start | bytes 589832 | tf_op jit(solution)/shard_map/ppermute | solution.py:175
  20.6 30.7 %copy-start.6 = (bf16[4,64,384]{2,1,0:T(8,128)(2,1)}, bf16[4,64,384]{2,1,0:T(8,128)(2,1)S(1)}, u32[]{:S(2)}) copy-start(bf16[4,64,384]{2,1,0:T(8,128)(2,1)S(1)} %collective-permute-done.18.refs_20_) | copy-start | bytes 589828
  20.6 6.6 %collective-permute-start.1 = (bf16[4,64,384]{2,1,0:T(8,128)(2,1)S(1)}, bf16[4,64,384]{2,1,0:T(8,128)(2,1)S(1)}, u32[]{:S(2)}, u32[]{:S(2)}) collective-permute-start(bf16[4,64,384]{2,1,0:T(8,128)(2,1)S(1)} %get-tuple-element.19.refs_0_), channel_id=1, source_target_pairs={{0,1},{1,0},{2,3},{3,2},{4,5},{5,4},{6,7},{7,6},{8,9},{9,8},{10,11... | collective-permute-start | bytes 589832 | tf_op jit(solution)/shard_map/ppermute | solution.py:175
  21.1 30.2 %copy-start.7 = (bf16[4,64,384]{2,1,0:T(8,128)(2,1)}, bf16[4,64,384]{2,1,0:T(8,128)(2,1)S(1)}, u32[]{:S(2)}) copy-start(bf16[4,64,384]{2,1,0:T(8,128)(2,1)S(1)} %collective-permute-done.11.refs_13_) | copy-start | bytes 589828
  21.1 6.7 %collective-permute-start.12 = (bf16[4,64,384]{2,1,0:T(8,128)(2,1)S(1)}, bf16[4,64,384]{2,1,0:T(8,128)(2,1)S(1)}, u32[]{:S(2)}, u32[]{:S(2)}) collective-permute-start(bf16[4,64,384]{2,1,0:T(8,128)(2,1)S(1)} %collective-permute-done.10.refs_12_), channel_id=1, source_target_pairs={{0,1},{1,0},{2,3},{3,2},{4,5},{5,4},{6,7},{7,6},{8,9},{9,8},{10,11... | collective-permute-start | bytes 589832 | tf_op jit(solution)/shard_map/ppermute | solution.py:175
  24.4 26.9 %copy-start.8 = (bf16[4,64,384]{2,1,0:T(8,128)(2,1)}, bf16[4,64,384]{2,1,0:T(8,128)(2,1)S(1)}, u32[]{:S(2)}) copy-start(bf16[4,64,384]{2,1,0:T(8,128)(2,1)S(1)} %collective-permute-done.14.refs_16_) | copy-start | bytes 589828
  24.4 3.4 %collective-permute-start.5 = (bf16[4,64,384]{2,1,0:T(8,128)(2,1)S(1)}, bf16[4,64,384]{2,1,0:T(8,128)(2,1)S(1)}, u32[]{:S(2)}, u32[]{:S(2)}) collective-permute-start(bf16[4,64,384]{2,1,0:T(8,128)(2,1)S(1)} %collective-permute-done.3.refs_5_), channel_id=1, source_target_pairs={{0,1},{1,0},{2,3},{3,2},{4,5},{5,4},{6,7},{7,6},{8,9},{9,8},{10,11... | collective-permute-start | bytes 589832 | tf_op jit(solution)/shard_map/ppermute | solution.py:175
  24.4 26.9 %copy-start.9 = (bf16[4,64,384]{2,1,0:T(8,128)(2,1)}, bf16[4,64,384]{2,1,0:T(8,128)(2,1)S(1)}, u32[]{:S(2)}) copy-start(bf16[4,64,384]{2,1,0:T(8,128)(2,1)S(1)} %collective-permute-done.7.refs_9_) | copy-start | bytes 589828
  24.4 7.8 %collective-permute-start.19 = (bf16[4,64,384]{2,1,0:T(8,128)(2,1)S(1)}, bf16[4,64,384]{2,1,0:T(8,128)(2,1)S(1)}, u32[]{:S(2)}, u32[]{:S(2)}) collective-permute-start(bf16[4,64,384]{2,1,0:T(8,128)(2,1)S(1)} %collective-permute-done.18.refs_20_), channel_id=1, source_target_pairs={{0,2},{1,3},{2,0},{3,1},{4,6},{5,7},{6,4},{7,5},{8,10},{9,11},{10,... | collective-permute-start | bytes 589832 | tf_op jit(solution)/shard_map/ppermute | solution.py:175
  26.1 25.2 %copy-start.10 = (bf16[4,64,384]{2,1,0:T(8,128)(2,1)}, bf16[4,64,384]{2,1,0:T(8,128)(2,1)S(1)}, u32[]{:S(2)}) copy-start(bf16[4,64,384]{2,1,0:T(8,128)(2,1)S(1)} %collective-permute-done.4.refs_6_) | copy-start | bytes 589828
  26.1 8.8 %collective-permute-start.22 = (bf16[4,64,384]{2,1,0:T(8,128)(2,1)S(1)}, bf16[4,64,384]{2,1,0:T(8,128)(2,1)S(1)}, u32[]{:S(2)}, u32[]{:S(2)}) collective-permute-start(bf16[4,64,384]{2,1,0:T(8,128)(2,1)S(1)} %collective-permute-done.14.refs_16_), channel_id=1, source_target_pairs={{0,4},{1,5},{2,6},{3,7},{4,8},{5,9},{6,10},{7,11},{8,12},{9,13},{1... | collective-permute-start | bytes 589832 | tf_op jit(solution)/shard_map/ppermute | solution.py:172
  27.2 8.7 %collective-permute-start.15 = (bf16[4,64,384]{2,1,0:T(8,128)(2,1)S(1)}, bf16[4,64,384]{2,1,0:T(8,128)(2,1)S(1)}, u32[]{:S(2)}, u32[]{:S(2)}) collective-permute-start(bf16[4,64,384]{2,1,0:T(8,128)(2,1)S(1)} %collective-permute-done.14.refs_16_), channel_id=1, source_target_pairs={{0,2},{1,3},{2,0},{3,1},{4,6},{5,7},{6,4},{7,5},{8,10},{9,11},{10,... | collective-permute-start | bytes 589832 | tf_op jit(solution)/shard_map/ppermute | solution.py:175
  27.7 8.2 %collective-permute-start.8 = (bf16[4,64,384]{2,1,0:T(8,128)(2,1)S(1)}, bf16[4,64,384]{2,1,0:T(8,128)(2,1)S(1)}, u32[]{:S(2)}, u32[]{:S(2)}) collective-permute-start(bf16[4,64,384]{2,1,0:T(8,128)(2,1)S(1)} %collective-permute-done.6.refs_8_), channel_id=1, source_target_pairs={{0,1},{1,0},{2,3},{3,2},{4,5},{5,4},{6,7},{7,6},{8,9},{9,8},{10,11... | collective-permute-start | bytes 589832 | tf_op jit(solution)/shard_map/ppermute | solution.py:175
  27.7 8.7 %collective-permute-start.2 = (bf16[4,64,384]{2,1,0:T(8,128)(2,1)S(1)}, bf16[4,64,384]{2,1,0:T(8,128)(2,1)S(1)}, u32[]{:S(2)}, u32[]{:S(2)}) collective-permute-start(bf16[4,64,384]{2,1,0:T(8,128)(2,1)S(1)} %collective-permute-done.refs_1_), channel_id=1, source_target_pairs={{0,1},{1,0},{2,3},{3,2},{4,5},{5,4},{6,7},{7,6},{8,9},{9,8},{10,11... | collective-permute-start | bytes 589832 | tf_op jit(solution)/shard_map/ppermute | solution.py:175
  32.2 7.9 %collective-permute-start.26 = (bf16[4,64,384]{2,1,0:T(8,128)(2,1)S(1)}, bf16[4,64,384]{2,1,0:T(8,128)(2,1)}, u32[]{:S(2)}, u32[]{:S(2)}) collective-permute-start(bf16[4,64,384]{2,1,0:T(8,128)(2,1)S(1)} %collective-permute-done.18.refs_20_), channel_id=1, source_target_pairs={{0,4},{1,5},{2,6},{3,7},{4,8},{5,9},{6,10},{7,11},{8,12},{9,13},{1... | collective-permute-start | bytes 589832 | tf_op jit(solution)/shard_map/ppermute | solution.py:172
  34.9 5.2 %collective-permute-start.20 = (bf16[4,64,384]{2,1,0:T(8,128)(2,1)S(1)}, bf16[4,64,384]{2,1,0:T(8,128)(2,1)S(1)}, u32[]{:S(2)}, u32[]{:S(2)}) collective-permute-start(bf16[4,64,384]{2,1,0:T(8,128)(2,1)S(1)} %collective-permute-done.18.refs_20_), channel_id=1, source_target_pairs={{0,1},{1,0},{2,3},{3,2},{4,5},{5,4},{6,7},{7,6},{8,9},{9,8},{10,11... | collective-permute-start | bytes 589832 | tf_op jit(solution)/shard_map/ppermute | solution.py:175
  35.9 4.2 %collective-permute-start.13 = (bf16[4,64,384]{2,1,0:T(8,128)(2,1)S(1)}, bf16[4,64,384]{2,1,0:T(8,128)(2,1)S(1)}, u32[]{:S(2)}, u32[]{:S(2)}) collective-permute-start(bf16[4,64,384]{2,1,0:T(8,128)(2,1)S(1)} %collective-permute-done.11.refs_13_), channel_id=1, source_target_pairs={{0,1},{1,0},{2,3},{3,2},{4,5},{5,4},{6,7},{7,6},{8,9},{9,8},{10,11... | collective-permute-start | bytes 589832 | tf_op jit(solution)/shard_map/ppermute | solution.py:175
  35.9 6.1 %collective-permute-start.16 = (bf16[4,64,384]{2,1,0:T(8,128)(2,1)S(1)}, bf16[4,64,384]{2,1,0:T(8,128)(2,1)}, u32[]{:S(2)}, u32[]{:S(2)}) collective-permute-start(bf16[4,64,384]{2,1,0:T(8,128)(2,1)S(1)} %collective-permute-done.14.refs_16_), channel_id=1, source_target_pairs={{0,1},{1,0},{2,3},{3,2},{4,5},{5,4},{6,7},{7,6},{8,9},{9,8},{10,11... | collective-permute-start | bytes 589832 | tf_op jit(solution)/shard_map/ppermute | solution.py:175
  36.5 5.8 %collective-permute-start.9 = (bf16[4,64,384]{2,1,0:T(8,128)(2,1)S(1)}, bf16[4,64,384]{2,1,0:T(8,128)(2,1)}, u32[]{:S(2)}, u32[]{:S(2)}) collective-permute-start(bf16[4,64,384]{2,1,0:T(8,128)(2,1)S(1)} %collective-permute-done.7.refs_9_), channel_id=1, source_target_pairs={{0,1},{1,0},{2,3},{3,2},{4,5},{5,4},{6,7},{7,6},{8,9},{9,8},{10,11... | collective-permute-start | bytes 589832 | tf_op jit(solution)/shard_map/ppermute | solution.py:175
  40.1 2.5 %collective-permute-start.28 = (bf16[4,64,384]{2,1,0:T(8,128)(2,1)}, bf16[4,64,384]{2,1,0:T(8,128)(2,1)}, u32[]{:S(2)}, u32[]{:S(2)}) collective-permute-start(bf16[4,64,384]{2,1,0:T(8,128)(2,1)} %collective-permute-done.26.refs_28_), channel_id=1, source_target_pairs={{0,1},{1,0},{2,3},{3,2},{4,5},{5,4},{6,7},{7,6},{8,9},{9,8},{10,11... | collective-permute-start | bytes 589832 | tf_op jit(solution)/shard_map/ppermute | solution.py:175
  40.1 9.2 %collective-permute-start.27 = (bf16[4,64,384]{2,1,0:T(8,128)(2,1)S(1)}, bf16[4,64,384]{2,1,0:T(8,128)(2,1)}, u32[]{:S(2)}, u32[]{:S(2)}) collective-permute-start(bf16[4,64,384]{2,1,0:T(8,128)(2,1)S(1)} %collective-permute-done.19.refs_21_), channel_id=1, source_target_pairs={{0,4},{1,5},{2,6},{3,7},{4,8},{5,9},{6,10},{7,11},{8,12},{9,13},{1... | collective-permute-start | bytes 589832 | tf_op jit(solution)/shard_map/ppermute | solution.py:172
  40.2 9.1 %collective-permute-start.23 = (bf16[4,64,384]{2,1,0:T(8,128)(2,1)S(1)}, bf16[4,64,384]{2,1,0:T(8,128)(2,1)}, u32[]{:S(2)}, u32[]{:S(2)}) collective-permute-start(bf16[4,64,384]{2,1,0:T(8,128)(2,1)S(1)} %collective-permute-done.22.refs_24_), channel_id=1, source_target_pairs={{0,2},{1,3},{2,0},{3,1},{4,6},{5,7},{6,4},{7,5},{8,10},{9,11},{10,... | collective-permute-start | bytes 589832 | tf_op jit(solution)/shard_map/ppermute | solution.py:175
  42.0 8.3 %collective-permute-start.21 = (bf16[4,64,384]{2,1,0:T(8,128)(2,1)S(1)}, bf16[4,64,384]{2,1,0:T(8,128)(2,1)S(1)}, u32[]{:S(2)}, u32[]{:S(2)}) collective-permute-start(bf16[4,64,384]{2,1,0:T(8,128)(2,1)S(1)} %collective-permute-done.19.refs_21_), channel_id=1, source_target_pairs={{0,1},{1,0},{2,3},{3,2},{4,5},{5,4},{6,7},{7,6},{8,9},{9,8},{10,11... | collective-permute-start | bytes 589832 | tf_op jit(solution)/shard_map/ppermute | solution.py:175
  42.3 8.1 %collective-permute-start.24 = (bf16[4,64,384]{2,1,0:T(8,128)(2,1)S(1)}, bf16[4,64,384]{2,1,0:T(8,128)(2,1)S(1)}, u32[]{:S(2)}, u32[]{:S(2)}) collective-permute-start(bf16[4,64,384]{2,1,0:T(8,128)(2,1)S(1)} %collective-permute-done.22.refs_24_), channel_id=1, source_target_pairs={{0,1},{1,0},{2,3},{3,2},{4,5},{5,4},{6,7},{7,6},{8,9},{9,8},{10,11... | collective-permute-start | bytes 589832 | tf_op jit(solution)/shard_map/ppermute | solution.py:175
  42.6 7.8 %collective-permute-start.17 = (bf16[4,64,384]{2,1,0:T(8,128)(2,1)S(1)}, bf16[4,64,384]{2,1,0:T(8,128)(2,1)S(1)}, u32[]{:S(2)}, u32[]{:S(2)}) collective-permute-start(bf16[4,64,384]{2,1,0:T(8,128)(2,1)S(1)} %collective-permute-done.15.refs_17_), channel_id=1, source_target_pairs={{0,1},{1,0},{2,3},{3,2},{4,5},{5,4},{6,7},{7,6},{8,9},{9,8},{10,11... | collective-permute-start | bytes 589832 | tf_op jit(solution)/shard_map/ppermute | solution.py:175
  49.3 1.7 %collective-permute-start.29 = (bf16[4,64,384]{2,1,0:T(8,128)(2,1)}, bf16[4,64,384]{2,1,0:T(8,128)(2,1)S(1)}, u32[]{:S(2)}, u32[]{:S(2)}) collective-permute-start(bf16[4,64,384]{2,1,0:T(8,128)(2,1)} %collective-permute-done.27.refs_29_), channel_id=1, source_target_pairs={{0,1},{1,0},{2,3},{3,2},{4,5},{5,4},{6,7},{7,6},{8,9},{9,8},{10,11... | collective-permute-start | bytes 589832 | tf_op jit(solution)/shard_map/ppermute | solution.py:175
  49.3 1.9 %collective-permute-start.25 = (bf16[4,64,384]{2,1,0:T(8,128)(2,1)}, bf16[4,64,384]{2,1,0:T(8,128)(2,1)S(1)}, u32[]{:S(2)}, u32[]{:S(2)}) collective-permute-start(bf16[4,64,384]{2,1,0:T(8,128)(2,1)} %collective-permute-done.23.refs_25_), channel_id=1, source_target_pairs={{0,1},{1,0},{2,3},{3,2},{4,5},{5,4},{6,7},{7,6},{8,9},{9,8},{10,11... | collective-permute-start | bytes 589832 | tf_op jit(solution)/shard_map/ppermute | solution.py:175
  73.2 3.9 %collective-permute-start.32 = (f32[2,8,128]{2,1,0:T(8,128)}, f32[2,8,128]{2,1,0:T(8,128)S(1)}, u32[]{:S(2)}, u32[]{:S(2)}) collective-permute-start(f32[2,8,128]{2,1,0:T(8,128)} %get-tuple-element.17), channel_id=1, source_target_pairs={{0,12},{1,13},{2,14},{3,15},{4,0},{5,1},{6,2},{7,3},{8,4},{9,5},{1... | collective-permute-start | bytes 24584 | tf_op jit(solution)/shard_map/ppermute | solution.py:172
  73.2 4.8 %collective-permute-start.31 = (f32[2,8,128]{2,1,0:T(8,128)}, f32[2,8,128]{2,1,0:T(8,128)S(1)}, u32[]{:S(2)}, u32[]{:S(2)}) collective-permute-start(f32[2,8,128]{2,1,0:T(8,128)} %get-tuple-element.17), channel_id=1, source_target_pairs={{0,8},{1,9},{2,10},{3,11},{4,12},{5,13},{6,14},{7,15},{8,0},{9,1},... | collective-permute-start | bytes 24584 | tf_op jit(solution)/shard_map/ppermute | solution.py:172
  73.3 6.2 %collective-permute-start.30 = (f32[2,8,128]{2,1,0:T(8,128)}, f32[2,8,128]{2,1,0:T(8,128)S(1)}, u32[]{:S(2)}, u32[]{:S(2)}) collective-permute-start(f32[2,8,128]{2,1,0:T(8,128)} %get-tuple-element.17), channel_id=1, source_target_pairs={{0,4},{1,5},{2,6},{3,7},{4,8},{5,9},{6,10},{7,11},{8,12},{9,13},{1... | collective-permute-start | bytes 24584 | tf_op jit(solution)/shard_map/ppermute | solution.py:172
  80.2 3.1 %collective-permute-start.35 = (f32[2,8,128]{2,1,0:T(8,128)S(1)}, f32[2,8,128]{2,1,0:T(8,128)S(1)}, u32[]{:S(2)}, u32[]{:S(2)}) collective-permute-start(f32[2,8,128]{2,1,0:T(8,128)S(1)} %add_add_fusion), channel_id=1, source_target_pairs={{0,3},{1,2},{2,1},{3,0},{4,7},{5,6},{6,5},{7,4},{8,11},{9,10},{10,... | collective-permute-start | bytes 24584 | tf_op jit(solution)/shard_map/ppermute | solution.py:175
  80.2 3.7 %collective-permute-start.34 = (f32[2,8,128]{2,1,0:T(8,128)S(1)}, f32[2,8,128]{2,1,0:T(8,128)S(1)}, u32[]{:S(2)}, u32[]{:S(2)}) collective-permute-start(f32[2,8,128]{2,1,0:T(8,128)S(1)} %add_add_fusion), channel_id=1, source_target_pairs={{0,2},{1,3},{2,0},{3,1},{4,6},{5,7},{6,4},{7,5},{8,10},{9,11},{10,... | collective-permute-start | bytes 24584 | tf_op jit(solution)/shard_map/ppermute | solution.py:175
  80.9 3.0 %collective-permute-start.33 = (f32[2,8,128]{2,1,0:T(8,128)S(1)}, f32[2,8,128]{2,1,0:T(8,128)S(1)}, u32[]{:S(2)}, u32[]{:S(2)}) collective-permute-start(f32[2,8,128]{2,1,0:T(8,128)S(1)} %add_add_fusion), channel_id=1, source_target_pairs={{0,1},{1,0},{2,3},{3,2},{4,5},{5,4},{6,7},{7,6},{8,9},{9,8},{10,11... | collective-permute-start | bytes 24584 | tf_op jit(solution)/shard_map/ppermute | solution.py:175
  (15 other events, 149.8 us)

commit v4 on v2

v4 whole, which is shorter than its diff:
```python
import functools

import jax
import jax.numpy as jnp
from jax import lax
from jax.experimental import pallas as pl
from jax.experimental.pallas import tpu as pltpu
from jax.sharding import PartitionSpec as P

BATCH = 4
EDGE = BATCH - 1


def prepare_kernel(
    counts_ref, irrep_ref, v_ref, sorted_ref, order_ref, size_ref, first_ref, offset_ref,
    stats_ref, next_ref, sem,
):
    own_tiles = v_ref.shape[0]
    irreps = counts_ref.shape[0]
    for s in range(irreps):
        size_ref[s] = 0

    def count(l, carry):
        s = irrep_ref[l]
        size_ref[s] = size_ref[s] + 1
        return carry

    lax.fori_loop(0, own_tiles, count, 0)
    first, offset = jnp.int32(0), jnp.int32(0)
    for s in range(irreps):
        first_ref[s] = first
        next_ref[s] = first
        offset_ref[s] = offset
        first = first + size_ref[s]
        offset = offset + counts_ref[s]

    def place(l, carry):
        s = irrep_ref[l]
        slot = next_ref[s]
        next_ref[s] = slot + 1
        order_ref[slot] = l
        pltpu.make_async_copy(v_ref.at[l], sorted_ref.at[slot], sem).start()
        return carry

    lax.fori_loop(0, own_tiles, place, 0)
    shape = stats_ref.shape[1:]
    at_row = lax.broadcasted_iota(jnp.int32, shape, 0)
    at_lane = lax.broadcasted_iota(jnp.int32, shape, 1)
    sizes = jnp.zeros(shape, jnp.int32)
    for s in range(irreps):
        sizes = jnp.where((at_row == s) & (at_lane == 0), size_ref[s], sizes)
    stats_ref[0] = jnp.zeros(shape, jnp.float32)
    stats_ref[1] = sizes.astype(jnp.float32)
    pltpu.make_async_copy(v_ref, sorted_ref.at[pl.ds(0, own_tiles)], sem).wait()


def prepare(counts, irrep, integrals):
    own_tiles, rows, width = integrals.shape
    irreps = counts.shape[0]
    smem = pl.BlockSpec(memory_space=pltpu.SMEM)
    anywhere = pl.BlockSpec(memory_space=pl.ANY)
    return pl.pallas_call(
        prepare_kernel,
        out_shape=(
            jax.ShapeDtypeStruct((own_tiles + BATCH, rows, width), integrals.dtype),
            jax.ShapeDtypeStruct((own_tiles,), jnp.int32),
            jax.ShapeDtypeStruct((irreps,), jnp.int32),
            jax.ShapeDtypeStruct((irreps,), jnp.int32),
            jax.ShapeDtypeStruct((irreps,), jnp.int32),
            jax.ShapeDtypeStruct((2, irreps, 128), jnp.float32),
        ),
        in_specs=[smem, smem, anywhere],
        out_specs=(anywhere, smem, smem, smem, smem, pl.BlockSpec(memory_space=pltpu.VMEM)),
        scratch_shapes=[pltpu.SMEM((irreps,), jnp.int32), pltpu.SemaphoreType.DMA],
        name="prepare",
    )(counts, irrep, integrals)


def ladder_kernel(
    step, depth, shard_tiles, layout, n_above, n_below,
    me_ref, counts_ref, order_ref, size_ref, first_ref, offset_ref,
    stats_in_ref, v_hbm, res_in_ref, *refs,
):
    del res_in_ref
    fresh, refs = refs[:len(layout)], refs[len(layout):]
    above, refs = refs[:n_above], refs[n_above:]
    below, refs = refs[:n_below], refs[n_below:]
    res_hbm, stats_ref, a_buf, v_buf, o_buf, acc_ref, a_sem, v_sem, o_sem = refs
    own_tiles = order_ref.shape[0]
    irreps = counts_ref.shape[0]
    rows, width = a_buf.shape[1:]
    side = BATCH * rows
    reach = 4 * shard_tiles

    me = me_ref[0]
    z, y, core = me // 4, me // 2 % 2, me % 2
    position = lax.rem(z + depth - step, depth)
    low, high = position * reach, (position + 1) * reach

    pltpu.make_async_copy(v_hbm, v_buf, v_sem).start()
    for source, (other_y, other_core, tile) in zip(fresh, layout):
        own_y = (1 - y) if other_y else y
        own_core = (1 - core) if other_core else core
        pltpu.make_async_copy(
            source,
            a_buf.at[pl.ds(BATCH + (own_y * 2 + own_core) * shard_tiles + tile, source.shape[0])],
            a_sem,
        ).start()
    for index, source in enumerate(above):
        @pl.when(y + 2 * core == index)
        def _():
            pltpu.make_async_copy(
                source.at[pl.ds(0, EDGE)], a_buf.at[pl.ds(BATCH + reach, EDGE)], a_sem
            ).start()
    for index, source in enumerate(below):
        @pl.when(3 - y - 2 * core == index)
        def _():
            pltpu.make_async_copy(
                source.at[pl.ds(shard_tiles - EDGE, EDGE)], a_buf.at[pl.ds(1, EDGE)], a_sem
            ).start()
    arrived = reach + EDGE * (bool(above) + bool(below))
    whole = a_buf.at[pl.ds(0, arrived)]
    pltpu.make_async_copy(v_hbm, v_buf, v_sem).wait()
    pltpu.make_async_copy(whole, whole, a_sem).wait()

    row_at = lax.broadcasted_iota(jnp.int32, (side, side), 0)
    col_at = lax.broadcasted_iota(jnp.int32, (side, side), 1)

    def symmetry(s, started):
        size, slot0 = size_ref[s], first_ref[s]
        tiles, offset = counts_ref[s], offset_ref[s]
        blocks = (tiles + BATCH - 1) // BATCH
        if below:
            block0 = jnp.maximum(low - offset, 0) // BATCH
        else:
            block0 = (jnp.maximum(low - offset, 0) + BATCH - 1) // BATCH
        if above:
            block1 = (jnp.maximum(high - offset, 0) + BATCH - 1) // BATCH
        else:
            block1 = jnp.where(
                offset + tiles <= high, blocks, jnp.maximum(high - offset, 0) // BATCH
            )
        block1 = jnp.where(offset + tiles <= low, block0, jnp.minimum(block1, blocks))
        block1 = jnp.maximum(block1, block0)
        batches = (size + BATCH - 1) // BATCH

        def member_batch(i, total):
            slot = slot0 + i * BATCH
            members = jnp.minimum(size - i * BATCH, BATCH)

            def column_block(j, total):
                columns = pl.ds(pl.multiple_of(j * side, side), side)
                left = v_buf[pl.ds(slot, BATCH)].reshape(side, width)
                right = a_buf[pl.ds(BATCH + offset + j * BATCH - low, BATCH)].reshape(side, width)
                product = lax.dot_general(
                    left, right, (((1,), (1,)), ((), ())),
                    preferred_element_type=jnp.float32,
                )
                keep = (row_at < members * rows) & (col_at < (tiles - j * BATCH) * rows)
                product = jnp.where(keep, product, 0.0)
                o_buf[pl.ds(slot, BATCH), :, columns] = (
                    product.astype(jnp.bfloat16).reshape(BATCH, rows, side)
                )
                for t in range(BATCH):
                    @pl.when(t < members)
                    def _():
                        pltpu.make_async_copy(
                            o_buf.at[slot + t, :, columns],
                            res_hbm.at[order_ref[slot + t], :, columns],
                            o_sem,
                        ).start()
                squares = (product * product).reshape(side // 8, 8, side)
                return total + jnp.sum(squares, axis=0)

            return lax.fori_loop(block0, block1, column_block, total)

        acc_ref[s] = lax.fori_loop(0, batches, member_batch, jnp.zeros((8, side), jnp.float32))
        return started + size * (block1 - block0)

    started = lax.fori_loop(0, irreps, symmetry, 0)
    sums = jnp.sum(acc_ref[...], axis=1)
    sums = sum(sums[:, k:k + 128] for k in range(0, side, 128))
    stats_ref[0] = stats_in_ref[0] + sums
    stats_ref[1] = stats_in_ref[1]

    def finish(n, carry):
        pltpu.make_async_copy(
            o_buf.at[0, :, pl.ds(0, side)], res_hbm.at[0, :, pl.ds(0, side)], o_sem
        ).wait()
        return carry

    lax.fori_loop(0, started, finish, 0)


def ladder(step, depth, shard_tiles, me, counts, plan, residual, stats, fresh, layout, above, below):
    ordered, order, size, first, offset = plan
    slots, rows, width = ordered.shape
    irreps = counts.shape[0]
    smem = pl.BlockSpec(memory_space=pltpu.SMEM)
    vmem = pl.BlockSpec(memory_space=pltpu.VMEM)
    anywhere = pl.BlockSpec(memory_space=pl.ANY)
    scratch = [
        pltpu.VMEM((4 * shard_tiles + 2 * BATCH, rows, width), jnp.bfloat16),
        pltpu.VMEM((slots, rows, width), jnp.bfloat16),
        pltpu.VMEM((slots, rows, residual.shape[2]), jnp.bfloat16),
        pltpu.VMEM((irreps, 8, BATCH * rows), jnp.float32),
    ]
    vmem_bytes = 2 * (scratch[0].shape[0] + slots) * rows * width + 2 * slots * residual[0].size
    flops = 2 * residual.size * width // (2 * depth)
    return pl.pallas_call(
        functools.partial(
            ladder_kernel, step, depth, shard_tiles, layout, len(above), len(below)
        ),
        out_shape=(
            jax.ShapeDtypeStruct(residual.shape, residual.dtype),
            jax.ShapeDtypeStruct(stats.shape, stats.dtype),
        ),
        in_specs=[smem] * 6 + [vmem] + [anywhere] * (2 + len(fresh) + len(above) + len(below)),
        out_specs=(anywhere, vmem),
        scratch_shapes=scratch + [pltpu.SemaphoreType.DMA] * 3,
        input_output_aliases={8: 0},
        compiler_params=pltpu.CompilerParams(vmem_limit_bytes=vmem_bytes + 6 * 1024 * 1024),
        cost_estimate=pl.CostEstimate(
            flops=flops, bytes_accessed=residual.size * 2 // depth, transcendentals=0
        ),
        name=f"ladder_{step}",
    )(
        me, counts, order, size, first, offset, stats, ordered, residual,
        *fresh, *above, *below,
    )


def per_device(amplitudes, ij_counts, integrals, ab_irrep):
    shard_tiles, rows, _ = amplitudes.shape
    own_tiles = integrals.shape[0]
    devices = lax.axis_size("vir")
    depth = devices // 4
    me = lax.axis_index("vir").astype(jnp.int32).reshape(1)
    capacity = shard_tiles * devices // 4

    def shift_z(x):
        return lax.ppermute(x, "vir", [(d, (d + 4) % devices) for d in range(devices)])

    def swap(x, bits):
        return lax.ppermute(x, "vir", [(d, d ^ bits) for d in range(devices)])

    *plan, stats = prepare(ij_counts, ab_irrep, integrals)
    residual = jnp.zeros((own_tiles, rows, capacity * rows), jnp.bfloat16)
    half = shard_tiles // 2
    full_layout = ((0, 0, 0), (1, 0, 0), (0, 1, 0), (1, 1, 0))
    split_layout = ((0, 0, 0), (1, 0, 0), (1, 0, half), (0, 1, 0), (1, 1, 0), (1, 1, half))

    def run(step, residual, stats, groups):
        fresh = groups[step]
        return ladder(
            step, depth, shard_tiles, me, ij_counts, plan, residual, stats, fresh,
            full_layout if len(fresh) == 4 else split_layout,
            groups[step - 1] if step else (),
            groups[0] if step == depth - 1 else (),
        )

    groups = []
    here, previous = amplitudes, None
    for k in range(depth):
        if k:
            here, residual, stats, *previous = lax.optimization_barrier(
                (here, residual, stats, *previous)
            )
        if k < depth - 1:
            following = shift_z(here)
            there = (swap(here, 2),)
        else:
            there = (swap(here[:half], 2), shift_z(previous[1][half:]))
        across = swap(here, 1)
        if k:
            groups.append((*previous, swap(previous[1], 1)))
            residual, stats = run(k - 1, residual, stats, groups)
        previous = (here, *there, across)
        here = following
    residual, stats, *previous = lax.optimization_barrier((residual, stats, *previous))
    groups.append((*previous, *(swap(piece, 1) for piece in previous[1:-1])))
    residual, stats = run(depth - 1, residual, stats, groups)

    stats = sum(
        [lax.ppermute(stats, "vir", [(d, (d + 4 * by) % devices) for d in range(devices)])
         for by in range(1, depth)],
        stats,
    )
    stats = sum([swap(stats, bits) for bits in (1, 2, 3)], stats)
    irrep_sums, ab_counts = jnp.sum(stats, axis=2)
    entries = ab_counts * ij_counts.astype(jnp.float32) * float(rows * rows)
    return residual, jnp.sqrt(irrep_sums / entries + 1e-06)


def solution(mesh):
    in_specs = (
        P(("groups", "vir"), None, None),
        P("groups"),
        P(("groups", "vir"), None, None),
        P(("groups", "vir")),
    )
    out_specs = (P(("groups", "vir"), None, None), P("groups"))
    return jax.shard_map(
        per_device, mesh=mesh, in_specs=in_specs, out_specs=out_specs, check_vma=False
    )
```

time: 93.4 us -> 116 us (1.24); the launches traced: 91.7 us -> 117 us
  Pallas kernels: 17.7 us -> 74.6 us
  waiting for transfers between devices: 54.6 us -> 12.6 us
  starting transfers between devices: 16 us -> 23.2 us
  local copies, waits for them, and re-layouts: 0.12 us -> 5.27 us
  other arithmetic: 2.5 us -> 0.63 us
    pallas_call x1 -> x5, Pallas kernels: 17.7 us -> 74.6 us  [the longest x1 50.3 us: prepare(): pl.pallas_call(prepare_kernel, out_shape=(jax.ShapeDtypeStruct((own_tiles...]
    ppermute x21 -> x23, waiting for transfers between devices: 54.6 us -> 12.6 us  [the longest x4 7.42 us: shift_z(): lax.ppermute(x, 'vir', [(d, (d + 4) % devices) for d in range(devices)])]
    ppermute x21 -> x23, starting transfers between devices: 16 us -> 23.2 us  [the longest x16 9.91 us: swap(): return lax.ppermute(x, 'vir', [(d, d ^ bits) for d in range(devices)])]
    broadcast_in_dim x0 -> x1, local copies, waits for them, and re-layouts: none -> 4.46 us  [per_device(): residual = jnp.zeros((own_tiles, rows, capacity * rows), jnp.bfloat16)]
  transfers between devices with their start and end apart: 21 -> 23, of which waited for: 10 -> 7; matrix products, arithmetic and copies ran while one was open for 1% -> 4% of each run, Pallas kernels for 0% -> 58%
where the time goes in v4:
time: 116 us; the launch traced here: 117 us
  Pallas kernels  74.6 us (64%)
  starting transfers between devices  23.2 us (20%)
  waiting for transfers between devices  12.6 us (11%)
  local copies, waits for them, and re-layouts  5.27 us (5%)
    pallas_call x1, Pallas kernels, prepare(): pl.pallas_call(prepare_kernel, out_shape=(jax.ShapeDtypeStruct((own_tiles...  50.3 us
    pallas_call x4, Pallas kernels, ladder(): pl.pallas_call(functools.partial(ladder_kernel, step, depth, shard_tiles,...  24.3 us
    ppermute x16, starting transfers between devices, swap(): return lax.ppermute(x, 'vir', [(d, d ^ bits) for d in range(devices)])  9.91 us
    ppermute x4, waiting for transfers between devices, shift_z(): lax.ppermute(x, 'vir', [(d, (d + 4) % devices) for d in range(devices)])  7.42 us
    ppermute x3, starting transfers between devices, per_device(): lax.ppermute(stats, 'vir', [(d, (d + 4 * by) % devices) for d in range(de...  7.32 us
    ppermute x4, starting transfers between devices, shift_z(): lax.ppermute(x, 'vir', [(d, (d + 4) % devices) for d in range(devices)])  6.01 us
    broadcast_in_dim x1, local copies, waits for them, and re-layouts, per_device(): residual = jnp.zeros((own_tiles, rows, capacity * rows), jnp.bfloat16)  4.46 us
    ppermute x16, waiting for transfers between devices, swap(): return lax.ppermute(x, 'vir', [(d, d ^ bits) for d in range(devices)])  3.12 us
  transfers between devices with their start and end apart: 23, of which 7 were waited for; matrix products, arithmetic and copies ran while one was open for 4% of the time, Pallas kernels for 58%

profile of v4, /device:TPU:0, one launch (start us, length us, event | category | flops | bytes accessed | tf_op | source)
XLA Modules:
  0.0 117.2 jit_solution(16662603611704310838)
XLA Ops:
  0.7 3.1 %collective-permute-start = (bf16[8,64,384]{2,1,0:T(8,128)(2,1)}, bf16[8,64,384]{2,1,0:T(8,128)(2,1)S(1)}, u32[]{:S(2)}, u32[]{:S(2)}) collective-permute-start(bf16[8,64,384]{2,1,0:T(8,128)(2,1)} %refs_10_), channel_id=1, source_target_pairs={{0,4},{1,5},{2,6},{3,7},{4,8},{5,9},{6,10},{7,11},{8,12},{9,13},{1... | collective-permute-start | bytes 1179656 | tf_op jit(solution)/shard_map/ppermute | solution.py:242
  3.7 1.5 %collective-permute-start.1 = (bf16[8,64,384]{2,1,0:T(8,128)(2,1)}, bf16[8,64,384]{2,1,0:T(8,128)(2,1)S(1)}, u32[]{:S(2)}, u32[]{:S(2)}) collective-permute-start(bf16[8,64,384]{2,1,0:T(8,128)(2,1)} %refs_10_), channel_id=1, source_target_pairs={{0,2},{1,3},{2,0},{3,1},{4,6},{5,7},{6,4},{7,5},{8,10},{9,11},{10,... | collective-permute-start | bytes 1179656 | tf_op jit(solution)/shard_map/ppermute | solution.py:245
  5.2 0.0 collective-permute-start.2
  5.3 50.3 %prepare.1 = (bf16[36,64,384]{2,1,0:T(8,128)(2,1)}, s32[32]{0:T(128)}, s32[8]{0:T(128)}, s32[8]{0:T(128)}, s32[8]{0:T(128)}, /*index=5*/f32[2,8,128]{2,1,0:T(8,128)}) custom-call(s32[8]{0:T(128)} %counts_ref.9, s32[32]{0:T(128)} %irrep_ref.1, bf16[32,64,384]{2,1,0:T(8,128)(2,1)} %v_ref.1), custom_call_target="tpu_custom_call" | custom-call | tf_op jit(solution)/shard_map/prepare/pallas_call | solution.py:62
  55.6 0.0 collective-permute-done.refs_0_.refs_4_
  55.6 0.0 collective-permute-done.1.refs_1_.refs_5_.refs_11_
  55.6 0.0 collective-permute-done.2.refs_2_.refs_6_.refs_12_
  55.7 0.7 copy-done.2
  56.4 0.5 collective-permute-start.4
  56.9 1.6 %collective-permute-start.3 = (bf16[8,64,384]{2,1,0:T(8,128)(2,1)}, bf16[8,64,384]{2,1,0:T(8,128)(2,1)}, u32[]{:S(2)}, u32[]{:S(2)}) collective-permute-start(bf16[8,64,384]{2,1,0:T(8,128)(2,1)} %copy-done.2), channel_id=1, source_target_pairs={{0,4},{1,5},{2,6},{3,7},{4,8},{5,9},{6,10},{7,11},{8,12},{9,13},{1... | collective-permute-start | bytes 1179656 | tf_op jit(solution)/shard_map/ppermute | solution.py:242
  58.5 0.5 collective-permute-start.5
  59.0 0.0 collective-permute-start.6
  59.0 0.0 collective-permute-done.4.refs_3_.refs_7_.refs_13_
  59.0 4.5 %broadcast_in_dim.3.res_in_ref = bf16[32,64,2048]{2,1,0:T(8,128)(2,1)} broadcast(bf16[]{:T(256)} %constant.1.clone.1), dimensions={} | broadcast | bytes 8388610 | tf_op jit(solution)/shard_map/broadcast_in_dim | solution.py:248
  63.5 4.5 %ladder_0.1 = (bf16[32,64,2048]{2,1,0:T(8,128)(2,1)}, f32[2,8,128]{2,1,0:T(8,128)S(1)}) custom-call(s32[1]{0:T(128)} %bitcast.me_ref, s32[8]{0:T(128)S(1)} %copy-done.4, s32[32]{0:T(128)S(1)} %copy-done.5, s32[8]{0:T(128)S(1)} %copy-done.6, s32[8]{0:T(128)S(1)} %copy-done.7, s32[8]{0:T(128)S(1)} %copy-done.8, ...), custom_call_target="tpu_custom_call", output_to_operand_aliasing={{0}: (8, {})} | custom-call | flops 402653184 | bytes 2097152 | tf_op jit(solution)/shard_map/ladder_0/pallas_call | solution.py:210
  68.1 2.0 %collective-permute-done.3.refs_0_.refs_6_ = bf16[8,64,384]{2,1,0:T(8,128)(2,1)} collective-permute-done((bf16[8,64,384]{2,1,0:T(8,128)(2,1)}, bf16[8,64,384]{2,1,0:T(8,128)(2,1)}, u32[]{:S(2)}, u32[]{:S(2)}) %collective-permute-start.3) | collective-permute-done | bytes 393248 | tf_op jit(solution)/shard_map/ppermute | solution.py:242
  70.0 0.0 collective-permute-done.5.refs_1_.refs_5_
  70.0 0.0 collective-permute-done.6.refs_2_.refs_6_
  70.0 0.0 collective-permute-start.8
  70.0 0.5 collective-permute-start.10
  70.5 1.1 collective-permute-start.7
  71.6 3.1 %collective-permute-start.9 = (bf16[8,64,384]{2,1,0:T(8,128)(2,1)}, bf16[8,64,384]{2,1,0:T(8,128)(2,1)S(1)}, u32[]{:S(2)}, u32[]{:S(2)}) collective-permute-start(bf16[8,64,384]{2,1,0:T(8,128)(2,1)} %collective-permute-done.3.refs_0_.refs_6_), channel_id=1, source_target_pairs={{0,2},{1,3},{2,0},{3,1},{4,6},{5,7},{6,4},{7,5},{8,10},{9,11},{10,... | collective-permute-start | bytes 1179656 | tf_op jit(solution)/shard_map/ppermute | solution.py:245
  74.7 0.0 collective-permute-done.8.refs_3_.refs_7_
  74.7 5.3 %ladder_1.1 = (bf16[32,64,2048]{2,1,0:T(8,128)(2,1)}, f32[2,8,128]{2,1,0:T(8,128)S(1)}) custom-call(s32[1]{0:T(128)} %bitcast.me_ref, s32[8]{0:T(128)S(1)} %copy-done.4, s32[32]{0:T(128)S(1)} %copy-done.5, s32[8]{0:T(128)S(1)} %copy-done.6, s32[8]{0:T(128)S(1)} %copy-done.7, s32[8]{0:T(128)S(1)} %copy-done.8, ...), custom_call_target="tpu_custom_call", output_to_operand_aliasing={{0}: (8, {})} | custom-call | flops 402653184 | bytes 2097152 | tf_op jit(solution)/shard_map/ladder_1/pallas_call | solution.py:210
  80.0 0.0 collective-permute-done.10.refs_2_.refs_8_
  80.0 4.9 %collective-permute-done.7.refs_0_ = bf16[8,64,384]{2,1,0:T(8,128)(2,1)S(1)} collective-permute-done((bf16[8,64,384]{2,1,0:T(8,128)(2,1)}, bf16[8,64,384]{2,1,0:T(8,128)(2,1)S(1)}, u32[]{:S(2)}, u32[]{:S(2)}) %collective-permute-start.7) | collective-permute-done | bytes 393248 | tf_op jit(solution)/shard_map/ppermute | solution.py:242
  84.9 0.0 collective-permute-done.9.refs_1_.refs_7_
  84.9 0.0 collective-permute-start.11
  84.9 0.5 collective-permute-start.14
  85.5 0.8 collective-permute-start.12
  86.4 0.3 collective-permute-start.13
  86.6 0.0 collective-permute-done.11.refs_3_.refs_9_
  86.7 7.5 %ladder_2.1 = (bf16[32,64,2048]{2,1,0:T(8,128)(2,1)}, f32[2,8,128]{2,1,0:T(8,128)S(1)}) custom-call(s32[1]{0:T(128)} %bitcast.me_ref, s32[8]{0:T(128)S(1)} %copy-done.4, s32[32]{0:T(128)S(1)} %copy-done.5, s32[8]{0:T(128)S(1)} %copy-done.6, s32[8]{0:T(128)S(1)} %copy-done.7, s32[8]{0:T(128)S(1)} %copy-done.8, ...), custom_call_target="tpu_custom_call", output_to_operand_aliasing={{0}: (8, {})} | custom-call | flops 402653184 | bytes 2097152 | tf_op jit(solution)/shard_map/ladder_2/pallas_call | solution.py:210
  94.2 0.5 collective-permute-done.13.refs_2_
  94.7 0.5 collective-permute-start.16
  95.2 0.9 collective-permute-done.15.refs_4_
  96.1 0.3 collective-permute-done.16.refs_5_
  96.4 7.0 %ladder_3.1 = (bf16[32,64,2048]{2,1,0:T(8,128)(2,1)}, f32[2,8,128]{2,1,0:T(8,128)S(1)}) custom-call(s32[1]{0:T(128)} %bitcast.me_ref, s32[8]{0:T(128)S(1)} %copy-done.4, s32[32]{0:T(128)S(1)} %copy-done.5, s32[8]{0:T(128)S(1)} %copy-done.6, s32[8]{0:T(128)S(1)} %copy-done.7, s32[8]{0:T(128)S(1)} %copy-done.8, ...), custom_call_target="tpu_custom_call", output_to_operand_aliasing={{0}: (8, {})} | custom-call | flops 402653184 | bytes 2097152 | tf_op jit(solution)/shard_map/ladder_3/pallas_call | solution.py:210
  103.4 4.9 %collective-permute-start.17 = (f32[2,8,128]{2,1,0:T(8,128)S(1)}, f32[2,8,128]{2,1,0:T(8,128)S(1)}, u32[]{:S(2)}, u32[]{:S(2)}) collective-permute-start(f32[2,8,128]{2,1,0:T(8,128)S(1)} %get-tuple-element.77), channel_id=1, source_target_pairs={{0,4},{1,5},{2,6},{3,7},{4,8},{5,9},{6,10},{7,11},{8,12},{9,13},{1... | collective-permute-start | bytes 24584 | tf_op jit(solution)/shard_map/ppermute | solution.py:285
  108.3 2.4 %collective-permute-start.19 = (f32[2,8,128]{2,1,0:T(8,128)S(1)}, f32[2,8,128]{2,1,0:T(8,128)S(1)}, u32[]{:S(2)}, u32[]{:S(2)}) collective-permute-start(f32[2,8,128]{2,1,0:T(8,128)S(1)} %get-tuple-element.77), channel_id=1, source_target_pairs={{0,12},{1,13},{2,14},{3,15},{4,0},{5,1},{6,2},{7,3},{8,4},{9,5},{1... | collective-permute-start | bytes 24584 | tf_op jit(solution)/shard_map/ppermute | solution.py:285
  110.7 2.1 %collective-permute-done.18 = f32[2,8,128]{2,1,0:T(8,128)S(1)} collective-permute-done((f32[2,8,128]{2,1,0:T(8,128)S(1)}, f32[2,8,128]{2,1,0:T(8,128)S(1)}, u32[]{:S(2)}, u32[]{:S(2)}) %collective-permute-start.18) | collective-permute-done | bytes 8224 | tf_op jit(solution)/shard_map/ppermute | solution.py:285
  112.8 0.1 collective-permute-start.20
  112.9 0.1 collective-permute-start.21
  113.0 1.8 %collective-permute-start.22 = (f32[2,8,128]{2,1,0:T(8,128)S(1)}, f32[2,8,128]{2,1,0:T(8,128)S(1)}, u32[]{:S(2)}, u32[]{:S(2)}) collective-permute-start(f32[2,8,128]{2,1,0:T(8,128)S(1)} %add_add_fusion), channel_id=1, source_target_pairs={{0,3},{1,2},{2,1},{3,0},{4,7},{5,6},{6,5},{7,4},{8,11},{9,10},{10,... | collective-permute-start | bytes 24584 | tf_op jit(solution)/shard_map/ppermute | solution.py:245
  114.8 0.0 collective-permute-done.20
  114.8 1.9 %collective-permute-done.21 = f32[2,8,128]{2,1,0:T(8,128)S(1)} collective-permute-done((f32[2,8,128]{2,1,0:T(8,128)S(1)}, f32[2,8,128]{2,1,0:T(8,128)S(1)}, u32[]{:S(2)}, u32[]{:S(2)}) %collective-permute-start.21) | collective-permute-done | bytes 8224 | tf_op jit(solution)/shard_map/ppermute | solution.py:245
  116.6 0.1 add_reduce_fusion
  116.7 0.5 add_sqrt_fusion
  (29 shorter events, 0.1 us)
Async XLA Ops:
  0.6 62.8 %copy-start.1 = (bf16[8,64,384]{2,1,0:T(8,128)(2,1)S(1)}, bf16[8,64,384]{2,1,0:T(8,128)(2,1)}, u32[]{:S(2)}) copy-start(bf16[8,64,384]{2,1,0:T(8,128)(2,1)} %refs_10_) | copy-start | bytes 1179652
  0.6 62.8 %copy-start.4 = (s32[8]{0:T(128)S(1)}, s32[8]{0:T(128)}, u32[]{:S(2)}) copy-start(s32[8]{0:T(128)} %counts_ref.9) | copy-start | bytes 100
  0.7 55.0 %collective-permute-start = (bf16[8,64,384]{2,1,0:T(8,128)(2,1)}, bf16[8,64,384]{2,1,0:T(8,128)(2,1)S(1)}, u32[]{:S(2)}, u32[]{:S(2)}) collective-permute-start(bf16[8,64,384]{2,1,0:T(8,128)(2,1)} %refs_10_), channel_id=1, source_target_pairs={{0,4},{1,5},{2,6},{3,7},{4,8},{5,9},{6,10},{7,11},{8,12},{9,13},{1... | collective-permute-start | bytes 1179656 | tf_op jit(solution)/shard_map/ppermute | solution.py:242
  3.7 51.9 %collective-permute-start.1 = (bf16[8,64,384]{2,1,0:T(8,128)(2,1)}, bf16[8,64,384]{2,1,0:T(8,128)(2,1)S(1)}, u32[]{:S(2)}, u32[]{:S(2)}) collective-permute-start(bf16[8,64,384]{2,1,0:T(8,128)(2,1)} %refs_10_), channel_id=1, source_target_pairs={{0,2},{1,3},{2,0},{3,1},{4,6},{5,7},{6,4},{7,5},{8,10},{9,11},{10,... | collective-permute-start | bytes 1179656 | tf_op jit(solution)/shard_map/ppermute | solution.py:245
  5.2 50.4 %collective-permute-start.2 = (bf16[8,64,384]{2,1,0:T(8,128)(2,1)}, bf16[8,64,384]{2,1,0:T(8,128)(2,1)S(1)}, u32[]{:S(2)}, u32[]{:S(2)}) collective-permute-start(bf16[8,64,384]{2,1,0:T(8,128)(2,1)} %refs_10_), channel_id=1, source_target_pairs={{0,1},{1,0},{2,3},{3,2},{4,5},{5,4},{6,7},{7,6},{8,9},{9,8},{10,11... | collective-permute-start | bytes 1179656 | tf_op jit(solution)/shard_map/ppermute | solution.py:245
  55.6 7.9 %copy-start = (bf16[36,64,384]{2,1,0:T(8,128)(2,1)S(1)}, bf16[36,64,384]{2,1,0:T(8,128)(2,1)}, u32[]{:S(2)}) copy-start(bf16[36,64,384]{2,1,0:T(8,128)(2,1)} %get-tuple-element.47.v_hbm) | copy-start | bytes 5308420
  55.6 7.9 %copy-start.5 = (s32[32]{0:T(128)S(1)}, s32[32]{0:T(128)}, u32[]{:S(2)}) copy-start(s32[32]{0:T(128)} %get-tuple-element.40.order_ref) | copy-start | bytes 388
  55.6 7.9 %copy-start.6 = (s32[8]{0:T(128)S(1)}, s32[8]{0:T(128)}, u32[]{:S(2)}) copy-start(s32[8]{0:T(128)} %get-tuple-element.41.size_ref) | copy-start | bytes 100
  55.6 7.9 %copy-start.7 = (s32[8]{0:T(128)S(1)}, s32[8]{0:T(128)}, u32[]{:S(2)}) copy-start(s32[8]{0:T(128)} %get-tuple-element.42.first_ref) | copy-start | bytes 100
  55.6 7.9 %copy-start.8 = (s32[8]{0:T(128)S(1)}, s32[8]{0:T(128)}, u32[]{:S(2)}) copy-start(s32[8]{0:T(128)} %get-tuple-element.43.offset_ref) | copy-start | bytes 100
  55.6 7.9 %copy-start.9 = (f32[2,8,128]{2,1,0:T(8,128)S(1)}, f32[2,8,128]{2,1,0:T(8,128)}, u32[]{:S(2)}) copy-start(f32[2,8,128]{2,1,0:T(8,128)} %get-tuple-element.46.stats_in_ref) | copy-start | bytes 24580
  55.6 0.8 copy-start.2
  56.4 2.6 %collective-permute-start.4 = (bf16[8,64,384]{2,1,0:T(8,128)(2,1)S(1)}, bf16[8,64,384]{2,1,0:T(8,128)(2,1)S(1)}, u32[]{:S(2)}, u32[]{:S(2)}) collective-permute-start(bf16[8,64,384]{2,1,0:T(8,128)(2,1)S(1)} %collective-permute-done.1.refs_1_.refs_5_.refs_11_), channel_id=1, source_target_pairs={{0,1},{1,0},{2,3},{3,2},{4,5},{5,4},{6,7},{7,6},{8,9},{9,8},{10,11... | collective-permute-start | bytes 1179656 | tf_op jit(solution)/shard_map/ppermute | solution.py:245
  56.9 13.1 %collective-permute-start.3 = (bf16[8,64,384]{2,1,0:T(8,128)(2,1)}, bf16[8,64,384]{2,1,0:T(8,128)(2,1)}, u32[]{:S(2)}, u32[]{:S(2)}) collective-permute-start(bf16[8,64,384]{2,1,0:T(8,128)(2,1)} %copy-done.2), channel_id=1, source_target_pairs={{0,4},{1,5},{2,6},{3,7},{4,8},{5,9},{6,10},{7,11},{8,12},{9,13},{1... | collective-permute-start | bytes 1179656 | tf_op jit(solution)/shard_map/ppermute | solution.py:242
  58.5 11.6 %collective-permute-start.5 = (bf16[8,64,384]{2,1,0:T(8,128)(2,1)}, bf16[8,64,384]{2,1,0:T(8,128)(2,1)}, u32[]{:S(2)}, u32[]{:S(2)}) collective-permute-start(bf16[8,64,384]{2,1,0:T(8,128)(2,1)} %copy-done.2), channel_id=1, source_target_pairs={{0,2},{1,3},{2,0},{3,1},{4,6},{5,7},{6,4},{7,5},{8,10},{9,11},{10,... | collective-permute-start | bytes 1179656 | tf_op jit(solution)/shard_map/ppermute | solution.py:245
  59.0 11.1 %collective-permute-start.6 = (bf16[8,64,384]{2,1,0:T(8,128)(2,1)}, bf16[8,64,384]{2,1,0:T(8,128)(2,1)}, u32[]{:S(2)}, u32[]{:S(2)}) collective-permute-start(bf16[8,64,384]{2,1,0:T(8,128)(2,1)} %copy-done.2), channel_id=1, source_target_pairs={{0,1},{1,0},{2,3},{3,2},{4,5},{5,4},{6,7},{7,6},{8,9},{9,8},{10,11... | collective-permute-start | bytes 1179656 | tf_op jit(solution)/shard_map/ppermute | solution.py:245
  59.0 15.7 %copy-start.3 = (bf16[8,64,384]{2,1,0:T(8,128)(2,1)S(1)}, bf16[8,64,384]{2,1,0:T(8,128)(2,1)}, u32[]{:S(2)}) copy-start(bf16[8,64,384]{2,1,0:T(8,128)(2,1)} %copy-done.2) | copy-start | bytes 1179652
  70.0 4.7 %collective-permute-start.8 = (bf16[8,64,384]{2,1,0:T(8,128)(2,1)}, bf16[8,64,384]{2,1,0:T(8,128)(2,1)S(1)}, u32[]{:S(2)}, u32[]{:S(2)}) collective-permute-start(bf16[8,64,384]{2,1,0:T(8,128)(2,1)} %collective-permute-done.5.refs_1_.refs_5_), channel_id=1, source_target_pairs={{0,1},{1,0},{2,3},{3,2},{4,5},{5,4},{6,7},{7,6},{8,9},{9,8},{10,11... | collective-permute-start | bytes 1179656 | tf_op jit(solution)/shard_map/ppermute | solution.py:245
  70.0 9.9 %collective-permute-start.10 = (bf16[8,64,384]{2,1,0:T(8,128)(2,1)}, bf16[8,64,384]{2,1,0:T(8,128)(2,1)S(1)}, u32[]{:S(2)}, u32[]{:S(2)}) collective-permute-start(bf16[8,64,384]{2,1,0:T(8,128)(2,1)} %collective-permute-done.3.refs_0_.refs_6_), channel_id=1, source_target_pairs={{0,1},{1,0},{2,3},{3,2},{4,5},{5,4},{6,7},{7,6},{8,9},{9,8},{10,11... | collective-permute-start | bytes 1179656 | tf_op jit(solution)/shard_map/ppermute | solution.py:245
  70.5 14.4 %collective-permute-start.7 = (bf16[8,64,384]{2,1,0:T(8,128)(2,1)}, bf16[8,64,384]{2,1,0:T(8,128)(2,1)S(1)}, u32[]{:S(2)}, u32[]{:S(2)}) collective-permute-start(bf16[8,64,384]{2,1,0:T(8,128)(2,1)} %collective-permute-done.3.refs_0_.refs_6_), channel_id=1, source_target_pairs={{0,4},{1,5},{2,6},{3,7},{4,8},{5,9},{6,10},{7,11},{8,12},{9,13},{1... | collective-permute-start | bytes 1179656 | tf_op jit(solution)/shard_map/ppermute | solution.py:242
  71.6 13.3 %collective-permute-start.9 = (bf16[8,64,384]{2,1,0:T(8,128)(2,1)}, bf16[8,64,384]{2,1,0:T(8,128)(2,1)S(1)}, u32[]{:S(2)}, u32[]{:S(2)}) collective-permute-start(bf16[8,64,384]{2,1,0:T(8,128)(2,1)} %collective-permute-done.3.refs_0_.refs_6_), channel_id=1, source_target_pairs={{0,2},{1,3},{2,0},{3,1},{4,6},{5,7},{6,4},{7,5},{8,10},{9,11},{10,... | collective-permute-start | bytes 1179656 | tf_op jit(solution)/shard_map/ppermute | solution.py:245
  84.9 1.7 %collective-permute-start.11 = (bf16[8,64,384]{2,1,0:T(8,128)(2,1)S(1)}, bf16[8,64,384]{2,1,0:T(8,128)(2,1)S(1)}, u32[]{:S(2)}, u32[]{:S(2)}) collective-permute-start(bf16[8,64,384]{2,1,0:T(8,128)(2,1)S(1)} %collective-permute-done.9.refs_1_.refs_7_), channel_id=1, source_target_pairs={{0,1},{1,0},{2,3},{3,2},{4,5},{5,4},{6,7},{7,6},{8,9},{9,8},{10,11... | collective-permute-start | bytes 1179656 | tf_op jit(solution)/shard_map/ppermute | solution.py:245
  84.9 9.7 %collective-permute-start.14 = (bf16[8,64,384]{2,1,0:T(8,128)(2,1)S(1)}, bf16[8,64,384]{2,1,0:T(8,128)(2,1)S(1)}, u32[]{:S(2)}, u32[]{:S(2)}) collective-permute-start(bf16[8,64,384]{2,1,0:T(8,128)(2,1)S(1)} %collective-permute-done.7.refs_0_), channel_id=1, source_target_pairs={{0,1},{1,0},{2,3},{3,2},{4,5},{5,4},{6,7},{7,6},{8,9},{9,8},{10,11... | collective-permute-start | bytes 1179656 | tf_op jit(solution)/shard_map/ppermute | solution.py:245
  85.5 8.7 %collective-permute-start.12 = (bf16[4,64,384]{2,1,0:T(8,128)(2,1)S(1)}, bf16[4,64,384]{2,1,0:T(8,128)(2,1)S(1)}, u32[]{:S(2)}, u32[]{:S(2)}) collective-permute-start(bf16[4,64,384]{2,1,0:T(8,128)(2,1)S(1)} %slice.6), channel_id=1, source_target_pairs={{0,2},{1,3},{2,0},{3,1},{4,6},{5,7},{6,4},{7,5},{8,10},{9,11},{10,... | collective-permute-start | bytes 589832 | tf_op jit(solution)/shard_map/ppermute | solution.py:245
  86.4 8.3 %collective-permute-start.13 = (bf16[4,64,384]{2,1,0:T(8,128)(2,1)S(1)}, bf16[4,64,384]{2,1,0:T(8,128)(2,1)S(1)}, u32[]{:S(2)}, u32[]{:S(2)}) collective-permute-start(bf16[4,64,384]{2,1,0:T(8,128)(2,1)S(1)} %slice.7), channel_id=1, source_target_pairs={{0,4},{1,5},{2,6},{3,7},{4,8},{5,9},{6,10},{7,11},{8,12},{9,13},{1... | collective-permute-start | bytes 589832 | tf_op jit(solution)/shard_map/ppermute | solution.py:242
  94.7 1.4 %collective-permute-start.15 = (bf16[4,64,384]{2,1,0:T(8,128)(2,1)S(1)}, bf16[4,64,384]{2,1,0:T(8,128)(2,1)S(1)}, u32[]{:S(2)}, u32[]{:S(2)}) collective-permute-start(bf16[4,64,384]{2,1,0:T(8,128)(2,1)S(1)} %collective-permute-done.12.refs_1_), channel_id=1, source_target_pairs={{0,1},{1,0},{2,3},{3,2},{4,5},{5,4},{6,7},{7,6},{8,9},{9,8},{10,11... | collective-permute-start | bytes 589832 | tf_op jit(solution)/shard_map/ppermute | solution.py:245
  94.7 1.7 %collective-permute-start.16 = (bf16[4,64,384]{2,1,0:T(8,128)(2,1)S(1)}, bf16[4,64,384]{2,1,0:T(8,128)(2,1)S(1)}, u32[]{:S(2)}, u32[]{:S(2)}) collective-permute-start(bf16[4,64,384]{2,1,0:T(8,128)(2,1)S(1)} %collective-permute-done.13.refs_2_), channel_id=1, source_target_pairs={{0,1},{1,0},{2,3},{3,2},{4,5},{5,4},{6,7},{7,6},{8,9},{9,8},{10,11... | collective-permute-start | bytes 589832 | tf_op jit(solution)/shard_map/ppermute | solution.py:245
  103.4 7.3 %collective-permute-start.17 = (f32[2,8,128]{2,1,0:T(8,128)S(1)}, f32[2,8,128]{2,1,0:T(8,128)S(1)}, u32[]{:S(2)}, u32[]{:S(2)}) collective-permute-start(f32[2,8,128]{2,1,0:T(8,128)S(1)} %get-tuple-element.77), channel_id=1, source_target_pairs={{0,4},{1,5},{2,6},{3,7},{4,8},{5,9},{6,10},{7,11},{8,12},{9,13},{1... | collective-permute-start | bytes 24584 | tf_op jit(solution)/shard_map/ppermute | solution.py:285
  108.3 4.5 %collective-permute-start.18 = (f32[2,8,128]{2,1,0:T(8,128)S(1)}, f32[2,8,128]{2,1,0:T(8,128)S(1)}, u32[]{:S(2)}, u32[]{:S(2)}) collective-permute-start(f32[2,8,128]{2,1,0:T(8,128)S(1)} %get-tuple-element.77), channel_id=1, source_target_pairs={{0,8},{1,9},{2,10},{3,11},{4,12},{5,13},{6,14},{7,15},{8,0},{9,1},... | collective-permute-start | bytes 24584 | tf_op jit(solution)/shard_map/ppermute | solution.py:285
  108.3 4.5 %collective-permute-start.19 = (f32[2,8,128]{2,1,0:T(8,128)S(1)}, f32[2,8,128]{2,1,0:T(8,128)S(1)}, u32[]{:S(2)}, u32[]{:S(2)}) collective-permute-start(f32[2,8,128]{2,1,0:T(8,128)S(1)} %get-tuple-element.77), channel_id=1, source_target_pairs={{0,12},{1,13},{2,14},{3,15},{4,0},{5,1},{6,2},{7,3},{8,4},{9,5},{1... | collective-permute-start | bytes 24584 | tf_op jit(solution)/shard_map/ppermute | solution.py:285
  112.8 1.9 %collective-permute-start.20 = (f32[2,8,128]{2,1,0:T(8,128)S(1)}, f32[2,8,128]{2,1,0:T(8,128)S(1)}, u32[]{:S(2)}, u32[]{:S(2)}) collective-permute-start(f32[2,8,128]{2,1,0:T(8,128)S(1)} %add_add_fusion), channel_id=1, source_target_pairs={{0,1},{1,0},{2,3},{3,2},{4,5},{5,4},{6,7},{7,6},{8,9},{9,8},{10,11... | collective-permute-start | bytes 24584 | tf_op jit(solution)/shard_map/ppermute | solution.py:245
  112.9 3.7 %collective-permute-start.21 = (f32[2,8,128]{2,1,0:T(8,128)S(1)}, f32[2,8,128]{2,1,0:T(8,128)S(1)}, u32[]{:S(2)}, u32[]{:S(2)}) collective-permute-start(f32[2,8,128]{2,1,0:T(8,128)S(1)} %add_add_fusion), channel_id=1, source_target_pairs={{0,2},{1,3},{2,0},{3,1},{4,6},{5,7},{6,4},{7,5},{8,10},{9,11},{10,... | collective-permute-start | bytes 24584 | tf_op jit(solution)/shard_map/ppermute | solution.py:245
  113.0 3.6 %collective-permute-start.22 = (f32[2,8,128]{2,1,0:T(8,128)S(1)}, f32[2,8,128]{2,1,0:T(8,128)S(1)}, u32[]{:S(2)}, u32[]{:S(2)}) collective-permute-start(f32[2,8,128]{2,1,0:T(8,128)S(1)} %add_add_fusion), channel_id=1, source_target_pairs={{0,3},{1,2},{2,1},{3,0},{4,7},{5,6},{6,5},{7,4},{8,11},{9,10},{10,... | collective-permute-start | bytes 24584 | tf_op jit(solution)/shard_map/ppermute | solution.py:245

commit v5 on v4

--- a/solution.py
+++ b/solution.py
@@ -8,15 +8,20 @@
 from jax.sharding import PartitionSpec as P
 
 BATCH = 4
+UNROLL = 4
 EDGE = BATCH - 1
 
 
 def prepare_kernel(
-    counts_ref, irrep_ref, v_ref, sorted_ref, order_ref, size_ref, first_ref, offset_ref,
-    stats_ref, next_ref, sem,
+    counts_ref, irrep_ref, v_ref, res_ref, sorted_ref, order_ref, size_ref, first_ref, offset_ref,
+    stats_ref, blank_ref, next_ref, sem, blank_sem,
 ):
     own_tiles = v_ref.shape[0]
     irreps = counts_ref.shape[0]
+    blank_ref[...] = jnp.zeros(blank_ref.shape, blank_ref.dtype)
+    group = blank_ref.shape[0]
+    for l in range(0, own_tiles, group):
+        pltpu.make_async_copy(blank_ref, res_ref.at[pl.ds(l, group)], blank_sem).start()
     for s in range(irreps):
         size_ref[s] = 0
 
@@ -43,6 +48,8 @@
         return carry
 
     lax.fori_loop(0, own_tiles, place, 0)
+    spare = sorted_ref.shape[0] - own_tiles
+    sorted_ref[pl.ds(own_tiles, spare)] = jnp.zeros((spare, *sorted_ref.shape[1:]), sorted_ref.dtype)
     shape = stats_ref.shape[1:]
     at_row = lax.broadcasted_iota(jnp.int32, shape, 0)
     at_lane = lax.broadcasted_iota(jnp.int32, shape, 1)
@@ -52,16 +59,19 @@
     stats_ref[0] = jnp.zeros(shape, jnp.float32)
     stats_ref[1] = sizes.astype(jnp.float32)
     pltpu.make_async_copy(v_ref, sorted_ref.at[pl.ds(0, own_tiles)], sem).wait()
-
-
-def prepare(counts, irrep, integrals):
+    pltpu.make_async_copy(res_ref, res_ref, blank_sem).wait()
+
+
+def prepare(counts, irrep, integrals, capacity):
     own_tiles, rows, width = integrals.shape
     irreps = counts.shape[0]
     smem = pl.BlockSpec(memory_space=pltpu.SMEM)
+    vmem = pl.BlockSpec(memory_space=pltpu.VMEM)
     anywhere = pl.BlockSpec(memory_space=pl.ANY)
     return pl.pallas_call(
         prepare_kernel,
         out_shape=(
+            jax.ShapeDtypeStruct((own_tiles, rows, capacity * rows), jnp.bfloat16),
             jax.ShapeDtypeStruct((own_tiles + BATCH, rows, width), integrals.dtype),
             jax.ShapeDtypeStruct((own_tiles,), jnp.int32),
             jax.ShapeDtypeStruct((irreps,), jnp.int32),
@@ -70,8 +80,17 @@
             jax.ShapeDtypeStruct((2, irreps, 128), jnp.float32),
         ),
         in_specs=[smem, smem, anywhere],
-        out_specs=(anywhere, smem, smem, smem, smem, pl.BlockSpec(memory_space=pltpu.VMEM)),
-        scratch_shapes=[pltpu.SMEM((irreps,), jnp.int32), pltpu.SemaphoreType.DMA],
+        out_specs=(anywhere, vmem, smem, smem, smem, smem, vmem),
+        scratch_shapes=[
+            pltpu.VMEM((2, rows, capacity * rows), jnp.bfloat16),
+            pltpu.SMEM((irreps,), jnp.int32),
+            pltpu.SemaphoreType.DMA,
+            pltpu.SemaphoreType.DMA,
+        ],
+        compiler_params=pltpu.CompilerParams(vmem_limit_bytes=8 * 1024 * 1024),
+        cost_estimate=pl.CostEstimate(
+            flops=0, bytes_accessed=2 * own_tiles * rows * capacity * rows, transcendentals=0
+        ),
         name="prepare",
     )(counts, irrep, integrals)
 
@@ -79,13 +98,16 @@
 def ladder_kernel(
     step, depth, shard_tiles, layout, n_above, n_below,
     me_ref, counts_ref, order_ref, size_ref, first_ref, offset_ref,
-    stats_in_ref, v_hbm, res_in_ref, *refs,
+    stats_in_ref, v_ref, res_in_ref, *refs,
 ):
     del res_in_ref
     fresh, refs = refs[:len(layout)], refs[len(layout):]
     above, refs = refs[:n_above], refs[n_above:]
     below, refs = refs[:n_below], refs[n_below:]
-    res_hbm, stats_ref, a_buf, v_buf, o_buf, acc_ref, a_sem, v_sem, o_sem = refs
+    (
+        res_hbm, stats_ref, a_buf, o_buf, acc_ref,
+        slot_ref, tile_ref, block_ref, member_ref, limit_ref, group_ref, a_sem, o_sem,
+    ) = refs
     own_tiles = order_ref.shape[0]
     irreps = counts_ref.shape[0]
     rows, width = a_buf.shape[1:]
@@ -97,7 +119,6 @@
     position = lax.rem(z + depth - step, depth)
     low, high = position * reach, (position + 1) * reach
 
-    pltpu.make_async_copy(v_hbm, v_buf, v_sem).start()
     for source, (other_y, other_core, tile) in zip(fresh, layout):
         own_y = (1 - y) if other_y else y
         own_core = (1 - core) if other_core else core
@@ -118,15 +139,8 @@
             pltpu.make_async_copy(
                 source.at[pl.ds(shard_tiles - EDGE, EDGE)], a_buf.at[pl.ds(1, EDGE)], a_sem
             ).start()
-    arrived = reach + EDGE * (bool(above) + bool(below))
-    whole = a_buf.at[pl.ds(0, arrived)]
-    pltpu.make_async_copy(v_hbm, v_buf, v_sem).wait()
-    pltpu.make_async_copy(whole, whole, a_sem).wait()
-
-    row_at = lax.broadcasted_iota(jnp.int32, (side, side), 0)
-    col_at = lax.broadcasted_iota(jnp.int32, (side, side), 1)
-
-    def symmetry(s, started):
+
+    def symmetry(s, items):
         size, slot0 = size_ref[s], first_ref[s]
         tiles, offset = counts_ref[s], offset_ref[s]
         blocks = (tiles + BATCH - 1) // BATCH
@@ -141,43 +155,77 @@
                 offset + tiles <= high, blocks, jnp.maximum(high - offset, 0) // BATCH
             )
         block1 = jnp.where(offset + tiles <= low, block0, jnp.minimum(block1, blocks))
-        block1 = jnp.maximum(block1, block0)
-        batches = (size + BATCH - 1) // BATCH
-
-        def member_batch(i, total):
-            slot = slot0 + i * BATCH
-            members = jnp.minimum(size - i * BATCH, BATCH)
-
-            def column_block(j, total):
-                columns = pl.ds(pl.multiple_of(j * side, side), side)
-                left = v_buf[pl.ds(slot, BATCH)].reshape(side, width)
-                right = a_buf[pl.ds(BATCH + offset + j * BATCH - low, BATCH)].reshape(side, width)
-                product = lax.dot_general(
-                    left, right, (((1,), (1,)), ((), ())),
-                    preferred_element_type=jnp.float32,
-                )
-                keep = (row_at < members * rows) & (col_at < (tiles - j * BATCH) * rows)
-                product = jnp.where(keep, product, 0.0)
-                o_buf[pl.ds(slot, BATCH), :, columns] = (
-                    product.astype(jnp.bfloat16).reshape(BATCH, rows, side)
-                )
-                for t in range(BATCH):
-                    @pl.when(t < members)
-                    def _():
-                        pltpu.make_async_copy(
-                            o_buf.at[slot + t, :, columns],
-                            res_hbm.at[order_ref[slot + t], :, columns],
-                            o_sem,
-                        ).start()
-                squares = (product * product).reshape(side // 8, 8, side)
-                return total + jnp.sum(squares, axis=0)
-
-            return lax.fori_loop(block0, block1, column_block, total)
-
-        acc_ref[s] = lax.fori_loop(0, batches, member_batch, jnp.zeros((8, side), jnp.float32))
-        return started + size * (block1 - block0)
-
-    started = lax.fori_loop(0, irreps, symmetry, 0)
+
+        def member_batch(i, items):
+            def column_block(j, items):
+                slot_ref[items] = slot0 + i * BATCH
+                tile_ref[items] = BATCH + offset + j * BATCH - low
+                block_ref[items] = j
+                member_ref[items] = jnp.minimum(size - i * BATCH, BATCH)
+                limit_ref[items] = (tiles - j * BATCH) * rows
+                group_ref[items] = s
+                return items + 1
+
+            return lax.fori_loop(block0, block1, column_block, items)
+
+        return lax.fori_loop(0, (size + BATCH - 1) // BATCH, member_batch, items)
+
+    items = lax.fori_loop(0, irreps, symmetry, 0)
+    for spare in range(UNROLL - 1):
+        slot_ref[items + spare] = own_tiles
+        tile_ref[items + spare] = BATCH
+        block_ref[items + spare] = 0
+        member_ref[items + spare] = 0
+        limit_ref[items + spare] = 0
+        group_ref[items + spare] = 0
+    acc_ref[...] = jnp.zeros(acc_ref.shape, acc_ref.dtype)
+    for start, stop in ((0, 1 if below else BATCH), (reach + BATCH + (EDGE if above else 0), a_buf.shape[0])):
+        a_buf[pl.ds(start, stop - start)] = jnp.zeros((stop - start, rows, width), a_buf.dtype)
+    arrived = reach + EDGE * (bool(above) + bool(below))
+    whole = a_buf.at[pl.ds(0, arrived)]
+    pltpu.make_async_copy(whole, whole, a_sem).wait()
+
+    col_at = lax.broadcasted_iota(jnp.int32, (1, side), 1)
+
+    def product(n):
+        slot, members = slot_ref[n], member_ref[n]
+        left = v_ref[pl.ds(slot, BATCH)].reshape(side, width)
+        right = a_buf[pl.ds(tile_ref[n], BATCH)].reshape(side, width)
+        values = lax.dot_general(
+            left, right, (((1,), (1,)), ((), ())), preferred_element_type=jnp.float32
+        )
+        values = jnp.where(col_at < limit_ref[n], values, 0.0).reshape(BATCH, rows, side)
+        columns = pl.ds(pl.multiple_of(block_ref[n] * side, side), side)
+        o_buf[pl.ds(slot, BATCH), :, columns] = values.astype(jnp.bfloat16)
+        squares = jnp.sum((values * values).reshape(BATCH, rows // 8, 8, side), axis=1)
+        total = jnp.zeros((8, side), jnp.float32)
+        for t in range(BATCH):
+            total = total + jnp.where(t < members, squares[t], 0.0)
+        acc_ref[group_ref[n]] += total
+
+    def send(n, started):
+        slot, members = slot_ref[n], member_ref[n]
+        columns = pl.ds(pl.multiple_of(block_ref[n] * side, side), side)
+
+        def one(t, carry):
+            pltpu.make_async_copy(
+                o_buf.at[slot + t, :, columns],
+                res_hbm.at[order_ref[slot + t], :, columns],
+                o_sem,
+            ).start()
+            return carry
+
+        lax.fori_loop(0, members, one, 0)
+        return started + members
+
+    def several(u, started):
+        for n in range(UNROLL):
+            product(u * UNROLL + n)
+        for n in range(UNROLL):
+            started = send(u * UNROLL + n, started)
+        return started
+
+    started = lax.fori_loop(0, (items + UNROLL - 1) // UNROLL, several, 0)
     sums = jnp.sum(acc_ref[...], axis=1)
     sums = sum(sums[:, k:k + 128] for k in range(0, side, 128))
     stats_ref[0] = stats_in_ref[0] + sums
@@ -199,13 +247,15 @@
     smem = pl.BlockSpec(memory_space=pltpu.SMEM)
     vmem = pl.BlockSpec(memory_space=pltpu.VMEM)
     anywhere = pl.BlockSpec(memory_space=pl.ANY)
+    own_tiles = order.shape[0]
+    most = (own_tiles // BATCH + irreps) * (4 * shard_tiles // BATCH + 2 * irreps) + UNROLL
+    a_tiles = 4 * shard_tiles + 2 * BATCH
     scratch = [
-        pltpu.VMEM((4 * shard_tiles + 2 * BATCH, rows, width), jnp.bfloat16),
-        pltpu.VMEM((slots, rows, width), jnp.bfloat16),
+        pltpu.VMEM((a_tiles, rows, width), jnp.bfloat16),
         pltpu.VMEM((slots, rows, residual.shape[2]), jnp.bfloat16),
         pltpu.VMEM((irreps, 8, BATCH * rows), jnp.float32),
-    ]
-    vmem_bytes = 2 * (scratch[0].shape[0] + slots) * rows * width + 2 * slots * residual[0].size
+    ] + [pltpu.SMEM((most,), jnp.int32)] * 6
+    vmem_bytes = 2 * (a_tiles + slots) * rows * width + 2 * slots * residual[0].size
     flops = 2 * residual.size * width // (2 * depth)
     return pl.pallas_call(
         functools.partial(
@@ -215,9 +265,9 @@
             jax.ShapeDtypeStruct(residual.shape, residual.dtype),
             jax.ShapeDtypeStruct(stats.shape, stats.dtype),
         ),
-        in_specs=[smem] * 6 + [vmem] + [anywhere] * (2 + len(fresh) + len(above) + len(below)),
+        in_specs=[smem] * 6 + [vmem] * 2 + [anywhere] * (1 + len(fresh) + len(above) + len(below)),
         out_specs=(anywhere, vmem),
-        scratch_shapes=scratch + [pltpu.SemaphoreType.DMA] * 3,
+        scratch_shapes=scratch + [pltpu.SemaphoreType.DMA] * 2,
         input_output_aliases={8: 0},
         compiler_params=pltpu.CompilerParams(vmem_limit_bytes=vmem_bytes + 6 * 1024 * 1024),
         cost_estimate=pl.CostEstimate(
@@ -232,7 +282,6 @@
 
 def per_device(amplitudes, ij_counts, integrals, ab_irrep):
     shard_tiles, rows, _ = amplitudes.shape
-    own_tiles = integrals.shape[0]
     devices = lax.axis_size("vir")
     depth = devices // 4
     me = lax.axis_index("vir").astype(jnp.int32).reshape(1)
@@ -244,8 +293,7 @@
     def swap(x, bits):
         return lax.ppermute(x, "vir", [(d, d ^ bits) for d in range(devices)])
 
-    *plan, stats = prepare(ij_counts, ab_irrep, integrals)
-    residual = jnp.zeros((own_tiles, rows, capacity * rows), jnp.bfloat16)
+    residual, *plan, stats = prepare(ij_counts, ab_irrep, integrals, capacity)
     half = shard_tiles // 2
     full_layout = ((0, 0, 0), (1, 0, 0), (0, 1, 0), (1, 1, 0))
     split_layout = ((0, 0, 0), (1, 0, 0), (1, 0, half), (0, 1, 0), (1, 1, 0), (1, 1, half))

time: 116 us -> 70.7 us (0.61); the launches traced: 117 us -> 70.3 us
  Pallas kernels: 74.6 us -> 22.4 us
  waiting for transfers between devices: 12.6 us -> 24.4 us
  starting transfers between devices: 23.2 us -> 17.8 us
    pallas_call x1, Pallas kernels: 50.3 us -> 4.48 us  [prepare(): pl.pallas_call(prepare_kernel, out_shape=(jax.ShapeDtypeStruct((own_tiles...]
    ppermute x4, waiting for transfers between devices: 7.42 us -> 18.1 us  [shift_z(): lax.ppermute(x, 'vir', [(d, (d + 4) % devices) for d in range(devices)])]
    pallas_call x4, Pallas kernels: 24.3 us -> 17.9 us  [ladder(): pl.pallas_call(functools.partial(ladder_kernel, step, depth, shard_tiles,...]
    broadcast_in_dim x1 -> x0, local copies, waits for them, and re-layouts: 4.46 us -> none  [per_device(): residual = jnp.zeros((own_tiles, rows, capacity * rows), jnp.bfloat16)]
    unnamed x20 -> x14, local copies, waits for them, and re-layouts: 0.76 us -> 4.38 us
    ppermute x3, starting transfers between devices: 7.32 us -> 3.87 us  [per_device(): lax.ppermute(stats, 'vir', [(d, (d + 4 * by) % devices) for d in range(de...]
    ppermute x4, starting transfers between devices: 6.01 us -> 4.36 us  [shift_z(): lax.ppermute(x, 'vir', [(d, (d + 4) % devices) for d in range(devices)])]
  transfers between devices with their start and end apart: 23 -> 23, of which waited for: 7 -> 11; matrix products, arithmetic and copies ran while one was open for 4% -> 0% of each run, Pallas kernels for 58% -> 25%
where the time goes in v5:
time: 70.7 us; the launch traced here: 70.3 us
  waiting for transfers between devices  24.4 us (35%)
  Pallas kernels  22.4 us (32%)
  starting transfers between devices  17.8 us (25%)
  local copies, waits for them, and re-layouts  4.42 us (6%)
  between operations  0.76 us (1%)
    ppermute x4, waiting for transfers between devices, shift_z(): lax.ppermute(x, 'vir', [(d, (d + 4) % devices) for d in range(devices)])  18.1 us
    pallas_call x4, Pallas kernels, ladder(): pl.pallas_call(functools.partial(ladder_kernel, step, depth, shard_tiles,...  17.9 us
    ppermute x16, starting transfers between devices, swap(): return lax.ppermute(x, 'vir', [(d, d ^ bits) for d in range(devices)])  9.54 us
    pallas_call x1, Pallas kernels, prepare(): pl.pallas_call(prepare_kernel, out_shape=(jax.ShapeDtypeStruct((own_tiles...  4.48 us
    unnamed x14, local copies, waits for them, and re-layouts  4.38 us
    ppermute x4, starting transfers between devices, shift_z(): lax.ppermute(x, 'vir', [(d, (d + 4) % devices) for d in range(devices)])  4.36 us
    ppermute x16, waiting for transfers between devices, swap(): return lax.ppermute(x, 'vir', [(d, d ^ bits) for d in range(devices)])  4.09 us
    ppermute x3, starting transfers between devices, per_device(): lax.ppermute(stats, 'vir', [(d, (d + 4 * by) % devices) for d in range(de...  3.87 us
  transfers between devices with their start and end apart: 23, of which 11 were waited for; matrix products, arithmetic and copies ran while one was open for 0% of the time, Pallas kernels for 25%

profile of v5, /device:TPU:0, one launch (start us, length us, event | category | flops | bytes accessed | tf_op | source)
XLA Modules:
  0.0 70.3 jit_solution(9734827733540270039)
XLA Ops:
  0.6 0.0 copy-start.1
  0.6 3.1 %collective-permute-start = (bf16[8,64,384]{2,1,0:T(8,128)(2,1)}, bf16[8,64,384]{2,1,0:T(8,128)(2,1)}, u32[]{:S(2)}, u32[]{:S(2)}) collective-permute-start(bf16[8,64,384]{2,1,0:T(8,128)(2,1)} %refs_10_), channel_id=1, source_target_pairs={{0,4},{1,5},{2,6},{3,7},{4,8},{5,9},{6,10},{7,11},{8,12},{9,13},{1... | collective-permute-start | bytes 1179656 | tf_op jit(solution)/shard_map/ppermute | solution.py:291
  3.7 1.5 %collective-permute-start.1 = (bf16[8,64,384]{2,1,0:T(8,128)(2,1)}, bf16[8,64,384]{2,1,0:T(8,128)(2,1)S(1)}, u32[]{:S(2)}, u32[]{:S(2)}) collective-permute-start(bf16[8,64,384]{2,1,0:T(8,128)(2,1)} %refs_10_), channel_id=1, source_target_pairs={{0,2},{1,3},{2,0},{3,1},{4,6},{5,7},{6,4},{7,5},{8,10},{9,11},{10,... | collective-permute-start | bytes 1179656 | tf_op jit(solution)/shard_map/ppermute | solution.py:294
  5.2 1.4 %copy-done.2 = bf16[32,64,384]{2,1,0:T(8,128)(2,1)S(1)} copy-done((bf16[32,64,384]{2,1,0:T(8,128)(2,1)S(1)}, bf16[32,64,384]{2,1,0:T(8,128)(2,1)}, u32[]{:S(2)}) %copy-start.2) | copy-done | bytes 1572888
  6.7 0.7 copy-done.3
  7.3 0.7 copy-done.6
  8.0 4.5 %prepare.1 = (bf16[32,64,2048]{2,1,0:T(8,128)(2,1)}, bf16[36,64,384]{2,1,0:T(8,128)(2,1)S(1)}, s32[32]{0:T(128)S(1)}, s32[8]{0:T(128)S(1)}, s32[8]{0:T(128)S(1)}...) custom-call(s32[8]{0:T(128)S(1)} %copy-done.3, s32[32]{0:T(128)S(1)} %copy-done.6, bf16[32,64,384]{2,1,0:T(8,128)(2,1)S(1)} %copy-done.2), custom_call_target="tpu_custom_call" | custom-call | bytes 8388608 | tf_op jit(solution)/shard_map/prepare/pallas_call | solution.py:71
  12.5 2.7 %collective-permute-done.refs_0_.refs_4_ = bf16[8,64,384]{2,1,0:T(8,128)(2,1)} collective-permute-done((bf16[8,64,384]{2,1,0:T(8,128)(2,1)}, bf16[8,64,384]{2,1,0:T(8,128)(2,1)}, u32[]{:S(2)}, u32[]{:S(2)}) %collective-permute-start) | collective-permute-done | bytes 393248 | tf_op jit(solution)/shard_map/ppermute | solution.py:291
  15.2 0.0 collective-permute-done.1.refs_1_.refs_5_.refs_11_
  15.2 0.0 collective-permute-done.2.refs_2_.refs_6_.refs_12_
  15.2 0.0 collective-permute-start.4
  15.2 0.9 %collective-permute-start.3 = (bf16[8,64,384]{2,1,0:T(8,128)(2,1)}, bf16[8,64,384]{2,1,0:T(8,128)(2,1)}, u32[]{:S(2)}, u32[]{:S(2)}) collective-permute-start(bf16[8,64,384]{2,1,0:T(8,128)(2,1)} %collective-permute-done.refs_0_.refs_4_), channel_id=1, source_target_pairs={{0,4},{1,5},{2,6},{3,7},{4,8},{5,9},{6,10},{7,11},{8,12},{9,13},{1... | collective-permute-start | bytes 1179656 | tf_op jit(solution)/shard_map/ppermute | solution.py:291
  16.1 1.5 %collective-permute-start.5 = (bf16[8,64,384]{2,1,0:T(8,128)(2,1)}, bf16[8,64,384]{2,1,0:T(8,128)(2,1)}, u32[]{:S(2)}, u32[]{:S(2)}) collective-permute-start(bf16[8,64,384]{2,1,0:T(8,128)(2,1)} %collective-permute-done.refs_0_.refs_4_), channel_id=1, source_target_pairs={{0,2},{1,3},{2,0},{3,1},{4,6},{5,7},{6,4},{7,5},{8,10},{9,11},{10,... | collective-permute-start | bytes 1179656 | tf_op jit(solution)/shard_map/ppermute | solution.py:294
  17.6 0.0 collective-permute-start.6
  17.6 0.0 collective-permute-done.4.refs_3_.refs_7_.refs_13_
  17.6 1.0 %copy-done = bf16[8,64,384]{2,1,0:T(8,128)(2,1)S(1)} copy-done((bf16[8,64,384]{2,1,0:T(8,128)(2,1)S(1)}, bf16[8,64,384]{2,1,0:T(8,128)(2,1)}, u32[]{:S(2)}) %copy-start) | copy-done | bytes 393240
  18.6 0.7 copy-done.4
  19.3 3.5 %ladder_0.1 = (bf16[32,64,2048]{2,1,0:T(8,128)(2,1)}, f32[2,8,128]{2,1,0:T(8,128)S(1)}) custom-call(s32[1]{0:T(128)} %bitcast.me_ref, s32[8]{0:T(128)S(1)} %copy-done.4, s32[32]{0:T(128)S(1)} %get-tuple-element.41.order_ref, s32[8]{0:T(128)S(1)} %get-tuple-element.42.size_ref, s32[8]{0:T(128)S(1)} %get-tuple-element.43.first_ref, ...), custom_call_target="tpu_custom_call", output_to_operand_aliasing={{0}: (8, {})} | custom-call | flops 402653184 | bytes 2097152 | tf_op jit(solution)/shard_map/ladder_0/pallas_call | solution.py:260
  22.8 0.0 copy-start.5
  22.8 6.0 %collective-permute-done.3.refs_0_.refs_6_ = bf16[8,64,384]{2,1,0:T(8,128)(2,1)} collective-permute-done((bf16[8,64,384]{2,1,0:T(8,128)(2,1)}, bf16[8,64,384]{2,1,0:T(8,128)(2,1)}, u32[]{:S(2)}, u32[]{:S(2)}) %collective-permute-start.3) | collective-permute-done | bytes 393248 | tf_op jit(solution)/shard_map/ppermute | solution.py:291
  28.8 0.0 collective-permute-done.5.refs_1_.refs_5_
  28.8 0.0 collective-permute-done.6.refs_2_.refs_6_
  28.9 0.5 collective-permute-start.10
  29.4 0.4 collective-permute-start.7
  29.7 1.5 %collective-permute-start.9 = (bf16[8,64,384]{2,1,0:T(8,128)(2,1)}, bf16[8,64,384]{2,1,0:T(8,128)(2,1)S(1)}, u32[]{:S(2)}, u32[]{:S(2)}) collective-permute-start(bf16[8,64,384]{2,1,0:T(8,128)(2,1)} %collective-permute-done.3.refs_0_.refs_6_), channel_id=1, source_target_pairs={{0,2},{1,3},{2,0},{3,1},{4,6},{5,7},{6,4},{7,5},{8,10},{9,11},{10,... | collective-permute-start | bytes 1179656 | tf_op jit(solution)/shard_map/ppermute | solution.py:294
  31.3 4.8 %ladder_1.1 = (bf16[32,64,2048]{2,1,0:T(8,128)(2,1)}, f32[2,8,128]{2,1,0:T(8,128)S(1)}) custom-call(s32[1]{0:T(128)} %bitcast.me_ref, s32[8]{0:T(128)S(1)} %copy-done.4, s32[32]{0:T(128)S(1)} %get-tuple-element.41.order_ref, s32[8]{0:T(128)S(1)} %get-tuple-element.42.size_ref, s32[8]{0:T(128)S(1)} %get-tuple-element.43.first_ref, ...), custom_call_target="tpu_custom_call", output_to_operand_aliasing={{0}: (8, {})} | custom-call | flops 402653184 | bytes 2097152 | tf_op jit(solution)/shard_map/ladder_1/pallas_call | solution.py:260
  36.1 6.3 %collective-permute-done.7.refs_0_ = bf16[8,64,384]{2,1,0:T(8,128)(2,1)S(1)} collective-permute-done((bf16[8,64,384]{2,1,0:T(8,128)(2,1)}, bf16[8,64,384]{2,1,0:T(8,128)(2,1)S(1)}, u32[]{:S(2)}, u32[]{:S(2)}) %collective-permute-start.7) | collective-permute-done | bytes 393248 | tf_op jit(solution)/shard_map/ppermute | solution.py:291
  42.5 0.5 collective-permute-start.14
  43.0 1.6 %collective-permute-start.12 = (bf16[4,64,384]{2,1,0:T(8,128)(2,1)S(1)}, bf16[4,64,384]{2,1,0:T(8,128)(2,1)S(1)}, u32[]{:S(2)}, u32[]{:S(2)}) collective-permute-start(bf16[4,64,384]{2,1,0:T(8,128)(2,1)S(1)} %slice.6), channel_id=1, source_target_pairs={{0,2},{1,3},{2,0},{3,1},{4,6},{5,7},{6,4},{7,5},{8,10},{9,11},{10,... | collective-permute-start | bytes 589832 | tf_op jit(solution)/shard_map/ppermute | solution.py:294
  44.6 4.7 %ladder_2.1 = (bf16[32,64,2048]{2,1,0:T(8,128)(2,1)}, f32[2,8,128]{2,1,0:T(8,128)S(1)}) custom-call(s32[1]{0:T(128)} %bitcast.me_ref, s32[8]{0:T(128)S(1)} %copy-done.5, s32[32]{0:T(128)S(1)} %get-tuple-element.41.order_ref, s32[8]{0:T(128)S(1)} %get-tuple-element.42.size_ref, s32[8]{0:T(128)S(1)} %get-tuple-element.43.first_ref, ...), custom_call_target="tpu_custom_call", output_to_operand_aliasing={{0}: (8, {})} | custom-call | flops 402653184 | bytes 2097152 | tf_op jit(solution)/shard_map/ladder_2/pallas_call | solution.py:260
  49.3 0.6 collective-permute-done.12.refs_1_
  49.9 3.0 %collective-permute-done.13.refs_2_ = bf16[4,64,384]{2,1,0:T(8,128)(2,1)S(1)} collective-permute-done((bf16[4,64,384]{2,1,0:T(8,128)(2,1)S(1)}, bf16[4,64,384]{2,1,0:T(8,128)(2,1)S(1)}, u32[]{:S(2)}, u32[]{:S(2)}) %collective-permute-start.13) | collective-permute-done | bytes 196640 | tf_op jit(solution)/shard_map/ppermute | solution.py:291
  52.9 0.5 collective-permute-start.16
  53.5 0.9 %collective-permute-done.15.refs_4_ = bf16[4,64,384]{2,1,0:T(8,128)(2,1)S(1)} collective-permute-done((bf16[4,64,384]{2,1,0:T(8,128)(2,1)S(1)}, bf16[4,64,384]{2,1,0:T(8,128)(2,1)S(1)}, u32[]{:S(2)}, u32[]{:S(2)}) %collective-permute-start.15) | collective-permute-done | bytes 196640 | tf_op jit(solution)/shard_map/ppermute | solution.py:294
  54.4 0.3 collective-permute-done.16.refs_5_
  54.7 4.8 %ladder_3.1 = (bf16[32,64,2048]{2,1,0:T(8,128)(2,1)}, f32[2,8,128]{2,1,0:T(8,128)S(1)}) custom-call(s32[1]{0:T(128)} %bitcast.me_ref, s32[8]{0:T(128)S(1)} %copy-done.5, s32[32]{0:T(128)S(1)} %get-tuple-element.41.order_ref, s32[8]{0:T(128)S(1)} %get-tuple-element.42.size_ref, s32[8]{0:T(128)S(1)} %get-tuple-element.43.first_ref, ...), custom_call_target="tpu_custom_call", output_to_operand_aliasing={{0}: (8, {})} | custom-call | flops 402653184 | bytes 2097152 | tf_op jit(solution)/shard_map/ladder_3/pallas_call | solution.py:260
  59.5 0.1 collective-permute-start.17
  59.6 0.8 %collective-permute-start.18 = (f32[2,8,128]{2,1,0:T(8,128)S(1)}, f32[2,8,128]{2,1,0:T(8,128)S(1)}, u32[]{:S(2)}, u32[]{:S(2)}) collective-permute-start(f32[2,8,128]{2,1,0:T(8,128)S(1)} %get-tuple-element.79), channel_id=1, source_target_pairs={{0,8},{1,9},{2,10},{3,11},{4,12},{5,13},{6,14},{7,15},{8,0},{9,1},... | collective-permute-start | bytes 24584 | tf_op jit(solution)/shard_map/ppermute | solution.py:333
  60.4 3.0 %collective-permute-start.19 = (f32[2,8,128]{2,1,0:T(8,128)S(1)}, f32[2,8,128]{2,1,0:T(8,128)S(1)}, u32[]{:S(2)}, u32[]{:S(2)}) collective-permute-start(f32[2,8,128]{2,1,0:T(8,128)S(1)} %get-tuple-element.79), channel_id=1, source_target_pairs={{0,12},{1,13},{2,14},{3,15},{4,0},{5,1},{6,2},{7,3},{8,4},{9,5},{1... | collective-permute-start | bytes 24584 | tf_op jit(solution)/shard_map/ppermute | solution.py:333
  63.4 1.6 %collective-permute-done.17 = f32[2,8,128]{2,1,0:T(8,128)S(1)} collective-permute-done((f32[2,8,128]{2,1,0:T(8,128)S(1)}, f32[2,8,128]{2,1,0:T(8,128)S(1)}, u32[]{:S(2)}, u32[]{:S(2)}) %collective-permute-start.17) | collective-permute-done | bytes 8224 | tf_op jit(solution)/shard_map/ppermute | solution.py:333
  65.0 0.6 collective-permute-done.19
  65.6 0.1 collective-permute-start.20
  65.7 0.9 %collective-permute-start.21 = (f32[2,8,128]{2,1,0:T(8,128)S(1)}, f32[2,8,128]{2,1,0:T(8,128)S(1)}, u32[]{:S(2)}, u32[]{:S(2)}) collective-permute-start(f32[2,8,128]{2,1,0:T(8,128)S(1)} %add_add_fusion), channel_id=1, source_target_pairs={{0,2},{1,3},{2,0},{3,1},{4,6},{5,7},{6,4},{7,5},{8,10},{9,11},{10,... | collective-permute-start | bytes 24584 | tf_op jit(solution)/shard_map/ppermute | solution.py:294
  66.6 0.8 %collective-permute-start.22 = (f32[2,8,128]{2,1,0:T(8,128)S(1)}, f32[2,8,128]{2,1,0:T(8,128)S(1)}, u32[]{:S(2)}, u32[]{:S(2)}) collective-permute-start(f32[2,8,128]{2,1,0:T(8,128)S(1)} %add_add_fusion), channel_id=1, source_target_pairs={{0,3},{1,2},{2,1},{3,0},{4,7},{5,6},{6,5},{7,4},{8,11},{9,10},{10,... | collective-permute-start | bytes 24584 | tf_op jit(solution)/shard_map/ppermute | solution.py:294
  67.4 1.9 %collective-permute-done.21 = f32[2,8,128]{2,1,0:T(8,128)S(1)} collective-permute-done((f32[2,8,128]{2,1,0:T(8,128)S(1)}, f32[2,8,128]{2,1,0:T(8,128)S(1)}, u32[]{:S(2)}, u32[]{:S(2)}) %collective-permute-start.21) | collective-permute-done | bytes 8224 | tf_op jit(solution)/shard_map/ppermute | solution.py:294
  69.4 0.3 collective-permute-done.22
  69.7 0.1 add_reduce_fusion
  69.8 0.5 add_sqrt_fusion
  (22 shorter events, 0.1 us)
Async XLA Ops:
  0.6 30.6 %copy-start.1 = (bf16[8,64,384]{2,1,0:T(8,128)(2,1)S(1)}, bf16[8,64,384]{2,1,0:T(8,128)(2,1)}, u32[]{:S(2)}) copy-start(bf16[8,64,384]{2,1,0:T(8,128)(2,1)} %refs_10_) | copy-start | bytes 1179652
  0.6 14.5 %collective-permute-start = (bf16[8,64,384]{2,1,0:T(8,128)(2,1)}, bf16[8,64,384]{2,1,0:T(8,128)(2,1)}, u32[]{:S(2)}, u32[]{:S(2)}) collective-permute-start(bf16[8,64,384]{2,1,0:T(8,128)(2,1)} %refs_10_), channel_id=1, source_target_pairs={{0,4},{1,5},{2,6},{3,7},{4,8},{5,9},{6,10},{7,11},{8,12},{9,13},{1... | collective-permute-start | bytes 1179656 | tf_op jit(solution)/shard_map/ppermute | solution.py:291
  3.7 11.5 %collective-permute-start.1 = (bf16[8,64,384]{2,1,0:T(8,128)(2,1)}, bf16[8,64,384]{2,1,0:T(8,128)(2,1)S(1)}, u32[]{:S(2)}, u32[]{:S(2)}) collective-permute-start(bf16[8,64,384]{2,1,0:T(8,128)(2,1)} %refs_10_), channel_id=1, source_target_pairs={{0,2},{1,3},{2,0},{3,1},{4,6},{5,7},{6,4},{7,5},{8,10},{9,11},{10,... | collective-permute-start | bytes 1179656 | tf_op jit(solution)/shard_map/ppermute | solution.py:294
  5.2 9.9 %collective-permute-start.2 = (bf16[8,64,384]{2,1,0:T(8,128)(2,1)}, bf16[8,64,384]{2,1,0:T(8,128)(2,1)S(1)}, u32[]{:S(2)}, u32[]{:S(2)}) collective-permute-start(bf16[8,64,384]{2,1,0:T(8,128)(2,1)} %refs_10_), channel_id=1, source_target_pairs={{0,1},{1,0},{2,3},{3,2},{4,5},{5,4},{6,7},{7,6},{8,9},{9,8},{10,11... | collective-permute-start | bytes 1179656 | tf_op jit(solution)/shard_map/ppermute | solution.py:294
  5.2 1.4 %copy-start.2 = (bf16[32,64,384]{2,1,0:T(8,128)(2,1)S(1)}, bf16[32,64,384]{2,1,0:T(8,128)(2,1)}, u32[]{:S(2)}) copy-start(bf16[32,64,384]{2,1,0:T(8,128)(2,1)} %v_ref.1) | copy-start | bytes 4718596
  6.7 0.7 copy-start.3
  7.3 0.7 copy-start.6
  15.2 2.4 %collective-permute-start.4 = (bf16[8,64,384]{2,1,0:T(8,128)(2,1)S(1)}, bf16[8,64,384]{2,1,0:T(8,128)(2,1)S(1)}, u32[]{:S(2)}, u32[]{:S(2)}) collective-permute-start(bf16[8,64,384]{2,1,0:T(8,128)(2,1)S(1)} %collective-permute-done.1.refs_1_.refs_5_.refs_11_), channel_id=1, source_target_pairs={{0,1},{1,0},{2,3},{3,2},{4,5},{5,4},{6,7},{7,6},{8,9},{9,8},{10,11... | collective-permute-start | bytes 1179656 | tf_op jit(solution)/shard_map/ppermute | solution.py:294
  15.2 13.6 %collective-permute-start.3 = (bf16[8,64,384]{2,1,0:T(8,128)(2,1)}, bf16[8,64,384]{2,1,0:T(8,128)(2,1)}, u32[]{:S(2)}, u32[]{:S(2)}) collective-permute-start(bf16[8,64,384]{2,1,0:T(8,128)(2,1)} %collective-permute-done.refs_0_.refs_4_), channel_id=1, source_target_pairs={{0,4},{1,5},{2,6},{3,7},{4,8},{5,9},{6,10},{7,11},{8,12},{9,13},{1... | collective-permute-start | bytes 1179656 | tf_op jit(solution)/shard_map/ppermute | solution.py:291
  16.1 12.7 %collective-permute-start.5 = (bf16[8,64,384]{2,1,0:T(8,128)(2,1)}, bf16[8,64,384]{2,1,0:T(8,128)(2,1)}, u32[]{:S(2)}, u32[]{:S(2)}) collective-permute-start(bf16[8,64,384]{2,1,0:T(8,128)(2,1)} %collective-permute-done.refs_0_.refs_4_), channel_id=1, source_target_pairs={{0,2},{1,3},{2,0},{3,1},{4,6},{5,7},{6,4},{7,5},{8,10},{9,11},{10,... | collective-permute-start | bytes 1179656 | tf_op jit(solution)/shard_map/ppermute | solution.py:294
  17.6 11.2 %collective-permute-start.6 = (bf16[8,64,384]{2,1,0:T(8,128)(2,1)}, bf16[8,64,384]{2,1,0:T(8,128)(2,1)}, u32[]{:S(2)}, u32[]{:S(2)}) collective-permute-start(bf16[8,64,384]{2,1,0:T(8,128)(2,1)} %collective-permute-done.refs_0_.refs_4_), channel_id=1, source_target_pairs={{0,1},{1,0},{2,3},{3,2},{4,5},{5,4},{6,7},{7,6},{8,9},{9,8},{10,11... | collective-permute-start | bytes 1179656 | tf_op jit(solution)/shard_map/ppermute | solution.py:294
  17.6 1.0 %copy-start = (bf16[8,64,384]{2,1,0:T(8,128)(2,1)S(1)}, bf16[8,64,384]{2,1,0:T(8,128)(2,1)}, u32[]{:S(2)}) copy-start(bf16[8,64,384]{2,1,0:T(8,128)(2,1)} %refs_10_) | copy-start | bytes 1179652
  18.6 0.7 copy-start.4
  22.8 21.8 %copy-start.5 = (s32[8]{0:T(128)S(1)}, s32[8]{0:T(128)}, u32[]{:S(2)}) copy-start(s32[8]{0:T(128)} %counts_ref.9) | copy-start | bytes 100
  28.8 2.4 %collective-permute-start.8 = (bf16[8,64,384]{2,1,0:T(8,128)(2,1)}, bf16[8,64,384]{2,1,0:T(8,128)(2,1)S(1)}, u32[]{:S(2)}, u32[]{:S(2)}) collective-permute-start(bf16[8,64,384]{2,1,0:T(8,128)(2,1)} %collective-permute-done.5.refs_1_.refs_5_), channel_id=1, source_target_pairs={{0,1},{1,0},{2,3},{3,2},{4,5},{5,4},{6,7},{7,6},{8,9},{9,8},{10,11... | collective-permute-start | bytes 1179656 | tf_op jit(solution)/shard_map/ppermute | solution.py:294
  28.9 7.3 %collective-permute-start.10 = (bf16[8,64,384]{2,1,0:T(8,128)(2,1)}, bf16[8,64,384]{2,1,0:T(8,128)(2,1)S(1)}, u32[]{:S(2)}, u32[]{:S(2)}) collective-permute-start(bf16[8,64,384]{2,1,0:T(8,128)(2,1)} %collective-permute-done.3.refs_0_.refs_6_), channel_id=1, source_target_pairs={{0,1},{1,0},{2,3},{3,2},{4,5},{5,4},{6,7},{7,6},{8,9},{9,8},{10,11... | collective-permute-start | bytes 1179656 | tf_op jit(solution)/shard_map/ppermute | solution.py:294
  29.4 13.1 %collective-permute-start.7 = (bf16[8,64,384]{2,1,0:T(8,128)(2,1)}, bf16[8,64,384]{2,1,0:T(8,128)(2,1)S(1)}, u32[]{:S(2)}, u32[]{:S(2)}) collective-permute-start(bf16[8,64,384]{2,1,0:T(8,128)(2,1)} %collective-permute-done.3.refs_0_.refs_6_), channel_id=1, source_target_pairs={{0,4},{1,5},{2,6},{3,7},{4,8},{5,9},{6,10},{7,11},{8,12},{9,13},{1... | collective-permute-start | bytes 1179656 | tf_op jit(solution)/shard_map/ppermute | solution.py:291
  29.7 12.7 %collective-permute-start.9 = (bf16[8,64,384]{2,1,0:T(8,128)(2,1)}, bf16[8,64,384]{2,1,0:T(8,128)(2,1)S(1)}, u32[]{:S(2)}, u32[]{:S(2)}) collective-permute-start(bf16[8,64,384]{2,1,0:T(8,128)(2,1)} %collective-permute-done.3.refs_0_.refs_6_), channel_id=1, source_target_pairs={{0,2},{1,3},{2,0},{3,1},{4,6},{5,7},{6,4},{7,5},{8,10},{9,11},{10,... | collective-permute-start | bytes 1179656 | tf_op jit(solution)/shard_map/ppermute | solution.py:294
  42.5 2.2 %collective-permute-start.11 = (bf16[8,64,384]{2,1,0:T(8,128)(2,1)S(1)}, bf16[8,64,384]{2,1,0:T(8,128)(2,1)S(1)}, u32[]{:S(2)}, u32[]{:S(2)}) collective-permute-start(bf16[8,64,384]{2,1,0:T(8,128)(2,1)S(1)} %collective-permute-done.9.refs_1_.refs_7_), channel_id=1, source_target_pairs={{0,1},{1,0},{2,3},{3,2},{4,5},{5,4},{6,7},{7,6},{8,9},{9,8},{10,11... | collective-permute-start | bytes 1179656 | tf_op jit(solution)/shard_map/ppermute | solution.py:294
  42.5 10.5 %collective-permute-start.14 = (bf16[8,64,384]{2,1,0:T(8,128)(2,1)S(1)}, bf16[8,64,384]{2,1,0:T(8,128)(2,1)S(1)}, u32[]{:S(2)}, u32[]{:S(2)}) collective-permute-start(bf16[8,64,384]{2,1,0:T(8,128)(2,1)S(1)} %collective-permute-done.7.refs_0_), channel_id=1, source_target_pairs={{0,1},{1,0},{2,3},{3,2},{4,5},{5,4},{6,7},{7,6},{8,9},{9,8},{10,11... | collective-permute-start | bytes 1179656 | tf_op jit(solution)/shard_map/ppermute | solution.py:294
  43.0 6.9 %collective-permute-start.12 = (bf16[4,64,384]{2,1,0:T(8,128)(2,1)S(1)}, bf16[4,64,384]{2,1,0:T(8,128)(2,1)S(1)}, u32[]{:S(2)}, u32[]{:S(2)}) collective-permute-start(bf16[4,64,384]{2,1,0:T(8,128)(2,1)S(1)} %slice.6), channel_id=1, source_target_pairs={{0,2},{1,3},{2,0},{3,1},{4,6},{5,7},{6,4},{7,5},{8,10},{9,11},{10,... | collective-permute-start | bytes 589832 | tf_op jit(solution)/shard_map/ppermute | solution.py:294
  44.6 8.3 %collective-permute-start.13 = (bf16[4,64,384]{2,1,0:T(8,128)(2,1)S(1)}, bf16[4,64,384]{2,1,0:T(8,128)(2,1)S(1)}, u32[]{:S(2)}, u32[]{:S(2)}) collective-permute-start(bf16[4,64,384]{2,1,0:T(8,128)(2,1)S(1)} %slice.7), channel_id=1, source_target_pairs={{0,4},{1,5},{2,6},{3,7},{4,8},{5,9},{6,10},{7,11},{8,12},{9,13},{1... | collective-permute-start | bytes 589832 | tf_op jit(solution)/shard_map/ppermute | solution.py:291
  52.9 1.4 %collective-permute-start.15 = (bf16[4,64,384]{2,1,0:T(8,128)(2,1)S(1)}, bf16[4,64,384]{2,1,0:T(8,128)(2,1)S(1)}, u32[]{:S(2)}, u32[]{:S(2)}) collective-permute-start(bf16[4,64,384]{2,1,0:T(8,128)(2,1)S(1)} %collective-permute-done.12.refs_1_), channel_id=1, source_target_pairs={{0,1},{1,0},{2,3},{3,2},{4,5},{5,4},{6,7},{7,6},{8,9},{9,8},{10,11... | collective-permute-start | bytes 589832 | tf_op jit(solution)/shard_map/ppermute | solution.py:294
  52.9 1.7 %collective-permute-start.16 = (bf16[4,64,384]{2,1,0:T(8,128)(2,1)S(1)}, bf16[4,64,384]{2,1,0:T(8,128)(2,1)S(1)}, u32[]{:S(2)}, u32[]{:S(2)}) collective-permute-start(bf16[4,64,384]{2,1,0:T(8,128)(2,1)S(1)} %collective-permute-done.13.refs_2_), channel_id=1, source_target_pairs={{0,1},{1,0},{2,3},{3,2},{4,5},{5,4},{6,7},{7,6},{8,9},{9,8},{10,11... | collective-permute-start | bytes 589832 | tf_op jit(solution)/shard_map/ppermute | solution.py:294
  59.5 5.5 %collective-permute-start.17 = (f32[2,8,128]{2,1,0:T(8,128)S(1)}, f32[2,8,128]{2,1,0:T(8,128)S(1)}, u32[]{:S(2)}, u32[]{:S(2)}) collective-permute-start(f32[2,8,128]{2,1,0:T(8,128)S(1)} %get-tuple-element.79), channel_id=1, source_target_pairs={{0,4},{1,5},{2,6},{3,7},{4,8},{5,9},{6,10},{7,11},{8,12},{9,13},{1... | collective-permute-start | bytes 24584 | tf_op jit(solution)/shard_map/ppermute | solution.py:333
  59.6 5.4 %collective-permute-start.18 = (f32[2,8,128]{2,1,0:T(8,128)S(1)}, f32[2,8,128]{2,1,0:T(8,128)S(1)}, u32[]{:S(2)}, u32[]{:S(2)}) collective-permute-start(f32[2,8,128]{2,1,0:T(8,128)S(1)} %get-tuple-element.79), channel_id=1, source_target_pairs={{0,8},{1,9},{2,10},{3,11},{4,12},{5,13},{6,14},{7,15},{8,0},{9,1},... | collective-permute-start | bytes 24584 | tf_op jit(solution)/shard_map/ppermute | solution.py:333
  60.4 5.2 %collective-permute-start.19 = (f32[2,8,128]{2,1,0:T(8,128)S(1)}, f32[2,8,128]{2,1,0:T(8,128)S(1)}, u32[]{:S(2)}, u32[]{:S(2)}) collective-permute-start(f32[2,8,128]{2,1,0:T(8,128)S(1)} %get-tuple-element.79), channel_id=1, source_target_pairs={{0,12},{1,13},{2,14},{3,15},{4,0},{5,1},{6,2},{7,3},{8,4},{9,5},{1... | collective-permute-start | bytes 24584 | tf_op jit(solution)/shard_map/ppermute | solution.py:333
  65.6 1.9 %collective-permute-start.20 = (f32[2,8,128]{2,1,0:T(8,128)S(1)}, f32[2,8,128]{2,1,0:T(8,128)S(1)}, u32[]{:S(2)}, u32[]{:S(2)}) collective-permute-start(f32[2,8,128]{2,1,0:T(8,128)S(1)} %add_add_fusion), channel_id=1, source_target_pairs={{0,1},{1,0},{2,3},{3,2},{4,5},{5,4},{6,7},{7,6},{8,9},{9,8},{10,11... | collective-permute-start | bytes 24584 | tf_op jit(solution)/shard_map/ppermute | solution.py:294
  65.7 3.7 %collective-permute-start.21 = (f32[2,8,128]{2,1,0:T(8,128)S(1)}, f32[2,8,128]{2,1,0:T(8,128)S(1)}, u32[]{:S(2)}, u32[]{:S(2)}) collective-permute-start(f32[2,8,128]{2,1,0:T(8,128)S(1)} %add_add_fusion), channel_id=1, source_target_pairs={{0,2},{1,3},{2,0},{3,1},{4,6},{5,7},{6,4},{7,5},{8,10},{9,11},{10,... | collective-permute-start | bytes 24584 | tf_op jit(solution)/shard_map/ppermute | solution.py:294
  66.6 3.1 %collective-permute-start.22 = (f32[2,8,128]{2,1,0:T(8,128)S(1)}, f32[2,8,128]{2,1,0:T(8,128)S(1)}, u32[]{:S(2)}, u32[]{:S(2)}) collective-permute-start(f32[2,8,128]{2,1,0:T(8,128)S(1)} %add_add_fusion), channel_id=1, source_target_pairs={{0,3},{1,2},{2,1},{3,0},{4,7},{5,6},{6,5},{7,4},{8,11},{9,10},{10,... | collective-permute-start | bytes 24584 | tf_op jit(solution)/shard_map/ppermute | solution.py:294

commit v6 on v5

v6 whole, which is shorter than its diff:
```python
import functools

import jax
import jax.numpy as jnp
from jax import lax
from jax.experimental import pallas as pl
from jax.experimental.pallas import tpu as pltpu
from jax.sharding import PartitionSpec as P

BATCH = 4
UNROLL = 4


def ring_of(depth):
    return [0, *range(1, depth, 2), *range(depth - 2 + depth % 2, 0, -2)]


def ring_place(z, depth):
    return jnp.where(z % 2 == 1, (z + 1) // 2, (depth - z // 2) % depth)


def ring_position(place, depth):
    return jnp.where(place <= depth // 2, jnp.maximum(2 * place - 1, 0), 2 * (depth - place))


def prepare_kernel(
    depth, shard_tiles,
    me_ref, counts_ref, irrep_ref, v_ref,
    res_ref, sorted_ref, gathered_ref, stats_ref, order_ref, begin_ref, item_ref,
    blank_ref, size_ref, first_ref, next_ref, cursor_ref, call_ref, sem, blank_sem,
):
    own_tiles = v_ref.shape[0]
    irreps = counts_ref.shape[0]
    rows = v_ref.shape[1]
    most = item_ref.shape[0] // 6
    blank_ref[...] = jnp.zeros(blank_ref.shape, blank_ref.dtype)
    group = blank_ref.shape[0]
    for l in range(0, own_tiles, group):
        pltpu.make_async_copy(blank_ref, res_ref.at[pl.ds(l, group)], blank_sem).start()

    for s in range(irreps):
        size_ref[s] = 0

    def count(l, carry):
        s = irrep_ref[l]
        size_ref[s] = size_ref[s] + 1
        return carry

    lax.fori_loop(0, own_tiles, count, 0)
    first = jnp.int32(0)
    for s in range(irreps):
        first_ref[s] = first
        next_ref[s] = first
        first = first + size_ref[s]

    def place(l, carry):
        s = irrep_ref[l]
        slot = next_ref[s]
        next_ref[s] = slot + 1
        order_ref[slot] = l
        pltpu.make_async_copy(v_ref.at[l], sorted_ref.at[slot], sem).start()
        return carry

    lax.fori_loop(0, own_tiles, place, 0)
    for buffer in (sorted_ref, gathered_ref):
        spare = jnp.zeros((BATCH, *buffer.shape[1:]), buffer.dtype)
        buffer[pl.ds(buffer.shape[0] - BATCH, BATCH)] = spare

    me = me_ref[0]
    z, y = me // 4, me // 2 % 2
    for part in range(2 * depth):
        lag = lax.rem(ring_place(z, depth) - ring_place(jnp.int32(part // 2), depth) + depth, depth)
        call_ref[part] = jnp.where(y == part % 2, jnp.maximum(lag - 1, 0), lag)
    for call in range(depth):
        cursor_ref[call] = 0

    def walk(visit):
        def symmetry(s, offset):
            tiles = counts_ref[s]
            batches = (size_ref[s] + BATCH - 1) // BATCH

            def block(j, carry):
                low = offset + j * BATCH
                high = offset + jnp.minimum(tiles, j * BATCH + BATCH) - 1
                call = jnp.maximum(
                    call_ref[low // (2 * shard_tiles)], call_ref[high // (2 * shard_tiles)]
                )
                visit(s, j, low, tiles, batches, call)
                return carry

            lax.fori_loop(0, (tiles + BATCH - 1) // BATCH, block, 0)
            return offset + tiles

        lax.fori_loop(0, irreps, symmetry, jnp.int32(0))

    def tally(s, j, low, tiles, batches, call):
        cursor_ref[call] = cursor_ref[call] + batches

    def write(n, slot, tile, block, members, limit, group):
        for field, value in enumerate((slot, tile, block, members, limit, group)):
            item_ref[field * most + n] = value

    def enter(s, j, low, tiles, batches, call):
        def one(i, n):
            write(
                n, first_ref[s] + i * BATCH, low, j,
                jnp.minimum(size_ref[s] - i * BATCH, BATCH), (tiles - j * BATCH) * rows, s,
            )
            return n + 1

        cursor_ref[call] = lax.fori_loop(0, batches, one, cursor_ref[call])

    walk(tally)
    begin = jnp.int32(0)
    for call in range(depth):
        begin_ref[call] = begin
        items = cursor_ref[call]
        cursor_ref[call] = begin
        begin = begin + (items + UNROLL - 1) // UNROLL * UNROLL
    begin_ref[depth] = begin
    walk(enter)
    for call in range(depth):
        def fill(n, carry):
            write(n, own_tiles, 0, 0, 0, 0, 0)
            return carry

        lax.fori_loop(cursor_ref[call], begin_ref[call + 1], fill, 0)

    shape = stats_ref.shape[1:]
    at_row = lax.broadcasted_iota(jnp.int32, shape, 0)
    at_lane = lax.broadcasted_iota(jnp.int32, shape, 1)
    sizes = jnp.zeros(shape, jnp.int32)
    for s in range(irreps):
        sizes = jnp.where((at_row == s) & (at_lane == 0), size_ref[s], sizes)
    stats_ref[0] = jnp.zeros(shape, jnp.float32)
    stats_ref[1] = sizes.astype(jnp.float32)
    pltpu.make_async_copy(v_ref, sorted_ref.at[pl.ds(0, own_tiles)], sem).wait()
    pltpu.make_async_copy(res_ref, res_ref, blank_sem).wait()


def prepare(me, counts, irrep, integrals, depth, shard_tiles):
    own_tiles, rows, width = integrals.shape
    irreps = counts.shape[0]
    capacity = shard_tiles * depth
    all_tiles = 4 * shard_tiles * depth
    most = (all_tiles // BATCH + irreps) * (own_tiles // BATCH) + depth * UNROLL
    smem = pl.BlockSpec(memory_space=pltpu.SMEM)
    vmem = pl.BlockSpec(memory_space=pltpu.VMEM)
    anywhere = pl.BlockSpec(memory_space=pl.ANY)
    return pl.pallas_call(
        functools.partial(prepare_kernel, depth, shard_tiles),
        out_shape=(
            jax.ShapeDtypeStruct((own_tiles, rows, capacity * rows), jnp.bfloat16),
            jax.ShapeDtypeStruct((own_tiles + BATCH, rows, width), integrals.dtype),
            jax.ShapeDtypeStruct((all_tiles + BATCH, rows, width), jnp.bfloat16),
            jax.ShapeDtypeStruct((2, irreps, 128), jnp.float32),
            jax.ShapeDtypeStruct((own_tiles,), jnp.int32),
            jax.ShapeDtypeStruct((depth + 1,), jnp.int32),
            jax.ShapeDtypeStruct((6 * most,), jnp.int32),
        ),
        in_specs=[smem, smem, smem, anywhere],
        out_specs=(anywhere, vmem, vmem, vmem, smem, smem, smem),
        scratch_shapes=[
            pltpu.VMEM((2, rows, capacity * rows), jnp.bfloat16),
            pltpu.SMEM((irreps,), jnp.int32),
            pltpu.SMEM((irreps,), jnp.int32),
            pltpu.SMEM((irreps,), jnp.int32),
            pltpu.SMEM((depth,), jnp.int32),
            pltpu.SMEM((2 * depth,), jnp.int32),
            pltpu.SemaphoreType.DMA,
            pltpu.SemaphoreType.DMA,
        ],
        compiler_params=pltpu.CompilerParams(vmem_limit_bytes=32 * 1024 * 1024),
        cost_estimate=pl.CostEstimate(
            flops=0, bytes_accessed=2 * own_tiles * rows * capacity * rows, transcendentals=0
        ),
        name="prepare",
    )(me, counts, irrep, integrals)


def ladder_kernel(
    call, depth, shard_tiles, layout,
    me_ref, order_ref, begin_ref, item_ref, stats_in_ref, v_ref, res_in_ref, gathered_in_ref, *refs,
):
    del res_in_ref, gathered_in_ref
    fresh, refs = refs[:len(layout)], refs[len(layout):]
    res_hbm, gathered_ref, stats_ref, o_buf, acc_ref, a_sem, o_sem = refs
    rows, width = v_ref.shape[1:]
    side = BATCH * rows
    most = item_ref.shape[0] // 6

    me = me_ref[0]
    z, y, core = me // 4, me // 2 % 2, me % 2
    arrivals = []
    for source, (lag, other_y, other_core, tile) in zip(fresh, layout):
        at = ring_position(lax.rem(ring_place(z, depth) - lag + depth, depth), depth)
        own_y = (1 - y) if other_y else y
        own_core = (1 - core) if other_core else core
        arrivals.append(pltpu.make_async_copy(
            source,
            gathered_ref.at[
                pl.ds(((at * 2 + own_y) * 2 + own_core) * shard_tiles + tile, source.shape[0])
            ],
            a_sem.at[len(arrivals)],
        ))
    for arrival in arrivals:
        arrival.start()
    acc_ref[...] = jnp.zeros(acc_ref.shape, acc_ref.dtype)
    for arrival in arrivals:
        arrival.wait()

    col_at = lax.broadcasted_iota(jnp.int32, (1, side), 1)

    def item(n):
        return [item_ref[field * most + n] for field in range(6)]

    def product(n):
        slot, tile, block, members, limit, group = item(n)
        left = v_ref[pl.ds(slot, BATCH)].reshape(side, width)
        right = gathered_ref[pl.ds(tile, BATCH)].reshape(side, width)
        values = lax.dot_general(
            left, right, (((1,), (1,)), ((), ())), preferred_element_type=jnp.float32
        )
        values = jnp.where(col_at < limit, values, 0.0).reshape(BATCH, rows, side)
        columns = pl.ds(pl.multiple_of(block * side, side), side)
        o_buf[pl.ds(slot, BATCH), :, columns] = values.astype(jnp.bfloat16)
        squares = jnp.sum((values * values).reshape(BATCH, rows // 8, 8, side), axis=1)
        total = jnp.zeros((8, side), jnp.float32)
        for t in range(BATCH):
            total = total + jnp.where(t < members, squares[t], 0.0)
        acc_ref[group] += total

    def send(n, started):
        slot, _, block, members, _, _ = item(n)
        columns = pl.ds(pl.multiple_of(block * side, side), side)

        def one(t, carry):
            pltpu.make_async_copy(
                o_buf.at[slot + t, :, columns],
                res_hbm.at[order_ref[slot + t], :, columns],
                o_sem,
            ).start()
            return carry

        lax.fori_loop(0, members, one, 0)
        return started + members

    def several(u, started):
        for n in range(UNROLL):
            product(u * UNROLL + n)
        for n in range(UNROLL):
            started = send(u * UNROLL + n, started)
        return started

    started = lax.fori_loop(
        begin_ref[call] // UNROLL, begin_ref[call + 1] // UNROLL, several, jnp.int32(0)
    )
    sums = jnp.sum(acc_ref[...], axis=1)
    sums = sum(sums[:, k:k + 128] for k in range(0, side, 128))
    stats_ref[0] = stats_in_ref[0] + sums
    stats_ref[1] = stats_in_ref[1]

    def finish(n, carry):
        pltpu.make_async_copy(
            o_buf.at[0, :, pl.ds(0, side)], res_hbm.at[0, :, pl.ds(0, side)], o_sem
        ).wait()
        return carry

    lax.fori_loop(0, started, finish, 0)


def ladder(call, depth, shard_tiles, me, plan, state, fresh, layout):
    ordered, order, begin, items = plan
    residual, gathered, stats = state
    slots, rows, width = ordered.shape
    smem = pl.BlockSpec(memory_space=pltpu.SMEM)
    vmem = pl.BlockSpec(memory_space=pltpu.VMEM)
    anywhere = pl.BlockSpec(memory_space=pl.ANY)
    out_bytes = 2 * slots * residual[0].size
    tiles = sum(source.shape[0] for source in fresh)
    return pl.pallas_call(
        functools.partial(ladder_kernel, call, depth, shard_tiles, layout),
        out_shape=tuple(jax.ShapeDtypeStruct(x.shape, x.dtype) for x in state),
        in_specs=[smem] * 4 + [vmem] * 2 + [anywhere, vmem] + [anywhere] * len(fresh),
        out_specs=(anywhere, vmem, vmem),
        scratch_shapes=[
            pltpu.VMEM((slots, rows, residual.shape[2]), jnp.bfloat16),
            pltpu.VMEM((stats.shape[1], 8, BATCH * rows), jnp.float32),
            pltpu.SemaphoreType.DMA((len(fresh),)),
            pltpu.SemaphoreType.DMA,
        ],
        input_output_aliases={6: 0, 7: 1},
        compiler_params=pltpu.CompilerParams(
            vmem_limit_bytes=out_bytes + 2 * ordered.size + 4 * gathered.size + 6 * 1024 * 1024
        ),
        cost_estimate=pl.CostEstimate(
            flops=residual.size * width * tiles // (4 * shard_tiles * depth),
            bytes_accessed=2 * residual.size * tiles // (4 * shard_tiles * depth),
            transcendentals=0,
        ),
        name=f"ladder_{call}",
    )(me, order, begin, items, stats, ordered, residual, gathered, *fresh)


def per_device(amplitudes, ij_counts, integrals, ab_irrep):
    shard_tiles, rows, _ = amplitudes.shape
    devices = lax.axis_size("vir")
    depth = devices // 4
    me = lax.axis_index("vir").astype(jnp.int32).reshape(1)
    ring = ring_of(depth)
    hop = []
    for d in range(devices):
        following = ring[(ring.index(d // 4) + 1) % depth]
        hop.append((d, following * 4 + d % 4))

    def shift_z(x):
        return lax.ppermute(x, "vir", hop)

    def swap(x, bits):
        return lax.ppermute(x, "vir", [(d, d ^ bits) for d in range(devices)])

    residual, ordered, gathered, stats, order, begin, items = prepare(
        me, ij_counts, ab_irrep, integrals, depth, shard_tiles
    )
    plan = (ordered, order, begin, items)
    state = (residual, gathered, stats)
    half = shard_tiles // 2

    a, b, c = amplitudes, None, None
    early, early_layout = (), ()
    for k in range(depth):
        if k:
            a, b, c, *state = lax.optimization_barrier((a, b, c, *state))
        if k < depth - 1:
            following = shift_z(a)
            there = swap(a, 2)
        else:
            there = (swap(a[:half], 2), shift_z(b[half:]))
        across = swap(a, 1)
        if k == 0:
            early, early_layout = (a, across), ((0, 0, 0, 0), (0, 0, 1, 0))
        else:
            state = ladder(
                k - 1, depth, shard_tiles, me, plan, state,
                (*early, b, swap(b, 1), a, across),
                (*early_layout, (k - 1, 1, 0, 0), (k - 1, 1, 1, 0), (k, 0, 0, 0), (k, 0, 1, 0)),
            )
            early, early_layout = (), ()
        a, b, c = following, there, across
    *b, residual, gathered, stats = lax.optimization_barrier((*b, *state))
    state = ladder(
        depth - 1, depth, shard_tiles, me, plan, (residual, gathered, stats),
        (*b, *(swap(piece, 1) for piece in b)),
        tuple((depth - 1, 1, core, tile) for core in range(2) for tile in (0, half)),
    )
    residual, _, stats = state

    stats = sum([swap(stats, bits) for bits in (1, 2, 3)], stats)
    bits = 4
    while bits < devices:
        stats = stats + swap(stats, bits)
        bits *= 2
    irrep_sums, ab_counts = jnp.sum(stats, axis=2)
    entries = ab_counts * ij_counts.astype(jnp.float32) * float(rows * rows)
    return residual, jnp.sqrt(irrep_sums / entries + 1e-06)


def solution(mesh):
    in_specs = (
        P(("groups", "vir"), None, None),
        P("groups"),
        P(("groups", "vir"), None, None),
        P(("groups", "vir")),
    )
    out_specs = (P(("groups", "vir"), None, None), P("groups"))
    return jax.shard_map(
        per_device, mesh=mesh, in_specs=in_specs, out_specs=out_specs, check_vma=False
    )
```

time: 70.7 us -> 70.6 us (level)
  waiting for transfers between devices: 24.4 us -> 21.6 us
  starting transfers between devices: 17.8 us -> 20.4 us
  Pallas kernels: 22.4 us -> 23.8 us
    ppermute x7 -> x4, waiting for transfers between devices: 20.3 us -> 4.26 us  [shift_z(): return lax.ppermute(x, 'vir', hop)]
    ppermute x16 -> x18, waiting for transfers between devices: 4.09 us -> 17.3 us  [swap(): return lax.ppermute(x, 'vir', [(d, d ^ bits) for d in range(devices)])]
    ppermute x16 -> x18, starting transfers between devices: 9.54 us -> 14.4 us  [swap(): return lax.ppermute(x, 'vir', [(d, d ^ bits) for d in range(devices)])]
    ppermute x7 -> x4, starting transfers between devices: 8.23 us -> 5.98 us  [shift_z(): return lax.ppermute(x, 'vir', hop)]
    pallas_call x5, Pallas kernels: 22.4 us -> 23.8 us  [the longest x4 17.2 us: ladder(): pl.pallas_call(functools.partial(ladder_kernel, call, depth, shard_tiles,...]
    unnamed x14 -> x8, local copies, waits for them, and re-layouts: 4.38 us -> 3.71 us
  transfers between devices with their start and end apart: 23 -> 22, of which waited for: 11 -> 13; matrix products, arithmetic and copies ran while one was open for 0% -> 0% of each run, Pallas kernels for 25% -> 28%
where the time goes in v6:
time: 70.6 us; the launch traced here: 70.8 us
  Pallas kernels  23.8 us (34%)
  waiting for transfers between devices  21.6 us (31%)
  starting transfers between devices  20.4 us (29%)
  local copies, waits for them, and re-layouts  3.75 us (5%)
  between operations  0.72 us (1%)
    ppermute x18, waiting for transfers between devices, swap(): return lax.ppermute(x, 'vir', [(d, d ^ bits) for d in range(devices)])  17.3 us
    pallas_call x4, Pallas kernels, ladder(): pl.pallas_call(functools.partial(ladder_kernel, call, depth, shard_tiles,...  17.2 us
    ppermute x18, starting transfers between devices, swap(): return lax.ppermute(x, 'vir', [(d, d ^ bits) for d in range(devices)])  14.4 us
    pallas_call x1, Pallas kernels, prepare(): pl.pallas_call(functools.partial(prepare_kernel, depth, shard_tiles), out...  6.6 us
    ppermute x4, starting transfers between devices, shift_z(): return lax.ppermute(x, 'vir', hop)  5.98 us
    ppermute x4, waiting for transfers between devices, shift_z(): return lax.ppermute(x, 'vir', hop)  4.26 us
    unnamed x8, local copies, waits for them, and re-layouts  3.71 us
  transfers between devices with their start and end apart: 22, of which 13 were waited for; matrix products, arithmetic and copies ran while one was open for 0% of the time, Pallas kernels for 28%

profile of v6, /device:TPU:0, one launch (start us, length us, event | category | flops | bytes accessed | tf_op | source)
XLA Modules:
  0.0 70.8 jit_solution(10222282817800747384)
XLA Ops:
  0.6 3.0 %collective-permute-start.1 = (bf16[8,64,384]{2,1,0:T(8,128)(2,1)}, bf16[8,64,384]{2,1,0:T(8,128)(2,1)S(1)}, u32[]{:S(2)}, u32[]{:S(2)}) collective-permute-start(bf16[8,64,384]{2,1,0:T(8,128)(2,1)} %refs_0_.1), channel_id=1, source_target_pairs={{0,2},{1,3},{2,0},{3,1},{4,6},{5,7},{6,4},{7,5},{8,10},{9,11},{10,... | collective-permute-start | bytes 1179656 | tf_op jit(solution)/shard_map/ppermute | solution.py:320
  3.7 1.6 %collective-permute-start = (bf16[8,64,384]{2,1,0:T(8,128)(2,1)}, bf16[8,64,384]{2,1,0:T(8,128)(2,1)S(1)}, u32[]{:S(2)}, u32[]{:S(2)}) collective-permute-start(bf16[8,64,384]{2,1,0:T(8,128)(2,1)} %refs_0_.1), channel_id=1, source_target_pairs={{0,4},{1,5},{2,6},{3,7},{4,12},{5,13},{6,14},{7,15},{8,0},{9,1},{1... | collective-permute-start | bytes 1179656 | tf_op jit(solution)/shard_map/ppermute | solution.py:317
  5.2 1.4 %copy-done = bf16[32,64,384]{2,1,0:T(8,128)(2,1)S(1)} copy-done((bf16[32,64,384]{2,1,0:T(8,128)(2,1)S(1)}, bf16[32,64,384]{2,1,0:T(8,128)(2,1)}, u32[]{:S(2)}) %copy-start) | copy-done | bytes 1572888
  6.7 0.7 copy-done.2
  7.3 0.7 copy-done.3
  8.0 6.6 %prepare.1 = (bf16[32,64,2048]{2,1,0:T(8,128)(2,1)}, bf16[36,64,384]{2,1,0:T(8,128)(2,1)S(1)}, bf16[132,64,384]{2,1,0:T(8,128)(2,1)S(1)}, f32[2,8,128]{2,1,0:T(8...) custom-call(s32[1]{0:T(128)} %bitcast.me_ref, s32[8]{0:T(128)S(1)} %copy-done.2, s32[32]{0:T(128)S(1)} %copy-done.3, ...), custom_call_target="tpu_custom_call" | custom-call | bytes 8388608 | tf_op jit(solution)/shard_map/prepare/pallas_call | solution.py:150
  14.6 0.8 %collective-permute-done.refs_4_ = bf16[8,64,384]{2,1,0:T(8,128)(2,1)S(1)} collective-permute-done((bf16[8,64,384]{2,1,0:T(8,128)(2,1)}, bf16[8,64,384]{2,1,0:T(8,128)(2,1)S(1)}, u32[]{:S(2)}, u32[]{:S(2)}) %collective-permute-start) | collective-permute-done | bytes 393248 | tf_op jit(solution)/shard_map/ppermute | solution.py:317
  15.4 0.0 collective-permute-done.2.refs_1_
  15.4 0.0 collective-permute-start.6
  15.4 0.5 collective-permute-start.5
  15.9 0.5 collective-permute-start.4
  16.3 2.1 %collective-permute-start.3 = (bf16[8,64,384]{2,1,0:T(8,128)(2,1)S(1)}, bf16[8,64,384]{2,1,0:T(8,128)(2,1)S(1)}, u32[]{:S(2)}, u32[]{:S(2)}) collective-permute-start(bf16[8,64,384]{2,1,0:T(8,128)(2,1)S(1)} %collective-permute-done.refs_4_), channel_id=1, source_target_pairs={{0,4},{1,5},{2,6},{3,7},{4,12},{5,13},{6,14},{7,15},{8,0},{9,1},{1... | collective-permute-start | bytes 1179656 | tf_op jit(solution)/shard_map/ppermute | solution.py:317
  18.4 0.0 collective-permute-done.6.refs_3_
  18.4 1.0 %copy-done.1 = bf16[8,64,384]{2,1,0:T(8,128)(2,1)S(1)} copy-done((bf16[8,64,384]{2,1,0:T(8,128)(2,1)S(1)}, bf16[8,64,384]{2,1,0:T(8,128)(2,1)}, u32[]{:S(2)}) %copy-start.1) | copy-done | bytes 393240
  19.4 4.3 %ladder_0.1 = (bf16[32,64,2048]{2,1,0:T(8,128)(2,1)}, bf16[132,64,384]{2,1,0:T(8,128)(2,1)S(1)}, f32[2,8,128]{2,1,0:T(8,128)S(1)}) custom-call(s32[1]{0:T(128)} %bitcast.me_ref, s32[32]{0:T(128)S(1)} %get-tuple-element.40.order_ref, s32[5]{0:T(128)S(1)} %get-tuple-element.41.begin_ref, ...), custom_call_target="tpu_custom_call", output_to_operand_aliasing={{0}: (6, {}), {1}: (7, {})} | custom-call | flops 603979776 | bytes 3145728 | tf_op jit(solution)/shard_map/ladder_0/pallas_call | solution.py:281
  23.7 3.2 %collective-permute-done.4.refs_0_ = bf16[8,64,384]{2,1,0:T(8,128)(2,1)S(1)} collective-permute-done((bf16[8,64,384]{2,1,0:T(8,128)(2,1)S(1)}, bf16[8,64,384]{2,1,0:T(8,128)(2,1)S(1)}, u32[]{:S(2)}, u32[]{:S(2)}) %collective-permute-start.4) | collective-permute-done | bytes 393248 | tf_op jit(solution)/shard_map/ppermute | solution.py:320
  26.9 1.1 %collective-permute-done.3.refs_2_ = bf16[8,64,384]{2,1,0:T(8,128)(2,1)S(1)} collective-permute-done((bf16[8,64,384]{2,1,0:T(8,128)(2,1)S(1)}, bf16[8,64,384]{2,1,0:T(8,128)(2,1)S(1)}, u32[]{:S(2)}, u32[]{:S(2)}) %collective-permute-start.3) | collective-permute-done | bytes 393248 | tf_op jit(solution)/shard_map/ppermute | solution.py:317
  28.0 0.0 collective-permute-start.10
  28.0 0.5 collective-permute-start.9
  28.5 1.6 %collective-permute-start.8 = (bf16[8,64,384]{2,1,0:T(8,128)(2,1)S(1)}, bf16[8,64,384]{2,1,0:T(8,128)(2,1)S(1)}, u32[]{:S(2)}, u32[]{:S(2)}) collective-permute-start(bf16[8,64,384]{2,1,0:T(8,128)(2,1)S(1)} %collective-permute-done.3.refs_2_), channel_id=1, source_target_pairs={{0,2},{1,3},{2,0},{3,1},{4,6},{5,7},{6,4},{7,5},{8,10},{9,11},{10,... | collective-permute-start | bytes 1179656 | tf_op jit(solution)/shard_map/ppermute | solution.py:320
  30.1 1.5 %collective-permute-start.7 = (bf16[8,64,384]{2,1,0:T(8,128)(2,1)S(1)}, bf16[8,64,384]{2,1,0:T(8,128)(2,1)S(1)}, u32[]{:S(2)}, u32[]{:S(2)}) collective-permute-start(bf16[8,64,384]{2,1,0:T(8,128)(2,1)S(1)} %collective-permute-done.3.refs_2_), channel_id=1, source_target_pairs={{0,4},{1,5},{2,6},{3,7},{4,12},{5,13},{6,14},{7,15},{8,0},{9,1},{1... | collective-permute-start | bytes 1179656 | tf_op jit(solution)/shard_map/ppermute | solution.py:317
  31.6 3.4 %ladder_1.1 = (bf16[32,64,2048]{2,1,0:T(8,128)(2,1)}, bf16[132,64,384]{2,1,0:T(8,128)(2,1)S(1)}, f32[2,8,128]{2,1,0:T(8,128)S(1)}) custom-call(s32[1]{0:T(128)} %bitcast.me_ref, s32[32]{0:T(128)S(1)} %get-tuple-element.40.order_ref, s32[5]{0:T(128)S(1)} %get-tuple-element.41.begin_ref, ...), custom_call_target="tpu_custom_call", output_to_operand_aliasing={{0}: (6, {}), {1}: (7, {})} | custom-call | flops 402653184 | bytes 2097152 | tf_op jit(solution)/shard_map/ladder_1/pallas_call | solution.py:281
  35.0 4.6 %collective-permute-done.8.refs_0_ = bf16[8,64,384]{2,1,0:T(8,128)(2,1)S(1)} collective-permute-done((bf16[8,64,384]{2,1,0:T(8,128)(2,1)S(1)}, bf16[8,64,384]{2,1,0:T(8,128)(2,1)S(1)}, u32[]{:S(2)}, u32[]{:S(2)}) %collective-permute-start.8) | collective-permute-done | bytes 393248 | tf_op jit(solution)/shard_map/ppermute | solution.py:320
  39.5 2.2 %collective-permute-done.7.refs_2_ = bf16[8,64,384]{2,1,0:T(8,128)(2,1)S(1)} collective-permute-done((bf16[8,64,384]{2,1,0:T(8,128)(2,1)S(1)}, bf16[8,64,384]{2,1,0:T(8,128)(2,1)S(1)}, u32[]{:S(2)}, u32[]{:S(2)}) %collective-permute-start.7) | collective-permute-done | bytes 393248 | tf_op jit(solution)/shard_map/ppermute | solution.py:317
  41.7 0.0 collective-permute-start.14
  41.7 0.5 collective-permute-start.13
  42.3 0.8 %collective-permute-start.12 = (bf16[4,64,384]{2,1,0:T(8,128)(2,1)S(1)}, bf16[4,64,384]{2,1,0:T(8,128)(2,1)S(1)}, u32[]{:S(2)}, u32[]{:S(2)}) collective-permute-start(bf16[4,64,384]{2,1,0:T(8,128)(2,1)S(1)} %slice.7), channel_id=1, source_target_pairs={{0,4},{1,5},{2,6},{3,7},{4,12},{5,13},{6,14},{7,15},{8,0},{9,1},{1... | collective-permute-start | bytes 589832 | tf_op jit(solution)/shard_map/ppermute | solution.py:317
  43.1 0.5 collective-permute-start.11
  43.6 0.0 collective-permute-done.14.refs_3_
  43.6 0.4 collective-permute-done.13.refs_1_
  44.0 5.8 %ladder_2.1 = (bf16[32,64,2048]{2,1,0:T(8,128)(2,1)}, bf16[132,64,384]{2,1,0:T(8,128)(2,1)S(1)}, f32[2,8,128]{2,1,0:T(8,128)S(1)}) custom-call(s32[1]{0:T(128)} %bitcast.me_ref, s32[32]{0:T(128)S(1)} %get-tuple-element.40.order_ref, s32[5]{0:T(128)S(1)} %get-tuple-element.41.begin_ref, ...), custom_call_target="tpu_custom_call", output_to_operand_aliasing={{0}: (6, {}), {1}: (7, {})} | custom-call | flops 402653184 | bytes 2097152 | tf_op jit(solution)/shard_map/ladder_2/pallas_call | solution.py:281
  49.8 0.2 collective-permute-done.12.refs_1_
  50.0 0.0 collective-permute-done.11.refs_0_
  50.0 0.5 collective-permute-start.16
  50.5 0.9 %collective-permute-done.15.refs_2_ = bf16[4,64,384]{2,1,0:T(8,128)(2,1)S(1)} collective-permute-done((bf16[4,64,384]{2,1,0:T(8,128)(2,1)S(1)}, bf16[4,64,384]{2,1,0:T(8,128)(2,1)S(1)}, u32[]{:S(2)}, u32[]{:S(2)}) %collective-permute-start.15) | collective-permute-done | bytes 196640 | tf_op jit(solution)/shard_map/ppermute | solution.py:320
  51.5 0.3 collective-permute-done.16.refs_3_
  51.8 3.7 %ladder_3.1 = (bf16[32,64,2048]{2,1,0:T(8,128)(2,1)}, bf16[132,64,384]{2,1,0:T(8,128)(2,1)S(1)}, f32[2,8,128]{2,1,0:T(8,128)S(1)}) custom-call(s32[1]{0:T(128)} %bitcast.me_ref, s32[32]{0:T(128)S(1)} %get-tuple-element.40.order_ref, s32[5]{0:T(128)S(1)} %get-tuple-element.41.begin_ref, ...), custom_call_target="tpu_custom_call", output_to_operand_aliasing={{0}: (6, {}), {1}: (7, {})} | custom-call | flops 201326592 | bytes 1048576 | tf_op jit(solution)/shard_map/ladder_3/pallas_call | solution.py:281
  55.4 0.3 collective-permute-start.19
  55.7 1.6 %collective-permute-start.18 = (f32[2,8,128]{2,1,0:T(8,128)S(1)}, f32[2,8,128]{2,1,0:T(8,128)S(1)}, u32[]{:S(2)}, u32[]{:S(2)}) collective-permute-start(f32[2,8,128]{2,1,0:T(8,128)S(1)} %get-tuple-element.77), channel_id=1, source_target_pairs={{0,2},{1,3},{2,0},{3,1},{4,6},{5,7},{6,4},{7,5},{8,10},{9,11},{10,... | collective-permute-start | bytes 24584 | tf_op jit(solution)/shard_map/ppermute | solution.py:320
  57.3 0.1 collective-permute-start.17
  57.4 1.2 %collective-permute-done.19 = f32[2,8,128]{2,1,0:T(8,128)S(1)} collective-permute-done((f32[2,8,128]{2,1,0:T(8,128)S(1)}, f32[2,8,128]{2,1,0:T(8,128)S(1)}, u32[]{:S(2)}, u32[]{:S(2)}) %collective-permute-start.19) | collective-permute-done | bytes 8224 | tf_op jit(solution)/shard_map/ppermute | solution.py:320
  58.6 0.8 %collective-permute-done.18 = f32[2,8,128]{2,1,0:T(8,128)S(1)} collective-permute-done((f32[2,8,128]{2,1,0:T(8,128)S(1)}, f32[2,8,128]{2,1,0:T(8,128)S(1)}, u32[]{:S(2)}, u32[]{:S(2)}) %collective-permute-start.18) | collective-permute-done | bytes 8224 | tf_op jit(solution)/shard_map/ppermute | solution.py:320
  59.4 4.7 %collective-permute-start.20 = (f32[2,8,128]{2,1,0:T(8,128)S(1)}, f32[2,8,128]{2,1,0:T(8,128)S(1)}, u32[]{:S(2)}, u32[]{:S(2)}) collective-permute-start(f32[2,8,128]{2,1,0:T(8,128)S(1)} %add_add_fusion), channel_id=1, source_target_pairs={{0,4},{1,5},{2,6},{3,7},{4,0},{5,1},{6,2},{7,3},{8,12},{9,13},{10,... | collective-permute-start | bytes 24584 | tf_op jit(solution)/shard_map/ppermute | solution.py:320
  64.0 1.6 %collective-permute-done.20 = f32[2,8,128]{2,1,0:T(8,128)S(1)} collective-permute-done((f32[2,8,128]{2,1,0:T(8,128)S(1)}, f32[2,8,128]{2,1,0:T(8,128)S(1)}, u32[]{:S(2)}, u32[]{:S(2)}) %collective-permute-start.20) | collective-permute-done | bytes 8224 | tf_op jit(solution)/shard_map/ppermute | solution.py:320
  65.7 0.2 collective-permute-start.21
  65.9 4.4 %collective-permute-done.21 = f32[2,8,128]{2,1,0:T(8,128)S(1)} collective-permute-done((f32[2,8,128]{2,1,0:T(8,128)S(1)}, f32[2,8,128]{2,1,0:T(8,128)S(1)}, u32[]{:S(2)}, u32[]{:S(2)}) %collective-permute-start.21) | collective-permute-done | bytes 8224 | tf_op jit(solution)/shard_map/ppermute | solution.py:320
  70.2 0.1 add_reduce_fusion
  70.3 0.5 add_sqrt_fusion
  (15 shorter events, 0.1 us)
Async XLA Ops:
  0.6 13.9 %collective-permute-start.1 = (bf16[8,64,384]{2,1,0:T(8,128)(2,1)}, bf16[8,64,384]{2,1,0:T(8,128)(2,1)S(1)}, u32[]{:S(2)}, u32[]{:S(2)}) collective-permute-start(bf16[8,64,384]{2,1,0:T(8,128)(2,1)} %refs_0_.1), channel_id=1, source_target_pairs={{0,2},{1,3},{2,0},{3,1},{4,6},{5,7},{6,4},{7,5},{8,10},{9,11},{10,... | collective-permute-start | bytes 1179656 | tf_op jit(solution)/shard_map/ppermute | solution.py:320
  3.7 11.7 %collective-permute-start = (bf16[8,64,384]{2,1,0:T(8,128)(2,1)}, bf16[8,64,384]{2,1,0:T(8,128)(2,1)S(1)}, u32[]{:S(2)}, u32[]{:S(2)}) collective-permute-start(bf16[8,64,384]{2,1,0:T(8,128)(2,1)} %refs_0_.1), channel_id=1, source_target_pairs={{0,4},{1,5},{2,6},{3,7},{4,12},{5,13},{6,14},{7,15},{8,0},{9,1},{1... | collective-permute-start | bytes 1179656 | tf_op jit(solution)/shard_map/ppermute | solution.py:317
  5.2 10.1 %collective-permute-start.2 = (bf16[8,64,384]{2,1,0:T(8,128)(2,1)}, bf16[8,64,384]{2,1,0:T(8,128)(2,1)S(1)}, u32[]{:S(2)}, u32[]{:S(2)}) collective-permute-start(bf16[8,64,384]{2,1,0:T(8,128)(2,1)} %refs_0_.1), channel_id=1, source_target_pairs={{0,1},{1,0},{2,3},{3,2},{4,5},{5,4},{6,7},{7,6},{8,9},{9,8},{10,11... | collective-permute-start | bytes 1179656 | tf_op jit(solution)/shard_map/ppermute | solution.py:320
  5.2 1.4 %copy-start = (bf16[32,64,384]{2,1,0:T(8,128)(2,1)S(1)}, bf16[32,64,384]{2,1,0:T(8,128)(2,1)}, u32[]{:S(2)}) copy-start(bf16[32,64,384]{2,1,0:T(8,128)(2,1)} %v_ref.1) | copy-start | bytes 4718596
  6.7 0.7 copy-start.2
  7.3 0.7 copy-start.3
  15.4 3.1 %collective-permute-start.6 = (bf16[8,64,384]{2,1,0:T(8,128)(2,1)S(1)}, bf16[8,64,384]{2,1,0:T(8,128)(2,1)S(1)}, u32[]{:S(2)}, u32[]{:S(2)}) collective-permute-start(bf16[8,64,384]{2,1,0:T(8,128)(2,1)S(1)} %collective-permute-done.1.refs_2_), channel_id=1, source_target_pairs={{0,1},{1,0},{2,3},{3,2},{4,5},{5,4},{6,7},{7,6},{8,9},{9,8},{10,11... | collective-permute-start | bytes 1179656 | tf_op jit(solution)/shard_map/ppermute | solution.py:320
  15.4 3.1 %collective-permute-start.5 = (bf16[8,64,384]{2,1,0:T(8,128)(2,1)S(1)}, bf16[8,64,384]{2,1,0:T(8,128)(2,1)S(1)}, u32[]{:S(2)}, u32[]{:S(2)}) collective-permute-start(bf16[8,64,384]{2,1,0:T(8,128)(2,1)S(1)} %collective-permute-done.refs_4_), channel_id=1, source_target_pairs={{0,1},{1,0},{2,3},{3,2},{4,5},{5,4},{6,7},{7,6},{8,9},{9,8},{10,11... | collective-permute-start | bytes 1179656 | tf_op jit(solution)/shard_map/ppermute | solution.py:320
  15.9 11.0 %collective-permute-start.4 = (bf16[8,64,384]{2,1,0:T(8,128)(2,1)S(1)}, bf16[8,64,384]{2,1,0:T(8,128)(2,1)S(1)}, u32[]{:S(2)}, u32[]{:S(2)}) collective-permute-start(bf16[8,64,384]{2,1,0:T(8,128)(2,1)S(1)} %collective-permute-done.refs_4_), channel_id=1, source_target_pairs={{0,2},{1,3},{2,0},{3,1},{4,6},{5,7},{6,4},{7,5},{8,10},{9,11},{10,... | collective-permute-start | bytes 1179656 | tf_op jit(solution)/shard_map/ppermute | solution.py:320
  16.3 11.6 %collective-permute-start.3 = (bf16[8,64,384]{2,1,0:T(8,128)(2,1)S(1)}, bf16[8,64,384]{2,1,0:T(8,128)(2,1)S(1)}, u32[]{:S(2)}, u32[]{:S(2)}) collective-permute-start(bf16[8,64,384]{2,1,0:T(8,128)(2,1)S(1)} %collective-permute-done.refs_4_), channel_id=1, source_target_pairs={{0,4},{1,5},{2,6},{3,7},{4,12},{5,13},{6,14},{7,15},{8,0},{9,1},{1... | collective-permute-start | bytes 1179656 | tf_op jit(solution)/shard_map/ppermute | solution.py:317
  18.4 1.0 %copy-start.1 = (bf16[8,64,384]{2,1,0:T(8,128)(2,1)S(1)}, bf16[8,64,384]{2,1,0:T(8,128)(2,1)}, u32[]{:S(2)}) copy-start(bf16[8,64,384]{2,1,0:T(8,128)(2,1)} %refs_0_.1) | copy-start | bytes 1179652
  28.0 3.6 %collective-permute-start.10 = (bf16[8,64,384]{2,1,0:T(8,128)(2,1)S(1)}, bf16[8,64,384]{2,1,0:T(8,128)(2,1)S(1)}, u32[]{:S(2)}, u32[]{:S(2)}) collective-permute-start(bf16[8,64,384]{2,1,0:T(8,128)(2,1)S(1)} %collective-permute-done.4.refs_0_), channel_id=1, source_target_pairs={{0,1},{1,0},{2,3},{3,2},{4,5},{5,4},{6,7},{7,6},{8,9},{9,8},{10,11... | collective-permute-start | bytes 1179656 | tf_op jit(solution)/shard_map/ppermute | solution.py:320
  28.0 3.6 %collective-permute-start.9 = (bf16[8,64,384]{2,1,0:T(8,128)(2,1)S(1)}, bf16[8,64,384]{2,1,0:T(8,128)(2,1)S(1)}, u32[]{:S(2)}, u32[]{:S(2)}) collective-permute-start(bf16[8,64,384]{2,1,0:T(8,128)(2,1)S(1)} %collective-permute-done.3.refs_2_), channel_id=1, source_target_pairs={{0,1},{1,0},{2,3},{3,2},{4,5},{5,4},{6,7},{7,6},{8,9},{9,8},{10,11... | collective-permute-start | bytes 1179656 | tf_op jit(solution)/shard_map/ppermute | solution.py:320
  28.5 11.0 %collective-permute-start.8 = (bf16[8,64,384]{2,1,0:T(8,128)(2,1)S(1)}, bf16[8,64,384]{2,1,0:T(8,128)(2,1)S(1)}, u32[]{:S(2)}, u32[]{:S(2)}) collective-permute-start(bf16[8,64,384]{2,1,0:T(8,128)(2,1)S(1)} %collective-permute-done.3.refs_2_), channel_id=1, source_target_pairs={{0,2},{1,3},{2,0},{3,1},{4,6},{5,7},{6,4},{7,5},{8,10},{9,11},{10,... | collective-permute-start | bytes 1179656 | tf_op jit(solution)/shard_map/ppermute | solution.py:320
  30.1 11.6 %collective-permute-start.7 = (bf16[8,64,384]{2,1,0:T(8,128)(2,1)S(1)}, bf16[8,64,384]{2,1,0:T(8,128)(2,1)S(1)}, u32[]{:S(2)}, u32[]{:S(2)}) collective-permute-start(bf16[8,64,384]{2,1,0:T(8,128)(2,1)S(1)} %collective-permute-done.3.refs_2_), channel_id=1, source_target_pairs={{0,4},{1,5},{2,6},{3,7},{4,12},{5,13},{6,14},{7,15},{8,0},{9,1},{1... | collective-permute-start | bytes 1179656 | tf_op jit(solution)/shard_map/ppermute | solution.py:317
  41.7 1.9 %collective-permute-start.14 = (bf16[8,64,384]{2,1,0:T(8,128)(2,1)S(1)}, bf16[8,64,384]{2,1,0:T(8,128)(2,1)S(1)}, u32[]{:S(2)}, u32[]{:S(2)}) collective-permute-start(bf16[8,64,384]{2,1,0:T(8,128)(2,1)S(1)} %collective-permute-done.7.refs_2_), channel_id=1, source_target_pairs={{0,1},{1,0},{2,3},{3,2},{4,5},{5,4},{6,7},{7,6},{8,9},{9,8},{10,11... | collective-permute-start | bytes 1179656 | tf_op jit(solution)/shard_map/ppermute | solution.py:320
  41.7 2.3 %collective-permute-start.13 = (bf16[8,64,384]{2,1,0:T(8,128)(2,1)S(1)}, bf16[8,64,384]{2,1,0:T(8,128)(2,1)S(1)}, u32[]{:S(2)}, u32[]{:S(2)}) collective-permute-start(bf16[8,64,384]{2,1,0:T(8,128)(2,1)S(1)} %collective-permute-done.8.refs_0_), channel_id=1, source_target_pairs={{0,1},{1,0},{2,3},{3,2},{4,5},{5,4},{6,7},{7,6},{8,9},{9,8},{10,11... | collective-permute-start | bytes 1179656 | tf_op jit(solution)/shard_map/ppermute | solution.py:320
  42.3 7.8 %collective-permute-start.12 = (bf16[4,64,384]{2,1,0:T(8,128)(2,1)S(1)}, bf16[4,64,384]{2,1,0:T(8,128)(2,1)S(1)}, u32[]{:S(2)}, u32[]{:S(2)}) collective-permute-start(bf16[4,64,384]{2,1,0:T(8,128)(2,1)S(1)} %slice.7), channel_id=1, source_target_pairs={{0,4},{1,5},{2,6},{3,7},{4,12},{5,13},{6,14},{7,15},{8,0},{9,1},{1... | collective-permute-start | bytes 589832 | tf_op jit(solution)/shard_map/ppermute | solution.py:317
  43.1 6.9 %collective-permute-start.11 = (bf16[4,64,384]{2,1,0:T(8,128)(2,1)S(1)}, bf16[4,64,384]{2,1,0:T(8,128)(2,1)S(1)}, u32[]{:S(2)}, u32[]{:S(2)}) collective-permute-start(bf16[4,64,384]{2,1,0:T(8,128)(2,1)S(1)} %slice.6), channel_id=1, source_target_pairs={{0,2},{1,3},{2,0},{3,1},{4,6},{5,7},{6,4},{7,5},{8,10},{9,11},{10,... | collective-permute-start | bytes 589832 | tf_op jit(solution)/shard_map/ppermute | solution.py:320
  50.0 1.4 %collective-permute-start.15 = (bf16[4,64,384]{2,1,0:T(8,128)(2,1)S(1)}, bf16[4,64,384]{2,1,0:T(8,128)(2,1)S(1)}, u32[]{:S(2)}, u32[]{:S(2)}) collective-permute-start(bf16[4,64,384]{2,1,0:T(8,128)(2,1)S(1)} %collective-permute-done.11.refs_0_), channel_id=1, source_target_pairs={{0,1},{1,0},{2,3},{3,2},{4,5},{5,4},{6,7},{7,6},{8,9},{9,8},{10,11... | collective-permute-start | bytes 589832 | tf_op jit(solution)/shard_map/ppermute | solution.py:320
  50.0 1.7 %collective-permute-start.16 = (bf16[4,64,384]{2,1,0:T(8,128)(2,1)S(1)}, bf16[4,64,384]{2,1,0:T(8,128)(2,1)S(1)}, u32[]{:S(2)}, u32[]{:S(2)}) collective-permute-start(bf16[4,64,384]{2,1,0:T(8,128)(2,1)S(1)} %collective-permute-done.12.refs_1_), channel_id=1, source_target_pairs={{0,1},{1,0},{2,3},{3,2},{4,5},{5,4},{6,7},{7,6},{8,9},{9,8},{10,11... | collective-permute-start | bytes 589832 | tf_op jit(solution)/shard_map/ppermute | solution.py:320
  55.4 3.1 %collective-permute-start.19 = (f32[2,8,128]{2,1,0:T(8,128)S(1)}, f32[2,8,128]{2,1,0:T(8,128)S(1)}, u32[]{:S(2)}, u32[]{:S(2)}) collective-permute-start(f32[2,8,128]{2,1,0:T(8,128)S(1)} %get-tuple-element.77), channel_id=1, source_target_pairs={{0,3},{1,2},{2,1},{3,0},{4,7},{5,6},{6,5},{7,4},{8,11},{9,10},{10,... | collective-permute-start | bytes 24584 | tf_op jit(solution)/shard_map/ppermute | solution.py:320
  55.7 3.7 %collective-permute-start.18 = (f32[2,8,128]{2,1,0:T(8,128)S(1)}, f32[2,8,128]{2,1,0:T(8,128)S(1)}, u32[]{:S(2)}, u32[]{:S(2)}) collective-permute-start(f32[2,8,128]{2,1,0:T(8,128)S(1)} %get-tuple-element.77), channel_id=1, source_target_pairs={{0,2},{1,3},{2,0},{3,1},{4,6},{5,7},{6,4},{7,5},{8,10},{9,11},{10,... | collective-permute-start | bytes 24584 | tf_op jit(solution)/shard_map/ppermute | solution.py:320
  57.3 2.1 %collective-permute-start.17 = (f32[2,8,128]{2,1,0:T(8,128)S(1)}, f32[2,8,128]{2,1,0:T(8,128)S(1)}, u32[]{:S(2)}, u32[]{:S(2)}) collective-permute-start(f32[2,8,128]{2,1,0:T(8,128)S(1)} %get-tuple-element.77), channel_id=1, source_target_pairs={{0,1},{1,0},{2,3},{3,2},{4,5},{5,4},{6,7},{7,6},{8,9},{9,8},{10,11... | collective-permute-start | bytes 24584 | tf_op jit(solution)/shard_map/ppermute | solution.py:320
  59.4 6.3 %collective-permute-start.20 = (f32[2,8,128]{2,1,0:T(8,128)S(1)}, f32[2,8,128]{2,1,0:T(8,128)S(1)}, u32[]{:S(2)}, u32[]{:S(2)}) collective-permute-start(f32[2,8,128]{2,1,0:T(8,128)S(1)} %add_add_fusion), channel_id=1, source_target_pairs={{0,4},{1,5},{2,6},{3,7},{4,0},{5,1},{6,2},{7,3},{8,12},{9,13},{10,... | collective-permute-start | bytes 24584 | tf_op jit(solution)/shard_map/ppermute | solution.py:320
  65.7 4.5 %collective-permute-start.21 = (f32[2,8,128]{2,1,0:T(8,128)S(1)}, f32[2,8,128]{2,1,0:T(8,128)S(1)}, u32[]{:S(2)}, u32[]{:S(2)}) collective-permute-start(f32[2,8,128]{2,1,0:T(8,128)S(1)} %add.21), channel_id=1, source_target_pairs={{0,8},{1,9},{2,10},{3,11},{4,12},{5,13},{6,14},{7,15},{8,0},{9,1},... | collective-permute-start | bytes 24584 | tf_op jit(solution)/shard_map/ppermute | solution.py:320

commit v7 on v6

--- a/solution.py
+++ b/solution.py
@@ -25,14 +25,19 @@
 
 def prepare_kernel(
     depth, shard_tiles,
-    me_ref, counts_ref, irrep_ref, v_ref,
+    me_ref, counts_hbm, irrep_hbm, v_ref,
     res_ref, sorted_ref, gathered_ref, stats_ref, order_ref, begin_ref, item_ref,
-    blank_ref, size_ref, first_ref, next_ref, cursor_ref, call_ref, sem, blank_sem,
+    counts_ref, irrep_ref, blank_ref, size_ref, first_ref, next_ref, cursor_ref, call_ref,
+    sem, blank_sem, counts_sem, irrep_sem,
 ):
     own_tiles = v_ref.shape[0]
     irreps = counts_ref.shape[0]
     rows = v_ref.shape[1]
     most = item_ref.shape[0] // 6
+    counts_copy = pltpu.make_async_copy(counts_hbm, counts_ref, counts_sem)
+    irrep_copy = pltpu.make_async_copy(irrep_hbm, irrep_ref, irrep_sem)
+    counts_copy.start()
+    irrep_copy.start()
     blank_ref[...] = jnp.zeros(blank_ref.shape, blank_ref.dtype)
     group = blank_ref.shape[0]
     for l in range(0, own_tiles, group):
@@ -40,6 +45,8 @@
 
     for s in range(irreps):
         size_ref[s] = 0
+    counts_copy.wait()
+    irrep_copy.wait()
 
     def count(l, carry):
         s = irrep_ref[l]
@@ -67,10 +74,14 @@
         buffer[pl.ds(buffer.shape[0] - BATCH, BATCH)] = spare
 
     me = me_ref[0]
-    z, y = me // 4, me // 2 % 2
-    for part in range(2 * depth):
-        lag = lax.rem(ring_place(z, depth) - ring_place(jnp.int32(part // 2), depth) + depth, depth)
-        call_ref[part] = jnp.where(y == part % 2, jnp.maximum(lag - 1, 0), lag)
+    z, y, core = me // 4, me // 2 % 2, me % 2
+    for shard in range(4 * depth):
+        lag = lax.rem(ring_place(z, depth) - ring_place(jnp.int32(shard // 4), depth) + depth, depth)
+        own_y = jnp.where(core == shard % 2, jnp.maximum(lag - 1, 0), jnp.minimum(lag, depth - 2))
+        other_y = jnp.where(
+            (core == shard % 2) | (lag == depth - 1), lag, jnp.minimum(lag + 1, depth - 2)
+        )
+        call_ref[shard] = jnp.where(y == shard // 2 % 2, own_y, other_y)
     for call in range(depth):
         cursor_ref[call] = 0
 
@@ -83,7 +94,7 @@
                 low = offset + j * BATCH
                 high = offset + jnp.minimum(tiles, j * BATCH + BATCH) - 1
                 call = jnp.maximum(
-                    call_ref[low // (2 * shard_tiles)], call_ref[high // (2 * shard_tiles)]
+                    call_ref[low // shard_tiles], call_ref[high // shard_tiles]
                 )
                 visit(s, j, low, tiles, batches, call)
                 return carry
@@ -126,14 +137,14 @@
 
         lax.fori_loop(cursor_ref[call], begin_ref[call + 1], fill, 0)
 
-    shape = stats_ref.shape[1:]
+    shape = stats_ref.shape[2:]
     at_row = lax.broadcasted_iota(jnp.int32, shape, 0)
     at_lane = lax.broadcasted_iota(jnp.int32, shape, 1)
     sizes = jnp.zeros(shape, jnp.int32)
     for s in range(irreps):
         sizes = jnp.where((at_row == s) & (at_lane == 0), size_ref[s], sizes)
-    stats_ref[0] = jnp.zeros(shape, jnp.float32)
-    stats_ref[1] = sizes.astype(jnp.float32)
+    stats_ref[0, 0] = jnp.zeros(shape, jnp.float32)
+    stats_ref[0, 1] = sizes.astype(jnp.float32)
     pltpu.make_async_copy(v_ref, sorted_ref.at[pl.ds(0, own_tiles)], sem).wait()
     pltpu.make_async_copy(res_ref, res_ref, blank_sem).wait()
 
@@ -147,26 +158,31 @@
     smem = pl.BlockSpec(memory_space=pltpu.SMEM)
     vmem = pl.BlockSpec(memory_space=pltpu.VMEM)
     anywhere = pl.BlockSpec(memory_space=pl.ANY)
+    hbm = pl.BlockSpec(memory_space=pltpu.HBM)
     return pl.pallas_call(
         functools.partial(prepare_kernel, depth, shard_tiles),
         out_shape=(
             jax.ShapeDtypeStruct((own_tiles, rows, capacity * rows), jnp.bfloat16),
             jax.ShapeDtypeStruct((own_tiles + BATCH, rows, width), integrals.dtype),
             jax.ShapeDtypeStruct((all_tiles + BATCH, rows, width), jnp.bfloat16),
-            jax.ShapeDtypeStruct((2, irreps, 128), jnp.float32),
+            jax.ShapeDtypeStruct((1, 2, irreps, 128), jnp.float32),
             jax.ShapeDtypeStruct((own_tiles,), jnp.int32),
             jax.ShapeDtypeStruct((depth + 1,), jnp.int32),
             jax.ShapeDtypeStruct((6 * most,), jnp.int32),
         ),
-        in_specs=[smem, smem, smem, anywhere],
+        in_specs=[smem, hbm, hbm, hbm],
         out_specs=(anywhere, vmem, vmem, vmem, smem, smem, smem),
         scratch_shapes=[
+            pltpu.SMEM((irreps,), jnp.int32),
+            pltpu.SMEM((own_tiles,), jnp.int32),
             pltpu.VMEM((2, rows, capacity * rows), jnp.bfloat16),
             pltpu.SMEM((irreps,), jnp.int32),
             pltpu.SMEM((irreps,), jnp.int32),
             pltpu.SMEM((irreps,), jnp.int32),
             pltpu.SMEM((depth,), jnp.int32),
-            pltpu.SMEM((2 * depth,), jnp.int32),
+            pltpu.SMEM((4 * depth,), jnp.int32),
+            pltpu.SemaphoreType.DMA,
+            pltpu.SemaphoreType.DMA,
             pltpu.SemaphoreType.DMA,
             pltpu.SemaphoreType.DMA,
         ],
@@ -192,14 +208,14 @@
     me = me_ref[0]
     z, y, core = me // 4, me // 2 % 2, me % 2
     arrivals = []
-    for source, (lag, other_y, other_core, tile) in zip(fresh, layout):
+    for source, (lag, other_y, other_core) in zip(fresh, layout):
         at = ring_position(lax.rem(ring_place(z, depth) - lag + depth, depth), depth)
         own_y = (1 - y) if other_y else y
         own_core = (1 - core) if other_core else core
         arrivals.append(pltpu.make_async_copy(
             source,
             gathered_ref.at[
-                pl.ds(((at * 2 + own_y) * 2 + own_core) * shard_tiles + tile, source.shape[0])
+                pl.ds(((at * 2 + own_y) * 2 + own_core) * shard_tiles, shard_tiles)
             ],
             a_sem.at[len(arrivals)],
         ))
@@ -257,8 +273,9 @@
     )
     sums = jnp.sum(acc_ref[...], axis=1)
     sums = sum(sums[:, k:k + 128] for k in range(0, side, 128))
-    stats_ref[0] = stats_in_ref[0] + sums
-    stats_ref[1] = stats_in_ref[1]
+    for copy in range(stats_ref.shape[0]):
+        stats_ref[copy, 0] = stats_in_ref[0, 0] + sums
+        stats_ref[copy, 1] = stats_in_ref[0, 1]
 
     def finish(n, carry):
         pltpu.make_async_copy(
@@ -269,23 +286,31 @@
     lax.fori_loop(0, started, finish, 0)
 
 
-def ladder(call, depth, shard_tiles, me, plan, state, fresh, layout):
+def ladder(call, depth, shard_tiles, me, plan, state, fresh, layout, copies=1):
     ordered, order, begin, items = plan
     residual, gathered, stats = state
     slots, rows, width = ordered.shape
+    irreps = stats.shape[2]
     smem = pl.BlockSpec(memory_space=pltpu.SMEM)
     vmem = pl.BlockSpec(memory_space=pltpu.VMEM)
     anywhere = pl.BlockSpec(memory_space=pl.ANY)
+    hbm = pl.BlockSpec(memory_space=pltpu.HBM)
     out_bytes = 2 * slots * residual[0].size
     tiles = sum(source.shape[0] for source in fresh)
     return pl.pallas_call(
         functools.partial(ladder_kernel, call, depth, shard_tiles, layout),
-        out_shape=tuple(jax.ShapeDtypeStruct(x.shape, x.dtype) for x in state),
-        in_specs=[smem] * 4 + [vmem] * 2 + [anywhere, vmem] + [anywhere] * len(fresh),
+        out_shape=(
+            jax.ShapeDtypeStruct(residual.shape, residual.dtype),
+            jax.ShapeDtypeStruct(gathered.shape, gathered.dtype),
+            jax.ShapeDtypeStruct((copies, 2, irreps, 128), jnp.float32),
+        ),
+        in_specs=[smem] * 4 + [vmem] * 2 + [anywhere, vmem] + [
+            hbm if where == (0, 0, 0) else anywhere for where in layout
+        ],
         out_specs=(anywhere, vmem, vmem),
         scratch_shapes=[
             pltpu.VMEM((slots, rows, residual.shape[2]), jnp.bfloat16),
-            pltpu.VMEM((stats.shape[1], 8, BATCH * rows), jnp.float32),
+            pltpu.VMEM((irreps, 8, BATCH * rows), jnp.float32),
             pltpu.SemaphoreType.DMA((len(fresh),)),
             pltpu.SemaphoreType.DMA,
         ],
@@ -324,43 +349,37 @@
     )
     plan = (ordered, order, begin, items)
     state = (residual, gathered, stats)
-    half = shard_tiles // 2
-
-    a, b, c = amplitudes, None, None
-    early, early_layout = (), ()
+
+    a, b, c, d = [amplitudes], [], [], []
     for k in range(depth):
         if k:
-            a, b, c, *state = lax.optimization_barrier((a, b, c, *state))
+            d[-1:], c[-1], b[-1], a[k], state = lax.optimization_barrier(
+                (d[-1:], c[-1], b[-1], a[k], state)
+            )
         if k < depth - 1:
-            following = shift_z(a)
-            there = swap(a, 2)
-        else:
-            there = (swap(a[:half], 2), shift_z(b[half:]))
-        across = swap(a, 1)
-        if k == 0:
-            early, early_layout = (a, across), ((0, 0, 0, 0), (0, 0, 1, 0))
-        else:
+            a.append(shift_z(a[k]))
+        b.append(swap(a[k], 2))
+        c.append(swap(a[k], 1))
+        if k:
+            d.append(swap(b[k - 1], 1))
+            fresh = {(k, 0, 0): a[k], (k - 1, 1, 0): b[k - 1], (k - 1, 0, 1): c[k - 1]}
+            if k == 1:
+                fresh[0, 0, 0] = a[0]
+            else:
+                fresh[k - 2, 1, 1] = d[k - 2]
+            if k == depth - 1:
+                fresh[k, 0, 1], fresh[k - 1, 1, 1] = c[k], d[k - 1]
             state = ladder(
-                k - 1, depth, shard_tiles, me, plan, state,
-                (*early, b, swap(b, 1), a, across),
-                (*early_layout, (k - 1, 1, 0, 0), (k - 1, 1, 1, 0), (k, 0, 0, 0), (k, 0, 1, 0)),
+                k - 1, depth, shard_tiles, me, plan, state, tuple(fresh.values()), tuple(fresh)
             )
-            early, early_layout = (), ()
-        a, b, c = following, there, across
-    *b, residual, gathered, stats = lax.optimization_barrier((*b, *state))
-    state = ladder(
-        depth - 1, depth, shard_tiles, me, plan, (residual, gathered, stats),
-        (*b, *(swap(piece, 1) for piece in b)),
-        tuple((depth - 1, 1, core, tile) for core in range(2) for tile in (0, half)),
-    )
-    residual, _, stats = state
-
-    stats = sum([swap(stats, bits) for bits in (1, 2, 3)], stats)
-    bits = 4
-    while bits < devices:
-        stats = stats + swap(stats, bits)
-        bits *= 2
-    irrep_sums, ab_counts = jnp.sum(stats, axis=2)
+    last, *state = lax.optimization_barrier((b[-1], *state))
+    residual, _, stats = ladder(
+        depth - 1, depth, shard_tiles, me, plan, state,
+        (last, swap(last, 1)), ((depth - 1, 1, 0), (depth - 1, 1, 1)), devices,
+    )
+
+    stats = lax.all_to_all(stats, "vir", 0, 0, tiled=True)
+    irrep_sums, ab_counts = jnp.sum(stats, axis=(0, 3))
     entries = ab_counts * ij_counts.astype(jnp.float32) * float(rows * rows)
     return residual, jnp.sqrt(irrep_sums / entries + 1e-06)
 

time: 70.6 us -> 71.6 us (1.014)
  blocking collectives: 0 us -> 11.6 us
  starting transfers between devices: 20.4 us -> 10.8 us
  waiting for transfers between devices: 21.6 us -> 20.8 us
    all_to_all x0 -> x1, blocking collectives: none -> 11.6 us  [per_device(): stats = lax.all_to_all(stats, 'vir', 0, 0, tiled=True)]
    ppermute x18 -> x12, waiting for transfers between devices: 17.3 us -> 7.74 us  [swap(): return lax.ppermute(x, 'vir', [(d, d ^ bits) for d in range(devices)])]
    ppermute x18 -> x12, starting transfers between devices: 14.4 us -> 4.97 us  [swap(): return lax.ppermute(x, 'vir', [(d, d ^ bits) for d in range(devices)])]
    ppermute x4 -> x3, waiting for transfers between devices: 4.26 us -> 13.1 us  [shift_z(): return lax.ppermute(x, 'vir', hop)]
    ppermute x4 -> x3, starting transfers between devices: 5.98 us -> 5.85 us  [shift_z(): return lax.ppermute(x, 'vir', hop)]
    unnamed x8 -> x10, local copies, waits for them, and re-layouts: 3.71 us -> 3.72 us
  transfers between devices with their start and end apart: 22 -> 15, of which waited for: 13 -> 8; matrix products, arithmetic and copies ran while one was open for 0% -> 0% of each run, Pallas kernels for 28% -> 28%
where the time goes in v7:
time: 71.6 us; the launch traced here: 71.4 us
  Pallas kernels  23.1 us (32%)
  waiting for transfers between devices  20.8 us (29%)
  blocking collectives  11.6 us (16%)
  starting transfers between devices  10.8 us (15%)
  local copies, waits for them, and re-layouts  3.72 us (5%)
  between operations  0.73 us (1%)
    pallas_call x4, Pallas kernels, ladder(): pl.pallas_call(functools.partial(ladder_kernel, call, depth, shard_tiles,...  16.5 us
    ppermute x3, waiting for transfers between devices, shift_z(): return lax.ppermute(x, 'vir', hop)  13.1 us
    all_to_all x1, blocking collectives, per_device(): stats = lax.all_to_all(stats, 'vir', 0, 0, tiled=True)  11.6 us
    ppermute x12, waiting for transfers between devices, swap(): return lax.ppermute(x, 'vir', [(d, d ^ bits) for d in range(devices)])  7.74 us
    pallas_call x1, Pallas kernels, prepare(): pl.pallas_call(functools.partial(prepare_kernel, depth, shard_tiles), out...  6.59 us
    ppermute x3, starting transfers between devices, shift_z(): return lax.ppermute(x, 'vir', hop)  5.85 us
    ppermute x12, starting transfers between devices, swap(): return lax.ppermute(x, 'vir', [(d, d ^ bits) for d in range(devices)])  4.97 us
    unnamed x10, local copies, waits for them, and re-layouts  3.72 us
  transfers between devices with their start and end apart: 15, of which 8 were waited for; matrix products, arithmetic and copies ran while one was open for 0% of the time, Pallas kernels for 28%

profile of v7, /device:TPU:0, one launch (start us, length us, event | category | flops | bytes accessed | tf_op | source)
XLA Modules:
  0.0 71.4 jit_solution(10597156555010354668)
XLA Ops:
  0.6 3.0 %collective-permute-start.1 = (bf16[8,64,384]{2,1,0:T(8,128)(2,1)}, bf16[8,64,384]{2,1,0:T(8,128)(2,1)S(1)}, u32[]{:S(2)}, u32[]{:S(2)}) collective-permute-start(bf16[8,64,384]{2,1,0:T(8,128)(2,1)} %refs_3_.1), channel_id=1, source_target_pairs={{0,2},{1,3},{2,0},{3,1},{4,6},{5,7},{6,4},{7,5},{8,10},{9,11},{10,... | collective-permute-start | bytes 1179656 | tf_op jit(solution)/shard_map/ppermute | solution.py:345
  3.7 0.0 collective-permute-start
  3.7 1.6 %collective-permute-start.2 = (bf16[8,64,384]{2,1,0:T(8,128)(2,1)}, bf16[8,64,384]{2,1,0:T(8,128)(2,1)S(1)}, u32[]{:S(2)}, u32[]{:S(2)}) collective-permute-start(bf16[8,64,384]{2,1,0:T(8,128)(2,1)} %refs_3_.1), channel_id=1, source_target_pairs={{0,4},{1,5},{2,6},{3,7},{4,12},{5,13},{6,14},{7,15},{8,0},{9,1},{1... | collective-permute-start | bytes 1179656 | tf_op jit(solution)/shard_map/ppermute | solution.py:342
  5.2 0.0 copy-start
  5.2 1.4 %copy-done = bf16[32,64,384]{2,1,0:T(8,128)(2,1)S(1)} copy-done((bf16[32,64,384]{2,1,0:T(8,128)(2,1)S(1)}, bf16[32,64,384]{2,1,0:T(8,128)(2,1)}, u32[]{:S(2)}) %copy-start) | copy-done | bytes 1572888
  6.7 0.0 copy-start.2
  6.7 0.7 copy-done.2
  7.3 0.0 copy-start.4
  7.3 0.7 copy-done.4
  8.0 6.6 %prepare.1 = (bf16[32,64,2048]{2,1,0:T(8,128)(2,1)}, bf16[36,64,384]{2,1,0:T(8,128)(2,1)S(1)}, bf16[132,64,384]{2,1,0:T(8,128)(2,1)S(1)}, f32[1,2,8,128]{3,2,1,0...) custom-call(s32[1]{0:T(128)} %bitcast.me_ref, s32[8]{0:T(128)S(1)} %copy-done.2, s32[32]{0:T(128)S(1)} %copy-done.4, ...), custom_call_target="tpu_custom_call" | custom-call | bytes 8388608 | tf_op jit(solution)/shard_map/prepare/pallas_call | solution.py:162
  14.6 0.0 collective-permute-done.1.refs_1_
  14.6 0.0 collective-permute-done.refs_2_
  14.6 1.7 %collective-permute-done.2.refs_0_ = bf16[8,64,384]{2,1,0:T(8,128)(2,1)S(1)} collective-permute-done((bf16[8,64,384]{2,1,0:T(8,128)(2,1)}, bf16[8,64,384]{2,1,0:T(8,128)(2,1)S(1)}, u32[]{:S(2)}, u32[]{:S(2)}) %collective-permute-start.2) | collective-permute-done | bytes 393248 | tf_op jit(solution)/shard_map/ppermute | solution.py:342
  16.3 0.0 collective-permute-start.3
  16.3 1.3 %collective-permute-start.6 = (bf16[8,64,384]{2,1,0:T(8,128)(2,1)S(1)}, bf16[8,64,384]{2,1,0:T(8,128)(2,1)S(1)}, u32[]{:S(2)}, u32[]{:S(2)}) collective-permute-start(bf16[8,64,384]{2,1,0:T(8,128)(2,1)S(1)} %collective-permute-done.2.refs_0_), channel_id=1, source_target_pairs={{0,4},{1,5},{2,6},{3,7},{4,12},{5,13},{6,14},{7,15},{8,0},{9,1},{1... | collective-permute-start | bytes 1179656 | tf_op jit(solution)/shard_map/ppermute | solution.py:342
  17.6 0.4 collective-permute-start.5
  18.0 0.0 collective-permute-start.4
  18.0 0.0 copy-start.1
  18.0 1.0 %copy-done.1 = bf16[8,64,384]{2,1,0:T(8,128)(2,1)S(1)} copy-done((bf16[8,64,384]{2,1,0:T(8,128)(2,1)S(1)}, bf16[8,64,384]{2,1,0:T(8,128)(2,1)}, u32[]{:S(2)}) %copy-start.1) | copy-done | bytes 393240
  19.0 3.3 %ladder_0.1 = (bf16[32,64,2048]{2,1,0:T(8,128)(2,1)}, bf16[132,64,384]{2,1,0:T(8,128)(2,1)S(1)}, f32[1,2,8,128]{3,2,1,0:T(8,128)S(1)}) custom-call(s32[1]{0:T(128)} %bitcast.me_ref, s32[32]{0:T(128)S(1)} %get-tuple-element.44.order_ref, s32[5]{0:T(128)S(1)} %get-tuple-element.45.begin_ref, ...), custom_call_target="tpu_custom_call", output_to_operand_aliasing={{0}: (6, {}), {1}: (7, {})} | custom-call | flops 402653184 | bytes 2097152 | tf_op jit(solution)/shard_map/ladder_0/pallas_call | solution.py:300
  22.3 0.0 collective-permute-done.3.refs_3_
  22.3 6.4 %collective-permute-done.6.refs_0_ = bf16[8,64,384]{2,1,0:T(8,128)(2,1)S(1)} collective-permute-done((bf16[8,64,384]{2,1,0:T(8,128)(2,1)S(1)}, bf16[8,64,384]{2,1,0:T(8,128)(2,1)S(1)}, u32[]{:S(2)}, u32[]{:S(2)}) %collective-permute-start.6) | collective-permute-done | bytes 393248 | tf_op jit(solution)/shard_map/ppermute | solution.py:342
  28.7 0.0 collective-permute-done.5.refs_1_
  28.7 0.0 collective-permute-done.4.refs_2_
  28.7 0.0 collective-permute-start.7
  28.7 3.0 %collective-permute-start.10 = (bf16[8,64,384]{2,1,0:T(8,128)(2,1)S(1)}, bf16[8,64,384]{2,1,0:T(8,128)(2,1)S(1)}, u32[]{:S(2)}, u32[]{:S(2)}) collective-permute-start(bf16[8,64,384]{2,1,0:T(8,128)(2,1)S(1)} %collective-permute-done.6.refs_0_), channel_id=1, source_target_pairs={{0,4},{1,5},{2,6},{3,7},{4,12},{5,13},{6,14},{7,15},{8,0},{9,1},{1... | collective-permute-start | bytes 1179656 | tf_op jit(solution)/shard_map/ppermute | solution.py:342
  31.7 0.5 collective-permute-start.9
  32.2 0.0 collective-permute-start.8
  32.2 4.0 %ladder_1.1 = (bf16[32,64,2048]{2,1,0:T(8,128)(2,1)}, bf16[132,64,384]{2,1,0:T(8,128)(2,1)S(1)}, f32[1,2,8,128]{3,2,1,0:T(8,128)S(1)}) custom-call(s32[1]{0:T(128)} %bitcast.me_ref, s32[32]{0:T(128)S(1)} %get-tuple-element.44.order_ref, s32[5]{0:T(128)S(1)} %get-tuple-element.45.begin_ref, ...), custom_call_target="tpu_custom_call", output_to_operand_aliasing={{0}: (6, {}), {1}: (7, {})} | custom-call | flops 402653184 | bytes 2097152 | tf_op jit(solution)/shard_map/ladder_1/pallas_call | solution.py:300
  36.2 0.0 collective-permute-done.7.refs_3_
  36.2 4.9 %collective-permute-done.10.refs_0_ = bf16[8,64,384]{2,1,0:T(8,128)(2,1)S(1)} collective-permute-done((bf16[8,64,384]{2,1,0:T(8,128)(2,1)S(1)}, bf16[8,64,384]{2,1,0:T(8,128)(2,1)S(1)}, u32[]{:S(2)}, u32[]{:S(2)}) %collective-permute-start.10) | collective-permute-done | bytes 393248 | tf_op jit(solution)/shard_map/ppermute | solution.py:342
  41.2 1.8 %collective-permute-done.9.refs_1_ = bf16[8,64,384]{2,1,0:T(8,128)(2,1)S(1)} collective-permute-done((bf16[8,64,384]{2,1,0:T(8,128)(2,1)S(1)}, bf16[8,64,384]{2,1,0:T(8,128)(2,1)S(1)}, u32[]{:S(2)}, u32[]{:S(2)}) %collective-permute-start.9) | collective-permute-done | bytes 393248 | tf_op jit(solution)/shard_map/ppermute | solution.py:345
  43.0 0.0 collective-permute-done.8.refs_2_
  43.0 0.0 collective-permute-start.13
  43.0 0.5 collective-permute-start.12
  43.5 0.5 collective-permute-start.11
  44.0 0.7 collective-permute-done.13.refs_5_
  44.7 0.6 collective-permute-done.12.refs_4_
  45.3 6.3 %ladder_2.1 = (bf16[32,64,2048]{2,1,0:T(8,128)(2,1)}, bf16[132,64,384]{2,1,0:T(8,128)(2,1)S(1)}, f32[1,2,8,128]{3,2,1,0:T(8,128)S(1)}) custom-call(s32[1]{0:T(128)} %bitcast.me_ref, s32[32]{0:T(128)S(1)} %get-tuple-element.44.order_ref, s32[5]{0:T(128)S(1)} %get-tuple-element.45.begin_ref, ...), custom_call_target="tpu_custom_call", output_to_operand_aliasing={{0}: (6, {}), {1}: (7, {})} | custom-call | flops 603979776 | bytes 3145728 | tf_op jit(solution)/shard_map/ladder_2/pallas_call | solution.py:300
  51.6 2.9 %collective-permute-done.11.refs_0_ = bf16[8,64,384]{2,1,0:T(8,128)(2,1)S(1)} collective-permute-done((bf16[8,64,384]{2,1,0:T(8,128)(2,1)S(1)}, bf16[8,64,384]{2,1,0:T(8,128)(2,1)S(1)}, u32[]{:S(2)}, u32[]{:S(2)}) %collective-permute-start.11) | collective-permute-done | bytes 393248 | tf_op jit(solution)/shard_map/ppermute | solution.py:345
  54.5 0.0 copy-start.3
  54.5 0.0 collective-permute-start.14
  54.5 1.7 %collective-permute-done.14.refs_1_ = bf16[8,64,384]{2,1,0:T(8,128)(2,1)S(1)} collective-permute-done((bf16[8,64,384]{2,1,0:T(8,128)(2,1)S(1)}, bf16[8,64,384]{2,1,0:T(8,128)(2,1)S(1)}, u32[]{:S(2)}, u32[]{:S(2)}) %collective-permute-start.14) | collective-permute-done | bytes 393248 | tf_op jit(solution)/shard_map/ppermute | solution.py:345
  56.2 2.9 %ladder_3.1 = (bf16[32,64,2048]{2,1,0:T(8,128)(2,1)}, bf16[132,64,384]{2,1,0:T(8,128)(2,1)S(1)}, f32[16,2,8,128]{3,2,1,0:T(8,128)S(1)}) custom-call(s32[1]{0:T(128)} %bitcast.me_ref, s32[32]{0:T(128)S(1)} %get-tuple-element.44.order_ref, s32[5]{0:T(128)S(1)} %get-tuple-element.45.begin_ref, ...), custom_call_target="tpu_custom_call", output_to_operand_aliasing={{0}: (6, {}), {1}: (7, {})} | custom-call | flops 201326592 | bytes 1048576 | tf_op jit(solution)/shard_map/ladder_3/pallas_call | solution.py:300
  59.1 11.6 %all_to_all.5 = f32[16,2,8,128]{3,2,1,0:T(8,128)S(1)} all-to-all(f32[16,2,8,128]{3,2,1,0:T(8,128)S(1)} %get-tuple-element.85), channel_id=1, replica_groups=mesh['groups'=2,'vir'=16] {'vir'}, dimensions={0} | all-to-all | bytes 262144 | tf_op jit(solution)/shard_map/all_to_all | solution.py:381
  70.7 0.1 reduce_sum.9
  70.8 0.0 copy-done.3
  70.8 0.5 add_sqrt_fusion
Async XLA Ops:
  0.6 13.9 %collective-permute-start.1 = (bf16[8,64,384]{2,1,0:T(8,128)(2,1)}, bf16[8,64,384]{2,1,0:T(8,128)(2,1)S(1)}, u32[]{:S(2)}, u32[]{:S(2)}) collective-permute-start(bf16[8,64,384]{2,1,0:T(8,128)(2,1)} %refs_3_.1), channel_id=1, source_target_pairs={{0,2},{1,3},{2,0},{3,1},{4,6},{5,7},{6,4},{7,5},{8,10},{9,11},{10,... | collective-permute-start | bytes 1179656 | tf_op jit(solution)/shard_map/ppermute | solution.py:345
  3.7 10.9 %collective-permute-start = (bf16[8,64,384]{2,1,0:T(8,128)(2,1)}, bf16[8,64,384]{2,1,0:T(8,128)(2,1)S(1)}, u32[]{:S(2)}, u32[]{:S(2)}) collective-permute-start(bf16[8,64,384]{2,1,0:T(8,128)(2,1)} %refs_3_.1), channel_id=1, source_target_pairs={{0,1},{1,0},{2,3},{3,2},{4,5},{5,4},{6,7},{7,6},{8,9},{9,8},{10,11... | collective-permute-start | bytes 1179656 | tf_op jit(solution)/shard_map/ppermute | solution.py:345
  3.7 12.6 %collective-permute-start.2 = (bf16[8,64,384]{2,1,0:T(8,128)(2,1)}, bf16[8,64,384]{2,1,0:T(8,128)(2,1)S(1)}, u32[]{:S(2)}, u32[]{:S(2)}) collective-permute-start(bf16[8,64,384]{2,1,0:T(8,128)(2,1)} %refs_3_.1), channel_id=1, source_target_pairs={{0,4},{1,5},{2,6},{3,7},{4,12},{5,13},{6,14},{7,15},{8,0},{9,1},{1... | collective-permute-start | bytes 1179656 | tf_op jit(solution)/shard_map/ppermute | solution.py:342
  5.2 1.4 %copy-start = (bf16[32,64,384]{2,1,0:T(8,128)(2,1)S(1)}, bf16[32,64,384]{2,1,0:T(8,128)(2,1)}, u32[]{:S(2)}) copy-start(bf16[32,64,384]{2,1,0:T(8,128)(2,1)} %v_ref.1) | copy-start | bytes 4718596
  6.7 0.7 copy-start.2
  7.3 0.7 copy-start.4
  16.3 6.0 %collective-permute-start.3 = (bf16[8,64,384]{2,1,0:T(8,128)(2,1)S(1)}, bf16[8,64,384]{2,1,0:T(8,128)(2,1)S(1)}, u32[]{:S(2)}, u32[]{:S(2)}) collective-permute-start(bf16[8,64,384]{2,1,0:T(8,128)(2,1)S(1)} %collective-permute-done.1.refs_1_), channel_id=1, source_target_pairs={{0,1},{1,0},{2,3},{3,2},{4,5},{5,4},{6,7},{7,6},{8,9},{9,8},{10,11... | collective-permute-start | bytes 1179656 | tf_op jit(solution)/shard_map/ppermute | solution.py:345
  16.3 12.4 %collective-permute-start.6 = (bf16[8,64,384]{2,1,0:T(8,128)(2,1)S(1)}, bf16[8,64,384]{2,1,0:T(8,128)(2,1)S(1)}, u32[]{:S(2)}, u32[]{:S(2)}) collective-permute-start(bf16[8,64,384]{2,1,0:T(8,128)(2,1)S(1)} %collective-permute-done.2.refs_0_), channel_id=1, source_target_pairs={{0,4},{1,5},{2,6},{3,7},{4,12},{5,13},{6,14},{7,15},{8,0},{9,1},{1... | collective-permute-start | bytes 1179656 | tf_op jit(solution)/shard_map/ppermute | solution.py:342
  17.6 11.1 %collective-permute-start.5 = (bf16[8,64,384]{2,1,0:T(8,128)(2,1)S(1)}, bf16[8,64,384]{2,1,0:T(8,128)(2,1)S(1)}, u32[]{:S(2)}, u32[]{:S(2)}) collective-permute-start(bf16[8,64,384]{2,1,0:T(8,128)(2,1)S(1)} %collective-permute-done.2.refs_0_), channel_id=1, source_target_pairs={{0,2},{1,3},{2,0},{3,1},{4,6},{5,7},{6,4},{7,5},{8,10},{9,11},{10,... | collective-permute-start | bytes 1179656 | tf_op jit(solution)/shard_map/ppermute | solution.py:345
  18.0 10.7 %collective-permute-start.4 = (bf16[8,64,384]{2,1,0:T(8,128)(2,1)S(1)}, bf16[8,64,384]{2,1,0:T(8,128)(2,1)S(1)}, u32[]{:S(2)}, u32[]{:S(2)}) collective-permute-start(bf16[8,64,384]{2,1,0:T(8,128)(2,1)S(1)} %collective-permute-done.2.refs_0_), channel_id=1, source_target_pairs={{0,1},{1,0},{2,3},{3,2},{4,5},{5,4},{6,7},{7,6},{8,9},{9,8},{10,11... | collective-permute-start | bytes 1179656 | tf_op jit(solution)/shard_map/ppermute | solution.py:345
  18.0 1.0 %copy-start.1 = (bf16[8,64,384]{2,1,0:T(8,128)(2,1)S(1)}, bf16[8,64,384]{2,1,0:T(8,128)(2,1)}, u32[]{:S(2)}) copy-start(bf16[8,64,384]{2,1,0:T(8,128)(2,1)} %refs_3_.1) | copy-start | bytes 1179652
  28.7 7.5 %collective-permute-start.7 = (bf16[8,64,384]{2,1,0:T(8,128)(2,1)S(1)}, bf16[8,64,384]{2,1,0:T(8,128)(2,1)S(1)}, u32[]{:S(2)}, u32[]{:S(2)}) collective-permute-start(bf16[8,64,384]{2,1,0:T(8,128)(2,1)S(1)} %collective-permute-done.5.refs_1_), channel_id=1, source_target_pairs={{0,1},{1,0},{2,3},{3,2},{4,5},{5,4},{6,7},{7,6},{8,9},{9,8},{10,11... | collective-permute-start | bytes 1179656 | tf_op jit(solution)/shard_map/ppermute | solution.py:345
  28.7 12.4 %collective-permute-start.10 = (bf16[8,64,384]{2,1,0:T(8,128)(2,1)S(1)}, bf16[8,64,384]{2,1,0:T(8,128)(2,1)S(1)}, u32[]{:S(2)}, u32[]{:S(2)}) collective-permute-start(bf16[8,64,384]{2,1,0:T(8,128)(2,1)S(1)} %collective-permute-done.6.refs_0_), channel_id=1, source_target_pairs={{0,4},{1,5},{2,6},{3,7},{4,12},{5,13},{6,14},{7,15},{8,0},{9,1},{1... | collective-permute-start | bytes 1179656 | tf_op jit(solution)/shard_map/ppermute | solution.py:342
  31.7 11.2 %collective-permute-start.9 = (bf16[8,64,384]{2,1,0:T(8,128)(2,1)S(1)}, bf16[8,64,384]{2,1,0:T(8,128)(2,1)S(1)}, u32[]{:S(2)}, u32[]{:S(2)}) collective-permute-start(bf16[8,64,384]{2,1,0:T(8,128)(2,1)S(1)} %collective-permute-done.6.refs_0_), channel_id=1, source_target_pairs={{0,2},{1,3},{2,0},{3,1},{4,6},{5,7},{6,4},{7,5},{8,10},{9,11},{10,... | collective-permute-start | bytes 1179656 | tf_op jit(solution)/shard_map/ppermute | solution.py:345
  32.2 10.7 %collective-permute-start.8 = (bf16[8,64,384]{2,1,0:T(8,128)(2,1)S(1)}, bf16[8,64,384]{2,1,0:T(8,128)(2,1)S(1)}, u32[]{:S(2)}, u32[]{:S(2)}) collective-permute-start(bf16[8,64,384]{2,1,0:T(8,128)(2,1)S(1)} %collective-permute-done.6.refs_0_), channel_id=1, source_target_pairs={{0,1},{1,0},{2,3},{3,2},{4,5},{5,4},{6,7},{7,6},{8,9},{9,8},{10,11... | collective-permute-start | bytes 1179656 | tf_op jit(solution)/shard_map/ppermute | solution.py:345
  43.0 1.7 %collective-permute-start.13 = (bf16[8,64,384]{2,1,0:T(8,128)(2,1)S(1)}, bf16[8,64,384]{2,1,0:T(8,128)(2,1)S(1)}, u32[]{:S(2)}, u32[]{:S(2)}) collective-permute-start(bf16[8,64,384]{2,1,0:T(8,128)(2,1)S(1)} %collective-permute-done.9.refs_1_), channel_id=1, source_target_pairs={{0,1},{1,0},{2,3},{3,2},{4,5},{5,4},{6,7},{7,6},{8,9},{9,8},{10,11... | collective-permute-start | bytes 1179656 | tf_op jit(solution)/shard_map/ppermute | solution.py:345
  43.0 2.3 %collective-permute-start.12 = (bf16[8,64,384]{2,1,0:T(8,128)(2,1)S(1)}, bf16[8,64,384]{2,1,0:T(8,128)(2,1)S(1)}, u32[]{:S(2)}, u32[]{:S(2)}) collective-permute-start(bf16[8,64,384]{2,1,0:T(8,128)(2,1)S(1)} %collective-permute-done.10.refs_0_), channel_id=1, source_target_pairs={{0,1},{1,0},{2,3},{3,2},{4,5},{5,4},{6,7},{7,6},{8,9},{9,8},{10,11... | collective-permute-start | bytes 1179656 | tf_op jit(solution)/shard_map/ppermute | solution.py:345
  43.5 11.0 %collective-permute-start.11 = (bf16[8,64,384]{2,1,0:T(8,128)(2,1)S(1)}, bf16[8,64,384]{2,1,0:T(8,128)(2,1)S(1)}, u32[]{:S(2)}, u32[]{:S(2)}) collective-permute-start(bf16[8,64,384]{2,1,0:T(8,128)(2,1)S(1)} %collective-permute-done.10.refs_0_), channel_id=1, source_target_pairs={{0,2},{1,3},{2,0},{3,1},{4,6},{5,7},{6,4},{7,5},{8,10},{9,11},{10,... | collective-permute-start | bytes 1179656 | tf_op jit(solution)/shard_map/ppermute | solution.py:345
  54.5 16.3 %copy-start.3 = (s32[8]{0:T(128)S(1)}, s32[8]{0:T(128)}, u32[]{:S(2)}) copy-start(s32[8]{0:T(128)} %counts_hbm.1) | copy-start | bytes 100
  54.5 1.7 %collective-permute-start.14 = (bf16[8,64,384]{2,1,0:T(8,128)(2,1)S(1)}, bf16[8,64,384]{2,1,0:T(8,128)(2,1)S(1)}, u32[]{:S(2)}, u32[]{:S(2)}) collective-permute-start(bf16[8,64,384]{2,1,0:T(8,128)(2,1)S(1)} %collective-permute-done.11.refs_0_), channel_id=1, source_target_pairs={{0,1},{1,0},{2,3},{3,2},{4,5},{5,4},{6,7},{7,6},{8,9},{9,8},{10,11... | collective-permute-start | bytes 1179656 | tf_op jit(solution)/shard_map/ppermute | solution.py:345

commit v8 on v7

--- a/solution.py
+++ b/solution.py
@@ -24,20 +24,12 @@
 
 
 def prepare_kernel(
-    depth, shard_tiles,
-    me_ref, counts_hbm, irrep_hbm, v_ref,
-    res_ref, sorted_ref, gathered_ref, stats_ref, order_ref, begin_ref, item_ref,
-    counts_ref, irrep_ref, blank_ref, size_ref, first_ref, next_ref, cursor_ref, call_ref,
-    sem, blank_sem, counts_sem, irrep_sem,
+    counts_ref, irrep_ref, v_ref,
+    res_ref, sorted_ref, gathered_ref, stats_ref, order_ref, size_ref, first_ref,
+    blank_ref, next_ref, sem, blank_sem,
 ):
     own_tiles = v_ref.shape[0]
     irreps = counts_ref.shape[0]
-    rows = v_ref.shape[1]
-    most = item_ref.shape[0] // 6
-    counts_copy = pltpu.make_async_copy(counts_hbm, counts_ref, counts_sem)
-    irrep_copy = pltpu.make_async_copy(irrep_hbm, irrep_ref, irrep_sem)
-    counts_copy.start()
-    irrep_copy.start()
     blank_ref[...] = jnp.zeros(blank_ref.shape, blank_ref.dtype)
     group = blank_ref.shape[0]
     for l in range(0, own_tiles, group):
@@ -45,8 +37,6 @@
 
     for s in range(irreps):
         size_ref[s] = 0
-    counts_copy.wait()
-    irrep_copy.wait()
 
     def count(l, carry):
         s = irrep_ref[l]
@@ -72,17 +62,71 @@
     for buffer in (sorted_ref, gathered_ref):
         spare = jnp.zeros((BATCH, *buffer.shape[1:]), buffer.dtype)
         buffer[pl.ds(buffer.shape[0] - BATCH, BATCH)] = spare
+    shape = stats_ref.shape[1:]
+    at_row = lax.broadcasted_iota(jnp.int32, shape, 0)
+    at_lane = lax.broadcasted_iota(jnp.int32, shape, 1)
+    sizes = jnp.zeros(shape, jnp.int32)
+    for s in range(irreps):
+        sizes = jnp.where((at_row == s) & (at_lane == 0), size_ref[s], sizes)
+    stats_ref[0] = jnp.zeros(shape, jnp.float32)
+    stats_ref[1] = sizes.astype(jnp.float32)
+    pltpu.make_async_copy(v_ref, sorted_ref.at[pl.ds(0, own_tiles)], sem).wait()
+    pltpu.make_async_copy(res_ref, res_ref, blank_sem).wait()
+
+
+def prepare(counts, irrep, integrals, depth, shard_tiles):
+    own_tiles, rows, width = integrals.shape
+    irreps = counts.shape[0]
+    columns = shard_tiles * depth * rows
+    smem = pl.BlockSpec(memory_space=pltpu.SMEM)
+    vmem = pl.BlockSpec(memory_space=pltpu.VMEM)
+    anywhere = pl.BlockSpec(memory_space=pl.ANY)
+    return pl.pallas_call(
+        prepare_kernel,
+        out_shape=(
+            jax.ShapeDtypeStruct((own_tiles, rows, columns), jnp.bfloat16),
+            jax.ShapeDtypeStruct((own_tiles + BATCH, rows, width), integrals.dtype),
+            jax.ShapeDtypeStruct((4 * shard_tiles * depth + BATCH, rows, width), jnp.bfloat16),
+            jax.ShapeDtypeStruct((2, irreps, 128), jnp.float32),
+            jax.ShapeDtypeStruct((own_tiles,), jnp.int32),
+            jax.ShapeDtypeStruct((irreps,), jnp.int32),
+            jax.ShapeDtypeStruct((irreps,), jnp.int32),
+        ),
+        in_specs=[smem, smem, anywhere],
+        out_specs=(anywhere, vmem, vmem, vmem, smem, smem, smem),
+        scratch_shapes=[
+            pltpu.VMEM((2, rows, columns), jnp.bfloat16),
+            pltpu.SMEM((irreps,), jnp.int32),
+            pltpu.SemaphoreType.DMA,
+            pltpu.SemaphoreType.DMA,
+        ],
+        compiler_params=pltpu.CompilerParams(vmem_limit_bytes=32 * 1024 * 1024),
+        cost_estimate=pl.CostEstimate(
+            flops=0, bytes_accessed=2 * own_tiles * rows * columns, transcendentals=0
+        ),
+        name="prepare",
+    )(counts, irrep, integrals)
+
+
+def plan_kernel(
+    depth, shard_tiles, rows, own_tiles,
+    me_ref, counts_ref, size_ref, first_ref, begin_ref, item_ref, cursor_ref, call_ref,
+):
+    irreps = counts_ref.shape[0]
+    calls = begin_ref.shape[0] - 1
+    most = item_ref.shape[0] // 6
 
     me = me_ref[0]
     z, y, core = me // 4, me // 2 % 2, me % 2
     for shard in range(4 * depth):
         lag = lax.rem(ring_place(z, depth) - ring_place(jnp.int32(shard // 4), depth) + depth, depth)
-        own_y = jnp.where(core == shard % 2, jnp.maximum(lag - 1, 0), jnp.minimum(lag, depth - 2))
+        same_core = core == shard % 2
+        own_y = jnp.where(same_core, jnp.maximum(lag - 1, 0), jnp.minimum(lag, depth - 2))
         other_y = jnp.where(
-            (core == shard % 2) | (lag == depth - 1), lag, jnp.minimum(lag + 1, depth - 2)
+            same_core | (lag == depth - 1), lag, jnp.minimum(lag + 1, depth - 2)
         )
         call_ref[shard] = jnp.where(y == shard // 2 % 2, own_y, other_y)
-    for call in range(depth):
+    for call in range(calls):
         cursor_ref[call] = 0
 
     def walk(visit):
@@ -93,9 +137,7 @@
             def block(j, carry):
                 low = offset + j * BATCH
                 high = offset + jnp.minimum(tiles, j * BATCH + BATCH) - 1
-                call = jnp.maximum(
-                    call_ref[low // shard_tiles], call_ref[high // shard_tiles]
-                )
+                call = jnp.maximum(call_ref[low // shard_tiles], call_ref[high // shard_tiles])
                 visit(s, j, low, tiles, batches, call)
                 return carry
 
@@ -123,75 +165,40 @@
 
     walk(tally)
     begin = jnp.int32(0)
-    for call in range(depth):
+    for call in range(calls):
         begin_ref[call] = begin
         items = cursor_ref[call]
         cursor_ref[call] = begin
         begin = begin + (items + UNROLL - 1) // UNROLL * UNROLL
-    begin_ref[depth] = begin
+    begin_ref[calls] = begin
     walk(enter)
-    for call in range(depth):
+    for call in range(calls):
         def fill(n, carry):
             write(n, own_tiles, 0, 0, 0, 0, 0)
             return carry
 
         lax.fori_loop(cursor_ref[call], begin_ref[call + 1], fill, 0)
 
-    shape = stats_ref.shape[2:]
-    at_row = lax.broadcasted_iota(jnp.int32, shape, 0)
-    at_lane = lax.broadcasted_iota(jnp.int32, shape, 1)
-    sizes = jnp.zeros(shape, jnp.int32)
-    for s in range(irreps):
-        sizes = jnp.where((at_row == s) & (at_lane == 0), size_ref[s], sizes)
-    stats_ref[0, 0] = jnp.zeros(shape, jnp.float32)
-    stats_ref[0, 1] = sizes.astype(jnp.float32)
-    pltpu.make_async_copy(v_ref, sorted_ref.at[pl.ds(0, own_tiles)], sem).wait()
-    pltpu.make_async_copy(res_ref, res_ref, blank_sem).wait()
-
-
-def prepare(me, counts, irrep, integrals, depth, shard_tiles):
-    own_tiles, rows, width = integrals.shape
+
+def plan(me, counts, size, first, depth, shard_tiles, rows, own_tiles):
     irreps = counts.shape[0]
-    capacity = shard_tiles * depth
-    all_tiles = 4 * shard_tiles * depth
-    most = (all_tiles // BATCH + irreps) * (own_tiles // BATCH) + depth * UNROLL
+    calls = depth
+    blocks = 4 * shard_tiles * depth // BATCH + irreps
+    most = blocks * (own_tiles // BATCH) + calls * UNROLL
     smem = pl.BlockSpec(memory_space=pltpu.SMEM)
-    vmem = pl.BlockSpec(memory_space=pltpu.VMEM)
-    anywhere = pl.BlockSpec(memory_space=pl.ANY)
-    hbm = pl.BlockSpec(memory_space=pltpu.HBM)
     return pl.pallas_call(
-        functools.partial(prepare_kernel, depth, shard_tiles),
+        functools.partial(plan_kernel, depth, shard_tiles, rows, own_tiles),
         out_shape=(
-            jax.ShapeDtypeStruct((own_tiles, rows, capacity * rows), jnp.bfloat16),
-            jax.ShapeDtypeStruct((own_tiles + BATCH, rows, width), integrals.dtype),
-            jax.ShapeDtypeStruct((all_tiles + BATCH, rows, width), jnp.bfloat16),
-            jax.ShapeDtypeStruct((1, 2, irreps, 128), jnp.float32),
-            jax.ShapeDtypeStruct((own_tiles,), jnp.int32),
-            jax.ShapeDtypeStruct((depth + 1,), jnp.int32),
+            jax.ShapeDtypeStruct((calls + 1,), jnp.int32),
             jax.ShapeDtypeStruct((6 * most,), jnp.int32),
         ),
-        in_specs=[smem, hbm, hbm, hbm],
-        out_specs=(anywhere, vmem, vmem, vmem, smem, smem, smem),
+        in_specs=[smem] * 4,
+        out_specs=(smem, smem),
         scratch_shapes=[
-            pltpu.SMEM((irreps,), jnp.int32),
-            pltpu.SMEM((own_tiles,), jnp.int32),
-            pltpu.VMEM((2, rows, capacity * rows), jnp.bfloat16),
-            pltpu.SMEM((irreps,), jnp.int32),
-            pltpu.SMEM((irreps,), jnp.int32),
-            pltpu.SMEM((irreps,), jnp.int32),
-            pltpu.SMEM((depth,), jnp.int32),
-            pltpu.SMEM((4 * depth,), jnp.int32),
-            pltpu.SemaphoreType.DMA,
-            pltpu.SemaphoreType.DMA,
-            pltpu.SemaphoreType.DMA,
-            pltpu.SemaphoreType.DMA,
+            pltpu.SMEM((calls,), jnp.int32), pltpu.SMEM((4 * depth,), jnp.int32)
         ],
-        compiler_params=pltpu.CompilerParams(vmem_limit_bytes=32 * 1024 * 1024),
-        cost_estimate=pl.CostEstimate(
-            flops=0, bytes_accessed=2 * own_tiles * rows * capacity * rows, transcendentals=0
-        ),
-        name="prepare",
-    )(me, counts, irrep, integrals)
+        name="plan",
+    )(me, counts, size, first)
 
 
 def ladder_kernel(
@@ -273,9 +280,8 @@
     )
     sums = jnp.sum(acc_ref[...], axis=1)
     sums = sum(sums[:, k:k + 128] for k in range(0, side, 128))
-    for copy in range(stats_ref.shape[0]):
-        stats_ref[copy, 0] = stats_in_ref[0, 0] + sums
-        stats_ref[copy, 1] = stats_in_ref[0, 1]
+    stats_ref[0] = stats_in_ref[0] + sums
+    stats_ref[1] = stats_in_ref[1]
 
     def finish(n, carry):
         pltpu.make_async_copy(
@@ -286,11 +292,12 @@
     lax.fori_loop(0, started, finish, 0)
 
 
-def ladder(call, depth, shard_tiles, me, plan, state, fresh, layout, copies=1):
-    ordered, order, begin, items = plan
+def ladder(call, depth, shard_tiles, me, listing, state, arrived):
+    ordered, order, begin, items = listing
     residual, gathered, stats = state
+    layout, fresh = tuple(arrived), tuple(arrived.values())
     slots, rows, width = ordered.shape
-    irreps = stats.shape[2]
+    irreps = stats.shape[1]
     smem = pl.BlockSpec(memory_space=pltpu.SMEM)
     vmem = pl.BlockSpec(memory_space=pltpu.VMEM)
     anywhere = pl.BlockSpec(memory_space=pl.ANY)
@@ -302,7 +309,7 @@
         out_shape=(
             jax.ShapeDtypeStruct(residual.shape, residual.dtype),
             jax.ShapeDtypeStruct(gathered.shape, gathered.dtype),
-            jax.ShapeDtypeStruct((copies, 2, irreps, 128), jnp.float32),
+            jax.ShapeDtypeStruct(stats.shape, stats.dtype),
         ),
         in_specs=[smem] * 4 + [vmem] * 2 + [anywhere, vmem] + [
             hbm if where == (0, 0, 0) else anywhere for where in layout
@@ -344,42 +351,46 @@
     def swap(x, bits):
         return lax.ppermute(x, "vir", [(d, d ^ bits) for d in range(devices)])
 
-    residual, ordered, gathered, stats, order, begin, items = prepare(
-        me, ij_counts, ab_irrep, integrals, depth, shard_tiles
+    residual, ordered, gathered, stats, order, size, first = prepare(
+        ij_counts, ab_irrep, integrals, depth, shard_tiles
     )
-    plan = (ordered, order, begin, items)
     state = (residual, gathered, stats)
 
     a, b, c, d = [amplitudes], [], [], []
     for k in range(depth):
         if k:
-            d[-1:], c[-1], b[-1], a[k], state = lax.optimization_barrier(
-                (d[-1:], c[-1], b[-1], a[k], state)
+            c[-1], a[k], b[-1], d[-1:], state = lax.optimization_barrier(
+                (c[-1], a[k], b[-1], d[-1:], state)
             )
+        b.append(swap(a[k], 2))
         if k < depth - 1:
             a.append(shift_z(a[k]))
-        b.append(swap(a[k], 2))
         c.append(swap(a[k], 1))
-        if k:
-            d.append(swap(b[k - 1], 1))
-            fresh = {(k, 0, 0): a[k], (k - 1, 1, 0): b[k - 1], (k - 1, 0, 1): c[k - 1]}
-            if k == 1:
-                fresh[0, 0, 0] = a[0]
-            else:
-                fresh[k - 2, 1, 1] = d[k - 2]
-            if k == depth - 1:
-                fresh[k, 0, 1], fresh[k - 1, 1, 1] = c[k], d[k - 1]
-            state = ladder(
-                k - 1, depth, shard_tiles, me, plan, state, tuple(fresh.values()), tuple(fresh)
+        if k == 0:
+            continue
+        d.append(swap(b[k - 1], 1))
+        arrived = {(k, 0, 0): a[k], (k - 1, 1, 0): b[k - 1], (k - 1, 0, 1): c[k - 1]}
+        if k == 1:
+            arrived[0, 0, 0] = a[0]
+            me, state = lax.optimization_barrier((me, state))
+            begin, items = plan(
+                me, ij_counts, size, first, depth, shard_tiles, rows, integrals.shape[0]
             )
-    last, *state = lax.optimization_barrier((b[-1], *state))
+            listing = (ordered, order, begin, items)
+        else:
+            arrived[k - 2, 1, 1] = d[k - 2]
+        if k == depth - 1:
+            arrived[k, 0, 1], arrived[k - 1, 1, 1] = c[k], d[k - 1]
+        state = ladder(k - 1, depth, shard_tiles, me, listing, state, arrived)
+    last, state = lax.optimization_barrier((b[-1], state))
     residual, _, stats = ladder(
-        depth - 1, depth, shard_tiles, me, plan, state,
-        (last, swap(last, 1)), ((depth - 1, 1, 0), (depth - 1, 1, 1)), devices,
+        depth - 1, depth, shard_tiles, me, listing, state,
+        {(depth - 1, 1, 0): last, (depth - 1, 1, 1): swap(last, 1)},
     )
 
-    stats = lax.all_to_all(stats, "vir", 0, 0, tiled=True)
-    irrep_sums, ab_counts = jnp.sum(stats, axis=(0, 3))
+    stats = sum([swap(stats, bits) for bits in (1, 2, 3)], stats)
+    stats = sum([swap(stats, 4 * bits) for bits in range(1, depth)], stats)
+    irrep_sums, ab_counts = jnp.sum(stats, axis=2)
     entries = ab_counts * ij_counts.astype(jnp.float32) * float(rows * rows)
     return residual, jnp.sqrt(irrep_sums / entries + 1e-06)
 

time: 71.6 us -> 75.7 us (1.057)
  blocking collectives: 11.6 us -> 0 us
  local copies, waits for them, and re-layouts: 3.72 us -> 13.4 us
  starting transfers between devices: 10.8 us -> 18.8 us
  waiting for transfers between devices: 20.8 us -> 16.2 us
  Pallas kernels: 23.1 us -> 25.5 us
    all_to_all x1 -> x0, blocking collectives: 11.6 us -> none  [per_device(): stats = lax.all_to_all(stats, 'vir', 0, 0, tiled=True)]
    ppermute x3, waiting for transfers between devices: 13.1 us -> 2.38 us  [shift_z(): return lax.ppermute(x, 'vir', hop)]
    unnamed x10 -> x28, local copies, waits for them, and re-layouts: 3.72 us -> 13.4 us
    ppermute x12 -> x18, starting transfers between devices: 4.97 us -> 12.2 us  [swap(): return lax.ppermute(x, 'vir', [(d, d ^ bits) for d in range(devices)])]
    ppermute x12 -> x18, waiting for transfers between devices: 7.74 us -> 13.8 us  [swap(): return lax.ppermute(x, 'vir', [(d, d ^ bits) for d in range(devices)])]
    pallas_call x1 -> x2, Pallas kernels: 6.59 us -> 8.33 us  [the longest x1 4.47 us: prepare(): pl.pallas_call(prepare_kernel, out_shape=(jax.ShapeDtypeStruct((own_tiles...]
  transfers between devices with their start and end apart: 15 -> 21, of which waited for: 8 -> 10; matrix products, arithmetic and copies ran while one was open for 0% -> 0% of each run, Pallas kernels for 28% -> 30%
where the time goes in v8:
time: 75.7 us; the launch traced here: 75.2 us
  Pallas kernels  25.5 us (34%)
  starting transfers between devices  18.8 us (25%)
  waiting for transfers between devices  16.2 us (21%)
  local copies, waits for them, and re-layouts  13.4 us (18%)
  between operations  0.78 us (1%)
    pallas_call x4, Pallas kernels, ladder(): pl.pallas_call(functools.partial(ladder_kernel, call, depth, shard_tiles,...  17.1 us
    ppermute x18, waiting for transfers between devices, swap(): return lax.ppermute(x, 'vir', [(d, d ^ bits) for d in range(devices)])  13.8 us
    unnamed x28, local copies, waits for them, and re-layouts  13.4 us
    ppermute x18, starting transfers between devices, swap(): return lax.ppermute(x, 'vir', [(d, d ^ bits) for d in range(devices)])  12.2 us
    ppermute x3, starting transfers between devices, shift_z(): return lax.ppermute(x, 'vir', hop)  6.52 us
    pallas_call x1, Pallas kernels, prepare(): pl.pallas_call(prepare_kernel, out_shape=(jax.ShapeDtypeStruct((own_tiles...  4.47 us
    pallas_call x1, Pallas kernels, plan(): pl.pallas_call(functools.partial(plan_kernel, depth, shard_tiles, rows, o...  3.86 us
    ppermute x3, waiting for transfers between devices, shift_z(): return lax.ppermute(x, 'vir', hop)  2.38 us
  transfers between devices with their start and end apart: 21, of which 10 were waited for; matrix products, arithmetic and copies ran while one was open for 0% of the time, Pallas kernels for 30%

profile of v8, /device:TPU:0, one launch (start us, length us, event | category | flops | bytes accessed | tf_op | source)
XLA Modules:
  0.0 75.2 jit_solution(16614598092970361738)
XLA Ops:
  0.6 3.1 %collective-permute-start.1 = (bf16[8,64,384]{2,1,0:T(8,128)(2,1)}, bf16[8,64,384]{2,1,0:T(8,128)(2,1)S(1)}, u32[]{:S(2)}, u32[]{:S(2)}) collective-permute-start(bf16[8,64,384]{2,1,0:T(8,128)(2,1)} %refs_3_.1), channel_id=1, source_target_pairs={{0,4},{1,5},{2,6},{3,7},{4,12},{5,13},{6,14},{7,15},{8,0},{9,1},{1... | collective-permute-start | bytes 1179656 | tf_op jit(solution)/shard_map/ppermute | solution.py:349
  3.7 0.0 collective-permute-start
  3.7 1.5 %collective-permute-start.2 = (bf16[8,64,384]{2,1,0:T(8,128)(2,1)}, bf16[8,64,384]{2,1,0:T(8,128)(2,1)}, u32[]{:S(2)}, u32[]{:S(2)}) collective-permute-start(bf16[8,64,384]{2,1,0:T(8,128)(2,1)} %refs_3_.1), channel_id=1, source_target_pairs={{0,2},{1,3},{2,0},{3,1},{4,6},{5,7},{6,4},{7,5},{8,10},{9,11},{10,... | collective-permute-start | bytes 1179656 | tf_op jit(solution)/shard_map/ppermute | solution.py:352
  5.2 1.4 %copy-done.2 = bf16[32,64,384]{2,1,0:T(8,128)(2,1)S(1)} copy-done((bf16[32,64,384]{2,1,0:T(8,128)(2,1)S(1)}, bf16[32,64,384]{2,1,0:T(8,128)(2,1)}, u32[]{:S(2)}) %copy-start.2) | copy-done | bytes 1572888
  6.6 0.7 copy-done.9
  7.3 0.7 copy-done.11
  7.9 4.5 %prepare.1 = (bf16[32,64,2048]{2,1,0:T(8,128)(2,1)}, bf16[36,64,384]{2,1,0:T(8,128)(2,1)S(1)}, bf16[132,64,384]{2,1,0:T(8,128)(2,1)S(1)}, f32[2,8,128]{2,1,0:T(8...) custom-call(s32[8]{0:T(128)S(1)} %copy-done.9, s32[32]{0:T(128)S(1)} %copy-done.11, ...), custom_call_target="tpu_custom_call" | custom-call | bytes 8388608 | tf_op jit(solution)/shard_map/prepare/pallas_call | solution.py:84
  12.4 2.7 %copy-done = bf16[132,64,384]{2,1,0:T(8,128)(2,1)} copy-done((bf16[132,64,384]{2,1,0:T(8,128)(2,1)}, bf16[132,64,384]{2,1,0:T(8,128)(2,1)S(1)}, u32[]{:S(2)}) %copy-start) | copy-done | bytes 6488088
  15.2 0.5 copy-done.12
  15.7 0.5 copy-done.13
  16.2 0.0 collective-permute-done.1.refs_0_
  16.2 0.7 copy-done.4
  17.0 0.2 collective-permute-start.6
  17.2 0.5 collective-permute-start.5
  17.7 2.6 %collective-permute-start.4 = (bf16[8,64,384]{2,1,0:T(8,128)(2,1)S(1)}, bf16[8,64,384]{2,1,0:T(8,128)(2,1)S(1)}, u32[]{:S(2)}, u32[]{:S(2)}) collective-permute-start(bf16[8,64,384]{2,1,0:T(8,128)(2,1)S(1)} %collective-permute-done.1.refs_0_), channel_id=1, source_target_pairs={{0,4},{1,5},{2,6},{3,7},{4,12},{5,13},{6,14},{7,15},{8,0},{9,1},{1... | collective-permute-start | bytes 1179656 | tf_op jit(solution)/shard_map/ppermute | solution.py:349
  20.3 3.9 %plan.1 = (s32[5]{0:T(128)}, s32[2016]{0:T(1024)}) custom-call(s32[1]{0:T(128)} %bitcast.me_ref, s32[8]{0:T(128)} %counts_ref.3, s32[8]{0:T(128)} %copy-done.12, s32[8]{0:T(128)} %copy-done.13), custom_call_target="tpu_custom_call" | custom-call | tf_op jit(solution)/shard_map/plan/pallas_call | solution.py:189
  24.2 2.8 %copy-done.1 = bf16[132,64,384]{2,1,0:T(8,128)(2,1)S(1)} copy-done((bf16[132,64,384]{2,1,0:T(8,128)(2,1)S(1)}, bf16[132,64,384]{2,1,0:T(8,128)(2,1)}, u32[]{:S(2)}) %copy-start.1) | copy-done | bytes 6488088
  27.0 1.0 %copy-done.3 = bf16[8,64,384]{2,1,0:T(8,128)(2,1)S(1)} copy-done((bf16[8,64,384]{2,1,0:T(8,128)(2,1)S(1)}, bf16[8,64,384]{2,1,0:T(8,128)(2,1)}, u32[]{:S(2)}) %copy-start.3) | copy-done | bytes 393240
  28.0 1.0 %copy-done.5 = bf16[8,64,384]{2,1,0:T(8,128)(2,1)S(1)} copy-done((bf16[8,64,384]{2,1,0:T(8,128)(2,1)S(1)}, bf16[8,64,384]{2,1,0:T(8,128)(2,1)}, u32[]{:S(2)}) %copy-start.5) | copy-done | bytes 393240
  29.0 0.7 copy-done.6
  29.7 0.7 copy-done.8
  30.4 3.1 %ladder_0.1 = (bf16[32,64,2048]{2,1,0:T(8,128)(2,1)}, bf16[132,64,384]{2,1,0:T(8,128)(2,1)S(1)}, f32[2,8,128]{2,1,0:T(8,128)S(1)}) custom-call(s32[1]{0:T(128)} %bitcast.me_ref, s32[32]{0:T(128)S(1)} %get-tuple-element.57.order_ref, s32[5]{0:T(128)S(1)} %copy-done.8, s32[2016]{0:T(1024)S(1)} %copy-done.6, ...), custom_call_target="tpu_custom_call", output_to_operand_aliasing={{0}: (6, {}), {1}: (7, {})} | custom-call | flops 402653184 | bytes 2097152 | tf_op jit(solution)/shard_map/ladder_0/pallas_call | solution.py:307
  33.5 0.5 collective-permute-start.10
  34.1 2.3 %collective-permute-start.9 = (bf16[8,64,384]{2,1,0:T(8,128)(2,1)S(1)}, bf16[8,64,384]{2,1,0:T(8,128)(2,1)S(1)}, u32[]{:S(2)}, u32[]{:S(2)}) collective-permute-start(bf16[8,64,384]{2,1,0:T(8,128)(2,1)S(1)} %collective-permute-done.4.refs_0_), channel_id=1, source_target_pairs={{0,2},{1,3},{2,0},{3,1},{4,6},{5,7},{6,4},{7,5},{8,10},{9,11},{10,... | collective-permute-start | bytes 1179656 | tf_op jit(solution)/shard_map/ppermute | solution.py:352
  36.3 0.9 %collective-permute-start.8 = (bf16[8,64,384]{2,1,0:T(8,128)(2,1)S(1)}, bf16[8,64,384]{2,1,0:T(8,128)(2,1)S(1)}, u32[]{:S(2)}, u32[]{:S(2)}) collective-permute-start(bf16[8,64,384]{2,1,0:T(8,128)(2,1)S(1)} %collective-permute-done.4.refs_0_), channel_id=1, source_target_pairs={{0,4},{1,5},{2,6},{3,7},{4,12},{5,13},{6,14},{7,15},{8,0},{9,1},{1... | collective-permute-start | bytes 1179656 | tf_op jit(solution)/shard_map/ppermute | solution.py:349
  37.2 4.5 %ladder_1.1 = (bf16[32,64,2048]{2,1,0:T(8,128)(2,1)}, bf16[132,64,384]{2,1,0:T(8,128)(2,1)S(1)}, f32[2,8,128]{2,1,0:T(8,128)S(1)}) custom-call(s32[1]{0:T(128)} %bitcast.me_ref, s32[32]{0:T(128)S(1)} %get-tuple-element.57.order_ref, s32[5]{0:T(128)S(1)} %copy-done.8, s32[2016]{0:T(1024)S(1)} %copy-done.7, ...), custom_call_target="tpu_custom_call", output_to_operand_aliasing={{0}: (6, {}), {1}: (7, {})} | custom-call | flops 402653184 | bytes 2097152 | tf_op jit(solution)/shard_map/ladder_1/pallas_call | solution.py:307
  41.7 4.3 %collective-permute-done.9.refs_1_ = bf16[8,64,384]{2,1,0:T(8,128)(2,1)S(1)} collective-permute-done((bf16[8,64,384]{2,1,0:T(8,128)(2,1)S(1)}, bf16[8,64,384]{2,1,0:T(8,128)(2,1)S(1)}, u32[]{:S(2)}, u32[]{:S(2)}) %collective-permute-start.9) | collective-permute-done | bytes 393248 | tf_op jit(solution)/shard_map/ppermute | solution.py:352
  46.0 2.4 %collective-permute-done.8.refs_0_ = bf16[8,64,384]{2,1,0:T(8,128)(2,1)S(1)} collective-permute-done((bf16[8,64,384]{2,1,0:T(8,128)(2,1)S(1)}, bf16[8,64,384]{2,1,0:T(8,128)(2,1)S(1)}, u32[]{:S(2)}, u32[]{:S(2)}) %collective-permute-start.8) | collective-permute-done | bytes 393248 | tf_op jit(solution)/shard_map/ppermute | solution.py:349
  48.4 0.5 collective-permute-start.12
  48.9 0.3 collective-permute-start.11
  49.2 0.9 %collective-permute-done.13.refs_5_ = bf16[8,64,384]{2,1,0:T(8,128)(2,1)S(1)} collective-permute-done((bf16[8,64,384]{2,1,0:T(8,128)(2,1)S(1)}, bf16[8,64,384]{2,1,0:T(8,128)(2,1)S(1)}, u32[]{:S(2)}, u32[]{:S(2)}) %collective-permute-start.13) | collective-permute-done | bytes 393248 | tf_op jit(solution)/shard_map/ppermute | solution.py:352
  50.1 0.6 collective-permute-done.12.refs_4_
  50.7 6.8 %ladder_2.1 = (bf16[32,64,2048]{2,1,0:T(8,128)(2,1)}, bf16[132,64,384]{2,1,0:T(8,128)(2,1)S(1)}, f32[2,8,128]{2,1,0:T(8,128)S(1)}) custom-call(s32[1]{0:T(128)} %bitcast.me_ref, s32[32]{0:T(128)S(1)} %get-tuple-element.57.order_ref, s32[5]{0:T(128)S(1)} %copy-done.8, s32[2016]{0:T(1024)S(1)} %copy-done.7, ...), custom_call_target="tpu_custom_call", output_to_operand_aliasing={{0}: (6, {}), {1}: (7, {})} | custom-call | flops 603979776 | bytes 3145728 | tf_op jit(solution)/shard_map/ladder_2/pallas_call | solution.py:307
  57.5 2.5 %collective-permute-done.11.refs_0_ = bf16[8,64,384]{2,1,0:T(8,128)(2,1)S(1)} collective-permute-done((bf16[8,64,384]{2,1,0:T(8,128)(2,1)S(1)}, bf16[8,64,384]{2,1,0:T(8,128)(2,1)S(1)}, u32[]{:S(2)}, u32[]{:S(2)}) %collective-permute-start.11) | collective-permute-done | bytes 393248 | tf_op jit(solution)/shard_map/ppermute | solution.py:352
  60.0 1.7 %collective-permute-done.14.refs_1_ = bf16[8,64,384]{2,1,0:T(8,128)(2,1)S(1)} collective-permute-done((bf16[8,64,384]{2,1,0:T(8,128)(2,1)S(1)}, bf16[8,64,384]{2,1,0:T(8,128)(2,1)S(1)}, u32[]{:S(2)}, u32[]{:S(2)}) %collective-permute-start.14) | collective-permute-done | bytes 393248 | tf_op jit(solution)/shard_map/ppermute | solution.py:352
  61.7 2.8 %ladder_3.1 = (bf16[32,64,2048]{2,1,0:T(8,128)(2,1)}, bf16[132,64,384]{2,1,0:T(8,128)(2,1)S(1)}, f32[2,8,128]{2,1,0:T(8,128)S(1)}) custom-call(s32[1]{0:T(128)} %bitcast.me_ref, s32[32]{0:T(128)S(1)} %get-tuple-element.57.order_ref, s32[5]{0:T(128)S(1)} %copy-done.8, s32[2016]{0:T(1024)S(1)} %copy-done.7, ...), custom_call_target="tpu_custom_call", output_to_operand_aliasing={{0}: (6, {}), {1}: (7, {})} | custom-call | flops 201326592 | bytes 1048576 | tf_op jit(solution)/shard_map/ladder_3/pallas_call | solution.py:307
  64.5 0.1 collective-permute-start.17
  64.6 1.8 %collective-permute-start.16 = (f32[2,8,128]{2,1,0:T(8,128)S(1)}, f32[2,8,128]{2,1,0:T(8,128)S(1)}, u32[]{:S(2)}, u32[]{:S(2)}) collective-permute-start(f32[2,8,128]{2,1,0:T(8,128)S(1)} %get-tuple-element.97), channel_id=1, source_target_pairs={{0,2},{1,3},{2,0},{3,1},{4,6},{5,7},{6,4},{7,5},{8,10},{9,11},{10,... | collective-permute-start | bytes 24584 | tf_op jit(solution)/shard_map/ppermute | solution.py:352
  66.4 0.0 collective-permute-start.15
  66.4 1.2 %collective-permute-done.17 = f32[2,8,128]{2,1,0:T(8,128)S(1)} collective-permute-done((f32[2,8,128]{2,1,0:T(8,128)S(1)}, f32[2,8,128]{2,1,0:T(8,128)S(1)}, u32[]{:S(2)}, u32[]{:S(2)}) %collective-permute-start.17) | collective-permute-done | bytes 8224 | tf_op jit(solution)/shard_map/ppermute | solution.py:352
  67.7 0.7 collective-permute-done.16
  68.3 1.7 %collective-permute-start.20 = (f32[2,8,128]{2,1,0:T(8,128)S(1)}, f32[2,8,128]{2,1,0:T(8,128)S(1)}, u32[]{:S(2)}, u32[]{:S(2)}) collective-permute-start(f32[2,8,128]{2,1,0:T(8,128)S(1)} %add_add_fusion), channel_id=1, source_target_pairs={{0,12},{1,13},{2,14},{3,15},{4,8},{5,9},{6,10},{7,11},{8,4},{9,5},... | collective-permute-start | bytes 24584 | tf_op jit(solution)/shard_map/ppermute | solution.py:352
  70.1 0.7 collective-permute-start.19
  70.8 2.0 %collective-permute-start.18 = (f32[2,8,128]{2,1,0:T(8,128)S(1)}, f32[2,8,128]{2,1,0:T(8,128)S(1)}, u32[]{:S(2)}, u32[]{:S(2)}) collective-permute-start(f32[2,8,128]{2,1,0:T(8,128)S(1)} %add_add_fusion), channel_id=1, source_target_pairs={{0,4},{1,5},{2,6},{3,7},{4,0},{5,1},{6,2},{7,3},{8,12},{9,13},{10,... | collective-permute-start | bytes 24584 | tf_op jit(solution)/shard_map/ppermute | solution.py:352
  72.8 1.1 %collective-permute-done.20 = f32[2,8,128]{2,1,0:T(8,128)S(1)} collective-permute-done((f32[2,8,128]{2,1,0:T(8,128)S(1)}, f32[2,8,128]{2,1,0:T(8,128)S(1)}, u32[]{:S(2)}, u32[]{:S(2)}) %collective-permute-start.20) | collective-permute-done | bytes 8224 | tf_op jit(solution)/shard_map/ppermute | solution.py:352
  73.8 0.8 %collective-permute-done.19 = f32[2,8,128]{2,1,0:T(8,128)S(1)} collective-permute-done((f32[2,8,128]{2,1,0:T(8,128)S(1)}, f32[2,8,128]{2,1,0:T(8,128)S(1)}, u32[]{:S(2)}, u32[]{:S(2)}) %collective-permute-start.19) | collective-permute-done | bytes 8224 | tf_op jit(solution)/shard_map/ppermute | solution.py:352
  74.6 0.1 add_reduce_fusion
  74.7 0.5 add_sqrt_fusion
  (31 shorter events, 0.1 us)
Async XLA Ops:
  0.6 15.6 %collective-permute-start.1 = (bf16[8,64,384]{2,1,0:T(8,128)(2,1)}, bf16[8,64,384]{2,1,0:T(8,128)(2,1)S(1)}, u32[]{:S(2)}, u32[]{:S(2)}) collective-permute-start(bf16[8,64,384]{2,1,0:T(8,128)(2,1)} %refs_3_.1), channel_id=1, source_target_pairs={{0,4},{1,5},{2,6},{3,7},{4,12},{5,13},{6,14},{7,15},{8,0},{9,1},{1... | collective-permute-start | bytes 1179656 | tf_op jit(solution)/shard_map/ppermute | solution.py:349
  3.7 12.5 %collective-permute-start = (bf16[8,64,384]{2,1,0:T(8,128)(2,1)}, bf16[8,64,384]{2,1,0:T(8,128)(2,1)S(1)}, u32[]{:S(2)}, u32[]{:S(2)}) collective-permute-start(bf16[8,64,384]{2,1,0:T(8,128)(2,1)} %refs_3_.1), channel_id=1, source_target_pairs={{0,1},{1,0},{2,3},{3,2},{4,5},{5,4},{6,7},{7,6},{8,9},{9,8},{10,11... | collective-permute-start | bytes 1179656 | tf_op jit(solution)/shard_map/ppermute | solution.py:352
  3.7 13.3 %collective-permute-start.2 = (bf16[8,64,384]{2,1,0:T(8,128)(2,1)}, bf16[8,64,384]{2,1,0:T(8,128)(2,1)}, u32[]{:S(2)}, u32[]{:S(2)}) collective-permute-start(bf16[8,64,384]{2,1,0:T(8,128)(2,1)} %refs_3_.1), channel_id=1, source_target_pairs={{0,2},{1,3},{2,0},{3,1},{4,6},{5,7},{6,4},{7,5},{8,10},{9,11},{10,... | collective-permute-start | bytes 1179656 | tf_op jit(solution)/shard_map/ppermute | solution.py:352
  5.2 1.4 %copy-start.2 = (bf16[32,64,384]{2,1,0:T(8,128)(2,1)S(1)}, bf16[32,64,384]{2,1,0:T(8,128)(2,1)}, u32[]{:S(2)}) copy-start(bf16[32,64,384]{2,1,0:T(8,128)(2,1)} %v_ref.1) | copy-start | bytes 4718596
  6.6 0.7 copy-start.9
  7.3 0.7 copy-start.11
  12.4 2.7 %copy-start = (bf16[132,64,384]{2,1,0:T(8,128)(2,1)}, bf16[132,64,384]{2,1,0:T(8,128)(2,1)S(1)}, u32[]{:S(2)}) copy-start(bf16[132,64,384]{2,1,0:T(8,128)(2,1)S(1)} %get-tuple-element.67.gathered_in_ref) | copy-start | bytes 19464196
  15.2 0.5 copy-start.12
  15.7 0.5 copy-start.13
  16.2 0.8 copy-start.4
  17.0 16.5 %collective-permute-start.6 = (bf16[8,64,384]{2,1,0:T(8,128)(2,1)}, bf16[8,64,384]{2,1,0:T(8,128)(2,1)S(1)}, u32[]{:S(2)}, u32[]{:S(2)}) collective-permute-start(bf16[8,64,384]{2,1,0:T(8,128)(2,1)} %collective-permute-done.2.refs_1_), channel_id=1, source_target_pairs={{0,1},{1,0},{2,3},{3,2},{4,5},{5,4},{6,7},{7,6},{8,9},{9,8},{10,11... | collective-permute-start | bytes 1179656 | tf_op jit(solution)/shard_map/ppermute | solution.py:352
  17.2 16.3 %collective-permute-start.5 = (bf16[8,64,384]{2,1,0:T(8,128)(2,1)S(1)}, bf16[8,64,384]{2,1,0:T(8,128)(2,1)S(1)}, u32[]{:S(2)}, u32[]{:S(2)}) collective-permute-start(bf16[8,64,384]{2,1,0:T(8,128)(2,1)S(1)} %collective-permute-done.1.refs_0_), channel_id=1, source_target_pairs={{0,2},{1,3},{2,0},{3,1},{4,6},{5,7},{6,4},{7,5},{8,10},{9,11},{10,... | collective-permute-start | bytes 1179656 | tf_op jit(solution)/shard_map/ppermute | solution.py:352
  17.7 15.8 %collective-permute-start.4 = (bf16[8,64,384]{2,1,0:T(8,128)(2,1)S(1)}, bf16[8,64,384]{2,1,0:T(8,128)(2,1)S(1)}, u32[]{:S(2)}, u32[]{:S(2)}) collective-permute-start(bf16[8,64,384]{2,1,0:T(8,128)(2,1)S(1)} %collective-permute-done.1.refs_0_), channel_id=1, source_target_pairs={{0,4},{1,5},{2,6},{3,7},{4,12},{5,13},{6,14},{7,15},{8,0},{9,1},{1... | collective-permute-start | bytes 1179656 | tf_op jit(solution)/shard_map/ppermute | solution.py:349
  20.3 13.2 %collective-permute-start.3 = (bf16[8,64,384]{2,1,0:T(8,128)(2,1)S(1)}, bf16[8,64,384]{2,1,0:T(8,128)(2,1)}, u32[]{:S(2)}, u32[]{:S(2)}) collective-permute-start(bf16[8,64,384]{2,1,0:T(8,128)(2,1)S(1)} %collective-permute-done.1.refs_0_), channel_id=1, source_target_pairs={{0,1},{1,0},{2,3},{3,2},{4,5},{5,4},{6,7},{7,6},{8,9},{9,8},{10,11... | collective-permute-start | bytes 1179656 | tf_op jit(solution)/shard_map/ppermute | solution.py:352
  24.2 2.8 %copy-start.1 = (bf16[132,64,384]{2,1,0:T(8,128)(2,1)S(1)}, bf16[132,64,384]{2,1,0:T(8,128)(2,1)}, u32[]{:S(2)}) copy-start(bf16[132,64,384]{2,1,0:T(8,128)(2,1)} %copy-done) | copy-start | bytes 19464196
  27.0 1.0 %copy-start.3 = (bf16[8,64,384]{2,1,0:T(8,128)(2,1)S(1)}, bf16[8,64,384]{2,1,0:T(8,128)(2,1)}, u32[]{:S(2)}) copy-start(bf16[8,64,384]{2,1,0:T(8,128)(2,1)} %refs_3_.1) | copy-start | bytes 1179652
  28.0 1.0 %copy-start.5 = (bf16[8,64,384]{2,1,0:T(8,128)(2,1)S(1)}, bf16[8,64,384]{2,1,0:T(8,128)(2,1)}, u32[]{:S(2)}) copy-start(bf16[8,64,384]{2,1,0:T(8,128)(2,1)} %copy-done.4) | copy-start | bytes 1179652
  29.0 0.7 copy-start.6
  29.7 0.7 copy-start.8
  30.4 6.8 %copy-start.7 = (s32[2016]{0:T(1024)S(1)}, s32[2016]{0:T(1024)}, u32[]{:S(2)}) copy-start(s32[2016]{0:T(1024)} %get-tuple-element.61.item_ref) | copy-start | bytes 24196
  33.5 8.2 %collective-permute-start.10 = (bf16[8,64,384]{2,1,0:T(8,128)(2,1)S(1)}, bf16[8,64,384]{2,1,0:T(8,128)(2,1)S(1)}, u32[]{:S(2)}, u32[]{:S(2)}) collective-permute-start(bf16[8,64,384]{2,1,0:T(8,128)(2,1)S(1)} %collective-permute-done.5.refs_1_), channel_id=1, source_target_pairs={{0,1},{1,0},{2,3},{3,2},{4,5},{5,4},{6,7},{7,6},{8,9},{9,8},{10,11... | collective-permute-start | bytes 1179656 | tf_op jit(solution)/shard_map/ppermute | solution.py:352
  34.1 12.0 %collective-permute-start.9 = (bf16[8,64,384]{2,1,0:T(8,128)(2,1)S(1)}, bf16[8,64,384]{2,1,0:T(8,128)(2,1)S(1)}, u32[]{:S(2)}, u32[]{:S(2)}) collective-permute-start(bf16[8,64,384]{2,1,0:T(8,128)(2,1)S(1)} %collective-permute-done.4.refs_0_), channel_id=1, source_target_pairs={{0,2},{1,3},{2,0},{3,1},{4,6},{5,7},{6,4},{7,5},{8,10},{9,11},{10,... | collective-permute-start | bytes 1179656 | tf_op jit(solution)/shard_map/ppermute | solution.py:352
  36.3 12.1 %collective-permute-start.8 = (bf16[8,64,384]{2,1,0:T(8,128)(2,1)S(1)}, bf16[8,64,384]{2,1,0:T(8,128)(2,1)S(1)}, u32[]{:S(2)}, u32[]{:S(2)}) collective-permute-start(bf16[8,64,384]{2,1,0:T(8,128)(2,1)S(1)} %collective-permute-done.4.refs_0_), channel_id=1, source_target_pairs={{0,4},{1,5},{2,6},{3,7},{4,12},{5,13},{6,14},{7,15},{8,0},{9,1},{1... | collective-permute-start | bytes 1179656 | tf_op jit(solution)/shard_map/ppermute | solution.py:349
  37.2 11.2 %collective-permute-start.7 = (bf16[8,64,384]{2,1,0:T(8,128)(2,1)S(1)}, bf16[8,64,384]{2,1,0:T(8,128)(2,1)S(1)}, u32[]{:S(2)}, u32[]{:S(2)}) collective-permute-start(bf16[8,64,384]{2,1,0:T(8,128)(2,1)S(1)} %collective-permute-done.4.refs_0_), channel_id=1, source_target_pairs={{0,1},{1,0},{2,3},{3,2},{4,5},{5,4},{6,7},{7,6},{8,9},{9,8},{10,11... | collective-permute-start | bytes 1179656 | tf_op jit(solution)/shard_map/ppermute | solution.py:352
  48.4 1.7 %collective-permute-start.13 = (bf16[8,64,384]{2,1,0:T(8,128)(2,1)S(1)}, bf16[8,64,384]{2,1,0:T(8,128)(2,1)S(1)}, u32[]{:S(2)}, u32[]{:S(2)}) collective-permute-start(bf16[8,64,384]{2,1,0:T(8,128)(2,1)S(1)} %collective-permute-done.9.refs_1_), channel_id=1, source_target_pairs={{0,1},{1,0},{2,3},{3,2},{4,5},{5,4},{6,7},{7,6},{8,9},{9,8},{10,11... | collective-permute-start | bytes 1179656 | tf_op jit(solution)/shard_map/ppermute | solution.py:352
  48.4 2.3 %collective-permute-start.12 = (bf16[8,64,384]{2,1,0:T(8,128)(2,1)S(1)}, bf16[8,64,384]{2,1,0:T(8,128)(2,1)S(1)}, u32[]{:S(2)}, u32[]{:S(2)}) collective-permute-start(bf16[8,64,384]{2,1,0:T(8,128)(2,1)S(1)} %collective-permute-done.8.refs_0_), channel_id=1, source_target_pairs={{0,1},{1,0},{2,3},{3,2},{4,5},{5,4},{6,7},{7,6},{8,9},{9,8},{10,11... | collective-permute-start | bytes 1179656 | tf_op jit(solution)/shard_map/ppermute | solution.py:352
  48.9 11.0 %collective-permute-start.11 = (bf16[8,64,384]{2,1,0:T(8,128)(2,1)S(1)}, bf16[8,64,384]{2,1,0:T(8,128)(2,1)S(1)}, u32[]{:S(2)}, u32[]{:S(2)}) collective-permute-start(bf16[8,64,384]{2,1,0:T(8,128)(2,1)S(1)} %collective-permute-done.8.refs_0_), channel_id=1, source_target_pairs={{0,2},{1,3},{2,0},{3,1},{4,6},{5,7},{6,4},{7,5},{8,10},{9,11},{10,... | collective-permute-start | bytes 1179656 | tf_op jit(solution)/shard_map/ppermute | solution.py:352
  60.0 14.7 %copy-start.10 = (s32[8]{0:T(128)S(1)}, s32[8]{0:T(128)}, u32[]{:S(2)}) copy-start(s32[8]{0:T(128)} %counts_ref.3) | copy-start | bytes 100
  60.0 1.7 %collective-permute-start.14 = (bf16[8,64,384]{2,1,0:T(8,128)(2,1)S(1)}, bf16[8,64,384]{2,1,0:T(8,128)(2,1)S(1)}, u32[]{:S(2)}, u32[]{:S(2)}) collective-permute-start(bf16[8,64,384]{2,1,0:T(8,128)(2,1)S(1)} %collective-permute-done.11.refs_0_), channel_id=1, source_target_pairs={{0,1},{1,0},{2,3},{3,2},{4,5},{5,4},{6,7},{7,6},{8,9},{9,8},{10,11... | collective-permute-start | bytes 1179656 | tf_op jit(solution)/shard_map/ppermute | solution.py:352
  64.5 3.1 %collective-permute-start.17 = (f32[2,8,128]{2,1,0:T(8,128)S(1)}, f32[2,8,128]{2,1,0:T(8,128)S(1)}, u32[]{:S(2)}, u32[]{:S(2)}) collective-permute-start(f32[2,8,128]{2,1,0:T(8,128)S(1)} %get-tuple-element.97), channel_id=1, source_target_pairs={{0,3},{1,2},{2,1},{3,0},{4,7},{5,6},{6,5},{7,4},{8,11},{9,10},{10,... | collective-permute-start | bytes 24584 | tf_op jit(solution)/shard_map/ppermute | solution.py:352
  64.6 3.7 %collective-permute-start.16 = (f32[2,8,128]{2,1,0:T(8,128)S(1)}, f32[2,8,128]{2,1,0:T(8,128)S(1)}, u32[]{:S(2)}, u32[]{:S(2)}) collective-permute-start(f32[2,8,128]{2,1,0:T(8,128)S(1)} %get-tuple-element.97), channel_id=1, source_target_pairs={{0,2},{1,3},{2,0},{3,1},{4,6},{5,7},{6,4},{7,5},{8,10},{9,11},{10,... | collective-permute-start | bytes 24584 | tf_op jit(solution)/shard_map/ppermute | solution.py:352
  66.4 1.9 %collective-permute-start.15 = (f32[2,8,128]{2,1,0:T(8,128)S(1)}, f32[2,8,128]{2,1,0:T(8,128)S(1)}, u32[]{:S(2)}, u32[]{:S(2)}) collective-permute-start(f32[2,8,128]{2,1,0:T(8,128)S(1)} %get-tuple-element.97), channel_id=1, source_target_pairs={{0,1},{1,0},{2,3},{3,2},{4,5},{5,4},{6,7},{7,6},{8,9},{9,8},{10,11... | collective-permute-start | bytes 24584 | tf_op jit(solution)/shard_map/ppermute | solution.py:352
  68.3 5.5 %collective-permute-start.20 = (f32[2,8,128]{2,1,0:T(8,128)S(1)}, f32[2,8,128]{2,1,0:T(8,128)S(1)}, u32[]{:S(2)}, u32[]{:S(2)}) collective-permute-start(f32[2,8,128]{2,1,0:T(8,128)S(1)} %add_add_fusion), channel_id=1, source_target_pairs={{0,12},{1,13},{2,14},{3,15},{4,8},{5,9},{6,10},{7,11},{8,4},{9,5},... | collective-permute-start | bytes 24584 | tf_op jit(solution)/shard_map/ppermute | solution.py:352
  70.1 4.5 %collective-permute-start.19 = (f32[2,8,128]{2,1,0:T(8,128)S(1)}, f32[2,8,128]{2,1,0:T(8,128)S(1)}, u32[]{:S(2)}, u32[]{:S(2)}) collective-permute-start(f32[2,8,128]{2,1,0:T(8,128)S(1)} %add_add_fusion), channel_id=1, source_target_pairs={{0,8},{1,9},{2,10},{3,11},{4,12},{5,13},{6,14},{7,15},{8,0},{9,1},... | collective-permute-start | bytes 24584 | tf_op jit(solution)/shard_map/ppermute | solution.py:352
  70.8 3.8 %collective-permute-start.18 = (f32[2,8,128]{2,1,0:T(8,128)S(1)}, f32[2,8,128]{2,1,0:T(8,128)S(1)}, u32[]{:S(2)}, u32[]{:S(2)}) collective-permute-start(f32[2,8,128]{2,1,0:T(8,128)S(1)} %add_add_fusion), channel_id=1, source_target_pairs={{0,4},{1,5},{2,6},{3,7},{4,0},{5,1},{6,2},{7,3},{8,12},{9,13},{10,... | collective-permute-start | bytes 24584 | tf_op jit(solution)/shard_map/ppermute | solution.py:352

commit v9 on v8

v9 whole, which is shorter than its diff:
```python
import functools

import jax
import jax.numpy as jnp
from jax import lax
from jax.experimental import pallas as pl
from jax.experimental.pallas import tpu as pltpu
from jax.sharding import PartitionSpec as P

BATCH = 4
UNROLL = 4


def ring_of(depth):
    return [0, *range(1, depth, 2), *range(depth - 2 + depth % 2, 0, -2)]


def ring_place(z, depth):
    return jnp.where(z % 2 == 1, (z + 1) // 2, (depth - z // 2) % depth)


def ring_position(place, depth):
    return jnp.where(place <= depth // 2, jnp.maximum(2 * place - 1, 0), 2 * (depth - place))


def prepare_kernel(
    depth, shard_tiles,
    me_ref, counts_ref, irrep_ref,
    res_ref, gathered_ref, stats_ref, order_ref, offset_ref, stop_ref, end_ref, item_ref,
    blank_ref, next_ref, call_ref, blank_sem,
):
    own_tiles = irrep_ref.shape[0]
    irreps = counts_ref.shape[0]
    most = item_ref.shape[0] // depth
    blank_ref[...] = jnp.zeros(blank_ref.shape, blank_ref.dtype)
    group = blank_ref.shape[0]
    for l in range(0, own_tiles, group):
        pltpu.make_async_copy(blank_ref, res_ref.at[pl.ds(l, group)], blank_sem).start()

    for s in range(irreps):
        stop_ref[s] = 0
    for t in range(BATCH):
        order_ref[own_tiles + t] = 0

    def count(l, carry):
        s = irrep_ref[l]
        stop_ref[s] = stop_ref[s] + 1
        return carry

    lax.fori_loop(0, own_tiles, count, 0)
    first, offset = jnp.int32(0), jnp.int32(0)
    for s in range(irreps):
        next_ref[s] = first
        first = first + stop_ref[s]
        stop_ref[s] = first
        offset_ref[s] = offset
        offset = offset + counts_ref[s]

    def place(l, carry):
        s = irrep_ref[l]
        slot = next_ref[s]
        next_ref[s] = slot + 1
        order_ref[slot] = l
        return carry

    lax.fori_loop(0, own_tiles, place, 0)

    me = me_ref[0]
    z, y, core = me // 4, me // 2 % 2, me % 2
    for shard in range(4 * depth):
        lag = lax.rem(ring_place(z, depth) - ring_place(jnp.int32(shard // 4), depth) + depth, depth)
        same_core = core == shard % 2
        own_y = jnp.where(same_core, jnp.maximum(lag - 1, 0), jnp.minimum(lag, depth - 2))
        other_y = jnp.where(
            same_core | (lag == depth - 1), lag, jnp.minimum(lag + 1, depth - 2)
        )
        call_ref[shard] = jnp.where(y == shard // 2 % 2, own_y, other_y)

    for call in range(depth):
        end_ref[call] = call * most

    def symmetry(s, first):
        tiles, offset, stop = counts_ref[s], offset_ref[s], stop_ref[s]

        def block(j, carry):
            low = offset + j * BATCH
            high = offset + jnp.minimum(tiles, j * BATCH + BATCH) - 1
            call = jnp.maximum(call_ref[low // shard_tiles], call_ref[high // shard_tiles])
            word = (j * 256 + s) * 256 + first

            def batch(i, n):
                item_ref[n] = word + i * BATCH
                return n + 1

            end_ref[call] = lax.fori_loop(
                0, (stop - first + BATCH - 1) // BATCH, batch, end_ref[call]
            )
            return carry

        lax.fori_loop(0, (tiles + BATCH - 1) // BATCH, block, 0)
        return stop

    lax.fori_loop(0, irreps, symmetry, jnp.int32(0))
    for call in range(depth):
        end = end_ref[call]
        for spare in range(UNROLL - 1):
            item_ref[end + spare] = own_tiles

    spare = jnp.zeros((BATCH, *gathered_ref.shape[1:]), gathered_ref.dtype)
    gathered_ref[pl.ds(gathered_ref.shape[0] - BATCH, BATCH)] = spare
    shape = stats_ref.shape[1:]
    at_row = lax.broadcasted_iota(jnp.int32, shape, 0)
    at_lane = lax.broadcasted_iota(jnp.int32, shape, 1)
    sizes = jnp.zeros(shape, jnp.int32)
    first = jnp.int32(0)
    for s in range(irreps):
        sizes = jnp.where((at_row == s) & (at_lane == 0), stop_ref[s] - first, sizes)
        first = stop_ref[s]
    stats_ref[0] = jnp.zeros(shape, jnp.float32)
    stats_ref[1] = sizes.astype(jnp.float32)
    pltpu.make_async_copy(res_ref, res_ref, blank_sem).wait()


def prepare(me, counts, irrep, depth, shard_tiles, rows, width):
    own_tiles = irrep.shape[0]
    irreps = counts.shape[0]
    columns = shard_tiles * depth * rows
    all_tiles = 4 * shard_tiles * depth
    most = (all_tiles // BATCH + irreps) * (own_tiles // BATCH) + UNROLL
    smem = pl.BlockSpec(memory_space=pltpu.SMEM)
    vmem = pl.BlockSpec(memory_space=pltpu.VMEM)
    anywhere = pl.BlockSpec(memory_space=pl.ANY)
    return pl.pallas_call(
        functools.partial(prepare_kernel, depth, shard_tiles),
        out_shape=(
            jax.ShapeDtypeStruct((own_tiles, rows, columns), jnp.bfloat16),
            jax.ShapeDtypeStruct((all_tiles + BATCH, rows, width), jnp.bfloat16),
            jax.ShapeDtypeStruct((2, irreps, 128), jnp.float32),
            jax.ShapeDtypeStruct((own_tiles + BATCH,), jnp.int32),
            jax.ShapeDtypeStruct((irreps,), jnp.int32),
            jax.ShapeDtypeStruct((irreps,), jnp.int32),
            jax.ShapeDtypeStruct((depth,), jnp.int32),
            jax.ShapeDtypeStruct((depth * most,), jnp.int32),
        ),
        in_specs=[smem] * 3,
        out_specs=(anywhere, vmem, vmem, smem, smem, smem, smem, smem),
        scratch_shapes=[
            pltpu.VMEM((2, rows, columns), jnp.bfloat16),
            pltpu.SMEM((irreps,), jnp.int32),
            pltpu.SMEM((4 * depth,), jnp.int32),
            pltpu.SemaphoreType.DMA,
        ],
        compiler_params=pltpu.CompilerParams(
            vmem_limit_bytes=4 * all_tiles * rows * width + 4 * 1024 * 1024
        ),
        cost_estimate=pl.CostEstimate(
            flops=0, bytes_accessed=2 * own_tiles * rows * columns, transcendentals=0
        ),
        name="prepare",
    )(me, counts, irrep)


def ladder_kernel(
    call, depth, shard_tiles, layout,
    me_ref, counts_ref, order_ref, offset_ref, stop_ref, end_ref, item_ref,
    stats_in_ref, v_ref, res_in_ref, gathered_in_ref, *refs,
):
    del res_in_ref, gathered_in_ref
    fresh, refs = refs[:len(layout)], refs[len(layout):]
    res_hbm, gathered_ref, stats_ref, o_buf, acc_ref, a_sem, o_sem = refs
    rows, width = v_ref.shape[1:]
    side = BATCH * rows
    most = item_ref.shape[0] // depth

    me = me_ref[0]
    z, y, core = me // 4, me // 2 % 2, me % 2
    arrivals = []
    for source, (lag, other_y, other_core) in zip(fresh, layout):
        at = ring_position(lax.rem(ring_place(z, depth) - lag + depth, depth), depth)
        own_y = (1 - y) if other_y else y
        own_core = (1 - core) if other_core else core
        arrivals.append(pltpu.make_async_copy(
            source,
            gathered_ref.at[
                pl.ds(((at * 2 + own_y) * 2 + own_core) * shard_tiles, shard_tiles)
            ],
            a_sem.at[len(arrivals)],
        ))
    for arrival in arrivals:
        arrival.start()
    acc_ref[...] = jnp.zeros(acc_ref.shape, acc_ref.dtype)
    for arrival in arrivals:
        arrival.wait()

    col_at = lax.broadcasted_iota(jnp.int32, (1, side), 1)

    def item(n):
        word = item_ref[n]
        slot, group, block = word & 255, (word >> 8) & 255, word >> 16
        return slot, group, block, jnp.minimum(stop_ref[group] - slot, BATCH)

    def product(n):
        slot, group, block, members = item(n)
        left = jnp.concatenate([v_ref[order_ref[slot + t]] for t in range(BATCH)])
        right = gathered_ref[pl.ds(offset_ref[group] + block * BATCH, BATCH)].reshape(side, width)
        values = lax.dot_general(
            left, right, (((1,), (1,)), ((), ())), preferred_element_type=jnp.float32
        )
        limit = (counts_ref[group] - block * BATCH) * rows
        values = jnp.where(col_at < limit, values, 0.0).reshape(BATCH, rows, side)
        columns = pl.ds(pl.multiple_of(block * side, side), side)
        o_buf[pl.ds(slot, BATCH), :, columns] = values.astype(jnp.bfloat16)
        squares = jnp.sum((values * values).reshape(BATCH, rows // 8, 8, side), axis=1)
        total = jnp.zeros((8, side), jnp.float32)
        for t in range(BATCH):
            total = total + jnp.where(t < members, squares[t], 0.0)
        acc_ref[group] += total

    def send(n, started):
        slot, _, block, members = item(n)
        members = jnp.maximum(members, 0)
        columns = pl.ds(pl.multiple_of(block * side, side), side)

        def one(t, carry):
            pltpu.make_async_copy(
                o_buf.at[slot + t, :, columns],
                res_hbm.at[order_ref[slot + t], :, columns],
                o_sem,
            ).start()
            return carry

        lax.fori_loop(0, members, one, 0)
        return started + members

    def several(u, started):
        for n in range(UNROLL):
            product(call * most + u * UNROLL + n)
        for n in range(UNROLL):
            started = send(call * most + u * UNROLL + n, started)
        return started

    items = end_ref[call] - call * most
    started = lax.fori_loop(0, (items + UNROLL - 1) // UNROLL, several, jnp.int32(0))
    sums = jnp.sum(acc_ref[...], axis=1)
    sums = sum(sums[:, k:k + 128] for k in range(0, side, 128))
    stats_ref[0] = stats_in_ref[0] + sums
    stats_ref[1] = stats_in_ref[1]

    def finish(n, carry):
        pltpu.make_async_copy(
            o_buf.at[0, :, pl.ds(0, side)], res_hbm.at[0, :, pl.ds(0, side)], o_sem
        ).wait()
        return carry

    lax.fori_loop(0, started, finish, 0)


def ladder(call, depth, shard_tiles, integrals, listing, state, arrived):
    residual, gathered, stats = state
    layout, fresh = tuple(arrived), tuple(arrived.values())
    own_tiles, rows, width = integrals.shape
    slots = own_tiles + BATCH
    irreps = stats.shape[1]
    smem = pl.BlockSpec(memory_space=pltpu.SMEM)
    vmem = pl.BlockSpec(memory_space=pltpu.VMEM)
    anywhere = pl.BlockSpec(memory_space=pl.ANY)
    out_bytes = 2 * slots * residual[0].size
    tiles = sum(source.shape[0] for source in fresh)
    return pl.pallas_call(
        functools.partial(ladder_kernel, call, depth, shard_tiles, layout),
        out_shape=(
            jax.ShapeDtypeStruct(residual.shape, residual.dtype),
            jax.ShapeDtypeStruct(gathered.shape, gathered.dtype),
            jax.ShapeDtypeStruct(stats.shape, stats.dtype),
        ),
        in_specs=[smem] * 7 + [vmem] * 2 + [anywhere, vmem] + [anywhere] * len(fresh),
        out_specs=(anywhere, vmem, vmem),
        scratch_shapes=[
            pltpu.VMEM((slots, rows, residual.shape[2]), jnp.bfloat16),
            pltpu.VMEM((irreps, 8, BATCH * rows), jnp.float32),
            pltpu.SemaphoreType.DMA((len(fresh),)),
            pltpu.SemaphoreType.DMA,
        ],
        input_output_aliases={9: 0, 10: 1},
        compiler_params=pltpu.CompilerParams(
            vmem_limit_bytes=out_bytes + 2 * integrals.size + 4 * gathered.size + 6 * 1024 * 1024
        ),
        cost_estimate=pl.CostEstimate(
            flops=residual.size * width * tiles // (4 * shard_tiles * depth),
            bytes_accessed=2 * residual.size * tiles // (4 * shard_tiles * depth),
            transcendentals=0,
        ),
        name=f"ladder_{call}",
    )(*listing, stats, integrals, residual, gathered, *fresh)


def per_device(amplitudes, ij_counts, integrals, ab_irrep):
    shard_tiles, rows, width = amplitudes.shape
    devices = lax.axis_size("vir")
    depth = devices // 4
    me = lax.axis_index("vir").astype(jnp.int32).reshape(1)
    ring = ring_of(depth)
    hop = []
    for d in range(devices):
        following = ring[(ring.index(d // 4) + 1) % depth]
        hop.append((d, following * 4 + d % 4))

    def shift_z(x):
        return lax.ppermute(x, "vir", hop)

    def swap(x, bits):
        return lax.ppermute(x, "vir", [(d, d ^ bits) for d in range(devices)])

    residual, gathered, stats, *listing = prepare(
        me, ij_counts, ab_irrep, depth, shard_tiles, rows, width
    )
    listing = (me, ij_counts, *listing)
    state = (residual, gathered, stats)

    a, b, c, d = [amplitudes], [], [], []
    for k in range(depth):
        if k:
            c[-1], a[k], b[-1], d[-1:], state = lax.optimization_barrier(
                (c[-1], a[k], b[-1], d[-1:], state)
            )
        b.append(swap(a[k], 2))
        if k < depth - 1:
            a.append(shift_z(a[k]))
        c.append(swap(a[k], 1))
        if k == 0:
            continue
        d.append(swap(b[k - 1], 1))
        arrived = {(k, 0, 0): a[k], (k - 1, 1, 0): b[k - 1], (k - 1, 0, 1): c[k - 1]}
        if k == 1:
            arrived[0, 0, 0] = a[0]
        else:
            arrived[k - 2, 1, 1] = d[k - 2]
        if k == depth - 1:
            arrived[k, 0, 1], arrived[k - 1, 1, 1] = c[k], d[k - 1]
        state = ladder(k - 1, depth, shard_tiles, integrals, listing, state, arrived)
    last, state = lax.optimization_barrier((b[-1], state))
    residual, _, stats = ladder(
        depth - 1, depth, shard_tiles, integrals, listing, state,
        {(depth - 1, 1, 0): last, (depth - 1, 1, 1): swap(last, 1)},
    )

    stats = sum([swap(stats, bits) for bits in (1, 2, 3)], stats)
    stats = sum([swap(stats, 4 * bits) for bits in range(1, depth)], stats)
    irrep_sums, ab_counts = jnp.sum(stats, axis=2)
    entries = ab_counts * ij_counts.astype(jnp.float32) * float(rows * rows)
    return residual, jnp.sqrt(irrep_sums / entries + 1e-06)


def solution(mesh):
    in_specs = (
        P(("groups", "vir"), None, None),
        P("groups"),
        P(("groups", "vir"), None, None),
        P(("groups", "vir")),
    )
    out_specs = (P(("groups", "vir"), None, None), P("groups"))
    return jax.shard_map(
        per_device, mesh=mesh, in_specs=in_specs, out_specs=out_specs, check_vma=False
    )
```

time: 75.7 us -> 71.3 us (0.942)
  local copies, waits for them, and re-layouts: 13.4 us -> 4.37 us
  waiting for transfers between devices: 16.2 us -> 25 us
  Pallas kernels: 25.5 us -> 21.3 us
    unnamed x28 -> x12, local copies, waits for them, and re-layouts: 13.4 us -> 4.37 us
    ppermute x18, waiting for transfers between devices: 13.8 us -> 18.8 us  [swap(): return lax.ppermute(x, 'vir', [(d, d ^ bits) for d in range(devices)])]
    ppermute x3, waiting for transfers between devices: 2.38 us -> 6.19 us  [shift_z(): return lax.ppermute(x, 'vir', hop)]
    pallas_call x2 -> x1, Pallas kernels: 8.33 us -> 4.57 us  [prepare(): pl.pallas_call(functools.partial(prepare_kernel, depth, shard_tiles), out...]
    ppermute x3, starting transfers between devices: 6.52 us -> 7.36 us  [shift_z(): return lax.ppermute(x, 'vir', hop)]
  transfers between devices with their start and end apart: 21 -> 21, of which waited for: 10 -> 13; matrix products, arithmetic and copies ran while one was open for 0% -> 0% of each run, Pallas kernels for 30% -> 26%
where the time goes in v9:
time: 71.3 us; the launch traced here: 71.4 us
  waiting for transfers between devices  25 us (35%)
  Pallas kernels  21.3 us (30%)
  starting transfers between devices  19.3 us (27%)
  local copies, waits for them, and re-layouts  4.37 us (6%)
    ppermute x18, waiting for transfers between devices, swap(): return lax.ppermute(x, 'vir', [(d, d ^ bits) for d in range(devices)])  18.8 us
    pallas_call x4, Pallas kernels, ladder(): pl.pallas_call(functools.partial(ladder_kernel, call, depth, shard_tiles,...  16.7 us
    ppermute x18, starting transfers between devices, swap(): return lax.ppermute(x, 'vir', [(d, d ^ bits) for d in range(devices)])  12 us
    ppermute x3, starting transfers between devices, shift_z(): return lax.ppermute(x, 'vir', hop)  7.36 us
    ppermute x3, waiting for transfers between devices, shift_z(): return lax.ppermute(x, 'vir', hop)  6.19 us
    pallas_call x1, Pallas kernels, prepare(): pl.pallas_call(functools.partial(prepare_kernel, depth, shard_tiles), out...  4.57 us
    unnamed x12, local copies, waits for them, and re-layouts  4.37 us
  transfers between devices with their start and end apart: 21, of which 13 were waited for; matrix products, arithmetic and copies ran while one was open for 0% of the time, Pallas kernels for 26%

profile of v9, /device:TPU:0, one launch (start us, length us, event | category | flops | bytes accessed | tf_op | source)
XLA Modules:
  0.0 71.4 jit_solution(8391572835632933008)
XLA Ops:
  0.6 3.1 %collective-permute-start.1 = (bf16[8,64,384]{2,1,0:T(8,128)(2,1)}, bf16[8,64,384]{2,1,0:T(8,128)(2,1)S(1)}, u32[]{:S(2)}, u32[]{:S(2)}) collective-permute-start(bf16[8,64,384]{2,1,0:T(8,128)(2,1)} %refs_3_.1), channel_id=1, source_target_pairs={{0,4},{1,5},{2,6},{3,7},{4,12},{5,13},{6,14},{7,15},{8,0},{9,1},{1... | collective-permute-start | bytes 1179656 | tf_op jit(solution)/shard_map/ppermute | solution.py:309
  3.7 0.0 collective-permute-start
  3.7 1.5 %collective-permute-start.2 = (bf16[8,64,384]{2,1,0:T(8,128)(2,1)}, bf16[8,64,384]{2,1,0:T(8,128)(2,1)S(1)}, u32[]{:S(2)}, u32[]{:S(2)}) collective-permute-start(bf16[8,64,384]{2,1,0:T(8,128)(2,1)} %refs_3_.1), channel_id=1, source_target_pairs={{0,2},{1,3},{2,0},{3,1},{4,6},{5,7},{6,4},{7,5},{8,10},{9,11},{10,... | collective-permute-start | bytes 1179656 | tf_op jit(solution)/shard_map/ppermute | solution.py:312
  5.2 0.7 copy-done.3
  5.9 0.7 copy-done.5
  6.5 4.6 %prepare.1 = (bf16[32,64,2048]{2,1,0:T(8,128)(2,1)}, bf16[132,64,384]{2,1,0:T(8,128)(2,1)S(1)}, f32[2,8,128]{2,1,0:T(8,128)S(1)}, s32[36]{0:T(128)S(1)}, s32[8]{...) custom-call(s32[1]{0:T(128)} %bitcast.me_ref, s32[8]{0:T(128)S(1)} %copy-done.3, s32[32]{0:T(128)S(1)} %copy-done.5), custom_call_target="tpu_custom_call" | custom-call | bytes 8388608 | tf_op jit(solution)/shard_map/prepare/pallas_call | solution.py:133
  11.1 2.9 %collective-permute-done.1.refs_0_ = bf16[8,64,384]{2,1,0:T(8,128)(2,1)S(1)} collective-permute-done((bf16[8,64,384]{2,1,0:T(8,128)(2,1)}, bf16[8,64,384]{2,1,0:T(8,128)(2,1)S(1)}, u32[]{:S(2)}, u32[]{:S(2)}) %collective-permute-start.1) | collective-permute-done | bytes 393248 | tf_op jit(solution)/shard_map/ppermute | solution.py:309
  14.0 0.0 collective-permute-done.refs_2_
  14.0 1.4 %collective-permute-done.2.refs_1_ = bf16[8,64,384]{2,1,0:T(8,128)(2,1)S(1)} collective-permute-done((bf16[8,64,384]{2,1,0:T(8,128)(2,1)}, bf16[8,64,384]{2,1,0:T(8,128)(2,1)S(1)}, u32[]{:S(2)}, u32[]{:S(2)}) %collective-permute-start.2) | collective-permute-done | bytes 393248 | tf_op jit(solution)/shard_map/ppermute | solution.py:312
  15.4 0.0 collective-permute-start.6
  15.5 1.5 %collective-permute-start.5 = (bf16[8,64,384]{2,1,0:T(8,128)(2,1)S(1)}, bf16[8,64,384]{2,1,0:T(8,128)(2,1)S(1)}, u32[]{:S(2)}, u32[]{:S(2)}) collective-permute-start(bf16[8,64,384]{2,1,0:T(8,128)(2,1)S(1)} %collective-permute-done.1.refs_0_), channel_id=1, source_target_pairs={{0,2},{1,3},{2,0},{3,1},{4,6},{5,7},{6,4},{7,5},{8,10},{9,11},{10,... | collective-permute-start | bytes 1179656 | tf_op jit(solution)/shard_map/ppermute | solution.py:312
  17.0 2.6 %collective-permute-start.4 = (bf16[8,64,384]{2,1,0:T(8,128)(2,1)S(1)}, bf16[8,64,384]{2,1,0:T(8,128)(2,1)S(1)}, u32[]{:S(2)}, u32[]{:S(2)}) collective-permute-start(bf16[8,64,384]{2,1,0:T(8,128)(2,1)S(1)} %collective-permute-done.1.refs_0_), channel_id=1, source_target_pairs={{0,4},{1,5},{2,6},{3,7},{4,12},{5,13},{6,14},{7,15},{8,0},{9,1},{1... | collective-permute-start | bytes 1179656 | tf_op jit(solution)/shard_map/ppermute | solution.py:309
  19.6 1.4 %copy-done = bf16[32,64,384]{2,1,0:T(8,128)(2,1)S(1)} copy-done((bf16[32,64,384]{2,1,0:T(8,128)(2,1)S(1)}, bf16[32,64,384]{2,1,0:T(8,128)(2,1)}, u32[]{:S(2)}) %copy-start) | copy-done | bytes 1572888
  21.0 1.0 %copy-done.2 = bf16[8,64,384]{2,1,0:T(8,128)(2,1)S(1)} copy-done((bf16[8,64,384]{2,1,0:T(8,128)(2,1)S(1)}, bf16[8,64,384]{2,1,0:T(8,128)(2,1)}, u32[]{:S(2)}) %copy-start.2) | copy-done | bytes 393240
  22.0 0.7 copy-done.4
  22.6 3.4 %ladder_0.1 = (bf16[32,64,2048]{2,1,0:T(8,128)(2,1)}, bf16[132,64,384]{2,1,0:T(8,128)(2,1)S(1)}, f32[2,8,128]{2,1,0:T(8,128)S(1)}) custom-call(s32[1]{0:T(128)} %bitcast.me_ref, s32[8]{0:T(128)S(1)} %copy-done.4, s32[36]{0:T(128)S(1)} %get-tuple-element.45.order_ref, ...), custom_call_target="tpu_custom_call", output_to_operand_aliasing={{0}: (9, {}), {1}: (10, {})} | custom-call | flops 402653184 | bytes 2097152 | tf_op jit(solution)/shard_map/ladder_0/pallas_call | solution.py:269
  26.0 0.0 collective-permute-done.6.refs_3_
  26.0 0.9 %collective-permute-done.5.refs_1_ = bf16[8,64,384]{2,1,0:T(8,128)(2,1)S(1)} collective-permute-done((bf16[8,64,384]{2,1,0:T(8,128)(2,1)S(1)}, bf16[8,64,384]{2,1,0:T(8,128)(2,1)S(1)}, u32[]{:S(2)}, u32[]{:S(2)}) %collective-permute-start.5) | collective-permute-done | bytes 393248 | tf_op jit(solution)/shard_map/ppermute | solution.py:312
  27.0 2.1 %collective-permute-done.4.refs_0_ = bf16[8,64,384]{2,1,0:T(8,128)(2,1)S(1)} collective-permute-done((bf16[8,64,384]{2,1,0:T(8,128)(2,1)S(1)}, bf16[8,64,384]{2,1,0:T(8,128)(2,1)S(1)}, u32[]{:S(2)}, u32[]{:S(2)}) %collective-permute-start.4) | collective-permute-done | bytes 393248 | tf_op jit(solution)/shard_map/ppermute | solution.py:309
  29.1 0.5 collective-permute-start.9
  29.6 1.7 %collective-permute-start.8 = (bf16[8,64,384]{2,1,0:T(8,128)(2,1)S(1)}, bf16[8,64,384]{2,1,0:T(8,128)(2,1)S(1)}, u32[]{:S(2)}, u32[]{:S(2)}) collective-permute-start(bf16[8,64,384]{2,1,0:T(8,128)(2,1)S(1)} %collective-permute-done.4.refs_0_), channel_id=1, source_target_pairs={{0,4},{1,5},{2,6},{3,7},{4,12},{5,13},{6,14},{7,15},{8,0},{9,1},{1... | collective-permute-start | bytes 1179656 | tf_op jit(solution)/shard_map/ppermute | solution.py:309
  31.3 0.0 collective-permute-start.7
  31.3 4.0 %ladder_1.1 = (bf16[32,64,2048]{2,1,0:T(8,128)(2,1)}, bf16[132,64,384]{2,1,0:T(8,128)(2,1)S(1)}, f32[2,8,128]{2,1,0:T(8,128)S(1)}) custom-call(s32[1]{0:T(128)} %bitcast.me_ref, s32[8]{0:T(128)S(1)} %copy-done.4, s32[36]{0:T(128)S(1)} %get-tuple-element.45.order_ref, ...), custom_call_target="tpu_custom_call", output_to_operand_aliasing={{0}: (9, {}), {1}: (10, {})} | custom-call | flops 402653184 | bytes 2097152 | tf_op jit(solution)/shard_map/ladder_1/pallas_call | solution.py:269
  35.3 0.0 collective-permute-done.10.refs_3_
  35.3 5.3 %collective-permute-done.9.refs_1_ = bf16[8,64,384]{2,1,0:T(8,128)(2,1)S(1)} collective-permute-done((bf16[8,64,384]{2,1,0:T(8,128)(2,1)S(1)}, bf16[8,64,384]{2,1,0:T(8,128)(2,1)S(1)}, u32[]{:S(2)}, u32[]{:S(2)}) %collective-permute-start.9) | collective-permute-done | bytes 393248 | tf_op jit(solution)/shard_map/ppermute | solution.py:312
  40.7 1.1 %collective-permute-done.8.refs_0_ = bf16[8,64,384]{2,1,0:T(8,128)(2,1)S(1)} collective-permute-done((bf16[8,64,384]{2,1,0:T(8,128)(2,1)S(1)}, bf16[8,64,384]{2,1,0:T(8,128)(2,1)S(1)}, u32[]{:S(2)}, u32[]{:S(2)}) %collective-permute-start.8) | collective-permute-done | bytes 393248 | tf_op jit(solution)/shard_map/ppermute | solution.py:309
  41.8 0.0 collective-permute-done.7.refs_2_
  41.8 0.0 collective-permute-start.13
  41.8 0.5 collective-permute-start.12
  42.3 1.5 %collective-permute-start.11 = (bf16[8,64,384]{2,1,0:T(8,128)(2,1)S(1)}, bf16[8,64,384]{2,1,0:T(8,128)(2,1)S(1)}, u32[]{:S(2)}, u32[]{:S(2)}) collective-permute-start(bf16[8,64,384]{2,1,0:T(8,128)(2,1)S(1)} %collective-permute-done.8.refs_0_), channel_id=1, source_target_pairs={{0,2},{1,3},{2,0},{3,1},{4,6},{5,7},{6,4},{7,5},{8,10},{9,11},{10,... | collective-permute-start | bytes 1179656 | tf_op jit(solution)/shard_map/ppermute | solution.py:312
  43.8 0.3 collective-permute-done.12.refs_4_
  44.1 6.5 %ladder_2.1 = (bf16[32,64,2048]{2,1,0:T(8,128)(2,1)}, bf16[132,64,384]{2,1,0:T(8,128)(2,1)S(1)}, f32[2,8,128]{2,1,0:T(8,128)S(1)}) custom-call(s32[1]{0:T(128)} %bitcast.me_ref, s32[8]{0:T(128)S(1)} %copy-done.4, s32[36]{0:T(128)S(1)} %get-tuple-element.45.order_ref, ...), custom_call_target="tpu_custom_call", output_to_operand_aliasing={{0}: (9, {}), {1}: (10, {})} | custom-call | flops 603979776 | bytes 3145728 | tf_op jit(solution)/shard_map/ladder_2/pallas_call | solution.py:269
  50.5 2.8 %collective-permute-done.11.refs_0_ = bf16[8,64,384]{2,1,0:T(8,128)(2,1)S(1)} collective-permute-done((bf16[8,64,384]{2,1,0:T(8,128)(2,1)S(1)}, bf16[8,64,384]{2,1,0:T(8,128)(2,1)S(1)}, u32[]{:S(2)}, u32[]{:S(2)}) %collective-permute-start.11) | collective-permute-done | bytes 393248 | tf_op jit(solution)/shard_map/ppermute | solution.py:312
  53.3 1.7 %collective-permute-done.14.refs_1_ = bf16[8,64,384]{2,1,0:T(8,128)(2,1)S(1)} collective-permute-done((bf16[8,64,384]{2,1,0:T(8,128)(2,1)S(1)}, bf16[8,64,384]{2,1,0:T(8,128)(2,1)S(1)}, u32[]{:S(2)}, u32[]{:S(2)}) %collective-permute-start.14) | collective-permute-done | bytes 393248 | tf_op jit(solution)/shard_map/ppermute | solution.py:312
  55.0 2.9 %ladder_3.1 = (bf16[32,64,2048]{2,1,0:T(8,128)(2,1)}, bf16[132,64,384]{2,1,0:T(8,128)(2,1)S(1)}, f32[2,8,128]{2,1,0:T(8,128)S(1)}) custom-call(s32[1]{0:T(128)} %bitcast.me_ref, s32[8]{0:T(128)S(1)} %copy-done.4, s32[36]{0:T(128)S(1)} %get-tuple-element.45.order_ref, ...), custom_call_target="tpu_custom_call", output_to_operand_aliasing={{0}: (9, {}), {1}: (10, {})} | custom-call | flops 201326592 | bytes 1048576 | tf_op jit(solution)/shard_map/ladder_3/pallas_call | solution.py:269
  58.0 0.7 collective-permute-start.17
  58.7 1.1 %collective-permute-start.16 = (f32[2,8,128]{2,1,0:T(8,128)S(1)}, f32[2,8,128]{2,1,0:T(8,128)S(1)}, u32[]{:S(2)}, u32[]{:S(2)}) collective-permute-start(f32[2,8,128]{2,1,0:T(8,128)S(1)} %get-tuple-element.87), channel_id=1, source_target_pairs={{0,2},{1,3},{2,0},{3,1},{4,6},{5,7},{6,4},{7,5},{8,10},{9,11},{10,... | collective-permute-start | bytes 24584 | tf_op jit(solution)/shard_map/ppermute | solution.py:312
  59.8 0.2 collective-permute-start.15
  59.9 1.2 %collective-permute-done.17 = f32[2,8,128]{2,1,0:T(8,128)S(1)} collective-permute-done((f32[2,8,128]{2,1,0:T(8,128)S(1)}, f32[2,8,128]{2,1,0:T(8,128)S(1)}, u32[]{:S(2)}, u32[]{:S(2)}) %collective-permute-start.17) | collective-permute-done | bytes 8224 | tf_op jit(solution)/shard_map/ppermute | solution.py:312
  61.1 1.2 %collective-permute-done.16 = f32[2,8,128]{2,1,0:T(8,128)S(1)} collective-permute-done((f32[2,8,128]{2,1,0:T(8,128)S(1)}, f32[2,8,128]{2,1,0:T(8,128)S(1)}, u32[]{:S(2)}, u32[]{:S(2)}) %collective-permute-start.16) | collective-permute-done | bytes 8224 | tf_op jit(solution)/shard_map/ppermute | solution.py:312
  62.4 0.0 collective-permute-done.15
  62.4 3.8 %collective-permute-start.20 = (f32[2,8,128]{2,1,0:T(8,128)S(1)}, f32[2,8,128]{2,1,0:T(8,128)S(1)}, u32[]{:S(2)}, u32[]{:S(2)}) collective-permute-start(f32[2,8,128]{2,1,0:T(8,128)S(1)} %add_add_fusion), channel_id=1, source_target_pairs={{0,12},{1,13},{2,14},{3,15},{4,8},{5,9},{6,10},{7,11},{8,4},{9,5},... | collective-permute-start | bytes 24584 | tf_op jit(solution)/shard_map/ppermute | solution.py:312
  66.2 0.6 collective-permute-start.18
  66.8 1.1 %collective-permute-done.20 = f32[2,8,128]{2,1,0:T(8,128)S(1)} collective-permute-done((f32[2,8,128]{2,1,0:T(8,128)S(1)}, f32[2,8,128]{2,1,0:T(8,128)S(1)}, u32[]{:S(2)}, u32[]{:S(2)}) %collective-permute-start.20) | collective-permute-done | bytes 8224 | tf_op jit(solution)/shard_map/ppermute | solution.py:312
  67.9 2.8 %collective-permute-done.19 = f32[2,8,128]{2,1,0:T(8,128)S(1)} collective-permute-done((f32[2,8,128]{2,1,0:T(8,128)S(1)}, f32[2,8,128]{2,1,0:T(8,128)S(1)}, u32[]{:S(2)}, u32[]{:S(2)}) %collective-permute-start.19) | collective-permute-done | bytes 8224 | tf_op jit(solution)/shard_map/ppermute | solution.py:312
  70.7 0.0 collective-permute-done.18
  70.7 0.1 add_reduce_fusion
  70.8 0.5 add_sqrt_fusion
  (14 shorter events, 0.0 us)
Async XLA Ops:
  0.6 13.4 %collective-permute-start.1 = (bf16[8,64,384]{2,1,0:T(8,128)(2,1)}, bf16[8,64,384]{2,1,0:T(8,128)(2,1)S(1)}, u32[]{:S(2)}, u32[]{:S(2)}) collective-permute-start(bf16[8,64,384]{2,1,0:T(8,128)(2,1)} %refs_3_.1), channel_id=1, source_target_pairs={{0,4},{1,5},{2,6},{3,7},{4,12},{5,13},{6,14},{7,15},{8,0},{9,1},{1... | collective-permute-start | bytes 1179656 | tf_op jit(solution)/shard_map/ppermute | solution.py:309
  3.7 10.3 %collective-permute-start = (bf16[8,64,384]{2,1,0:T(8,128)(2,1)}, bf16[8,64,384]{2,1,0:T(8,128)(2,1)S(1)}, u32[]{:S(2)}, u32[]{:S(2)}) collective-permute-start(bf16[8,64,384]{2,1,0:T(8,128)(2,1)} %refs_3_.1), channel_id=1, source_target_pairs={{0,1},{1,0},{2,3},{3,2},{4,5},{5,4},{6,7},{7,6},{8,9},{9,8},{10,11... | collective-permute-start | bytes 1179656 | tf_op jit(solution)/shard_map/ppermute | solution.py:312
  3.7 11.7 %collective-permute-start.2 = (bf16[8,64,384]{2,1,0:T(8,128)(2,1)}, bf16[8,64,384]{2,1,0:T(8,128)(2,1)S(1)}, u32[]{:S(2)}, u32[]{:S(2)}) collective-permute-start(bf16[8,64,384]{2,1,0:T(8,128)(2,1)} %refs_3_.1), channel_id=1, source_target_pairs={{0,2},{1,3},{2,0},{3,1},{4,6},{5,7},{6,4},{7,5},{8,10},{9,11},{10,... | collective-permute-start | bytes 1179656 | tf_op jit(solution)/shard_map/ppermute | solution.py:312
  5.2 0.7 copy-start.3
  5.9 0.7 copy-start.5
  15.4 10.6 %collective-permute-start.6 = (bf16[8,64,384]{2,1,0:T(8,128)(2,1)S(1)}, bf16[8,64,384]{2,1,0:T(8,128)(2,1)S(1)}, u32[]{:S(2)}, u32[]{:S(2)}) collective-permute-start(bf16[8,64,384]{2,1,0:T(8,128)(2,1)S(1)} %collective-permute-done.2.refs_1_), channel_id=1, source_target_pairs={{0,1},{1,0},{2,3},{3,2},{4,5},{5,4},{6,7},{7,6},{8,9},{9,8},{10,11... | collective-permute-start | bytes 1179656 | tf_op jit(solution)/shard_map/ppermute | solution.py:312
  15.5 11.5 %collective-permute-start.5 = (bf16[8,64,384]{2,1,0:T(8,128)(2,1)S(1)}, bf16[8,64,384]{2,1,0:T(8,128)(2,1)S(1)}, u32[]{:S(2)}, u32[]{:S(2)}) collective-permute-start(bf16[8,64,384]{2,1,0:T(8,128)(2,1)S(1)} %collective-permute-done.1.refs_0_), channel_id=1, source_target_pairs={{0,2},{1,3},{2,0},{3,1},{4,6},{5,7},{6,4},{7,5},{8,10},{9,11},{10,... | collective-permute-start | bytes 1179656 | tf_op jit(solution)/shard_map/ppermute | solution.py:312
  17.0 12.1 %collective-permute-start.4 = (bf16[8,64,384]{2,1,0:T(8,128)(2,1)S(1)}, bf16[8,64,384]{2,1,0:T(8,128)(2,1)S(1)}, u32[]{:S(2)}, u32[]{:S(2)}) collective-permute-start(bf16[8,64,384]{2,1,0:T(8,128)(2,1)S(1)} %collective-permute-done.1.refs_0_), channel_id=1, source_target_pairs={{0,4},{1,5},{2,6},{3,7},{4,12},{5,13},{6,14},{7,15},{8,0},{9,1},{1... | collective-permute-start | bytes 1179656 | tf_op jit(solution)/shard_map/ppermute | solution.py:309
  19.6 9.6 %collective-permute-start.3 = (bf16[8,64,384]{2,1,0:T(8,128)(2,1)S(1)}, bf16[8,64,384]{2,1,0:T(8,128)(2,1)S(1)}, u32[]{:S(2)}, u32[]{:S(2)}) collective-permute-start(bf16[8,64,384]{2,1,0:T(8,128)(2,1)S(1)} %collective-permute-done.1.refs_0_), channel_id=1, source_target_pairs={{0,1},{1,0},{2,3},{3,2},{4,5},{5,4},{6,7},{7,6},{8,9},{9,8},{10,11... | collective-permute-start | bytes 1179656 | tf_op jit(solution)/shard_map/ppermute | solution.py:312
  19.6 1.4 %copy-start = (bf16[32,64,384]{2,1,0:T(8,128)(2,1)S(1)}, bf16[32,64,384]{2,1,0:T(8,128)(2,1)}, u32[]{:S(2)}) copy-start(bf16[32,64,384]{2,1,0:T(8,128)(2,1)} %v_ref.7) | copy-start | bytes 4718596
  21.0 1.0 %copy-start.2 = (bf16[8,64,384]{2,1,0:T(8,128)(2,1)S(1)}, bf16[8,64,384]{2,1,0:T(8,128)(2,1)}, u32[]{:S(2)}) copy-start(bf16[8,64,384]{2,1,0:T(8,128)(2,1)} %refs_3_.1) | copy-start | bytes 1179652
  22.0 0.7 copy-start.4
  22.6 8.7 %copy-start.1 = (bf16[32,64,384]{2,1,0:T(8,128)(2,1)S(1)}, bf16[32,64,384]{2,1,0:T(8,128)(2,1)}, u32[]{:S(2)}) copy-start(bf16[32,64,384]{2,1,0:T(8,128)(2,1)} %v_ref.7) | copy-start | bytes 4718596
  29.1 6.2 %collective-permute-start.10 = (bf16[8,64,384]{2,1,0:T(8,128)(2,1)S(1)}, bf16[8,64,384]{2,1,0:T(8,128)(2,1)S(1)}, u32[]{:S(2)}, u32[]{:S(2)}) collective-permute-start(bf16[8,64,384]{2,1,0:T(8,128)(2,1)S(1)} %collective-permute-done.5.refs_1_), channel_id=1, source_target_pairs={{0,1},{1,0},{2,3},{3,2},{4,5},{5,4},{6,7},{7,6},{8,9},{9,8},{10,11... | collective-permute-start | bytes 1179656 | tf_op jit(solution)/shard_map/ppermute | solution.py:312
  29.1 11.5 %collective-permute-start.9 = (bf16[8,64,384]{2,1,0:T(8,128)(2,1)S(1)}, bf16[8,64,384]{2,1,0:T(8,128)(2,1)S(1)}, u32[]{:S(2)}, u32[]{:S(2)}) collective-permute-start(bf16[8,64,384]{2,1,0:T(8,128)(2,1)S(1)} %collective-permute-done.4.refs_0_), channel_id=1, source_target_pairs={{0,2},{1,3},{2,0},{3,1},{4,6},{5,7},{6,4},{7,5},{8,10},{9,11},{10,... | collective-permute-start | bytes 1179656 | tf_op jit(solution)/shard_map/ppermute | solution.py:312
  29.6 12.1 %collective-permute-start.8 = (bf16[8,64,384]{2,1,0:T(8,128)(2,1)S(1)}, bf16[8,64,384]{2,1,0:T(8,128)(2,1)S(1)}, u32[]{:S(2)}, u32[]{:S(2)}) collective-permute-start(bf16[8,64,384]{2,1,0:T(8,128)(2,1)S(1)} %collective-permute-done.4.refs_0_), channel_id=1, source_target_pairs={{0,4},{1,5},{2,6},{3,7},{4,12},{5,13},{6,14},{7,15},{8,0},{9,1},{1... | collective-permute-start | bytes 1179656 | tf_op jit(solution)/shard_map/ppermute | solution.py:309
  31.3 10.5 %collective-permute-start.7 = (bf16[8,64,384]{2,1,0:T(8,128)(2,1)S(1)}, bf16[8,64,384]{2,1,0:T(8,128)(2,1)S(1)}, u32[]{:S(2)}, u32[]{:S(2)}) collective-permute-start(bf16[8,64,384]{2,1,0:T(8,128)(2,1)S(1)} %collective-permute-done.4.refs_0_), channel_id=1, source_target_pairs={{0,1},{1,0},{2,3},{3,2},{4,5},{5,4},{6,7},{7,6},{8,9},{9,8},{10,11... | collective-permute-start | bytes 1179656 | tf_op jit(solution)/shard_map/ppermute | solution.py:312
  41.8 2.0 %collective-permute-start.13 = (bf16[8,64,384]{2,1,0:T(8,128)(2,1)S(1)}, bf16[8,64,384]{2,1,0:T(8,128)(2,1)S(1)}, u32[]{:S(2)}, u32[]{:S(2)}) collective-permute-start(bf16[8,64,384]{2,1,0:T(8,128)(2,1)S(1)} %collective-permute-done.9.refs_1_), channel_id=1, source_target_pairs={{0,1},{1,0},{2,3},{3,2},{4,5},{5,4},{6,7},{7,6},{8,9},{9,8},{10,11... | collective-permute-start | bytes 1179656 | tf_op jit(solution)/shard_map/ppermute | solution.py:312
  41.8 2.3 %collective-permute-start.12 = (bf16[8,64,384]{2,1,0:T(8,128)(2,1)S(1)}, bf16[8,64,384]{2,1,0:T(8,128)(2,1)S(1)}, u32[]{:S(2)}, u32[]{:S(2)}) collective-permute-start(bf16[8,64,384]{2,1,0:T(8,128)(2,1)S(1)} %collective-permute-done.8.refs_0_), channel_id=1, source_target_pairs={{0,1},{1,0},{2,3},{3,2},{4,5},{5,4},{6,7},{7,6},{8,9},{9,8},{10,11... | collective-permute-start | bytes 1179656 | tf_op jit(solution)/shard_map/ppermute | solution.py:312
  42.3 11.0 %collective-permute-start.11 = (bf16[8,64,384]{2,1,0:T(8,128)(2,1)S(1)}, bf16[8,64,384]{2,1,0:T(8,128)(2,1)S(1)}, u32[]{:S(2)}, u32[]{:S(2)}) collective-permute-start(bf16[8,64,384]{2,1,0:T(8,128)(2,1)S(1)} %collective-permute-done.8.refs_0_), channel_id=1, source_target_pairs={{0,2},{1,3},{2,0},{3,1},{4,6},{5,7},{6,4},{7,5},{8,10},{9,11},{10,... | collective-permute-start | bytes 1179656 | tf_op jit(solution)/shard_map/ppermute | solution.py:312
  53.3 1.7 %collective-permute-start.14 = (bf16[8,64,384]{2,1,0:T(8,128)(2,1)S(1)}, bf16[8,64,384]{2,1,0:T(8,128)(2,1)S(1)}, u32[]{:S(2)}, u32[]{:S(2)}) collective-permute-start(bf16[8,64,384]{2,1,0:T(8,128)(2,1)S(1)} %collective-permute-done.11.refs_0_), channel_id=1, source_target_pairs={{0,1},{1,0},{2,3},{3,2},{4,5},{5,4},{6,7},{7,6},{8,9},{9,8},{10,11... | collective-permute-start | bytes 1179656 | tf_op jit(solution)/shard_map/ppermute | solution.py:312
  58.0 3.1 %collective-permute-start.17 = (f32[2,8,128]{2,1,0:T(8,128)S(1)}, f32[2,8,128]{2,1,0:T(8,128)S(1)}, u32[]{:S(2)}, u32[]{:S(2)}) collective-permute-start(f32[2,8,128]{2,1,0:T(8,128)S(1)} %get-tuple-element.87), channel_id=1, source_target_pairs={{0,3},{1,2},{2,1},{3,0},{4,7},{5,6},{6,5},{7,4},{8,11},{9,10},{10,... | collective-permute-start | bytes 24584 | tf_op jit(solution)/shard_map/ppermute | solution.py:312
  58.7 3.7 %collective-permute-start.16 = (f32[2,8,128]{2,1,0:T(8,128)S(1)}, f32[2,8,128]{2,1,0:T(8,128)S(1)}, u32[]{:S(2)}, u32[]{:S(2)}) collective-permute-start(f32[2,8,128]{2,1,0:T(8,128)S(1)} %get-tuple-element.87), channel_id=1, source_target_pairs={{0,2},{1,3},{2,0},{3,1},{4,6},{5,7},{6,4},{7,5},{8,10},{9,11},{10,... | collective-permute-start | bytes 24584 | tf_op jit(solution)/shard_map/ppermute | solution.py:312
  59.8 2.6 %collective-permute-start.15 = (f32[2,8,128]{2,1,0:T(8,128)S(1)}, f32[2,8,128]{2,1,0:T(8,128)S(1)}, u32[]{:S(2)}, u32[]{:S(2)}) collective-permute-start(f32[2,8,128]{2,1,0:T(8,128)S(1)} %get-tuple-element.87), channel_id=1, source_target_pairs={{0,1},{1,0},{2,3},{3,2},{4,5},{5,4},{6,7},{7,6},{8,9},{9,8},{10,11... | collective-permute-start | bytes 24584 | tf_op jit(solution)/shard_map/ppermute | solution.py:312
  62.4 5.5 %collective-permute-start.20 = (f32[2,8,128]{2,1,0:T(8,128)S(1)}, f32[2,8,128]{2,1,0:T(8,128)S(1)}, u32[]{:S(2)}, u32[]{:S(2)}) collective-permute-start(f32[2,8,128]{2,1,0:T(8,128)S(1)} %add_add_fusion), channel_id=1, source_target_pairs={{0,12},{1,13},{2,14},{3,15},{4,8},{5,9},{6,10},{7,11},{8,4},{9,5},... | collective-permute-start | bytes 24584 | tf_op jit(solution)/shard_map/ppermute | solution.py:312
  66.2 4.5 %collective-permute-start.19 = (f32[2,8,128]{2,1,0:T(8,128)S(1)}, f32[2,8,128]{2,1,0:T(8,128)S(1)}, u32[]{:S(2)}, u32[]{:S(2)}) collective-permute-start(f32[2,8,128]{2,1,0:T(8,128)S(1)} %add_add_fusion), channel_id=1, source_target_pairs={{0,8},{1,9},{2,10},{3,11},{4,12},{5,13},{6,14},{7,15},{8,0},{9,1},... | collective-permute-start | bytes 24584 | tf_op jit(solution)/shard_map/ppermute | solution.py:312
  66.2 4.5 %collective-permute-start.18 = (f32[2,8,128]{2,1,0:T(8,128)S(1)}, f32[2,8,128]{2,1,0:T(8,128)S(1)}, u32[]{:S(2)}, u32[]{:S(2)}) collective-permute-start(f32[2,8,128]{2,1,0:T(8,128)S(1)} %add_add_fusion), channel_id=1, source_target_pairs={{0,4},{1,5},{2,6},{3,7},{4,0},{5,1},{6,2},{7,3},{8,12},{9,13},{10,... | collective-permute-start | bytes 24584 | tf_op jit(solution)/shard_map/ppermute | solution.py:312

commit v10 on v9

--- a/solution.py
+++ b/solution.py
@@ -199,13 +199,16 @@
         slot, group, block = word & 255, (word >> 8) & 255, word >> 16
         return slot, group, block, jnp.minimum(stop_ref[group] - slot, BATCH)
 
-    def product(n):
-        slot, group, block, members = item(n)
+    def multiply(n):
+        slot, group, block, _ = item(n)
         left = jnp.concatenate([v_ref[order_ref[slot + t]] for t in range(BATCH)])
         right = gathered_ref[pl.ds(offset_ref[group] + block * BATCH, BATCH)].reshape(side, width)
-        values = lax.dot_general(
+        return lax.dot_general(
             left, right, (((1,), (1,)), ((), ())), preferred_element_type=jnp.float32
         )
+
+    def keep(n, values):
+        slot, group, block, members = item(n)
         limit = (counts_ref[group] - block * BATCH) * rows
         values = jnp.where(col_at < limit, values, 0.0).reshape(BATCH, rows, side)
         columns = pl.ds(pl.multiple_of(block * side, side), side)
@@ -233,10 +236,15 @@
         return started + members
 
     def several(u, started):
+        first = call * most + u * UNROLL
+        values = multiply(first)
+        for n in range(1, UNROLL):
+            following = multiply(first + n)
+            keep(first + n - 1, values)
+            values = following
+        keep(first + UNROLL - 1, values)
         for n in range(UNROLL):
-            product(call * most + u * UNROLL + n)
-        for n in range(UNROLL):
-            started = send(call * most + u * UNROLL + n, started)
+            started = send(first + n, started)
         return started
 
     items = end_ref[call] - call * most
@@ -320,9 +328,12 @@
     a, b, c, d = [amplitudes], [], [], []
     for k in range(depth):
         if k:
-            c[-1], a[k], b[-1], d[-1:], state = lax.optimization_barrier(
-                (c[-1], a[k], b[-1], d[-1:], state)
-            )
+            if k == 1:
+                a[k], b[-1], c[-1], state = lax.optimization_barrier((a[k], b[-1], c[-1], state))
+            else:
+                c[-1], a[k], b[-1], d[-1], state = lax.optimization_barrier(
+                    (c[-1], a[k], b[-1], d[-1], state)
+                )
         b.append(swap(a[k], 2))
         if k < depth - 1:
             a.append(shift_z(a[k]))

time: 71.3 us -> 71.4 us (level)
  waiting for transfers between devices: 25 us -> 28.5 us
  starting transfers between devices: 19.3 us -> 16.3 us
    ppermute x3, starting transfers between devices: 7.36 us -> 3.25 us  [shift_z(): return lax.ppermute(x, 'vir', hop)]
    ppermute x18, waiting for transfers between devices: 18.8 us -> 22.9 us  [swap(): return lax.ppermute(x, 'vir', [(d, d ^ bits) for d in range(devices)])]
    ppermute x18, starting transfers between devices: 12 us -> 13.1 us  [swap(): return lax.ppermute(x, 'vir', [(d, d ^ bits) for d in range(devices)])]
  transfers between devices with their start and end apart: 21 -> 21, of which waited for: 13 -> 14; matrix products, arithmetic and copies ran while one was open for 0% -> 0% of each run, Pallas kernels for 26% -> 25%
where the time goes in v10:
time: 71.4 us
  waiting for transfers between devices  28.5 us (40%)
  Pallas kernels  20.8 us (29%)
  starting transfers between devices  16.3 us (23%)
  local copies, waits for them, and re-layouts  4.37 us (6%)
  between operations  0.72 us (1%)
    ppermute x18, waiting for transfers between devices, swap(): return lax.ppermute(x, 'vir', [(d, d ^ bits) for d in range(devices)])  22.9 us
    pallas_call x4, Pallas kernels, ladder(): pl.pallas_call(functools.partial(ladder_kernel, call, depth, shard_tiles,...  16.2 us
    ppermute x18, starting transfers between devices, swap(): return lax.ppermute(x, 'vir', [(d, d ^ bits) for d in range(devices)])  13.1 us
    ppermute x3, waiting for transfers between devices, shift_z(): return lax.ppermute(x, 'vir', hop)  5.64 us
    pallas_call x1, Pallas kernels, prepare(): pl.pallas_call(functools.partial(prepare_kernel, depth, shard_tiles), out...  4.57 us
    unnamed x12, local copies, waits for them, and re-layouts  4.37 us
    ppermute x3, starting transfers between devices, shift_z(): return lax.ppermute(x, 'vir', hop)  3.25 us
  transfers between devices with their start and end apart: 21, of which 14 were waited for; matrix products, arithmetic and copies ran while one was open for 0% of the time, Pallas kernels for 25%

profile of v10, /device:TPU:0, one launch (start us, length us, event | category | flops | bytes accessed | tf_op | source)
XLA Modules:
  0.0 71.4 jit_solution(3629683966756598542)
XLA Ops:
  0.6 3.0 %collective-permute-start.1 = (bf16[8,64,384]{2,1,0:T(8,128)(2,1)}, bf16[8,64,384]{2,1,0:T(8,128)(2,1)S(1)}, u32[]{:S(2)}, u32[]{:S(2)}) collective-permute-start(bf16[8,64,384]{2,1,0:T(8,128)(2,1)} %refs_3_.1), channel_id=1, source_target_pairs={{0,2},{1,3},{2,0},{3,1},{4,6},{5,7},{6,4},{7,5},{8,10},{9,11},{10,... | collective-permute-start | bytes 1179656 | tf_op jit(solution)/shard_map/ppermute | solution.py:320
  3.7 1.6 %collective-permute-start = (bf16[8,64,384]{2,1,0:T(8,128)(2,1)}, bf16[8,64,384]{2,1,0:T(8,128)(2,1)S(1)}, u32[]{:S(2)}, u32[]{:S(2)}) collective-permute-start(bf16[8,64,384]{2,1,0:T(8,128)(2,1)} %refs_3_.1), channel_id=1, source_target_pairs={{0,4},{1,5},{2,6},{3,7},{4,12},{5,13},{6,14},{7,15},{8,0},{9,1},{1... | collective-permute-start | bytes 1179656 | tf_op jit(solution)/shard_map/ppermute | solution.py:317
  5.2 0.0 collective-permute-start.2
  5.2 0.7 copy-done.3
  5.9 0.7 copy-done.5
  6.6 4.6 %prepare.1 = (bf16[32,64,2048]{2,1,0:T(8,128)(2,1)}, bf16[132,64,384]{2,1,0:T(8,128)(2,1)S(1)}, f32[2,8,128]{2,1,0:T(8,128)S(1)}, s32[36]{0:T(128)S(1)}, s32[8]{...) custom-call(s32[1]{0:T(128)} %bitcast.me_ref, s32[8]{0:T(128)S(1)} %copy-done.3, s32[32]{0:T(128)S(1)} %copy-done.5), custom_call_target="tpu_custom_call" | custom-call | bytes 8388608 | tf_op jit(solution)/shard_map/prepare/pallas_call | solution.py:133
  11.1 1.9 %collective-permute-done.1.refs_1_ = bf16[8,64,384]{2,1,0:T(8,128)(2,1)S(1)} collective-permute-done((bf16[8,64,384]{2,1,0:T(8,128)(2,1)}, bf16[8,64,384]{2,1,0:T(8,128)(2,1)S(1)}, u32[]{:S(2)}, u32[]{:S(2)}) %collective-permute-start.1) | collective-permute-done | bytes 393248 | tf_op jit(solution)/shard_map/ppermute | solution.py:320
  13.0 2.4 %collective-permute-done.refs_0_ = bf16[8,64,384]{2,1,0:T(8,128)(2,1)S(1)} collective-permute-done((bf16[8,64,384]{2,1,0:T(8,128)(2,1)}, bf16[8,64,384]{2,1,0:T(8,128)(2,1)S(1)}, u32[]{:S(2)}, u32[]{:S(2)}) %collective-permute-start) | collective-permute-done | bytes 393248 | tf_op jit(solution)/shard_map/ppermute | solution.py:317
  15.4 0.0 collective-permute-start.6
  15.4 0.5 collective-permute-start.5
  15.8 0.9 %collective-permute-start.4 = (bf16[8,64,384]{2,1,0:T(8,128)(2,1)S(1)}, bf16[8,64,384]{2,1,0:T(8,128)(2,1)S(1)}, u32[]{:S(2)}, u32[]{:S(2)}) collective-permute-start(bf16[8,64,384]{2,1,0:T(8,128)(2,1)S(1)} %collective-permute-done.refs_0_), channel_id=1, source_target_pairs={{0,4},{1,5},{2,6},{3,7},{4,12},{5,13},{6,14},{7,15},{8,0},{9,1},{1... | collective-permute-start | bytes 1179656 | tf_op jit(solution)/shard_map/ppermute | solution.py:317
  16.8 0.0 collective-permute-start.3
  16.8 1.4 %copy-done = bf16[32,64,384]{2,1,0:T(8,128)(2,1)S(1)} copy-done((bf16[32,64,384]{2,1,0:T(8,128)(2,1)S(1)}, bf16[32,64,384]{2,1,0:T(8,128)(2,1)}, u32[]{:S(2)}) %copy-start) | copy-done | bytes 1572888
  18.2 1.0 %copy-done.2 = bf16[8,64,384]{2,1,0:T(8,128)(2,1)S(1)} copy-done((bf16[8,64,384]{2,1,0:T(8,128)(2,1)S(1)}, bf16[8,64,384]{2,1,0:T(8,128)(2,1)}, u32[]{:S(2)}) %copy-start.2) | copy-done | bytes 393240
  19.2 0.7 copy-done.4
  19.8 3.4 %ladder_0.1 = (bf16[32,64,2048]{2,1,0:T(8,128)(2,1)}, bf16[132,64,384]{2,1,0:T(8,128)(2,1)S(1)}, f32[2,8,128]{2,1,0:T(8,128)S(1)}) custom-call(s32[1]{0:T(128)} %bitcast.me_ref, s32[8]{0:T(128)S(1)} %copy-done.4, s32[36]{0:T(128)S(1)} %get-tuple-element.45.order_ref, ...), custom_call_target="tpu_custom_call", output_to_operand_aliasing={{0}: (9, {}), {1}: (10, {})} | custom-call | flops 402653184 | bytes 2097152 | tf_op jit(solution)/shard_map/ladder_0/pallas_call | solution.py:277
  23.2 0.0 collective-permute-done.6.refs_3_
  23.2 3.7 %collective-permute-done.5.refs_1_ = bf16[8,64,384]{2,1,0:T(8,128)(2,1)S(1)} collective-permute-done((bf16[8,64,384]{2,1,0:T(8,128)(2,1)S(1)}, bf16[8,64,384]{2,1,0:T(8,128)(2,1)S(1)}, u32[]{:S(2)}, u32[]{:S(2)}) %collective-permute-start.5) | collective-permute-done | bytes 393248 | tf_op jit(solution)/shard_map/ppermute | solution.py:320
  26.9 1.1 %collective-permute-done.4.refs_0_ = bf16[8,64,384]{2,1,0:T(8,128)(2,1)S(1)} collective-permute-done((bf16[8,64,384]{2,1,0:T(8,128)(2,1)S(1)}, bf16[8,64,384]{2,1,0:T(8,128)(2,1)S(1)}, u32[]{:S(2)}, u32[]{:S(2)}) %collective-permute-start.4) | collective-permute-done | bytes 393248 | tf_op jit(solution)/shard_map/ppermute | solution.py:317
  28.0 0.0 collective-permute-done.3.refs_2_
  28.0 0.0 collective-permute-start.10
  28.0 1.6 %collective-permute-start.9 = (bf16[8,64,384]{2,1,0:T(8,128)(2,1)S(1)}, bf16[8,64,384]{2,1,0:T(8,128)(2,1)S(1)}, u32[]{:S(2)}, u32[]{:S(2)}) collective-permute-start(bf16[8,64,384]{2,1,0:T(8,128)(2,1)S(1)} %collective-permute-done.4.refs_0_), channel_id=1, source_target_pairs={{0,2},{1,3},{2,0},{3,1},{4,6},{5,7},{6,4},{7,5},{8,10},{9,11},{10,... | collective-permute-start | bytes 1179656 | tf_op jit(solution)/shard_map/ppermute | solution.py:320
  29.6 0.8 %collective-permute-start.8 = (bf16[8,64,384]{2,1,0:T(8,128)(2,1)S(1)}, bf16[8,64,384]{2,1,0:T(8,128)(2,1)S(1)}, u32[]{:S(2)}, u32[]{:S(2)}) collective-permute-start(bf16[8,64,384]{2,1,0:T(8,128)(2,1)S(1)} %collective-permute-done.4.refs_0_), channel_id=1, source_target_pairs={{0,4},{1,5},{2,6},{3,7},{4,12},{5,13},{6,14},{7,15},{8,0},{9,1},{1... | collective-permute-start | bytes 1179656 | tf_op jit(solution)/shard_map/ppermute | solution.py:317
  30.3 0.0 collective-permute-start.7
  30.3 4.1 %ladder_1.1 = (bf16[32,64,2048]{2,1,0:T(8,128)(2,1)}, bf16[132,64,384]{2,1,0:T(8,128)(2,1)S(1)}, f32[2,8,128]{2,1,0:T(8,128)S(1)}) custom-call(s32[1]{0:T(128)} %bitcast.me_ref, s32[8]{0:T(128)S(1)} %copy-done.4, s32[36]{0:T(128)S(1)} %get-tuple-element.45.order_ref, ...), custom_call_target="tpu_custom_call", output_to_operand_aliasing={{0}: (9, {}), {1}: (10, {})} | custom-call | flops 402653184 | bytes 2097152 | tf_op jit(solution)/shard_map/ladder_1/pallas_call | solution.py:277
  34.5 0.0 collective-permute-done.10.refs_3_
  34.5 5.0 %collective-permute-done.9.refs_1_ = bf16[8,64,384]{2,1,0:T(8,128)(2,1)S(1)} collective-permute-done((bf16[8,64,384]{2,1,0:T(8,128)(2,1)S(1)}, bf16[8,64,384]{2,1,0:T(8,128)(2,1)S(1)}, u32[]{:S(2)}, u32[]{:S(2)}) %collective-permute-start.9) | collective-permute-done | bytes 393248 | tf_op jit(solution)/shard_map/ppermute | solution.py:320
  39.5 2.2 %collective-permute-done.8.refs_0_ = bf16[8,64,384]{2,1,0:T(8,128)(2,1)S(1)} collective-permute-done((bf16[8,64,384]{2,1,0:T(8,128)(2,1)S(1)}, bf16[8,64,384]{2,1,0:T(8,128)(2,1)S(1)}, u32[]{:S(2)}, u32[]{:S(2)}) %collective-permute-start.8) | collective-permute-done | bytes 393248 | tf_op jit(solution)/shard_map/ppermute | solution.py:317
  41.7 0.5 collective-permute-start.12
  42.2 0.5 collective-permute-start.11
  42.7 0.7 %collective-permute-done.13.refs_5_ = bf16[8,64,384]{2,1,0:T(8,128)(2,1)S(1)} collective-permute-done((bf16[8,64,384]{2,1,0:T(8,128)(2,1)S(1)}, bf16[8,64,384]{2,1,0:T(8,128)(2,1)S(1)}, u32[]{:S(2)}, u32[]{:S(2)}) %collective-permute-start.13) | collective-permute-done | bytes 393248 | tf_op jit(solution)/shard_map/ppermute | solution.py:320
  43.4 0.6 collective-permute-done.12.refs_4_
  44.0 5.8 %ladder_2.1 = (bf16[32,64,2048]{2,1,0:T(8,128)(2,1)}, bf16[132,64,384]{2,1,0:T(8,128)(2,1)S(1)}, f32[2,8,128]{2,1,0:T(8,128)S(1)}) custom-call(s32[1]{0:T(128)} %bitcast.me_ref, s32[8]{0:T(128)S(1)} %copy-done.4, s32[36]{0:T(128)S(1)} %get-tuple-element.45.order_ref, ...), custom_call_target="tpu_custom_call", output_to_operand_aliasing={{0}: (9, {}), {1}: (10, {})} | custom-call | flops 603979776 | bytes 3145728 | tf_op jit(solution)/shard_map/ladder_2/pallas_call | solution.py:277
  49.8 3.5 %collective-permute-done.11.refs_0_ = bf16[8,64,384]{2,1,0:T(8,128)(2,1)S(1)} collective-permute-done((bf16[8,64,384]{2,1,0:T(8,128)(2,1)S(1)}, bf16[8,64,384]{2,1,0:T(8,128)(2,1)S(1)}, u32[]{:S(2)}, u32[]{:S(2)}) %collective-permute-start.11) | collective-permute-done | bytes 393248 | tf_op jit(solution)/shard_map/ppermute | solution.py:320
  53.2 0.0 collective-permute-start.14
  53.2 1.7 %collective-permute-done.14.refs_1_ = bf16[8,64,384]{2,1,0:T(8,128)(2,1)S(1)} collective-permute-done((bf16[8,64,384]{2,1,0:T(8,128)(2,1)S(1)}, bf16[8,64,384]{2,1,0:T(8,128)(2,1)S(1)}, u32[]{:S(2)}, u32[]{:S(2)}) %collective-permute-start.14) | collective-permute-done | bytes 393248 | tf_op jit(solution)/shard_map/ppermute | solution.py:320
  55.0 3.0 %ladder_3.1 = (bf16[32,64,2048]{2,1,0:T(8,128)(2,1)}, bf16[132,64,384]{2,1,0:T(8,128)(2,1)S(1)}, f32[2,8,128]{2,1,0:T(8,128)S(1)}) custom-call(s32[1]{0:T(128)} %bitcast.me_ref, s32[8]{0:T(128)S(1)} %copy-done.4, s32[36]{0:T(128)S(1)} %get-tuple-element.45.order_ref, ...), custom_call_target="tpu_custom_call", output_to_operand_aliasing={{0}: (9, {}), {1}: (10, {})} | custom-call | flops 201326592 | bytes 1048576 | tf_op jit(solution)/shard_map/ladder_3/pallas_call | solution.py:277
  57.9 0.1 collective-permute-start.17
  58.0 1.8 %collective-permute-start.16 = (f32[2,8,128]{2,1,0:T(8,128)S(1)}, f32[2,8,128]{2,1,0:T(8,128)S(1)}, u32[]{:S(2)}, u32[]{:S(2)}) collective-permute-start(f32[2,8,128]{2,1,0:T(8,128)S(1)} %get-tuple-element.87), channel_id=1, source_target_pairs={{0,2},{1,3},{2,0},{3,1},{4,6},{5,7},{6,4},{7,5},{8,10},{9,11},{10,... | collective-permute-start | bytes 24584 | tf_op jit(solution)/shard_map/ppermute | solution.py:320
  59.8 0.1 collective-permute-start.15
  59.9 1.2 %collective-permute-done.17 = f32[2,8,128]{2,1,0:T(8,128)S(1)} collective-permute-done((f32[2,8,128]{2,1,0:T(8,128)S(1)}, f32[2,8,128]{2,1,0:T(8,128)S(1)}, u32[]{:S(2)}, u32[]{:S(2)}) %collective-permute-start.17) | collective-permute-done | bytes 8224 | tf_op jit(solution)/shard_map/ppermute | solution.py:320
  61.1 0.7 collective-permute-done.16
  61.7 4.4 %collective-permute-start.20 = (f32[2,8,128]{2,1,0:T(8,128)S(1)}, f32[2,8,128]{2,1,0:T(8,128)S(1)}, u32[]{:S(2)}, u32[]{:S(2)}) collective-permute-start(f32[2,8,128]{2,1,0:T(8,128)S(1)} %add_add_fusion), channel_id=1, source_target_pairs={{0,12},{1,13},{2,14},{3,15},{4,8},{5,9},{6,10},{7,11},{8,4},{9,5},... | collective-permute-start | bytes 24584 | tf_op jit(solution)/shard_map/ppermute | solution.py:320
  66.2 0.6 collective-permute-start.18
  66.8 1.0 %collective-permute-done.20 = f32[2,8,128]{2,1,0:T(8,128)S(1)} collective-permute-done((f32[2,8,128]{2,1,0:T(8,128)S(1)}, f32[2,8,128]{2,1,0:T(8,128)S(1)}, u32[]{:S(2)}, u32[]{:S(2)}) %collective-permute-start.20) | collective-permute-done | bytes 8224 | tf_op jit(solution)/shard_map/ppermute | solution.py:320
  67.8 2.9 %collective-permute-done.19 = f32[2,8,128]{2,1,0:T(8,128)S(1)} collective-permute-done((f32[2,8,128]{2,1,0:T(8,128)S(1)}, f32[2,8,128]{2,1,0:T(8,128)S(1)}, u32[]{:S(2)}, u32[]{:S(2)}) %collective-permute-start.19) | collective-permute-done | bytes 8224 | tf_op jit(solution)/shard_map/ppermute | solution.py:320
  70.7 0.1 add_reduce_fusion
  70.8 0.5 add_sqrt_fusion
  (14 shorter events, 0.0 us)
Async XLA Ops:
  0.6 12.4 %collective-permute-start.1 = (bf16[8,64,384]{2,1,0:T(8,128)(2,1)}, bf16[8,64,384]{2,1,0:T(8,128)(2,1)S(1)}, u32[]{:S(2)}, u32[]{:S(2)}) collective-permute-start(bf16[8,64,384]{2,1,0:T(8,128)(2,1)} %refs_3_.1), channel_id=1, source_target_pairs={{0,2},{1,3},{2,0},{3,1},{4,6},{5,7},{6,4},{7,5},{8,10},{9,11},{10,... | collective-permute-start | bytes 1179656 | tf_op jit(solution)/shard_map/ppermute | solution.py:320
  3.7 11.7 %collective-permute-start = (bf16[8,64,384]{2,1,0:T(8,128)(2,1)}, bf16[8,64,384]{2,1,0:T(8,128)(2,1)S(1)}, u32[]{:S(2)}, u32[]{:S(2)}) collective-permute-start(bf16[8,64,384]{2,1,0:T(8,128)(2,1)} %refs_3_.1), channel_id=1, source_target_pairs={{0,4},{1,5},{2,6},{3,7},{4,12},{5,13},{6,14},{7,15},{8,0},{9,1},{1... | collective-permute-start | bytes 1179656 | tf_op jit(solution)/shard_map/ppermute | solution.py:317
  5.2 10.1 %collective-permute-start.2 = (bf16[8,64,384]{2,1,0:T(8,128)(2,1)}, bf16[8,64,384]{2,1,0:T(8,128)(2,1)S(1)}, u32[]{:S(2)}, u32[]{:S(2)}) collective-permute-start(bf16[8,64,384]{2,1,0:T(8,128)(2,1)} %refs_3_.1), channel_id=1, source_target_pairs={{0,1},{1,0},{2,3},{3,2},{4,5},{5,4},{6,7},{7,6},{8,9},{9,8},{10,11... | collective-permute-start | bytes 1179656 | tf_op jit(solution)/shard_map/ppermute | solution.py:320
  5.2 0.7 copy-start.3
  5.9 0.7 copy-start.5
  15.4 7.8 %collective-permute-start.6 = (bf16[8,64,384]{2,1,0:T(8,128)(2,1)S(1)}, bf16[8,64,384]{2,1,0:T(8,128)(2,1)S(1)}, u32[]{:S(2)}, u32[]{:S(2)}) collective-permute-start(bf16[8,64,384]{2,1,0:T(8,128)(2,1)S(1)} %collective-permute-done.1.refs_1_), channel_id=1, source_target_pairs={{0,1},{1,0},{2,3},{3,2},{4,5},{5,4},{6,7},{7,6},{8,9},{9,8},{10,11... | collective-permute-start | bytes 1179656 | tf_op jit(solution)/shard_map/ppermute | solution.py:320
  15.4 11.5 %collective-permute-start.5 = (bf16[8,64,384]{2,1,0:T(8,128)(2,1)S(1)}, bf16[8,64,384]{2,1,0:T(8,128)(2,1)S(1)}, u32[]{:S(2)}, u32[]{:S(2)}) collective-permute-start(bf16[8,64,384]{2,1,0:T(8,128)(2,1)S(1)} %collective-permute-done.refs_0_), channel_id=1, source_target_pairs={{0,2},{1,3},{2,0},{3,1},{4,6},{5,7},{6,4},{7,5},{8,10},{9,11},{10,... | collective-permute-start | bytes 1179656 | tf_op jit(solution)/shard_map/ppermute | solution.py:320
  15.8 12.1 %collective-permute-start.4 = (bf16[8,64,384]{2,1,0:T(8,128)(2,1)S(1)}, bf16[8,64,384]{2,1,0:T(8,128)(2,1)S(1)}, u32[]{:S(2)}, u32[]{:S(2)}) collective-permute-start(bf16[8,64,384]{2,1,0:T(8,128)(2,1)S(1)} %collective-permute-done.refs_0_), channel_id=1, source_target_pairs={{0,4},{1,5},{2,6},{3,7},{4,12},{5,13},{6,14},{7,15},{8,0},{9,1},{1... | collective-permute-start | bytes 1179656 | tf_op jit(solution)/shard_map/ppermute | solution.py:317
  16.8 11.2 %collective-permute-start.3 = (bf16[8,64,384]{2,1,0:T(8,128)(2,1)S(1)}, bf16[8,64,384]{2,1,0:T(8,128)(2,1)S(1)}, u32[]{:S(2)}, u32[]{:S(2)}) collective-permute-start(bf16[8,64,384]{2,1,0:T(8,128)(2,1)S(1)} %collective-permute-done.refs_0_), channel_id=1, source_target_pairs={{0,1},{1,0},{2,3},{3,2},{4,5},{5,4},{6,7},{7,6},{8,9},{9,8},{10,11... | collective-permute-start | bytes 1179656 | tf_op jit(solution)/shard_map/ppermute | solution.py:320
  16.8 1.4 %copy-start = (bf16[32,64,384]{2,1,0:T(8,128)(2,1)S(1)}, bf16[32,64,384]{2,1,0:T(8,128)(2,1)}, u32[]{:S(2)}) copy-start(bf16[32,64,384]{2,1,0:T(8,128)(2,1)} %v_ref.7) | copy-start | bytes 4718596
  18.2 1.0 %copy-start.2 = (bf16[8,64,384]{2,1,0:T(8,128)(2,1)S(1)}, bf16[8,64,384]{2,1,0:T(8,128)(2,1)}, u32[]{:S(2)}) copy-start(bf16[8,64,384]{2,1,0:T(8,128)(2,1)} %refs_3_.1) | copy-start | bytes 1179652
  19.2 0.7 copy-start.4
  19.8 10.5 %copy-start.1 = (bf16[32,64,384]{2,1,0:T(8,128)(2,1)S(1)}, bf16[32,64,384]{2,1,0:T(8,128)(2,1)}, u32[]{:S(2)}) copy-start(bf16[32,64,384]{2,1,0:T(8,128)(2,1)} %v_ref.7) | copy-start | bytes 4718596
  28.0 6.5 %collective-permute-start.10 = (bf16[8,64,384]{2,1,0:T(8,128)(2,1)S(1)}, bf16[8,64,384]{2,1,0:T(8,128)(2,1)S(1)}, u32[]{:S(2)}, u32[]{:S(2)}) collective-permute-start(bf16[8,64,384]{2,1,0:T(8,128)(2,1)S(1)} %collective-permute-done.5.refs_1_), channel_id=1, source_target_pairs={{0,1},{1,0},{2,3},{3,2},{4,5},{5,4},{6,7},{7,6},{8,9},{9,8},{10,11... | collective-permute-start | bytes 1179656 | tf_op jit(solution)/shard_map/ppermute | solution.py:320
  28.0 11.5 %collective-permute-start.9 = (bf16[8,64,384]{2,1,0:T(8,128)(2,1)S(1)}, bf16[8,64,384]{2,1,0:T(8,128)(2,1)S(1)}, u32[]{:S(2)}, u32[]{:S(2)}) collective-permute-start(bf16[8,64,384]{2,1,0:T(8,128)(2,1)S(1)} %collective-permute-done.4.refs_0_), channel_id=1, source_target_pairs={{0,2},{1,3},{2,0},{3,1},{4,6},{5,7},{6,4},{7,5},{8,10},{9,11},{10,... | collective-permute-start | bytes 1179656 | tf_op jit(solution)/shard_map/ppermute | solution.py:320
  29.6 12.1 %collective-permute-start.8 = (bf16[8,64,384]{2,1,0:T(8,128)(2,1)S(1)}, bf16[8,64,384]{2,1,0:T(8,128)(2,1)S(1)}, u32[]{:S(2)}, u32[]{:S(2)}) collective-permute-start(bf16[8,64,384]{2,1,0:T(8,128)(2,1)S(1)} %collective-permute-done.4.refs_0_), channel_id=1, source_target_pairs={{0,4},{1,5},{2,6},{3,7},{4,12},{5,13},{6,14},{7,15},{8,0},{9,1},{1... | collective-permute-start | bytes 1179656 | tf_op jit(solution)/shard_map/ppermute | solution.py:317
  30.3 11.4 %collective-permute-start.7 = (bf16[8,64,384]{2,1,0:T(8,128)(2,1)S(1)}, bf16[8,64,384]{2,1,0:T(8,128)(2,1)S(1)}, u32[]{:S(2)}, u32[]{:S(2)}) collective-permute-start(bf16[8,64,384]{2,1,0:T(8,128)(2,1)S(1)} %collective-permute-done.4.refs_0_), channel_id=1, source_target_pairs={{0,1},{1,0},{2,3},{3,2},{4,5},{5,4},{6,7},{7,6},{8,9},{9,8},{10,11... | collective-permute-start | bytes 1179656 | tf_op jit(solution)/shard_map/ppermute | solution.py:320
  41.7 1.7 %collective-permute-start.13 = (bf16[8,64,384]{2,1,0:T(8,128)(2,1)S(1)}, bf16[8,64,384]{2,1,0:T(8,128)(2,1)S(1)}, u32[]{:S(2)}, u32[]{:S(2)}) collective-permute-start(bf16[8,64,384]{2,1,0:T(8,128)(2,1)S(1)} %collective-permute-done.9.refs_1_), channel_id=1, source_target_pairs={{0,1},{1,0},{2,3},{3,2},{4,5},{5,4},{6,7},{7,6},{8,9},{9,8},{10,11... | collective-permute-start | bytes 1179656 | tf_op jit(solution)/shard_map/ppermute | solution.py:320
  41.7 2.3 %collective-permute-start.12 = (bf16[8,64,384]{2,1,0:T(8,128)(2,1)S(1)}, bf16[8,64,384]{2,1,0:T(8,128)(2,1)S(1)}, u32[]{:S(2)}, u32[]{:S(2)}) collective-permute-start(bf16[8,64,384]{2,1,0:T(8,128)(2,1)S(1)} %collective-permute-done.8.refs_0_), channel_id=1, source_target_pairs={{0,1},{1,0},{2,3},{3,2},{4,5},{5,4},{6,7},{7,6},{8,9},{9,8},{10,11... | collective-permute-start | bytes 1179656 | tf_op jit(solution)/shard_map/ppermute | solution.py:320
  42.2 11.0 %collective-permute-start.11 = (bf16[8,64,384]{2,1,0:T(8,128)(2,1)S(1)}, bf16[8,64,384]{2,1,0:T(8,128)(2,1)S(1)}, u32[]{:S(2)}, u32[]{:S(2)}) collective-permute-start(bf16[8,64,384]{2,1,0:T(8,128)(2,1)S(1)} %collective-permute-done.8.refs_0_), channel_id=1, source_target_pairs={{0,2},{1,3},{2,0},{3,1},{4,6},{5,7},{6,4},{7,5},{8,10},{9,11},{10,... | collective-permute-start | bytes 1179656 | tf_op jit(solution)/shard_map/ppermute | solution.py:320
  53.2 1.7 %collective-permute-start.14 = (bf16[8,64,384]{2,1,0:T(8,128)(2,1)S(1)}, bf16[8,64,384]{2,1,0:T(8,128)(2,1)S(1)}, u32[]{:S(2)}, u32[]{:S(2)}) collective-permute-start(bf16[8,64,384]{2,1,0:T(8,128)(2,1)S(1)} %collective-permute-done.11.refs_0_), channel_id=1, source_target_pairs={{0,1},{1,0},{2,3},{3,2},{4,5},{5,4},{6,7},{7,6},{8,9},{9,8},{10,11... | collective-permute-start | bytes 1179656 | tf_op jit(solution)/shard_map/ppermute | solution.py:320
  57.9 3.1 %collective-permute-start.17 = (f32[2,8,128]{2,1,0:T(8,128)S(1)}, f32[2,8,128]{2,1,0:T(8,128)S(1)}, u32[]{:S(2)}, u32[]{:S(2)}) collective-permute-start(f32[2,8,128]{2,1,0:T(8,128)S(1)} %get-tuple-element.87), channel_id=1, source_target_pairs={{0,3},{1,2},{2,1},{3,0},{4,7},{5,6},{6,5},{7,4},{8,11},{9,10},{10,... | collective-permute-start | bytes 24584 | tf_op jit(solution)/shard_map/ppermute | solution.py:320
  58.0 3.7 %collective-permute-start.16 = (f32[2,8,128]{2,1,0:T(8,128)S(1)}, f32[2,8,128]{2,1,0:T(8,128)S(1)}, u32[]{:S(2)}, u32[]{:S(2)}) collective-permute-start(f32[2,8,128]{2,1,0:T(8,128)S(1)} %get-tuple-element.87), channel_id=1, source_target_pairs={{0,2},{1,3},{2,0},{3,1},{4,6},{5,7},{6,4},{7,5},{8,10},{9,11},{10,... | collective-permute-start | bytes 24584 | tf_op jit(solution)/shard_map/ppermute | solution.py:320
  59.8 2.0 %collective-permute-start.15 = (f32[2,8,128]{2,1,0:T(8,128)S(1)}, f32[2,8,128]{2,1,0:T(8,128)S(1)}, u32[]{:S(2)}, u32[]{:S(2)}) collective-permute-start(f32[2,8,128]{2,1,0:T(8,128)S(1)} %get-tuple-element.87), channel_id=1, source_target_pairs={{0,1},{1,0},{2,3},{3,2},{4,5},{5,4},{6,7},{7,6},{8,9},{9,8},{10,11... | collective-permute-start | bytes 24584 | tf_op jit(solution)/shard_map/ppermute | solution.py:320
  61.7 6.1 %collective-permute-start.20 = (f32[2,8,128]{2,1,0:T(8,128)S(1)}, f32[2,8,128]{2,1,0:T(8,128)S(1)}, u32[]{:S(2)}, u32[]{:S(2)}) collective-permute-start(f32[2,8,128]{2,1,0:T(8,128)S(1)} %add_add_fusion), channel_id=1, source_target_pairs={{0,12},{1,13},{2,14},{3,15},{4,8},{5,9},{6,10},{7,11},{8,4},{9,5},... | collective-permute-start | bytes 24584 | tf_op jit(solution)/shard_map/ppermute | solution.py:320
  66.2 4.5 %collective-permute-start.19 = (f32[2,8,128]{2,1,0:T(8,128)S(1)}, f32[2,8,128]{2,1,0:T(8,128)S(1)}, u32[]{:S(2)}, u32[]{:S(2)}) collective-permute-start(f32[2,8,128]{2,1,0:T(8,128)S(1)} %add_add_fusion), channel_id=1, source_target_pairs={{0,8},{1,9},{2,10},{3,11},{4,12},{5,13},{6,14},{7,15},{8,0},{9,1},... | collective-permute-start | bytes 24584 | tf_op jit(solution)/shard_map/ppermute | solution.py:320
  66.2 4.5 %collective-permute-start.18 = (f32[2,8,128]{2,1,0:T(8,128)S(1)}, f32[2,8,128]{2,1,0:T(8,128)S(1)}, u32[]{:S(2)}, u32[]{:S(2)}) collective-permute-start(f32[2,8,128]{2,1,0:T(8,128)S(1)} %add_add_fusion), channel_id=1, source_target_pairs={{0,4},{1,5},{2,6},{3,7},{4,0},{5,1},{6,2},{7,3},{8,12},{9,13},{10,... | collective-permute-start | bytes 24584 | tf_op jit(solution)/shard_map/ppermute | solution.py:320

commit v11 on v10

--- a/solution.py
+++ b/solution.py
@@ -328,12 +328,7 @@
     a, b, c, d = [amplitudes], [], [], []
     for k in range(depth):
         if k:
-            if k == 1:
-                a[k], b[-1], c[-1], state = lax.optimization_barrier((a[k], b[-1], c[-1], state))
-            else:
-                c[-1], a[k], b[-1], d[-1], state = lax.optimization_barrier(
-                    (c[-1], a[k], b[-1], d[-1], state)
-                )
+            c[-1], a[k], state = lax.optimization_barrier((c[-1], a[k], state))
         b.append(swap(a[k], 2))
         if k < depth - 1:
             a.append(shift_z(a[k]))

time: 71.4 us -> 68.6 us (0.961)
  waiting for transfers between devices: 28.5 us -> 23.2 us
  starting transfers between devices: 16.3 us -> 18.4 us
    ppermute x18, waiting for transfers between devices: 22.9 us -> 14.2 us  [swap(): return lax.ppermute(x, 'vir', [(d, d ^ bits) for d in range(devices)])]
    ppermute x3, waiting for transfers between devices: 5.64 us -> 8.98 us  [shift_z(): return lax.ppermute(x, 'vir', hop)]
    ppermute x3, starting transfers between devices: 3.25 us -> 5.23 us  [shift_z(): return lax.ppermute(x, 'vir', hop)]
  transfers between devices with their start and end apart: 21 -> 21, of which waited for: 14 -> 12; matrix products, arithmetic and copies ran while one was open for 0% -> 0% of each run, Pallas kernels for 25% -> 26%
where the time goes in v11:
time: 68.6 us; the launch traced here: 68.4 us
  waiting for transfers between devices  23.2 us (34%)
  Pallas kernels  21.1 us (31%)
  starting transfers between devices  18.4 us (27%)
  local copies, waits for them, and re-layouts  4.37 us (6%)
  between operations  0.72 us (1%)
    pallas_call x4, Pallas kernels, ladder(): pl.pallas_call(functools.partial(ladder_kernel, call, depth, shard_tiles,...  16.5 us
    ppermute x18, waiting for transfers between devices, swap(): return lax.ppermute(x, 'vir', [(d, d ^ bits) for d in range(devices)])  14.2 us
    ppermute x18, starting transfers between devices, swap(): return lax.ppermute(x, 'vir', [(d, d ^ bits) for d in range(devices)])  13.1 us
    ppermute x3, waiting for transfers between devices, shift_z(): return lax.ppermute(x, 'vir', hop)  8.98 us
    ppermute x3, starting transfers between devices, shift_z(): return lax.ppermute(x, 'vir', hop)  5.23 us
    pallas_call x1, Pallas kernels, prepare(): pl.pallas_call(functools.partial(prepare_kernel, depth, shard_tiles), out...  4.57 us
    unnamed x12, local copies, waits for them, and re-layouts  4.37 us
  transfers between devices with their start and end apart: 21, of which 12 were waited for; matrix products, arithmetic and copies ran while one was open for 0% of the time, Pallas kernels for 26%

profile of v11, /device:TPU:0, one launch (start us, length us, event | category | flops | bytes accessed | tf_op | source)
XLA Modules:
  0.0 68.4 jit_solution(4322863686692704417)
XLA Ops:
  0.6 3.1 %collective-permute-start.1 = (bf16[8,64,384]{2,1,0:T(8,128)(2,1)}, bf16[8,64,384]{2,1,0:T(8,128)(2,1)S(1)}, u32[]{:S(2)}, u32[]{:S(2)}) collective-permute-start(bf16[8,64,384]{2,1,0:T(8,128)(2,1)} %refs_3_.1), channel_id=1, source_target_pairs={{0,4},{1,5},{2,6},{3,7},{4,12},{5,13},{6,14},{7,15},{8,0},{9,1},{1... | collective-permute-start | bytes 1179656 | tf_op jit(solution)/shard_map/ppermute | solution.py:317
  3.7 0.0 collective-permute-start
  3.7 1.5 %collective-permute-start.4 = (bf16[8,64,384]{2,1,0:T(8,128)(2,1)}, bf16[8,64,384]{2,1,0:T(8,128)(2,1)S(1)}, u32[]{:S(2)}, u32[]{:S(2)}) collective-permute-start(bf16[8,64,384]{2,1,0:T(8,128)(2,1)} %refs_3_.1), channel_id=1, source_target_pairs={{0,2},{1,3},{2,0},{3,1},{4,6},{5,7},{6,4},{7,5},{8,10},{9,11},{10,... | collective-permute-start | bytes 1179656 | tf_op jit(solution)/shard_map/ppermute | solution.py:320
  5.2 0.7 copy-done.3
  5.9 0.7 copy-done.5
  6.5 4.6 %prepare.1 = (bf16[32,64,2048]{2,1,0:T(8,128)(2,1)}, bf16[132,64,384]{2,1,0:T(8,128)(2,1)S(1)}, f32[2,8,128]{2,1,0:T(8,128)S(1)}, s32[36]{0:T(128)S(1)}, s32[8]{...) custom-call(s32[1]{0:T(128)} %bitcast.me_ref, s32[8]{0:T(128)S(1)} %copy-done.3, s32[32]{0:T(128)S(1)} %copy-done.5), custom_call_target="tpu_custom_call" | custom-call | bytes 8388608 | tf_op jit(solution)/shard_map/prepare/pallas_call | solution.py:133
  11.1 2.9 %collective-permute-done.1.refs_0_ = bf16[8,64,384]{2,1,0:T(8,128)(2,1)S(1)} collective-permute-done((bf16[8,64,384]{2,1,0:T(8,128)(2,1)}, bf16[8,64,384]{2,1,0:T(8,128)(2,1)S(1)}, u32[]{:S(2)}, u32[]{:S(2)}) %collective-permute-start.1) | collective-permute-done | bytes 393248 | tf_op jit(solution)/shard_map/ppermute | solution.py:317
  14.0 0.0 collective-permute-done.refs_2_
  14.0 0.9 %collective-permute-start.3 = (bf16[8,64,384]{2,1,0:T(8,128)(2,1)S(1)}, bf16[8,64,384]{2,1,0:T(8,128)(2,1)S(1)}, u32[]{:S(2)}, u32[]{:S(2)}) collective-permute-start(bf16[8,64,384]{2,1,0:T(8,128)(2,1)S(1)} %collective-permute-done.1.refs_0_), channel_id=1, source_target_pairs={{0,4},{1,5},{2,6},{3,7},{4,12},{5,13},{6,14},{7,15},{8,0},{9,1},{1... | collective-permute-start | bytes 1179656 | tf_op jit(solution)/shard_map/ppermute | solution.py:317
  15.0 1.5 %collective-permute-start.7 = (bf16[8,64,384]{2,1,0:T(8,128)(2,1)S(1)}, bf16[8,64,384]{2,1,0:T(8,128)(2,1)S(1)}, u32[]{:S(2)}, u32[]{:S(2)}) collective-permute-start(bf16[8,64,384]{2,1,0:T(8,128)(2,1)S(1)} %collective-permute-done.1.refs_0_), channel_id=1, source_target_pairs={{0,2},{1,3},{2,0},{3,1},{4,6},{5,7},{6,4},{7,5},{8,10},{9,11},{10,... | collective-permute-start | bytes 1179656 | tf_op jit(solution)/shard_map/ppermute | solution.py:320
  16.5 0.0 collective-permute-done.4.refs_1_
  16.5 0.2 collective-permute-start.8
  16.7 1.4 %copy-done = bf16[32,64,384]{2,1,0:T(8,128)(2,1)S(1)} copy-done((bf16[32,64,384]{2,1,0:T(8,128)(2,1)S(1)}, bf16[32,64,384]{2,1,0:T(8,128)(2,1)}, u32[]{:S(2)}) %copy-start) | copy-done | bytes 1572888
  18.2 1.0 %copy-done.2 = bf16[8,64,384]{2,1,0:T(8,128)(2,1)S(1)} copy-done((bf16[8,64,384]{2,1,0:T(8,128)(2,1)S(1)}, bf16[8,64,384]{2,1,0:T(8,128)(2,1)}, u32[]{:S(2)}) %copy-start.2) | copy-done | bytes 393240
  19.1 0.7 copy-done.4
  19.8 3.3 %ladder_0.1 = (bf16[32,64,2048]{2,1,0:T(8,128)(2,1)}, bf16[132,64,384]{2,1,0:T(8,128)(2,1)S(1)}, f32[2,8,128]{2,1,0:T(8,128)S(1)}) custom-call(s32[1]{0:T(128)} %bitcast.me_ref, s32[8]{0:T(128)S(1)} %copy-done.4, s32[36]{0:T(128)S(1)} %get-tuple-element.40.order_ref, ...), custom_call_target="tpu_custom_call", output_to_operand_aliasing={{0}: (9, {}), {1}: (10, {})} | custom-call | flops 402653184 | bytes 2097152 | tf_op jit(solution)/shard_map/ladder_0/pallas_call | solution.py:277
  23.1 2.1 %collective-permute-done.3.refs_0_ = bf16[8,64,384]{2,1,0:T(8,128)(2,1)S(1)} collective-permute-done((bf16[8,64,384]{2,1,0:T(8,128)(2,1)S(1)}, bf16[8,64,384]{2,1,0:T(8,128)(2,1)S(1)}, u32[]{:S(2)}, u32[]{:S(2)}) %collective-permute-start.3) | collective-permute-done | bytes 393248 | tf_op jit(solution)/shard_map/ppermute | solution.py:317
  25.3 0.0 collective-permute-done.2.refs_2_
  25.3 1.2 %collective-permute-start.6 = (bf16[8,64,384]{2,1,0:T(8,128)(2,1)S(1)}, bf16[8,64,384]{2,1,0:T(8,128)(2,1)S(1)}, u32[]{:S(2)}, u32[]{:S(2)}) collective-permute-start(bf16[8,64,384]{2,1,0:T(8,128)(2,1)S(1)} %collective-permute-done.3.refs_0_), channel_id=1, source_target_pairs={{0,4},{1,5},{2,6},{3,7},{4,12},{5,13},{6,14},{7,15},{8,0},{9,1},{1... | collective-permute-start | bytes 1179656 | tf_op jit(solution)/shard_map/ppermute | solution.py:317
  26.5 0.0 collective-permute-start.5
  26.5 1.1 %collective-permute-start.10 = (bf16[8,64,384]{2,1,0:T(8,128)(2,1)S(1)}, bf16[8,64,384]{2,1,0:T(8,128)(2,1)S(1)}, u32[]{:S(2)}, u32[]{:S(2)}) collective-permute-start(bf16[8,64,384]{2,1,0:T(8,128)(2,1)S(1)} %collective-permute-done.3.refs_0_), channel_id=1, source_target_pairs={{0,2},{1,3},{2,0},{3,1},{4,6},{5,7},{6,4},{7,5},{8,10},{9,11},{10,... | collective-permute-start | bytes 1179656 | tf_op jit(solution)/shard_map/ppermute | solution.py:320
  27.6 0.0 collective-permute-done.7.refs_1_
  27.6 0.0 collective-permute-start.11
  27.6 0.0 collective-permute-done.8.refs_3_
  27.6 4.0 %ladder_1.1 = (bf16[32,64,2048]{2,1,0:T(8,128)(2,1)}, bf16[132,64,384]{2,1,0:T(8,128)(2,1)S(1)}, f32[2,8,128]{2,1,0:T(8,128)S(1)}) custom-call(s32[1]{0:T(128)} %bitcast.me_ref, s32[8]{0:T(128)S(1)} %copy-done.4, s32[36]{0:T(128)S(1)} %get-tuple-element.40.order_ref, ...), custom_call_target="tpu_custom_call", output_to_operand_aliasing={{0}: (9, {}), {1}: (10, {})} | custom-call | flops 402653184 | bytes 2097152 | tf_op jit(solution)/shard_map/ladder_1/pallas_call | solution.py:277
  31.6 3.9 %collective-permute-done.6.refs_0_ = bf16[8,64,384]{2,1,0:T(8,128)(2,1)S(1)} collective-permute-done((bf16[8,64,384]{2,1,0:T(8,128)(2,1)S(1)}, bf16[8,64,384]{2,1,0:T(8,128)(2,1)S(1)}, u32[]{:S(2)}, u32[]{:S(2)}) %collective-permute-start.6) | collective-permute-done | bytes 393248 | tf_op jit(solution)/shard_map/ppermute | solution.py:317
  35.5 0.0 collective-permute-done.5.refs_2_
  35.5 2.5 %collective-permute-done.10.refs_1_ = bf16[8,64,384]{2,1,0:T(8,128)(2,1)S(1)} collective-permute-done((bf16[8,64,384]{2,1,0:T(8,128)(2,1)S(1)}, bf16[8,64,384]{2,1,0:T(8,128)(2,1)S(1)}, u32[]{:S(2)}, u32[]{:S(2)}) %collective-permute-start.10) | collective-permute-done | bytes 393248 | tf_op jit(solution)/shard_map/ppermute | solution.py:320
  38.0 0.5 collective-permute-start.12
  38.5 0.8 %collective-permute-start.9 = (bf16[8,64,384]{2,1,0:T(8,128)(2,1)S(1)}, bf16[8,64,384]{2,1,0:T(8,128)(2,1)S(1)}, u32[]{:S(2)}, u32[]{:S(2)}) collective-permute-start(bf16[8,64,384]{2,1,0:T(8,128)(2,1)S(1)} %collective-permute-done.6.refs_0_), channel_id=1, source_target_pairs={{0,2},{1,3},{2,0},{3,1},{4,6},{5,7},{6,4},{7,5},{8,10},{9,11},{10,... | collective-permute-start | bytes 1179656 | tf_op jit(solution)/shard_map/ppermute | solution.py:320
  39.3 0.4 collective-permute-done.13.refs_5_
  39.7 0.6 collective-permute-done.12.refs_4_
  40.3 5.7 %ladder_2.1 = (bf16[32,64,2048]{2,1,0:T(8,128)(2,1)}, bf16[132,64,384]{2,1,0:T(8,128)(2,1)S(1)}, f32[2,8,128]{2,1,0:T(8,128)S(1)}) custom-call(s32[1]{0:T(128)} %bitcast.me_ref, s32[8]{0:T(128)S(1)} %copy-done.4, s32[36]{0:T(128)S(1)} %get-tuple-element.40.order_ref, ...), custom_call_target="tpu_custom_call", output_to_operand_aliasing={{0}: (9, {}), {1}: (10, {})} | custom-call | flops 603979776 | bytes 3145728 | tf_op jit(solution)/shard_map/ladder_2/pallas_call | solution.py:277
  46.0 3.5 %collective-permute-done.9.refs_0_ = bf16[8,64,384]{2,1,0:T(8,128)(2,1)S(1)} collective-permute-done((bf16[8,64,384]{2,1,0:T(8,128)(2,1)S(1)}, bf16[8,64,384]{2,1,0:T(8,128)(2,1)S(1)}, u32[]{:S(2)}, u32[]{:S(2)}) %collective-permute-start.9) | collective-permute-done | bytes 393248 | tf_op jit(solution)/shard_map/ppermute | solution.py:320
  49.5 1.7 %collective-permute-done.14.refs_1_ = bf16[8,64,384]{2,1,0:T(8,128)(2,1)S(1)} collective-permute-done((bf16[8,64,384]{2,1,0:T(8,128)(2,1)S(1)}, bf16[8,64,384]{2,1,0:T(8,128)(2,1)S(1)}, u32[]{:S(2)}, u32[]{:S(2)}) %collective-permute-start.14) | collective-permute-done | bytes 393248 | tf_op jit(solution)/shard_map/ppermute | solution.py:320
  51.3 3.5 %ladder_3.1 = (bf16[32,64,2048]{2,1,0:T(8,128)(2,1)}, bf16[132,64,384]{2,1,0:T(8,128)(2,1)S(1)}, f32[2,8,128]{2,1,0:T(8,128)S(1)}) custom-call(s32[1]{0:T(128)} %bitcast.me_ref, s32[8]{0:T(128)S(1)} %copy-done.4, s32[36]{0:T(128)S(1)} %get-tuple-element.40.order_ref, ...), custom_call_target="tpu_custom_call", output_to_operand_aliasing={{0}: (9, {}), {1}: (10, {})} | custom-call | flops 201326592 | bytes 1048576 | tf_op jit(solution)/shard_map/ladder_3/pallas_call | solution.py:277
  54.8 0.1 collective-permute-start.17
  54.9 0.6 collective-permute-start.16
  55.5 1.2 %collective-permute-start.15 = (f32[2,8,128]{2,1,0:T(8,128)S(1)}, f32[2,8,128]{2,1,0:T(8,128)S(1)}, u32[]{:S(2)}, u32[]{:S(2)}) collective-permute-start(f32[2,8,128]{2,1,0:T(8,128)S(1)} %get-tuple-element.77), channel_id=1, source_target_pairs={{0,1},{1,0},{2,3},{3,2},{4,5},{5,4},{6,7},{7,6},{8,9},{9,8},{10,11... | collective-permute-start | bytes 24584 | tf_op jit(solution)/shard_map/ppermute | solution.py:320
  56.7 1.2 %collective-permute-done.17 = f32[2,8,128]{2,1,0:T(8,128)S(1)} collective-permute-done((f32[2,8,128]{2,1,0:T(8,128)S(1)}, f32[2,8,128]{2,1,0:T(8,128)S(1)}, u32[]{:S(2)}, u32[]{:S(2)}) %collective-permute-start.17) | collective-permute-done | bytes 8224 | tf_op jit(solution)/shard_map/ppermute | solution.py:320
  57.9 0.7 collective-permute-done.16
  58.6 2.9 %collective-permute-start.20 = (f32[2,8,128]{2,1,0:T(8,128)S(1)}, f32[2,8,128]{2,1,0:T(8,128)S(1)}, u32[]{:S(2)}, u32[]{:S(2)}) collective-permute-start(f32[2,8,128]{2,1,0:T(8,128)S(1)} %add_add_fusion), channel_id=1, source_target_pairs={{0,12},{1,13},{2,14},{3,15},{4,8},{5,9},{6,10},{7,11},{8,4},{9,5},... | collective-permute-start | bytes 24584 | tf_op jit(solution)/shard_map/ppermute | solution.py:320
  61.5 2.6 %collective-permute-start.19 = (f32[2,8,128]{2,1,0:T(8,128)S(1)}, f32[2,8,128]{2,1,0:T(8,128)S(1)}, u32[]{:S(2)}, u32[]{:S(2)}) collective-permute-start(f32[2,8,128]{2,1,0:T(8,128)S(1)} %add_add_fusion), channel_id=1, source_target_pairs={{0,8},{1,9},{2,10},{3,11},{4,12},{5,13},{6,14},{7,15},{8,0},{9,1},... | collective-permute-start | bytes 24584 | tf_op jit(solution)/shard_map/ppermute | solution.py:320
  64.1 0.0 collective-permute-done.20
  64.1 1.9 %collective-permute-done.19 = f32[2,8,128]{2,1,0:T(8,128)S(1)} collective-permute-done((f32[2,8,128]{2,1,0:T(8,128)S(1)}, f32[2,8,128]{2,1,0:T(8,128)S(1)}, u32[]{:S(2)}, u32[]{:S(2)}) %collective-permute-start.19) | collective-permute-done | bytes 8224 | tf_op jit(solution)/shard_map/ppermute | solution.py:320
  66.0 1.7 %collective-permute-done.18 = f32[2,8,128]{2,1,0:T(8,128)S(1)} collective-permute-done((f32[2,8,128]{2,1,0:T(8,128)S(1)}, f32[2,8,128]{2,1,0:T(8,128)S(1)}, u32[]{:S(2)}, u32[]{:S(2)}) %collective-permute-start.18) | collective-permute-done | bytes 8224 | tf_op jit(solution)/shard_map/ppermute | solution.py:320
  67.7 0.1 add_reduce_fusion
  67.8 0.5 add_sqrt_fusion
  (14 shorter events, 0.0 us)
Async XLA Ops:
  0.6 13.4 %collective-permute-start.1 = (bf16[8,64,384]{2,1,0:T(8,128)(2,1)}, bf16[8,64,384]{2,1,0:T(8,128)(2,1)S(1)}, u32[]{:S(2)}, u32[]{:S(2)}) collective-permute-start(bf16[8,64,384]{2,1,0:T(8,128)(2,1)} %refs_3_.1), channel_id=1, source_target_pairs={{0,4},{1,5},{2,6},{3,7},{4,12},{5,13},{6,14},{7,15},{8,0},{9,1},{1... | collective-permute-start | bytes 1179656 | tf_op jit(solution)/shard_map/ppermute | solution.py:317
  3.7 10.3 %collective-permute-start = (bf16[8,64,384]{2,1,0:T(8,128)(2,1)}, bf16[8,64,384]{2,1,0:T(8,128)(2,1)S(1)}, u32[]{:S(2)}, u32[]{:S(2)}) collective-permute-start(bf16[8,64,384]{2,1,0:T(8,128)(2,1)} %refs_3_.1), channel_id=1, source_target_pairs={{0,1},{1,0},{2,3},{3,2},{4,5},{5,4},{6,7},{7,6},{8,9},{9,8},{10,11... | collective-permute-start | bytes 1179656 | tf_op jit(solution)/shard_map/ppermute | solution.py:320
  3.7 12.8 %collective-permute-start.4 = (bf16[8,64,384]{2,1,0:T(8,128)(2,1)}, bf16[8,64,384]{2,1,0:T(8,128)(2,1)S(1)}, u32[]{:S(2)}, u32[]{:S(2)}) collective-permute-start(bf16[8,64,384]{2,1,0:T(8,128)(2,1)} %refs_3_.1), channel_id=1, source_target_pairs={{0,2},{1,3},{2,0},{3,1},{4,6},{5,7},{6,4},{7,5},{8,10},{9,11},{10,... | collective-permute-start | bytes 1179656 | tf_op jit(solution)/shard_map/ppermute | solution.py:320
  5.2 0.7 copy-start.3
  5.9 0.7 copy-start.5
  14.0 11.2 %collective-permute-start.3 = (bf16[8,64,384]{2,1,0:T(8,128)(2,1)S(1)}, bf16[8,64,384]{2,1,0:T(8,128)(2,1)S(1)}, u32[]{:S(2)}, u32[]{:S(2)}) collective-permute-start(bf16[8,64,384]{2,1,0:T(8,128)(2,1)S(1)} %collective-permute-done.1.refs_0_), channel_id=1, source_target_pairs={{0,4},{1,5},{2,6},{3,7},{4,12},{5,13},{6,14},{7,15},{8,0},{9,1},{1... | collective-permute-start | bytes 1179656 | tf_op jit(solution)/shard_map/ppermute | solution.py:317
  15.0 10.3 %collective-permute-start.2 = (bf16[8,64,384]{2,1,0:T(8,128)(2,1)S(1)}, bf16[8,64,384]{2,1,0:T(8,128)(2,1)S(1)}, u32[]{:S(2)}, u32[]{:S(2)}) collective-permute-start(bf16[8,64,384]{2,1,0:T(8,128)(2,1)S(1)} %collective-permute-done.1.refs_0_), channel_id=1, source_target_pairs={{0,1},{1,0},{2,3},{3,2},{4,5},{5,4},{6,7},{7,6},{8,9},{9,8},{10,11... | collective-permute-start | bytes 1179656 | tf_op jit(solution)/shard_map/ppermute | solution.py:320
  15.0 12.6 %collective-permute-start.7 = (bf16[8,64,384]{2,1,0:T(8,128)(2,1)S(1)}, bf16[8,64,384]{2,1,0:T(8,128)(2,1)S(1)}, u32[]{:S(2)}, u32[]{:S(2)}) collective-permute-start(bf16[8,64,384]{2,1,0:T(8,128)(2,1)S(1)} %collective-permute-done.1.refs_0_), channel_id=1, source_target_pairs={{0,2},{1,3},{2,0},{3,1},{4,6},{5,7},{6,4},{7,5},{8,10},{9,11},{10,... | collective-permute-start | bytes 1179656 | tf_op jit(solution)/shard_map/ppermute | solution.py:320
  16.5 11.1 %collective-permute-start.8 = (bf16[8,64,384]{2,1,0:T(8,128)(2,1)S(1)}, bf16[8,64,384]{2,1,0:T(8,128)(2,1)S(1)}, u32[]{:S(2)}, u32[]{:S(2)}) collective-permute-start(bf16[8,64,384]{2,1,0:T(8,128)(2,1)S(1)} %collective-permute-done.4.refs_1_), channel_id=1, source_target_pairs={{0,1},{1,0},{2,3},{3,2},{4,5},{5,4},{6,7},{7,6},{8,9},{9,8},{10,11... | collective-permute-start | bytes 1179656 | tf_op jit(solution)/shard_map/ppermute | solution.py:320
  16.7 1.4 %copy-start = (bf16[32,64,384]{2,1,0:T(8,128)(2,1)S(1)}, bf16[32,64,384]{2,1,0:T(8,128)(2,1)}, u32[]{:S(2)}) copy-start(bf16[32,64,384]{2,1,0:T(8,128)(2,1)} %v_ref.7) | copy-start | bytes 4718596
  18.2 1.0 %copy-start.2 = (bf16[8,64,384]{2,1,0:T(8,128)(2,1)S(1)}, bf16[8,64,384]{2,1,0:T(8,128)(2,1)}, u32[]{:S(2)}) copy-start(bf16[8,64,384]{2,1,0:T(8,128)(2,1)} %refs_3_.1) | copy-start | bytes 1179652
  19.1 0.7 copy-start.4
  19.8 7.8 %copy-start.1 = (bf16[32,64,384]{2,1,0:T(8,128)(2,1)S(1)}, bf16[32,64,384]{2,1,0:T(8,128)(2,1)}, u32[]{:S(2)}) copy-start(bf16[32,64,384]{2,1,0:T(8,128)(2,1)} %v_ref.7) | copy-start | bytes 4718596
  25.3 10.3 %collective-permute-start.6 = (bf16[8,64,384]{2,1,0:T(8,128)(2,1)S(1)}, bf16[8,64,384]{2,1,0:T(8,128)(2,1)S(1)}, u32[]{:S(2)}, u32[]{:S(2)}) collective-permute-start(bf16[8,64,384]{2,1,0:T(8,128)(2,1)S(1)} %collective-permute-done.3.refs_0_), channel_id=1, source_target_pairs={{0,4},{1,5},{2,6},{3,7},{4,12},{5,13},{6,14},{7,15},{8,0},{9,1},{1... | collective-permute-start | bytes 1179656 | tf_op jit(solution)/shard_map/ppermute | solution.py:317
  26.5 9.1 %collective-permute-start.5 = (bf16[8,64,384]{2,1,0:T(8,128)(2,1)S(1)}, bf16[8,64,384]{2,1,0:T(8,128)(2,1)S(1)}, u32[]{:S(2)}, u32[]{:S(2)}) collective-permute-start(bf16[8,64,384]{2,1,0:T(8,128)(2,1)S(1)} %collective-permute-done.3.refs_0_), channel_id=1, source_target_pairs={{0,1},{1,0},{2,3},{3,2},{4,5},{5,4},{6,7},{7,6},{8,9},{9,8},{10,11... | collective-permute-start | bytes 1179656 | tf_op jit(solution)/shard_map/ppermute | solution.py:320
  26.5 11.5 %collective-permute-start.10 = (bf16[8,64,384]{2,1,0:T(8,128)(2,1)S(1)}, bf16[8,64,384]{2,1,0:T(8,128)(2,1)S(1)}, u32[]{:S(2)}, u32[]{:S(2)}) collective-permute-start(bf16[8,64,384]{2,1,0:T(8,128)(2,1)S(1)} %collective-permute-done.3.refs_0_), channel_id=1, source_target_pairs={{0,2},{1,3},{2,0},{3,1},{4,6},{5,7},{6,4},{7,5},{8,10},{9,11},{10,... | collective-permute-start | bytes 1179656 | tf_op jit(solution)/shard_map/ppermute | solution.py:320
  27.6 11.8 %collective-permute-start.11 = (bf16[8,64,384]{2,1,0:T(8,128)(2,1)S(1)}, bf16[8,64,384]{2,1,0:T(8,128)(2,1)S(1)}, u32[]{:S(2)}, u32[]{:S(2)}) collective-permute-start(bf16[8,64,384]{2,1,0:T(8,128)(2,1)S(1)} %collective-permute-done.7.refs_1_), channel_id=1, source_target_pairs={{0,1},{1,0},{2,3},{3,2},{4,5},{5,4},{6,7},{7,6},{8,9},{9,8},{10,11... | collective-permute-start | bytes 1179656 | tf_op jit(solution)/shard_map/ppermute | solution.py:320
  38.0 1.7 %collective-permute-start.13 = (bf16[8,64,384]{2,1,0:T(8,128)(2,1)S(1)}, bf16[8,64,384]{2,1,0:T(8,128)(2,1)S(1)}, u32[]{:S(2)}, u32[]{:S(2)}) collective-permute-start(bf16[8,64,384]{2,1,0:T(8,128)(2,1)S(1)} %collective-permute-done.10.refs_1_), channel_id=1, source_target_pairs={{0,1},{1,0},{2,3},{3,2},{4,5},{5,4},{6,7},{7,6},{8,9},{9,8},{10,11... | collective-permute-start | bytes 1179656 | tf_op jit(solution)/shard_map/ppermute | solution.py:320
  38.0 2.3 %collective-permute-start.12 = (bf16[8,64,384]{2,1,0:T(8,128)(2,1)S(1)}, bf16[8,64,384]{2,1,0:T(8,128)(2,1)S(1)}, u32[]{:S(2)}, u32[]{:S(2)}) collective-permute-start(bf16[8,64,384]{2,1,0:T(8,128)(2,1)S(1)} %collective-permute-done.6.refs_0_), channel_id=1, source_target_pairs={{0,1},{1,0},{2,3},{3,2},{4,5},{5,4},{6,7},{7,6},{8,9},{9,8},{10,11... | collective-permute-start | bytes 1179656 | tf_op jit(solution)/shard_map/ppermute | solution.py:320
  38.5 11.0 %collective-permute-start.9 = (bf16[8,64,384]{2,1,0:T(8,128)(2,1)S(1)}, bf16[8,64,384]{2,1,0:T(8,128)(2,1)S(1)}, u32[]{:S(2)}, u32[]{:S(2)}) collective-permute-start(bf16[8,64,384]{2,1,0:T(8,128)(2,1)S(1)} %collective-permute-done.6.refs_0_), channel_id=1, source_target_pairs={{0,2},{1,3},{2,0},{3,1},{4,6},{5,7},{6,4},{7,5},{8,10},{9,11},{10,... | collective-permute-start | bytes 1179656 | tf_op jit(solution)/shard_map/ppermute | solution.py:320
  49.5 1.7 %collective-permute-start.14 = (bf16[8,64,384]{2,1,0:T(8,128)(2,1)S(1)}, bf16[8,64,384]{2,1,0:T(8,128)(2,1)S(1)}, u32[]{:S(2)}, u32[]{:S(2)}) collective-permute-start(bf16[8,64,384]{2,1,0:T(8,128)(2,1)S(1)} %collective-permute-done.9.refs_0_), channel_id=1, source_target_pairs={{0,1},{1,0},{2,3},{3,2},{4,5},{5,4},{6,7},{7,6},{8,9},{9,8},{10,11... | collective-permute-start | bytes 1179656 | tf_op jit(solution)/shard_map/ppermute | solution.py:320
  54.8 3.1 %collective-permute-start.17 = (f32[2,8,128]{2,1,0:T(8,128)S(1)}, f32[2,8,128]{2,1,0:T(8,128)S(1)}, u32[]{:S(2)}, u32[]{:S(2)}) collective-permute-start(f32[2,8,128]{2,1,0:T(8,128)S(1)} %get-tuple-element.77), channel_id=1, source_target_pairs={{0,3},{1,2},{2,1},{3,0},{4,7},{5,6},{6,5},{7,4},{8,11},{9,10},{10,... | collective-permute-start | bytes 24584 | tf_op jit(solution)/shard_map/ppermute | solution.py:320
  54.9 3.7 %collective-permute-start.16 = (f32[2,8,128]{2,1,0:T(8,128)S(1)}, f32[2,8,128]{2,1,0:T(8,128)S(1)}, u32[]{:S(2)}, u32[]{:S(2)}) collective-permute-start(f32[2,8,128]{2,1,0:T(8,128)S(1)} %get-tuple-element.77), channel_id=1, source_target_pairs={{0,2},{1,3},{2,0},{3,1},{4,6},{5,7},{6,4},{7,5},{8,10},{9,11},{10,... | collective-permute-start | bytes 24584 | tf_op jit(solution)/shard_map/ppermute | solution.py:320
  55.5 3.1 %collective-permute-start.15 = (f32[2,8,128]{2,1,0:T(8,128)S(1)}, f32[2,8,128]{2,1,0:T(8,128)S(1)}, u32[]{:S(2)}, u32[]{:S(2)}) collective-permute-start(f32[2,8,128]{2,1,0:T(8,128)S(1)} %get-tuple-element.77), channel_id=1, source_target_pairs={{0,1},{1,0},{2,3},{3,2},{4,5},{5,4},{6,7},{7,6},{8,9},{9,8},{10,11... | collective-permute-start | bytes 24584 | tf_op jit(solution)/shard_map/ppermute | solution.py:320
  58.6 5.5 %collective-permute-start.20 = (f32[2,8,128]{2,1,0:T(8,128)S(1)}, f32[2,8,128]{2,1,0:T(8,128)S(1)}, u32[]{:S(2)}, u32[]{:S(2)}) collective-permute-start(f32[2,8,128]{2,1,0:T(8,128)S(1)} %add_add_fusion), channel_id=1, source_target_pairs={{0,12},{1,13},{2,14},{3,15},{4,8},{5,9},{6,10},{7,11},{8,4},{9,5},... | collective-permute-start | bytes 24584 | tf_op jit(solution)/shard_map/ppermute | solution.py:320
  61.5 4.5 %collective-permute-start.19 = (f32[2,8,128]{2,1,0:T(8,128)S(1)}, f32[2,8,128]{2,1,0:T(8,128)S(1)}, u32[]{:S(2)}, u32[]{:S(2)}) collective-permute-start(f32[2,8,128]{2,1,0:T(8,128)S(1)} %add_add_fusion), channel_id=1, source_target_pairs={{0,8},{1,9},{2,10},{3,11},{4,12},{5,13},{6,14},{7,15},{8,0},{9,1},... | collective-permute-start | bytes 24584 | tf_op jit(solution)/shard_map/ppermute | solution.py:320
  64.1 3.7 %collective-permute-start.18 = (f32[2,8,128]{2,1,0:T(8,128)S(1)}, f32[2,8,128]{2,1,0:T(8,128)S(1)}, u32[]{:S(2)}, u32[]{:S(2)}) collective-permute-start(f32[2,8,128]{2,1,0:T(8,128)S(1)} %add_add_fusion), channel_id=1, source_target_pairs={{0,4},{1,5},{2,6},{3,7},{4,0},{5,1},{6,2},{7,3},{8,12},{9,13},{10,... | collective-permute-start | bytes 24584 | tf_op jit(solution)/shard_map/ppermute | solution.py:320

commit v12 on v11

--- a/solution.py
+++ b/solution.py
@@ -2,6 +2,7 @@
 
 import jax
 import jax.numpy as jnp
+import numpy as np
 from jax import lax
 from jax.experimental import pallas as pl
 from jax.experimental.pallas import tpu as pltpu
@@ -21,6 +22,12 @@
 
 def ring_position(place, depth):
     return jnp.where(place <= depth // 2, jnp.maximum(2 * place - 1, 0), 2 * (depth - place))
+
+
+def call_of(depth, lag, other_y, other_core):
+    if other_y:
+        return min(lag + other_core, depth - 1)
+    return lag if other_core else max(lag - 1, 0)
 
 
 def prepare_kernel(
@@ -31,7 +38,8 @@
 ):
     own_tiles = irrep_ref.shape[0]
     irreps = counts_ref.shape[0]
-    most = item_ref.shape[0] // depth
+    calls = end_ref.shape[0]
+    most = item_ref.shape[0] // calls
     blank_ref[...] = jnp.zeros(blank_ref.shape, blank_ref.dtype)
     group = blank_ref.shape[0]
     for l in range(0, own_tiles, group):
@@ -67,16 +75,13 @@
 
     me = me_ref[0]
     z, y, core = me // 4, me // 2 % 2, me % 2
-    for shard in range(4 * depth):
-        lag = lax.rem(ring_place(z, depth) - ring_place(jnp.int32(shard // 4), depth) + depth, depth)
-        same_core = core == shard % 2
-        own_y = jnp.where(same_core, jnp.maximum(lag - 1, 0), jnp.minimum(lag, depth - 2))
-        other_y = jnp.where(
-            same_core | (lag == depth - 1), lag, jnp.minimum(lag + 1, depth - 2)
-        )
-        call_ref[shard] = jnp.where(y == shard // 2 % 2, own_y, other_y)
-
-    for call in range(depth):
+    for lag in range(depth):
+        at = ring_position(lax.rem(ring_place(z, depth) - lag + depth, depth), depth)
+        for other_y, other_core in np.ndindex(2, 2):
+            shard = (at * 2 + (1 - y if other_y else y)) * 2 + (1 - core if other_core else core)
+            call_ref[shard] = call_of(depth, lag, other_y, other_core)
+
+    for call in range(calls):
         end_ref[call] = call * most
 
     def symmetry(s, first):
@@ -101,7 +106,7 @@
         return stop
 
     lax.fori_loop(0, irreps, symmetry, jnp.int32(0))
-    for call in range(depth):
+    for call in range(calls):
         end = end_ref[call]
         for spare in range(UNROLL - 1):
             item_ref[end + spare] = own_tiles
@@ -170,20 +175,20 @@
     res_hbm, gathered_ref, stats_ref, o_buf, acc_ref, a_sem, o_sem = refs
     rows, width = v_ref.shape[1:]
     side = BATCH * rows
-    most = item_ref.shape[0] // depth
+    most = item_ref.shape[0] // end_ref.shape[0]
 
     me = me_ref[0]
     z, y, core = me // 4, me // 2 % 2, me % 2
     arrivals = []
-    for source, (lag, other_y, other_core) in zip(fresh, layout):
+    for source, (lag, other_y, other_core, tile) in zip(fresh, layout):
         at = ring_position(lax.rem(ring_place(z, depth) - lag + depth, depth), depth)
         own_y = (1 - y) if other_y else y
         own_core = (1 - core) if other_core else core
         arrivals.append(pltpu.make_async_copy(
             source,
-            gathered_ref.at[
-                pl.ds(((at * 2 + own_y) * 2 + own_core) * shard_tiles, shard_tiles)
-            ],
+            gathered_ref.at[pl.ds(
+                ((at * 2 + own_y) * 2 + own_core) * shard_tiles + tile, source.shape[0]
+            )],
             a_sem.at[len(arrivals)],
         ))
     for arrival in arrivals:
@@ -308,13 +313,13 @@
     depth = devices // 4
     me = lax.axis_index("vir").astype(jnp.int32).reshape(1)
     ring = ring_of(depth)
-    hop = []
-    for d in range(devices):
-        following = ring[(ring.index(d // 4) + 1) % depth]
-        hop.append((d, following * 4 + d % 4))
-
-    def shift_z(x):
-        return lax.ppermute(x, "vir", hop)
+
+    def shift_z(x, by):
+        pairs = []
+        for d in range(devices):
+            target = ring[(ring.index(d // 4) + by) % depth]
+            pairs.append((d, target * 4 + d % 4))
+        return lax.ppermute(x, "vir", pairs)
 
     def swap(x, bits):
         return lax.ppermute(x, "vir", [(d, d ^ bits) for d in range(devices)])
@@ -327,28 +332,33 @@
 
     a, b, c, d = [amplitudes], [], [], []
     for k in range(depth):
-        if k:
+        if 0 < k < depth - 1:
             c[-1], a[k], state = lax.optimization_barrier((c[-1], a[k], state))
-        b.append(swap(a[k], 2))
         if k < depth - 1:
-            a.append(shift_z(a[k]))
+            b.append(swap(a[k], 2))
+            a.append(shift_z(a[k], 1))
+        else:
+            part = 3 * shard_tiles // 8
+            c[-1], a[k], back, state = lax.optimization_barrier(
+                (c[-1], a[k], b[0][part:], state)
+            )
+            last = {part: shift_z(back, -1), 0: swap(a[k][:part], 2)}
         c.append(swap(a[k], 1))
         if k == 0:
             continue
-        d.append(swap(b[k - 1], 1))
-        arrived = {(k, 0, 0): a[k], (k - 1, 1, 0): b[k - 1], (k - 1, 0, 1): c[k - 1]}
+        fresh = {(k, 0, 0, 0): a[k], (k - 1, 0, 1, 0): c[k - 1], (k - 1, 1, 0, 0): b[k - 1]}
         if k == 1:
-            arrived[0, 0, 0] = a[0]
+            fresh[0, 0, 0, 0] = a[0]
         else:
-            arrived[k - 2, 1, 1] = d[k - 2]
-        if k == depth - 1:
-            arrived[k, 0, 1], arrived[k - 1, 1, 1] = c[k], d[k - 1]
-        state = ladder(k - 1, depth, shard_tiles, integrals, listing, state, arrived)
-    last, state = lax.optimization_barrier((b[-1], state))
-    residual, _, stats = ladder(
-        depth - 1, depth, shard_tiles, integrals, listing, state,
-        {(depth - 1, 1, 0): last, (depth - 1, 1, 1): swap(last, 1)},
-    )
+            fresh[k - 2, 1, 1, 0] = d[k - 2]
+        if k < depth - 1:
+            d.append(swap(b[k - 1], 1))
+        state = ladder(k - 1, depth, shard_tiles, integrals, listing, state, fresh)
+    b[-1], last, state = lax.optimization_barrier((b[-1], last, state))
+    fresh = {(k, 0, 1, 0): c[k], (k - 1, 1, 1, 0): swap(b[k - 1], 1)}
+    for tile, piece in last.items():
+        fresh[k, 1, 0, tile], fresh[k, 1, 1, tile] = piece, swap(piece, 1)
+    residual, _, stats = ladder(k, depth, shard_tiles, integrals, listing, state, fresh)
 
     stats = sum([swap(stats, bits) for bits in (1, 2, 3)], stats)
     stats = sum([swap(stats, 4 * bits) for bits in range(1, depth)], stats)

time: 68.6 us -> 69.8 us (1.017)
  starting transfers between devices: 18.4 us -> 22.6 us
  waiting for transfers between devices: 23.2 us -> 20.9 us
  Pallas kernels: 21.1 us -> 20 us
    ppermute x18 -> x19, waiting for transfers between devices: 14.2 us -> 7.16 us  [swap(): return lax.ppermute(x, 'vir', [(d, d ^ bits) for d in range(devices)])]
    ppermute x3 -> x4, waiting for transfers between devices: 8.98 us -> 13.8 us  [shift_z(): return lax.ppermute(x, 'vir', pairs)]
    ppermute x18 -> x19, starting transfers between devices: 13.1 us -> 16.6 us  [swap(): return lax.ppermute(x, 'vir', [(d, d ^ bits) for d in range(devices)])]
    pallas_call x4, Pallas kernels: 16.5 us -> 15.4 us  [ladder(): pl.pallas_call(functools.partial(ladder_kernel, call, depth, shard_tiles,...]
    ppermute x3 -> x4, starting transfers between devices: 5.23 us -> 6 us  [shift_z(): return lax.ppermute(x, 'vir', pairs)]
  transfers between devices with their start and end apart: 21 -> 23, of which waited for: 12 -> 7; matrix products, arithmetic and copies ran while one was open for 0% -> 0% of each run, Pallas kernels for 26% -> 23%
where the time goes in v12:
time: 69.8 us; the launch traced here: 69.3 us
  starting transfers between devices  22.6 us (32%)
  waiting for transfers between devices  20.9 us (30%)
  Pallas kernels  20 us (29%)
  local copies, waits for them, and re-layouts  4.41 us (6%)
  between operations  0.77 us (1%)
    ppermute x19, starting transfers between devices, swap(): return lax.ppermute(x, 'vir', [(d, d ^ bits) for d in range(devices)])  16.6 us
    pallas_call x4, Pallas kernels, ladder(): pl.pallas_call(functools.partial(ladder_kernel, call, depth, shard_tiles,...  15.4 us
    ppermute x4, waiting for transfers between devices, shift_z(): return lax.ppermute(x, 'vir', pairs)  13.8 us
    ppermute x19, waiting for transfers between devices, swap(): return lax.ppermute(x, 'vir', [(d, d ^ bits) for d in range(devices)])  7.16 us
    ppermute x4, starting transfers between devices, shift_z(): return lax.ppermute(x, 'vir', pairs)  6 us
    pallas_call x1, Pallas kernels, prepare(): pl.pallas_call(functools.partial(prepare_kernel, depth, shard_tiles), out...  4.57 us
    unnamed x12, local copies, waits for them, and re-layouts  4.37 us
  transfers between devices with their start and end apart: 23, of which 7 were waited for; matrix products, arithmetic and copies ran while one was open for 0% of the time, Pallas kernels for 23%

profile of v12, /device:TPU:0, one launch (start us, length us, event | category | flops | bytes accessed | tf_op | source)
XLA Modules:
  0.0 69.3 jit_solution(16177714544657490116)
XLA Ops:
  0.6 0.5 collective-permute-start
  1.1 2.6 %collective-permute-start.1 = (bf16[8,64,384]{2,1,0:T(8,128)(2,1)}, bf16[8,64,384]{2,1,0:T(8,128)(2,1)S(1)}, u32[]{:S(2)}, u32[]{:S(2)}) collective-permute-start(bf16[8,64,384]{2,1,0:T(8,128)(2,1)} %refs_3_.1), channel_id=1, source_target_pairs={{0,4},{1,5},{2,6},{3,7},{4,12},{5,13},{6,14},{7,15},{8,0},{9,1},{1... | collective-permute-start | bytes 1179656 | tf_op jit(solution)/shard_map/ppermute | solution.py:322
  3.8 1.5 %collective-permute-start.4 = (bf16[8,64,384]{2,1,0:T(8,128)(2,1)}, bf16[8,64,384]{2,1,0:T(8,128)(2,1)S(1)}, u32[]{:S(2)}, u32[]{:S(2)}) collective-permute-start(bf16[8,64,384]{2,1,0:T(8,128)(2,1)} %refs_3_.1), channel_id=1, source_target_pairs={{0,2},{1,3},{2,0},{3,1},{4,6},{5,7},{6,4},{7,5},{8,10},{9,11},{10,... | collective-permute-start | bytes 1179656 | tf_op jit(solution)/shard_map/ppermute | solution.py:325
  5.3 0.7 copy-done.3
  6.0 0.7 copy-done.5
  6.6 4.6 %prepare.1 = (bf16[32,64,2048]{2,1,0:T(8,128)(2,1)}, bf16[132,64,384]{2,1,0:T(8,128)(2,1)S(1)}, f32[2,8,128]{2,1,0:T(8,128)S(1)}, s32[36]{0:T(128)S(1)}, s32[8]{...) custom-call(s32[1]{0:T(128)} %bitcast.me_ref, s32[8]{0:T(128)S(1)} %copy-done.3, s32[32]{0:T(128)S(1)} %copy-done.5), custom_call_target="tpu_custom_call" | custom-call | bytes 8388608 | tf_op jit(solution)/shard_map/prepare/pallas_call | solution.py:138
  11.2 0.0 collective-permute-done.refs_1_
  11.2 3.5 %collective-permute-done.1.refs_0_ = bf16[8,64,384]{2,1,0:T(8,128)(2,1)S(1)} collective-permute-done((bf16[8,64,384]{2,1,0:T(8,128)(2,1)}, bf16[8,64,384]{2,1,0:T(8,128)(2,1)S(1)}, u32[]{:S(2)}, u32[]{:S(2)}) %collective-permute-start.1) | collective-permute-done | bytes 393248 | tf_op jit(solution)/shard_map/ppermute | solution.py:322
  14.7 0.0 collective-permute-start.2
  14.7 0.9 %collective-permute-start.3 = (bf16[8,64,384]{2,1,0:T(8,128)(2,1)S(1)}, bf16[8,64,384]{2,1,0:T(8,128)(2,1)S(1)}, u32[]{:S(2)}, u32[]{:S(2)}) collective-permute-start(bf16[8,64,384]{2,1,0:T(8,128)(2,1)S(1)} %collective-permute-done.1.refs_0_), channel_id=1, source_target_pairs={{0,4},{1,5},{2,6},{3,7},{4,12},{5,13},{6,14},{7,15},{8,0},{9,1},{1... | collective-permute-start | bytes 1179656 | tf_op jit(solution)/shard_map/ppermute | solution.py:322
  15.7 1.5 %collective-permute-start.8 = (bf16[8,64,384]{2,1,0:T(8,128)(2,1)S(1)}, bf16[8,64,384]{2,1,0:T(8,128)(2,1)S(1)}, u32[]{:S(2)}, u32[]{:S(2)}) collective-permute-start(bf16[8,64,384]{2,1,0:T(8,128)(2,1)S(1)} %collective-permute-done.1.refs_0_), channel_id=1, source_target_pairs={{0,2},{1,3},{2,0},{3,1},{4,6},{5,7},{6,4},{7,5},{8,10},{9,11},{10,... | collective-permute-start | bytes 1179656 | tf_op jit(solution)/shard_map/ppermute | solution.py:325
  17.2 0.0 collective-permute-done.4.refs_2_
  17.2 1.4 %copy-done = bf16[32,64,384]{2,1,0:T(8,128)(2,1)S(1)} copy-done((bf16[32,64,384]{2,1,0:T(8,128)(2,1)S(1)}, bf16[32,64,384]{2,1,0:T(8,128)(2,1)}, u32[]{:S(2)}) %copy-start) | copy-done | bytes 1572888
  18.6 1.0 %copy-done.2 = bf16[8,64,384]{2,1,0:T(8,128)(2,1)S(1)} copy-done((bf16[8,64,384]{2,1,0:T(8,128)(2,1)S(1)}, bf16[8,64,384]{2,1,0:T(8,128)(2,1)}, u32[]{:S(2)}) %copy-start.2) | copy-done | bytes 393240
  19.6 0.7 copy-done.4
  20.3 3.3 %ladder_0.1 = (bf16[32,64,2048]{2,1,0:T(8,128)(2,1)}, bf16[132,64,384]{2,1,0:T(8,128)(2,1)S(1)}, f32[2,8,128]{2,1,0:T(8,128)S(1)}) custom-call(s32[1]{0:T(128)} %bitcast.me_ref, s32[8]{0:T(128)S(1)} %copy-done.4, s32[36]{0:T(128)S(1)} %get-tuple-element.43.order_ref, ...), custom_call_target="tpu_custom_call", output_to_operand_aliasing={{0}: (9, {}), {1}: (10, {})} | custom-call | flops 402653184 | bytes 2097152 | tf_op jit(solution)/shard_map/ladder_0/pallas_call | solution.py:282
  23.5 3.6 %collective-permute-done.3.refs_0_ = bf16[8,64,384]{2,1,0:T(8,128)(2,1)S(1)} collective-permute-done((bf16[8,64,384]{2,1,0:T(8,128)(2,1)S(1)}, bf16[8,64,384]{2,1,0:T(8,128)(2,1)S(1)}, u32[]{:S(2)}, u32[]{:S(2)}) %collective-permute-start.3) | collective-permute-done | bytes 393248 | tf_op jit(solution)/shard_map/ppermute | solution.py:322
  27.2 0.0 collective-permute-start.6
  27.2 0.8 %collective-permute-start.7 = (bf16[8,64,384]{2,1,0:T(8,128)(2,1)S(1)}, bf16[8,64,384]{2,1,0:T(8,128)(2,1)S(1)}, u32[]{:S(2)}, u32[]{:S(2)}) collective-permute-start(bf16[8,64,384]{2,1,0:T(8,128)(2,1)S(1)} %collective-permute-done.3.refs_0_), channel_id=1, source_target_pairs={{0,4},{1,5},{2,6},{3,7},{4,12},{5,13},{6,14},{7,15},{8,0},{9,1},{1... | collective-permute-start | bytes 1179656 | tf_op jit(solution)/shard_map/ppermute | solution.py:322
  28.0 1.5 %collective-permute-start.5 = (bf16[8,64,384]{2,1,0:T(8,128)(2,1)S(1)}, bf16[8,64,384]{2,1,0:T(8,128)(2,1)S(1)}, u32[]{:S(2)}, u32[]{:S(2)}) collective-permute-start(bf16[8,64,384]{2,1,0:T(8,128)(2,1)S(1)} %collective-permute-done.3.refs_0_), channel_id=1, source_target_pairs={{0,2},{1,3},{2,0},{3,1},{4,6},{5,7},{6,4},{7,5},{8,10},{9,11},{10,... | collective-permute-start | bytes 1179656 | tf_op jit(solution)/shard_map/ppermute | solution.py:325
  29.5 0.0 collective-permute-start.12
  29.6 0.0 collective-permute-done.9.refs_3_
  29.6 3.4 %ladder_1.1 = (bf16[32,64,2048]{2,1,0:T(8,128)(2,1)}, bf16[132,64,384]{2,1,0:T(8,128)(2,1)S(1)}, f32[2,8,128]{2,1,0:T(8,128)S(1)}) custom-call(s32[1]{0:T(128)} %bitcast.me_ref, s32[8]{0:T(128)S(1)} %copy-done.4, s32[36]{0:T(128)S(1)} %get-tuple-element.43.order_ref, ...), custom_call_target="tpu_custom_call", output_to_operand_aliasing={{0}: (9, {}), {1}: (10, {})} | custom-call | flops 402653184 | bytes 2097152 | tf_op jit(solution)/shard_map/ladder_1/pallas_call | solution.py:282
  33.0 0.0 collective-permute-done.6.refs_1_
  33.0 6.6 %collective-permute-done.7.refs_0_ = bf16[8,64,384]{2,1,0:T(8,128)(2,1)S(1)} collective-permute-done((bf16[8,64,384]{2,1,0:T(8,128)(2,1)S(1)}, bf16[8,64,384]{2,1,0:T(8,128)(2,1)S(1)}, u32[]{:S(2)}, u32[]{:S(2)}) %collective-permute-start.7) | collective-permute-done | bytes 393248 | tf_op jit(solution)/shard_map/ppermute | solution.py:322
  39.6 1.6 %collective-permute-start.11 = (bf16[5,64,384]{2,1,0:T(8,128)(2,1)S(1)}, bf16[5,64,384]{2,1,0:T(8,128)(2,1)S(1)}, u32[]{:S(2)}, u32[]{:S(2)}) collective-permute-start(bf16[5,64,384]{2,1,0:T(8,128)(2,1)S(1)} %slice.8), channel_id=1, source_target_pairs={{0,8},{1,9},{2,10},{3,11},{4,0},{5,1},{6,2},{7,3},{8,12},{9,13},{1... | collective-permute-start | bytes 737288 | tf_op jit(solution)/shard_map/ppermute | solution.py:322
  41.2 1.6 %collective-permute-start.10 = (bf16[3,64,384]{2,1,0:T(8,128)(2,1)S(1)}, bf16[3,64,384]{2,1,0:T(8,128)(2,1)S(1)}, u32[]{:S(2)}, u32[]{:S(2)}) collective-permute-start(bf16[3,64,384]{2,1,0:T(8,128)(2,1)S(1)} %slice.7), channel_id=1, source_target_pairs={{0,2},{1,3},{2,0},{3,1},{4,6},{5,7},{6,4},{7,5},{8,10},{9,11},{10,... | collective-permute-start | bytes 442376 | tf_op jit(solution)/shard_map/ppermute | solution.py:325
  42.8 4.7 %ladder_2.1 = (bf16[32,64,2048]{2,1,0:T(8,128)(2,1)}, bf16[132,64,384]{2,1,0:T(8,128)(2,1)S(1)}, f32[2,8,128]{2,1,0:T(8,128)S(1)}) custom-call(s32[1]{0:T(128)} %bitcast.me_ref, s32[8]{0:T(128)S(1)} %copy-done.4, s32[36]{0:T(128)S(1)} %get-tuple-element.43.order_ref, ...), custom_call_target="tpu_custom_call", output_to_operand_aliasing={{0}: (9, {}), {1}: (10, {})} | custom-call | flops 402653184 | bytes 2097152 | tf_op jit(solution)/shard_map/ladder_2/pallas_call | solution.py:282
  47.5 0.0 collective-permute-done.10.refs_2_
  47.5 0.6 collective-permute-start.14
  48.1 0.1 collective-permute-start.16
  48.2 0.4 collective-permute-start.15
  48.6 1.4 %collective-permute-done.15.refs_3_ = bf16[3,64,384]{2,1,0:T(8,128)(2,1)S(1)} collective-permute-done((bf16[3,64,384]{2,1,0:T(8,128)(2,1)S(1)}, bf16[3,64,384]{2,1,0:T(8,128)(2,1)S(1)}, u32[]{:S(2)}, u32[]{:S(2)}) %collective-permute-start.15) | collective-permute-done | bytes 147488 | tf_op jit(solution)/shard_map/ppermute | solution.py:325
  50.0 0.0 collective-permute-done.13.refs_0_
  50.0 4.1 %ladder_3.1 = (bf16[32,64,2048]{2,1,0:T(8,128)(2,1)}, bf16[132,64,384]{2,1,0:T(8,128)(2,1)S(1)}, f32[2,8,128]{2,1,0:T(8,128)S(1)}) custom-call(s32[1]{0:T(128)} %bitcast.me_ref, s32[8]{0:T(128)S(1)} %copy-done.4, s32[36]{0:T(128)S(1)} %get-tuple-element.43.order_ref, ...), custom_call_target="tpu_custom_call", output_to_operand_aliasing={{0}: (9, {}), {1}: (10, {})} | custom-call | flops 402653184 | bytes 2097152 | tf_op jit(solution)/shard_map/ladder_3/pallas_call | solution.py:282
  54.1 2.9 %collective-permute-start.17 = (f32[2,8,128]{2,1,0:T(8,128)S(1)}, f32[2,8,128]{2,1,0:T(8,128)S(1)}, u32[]{:S(2)}, u32[]{:S(2)}) collective-permute-start(f32[2,8,128]{2,1,0:T(8,128)S(1)} %get-tuple-element.83), channel_id=1, source_target_pairs={{0,1},{1,0},{2,3},{3,2},{4,5},{5,4},{6,7},{7,6},{8,9},{9,8},{10,11... | collective-permute-start | bytes 24584 | tf_op jit(solution)/shard_map/ppermute | solution.py:325
  57.1 0.1 collective-permute-start.18
  57.1 1.4 %collective-permute-start.19 = (f32[2,8,128]{2,1,0:T(8,128)S(1)}, f32[2,8,128]{2,1,0:T(8,128)S(1)}, u32[]{:S(2)}, u32[]{:S(2)}) collective-permute-start(f32[2,8,128]{2,1,0:T(8,128)S(1)} %get-tuple-element.83), channel_id=1, source_target_pairs={{0,3},{1,2},{2,1},{3,0},{4,7},{5,6},{6,5},{7,4},{8,11},{9,10},{10,... | collective-permute-start | bytes 24584 | tf_op jit(solution)/shard_map/ppermute | solution.py:325
  58.5 2.2 %collective-permute-done.18 = f32[2,8,128]{2,1,0:T(8,128)S(1)} collective-permute-done((f32[2,8,128]{2,1,0:T(8,128)S(1)}, f32[2,8,128]{2,1,0:T(8,128)S(1)}, u32[]{:S(2)}, u32[]{:S(2)}) %collective-permute-start.18) | collective-permute-done | bytes 8224 | tf_op jit(solution)/shard_map/ppermute | solution.py:325
  60.7 0.0 collective-permute-done.19
  60.7 2.1 %collective-permute-start.20 = (f32[2,8,128]{2,1,0:T(8,128)S(1)}, f32[2,8,128]{2,1,0:T(8,128)S(1)}, u32[]{:S(2)}, u32[]{:S(2)}) collective-permute-start(f32[2,8,128]{2,1,0:T(8,128)S(1)} %add_add_fusion), channel_id=1, source_target_pairs={{0,4},{1,5},{2,6},{3,7},{4,0},{5,1},{6,2},{7,3},{8,12},{9,13},{10,... | collective-permute-start | bytes 24584 | tf_op jit(solution)/shard_map/ppermute | solution.py:325
  62.8 0.5 collective-permute-start.21
  63.3 1.9 %collective-permute-start.22 = (f32[2,8,128]{2,1,0:T(8,128)S(1)}, f32[2,8,128]{2,1,0:T(8,128)S(1)}, u32[]{:S(2)}, u32[]{:S(2)}) collective-permute-start(f32[2,8,128]{2,1,0:T(8,128)S(1)} %add_add_fusion), channel_id=1, source_target_pairs={{0,12},{1,13},{2,14},{3,15},{4,8},{5,9},{6,10},{7,11},{8,4},{9,5},... | collective-permute-start | bytes 24584 | tf_op jit(solution)/shard_map/ppermute | solution.py:325
  65.2 0.0 collective-permute-done.20
  65.2 2.1 %collective-permute-done.21 = f32[2,8,128]{2,1,0:T(8,128)S(1)} collective-permute-done((f32[2,8,128]{2,1,0:T(8,128)S(1)}, f32[2,8,128]{2,1,0:T(8,128)S(1)}, u32[]{:S(2)}, u32[]{:S(2)}) %collective-permute-start.21) | collective-permute-done | bytes 8224 | tf_op jit(solution)/shard_map/ppermute | solution.py:325
  67.3 1.4 %collective-permute-done.22 = f32[2,8,128]{2,1,0:T(8,128)S(1)} collective-permute-done((f32[2,8,128]{2,1,0:T(8,128)S(1)}, f32[2,8,128]{2,1,0:T(8,128)S(1)}, u32[]{:S(2)}, u32[]{:S(2)}) %collective-permute-start.22) | collective-permute-done | bytes 8224 | tf_op jit(solution)/shard_map/ppermute | solution.py:325
  68.7 0.1 add_reduce_fusion
  68.8 0.5 add_sqrt_fusion
  (20 shorter events, 0.1 us)
Async XLA Ops:
  0.6 10.6 %collective-permute-start = (bf16[8,64,384]{2,1,0:T(8,128)(2,1)}, bf16[8,64,384]{2,1,0:T(8,128)(2,1)S(1)}, u32[]{:S(2)}, u32[]{:S(2)}) collective-permute-start(bf16[8,64,384]{2,1,0:T(8,128)(2,1)} %refs_3_.1), channel_id=1, source_target_pairs={{0,1},{1,0},{2,3},{3,2},{4,5},{5,4},{6,7},{7,6},{8,9},{9,8},{10,11... | collective-permute-start | bytes 1179656 | tf_op jit(solution)/shard_map/ppermute | solution.py:325
  1.1 13.6 %collective-permute-start.1 = (bf16[8,64,384]{2,1,0:T(8,128)(2,1)}, bf16[8,64,384]{2,1,0:T(8,128)(2,1)S(1)}, u32[]{:S(2)}, u32[]{:S(2)}) collective-permute-start(bf16[8,64,384]{2,1,0:T(8,128)(2,1)} %refs_3_.1), channel_id=1, source_target_pairs={{0,4},{1,5},{2,6},{3,7},{4,12},{5,13},{6,14},{7,15},{8,0},{9,1},{1... | collective-permute-start | bytes 1179656 | tf_op jit(solution)/shard_map/ppermute | solution.py:322
  3.8 13.4 %collective-permute-start.4 = (bf16[8,64,384]{2,1,0:T(8,128)(2,1)}, bf16[8,64,384]{2,1,0:T(8,128)(2,1)S(1)}, u32[]{:S(2)}, u32[]{:S(2)}) collective-permute-start(bf16[8,64,384]{2,1,0:T(8,128)(2,1)} %refs_3_.1), channel_id=1, source_target_pairs={{0,2},{1,3},{2,0},{3,1},{4,6},{5,7},{6,4},{7,5},{8,10},{9,11},{10,... | collective-permute-start | bytes 1179656 | tf_op jit(solution)/shard_map/ppermute | solution.py:325
  5.3 0.7 copy-start.3
  6.0 0.7 copy-start.5
  14.7 8.8 %collective-permute-start.2 = (bf16[8,64,384]{2,1,0:T(8,128)(2,1)S(1)}, bf16[8,64,384]{2,1,0:T(8,128)(2,1)S(1)}, u32[]{:S(2)}, u32[]{:S(2)}) collective-permute-start(bf16[8,64,384]{2,1,0:T(8,128)(2,1)S(1)} %collective-permute-done.1.refs_0_), channel_id=1, source_target_pairs={{0,1},{1,0},{2,3},{3,2},{4,5},{5,4},{6,7},{7,6},{8,9},{9,8},{10,11... | collective-permute-start | bytes 1179656 | tf_op jit(solution)/shard_map/ppermute | solution.py:325
  14.7 12.4 %collective-permute-start.3 = (bf16[8,64,384]{2,1,0:T(8,128)(2,1)S(1)}, bf16[8,64,384]{2,1,0:T(8,128)(2,1)S(1)}, u32[]{:S(2)}, u32[]{:S(2)}) collective-permute-start(bf16[8,64,384]{2,1,0:T(8,128)(2,1)S(1)} %collective-permute-done.1.refs_0_), channel_id=1, source_target_pairs={{0,4},{1,5},{2,6},{3,7},{4,12},{5,13},{6,14},{7,15},{8,0},{9,1},{1... | collective-permute-start | bytes 1179656 | tf_op jit(solution)/shard_map/ppermute | solution.py:322
  15.7 13.8 %collective-permute-start.8 = (bf16[8,64,384]{2,1,0:T(8,128)(2,1)S(1)}, bf16[8,64,384]{2,1,0:T(8,128)(2,1)S(1)}, u32[]{:S(2)}, u32[]{:S(2)}) collective-permute-start(bf16[8,64,384]{2,1,0:T(8,128)(2,1)S(1)} %collective-permute-done.1.refs_0_), channel_id=1, source_target_pairs={{0,2},{1,3},{2,0},{3,1},{4,6},{5,7},{6,4},{7,5},{8,10},{9,11},{10,... | collective-permute-start | bytes 1179656 | tf_op jit(solution)/shard_map/ppermute | solution.py:325
  17.2 12.4 %collective-permute-start.9 = (bf16[8,64,384]{2,1,0:T(8,128)(2,1)S(1)}, bf16[8,64,384]{2,1,0:T(8,128)(2,1)S(1)}, u32[]{:S(2)}, u32[]{:S(2)}) collective-permute-start(bf16[8,64,384]{2,1,0:T(8,128)(2,1)S(1)} %collective-permute-done.4.refs_2_), channel_id=1, source_target_pairs={{0,1},{1,0},{2,3},{3,2},{4,5},{5,4},{6,7},{7,6},{8,9},{9,8},{10,11... | collective-permute-start | bytes 1179656 | tf_op jit(solution)/shard_map/ppermute | solution.py:325
  17.2 1.4 %copy-start = (bf16[32,64,384]{2,1,0:T(8,128)(2,1)S(1)}, bf16[32,64,384]{2,1,0:T(8,128)(2,1)}, u32[]{:S(2)}) copy-start(bf16[32,64,384]{2,1,0:T(8,128)(2,1)} %v_ref.7) | copy-start | bytes 4718596
  18.6 1.0 %copy-start.2 = (bf16[8,64,384]{2,1,0:T(8,128)(2,1)S(1)}, bf16[8,64,384]{2,1,0:T(8,128)(2,1)}, u32[]{:S(2)}) copy-start(bf16[8,64,384]{2,1,0:T(8,128)(2,1)} %refs_3_.1) | copy-start | bytes 1179652
  19.6 0.7 copy-start.4
  20.3 9.3 %copy-start.1 = (bf16[32,64,384]{2,1,0:T(8,128)(2,1)S(1)}, bf16[32,64,384]{2,1,0:T(8,128)(2,1)}, u32[]{:S(2)}) copy-start(bf16[32,64,384]{2,1,0:T(8,128)(2,1)} %v_ref.7) | copy-start | bytes 4718596
  27.2 5.8 %collective-permute-start.6 = (bf16[8,64,384]{2,1,0:T(8,128)(2,1)S(1)}, bf16[8,64,384]{2,1,0:T(8,128)(2,1)S(1)}, u32[]{:S(2)}, u32[]{:S(2)}) collective-permute-start(bf16[8,64,384]{2,1,0:T(8,128)(2,1)S(1)} %collective-permute-done.3.refs_0_), channel_id=1, source_target_pairs={{0,1},{1,0},{2,3},{3,2},{4,5},{5,4},{6,7},{7,6},{8,9},{9,8},{10,11... | collective-permute-start | bytes 1179656 | tf_op jit(solution)/shard_map/ppermute | solution.py:325
  27.2 12.4 %collective-permute-start.7 = (bf16[8,64,384]{2,1,0:T(8,128)(2,1)S(1)}, bf16[8,64,384]{2,1,0:T(8,128)(2,1)S(1)}, u32[]{:S(2)}, u32[]{:S(2)}) collective-permute-start(bf16[8,64,384]{2,1,0:T(8,128)(2,1)S(1)} %collective-permute-done.3.refs_0_), channel_id=1, source_target_pairs={{0,4},{1,5},{2,6},{3,7},{4,12},{5,13},{6,14},{7,15},{8,0},{9,1},{1... | collective-permute-start | bytes 1179656 | tf_op jit(solution)/shard_map/ppermute | solution.py:322
  28.0 14.8 %collective-permute-start.5 = (bf16[8,64,384]{2,1,0:T(8,128)(2,1)S(1)}, bf16[8,64,384]{2,1,0:T(8,128)(2,1)S(1)}, u32[]{:S(2)}, u32[]{:S(2)}) collective-permute-start(bf16[8,64,384]{2,1,0:T(8,128)(2,1)S(1)} %collective-permute-done.3.refs_0_), channel_id=1, source_target_pairs={{0,2},{1,3},{2,0},{3,1},{4,6},{5,7},{6,4},{7,5},{8,10},{9,11},{10,... | collective-permute-start | bytes 1179656 | tf_op jit(solution)/shard_map/ppermute | solution.py:325
  29.5 13.3 %collective-permute-start.12 = (bf16[8,64,384]{2,1,0:T(8,128)(2,1)S(1)}, bf16[8,64,384]{2,1,0:T(8,128)(2,1)S(1)}, u32[]{:S(2)}, u32[]{:S(2)}) collective-permute-start(bf16[8,64,384]{2,1,0:T(8,128)(2,1)S(1)} %collective-permute-done.8.refs_2_), channel_id=1, source_target_pairs={{0,1},{1,0},{2,3},{3,2},{4,5},{5,4},{6,7},{7,6},{8,9},{9,8},{10,11... | collective-permute-start | bytes 1179656 | tf_op jit(solution)/shard_map/ppermute | solution.py:325
  39.6 7.9 %collective-permute-start.11 = (bf16[5,64,384]{2,1,0:T(8,128)(2,1)S(1)}, bf16[5,64,384]{2,1,0:T(8,128)(2,1)S(1)}, u32[]{:S(2)}, u32[]{:S(2)}) collective-permute-start(bf16[5,64,384]{2,1,0:T(8,128)(2,1)S(1)} %slice.8), channel_id=1, source_target_pairs={{0,8},{1,9},{2,10},{3,11},{4,0},{5,1},{6,2},{7,3},{8,12},{9,13},{1... | collective-permute-start | bytes 737288 | tf_op jit(solution)/shard_map/ppermute | solution.py:322
  41.2 6.3 %collective-permute-start.10 = (bf16[3,64,384]{2,1,0:T(8,128)(2,1)S(1)}, bf16[3,64,384]{2,1,0:T(8,128)(2,1)S(1)}, u32[]{:S(2)}, u32[]{:S(2)}) collective-permute-start(bf16[3,64,384]{2,1,0:T(8,128)(2,1)S(1)} %slice.7), channel_id=1, source_target_pairs={{0,2},{1,3},{2,0},{3,1},{4,6},{5,7},{6,4},{7,5},{8,10},{9,11},{10,... | collective-permute-start | bytes 442376 | tf_op jit(solution)/shard_map/ppermute | solution.py:325
  42.8 7.2 %collective-permute-start.13 = (bf16[8,64,384]{2,1,0:T(8,128)(2,1)S(1)}, bf16[8,64,384]{2,1,0:T(8,128)(2,1)S(1)}, u32[]{:S(2)}, u32[]{:S(2)}) collective-permute-start(bf16[8,64,384]{2,1,0:T(8,128)(2,1)S(1)} %collective-permute-done.7.refs_0_), channel_id=1, source_target_pairs={{0,1},{1,0},{2,3},{3,2},{4,5},{5,4},{6,7},{7,6},{8,9},{9,8},{10,11... | collective-permute-start | bytes 1179656 | tf_op jit(solution)/shard_map/ppermute | solution.py:325
  47.5 2.5 %collective-permute-start.14 = (bf16[8,64,384]{2,1,0:T(8,128)(2,1)S(1)}, bf16[8,64,384]{2,1,0:T(8,128)(2,1)S(1)}, u32[]{:S(2)}, u32[]{:S(2)}) collective-permute-start(bf16[8,64,384]{2,1,0:T(8,128)(2,1)S(1)} %collective-permute-done.5.refs_2_), channel_id=1, source_target_pairs={{0,1},{1,0},{2,3},{3,2},{4,5},{5,4},{6,7},{7,6},{8,9},{9,8},{10,11... | collective-permute-start | bytes 1179656 | tf_op jit(solution)/shard_map/ppermute | solution.py:325
  48.1 1.9 %collective-permute-start.16 = (bf16[5,64,384]{2,1,0:T(8,128)(2,1)S(1)}, bf16[5,64,384]{2,1,0:T(8,128)(2,1)S(1)}, u32[]{:S(2)}, u32[]{:S(2)}) collective-permute-start(bf16[5,64,384]{2,1,0:T(8,128)(2,1)S(1)} %collective-permute-done.11.refs_4_), channel_id=1, source_target_pairs={{0,1},{1,0},{2,3},{3,2},{4,5},{5,4},{6,7},{7,6},{8,9},{9,8},{10,11... | collective-permute-start | bytes 737288 | tf_op jit(solution)/shard_map/ppermute | solution.py:325
  48.2 1.8 %collective-permute-start.15 = (bf16[3,64,384]{2,1,0:T(8,128)(2,1)S(1)}, bf16[3,64,384]{2,1,0:T(8,128)(2,1)S(1)}, u32[]{:S(2)}, u32[]{:S(2)}) collective-permute-start(bf16[3,64,384]{2,1,0:T(8,128)(2,1)S(1)} %collective-permute-done.10.refs_2_), channel_id=1, source_target_pairs={{0,1},{1,0},{2,3},{3,2},{4,5},{5,4},{6,7},{7,6},{8,9},{9,8},{10,11... | collective-permute-start | bytes 442376 | tf_op jit(solution)/shard_map/ppermute | solution.py:325
  54.1 4.4 %collective-permute-start.17 = (f32[2,8,128]{2,1,0:T(8,128)S(1)}, f32[2,8,128]{2,1,0:T(8,128)S(1)}, u32[]{:S(2)}, u32[]{:S(2)}) collective-permute-start(f32[2,8,128]{2,1,0:T(8,128)S(1)} %get-tuple-element.83), channel_id=1, source_target_pairs={{0,1},{1,0},{2,3},{3,2},{4,5},{5,4},{6,7},{7,6},{8,9},{9,8},{10,11... | collective-permute-start | bytes 24584 | tf_op jit(solution)/shard_map/ppermute | solution.py:325
  57.1 3.7 %collective-permute-start.18 = (f32[2,8,128]{2,1,0:T(8,128)S(1)}, f32[2,8,128]{2,1,0:T(8,128)S(1)}, u32[]{:S(2)}, u32[]{:S(2)}) collective-permute-start(f32[2,8,128]{2,1,0:T(8,128)S(1)} %get-tuple-element.83), channel_id=1, source_target_pairs={{0,2},{1,3},{2,0},{3,1},{4,6},{5,7},{6,4},{7,5},{8,10},{9,11},{10,... | collective-permute-start | bytes 24584 | tf_op jit(solution)/shard_map/ppermute | solution.py:325
  57.1 3.6 %collective-permute-start.19 = (f32[2,8,128]{2,1,0:T(8,128)S(1)}, f32[2,8,128]{2,1,0:T(8,128)S(1)}, u32[]{:S(2)}, u32[]{:S(2)}) collective-permute-start(f32[2,8,128]{2,1,0:T(8,128)S(1)} %get-tuple-element.83), channel_id=1, source_target_pairs={{0,3},{1,2},{2,1},{3,0},{4,7},{5,6},{6,5},{7,4},{8,11},{9,10},{10,... | collective-permute-start | bytes 24584 | tf_op jit(solution)/shard_map/ppermute | solution.py:325
  60.7 4.5 %collective-permute-start.20 = (f32[2,8,128]{2,1,0:T(8,128)S(1)}, f32[2,8,128]{2,1,0:T(8,128)S(1)}, u32[]{:S(2)}, u32[]{:S(2)}) collective-permute-start(f32[2,8,128]{2,1,0:T(8,128)S(1)} %add_add_fusion), channel_id=1, source_target_pairs={{0,4},{1,5},{2,6},{3,7},{4,0},{5,1},{6,2},{7,3},{8,12},{9,13},{10,... | collective-permute-start | bytes 24584 | tf_op jit(solution)/shard_map/ppermute | solution.py:325
  62.8 4.6 %collective-permute-start.21 = (f32[2,8,128]{2,1,0:T(8,128)S(1)}, f32[2,8,128]{2,1,0:T(8,128)S(1)}, u32[]{:S(2)}, u32[]{:S(2)}) collective-permute-start(f32[2,8,128]{2,1,0:T(8,128)S(1)} %add_add_fusion), channel_id=1, source_target_pairs={{0,8},{1,9},{2,10},{3,11},{4,12},{5,13},{6,14},{7,15},{8,0},{9,1},... | collective-permute-start | bytes 24584 | tf_op jit(solution)/shard_map/ppermute | solution.py:325
  63.3 5.4 %collective-permute-start.22 = (f32[2,8,128]{2,1,0:T(8,128)S(1)}, f32[2,8,128]{2,1,0:T(8,128)S(1)}, u32[]{:S(2)}, u32[]{:S(2)}) collective-permute-start(f32[2,8,128]{2,1,0:T(8,128)S(1)} %add_add_fusion), channel_id=1, source_target_pairs={{0,12},{1,13},{2,14},{3,15},{4,8},{5,9},{6,10},{7,11},{8,4},{9,5},... | collective-permute-start | bytes 24584 | tf_op jit(solution)/shard_map/ppermute | solution.py:325

commit v13 on v12

--- a/solution.py
+++ b/solution.py
@@ -10,6 +10,7 @@
 
 BATCH = 4
 UNROLL = 4
+MUTE = 1 << 28
 
 
 def ring_of(depth):
@@ -34,21 +35,14 @@
     depth, shard_tiles,
     me_ref, counts_ref, irrep_ref,
     res_ref, gathered_ref, stats_ref, order_ref, offset_ref, stop_ref, end_ref, item_ref,
-    blank_ref, next_ref, call_ref, blank_sem,
+    next_ref, call_ref,
 ):
     own_tiles = irrep_ref.shape[0]
     irreps = counts_ref.shape[0]
     calls = end_ref.shape[0]
     most = item_ref.shape[0] // calls
-    blank_ref[...] = jnp.zeros(blank_ref.shape, blank_ref.dtype)
-    group = blank_ref.shape[0]
-    for l in range(0, own_tiles, group):
-        pltpu.make_async_copy(blank_ref, res_ref.at[pl.ds(l, group)], blank_sem).start()
-
     for s in range(irreps):
         stop_ref[s] = 0
-    for t in range(BATCH):
-        order_ref[own_tiles + t] = 0
 
     def count(l, carry):
         s = irrep_ref[l]
@@ -109,8 +103,13 @@
     for call in range(calls):
         end = end_ref[call]
         for spare in range(UNROLL - 1):
-            item_ref[end + spare] = own_tiles
-
+            item_ref[end + spare] = item_ref[jnp.maximum(end - 1, 0)] | MUTE
+
+    def blank(l, carry):
+        res_ref[l] = jnp.zeros(res_ref.shape[1:], res_ref.dtype)
+        return carry
+
+    lax.fori_loop(0, own_tiles, blank, 0)
     spare = jnp.zeros((BATCH, *gathered_ref.shape[1:]), gathered_ref.dtype)
     gathered_ref[pl.ds(gathered_ref.shape[0] - BATCH, BATCH)] = spare
     shape = stats_ref.shape[1:]
@@ -123,7 +122,6 @@
         first = stop_ref[s]
     stats_ref[0] = jnp.zeros(shape, jnp.float32)
     stats_ref[1] = sizes.astype(jnp.float32)
-    pltpu.make_async_copy(res_ref, res_ref, blank_sem).wait()
 
 
 def prepare(me, counts, irrep, depth, shard_tiles, rows, width):
@@ -134,29 +132,27 @@
     most = (all_tiles // BATCH + irreps) * (own_tiles // BATCH) + UNROLL
     smem = pl.BlockSpec(memory_space=pltpu.SMEM)
     vmem = pl.BlockSpec(memory_space=pltpu.VMEM)
-    anywhere = pl.BlockSpec(memory_space=pl.ANY)
     return pl.pallas_call(
         functools.partial(prepare_kernel, depth, shard_tiles),
         out_shape=(
             jax.ShapeDtypeStruct((own_tiles, rows, columns), jnp.bfloat16),
             jax.ShapeDtypeStruct((all_tiles + BATCH, rows, width), jnp.bfloat16),
             jax.ShapeDtypeStruct((2, irreps, 128), jnp.float32),
-            jax.ShapeDtypeStruct((own_tiles + BATCH,), jnp.int32),
+            jax.ShapeDtypeStruct((own_tiles,), jnp.int32),
             jax.ShapeDtypeStruct((irreps,), jnp.int32),
             jax.ShapeDtypeStruct((irreps,), jnp.int32),
             jax.ShapeDtypeStruct((depth,), jnp.int32),
             jax.ShapeDtypeStruct((depth * most,), jnp.int32),
         ),
         in_specs=[smem] * 3,
-        out_specs=(anywhere, vmem, vmem, smem, smem, smem, smem, smem),
+        out_specs=(vmem, vmem, vmem, smem, smem, smem, smem, smem),
         scratch_shapes=[
-            pltpu.VMEM((2, rows, columns), jnp.bfloat16),
             pltpu.SMEM((irreps,), jnp.int32),
             pltpu.SMEM((4 * depth,), jnp.int32),
-            pltpu.SemaphoreType.DMA,
         ],
         compiler_params=pltpu.CompilerParams(
-            vmem_limit_bytes=4 * all_tiles * rows * width + 4 * 1024 * 1024
+            vmem_limit_bytes=2 * all_tiles * rows * width + 2 * own_tiles * rows * columns
+            + 4 * 1024 * 1024
         ),
         cost_estimate=pl.CostEstimate(
             flops=0, bytes_accessed=2 * own_tiles * rows * columns, transcendentals=0
@@ -172,7 +168,7 @@
 ):
     del res_in_ref, gathered_in_ref
     fresh, refs = refs[:len(layout)], refs[len(layout):]
-    res_hbm, gathered_ref, stats_ref, o_buf, acc_ref, a_sem, o_sem = refs
+    res_ref, gathered_ref, stats_ref, acc_ref, a_sem = refs
     rows, width = v_ref.shape[1:]
     side = BATCH * rows
     most = item_ref.shape[0] // end_ref.shape[0]
@@ -201,46 +197,32 @@
 
     def item(n):
         word = item_ref[n]
-        slot, group, block = word & 255, (word >> 8) & 255, word >> 16
-        return slot, group, block, jnp.minimum(stop_ref[group] - slot, BATCH)
+        slot, group, block = word & 255, (word >> 8) & 255, (word >> 16) & 255
+        members = stop_ref[group] - slot
+        tiles = [order_ref[slot + jnp.minimum(t, members - 1)] for t in range(BATCH)]
+        return group, block, tiles, jnp.where(word >= MUTE, 0, members)
 
     def multiply(n):
-        slot, group, block, _ = item(n)
-        left = jnp.concatenate([v_ref[order_ref[slot + t]] for t in range(BATCH)])
+        group, block, tiles, _ = item(n)
+        left = jnp.concatenate([v_ref[tile] for tile in tiles])
         right = gathered_ref[pl.ds(offset_ref[group] + block * BATCH, BATCH)].reshape(side, width)
         return lax.dot_general(
             left, right, (((1,), (1,)), ((), ())), preferred_element_type=jnp.float32
         )
 
     def keep(n, values):
-        slot, group, block, members = item(n)
+        group, block, tiles, members = item(n)
         limit = (counts_ref[group] - block * BATCH) * rows
         values = jnp.where(col_at < limit, values, 0.0).reshape(BATCH, rows, side)
         columns = pl.ds(pl.multiple_of(block * side, side), side)
-        o_buf[pl.ds(slot, BATCH), :, columns] = values.astype(jnp.bfloat16)
-        squares = jnp.sum((values * values).reshape(BATCH, rows // 8, 8, side), axis=1)
         total = jnp.zeros((8, side), jnp.float32)
         for t in range(BATCH):
-            total = total + jnp.where(t < members, squares[t], 0.0)
+            res_ref[tiles[t], :, columns] = values[t].astype(jnp.bfloat16)
+            squares = jnp.sum((values[t] * values[t]).reshape(rows // 8, 8, side), axis=0)
+            total = total + jnp.where(t < members, squares, 0.0)
         acc_ref[group] += total
 
-    def send(n, started):
-        slot, _, block, members = item(n)
-        members = jnp.maximum(members, 0)
-        columns = pl.ds(pl.multiple_of(block * side, side), side)
-
-        def one(t, carry):
-            pltpu.make_async_copy(
-                o_buf.at[slot + t, :, columns],
-                res_hbm.at[order_ref[slot + t], :, columns],
-                o_sem,
-            ).start()
-            return carry
-
-        lax.fori_loop(0, members, one, 0)
-        return started + members
-
-    def several(u, started):
+    def several(u, carry):
         first = call * most + u * UNROLL
         values = multiply(first)
         for n in range(1, UNROLL):
@@ -248,36 +230,24 @@
             keep(first + n - 1, values)
             values = following
         keep(first + UNROLL - 1, values)
-        for n in range(UNROLL):
-            started = send(first + n, started)
-        return started
+        return carry
 
     items = end_ref[call] - call * most
-    started = lax.fori_loop(0, (items + UNROLL - 1) // UNROLL, several, jnp.int32(0))
+    lax.fori_loop(0, (items + UNROLL - 1) // UNROLL, several, 0)
     sums = jnp.sum(acc_ref[...], axis=1)
     sums = sum(sums[:, k:k + 128] for k in range(0, side, 128))
     stats_ref[0] = stats_in_ref[0] + sums
     stats_ref[1] = stats_in_ref[1]
 
-    def finish(n, carry):
-        pltpu.make_async_copy(
-            o_buf.at[0, :, pl.ds(0, side)], res_hbm.at[0, :, pl.ds(0, side)], o_sem
-        ).wait()
-        return carry
-
-    lax.fori_loop(0, started, finish, 0)
-
 
 def ladder(call, depth, shard_tiles, integrals, listing, state, arrived):
     residual, gathered, stats = state
     layout, fresh = tuple(arrived), tuple(arrived.values())
-    own_tiles, rows, width = integrals.shape
-    slots = own_tiles + BATCH
+    rows, width = integrals.shape[1:]
     irreps = stats.shape[1]
     smem = pl.BlockSpec(memory_space=pltpu.SMEM)
     vmem = pl.BlockSpec(memory_space=pltpu.VMEM)
     anywhere = pl.BlockSpec(memory_space=pl.ANY)
-    out_bytes = 2 * slots * residual[0].size
     tiles = sum(source.shape[0] for source in fresh)
     return pl.pallas_call(
         functools.partial(ladder_kernel, call, depth, shard_tiles, layout),
@@ -286,17 +256,15 @@
             jax.ShapeDtypeStruct(gathered.shape, gathered.dtype),
             jax.ShapeDtypeStruct(stats.shape, stats.dtype),
         ),
-        in_specs=[smem] * 7 + [vmem] * 2 + [anywhere, vmem] + [anywhere] * len(fresh),
-        out_specs=(anywhere, vmem, vmem),
+        in_specs=[smem] * 7 + [vmem] * 4 + [anywhere] * len(fresh),
+        out_specs=(vmem, vmem, vmem),
         scratch_shapes=[
-            pltpu.VMEM((slots, rows, residual.shape[2]), jnp.bfloat16),
             pltpu.VMEM((irreps, 8, BATCH * rows), jnp.float32),
             pltpu.SemaphoreType.DMA((len(fresh),)),
-            pltpu.SemaphoreType.DMA,
         ],
         input_output_aliases={9: 0, 10: 1},
         compiler_params=pltpu.CompilerParams(
-            vmem_limit_bytes=out_bytes + 2 * integrals.size + 4 * gathered.size + 6 * 1024 * 1024
+            vmem_limit_bytes=2 * (residual.size + integrals.size + gathered.size) + 6 * 1024 * 1024
         ),
         cost_estimate=pl.CostEstimate(
             flops=residual.size * width * tiles // (4 * shard_tiles * depth),
@@ -305,6 +273,24 @@
         ),
         name=f"ladder_{call}",
     )(*listing, stats, integrals, residual, gathered, *fresh)
+
+
+def deliver_kernel(held_ref, out_ref, sem):
+    copy = pltpu.make_async_copy(held_ref, out_ref, sem)
+    copy.start()
+    copy.wait()
+
+
+def deliver(held):
+    return pl.pallas_call(
+        deliver_kernel,
+        out_shape=jax.ShapeDtypeStruct(held.shape, held.dtype),
+        in_specs=[pl.BlockSpec(memory_space=pltpu.VMEM)],
+        out_specs=pl.BlockSpec(memory_space=pl.ANY),
+        scratch_shapes=[pltpu.SemaphoreType.DMA],
+        compiler_params=pltpu.CompilerParams(vmem_limit_bytes=2 * held.size + 1024 * 1024),
+        name="deliver",
+    )(held)
 
 
 def per_device(amplitudes, ij_counts, integrals, ab_irrep):
@@ -333,7 +319,7 @@
     a, b, c, d = [amplitudes], [], [], []
     for k in range(depth):
         if 0 < k < depth - 1:
-            c[-1], a[k], state = lax.optimization_barrier((c[-1], a[k], state))
+            a[k], c[-1], state = lax.optimization_barrier((a[k], c[-1], state))
         if k < depth - 1:
             b.append(swap(a[k], 2))
             a.append(shift_z(a[k], 1))
@@ -346,7 +332,7 @@
         c.append(swap(a[k], 1))
         if k == 0:
             continue
-        fresh = {(k, 0, 0, 0): a[k], (k - 1, 0, 1, 0): c[k - 1], (k - 1, 1, 0, 0): b[k - 1]}
+        fresh = {(k, 0, 0, 0): a[k], (k - 1, 1, 0, 0): b[k - 1], (k - 1, 0, 1, 0): c[k - 1]}
         if k == 1:
             fresh[0, 0, 0, 0] = a[0]
         else:
@@ -364,7 +350,7 @@
     stats = sum([swap(stats, 4 * bits) for bits in range(1, depth)], stats)
     irrep_sums, ab_counts = jnp.sum(stats, axis=2)
     entries = ab_counts * ij_counts.astype(jnp.float32) * float(rows * rows)
-    return residual, jnp.sqrt(irrep_sums / entries + 1e-06)
+    return deliver(residual), jnp.sqrt(irrep_sums / entries + 1e-06)
 
 
 def solution(mesh):

time: 69.8 us -> 67.3 us (0.964)
  starting transfers between devices: 22.6 us -> 20 us
  Pallas kernels: 20 us -> 20.8 us
    pallas_call x0 -> x1, Pallas kernels: none -> 3.4 us  [deliver(): pl.pallas_call(deliver_kernel, out_shape=jax.ShapeDtypeStruct(held.shape,...]
    ppermute x19, starting transfers between devices: 16.6 us -> 14 us  [swap(): return lax.ppermute(x, 'vir', [(d, d ^ bits) for d in range(devices)])]
    pallas_call x4, Pallas kernels: 15.4 us -> 13.5 us  [ladder(): pl.pallas_call(functools.partial(ladder_kernel, call, depth, shard_tiles,...]
    ppermute x19, waiting for transfers between devices: 7.16 us -> 5.95 us  [swap(): return lax.ppermute(x, 'vir', [(d, d ^ bits) for d in range(devices)])]
    ppermute x4, waiting for transfers between devices: 13.8 us -> 14.5 us  [shift_z(): return lax.ppermute(x, 'vir', pairs)]
  transfers between devices with their start and end apart: 23 -> 23, of which waited for: 7 -> 9; matrix products, arithmetic and copies ran while one was open for 0% -> 0% of each run, Pallas kernels for 23% -> 25%
where the time goes in v13:
time: 67.3 us; the launch traced here: 67.1 us
  Pallas kernels  20.8 us (31%)
  waiting for transfers between devices  20.4 us (30%)
  starting transfers between devices  20 us (30%)
  local copies, waits for them, and re-layouts  4.41 us (7%)
  between operations  0.76 us (1%)
    ppermute x4, waiting for transfers between devices, shift_z(): return lax.ppermute(x, 'vir', pairs)  14.5 us
    ppermute x19, starting transfers between devices, swap(): return lax.ppermute(x, 'vir', [(d, d ^ bits) for d in range(devices)])  14 us
    pallas_call x4, Pallas kernels, ladder(): pl.pallas_call(functools.partial(ladder_kernel, call, depth, shard_tiles,...  13.5 us
    ppermute x4, starting transfers between devices, shift_z(): return lax.ppermute(x, 'vir', pairs)  6.01 us
    ppermute x19, waiting for transfers between devices, swap(): return lax.ppermute(x, 'vir', [(d, d ^ bits) for d in range(devices)])  5.95 us
    unnamed x12, local copies, waits for them, and re-layouts  4.37 us
    pallas_call x1, Pallas kernels, prepare(): pl.pallas_call(functools.partial(prepare_kernel, depth, shard_tiles), out...  3.97 us
    pallas_call x1, Pallas kernels, deliver(): pl.pallas_call(deliver_kernel, out_shape=jax.ShapeDtypeStruct(held.shape,...  3.4 us
  transfers between devices with their start and end apart: 23, of which 9 were waited for; matrix products, arithmetic and copies ran while one was open for 0% of the time, Pallas kernels for 25%

profile of v13, /device:TPU:0, one launch (start us, length us, event | category | flops | bytes accessed | tf_op | source)
XLA Modules:
  0.0 67.1 jit_solution(16746190978275924912)
XLA Ops:
  0.6 3.1 %collective-permute-start = (bf16[8,64,384]{2,1,0:T(8,128)(2,1)}, bf16[8,64,384]{2,1,0:T(8,128)(2,1)S(1)}, u32[]{:S(2)}, u32[]{:S(2)}) collective-permute-start(bf16[8,64,384]{2,1,0:T(8,128)(2,1)} %refs_3_.1), channel_id=1, source_target_pairs={{0,4},{1,5},{2,6},{3,7},{4,12},{5,13},{6,14},{7,15},{8,0},{9,1},{1... | collective-permute-start | bytes 1179656 | tf_op jit(solution)/shard_map/ppermute | solution.py:308
  3.7 1.5 %collective-permute-start.4 = (bf16[8,64,384]{2,1,0:T(8,128)(2,1)}, bf16[8,64,384]{2,1,0:T(8,128)(2,1)S(1)}, u32[]{:S(2)}, u32[]{:S(2)}) collective-permute-start(bf16[8,64,384]{2,1,0:T(8,128)(2,1)} %refs_3_.1), channel_id=1, source_target_pairs={{0,2},{1,3},{2,0},{3,1},{4,6},{5,7},{6,4},{7,5},{8,10},{9,11},{10,... | collective-permute-start | bytes 1179656 | tf_op jit(solution)/shard_map/ppermute | solution.py:311
  5.2 0.7 copy-done.3
  5.9 0.7 copy-done.5
  6.5 4.0 %prepare.1 = (bf16[32,64,2048]{2,1,0:T(8,128)(2,1)S(1)}, bf16[132,64,384]{2,1,0:T(8,128)(2,1)S(1)}, f32[2,8,128]{2,1,0:T(8,128)S(1)}, s32[32]{0:T(128)S(1)}, s32...) custom-call(s32[1]{0:T(128)} %bitcast.me_ref, s32[8]{0:T(128)S(1)} %copy-done.3, s32[32]{0:T(128)S(1)} %copy-done.5), custom_call_target="tpu_custom_call" | custom-call | bytes 8388608 | tf_op jit(solution)/shard_map/prepare/pallas_call | solution.py:135
  10.5 3.5 %collective-permute-done.refs_0_ = bf16[8,64,384]{2,1,0:T(8,128)(2,1)S(1)} collective-permute-done((bf16[8,64,384]{2,1,0:T(8,128)(2,1)}, bf16[8,64,384]{2,1,0:T(8,128)(2,1)S(1)}, u32[]{:S(2)}, u32[]{:S(2)}) %collective-permute-start) | collective-permute-done | bytes 393248 | tf_op jit(solution)/shard_map/ppermute | solution.py:308
  14.0 0.9 %collective-permute-start.2 = (bf16[8,64,384]{2,1,0:T(8,128)(2,1)S(1)}, bf16[8,64,384]{2,1,0:T(8,128)(2,1)S(1)}, u32[]{:S(2)}, u32[]{:S(2)}) collective-permute-start(bf16[8,64,384]{2,1,0:T(8,128)(2,1)S(1)} %collective-permute-done.refs_0_), channel_id=1, source_target_pairs={{0,4},{1,5},{2,6},{3,7},{4,12},{5,13},{6,14},{7,15},{8,0},{9,1},{1... | collective-permute-start | bytes 1179656 | tf_op jit(solution)/shard_map/ppermute | solution.py:308
  15.0 0.0 collective-permute-start.3
  15.0 1.5 %collective-permute-start.8 = (bf16[8,64,384]{2,1,0:T(8,128)(2,1)S(1)}, bf16[8,64,384]{2,1,0:T(8,128)(2,1)S(1)}, u32[]{:S(2)}, u32[]{:S(2)}) collective-permute-start(bf16[8,64,384]{2,1,0:T(8,128)(2,1)S(1)} %collective-permute-done.refs_0_), channel_id=1, source_target_pairs={{0,2},{1,3},{2,0},{3,1},{4,6},{5,7},{6,4},{7,5},{8,10},{9,11},{10,... | collective-permute-start | bytes 1179656 | tf_op jit(solution)/shard_map/ppermute | solution.py:311
  16.5 0.0 collective-permute-done.4.refs_1_
  16.5 0.2 collective-permute-start.9
  16.7 1.4 %copy-done = bf16[32,64,384]{2,1,0:T(8,128)(2,1)S(1)} copy-done((bf16[32,64,384]{2,1,0:T(8,128)(2,1)S(1)}, bf16[32,64,384]{2,1,0:T(8,128)(2,1)}, u32[]{:S(2)}) %copy-start) | copy-done | bytes 1572888
  18.2 1.0 %copy-done.2 = bf16[8,64,384]{2,1,0:T(8,128)(2,1)S(1)} copy-done((bf16[8,64,384]{2,1,0:T(8,128)(2,1)S(1)}, bf16[8,64,384]{2,1,0:T(8,128)(2,1)}, u32[]{:S(2)}) %copy-start.2) | copy-done | bytes 393240
  19.1 0.7 copy-done.4
  19.8 2.5 %ladder_0.1 = (bf16[32,64,2048]{2,1,0:T(8,128)(2,1)S(1)}, bf16[132,64,384]{2,1,0:T(8,128)(2,1)S(1)}, f32[2,8,128]{2,1,0:T(8,128)S(1)}) custom-call(s32[1]{0:T(128)} %bitcast.me_ref, s32[8]{0:T(128)S(1)} %copy-done.4, s32[32]{0:T(128)S(1)} %get-tuple-element.43.order_ref, ...), custom_call_target="tpu_custom_call", output_to_operand_aliasing={{0}: (9, {}), {1}: (10, {})} | custom-call | flops 402653184 | bytes 2097152 | tf_op jit(solution)/shard_map/ladder_0/pallas_call | solution.py:252
  22.4 2.9 %collective-permute-done.2.refs_0_ = bf16[8,64,384]{2,1,0:T(8,128)(2,1)S(1)} collective-permute-done((bf16[8,64,384]{2,1,0:T(8,128)(2,1)S(1)}, bf16[8,64,384]{2,1,0:T(8,128)(2,1)S(1)}, u32[]{:S(2)}, u32[]{:S(2)}) %collective-permute-start.2) | collective-permute-done | bytes 393248 | tf_op jit(solution)/shard_map/ppermute | solution.py:308
  25.3 0.7 %collective-permute-start.7 = (bf16[8,64,384]{2,1,0:T(8,128)(2,1)S(1)}, bf16[8,64,384]{2,1,0:T(8,128)(2,1)S(1)}, u32[]{:S(2)}, u32[]{:S(2)}) collective-permute-start(bf16[8,64,384]{2,1,0:T(8,128)(2,1)S(1)} %collective-permute-done.2.refs_0_), channel_id=1, source_target_pairs={{0,4},{1,5},{2,6},{3,7},{4,12},{5,13},{6,14},{7,15},{8,0},{9,1},{1... | collective-permute-start | bytes 1179656 | tf_op jit(solution)/shard_map/ppermute | solution.py:308
  26.0 1.3 %collective-permute-start.5 = (bf16[8,64,384]{2,1,0:T(8,128)(2,1)S(1)}, bf16[8,64,384]{2,1,0:T(8,128)(2,1)S(1)}, u32[]{:S(2)}, u32[]{:S(2)}) collective-permute-start(bf16[8,64,384]{2,1,0:T(8,128)(2,1)S(1)} %collective-permute-done.2.refs_0_), channel_id=1, source_target_pairs={{0,2},{1,3},{2,0},{3,1},{4,6},{5,7},{6,4},{7,5},{8,10},{9,11},{10,... | collective-permute-start | bytes 1179656 | tf_op jit(solution)/shard_map/ppermute | solution.py:311
  27.3 0.0 collective-permute-done.8.refs_1_
  27.3 0.0 collective-permute-start.12
  27.3 0.0 collective-permute-done.9.refs_3_
  27.4 3.1 %ladder_1.1 = (bf16[32,64,2048]{2,1,0:T(8,128)(2,1)S(1)}, bf16[132,64,384]{2,1,0:T(8,128)(2,1)S(1)}, f32[2,8,128]{2,1,0:T(8,128)S(1)}) custom-call(s32[1]{0:T(128)} %bitcast.me_ref, s32[8]{0:T(128)S(1)} %copy-done.4, s32[32]{0:T(128)S(1)} %get-tuple-element.43.order_ref, ...), custom_call_target="tpu_custom_call", output_to_operand_aliasing={{0}: (9, {}), {1}: (10, {})} | custom-call | flops 402653184 | bytes 2097152 | tf_op jit(solution)/shard_map/ladder_1/pallas_call | solution.py:252
  30.4 0.0 collective-permute-done.6.refs_2_
  30.4 7.2 %collective-permute-done.7.refs_0_ = bf16[8,64,384]{2,1,0:T(8,128)(2,1)S(1)} collective-permute-done((bf16[8,64,384]{2,1,0:T(8,128)(2,1)S(1)}, bf16[8,64,384]{2,1,0:T(8,128)(2,1)S(1)}, u32[]{:S(2)}, u32[]{:S(2)}) %collective-permute-start.7) | collective-permute-done | bytes 393248 | tf_op jit(solution)/shard_map/ppermute | solution.py:308
  37.7 1.3 %collective-permute-start.11 = (bf16[5,64,384]{2,1,0:T(8,128)(2,1)S(1)}, bf16[5,64,384]{2,1,0:T(8,128)(2,1)S(1)}, u32[]{:S(2)}, u32[]{:S(2)}) collective-permute-start(bf16[5,64,384]{2,1,0:T(8,128)(2,1)S(1)} %slice.8), channel_id=1, source_target_pairs={{0,8},{1,9},{2,10},{3,11},{4,0},{5,1},{6,2},{7,3},{8,12},{9,13},{1... | collective-permute-start | bytes 737288 | tf_op jit(solution)/shard_map/ppermute | solution.py:308
  39.0 1.6 %collective-permute-start.10 = (bf16[3,64,384]{2,1,0:T(8,128)(2,1)S(1)}, bf16[3,64,384]{2,1,0:T(8,128)(2,1)S(1)}, u32[]{:S(2)}, u32[]{:S(2)}) collective-permute-start(bf16[3,64,384]{2,1,0:T(8,128)(2,1)S(1)} %slice.7), channel_id=1, source_target_pairs={{0,2},{1,3},{2,0},{3,1},{4,6},{5,7},{6,4},{7,5},{8,10},{9,11},{10,... | collective-permute-start | bytes 442376 | tf_op jit(solution)/shard_map/ppermute | solution.py:311
  40.6 3.6 %ladder_2.1 = (bf16[32,64,2048]{2,1,0:T(8,128)(2,1)S(1)}, bf16[132,64,384]{2,1,0:T(8,128)(2,1)S(1)}, f32[2,8,128]{2,1,0:T(8,128)S(1)}) custom-call(s32[1]{0:T(128)} %bitcast.me_ref, s32[8]{0:T(128)S(1)} %copy-done.4, s32[32]{0:T(128)S(1)} %get-tuple-element.43.order_ref, ...), custom_call_target="tpu_custom_call", output_to_operand_aliasing={{0}: (9, {}), {1}: (10, {})} | custom-call | flops 402653184 | bytes 2097152 | tf_op jit(solution)/shard_map/ladder_2/pallas_call | solution.py:252
  44.2 0.3 collective-permute-done.10.refs_2_
  44.4 0.8 %collective-permute-done.11.refs_4_ = bf16[5,64,384]{2,1,0:T(8,128)(2,1)S(1)} collective-permute-done((bf16[5,64,384]{2,1,0:T(8,128)(2,1)S(1)}, bf16[5,64,384]{2,1,0:T(8,128)(2,1)S(1)}, u32[]{:S(2)}, u32[]{:S(2)}) %collective-permute-start.11) | collective-permute-done | bytes 245792 | tf_op jit(solution)/shard_map/ppermute | solution.py:308
  45.3 0.0 collective-permute-start.14
  45.3 0.5 collective-permute-start.16
  45.8 0.0 collective-permute-start.15
  45.8 1.8 %collective-permute-done.15.refs_3_ = bf16[3,64,384]{2,1,0:T(8,128)(2,1)S(1)} collective-permute-done((bf16[3,64,384]{2,1,0:T(8,128)(2,1)S(1)}, bf16[3,64,384]{2,1,0:T(8,128)(2,1)S(1)}, u32[]{:S(2)}, u32[]{:S(2)}) %collective-permute-start.15) | collective-permute-done | bytes 147488 | tf_op jit(solution)/shard_map/ppermute | solution.py:311
  47.6 4.2 %ladder_3.1 = (bf16[32,64,2048]{2,1,0:T(8,128)(2,1)S(1)}, bf16[132,64,384]{2,1,0:T(8,128)(2,1)S(1)}, f32[2,8,128]{2,1,0:T(8,128)S(1)}) custom-call(s32[1]{0:T(128)} %bitcast.me_ref, s32[8]{0:T(128)S(1)} %copy-done.4, s32[32]{0:T(128)S(1)} %get-tuple-element.43.order_ref, ...), custom_call_target="tpu_custom_call", output_to_operand_aliasing={{0}: (9, {}), {1}: (10, {})} | custom-call | flops 402653184 | bytes 2097152 | tf_op jit(solution)/shard_map/ladder_3/pallas_call | solution.py:252
  51.8 0.2 collective-permute-start.17
  52.0 1.3 %collective-permute-start.18 = (f32[2,8,128]{2,1,0:T(8,128)S(1)}, f32[2,8,128]{2,1,0:T(8,128)S(1)}, u32[]{:S(2)}, u32[]{:S(2)}) collective-permute-start(f32[2,8,128]{2,1,0:T(8,128)S(1)} %get-tuple-element.83), channel_id=1, source_target_pairs={{0,2},{1,3},{2,0},{3,1},{4,6},{5,7},{6,4},{7,5},{8,10},{9,11},{10,... | collective-permute-start | bytes 24584 | tf_op jit(solution)/shard_map/ppermute | solution.py:311
  53.3 0.4 collective-permute-start.19
  53.8 0.0 collective-permute-done.17
  53.8 1.9 %collective-permute-done.18 = f32[2,8,128]{2,1,0:T(8,128)S(1)} collective-permute-done((f32[2,8,128]{2,1,0:T(8,128)S(1)}, f32[2,8,128]{2,1,0:T(8,128)S(1)}, u32[]{:S(2)}, u32[]{:S(2)}) %collective-permute-start.18) | collective-permute-done | bytes 8224 | tf_op jit(solution)/shard_map/ppermute | solution.py:311
  55.7 0.7 %collective-permute-done.19 = f32[2,8,128]{2,1,0:T(8,128)S(1)} collective-permute-done((f32[2,8,128]{2,1,0:T(8,128)S(1)}, f32[2,8,128]{2,1,0:T(8,128)S(1)}, u32[]{:S(2)}, u32[]{:S(2)}) %collective-permute-start.19) | collective-permute-done | bytes 8224 | tf_op jit(solution)/shard_map/ppermute | solution.py:311
  56.4 2.9 %collective-permute-start.20 = (f32[2,8,128]{2,1,0:T(8,128)S(1)}, f32[2,8,128]{2,1,0:T(8,128)S(1)}, u32[]{:S(2)}, u32[]{:S(2)}) collective-permute-start(f32[2,8,128]{2,1,0:T(8,128)S(1)} %add_add_fusion), channel_id=1, source_target_pairs={{0,4},{1,5},{2,6},{3,7},{4,0},{5,1},{6,2},{7,3},{8,12},{9,13},{10,... | collective-permute-start | bytes 24584 | tf_op jit(solution)/shard_map/ppermute | solution.py:311
  59.3 1.7 %collective-permute-start.21 = (f32[2,8,128]{2,1,0:T(8,128)S(1)}, f32[2,8,128]{2,1,0:T(8,128)S(1)}, u32[]{:S(2)}, u32[]{:S(2)}) collective-permute-start(f32[2,8,128]{2,1,0:T(8,128)S(1)} %add_add_fusion), channel_id=1, source_target_pairs={{0,8},{1,9},{2,10},{3,11},{4,12},{5,13},{6,14},{7,15},{8,0},{9,1},... | collective-permute-start | bytes 24584 | tf_op jit(solution)/shard_map/ppermute | solution.py:311
  61.0 0.8 %collective-permute-start.22 = (f32[2,8,128]{2,1,0:T(8,128)S(1)}, f32[2,8,128]{2,1,0:T(8,128)S(1)}, u32[]{:S(2)}, u32[]{:S(2)}) collective-permute-start(f32[2,8,128]{2,1,0:T(8,128)S(1)} %add_add_fusion), channel_id=1, source_target_pairs={{0,12},{1,13},{2,14},{3,15},{4,8},{5,9},{6,10},{7,11},{8,4},{9,5},... | collective-permute-start | bytes 24584 | tf_op jit(solution)/shard_map/ppermute | solution.py:311
  61.8 3.4 %deliver.1 = bf16[32,64,2048]{2,1,0:T(8,128)(2,1)} custom-call(bf16[32,64,2048]{2,1,0:T(8,128)(2,1)S(1)} %get-tuple-element.82.held_ref), custom_call_target="tpu_custom_call" | custom-call | tf_op jit(solution)/shard_map/deliver/pallas_call | solution.py:285
  65.2 0.0 collective-permute-done.20
  65.2 1.3 %collective-permute-done.22 = f32[2,8,128]{2,1,0:T(8,128)S(1)} collective-permute-done((f32[2,8,128]{2,1,0:T(8,128)S(1)}, f32[2,8,128]{2,1,0:T(8,128)S(1)}, u32[]{:S(2)}, u32[]{:S(2)}) %collective-permute-start.22) | collective-permute-done | bytes 8224 | tf_op jit(solution)/shard_map/ppermute | solution.py:311
  66.4 0.1 add_reduce_fusion
  66.5 0.5 add_sqrt_fusion
  (21 shorter events, 0.1 us)
Async XLA Ops:
  0.6 13.4 %collective-permute-start = (bf16[8,64,384]{2,1,0:T(8,128)(2,1)}, bf16[8,64,384]{2,1,0:T(8,128)(2,1)S(1)}, u32[]{:S(2)}, u32[]{:S(2)}) collective-permute-start(bf16[8,64,384]{2,1,0:T(8,128)(2,1)} %refs_3_.1), channel_id=1, source_target_pairs={{0,4},{1,5},{2,6},{3,7},{4,12},{5,13},{6,14},{7,15},{8,0},{9,1},{1... | collective-permute-start | bytes 1179656 | tf_op jit(solution)/shard_map/ppermute | solution.py:308
  3.7 10.3 %collective-permute-start.1 = (bf16[8,64,384]{2,1,0:T(8,128)(2,1)}, bf16[8,64,384]{2,1,0:T(8,128)(2,1)S(1)}, u32[]{:S(2)}, u32[]{:S(2)}) collective-permute-start(bf16[8,64,384]{2,1,0:T(8,128)(2,1)} %refs_3_.1), channel_id=1, source_target_pairs={{0,1},{1,0},{2,3},{3,2},{4,5},{5,4},{6,7},{7,6},{8,9},{9,8},{10,11... | collective-permute-start | bytes 1179656 | tf_op jit(solution)/shard_map/ppermute | solution.py:311
  3.7 12.8 %collective-permute-start.4 = (bf16[8,64,384]{2,1,0:T(8,128)(2,1)}, bf16[8,64,384]{2,1,0:T(8,128)(2,1)S(1)}, u32[]{:S(2)}, u32[]{:S(2)}) collective-permute-start(bf16[8,64,384]{2,1,0:T(8,128)(2,1)} %refs_3_.1), channel_id=1, source_target_pairs={{0,2},{1,3},{2,0},{3,1},{4,6},{5,7},{6,4},{7,5},{8,10},{9,11},{10,... | collective-permute-start | bytes 1179656 | tf_op jit(solution)/shard_map/ppermute | solution.py:311
  5.2 0.7 copy-start.3
  5.9 0.7 copy-start.5
  14.0 11.2 %collective-permute-start.2 = (bf16[8,64,384]{2,1,0:T(8,128)(2,1)S(1)}, bf16[8,64,384]{2,1,0:T(8,128)(2,1)S(1)}, u32[]{:S(2)}, u32[]{:S(2)}) collective-permute-start(bf16[8,64,384]{2,1,0:T(8,128)(2,1)S(1)} %collective-permute-done.refs_0_), channel_id=1, source_target_pairs={{0,4},{1,5},{2,6},{3,7},{4,12},{5,13},{6,14},{7,15},{8,0},{9,1},{1... | collective-permute-start | bytes 1179656 | tf_op jit(solution)/shard_map/ppermute | solution.py:308
  15.0 10.3 %collective-permute-start.3 = (bf16[8,64,384]{2,1,0:T(8,128)(2,1)S(1)}, bf16[8,64,384]{2,1,0:T(8,128)(2,1)S(1)}, u32[]{:S(2)}, u32[]{:S(2)}) collective-permute-start(bf16[8,64,384]{2,1,0:T(8,128)(2,1)S(1)} %collective-permute-done.refs_0_), channel_id=1, source_target_pairs={{0,1},{1,0},{2,3},{3,2},{4,5},{5,4},{6,7},{7,6},{8,9},{9,8},{10,11... | collective-permute-start | bytes 1179656 | tf_op jit(solution)/shard_map/ppermute | solution.py:311
  15.0 12.3 %collective-permute-start.8 = (bf16[8,64,384]{2,1,0:T(8,128)(2,1)S(1)}, bf16[8,64,384]{2,1,0:T(8,128)(2,1)S(1)}, u32[]{:S(2)}, u32[]{:S(2)}) collective-permute-start(bf16[8,64,384]{2,1,0:T(8,128)(2,1)S(1)} %collective-permute-done.refs_0_), channel_id=1, source_target_pairs={{0,2},{1,3},{2,0},{3,1},{4,6},{5,7},{6,4},{7,5},{8,10},{9,11},{10,... | collective-permute-start | bytes 1179656 | tf_op jit(solution)/shard_map/ppermute | solution.py:311
  16.5 10.8 %collective-permute-start.9 = (bf16[8,64,384]{2,1,0:T(8,128)(2,1)S(1)}, bf16[8,64,384]{2,1,0:T(8,128)(2,1)S(1)}, u32[]{:S(2)}, u32[]{:S(2)}) collective-permute-start(bf16[8,64,384]{2,1,0:T(8,128)(2,1)S(1)} %collective-permute-done.4.refs_1_), channel_id=1, source_target_pairs={{0,1},{1,0},{2,3},{3,2},{4,5},{5,4},{6,7},{7,6},{8,9},{9,8},{10,11... | collective-permute-start | bytes 1179656 | tf_op jit(solution)/shard_map/ppermute | solution.py:311
  16.7 1.4 %copy-start = (bf16[32,64,384]{2,1,0:T(8,128)(2,1)S(1)}, bf16[32,64,384]{2,1,0:T(8,128)(2,1)}, u32[]{:S(2)}) copy-start(bf16[32,64,384]{2,1,0:T(8,128)(2,1)} %v_ref.7) | copy-start | bytes 4718596
  18.2 1.0 %copy-start.2 = (bf16[8,64,384]{2,1,0:T(8,128)(2,1)S(1)}, bf16[8,64,384]{2,1,0:T(8,128)(2,1)}, u32[]{:S(2)}) copy-start(bf16[8,64,384]{2,1,0:T(8,128)(2,1)} %refs_3_.1) | copy-start | bytes 1179652
  19.1 0.7 copy-start.4
  19.8 7.5 %copy-start.1 = (bf16[32,64,384]{2,1,0:T(8,128)(2,1)S(1)}, bf16[32,64,384]{2,1,0:T(8,128)(2,1)}, u32[]{:S(2)}) copy-start(bf16[32,64,384]{2,1,0:T(8,128)(2,1)} %v_ref.7) | copy-start | bytes 4718596
  25.3 5.2 %collective-permute-start.6 = (bf16[8,64,384]{2,1,0:T(8,128)(2,1)S(1)}, bf16[8,64,384]{2,1,0:T(8,128)(2,1)S(1)}, u32[]{:S(2)}, u32[]{:S(2)}) collective-permute-start(bf16[8,64,384]{2,1,0:T(8,128)(2,1)S(1)} %collective-permute-done.2.refs_0_), channel_id=1, source_target_pairs={{0,1},{1,0},{2,3},{3,2},{4,5},{5,4},{6,7},{7,6},{8,9},{9,8},{10,11... | collective-permute-start | bytes 1179656 | tf_op jit(solution)/shard_map/ppermute | solution.py:311
  25.3 12.4 %collective-permute-start.7 = (bf16[8,64,384]{2,1,0:T(8,128)(2,1)S(1)}, bf16[8,64,384]{2,1,0:T(8,128)(2,1)S(1)}, u32[]{:S(2)}, u32[]{:S(2)}) collective-permute-start(bf16[8,64,384]{2,1,0:T(8,128)(2,1)S(1)} %collective-permute-done.2.refs_0_), channel_id=1, source_target_pairs={{0,4},{1,5},{2,6},{3,7},{4,12},{5,13},{6,14},{7,15},{8,0},{9,1},{1... | collective-permute-start | bytes 1179656 | tf_op jit(solution)/shard_map/ppermute | solution.py:308
  26.0 14.5 %collective-permute-start.5 = (bf16[8,64,384]{2,1,0:T(8,128)(2,1)S(1)}, bf16[8,64,384]{2,1,0:T(8,128)(2,1)S(1)}, u32[]{:S(2)}, u32[]{:S(2)}) collective-permute-start(bf16[8,64,384]{2,1,0:T(8,128)(2,1)S(1)} %collective-permute-done.2.refs_0_), channel_id=1, source_target_pairs={{0,2},{1,3},{2,0},{3,1},{4,6},{5,7},{6,4},{7,5},{8,10},{9,11},{10,... | collective-permute-start | bytes 1179656 | tf_op jit(solution)/shard_map/ppermute | solution.py:311
  27.3 13.3 %collective-permute-start.12 = (bf16[8,64,384]{2,1,0:T(8,128)(2,1)S(1)}, bf16[8,64,384]{2,1,0:T(8,128)(2,1)S(1)}, u32[]{:S(2)}, u32[]{:S(2)}) collective-permute-start(bf16[8,64,384]{2,1,0:T(8,128)(2,1)S(1)} %collective-permute-done.8.refs_1_), channel_id=1, source_target_pairs={{0,1},{1,0},{2,3},{3,2},{4,5},{5,4},{6,7},{7,6},{8,9},{9,8},{10,11... | collective-permute-start | bytes 1179656 | tf_op jit(solution)/shard_map/ppermute | solution.py:311
  37.7 7.6 %collective-permute-start.11 = (bf16[5,64,384]{2,1,0:T(8,128)(2,1)S(1)}, bf16[5,64,384]{2,1,0:T(8,128)(2,1)S(1)}, u32[]{:S(2)}, u32[]{:S(2)}) collective-permute-start(bf16[5,64,384]{2,1,0:T(8,128)(2,1)S(1)} %slice.8), channel_id=1, source_target_pairs={{0,8},{1,9},{2,10},{3,11},{4,0},{5,1},{6,2},{7,3},{8,12},{9,13},{1... | collective-permute-start | bytes 737288 | tf_op jit(solution)/shard_map/ppermute | solution.py:308
  39.0 5.5 %collective-permute-start.10 = (bf16[3,64,384]{2,1,0:T(8,128)(2,1)S(1)}, bf16[3,64,384]{2,1,0:T(8,128)(2,1)S(1)}, u32[]{:S(2)}, u32[]{:S(2)}) collective-permute-start(bf16[3,64,384]{2,1,0:T(8,128)(2,1)S(1)} %slice.7), channel_id=1, source_target_pairs={{0,2},{1,3},{2,0},{3,1},{4,6},{5,7},{6,4},{7,5},{8,10},{9,11},{10,... | collective-permute-start | bytes 442376 | tf_op jit(solution)/shard_map/ppermute | solution.py:311
  40.5 7.0 %collective-permute-start.13 = (bf16[8,64,384]{2,1,0:T(8,128)(2,1)S(1)}, bf16[8,64,384]{2,1,0:T(8,128)(2,1)S(1)}, u32[]{:S(2)}, u32[]{:S(2)}) collective-permute-start(bf16[8,64,384]{2,1,0:T(8,128)(2,1)S(1)} %collective-permute-done.7.refs_0_), channel_id=1, source_target_pairs={{0,1},{1,0},{2,3},{3,2},{4,5},{5,4},{6,7},{7,6},{8,9},{9,8},{10,11... | collective-permute-start | bytes 1179656 | tf_op jit(solution)/shard_map/ppermute | solution.py:311
  45.3 2.3 %collective-permute-start.14 = (bf16[8,64,384]{2,1,0:T(8,128)(2,1)S(1)}, bf16[8,64,384]{2,1,0:T(8,128)(2,1)S(1)}, u32[]{:S(2)}, u32[]{:S(2)}) collective-permute-start(bf16[8,64,384]{2,1,0:T(8,128)(2,1)S(1)} %collective-permute-done.5.refs_1_), channel_id=1, source_target_pairs={{0,1},{1,0},{2,3},{3,2},{4,5},{5,4},{6,7},{7,6},{8,9},{9,8},{10,11... | collective-permute-start | bytes 1179656 | tf_op jit(solution)/shard_map/ppermute | solution.py:311
  45.3 2.3 %collective-permute-start.16 = (bf16[5,64,384]{2,1,0:T(8,128)(2,1)S(1)}, bf16[5,64,384]{2,1,0:T(8,128)(2,1)S(1)}, u32[]{:S(2)}, u32[]{:S(2)}) collective-permute-start(bf16[5,64,384]{2,1,0:T(8,128)(2,1)S(1)} %collective-permute-done.11.refs_4_), channel_id=1, source_target_pairs={{0,1},{1,0},{2,3},{3,2},{4,5},{5,4},{6,7},{7,6},{8,9},{9,8},{10,11... | collective-permute-start | bytes 737288 | tf_op jit(solution)/shard_map/ppermute | solution.py:311
  45.8 1.8 %collective-permute-start.15 = (bf16[3,64,384]{2,1,0:T(8,128)(2,1)S(1)}, bf16[3,64,384]{2,1,0:T(8,128)(2,1)S(1)}, u32[]{:S(2)}, u32[]{:S(2)}) collective-permute-start(bf16[3,64,384]{2,1,0:T(8,128)(2,1)S(1)} %collective-permute-done.10.refs_2_), channel_id=1, source_target_pairs={{0,1},{1,0},{2,3},{3,2},{4,5},{5,4},{6,7},{7,6},{8,9},{9,8},{10,11... | collective-permute-start | bytes 442376 | tf_op jit(solution)/shard_map/ppermute | solution.py:311
  51.8 1.9 %collective-permute-start.17 = (f32[2,8,128]{2,1,0:T(8,128)S(1)}, f32[2,8,128]{2,1,0:T(8,128)S(1)}, u32[]{:S(2)}, u32[]{:S(2)}) collective-permute-start(f32[2,8,128]{2,1,0:T(8,128)S(1)} %get-tuple-element.83), channel_id=1, source_target_pairs={{0,1},{1,0},{2,3},{3,2},{4,5},{5,4},{6,7},{7,6},{8,9},{9,8},{10,11... | collective-permute-start | bytes 24584 | tf_op jit(solution)/shard_map/ppermute | solution.py:311
  52.0 3.7 %collective-permute-start.18 = (f32[2,8,128]{2,1,0:T(8,128)S(1)}, f32[2,8,128]{2,1,0:T(8,128)S(1)}, u32[]{:S(2)}, u32[]{:S(2)}) collective-permute-start(f32[2,8,128]{2,1,0:T(8,128)S(1)} %get-tuple-element.83), channel_id=1, source_target_pairs={{0,2},{1,3},{2,0},{3,1},{4,6},{5,7},{6,4},{7,5},{8,10},{9,11},{10,... | collective-permute-start | bytes 24584 | tf_op jit(solution)/shard_map/ppermute | solution.py:311
  53.3 3.1 %collective-permute-start.19 = (f32[2,8,128]{2,1,0:T(8,128)S(1)}, f32[2,8,128]{2,1,0:T(8,128)S(1)}, u32[]{:S(2)}, u32[]{:S(2)}) collective-permute-start(f32[2,8,128]{2,1,0:T(8,128)S(1)} %get-tuple-element.83), channel_id=1, source_target_pairs={{0,3},{1,2},{2,1},{3,0},{4,7},{5,6},{6,5},{7,4},{8,11},{9,10},{10,... | collective-permute-start | bytes 24584 | tf_op jit(solution)/shard_map/ppermute | solution.py:311
  56.4 8.8 %collective-permute-start.20 = (f32[2,8,128]{2,1,0:T(8,128)S(1)}, f32[2,8,128]{2,1,0:T(8,128)S(1)}, u32[]{:S(2)}, u32[]{:S(2)}) collective-permute-start(f32[2,8,128]{2,1,0:T(8,128)S(1)} %add_add_fusion), channel_id=1, source_target_pairs={{0,4},{1,5},{2,6},{3,7},{4,0},{5,1},{6,2},{7,3},{8,12},{9,13},{10,... | collective-permute-start | bytes 24584 | tf_op jit(solution)/shard_map/ppermute | solution.py:311
  59.3 5.9 %collective-permute-start.21 = (f32[2,8,128]{2,1,0:T(8,128)S(1)}, f32[2,8,128]{2,1,0:T(8,128)S(1)}, u32[]{:S(2)}, u32[]{:S(2)}) collective-permute-start(f32[2,8,128]{2,1,0:T(8,128)S(1)} %add_add_fusion), channel_id=1, source_target_pairs={{0,8},{1,9},{2,10},{3,11},{4,12},{5,13},{6,14},{7,15},{8,0},{9,1},... | collective-permute-start | bytes 24584 | tf_op jit(solution)/shard_map/ppermute | solution.py:311
  61.0 5.4 %collective-permute-start.22 = (f32[2,8,128]{2,1,0:T(8,128)S(1)}, f32[2,8,128]{2,1,0:T(8,128)S(1)}, u32[]{:S(2)}, u32[]{:S(2)}) collective-permute-start(f32[2,8,128]{2,1,0:T(8,128)S(1)} %add_add_fusion), channel_id=1, source_target_pairs={{0,12},{1,13},{2,14},{3,15},{4,8},{5,9},{6,10},{7,11},{8,4},{9,5},... | collective-permute-start | bytes 24584 | tf_op jit(solution)/shard_map/ppermute | solution.py:311

commit v14 on v13

--- a/solution.py
+++ b/solution.py
@@ -26,9 +26,9 @@
 
 
 def call_of(depth, lag, other_y, other_core):
-    if other_y:
-        return min(lag + other_core, depth - 1)
-    return lag if other_core else max(lag - 1, 0)
+    if other_y and other_core:
+        return lag + 1 if lag < depth - 2 else depth
+    return lag if other_y or other_core else max(lag - 1, 0)
 
 
 def prepare_kernel(
@@ -141,8 +141,8 @@
             jax.ShapeDtypeStruct((own_tiles,), jnp.int32),
             jax.ShapeDtypeStruct((irreps,), jnp.int32),
             jax.ShapeDtypeStruct((irreps,), jnp.int32),
-            jax.ShapeDtypeStruct((depth,), jnp.int32),
-            jax.ShapeDtypeStruct((depth * most,), jnp.int32),
+            jax.ShapeDtypeStruct((depth + 1,), jnp.int32),
+            jax.ShapeDtypeStruct(((depth + 1) * most,), jnp.int32),
         ),
         in_specs=[smem] * 3,
         out_specs=(vmem, vmem, vmem, smem, smem, smem, smem, smem),
@@ -275,22 +275,28 @@
     )(*listing, stats, integrals, residual, gathered, *fresh)
 
 
-def deliver_kernel(held_ref, out_ref, sem):
-    copy = pltpu.make_async_copy(held_ref, out_ref, sem)
+def deliver_kernel(part, held_ref, *refs):
+    out_ref, sem = refs[-2:]
+    tiles = held_ref.shape[0] // 2
+    copy = pltpu.make_async_copy(
+        held_ref.at[pl.ds(part * tiles, tiles)], out_ref.at[pl.ds(part * tiles, tiles)], sem
+    )
     copy.start()
     copy.wait()
 
 
-def deliver(held):
+def deliver(held, part, *out):
+    anywhere = pl.BlockSpec(memory_space=pl.ANY)
     return pl.pallas_call(
-        deliver_kernel,
+        functools.partial(deliver_kernel, part),
         out_shape=jax.ShapeDtypeStruct(held.shape, held.dtype),
-        in_specs=[pl.BlockSpec(memory_space=pltpu.VMEM)],
-        out_specs=pl.BlockSpec(memory_space=pl.ANY),
+        in_specs=[pl.BlockSpec(memory_space=pltpu.VMEM)] + [anywhere] * len(out),
+        out_specs=anywhere,
         scratch_shapes=[pltpu.SemaphoreType.DMA],
+        input_output_aliases={1: 0} if out else {},
         compiler_params=pltpu.CompilerParams(vmem_limit_bytes=2 * held.size + 1024 * 1024),
-        name="deliver",
-    )(held)
+        name=f"deliver_{part}",
+    )(held, *out)
 
 
 def per_device(amplitudes, ij_counts, integrals, ab_irrep):
@@ -341,16 +347,21 @@
             d.append(swap(b[k - 1], 1))
         state = ladder(k - 1, depth, shard_tiles, integrals, listing, state, fresh)
     b[-1], last, state = lax.optimization_barrier((b[-1], last, state))
-    fresh = {(k, 0, 1, 0): c[k], (k - 1, 1, 1, 0): swap(b[k - 1], 1)}
+    first, second = {(k, 0, 1, 0): c[k]}, {(k - 1, 1, 1, 0): swap(b[k - 1], 1)}
     for tile, piece in last.items():
-        fresh[k, 1, 0, tile], fresh[k, 1, 1, tile] = piece, swap(piece, 1)
-    residual, _, stats = ladder(k, depth, shard_tiles, integrals, listing, state, fresh)
-
+        first[k, 1, 0, tile], second[k, 1, 1, tile] = piece, swap(piece, 1)
+    for number, fresh in ((k, first), (k + 1, second)):
+        state = ladder(number, depth, shard_tiles, integrals, listing, state, fresh)
+
+    residual, _, stats = state
+    out = deliver(residual, 0)
     stats = sum([swap(stats, bits) for bits in (1, 2, 3)], stats)
+    stats, residual, out = lax.optimization_barrier((stats, residual, out))
+    out = deliver(residual, 1, out)
     stats = sum([swap(stats, 4 * bits) for bits in range(1, depth)], stats)
     irrep_sums, ab_counts = jnp.sum(stats, axis=2)
     entries = ab_counts * ij_counts.astype(jnp.float32) * float(rows * rows)
-    return deliver(residual), jnp.sqrt(irrep_sums / entries + 1e-06)
+    return out, jnp.sqrt(irrep_sums / entries + 1e-06)
 
 
 def solution(mesh):

time: 67.3 us -> 66.6 us (0.990)
  waiting for transfers between devices: 20.4 us -> 17.3 us
  starting transfers between devices: 20 us -> 21.3 us
  Pallas kernels: 20.8 us -> 21.8 us
    ppermute x19, waiting for transfers between devices: 5.95 us -> 2.31 us  [swap(): return lax.ppermute(x, 'vir', [(d, d ^ bits) for d in range(devices)])]
    ppermute x19, starting transfers between devices: 14 us -> 15.3 us  [swap(): return lax.ppermute(x, 'vir', [(d, d ^ bits) for d in range(devices)])]
    pallas_call x1 -> x2, Pallas kernels: 3.4 us -> 4.04 us  [deliver(): pl.pallas_call(functools.partial(deliver_kernel, part), out_shape=jax.Sha...]
    pallas_call x4 -> x5, Pallas kernels: 13.5 us -> 13.8 us  [ladder(): pl.pallas_call(functools.partial(ladder_kernel, call, depth, shard_tiles,...]
  transfers between devices with their start and end apart: 23 -> 23, of which waited for: 9 -> 8; matrix products, arithmetic and copies ran while one was open for 0% -> 0% of each run, Pallas kernels for 25% -> 28%
where the time goes in v14:
time: 66.6 us; the launch traced here: 66.2 us
  Pallas kernels  21.8 us (33%)
  starting transfers between devices  21.3 us (32%)
  waiting for transfers between devices  17.3 us (26%)
  local copies, waits for them, and re-layouts  4.41 us (7%)
  between operations  0.8 us (1%)
    ppermute x19, starting transfers between devices, swap(): return lax.ppermute(x, 'vir', [(d, d ^ bits) for d in range(devices)])  15.3 us
    ppermute x4, waiting for transfers between devices, shift_z(): return lax.ppermute(x, 'vir', pairs)  15 us
    pallas_call x5, Pallas kernels, ladder(): pl.pallas_call(functools.partial(ladder_kernel, call, depth, shard_tiles,...  13.8 us
    ppermute x4, starting transfers between devices, shift_z(): return lax.ppermute(x, 'vir', pairs)  6.03 us
    unnamed x12, local copies, waits for them, and re-layouts  4.37 us
    pallas_call x2, Pallas kernels, deliver(): pl.pallas_call(functools.partial(deliver_kernel, part), out_shape=jax.Sha...  4.04 us
    pallas_call x1, Pallas kernels, prepare(): pl.pallas_call(functools.partial(prepare_kernel, depth, shard_tiles), out...  3.97 us
    ppermute x19, waiting for transfers between devices, swap(): return lax.ppermute(x, 'vir', [(d, d ^ bits) for d in range(devices)])  2.31 us
  transfers between devices with their start and end apart: 23, of which 8 were waited for; matrix products, arithmetic and copies ran while one was open for 0% of the time, Pallas kernels for 28%

profile of v14, /device:TPU:0, one launch (start us, length us, event | category | flops | bytes accessed | tf_op | source)
XLA Modules:
  0.0 66.2 jit_solution(5222674251144525448)
XLA Ops:
  0.6 3.1 %collective-permute-start = (bf16[8,64,384]{2,1,0:T(8,128)(2,1)}, bf16[8,64,384]{2,1,0:T(8,128)(2,1)S(1)}, u32[]{:S(2)}, u32[]{:S(2)}) collective-permute-start(bf16[8,64,384]{2,1,0:T(8,128)(2,1)} %refs_3_.1), channel_id=1, source_target_pairs={{0,4},{1,5},{2,6},{3,7},{4,12},{5,13},{6,14},{7,15},{8,0},{9,1},{1... | collective-permute-start | bytes 1179656 | tf_op jit(solution)/shard_map/ppermute | solution.py:314
  3.7 0.0 collective-permute-start.1
  3.7 1.5 %collective-permute-start.4 = (bf16[8,64,384]{2,1,0:T(8,128)(2,1)}, bf16[8,64,384]{2,1,0:T(8,128)(2,1)S(1)}, u32[]{:S(2)}, u32[]{:S(2)}) collective-permute-start(bf16[8,64,384]{2,1,0:T(8,128)(2,1)} %refs_3_.1), channel_id=1, source_target_pairs={{0,2},{1,3},{2,0},{3,1},{4,6},{5,7},{6,4},{7,5},{8,10},{9,11},{10,... | collective-permute-start | bytes 1179656 | tf_op jit(solution)/shard_map/ppermute | solution.py:317
  5.2 0.7 copy-done.3
  5.9 0.7 copy-done.5
  6.5 4.0 %prepare.1 = (bf16[32,64,2048]{2,1,0:T(8,128)(2,1)S(1)}, bf16[132,64,384]{2,1,0:T(8,128)(2,1)S(1)}, f32[2,8,128]{2,1,0:T(8,128)S(1)}, s32[32]{0:T(128)S(1)}, s32...) custom-call(s32[1]{0:T(128)} %bitcast.me_ref, s32[8]{0:T(128)S(1)} %copy-done.3, s32[32]{0:T(128)S(1)} %copy-done.5), custom_call_target="tpu_custom_call" | custom-call | bytes 8388608 | tf_op jit(solution)/shard_map/prepare/pallas_call | solution.py:135
  10.5 3.5 %collective-permute-done.refs_0_ = bf16[8,64,384]{2,1,0:T(8,128)(2,1)S(1)} collective-permute-done((bf16[8,64,384]{2,1,0:T(8,128)(2,1)}, bf16[8,64,384]{2,1,0:T(8,128)(2,1)S(1)}, u32[]{:S(2)}, u32[]{:S(2)}) %collective-permute-start) | collective-permute-done | bytes 393248 | tf_op jit(solution)/shard_map/ppermute | solution.py:314
  14.0 0.0 collective-permute-done.1.refs_2_
  14.0 0.9 %collective-permute-start.2 = (bf16[8,64,384]{2,1,0:T(8,128)(2,1)S(1)}, bf16[8,64,384]{2,1,0:T(8,128)(2,1)S(1)}, u32[]{:S(2)}, u32[]{:S(2)}) collective-permute-start(bf16[8,64,384]{2,1,0:T(8,128)(2,1)S(1)} %collective-permute-done.refs_0_), channel_id=1, source_target_pairs={{0,4},{1,5},{2,6},{3,7},{4,12},{5,13},{6,14},{7,15},{8,0},{9,1},{1... | collective-permute-start | bytes 1179656 | tf_op jit(solution)/shard_map/ppermute | solution.py:314
  15.0 0.0 collective-permute-start.3
  15.0 1.5 %collective-permute-start.8 = (bf16[8,64,384]{2,1,0:T(8,128)(2,1)S(1)}, bf16[8,64,384]{2,1,0:T(8,128)(2,1)S(1)}, u32[]{:S(2)}, u32[]{:S(2)}) collective-permute-start(bf16[8,64,384]{2,1,0:T(8,128)(2,1)S(1)} %collective-permute-done.refs_0_), channel_id=1, source_target_pairs={{0,2},{1,3},{2,0},{3,1},{4,6},{5,7},{6,4},{7,5},{8,10},{9,11},{10,... | collective-permute-start | bytes 1179656 | tf_op jit(solution)/shard_map/ppermute | solution.py:317
  16.5 0.2 collective-permute-start.9
  16.7 1.4 %copy-done = bf16[32,64,384]{2,1,0:T(8,128)(2,1)S(1)} copy-done((bf16[32,64,384]{2,1,0:T(8,128)(2,1)S(1)}, bf16[32,64,384]{2,1,0:T(8,128)(2,1)}, u32[]{:S(2)}) %copy-start) | copy-done | bytes 1572888
  18.2 1.0 %copy-done.2 = bf16[8,64,384]{2,1,0:T(8,128)(2,1)S(1)} copy-done((bf16[8,64,384]{2,1,0:T(8,128)(2,1)S(1)}, bf16[8,64,384]{2,1,0:T(8,128)(2,1)}, u32[]{:S(2)}) %copy-start.2) | copy-done | bytes 393240
  19.1 0.7 copy-done.4
  19.8 2.0 %ladder_0.1 = (bf16[32,64,2048]{2,1,0:T(8,128)(2,1)S(1)}, bf16[132,64,384]{2,1,0:T(8,128)(2,1)S(1)}, f32[2,8,128]{2,1,0:T(8,128)S(1)}) custom-call(s32[1]{0:T(128)} %bitcast.me_ref, s32[8]{0:T(128)S(1)} %copy-done.4, s32[32]{0:T(128)S(1)} %get-tuple-element.49.order_ref, ...), custom_call_target="tpu_custom_call", output_to_operand_aliasing={{0}: (9, {}), {1}: (10, {})} | custom-call | flops 402653184 | bytes 2097152 | tf_op jit(solution)/shard_map/ladder_0/pallas_call | solution.py:252
  21.9 3.4 %collective-permute-done.2.refs_0_ = bf16[8,64,384]{2,1,0:T(8,128)(2,1)S(1)} collective-permute-done((bf16[8,64,384]{2,1,0:T(8,128)(2,1)S(1)}, bf16[8,64,384]{2,1,0:T(8,128)(2,1)S(1)}, u32[]{:S(2)}, u32[]{:S(2)}) %collective-permute-start.2) | collective-permute-done | bytes 393248 | tf_op jit(solution)/shard_map/ppermute | solution.py:314
  25.3 0.0 collective-permute-start.6
  25.3 0.8 %collective-permute-start.7 = (bf16[8,64,384]{2,1,0:T(8,128)(2,1)S(1)}, bf16[8,64,384]{2,1,0:T(8,128)(2,1)S(1)}, u32[]{:S(2)}, u32[]{:S(2)}) collective-permute-start(bf16[8,64,384]{2,1,0:T(8,128)(2,1)S(1)} %collective-permute-done.2.refs_0_), channel_id=1, source_target_pairs={{0,4},{1,5},{2,6},{3,7},{4,12},{5,13},{6,14},{7,15},{8,0},{9,1},{1... | collective-permute-start | bytes 1179656 | tf_op jit(solution)/shard_map/ppermute | solution.py:314
  26.0 1.3 %collective-permute-start.5 = (bf16[8,64,384]{2,1,0:T(8,128)(2,1)S(1)}, bf16[8,64,384]{2,1,0:T(8,128)(2,1)S(1)}, u32[]{:S(2)}, u32[]{:S(2)}) collective-permute-start(bf16[8,64,384]{2,1,0:T(8,128)(2,1)S(1)} %collective-permute-done.2.refs_0_), channel_id=1, source_target_pairs={{0,2},{1,3},{2,0},{3,1},{4,6},{5,7},{6,4},{7,5},{8,10},{9,11},{10,... | collective-permute-start | bytes 1179656 | tf_op jit(solution)/shard_map/ppermute | solution.py:317
  27.3 0.0 collective-permute-done.8.refs_1_
  27.3 0.0 collective-permute-start.12
  27.4 3.1 %ladder_1.1 = (bf16[32,64,2048]{2,1,0:T(8,128)(2,1)S(1)}, bf16[132,64,384]{2,1,0:T(8,128)(2,1)S(1)}, f32[2,8,128]{2,1,0:T(8,128)S(1)}) custom-call(s32[1]{0:T(128)} %bitcast.me_ref, s32[8]{0:T(128)S(1)} %copy-done.4, s32[32]{0:T(128)S(1)} %get-tuple-element.49.order_ref, ...), custom_call_target="tpu_custom_call", output_to_operand_aliasing={{0}: (9, {}), {1}: (10, {})} | custom-call | flops 402653184 | bytes 2097152 | tf_op jit(solution)/shard_map/ladder_1/pallas_call | solution.py:252
  30.5 0.0 collective-permute-done.6.refs_2_
  30.5 7.2 %collective-permute-done.7.refs_0_ = bf16[8,64,384]{2,1,0:T(8,128)(2,1)S(1)} collective-permute-done((bf16[8,64,384]{2,1,0:T(8,128)(2,1)S(1)}, bf16[8,64,384]{2,1,0:T(8,128)(2,1)S(1)}, u32[]{:S(2)}, u32[]{:S(2)}) %collective-permute-start.7) | collective-permute-done | bytes 393248 | tf_op jit(solution)/shard_map/ppermute | solution.py:314
  37.7 1.3 %collective-permute-start.11 = (bf16[5,64,384]{2,1,0:T(8,128)(2,1)S(1)}, bf16[5,64,384]{2,1,0:T(8,128)(2,1)S(1)}, u32[]{:S(2)}, u32[]{:S(2)}) collective-permute-start(bf16[5,64,384]{2,1,0:T(8,128)(2,1)S(1)} %slice.8), channel_id=1, source_target_pairs={{0,8},{1,9},{2,10},{3,11},{4,0},{5,1},{6,2},{7,3},{8,12},{9,13},{1... | collective-permute-start | bytes 737288 | tf_op jit(solution)/shard_map/ppermute | solution.py:314
  39.0 1.6 %collective-permute-start.10 = (bf16[3,64,384]{2,1,0:T(8,128)(2,1)S(1)}, bf16[3,64,384]{2,1,0:T(8,128)(2,1)S(1)}, u32[]{:S(2)}, u32[]{:S(2)}) collective-permute-start(bf16[3,64,384]{2,1,0:T(8,128)(2,1)S(1)} %slice.7), channel_id=1, source_target_pairs={{0,2},{1,3},{2,0},{3,1},{4,6},{5,7},{6,4},{7,5},{8,10},{9,11},{10,... | collective-permute-start | bytes 442376 | tf_op jit(solution)/shard_map/ppermute | solution.py:317
  40.5 0.0 collective-permute-done.5.refs_1_
  40.6 3.6 %ladder_2.1 = (bf16[32,64,2048]{2,1,0:T(8,128)(2,1)S(1)}, bf16[132,64,384]{2,1,0:T(8,128)(2,1)S(1)}, f32[2,8,128]{2,1,0:T(8,128)S(1)}) custom-call(s32[1]{0:T(128)} %bitcast.me_ref, s32[8]{0:T(128)S(1)} %copy-done.4, s32[32]{0:T(128)S(1)} %get-tuple-element.49.order_ref, ...), custom_call_target="tpu_custom_call", output_to_operand_aliasing={{0}: (9, {}), {1}: (10, {})} | custom-call | flops 402653184 | bytes 2097152 | tf_op jit(solution)/shard_map/ladder_2/pallas_call | solution.py:252
  44.2 0.3 collective-permute-done.10.refs_1_
  44.4 0.8 %collective-permute-done.11.refs_2_ = bf16[5,64,384]{2,1,0:T(8,128)(2,1)S(1)} collective-permute-done((bf16[5,64,384]{2,1,0:T(8,128)(2,1)S(1)}, bf16[5,64,384]{2,1,0:T(8,128)(2,1)S(1)}, u32[]{:S(2)}, u32[]{:S(2)}) %collective-permute-start.11) | collective-permute-done | bytes 245792 | tf_op jit(solution)/shard_map/ppermute | solution.py:314
  45.3 0.5 collective-permute-start.16
  45.8 0.0 collective-permute-start.15
  45.8 2.0 %ladder_3.1 = (bf16[32,64,2048]{2,1,0:T(8,128)(2,1)S(1)}, bf16[132,64,384]{2,1,0:T(8,128)(2,1)S(1)}, f32[2,8,128]{2,1,0:T(8,128)S(1)}) custom-call(s32[1]{0:T(128)} %bitcast.me_ref, s32[8]{0:T(128)S(1)} %copy-done.4, s32[32]{0:T(128)S(1)} %get-tuple-element.49.order_ref, ...), custom_call_target="tpu_custom_call", output_to_operand_aliasing={{0}: (9, {}), {1}: (10, {})} | custom-call | flops 201326592 | bytes 1048576 | tf_op jit(solution)/shard_map/ladder_3/pallas_call | solution.py:252
  47.8 3.0 %ladder_4.1 = (bf16[32,64,2048]{2,1,0:T(8,128)(2,1)S(1)}, bf16[132,64,384]{2,1,0:T(8,128)(2,1)S(1)}, f32[2,8,128]{2,1,0:T(8,128)S(1)}) custom-call(s32[1]{0:T(128)} %bitcast.me_ref, s32[8]{0:T(128)S(1)} %copy-done.4, s32[32]{0:T(128)S(1)} %get-tuple-element.49.order_ref, ...), custom_call_target="tpu_custom_call", output_to_operand_aliasing={{0}: (9, {}), {1}: (10, {})} | custom-call | flops 201326592 | bytes 1048576 | tf_op jit(solution)/shard_map/ladder_4/pallas_call | solution.py:252
  50.9 1.1 %collective-permute-start.17 = (f32[2,8,128]{2,1,0:T(8,128)S(1)}, f32[2,8,128]{2,1,0:T(8,128)S(1)}, u32[]{:S(2)}, u32[]{:S(2)}) collective-permute-start(f32[2,8,128]{2,1,0:T(8,128)S(1)} %get-tuple-element.91), channel_id=1, source_target_pairs={{0,1},{1,0},{2,3},{3,2},{4,5},{5,4},{6,7},{7,6},{8,9},{9,8},{10,11... | collective-permute-start | bytes 24584 | tf_op jit(solution)/shard_map/ppermute | solution.py:317
  51.9 0.2 collective-permute-start.18
  52.2 1.2 %collective-permute-start.19 = (f32[2,8,128]{2,1,0:T(8,128)S(1)}, f32[2,8,128]{2,1,0:T(8,128)S(1)}, u32[]{:S(2)}, u32[]{:S(2)}) collective-permute-start(f32[2,8,128]{2,1,0:T(8,128)S(1)} %get-tuple-element.91), channel_id=1, source_target_pairs={{0,3},{1,2},{2,1},{3,0},{4,7},{5,6},{6,5},{7,4},{8,11},{9,10},{10,... | collective-permute-start | bytes 24584 | tf_op jit(solution)/shard_map/ppermute | solution.py:317
  53.4 2.0 %deliver_0.1.refs_0_ = bf16[32,64,2048]{2,1,0:T(8,128)(2,1)} custom-call(bf16[32,64,2048]{2,1,0:T(8,128)(2,1)S(1)} %get-tuple-element.93.held_ref), custom_call_target="tpu_custom_call" | custom-call | tf_op jit(solution)/shard_map/deliver_0/pallas_call | solution.py:290
  55.4 0.2 collective-permute-done.18
  55.6 3.7 %collective-permute-start.20 = (f32[2,8,128]{2,1,0:T(8,128)S(1)}, f32[2,8,128]{2,1,0:T(8,128)S(1)}, u32[]{:S(2)}, u32[]{:S(2)}) collective-permute-start(f32[2,8,128]{2,1,0:T(8,128)S(1)} %add_add_fusion), channel_id=1, source_target_pairs={{0,4},{1,5},{2,6},{3,7},{4,0},{5,1},{6,2},{7,3},{8,12},{9,13},{10,... | collective-permute-start | bytes 24584 | tf_op jit(solution)/shard_map/ppermute | solution.py:317
  59.3 0.8 %collective-permute-start.21 = (f32[2,8,128]{2,1,0:T(8,128)S(1)}, f32[2,8,128]{2,1,0:T(8,128)S(1)}, u32[]{:S(2)}, u32[]{:S(2)}) collective-permute-start(f32[2,8,128]{2,1,0:T(8,128)S(1)} %add_add_fusion), channel_id=1, source_target_pairs={{0,8},{1,9},{2,10},{3,11},{4,12},{5,13},{6,14},{7,15},{8,0},{9,1},... | collective-permute-start | bytes 24584 | tf_op jit(solution)/shard_map/ppermute | solution.py:317
  60.1 1.6 %collective-permute-start.22 = (f32[2,8,128]{2,1,0:T(8,128)S(1)}, f32[2,8,128]{2,1,0:T(8,128)S(1)}, u32[]{:S(2)}, u32[]{:S(2)}) collective-permute-start(f32[2,8,128]{2,1,0:T(8,128)S(1)} %add_add_fusion), channel_id=1, source_target_pairs={{0,12},{1,13},{2,14},{3,15},{4,8},{5,9},{6,10},{7,11},{8,4},{9,5},... | collective-permute-start | bytes 24584 | tf_op jit(solution)/shard_map/ppermute | solution.py:317
  61.7 2.0 %deliver_1.1 = bf16[32,64,2048]{2,1,0:T(8,128)(2,1)} custom-call(bf16[32,64,2048]{2,1,0:T(8,128)(2,1)S(1)} %get-tuple-element.93.held_ref, bf16[32,64,2048]{2,1,0:T(8,128)(2,1)} %deliver_0.1.refs_0_), custom_call_target="tpu_custom_call", output_to_operand_aliasing={{}: (1, {})} | custom-call | tf_op jit(solution)/shard_map/deliver_1/pallas_call | solution.py:290
  63.8 0.1 collective-permute-done.21
  63.8 1.7 %collective-permute-done.22 = f32[2,8,128]{2,1,0:T(8,128)S(1)} collective-permute-done((f32[2,8,128]{2,1,0:T(8,128)S(1)}, f32[2,8,128]{2,1,0:T(8,128)S(1)}, u32[]{:S(2)}, u32[]{:S(2)}) %collective-permute-start.22) | collective-permute-done | bytes 8224 | tf_op jit(solution)/shard_map/ppermute | solution.py:317
  65.6 0.1 add_reduce_fusion
  65.7 0.5 add_sqrt_fusion
  (23 shorter events, 0.1 us)
Async XLA Ops:
  0.6 13.4 %collective-permute-start = (bf16[8,64,384]{2,1,0:T(8,128)(2,1)}, bf16[8,64,384]{2,1,0:T(8,128)(2,1)S(1)}, u32[]{:S(2)}, u32[]{:S(2)}) collective-permute-start(bf16[8,64,384]{2,1,0:T(8,128)(2,1)} %refs_3_.1), channel_id=1, source_target_pairs={{0,4},{1,5},{2,6},{3,7},{4,12},{5,13},{6,14},{7,15},{8,0},{9,1},{1... | collective-permute-start | bytes 1179656 | tf_op jit(solution)/shard_map/ppermute | solution.py:314
  3.7 10.3 %collective-permute-start.1 = (bf16[8,64,384]{2,1,0:T(8,128)(2,1)}, bf16[8,64,384]{2,1,0:T(8,128)(2,1)S(1)}, u32[]{:S(2)}, u32[]{:S(2)}) collective-permute-start(bf16[8,64,384]{2,1,0:T(8,128)(2,1)} %refs_3_.1), channel_id=1, source_target_pairs={{0,1},{1,0},{2,3},{3,2},{4,5},{5,4},{6,7},{7,6},{8,9},{9,8},{10,11... | collective-permute-start | bytes 1179656 | tf_op jit(solution)/shard_map/ppermute | solution.py:317
  3.7 12.8 %collective-permute-start.4 = (bf16[8,64,384]{2,1,0:T(8,128)(2,1)}, bf16[8,64,384]{2,1,0:T(8,128)(2,1)S(1)}, u32[]{:S(2)}, u32[]{:S(2)}) collective-permute-start(bf16[8,64,384]{2,1,0:T(8,128)(2,1)} %refs_3_.1), channel_id=1, source_target_pairs={{0,2},{1,3},{2,0},{3,1},{4,6},{5,7},{6,4},{7,5},{8,10},{9,11},{10,... | collective-permute-start | bytes 1179656 | tf_op jit(solution)/shard_map/ppermute | solution.py:317
  5.2 0.7 copy-start.3
  5.9 0.7 copy-start.5
  14.0 11.2 %collective-permute-start.2 = (bf16[8,64,384]{2,1,0:T(8,128)(2,1)S(1)}, bf16[8,64,384]{2,1,0:T(8,128)(2,1)S(1)}, u32[]{:S(2)}, u32[]{:S(2)}) collective-permute-start(bf16[8,64,384]{2,1,0:T(8,128)(2,1)S(1)} %collective-permute-done.refs_0_), channel_id=1, source_target_pairs={{0,4},{1,5},{2,6},{3,7},{4,12},{5,13},{6,14},{7,15},{8,0},{9,1},{1... | collective-permute-start | bytes 1179656 | tf_op jit(solution)/shard_map/ppermute | solution.py:314
  15.0 10.3 %collective-permute-start.3 = (bf16[8,64,384]{2,1,0:T(8,128)(2,1)S(1)}, bf16[8,64,384]{2,1,0:T(8,128)(2,1)S(1)}, u32[]{:S(2)}, u32[]{:S(2)}) collective-permute-start(bf16[8,64,384]{2,1,0:T(8,128)(2,1)S(1)} %collective-permute-done.refs_0_), channel_id=1, source_target_pairs={{0,1},{1,0},{2,3},{3,2},{4,5},{5,4},{6,7},{7,6},{8,9},{9,8},{10,11... | collective-permute-start | bytes 1179656 | tf_op jit(solution)/shard_map/ppermute | solution.py:317
  15.0 12.3 %collective-permute-start.8 = (bf16[8,64,384]{2,1,0:T(8,128)(2,1)S(1)}, bf16[8,64,384]{2,1,0:T(8,128)(2,1)S(1)}, u32[]{:S(2)}, u32[]{:S(2)}) collective-permute-start(bf16[8,64,384]{2,1,0:T(8,128)(2,1)S(1)} %collective-permute-done.refs_0_), channel_id=1, source_target_pairs={{0,2},{1,3},{2,0},{3,1},{4,6},{5,7},{6,4},{7,5},{8,10},{9,11},{10,... | collective-permute-start | bytes 1179656 | tf_op jit(solution)/shard_map/ppermute | solution.py:317
  16.5 10.8 %collective-permute-start.9 = (bf16[8,64,384]{2,1,0:T(8,128)(2,1)S(1)}, bf16[8,64,384]{2,1,0:T(8,128)(2,1)S(1)}, u32[]{:S(2)}, u32[]{:S(2)}) collective-permute-start(bf16[8,64,384]{2,1,0:T(8,128)(2,1)S(1)} %collective-permute-done.4.refs_1_), channel_id=1, source_target_pairs={{0,1},{1,0},{2,3},{3,2},{4,5},{5,4},{6,7},{7,6},{8,9},{9,8},{10,11... | collective-permute-start | bytes 1179656 | tf_op jit(solution)/shard_map/ppermute | solution.py:317
  16.7 1.4 %copy-start = (bf16[32,64,384]{2,1,0:T(8,128)(2,1)S(1)}, bf16[32,64,384]{2,1,0:T(8,128)(2,1)}, u32[]{:S(2)}) copy-start(bf16[32,64,384]{2,1,0:T(8,128)(2,1)} %v_ref.9) | copy-start | bytes 4718596
  18.2 1.0 %copy-start.2 = (bf16[8,64,384]{2,1,0:T(8,128)(2,1)S(1)}, bf16[8,64,384]{2,1,0:T(8,128)(2,1)}, u32[]{:S(2)}) copy-start(bf16[8,64,384]{2,1,0:T(8,128)(2,1)} %refs_3_.1) | copy-start | bytes 1179652
  19.1 0.7 copy-start.4
  19.8 7.5 %copy-start.1 = (bf16[32,64,384]{2,1,0:T(8,128)(2,1)S(1)}, bf16[32,64,384]{2,1,0:T(8,128)(2,1)}, u32[]{:S(2)}) copy-start(bf16[32,64,384]{2,1,0:T(8,128)(2,1)} %v_ref.9) | copy-start | bytes 4718596
  25.3 5.2 %collective-permute-start.6 = (bf16[8,64,384]{2,1,0:T(8,128)(2,1)S(1)}, bf16[8,64,384]{2,1,0:T(8,128)(2,1)S(1)}, u32[]{:S(2)}, u32[]{:S(2)}) collective-permute-start(bf16[8,64,384]{2,1,0:T(8,128)(2,1)S(1)} %collective-permute-done.2.refs_0_), channel_id=1, source_target_pairs={{0,1},{1,0},{2,3},{3,2},{4,5},{5,4},{6,7},{7,6},{8,9},{9,8},{10,11... | collective-permute-start | bytes 1179656 | tf_op jit(solution)/shard_map/ppermute | solution.py:317
  25.3 12.4 %collective-permute-start.7 = (bf16[8,64,384]{2,1,0:T(8,128)(2,1)S(1)}, bf16[8,64,384]{2,1,0:T(8,128)(2,1)S(1)}, u32[]{:S(2)}, u32[]{:S(2)}) collective-permute-start(bf16[8,64,384]{2,1,0:T(8,128)(2,1)S(1)} %collective-permute-done.2.refs_0_), channel_id=1, source_target_pairs={{0,4},{1,5},{2,6},{3,7},{4,12},{5,13},{6,14},{7,15},{8,0},{9,1},{1... | collective-permute-start | bytes 1179656 | tf_op jit(solution)/shard_map/ppermute | solution.py:314
  26.0 14.5 %collective-permute-start.5 = (bf16[8,64,384]{2,1,0:T(8,128)(2,1)S(1)}, bf16[8,64,384]{2,1,0:T(8,128)(2,1)S(1)}, u32[]{:S(2)}, u32[]{:S(2)}) collective-permute-start(bf16[8,64,384]{2,1,0:T(8,128)(2,1)S(1)} %collective-permute-done.2.refs_0_), channel_id=1, source_target_pairs={{0,2},{1,3},{2,0},{3,1},{4,6},{5,7},{6,4},{7,5},{8,10},{9,11},{10,... | collective-permute-start | bytes 1179656 | tf_op jit(solution)/shard_map/ppermute | solution.py:317
  27.3 13.3 %collective-permute-start.12 = (bf16[8,64,384]{2,1,0:T(8,128)(2,1)S(1)}, bf16[8,64,384]{2,1,0:T(8,128)(2,1)S(1)}, u32[]{:S(2)}, u32[]{:S(2)}) collective-permute-start(bf16[8,64,384]{2,1,0:T(8,128)(2,1)S(1)} %collective-permute-done.8.refs_1_), channel_id=1, source_target_pairs={{0,1},{1,0},{2,3},{3,2},{4,5},{5,4},{6,7},{7,6},{8,9},{9,8},{10,11... | collective-permute-start | bytes 1179656 | tf_op jit(solution)/shard_map/ppermute | solution.py:317
  37.7 7.6 %collective-permute-start.11 = (bf16[5,64,384]{2,1,0:T(8,128)(2,1)S(1)}, bf16[5,64,384]{2,1,0:T(8,128)(2,1)S(1)}, u32[]{:S(2)}, u32[]{:S(2)}) collective-permute-start(bf16[5,64,384]{2,1,0:T(8,128)(2,1)S(1)} %slice.8), channel_id=1, source_target_pairs={{0,8},{1,9},{2,10},{3,11},{4,0},{5,1},{6,2},{7,3},{8,12},{9,13},{1... | collective-permute-start | bytes 737288 | tf_op jit(solution)/shard_map/ppermute | solution.py:314
  39.0 5.5 %collective-permute-start.10 = (bf16[3,64,384]{2,1,0:T(8,128)(2,1)S(1)}, bf16[3,64,384]{2,1,0:T(8,128)(2,1)S(1)}, u32[]{:S(2)}, u32[]{:S(2)}) collective-permute-start(bf16[3,64,384]{2,1,0:T(8,128)(2,1)S(1)} %slice.7), channel_id=1, source_target_pairs={{0,2},{1,3},{2,0},{3,1},{4,6},{5,7},{6,4},{7,5},{8,10},{9,11},{10,... | collective-permute-start | bytes 442376 | tf_op jit(solution)/shard_map/ppermute | solution.py:317
  40.5 5.2 %collective-permute-start.13 = (bf16[8,64,384]{2,1,0:T(8,128)(2,1)S(1)}, bf16[8,64,384]{2,1,0:T(8,128)(2,1)S(1)}, u32[]{:S(2)}, u32[]{:S(2)}) collective-permute-start(bf16[8,64,384]{2,1,0:T(8,128)(2,1)S(1)} %collective-permute-done.7.refs_0_), channel_id=1, source_target_pairs={{0,1},{1,0},{2,3},{3,2},{4,5},{5,4},{6,7},{7,6},{8,9},{9,8},{10,11... | collective-permute-start | bytes 1179656 | tf_op jit(solution)/shard_map/ppermute | solution.py:317
  45.3 2.5 %collective-permute-start.14 = (bf16[8,64,384]{2,1,0:T(8,128)(2,1)S(1)}, bf16[8,64,384]{2,1,0:T(8,128)(2,1)S(1)}, u32[]{:S(2)}, u32[]{:S(2)}) collective-permute-start(bf16[8,64,384]{2,1,0:T(8,128)(2,1)S(1)} %collective-permute-done.5.refs_1_), channel_id=1, source_target_pairs={{0,1},{1,0},{2,3},{3,2},{4,5},{5,4},{6,7},{7,6},{8,9},{9,8},{10,11... | collective-permute-start | bytes 1179656 | tf_op jit(solution)/shard_map/ppermute | solution.py:317
  45.3 2.5 %collective-permute-start.16 = (bf16[5,64,384]{2,1,0:T(8,128)(2,1)S(1)}, bf16[5,64,384]{2,1,0:T(8,128)(2,1)S(1)}, u32[]{:S(2)}, u32[]{:S(2)}) collective-permute-start(bf16[5,64,384]{2,1,0:T(8,128)(2,1)S(1)} %collective-permute-done.11.refs_2_), channel_id=1, source_target_pairs={{0,1},{1,0},{2,3},{3,2},{4,5},{5,4},{6,7},{7,6},{8,9},{9,8},{10,11... | collective-permute-start | bytes 737288 | tf_op jit(solution)/shard_map/ppermute | solution.py:317
  45.8 2.0 %collective-permute-start.15 = (bf16[3,64,384]{2,1,0:T(8,128)(2,1)S(1)}, bf16[3,64,384]{2,1,0:T(8,128)(2,1)S(1)}, u32[]{:S(2)}, u32[]{:S(2)}) collective-permute-start(bf16[3,64,384]{2,1,0:T(8,128)(2,1)S(1)} %collective-permute-done.10.refs_1_), channel_id=1, source_target_pairs={{0,1},{1,0},{2,3},{3,2},{4,5},{5,4},{6,7},{7,6},{8,9},{9,8},{10,11... | collective-permute-start | bytes 442376 | tf_op jit(solution)/shard_map/ppermute | solution.py:317
  50.9 4.5 %collective-permute-start.17 = (f32[2,8,128]{2,1,0:T(8,128)S(1)}, f32[2,8,128]{2,1,0:T(8,128)S(1)}, u32[]{:S(2)}, u32[]{:S(2)}) collective-permute-start(f32[2,8,128]{2,1,0:T(8,128)S(1)} %get-tuple-element.91), channel_id=1, source_target_pairs={{0,1},{1,0},{2,3},{3,2},{4,5},{5,4},{6,7},{7,6},{8,9},{9,8},{10,11... | collective-permute-start | bytes 24584 | tf_op jit(solution)/shard_map/ppermute | solution.py:317
  51.9 3.7 %collective-permute-start.18 = (f32[2,8,128]{2,1,0:T(8,128)S(1)}, f32[2,8,128]{2,1,0:T(8,128)S(1)}, u32[]{:S(2)}, u32[]{:S(2)}) collective-permute-start(f32[2,8,128]{2,1,0:T(8,128)S(1)} %get-tuple-element.91), channel_id=1, source_target_pairs={{0,2},{1,3},{2,0},{3,1},{4,6},{5,7},{6,4},{7,5},{8,10},{9,11},{10,... | collective-permute-start | bytes 24584 | tf_op jit(solution)/shard_map/ppermute | solution.py:317
  52.2 3.4 %collective-permute-start.19 = (f32[2,8,128]{2,1,0:T(8,128)S(1)}, f32[2,8,128]{2,1,0:T(8,128)S(1)}, u32[]{:S(2)}, u32[]{:S(2)}) collective-permute-start(f32[2,8,128]{2,1,0:T(8,128)S(1)} %get-tuple-element.91), channel_id=1, source_target_pairs={{0,3},{1,2},{2,1},{3,0},{4,7},{5,6},{6,5},{7,4},{8,11},{9,10},{10,... | collective-permute-start | bytes 24584 | tf_op jit(solution)/shard_map/ppermute | solution.py:317
  55.6 8.1 %collective-permute-start.20 = (f32[2,8,128]{2,1,0:T(8,128)S(1)}, f32[2,8,128]{2,1,0:T(8,128)S(1)}, u32[]{:S(2)}, u32[]{:S(2)}) collective-permute-start(f32[2,8,128]{2,1,0:T(8,128)S(1)} %add_add_fusion), channel_id=1, source_target_pairs={{0,4},{1,5},{2,6},{3,7},{4,0},{5,1},{6,2},{7,3},{8,12},{9,13},{10,... | collective-permute-start | bytes 24584 | tf_op jit(solution)/shard_map/ppermute | solution.py:317
  59.3 4.5 %collective-permute-start.21 = (f32[2,8,128]{2,1,0:T(8,128)S(1)}, f32[2,8,128]{2,1,0:T(8,128)S(1)}, u32[]{:S(2)}, u32[]{:S(2)}) collective-permute-start(f32[2,8,128]{2,1,0:T(8,128)S(1)} %add_add_fusion), channel_id=1, source_target_pairs={{0,8},{1,9},{2,10},{3,11},{4,12},{5,13},{6,14},{7,15},{8,0},{9,1},... | collective-permute-start | bytes 24584 | tf_op jit(solution)/shard_map/ppermute | solution.py:317
  60.1 5.4 %collective-permute-start.22 = (f32[2,8,128]{2,1,0:T(8,128)S(1)}, f32[2,8,128]{2,1,0:T(8,128)S(1)}, u32[]{:S(2)}, u32[]{:S(2)}) collective-permute-start(f32[2,8,128]{2,1,0:T(8,128)S(1)} %add_add_fusion), channel_id=1, source_target_pairs={{0,12},{1,13},{2,14},{3,15},{4,8},{5,9},{6,10},{7,11},{8,4},{9,5},... | collective-permute-start | bytes 24584 | tf_op jit(solution)/shard_map/ppermute | solution.py:317

commit v15 on v14

--- a/solution.py
+++ b/solution.py
@@ -26,9 +26,9 @@
 
 
 def call_of(depth, lag, other_y, other_core):
-    if other_y and other_core:
-        return lag + 1 if lag < depth - 2 else depth
-    return lag if other_y or other_core else max(lag - 1, 0)
+    if other_y:
+        return depth if other_core and lag >= depth - 2 else lag + other_core
+    return min(lag, depth - 2) if other_core else max(lag - 1, 0)
 
 
 def prepare_kernel(
@@ -330,7 +330,7 @@
             b.append(swap(a[k], 2))
             a.append(shift_z(a[k], 1))
         else:
-            part = 3 * shard_tiles // 8
+            part = shard_tiles // 2
             c[-1], a[k], back, state = lax.optimization_barrier(
                 (c[-1], a[k], b[0][part:], state)
             )
@@ -345,9 +345,11 @@
             fresh[k - 2, 1, 1, 0] = d[k - 2]
         if k < depth - 1:
             d.append(swap(b[k - 1], 1))
+        else:
+            fresh[k, 0, 1, 0] = c[k]
         state = ladder(k - 1, depth, shard_tiles, integrals, listing, state, fresh)
     b[-1], last, state = lax.optimization_barrier((b[-1], last, state))
-    first, second = {(k, 0, 1, 0): c[k]}, {(k - 1, 1, 1, 0): swap(b[k - 1], 1)}
+    first, second = {}, {(k - 1, 1, 1, 0): swap(b[k - 1], 1)}
     for tile, piece in last.items():
         first[k, 1, 0, tile], second[k, 1, 1, tile] = piece, swap(piece, 1)
     for number, fresh in ((k, first), (k + 1, second)):

time: 66.6 us -> 66.1 us (level)
  Pallas kernels: 21.8 us -> 23.4 us
  starting transfers between devices: 21.3 us -> 20.2 us
  waiting for transfers between devices: 17.3 us -> 16.6 us
    ppermute x19, starting transfers between devices: 15.3 us -> 13.6 us  [swap(): return lax.ppermute(x, 'vir', [(d, d ^ bits) for d in range(devices)])]
    pallas_call x5, Pallas kernels: 13.8 us -> 15.3 us  [ladder(): pl.pallas_call(functools.partial(ladder_kernel, call, depth, shard_tiles,...]
    ppermute x4, waiting for transfers between devices: 15 us -> 13.9 us  [shift_z(): return lax.ppermute(x, 'vir', pairs)]
  transfers between devices with their start and end apart: 23 -> 23, of which waited for: 8 -> 8; matrix products, arithmetic and copies ran while one was open for 0% -> 0% of each run, Pallas kernels for 28% -> 31%
where the time goes in v15:
time: 66.1 us; the launch traced here: 66 us
  Pallas kernels  23.4 us (35%)
  starting transfers between devices  20.2 us (31%)
  waiting for transfers between devices  16.6 us (25%)
  local copies, waits for them, and re-layouts  4.41 us (7%)
  between operations  0.8 us (1%)
    pallas_call x5, Pallas kernels, ladder(): pl.pallas_call(functools.partial(ladder_kernel, call, depth, shard_tiles,...  15.3 us
    ppermute x4, waiting for transfers between devices, shift_z(): return lax.ppermute(x, 'vir', pairs)  13.9 us
    ppermute x19, starting transfers between devices, swap(): return lax.ppermute(x, 'vir', [(d, d ^ bits) for d in range(devices)])  13.6 us
    ppermute x4, starting transfers between devices, shift_z(): return lax.ppermute(x, 'vir', pairs)  6.58 us
    unnamed x12, local copies, waits for them, and re-layouts  4.37 us
    pallas_call x2, Pallas kernels, deliver(): pl.pallas_call(functools.partial(deliver_kernel, part), out_shape=jax.Sha...  4.04 us
    pallas_call x1, Pallas kernels, prepare(): pl.pallas_call(functools.partial(prepare_kernel, depth, shard_tiles), out...  4.03 us
    ppermute x19, waiting for transfers between devices, swap(): return lax.ppermute(x, 'vir', [(d, d ^ bits) for d in range(devices)])  2.7 us
  transfers between devices with their start and end apart: 23, of which 8 were waited for; matrix products, arithmetic and copies ran while one was open for 0% of the time, Pallas kernels for 31%

profile of v15, /device:TPU:0, one launch (start us, length us, event | category | flops | bytes accessed | tf_op | source)
XLA Modules:
  0.0 66.0 jit_solution(2492902640498189377)
XLA Ops:
  0.6 3.1 %collective-permute-start = (bf16[8,64,384]{2,1,0:T(8,128)(2,1)}, bf16[8,64,384]{2,1,0:T(8,128)(2,1)S(1)}, u32[]{:S(2)}, u32[]{:S(2)}) collective-permute-start(bf16[8,64,384]{2,1,0:T(8,128)(2,1)} %refs_3_.1), channel_id=1, source_target_pairs={{0,4},{1,5},{2,6},{3,7},{4,12},{5,13},{6,14},{7,15},{8,0},{9,1},{1... | collective-permute-start | bytes 1179656 | tf_op jit(solution)/shard_map/ppermute | solution.py:314
  3.7 0.0 collective-permute-start.1
  3.7 1.5 %collective-permute-start.4 = (bf16[8,64,384]{2,1,0:T(8,128)(2,1)}, bf16[8,64,384]{2,1,0:T(8,128)(2,1)S(1)}, u32[]{:S(2)}, u32[]{:S(2)}) collective-permute-start(bf16[8,64,384]{2,1,0:T(8,128)(2,1)} %refs_3_.1), channel_id=1, source_target_pairs={{0,2},{1,3},{2,0},{3,1},{4,6},{5,7},{6,4},{7,5},{8,10},{9,11},{10,... | collective-permute-start | bytes 1179656 | tf_op jit(solution)/shard_map/ppermute | solution.py:317
  5.2 0.7 copy-done.3
  5.9 0.7 copy-done.5
  6.5 4.0 %prepare.1 = (bf16[32,64,2048]{2,1,0:T(8,128)(2,1)S(1)}, bf16[132,64,384]{2,1,0:T(8,128)(2,1)S(1)}, f32[2,8,128]{2,1,0:T(8,128)S(1)}, s32[32]{0:T(128)S(1)}, s32...) custom-call(s32[1]{0:T(128)} %bitcast.me_ref, s32[8]{0:T(128)S(1)} %copy-done.3, s32[32]{0:T(128)S(1)} %copy-done.5), custom_call_target="tpu_custom_call" | custom-call | bytes 8388608 | tf_op jit(solution)/shard_map/prepare/pallas_call | solution.py:135
  10.6 3.5 %collective-permute-done.refs_0_ = bf16[8,64,384]{2,1,0:T(8,128)(2,1)S(1)} collective-permute-done((bf16[8,64,384]{2,1,0:T(8,128)(2,1)}, bf16[8,64,384]{2,1,0:T(8,128)(2,1)S(1)}, u32[]{:S(2)}, u32[]{:S(2)}) %collective-permute-start) | collective-permute-done | bytes 393248 | tf_op jit(solution)/shard_map/ppermute | solution.py:314
  14.0 0.0 collective-permute-done.1.refs_2_
  14.0 0.9 %collective-permute-start.2 = (bf16[8,64,384]{2,1,0:T(8,128)(2,1)S(1)}, bf16[8,64,384]{2,1,0:T(8,128)(2,1)S(1)}, u32[]{:S(2)}, u32[]{:S(2)}) collective-permute-start(bf16[8,64,384]{2,1,0:T(8,128)(2,1)S(1)} %collective-permute-done.refs_0_), channel_id=1, source_target_pairs={{0,4},{1,5},{2,6},{3,7},{4,12},{5,13},{6,14},{7,15},{8,0},{9,1},{1... | collective-permute-start | bytes 1179656 | tf_op jit(solution)/shard_map/ppermute | solution.py:314
  15.0 1.5 %collective-permute-start.8 = (bf16[8,64,384]{2,1,0:T(8,128)(2,1)S(1)}, bf16[8,64,384]{2,1,0:T(8,128)(2,1)S(1)}, u32[]{:S(2)}, u32[]{:S(2)}) collective-permute-start(bf16[8,64,384]{2,1,0:T(8,128)(2,1)S(1)} %collective-permute-done.refs_0_), channel_id=1, source_target_pairs={{0,2},{1,3},{2,0},{3,1},{4,6},{5,7},{6,4},{7,5},{8,10},{9,11},{10,... | collective-permute-start | bytes 1179656 | tf_op jit(solution)/shard_map/ppermute | solution.py:317
  16.5 0.2 collective-permute-start.9
  16.7 1.4 %copy-done = bf16[32,64,384]{2,1,0:T(8,128)(2,1)S(1)} copy-done((bf16[32,64,384]{2,1,0:T(8,128)(2,1)S(1)}, bf16[32,64,384]{2,1,0:T(8,128)(2,1)}, u32[]{:S(2)}) %copy-start) | copy-done | bytes 1572888
  18.2 1.0 %copy-done.2 = bf16[8,64,384]{2,1,0:T(8,128)(2,1)S(1)} copy-done((bf16[8,64,384]{2,1,0:T(8,128)(2,1)S(1)}, bf16[8,64,384]{2,1,0:T(8,128)(2,1)}, u32[]{:S(2)}) %copy-start.2) | copy-done | bytes 393240
  19.1 0.7 copy-done.4
  19.8 2.6 %ladder_0.1 = (bf16[32,64,2048]{2,1,0:T(8,128)(2,1)S(1)}, bf16[132,64,384]{2,1,0:T(8,128)(2,1)S(1)}, f32[2,8,128]{2,1,0:T(8,128)S(1)}) custom-call(s32[1]{0:T(128)} %bitcast.me_ref, s32[8]{0:T(128)S(1)} %copy-done.4, s32[32]{0:T(128)S(1)} %get-tuple-element.49.order_ref, ...), custom_call_target="tpu_custom_call", output_to_operand_aliasing={{0}: (9, {}), {1}: (10, {})} | custom-call | flops 402653184 | bytes 2097152 | tf_op jit(solution)/shard_map/ladder_0/pallas_call | solution.py:252
  22.4 2.9 %collective-permute-done.2.refs_0_ = bf16[8,64,384]{2,1,0:T(8,128)(2,1)S(1)} collective-permute-done((bf16[8,64,384]{2,1,0:T(8,128)(2,1)S(1)}, bf16[8,64,384]{2,1,0:T(8,128)(2,1)S(1)}, u32[]{:S(2)}, u32[]{:S(2)}) %collective-permute-start.2) | collective-permute-done | bytes 393248 | tf_op jit(solution)/shard_map/ppermute | solution.py:314
  25.3 0.0 collective-permute-done.3.refs_2_
  25.3 0.0 collective-permute-start.6
  25.3 1.0 %collective-permute-start.7 = (bf16[8,64,384]{2,1,0:T(8,128)(2,1)S(1)}, bf16[8,64,384]{2,1,0:T(8,128)(2,1)S(1)}, u32[]{:S(2)}, u32[]{:S(2)}) collective-permute-start(bf16[8,64,384]{2,1,0:T(8,128)(2,1)S(1)} %collective-permute-done.2.refs_0_), channel_id=1, source_target_pairs={{0,4},{1,5},{2,6},{3,7},{4,12},{5,13},{6,14},{7,15},{8,0},{9,1},{1... | collective-permute-start | bytes 1179656 | tf_op jit(solution)/shard_map/ppermute | solution.py:314
  26.3 1.3 %collective-permute-start.5 = (bf16[8,64,384]{2,1,0:T(8,128)(2,1)S(1)}, bf16[8,64,384]{2,1,0:T(8,128)(2,1)S(1)}, u32[]{:S(2)}, u32[]{:S(2)}) collective-permute-start(bf16[8,64,384]{2,1,0:T(8,128)(2,1)S(1)} %collective-permute-done.2.refs_0_), channel_id=1, source_target_pairs={{0,2},{1,3},{2,0},{3,1},{4,6},{5,7},{6,4},{7,5},{8,10},{9,11},{10,... | collective-permute-start | bytes 1179656 | tf_op jit(solution)/shard_map/ppermute | solution.py:317
  27.6 0.0 collective-permute-done.8.refs_1_
  27.6 3.1 %ladder_1.1 = (bf16[32,64,2048]{2,1,0:T(8,128)(2,1)S(1)}, bf16[132,64,384]{2,1,0:T(8,128)(2,1)S(1)}, f32[2,8,128]{2,1,0:T(8,128)S(1)}) custom-call(s32[1]{0:T(128)} %bitcast.me_ref, s32[8]{0:T(128)S(1)} %copy-done.4, s32[32]{0:T(128)S(1)} %get-tuple-element.49.order_ref, ...), custom_call_target="tpu_custom_call", output_to_operand_aliasing={{0}: (9, {}), {1}: (10, {})} | custom-call | flops 402653184 | bytes 2097152 | tf_op jit(solution)/shard_map/ladder_1/pallas_call | solution.py:252
  30.8 6.9 %collective-permute-done.7.refs_0_ = bf16[8,64,384]{2,1,0:T(8,128)(2,1)S(1)} collective-permute-done((bf16[8,64,384]{2,1,0:T(8,128)(2,1)S(1)}, bf16[8,64,384]{2,1,0:T(8,128)(2,1)S(1)}, u32[]{:S(2)}, u32[]{:S(2)}) %collective-permute-start.7) | collective-permute-done | bytes 393248 | tf_op jit(solution)/shard_map/ppermute | solution.py:314
  37.7 0.0 collective-permute-start.13
  37.7 1.3 %collective-permute-start.10 = (bf16[4,64,384]{2,1,0:T(8,128)(2,1)S(1)}, bf16[4,64,384]{2,1,0:T(8,128)(2,1)S(1)}, u32[]{:S(2)}, u32[]{:S(2)}) collective-permute-start(bf16[4,64,384]{2,1,0:T(8,128)(2,1)S(1)} %slice.7), channel_id=1, source_target_pairs={{0,2},{1,3},{2,0},{3,1},{4,6},{5,7},{6,4},{7,5},{8,10},{9,11},{10,... | collective-permute-start | bytes 589832 | tf_op jit(solution)/shard_map/ppermute | solution.py:317
  39.0 1.5 %collective-permute-start.11 = (bf16[4,64,384]{2,1,0:T(8,128)(2,1)S(1)}, bf16[4,64,384]{2,1,0:T(8,128)(2,1)S(1)}, u32[]{:S(2)}, u32[]{:S(2)}) collective-permute-start(bf16[4,64,384]{2,1,0:T(8,128)(2,1)S(1)} %slice.8), channel_id=1, source_target_pairs={{0,8},{1,9},{2,10},{3,11},{4,0},{5,1},{6,2},{7,3},{8,12},{9,13},{1... | collective-permute-start | bytes 589832 | tf_op jit(solution)/shard_map/ppermute | solution.py:314
  40.6 4.8 %ladder_2.1 = (bf16[32,64,2048]{2,1,0:T(8,128)(2,1)S(1)}, bf16[132,64,384]{2,1,0:T(8,128)(2,1)S(1)}, f32[2,8,128]{2,1,0:T(8,128)S(1)}) custom-call(s32[1]{0:T(128)} %bitcast.me_ref, s32[8]{0:T(128)S(1)} %copy-done.4, s32[32]{0:T(128)S(1)} %get-tuple-element.49.order_ref, ...), custom_call_target="tpu_custom_call", output_to_operand_aliasing={{0}: (9, {}), {1}: (10, {})} | custom-call | flops 503316480 | bytes 2621440 | tf_op jit(solution)/shard_map/ladder_2/pallas_call | solution.py:252
  45.4 0.0 collective-permute-done.10.refs_0_
  45.4 0.6 collective-permute-done.11.refs_1_
  46.1 0.5 collective-permute-start.15
  46.6 0.0 collective-permute-start.16
  46.6 1.8 %ladder_3.1 = (bf16[32,64,2048]{2,1,0:T(8,128)(2,1)S(1)}, bf16[132,64,384]{2,1,0:T(8,128)(2,1)S(1)}, f32[2,8,128]{2,1,0:T(8,128)S(1)}) custom-call(s32[1]{0:T(128)} %bitcast.me_ref, s32[8]{0:T(128)S(1)} %copy-done.4, s32[32]{0:T(128)S(1)} %get-tuple-element.49.order_ref, ...), custom_call_target="tpu_custom_call", output_to_operand_aliasing={{0}: (9, {}), {1}: (10, {})} | custom-call | flops 100663296 | bytes 524288 | tf_op jit(solution)/shard_map/ladder_3/pallas_call | solution.py:252
  48.4 0.0 collective-permute-done.15.refs_1_
  48.4 3.0 %ladder_4.1 = (bf16[32,64,2048]{2,1,0:T(8,128)(2,1)S(1)}, bf16[132,64,384]{2,1,0:T(8,128)(2,1)S(1)}, f32[2,8,128]{2,1,0:T(8,128)S(1)}) custom-call(s32[1]{0:T(128)} %bitcast.me_ref, s32[8]{0:T(128)S(1)} %copy-done.4, s32[32]{0:T(128)S(1)} %get-tuple-element.49.order_ref, ...), custom_call_target="tpu_custom_call", output_to_operand_aliasing={{0}: (9, {}), {1}: (10, {})} | custom-call | flops 201326592 | bytes 1048576 | tf_op jit(solution)/shard_map/ladder_4/pallas_call | solution.py:252
  51.4 0.6 collective-permute-start.17
  52.0 0.9 %collective-permute-start.18 = (f32[2,8,128]{2,1,0:T(8,128)S(1)}, f32[2,8,128]{2,1,0:T(8,128)S(1)}, u32[]{:S(2)}, u32[]{:S(2)}) collective-permute-start(f32[2,8,128]{2,1,0:T(8,128)S(1)} %get-tuple-element.91), channel_id=1, source_target_pairs={{0,2},{1,3},{2,0},{3,1},{4,6},{5,7},{6,4},{7,5},{8,10},{9,11},{10,... | collective-permute-start | bytes 24584 | tf_op jit(solution)/shard_map/ppermute | solution.py:317
  52.9 0.6 collective-permute-start.19
  53.4 2.0 %deliver_0.1.refs_0_ = bf16[32,64,2048]{2,1,0:T(8,128)(2,1)} custom-call(bf16[32,64,2048]{2,1,0:T(8,128)(2,1)S(1)} %get-tuple-element.93.held_ref), custom_call_target="tpu_custom_call" | custom-call | tf_op jit(solution)/shard_map/deliver_0/pallas_call | solution.py:290
  55.5 0.2 collective-permute-done.18
  55.7 0.3 collective-permute-done.19
  56.0 2.7 %collective-permute-start.20 = (f32[2,8,128]{2,1,0:T(8,128)S(1)}, f32[2,8,128]{2,1,0:T(8,128)S(1)}, u32[]{:S(2)}, u32[]{:S(2)}) collective-permute-start(f32[2,8,128]{2,1,0:T(8,128)S(1)} %add_add_fusion), channel_id=1, source_target_pairs={{0,4},{1,5},{2,6},{3,7},{4,0},{5,1},{6,2},{7,3},{8,12},{9,13},{10,... | collective-permute-start | bytes 24584 | tf_op jit(solution)/shard_map/ppermute | solution.py:317
  58.7 1.2 %collective-permute-start.21 = (f32[2,8,128]{2,1,0:T(8,128)S(1)}, f32[2,8,128]{2,1,0:T(8,128)S(1)}, u32[]{:S(2)}, u32[]{:S(2)}) collective-permute-start(f32[2,8,128]{2,1,0:T(8,128)S(1)} %add_add_fusion), channel_id=1, source_target_pairs={{0,8},{1,9},{2,10},{3,11},{4,12},{5,13},{6,14},{7,15},{8,0},{9,1},... | collective-permute-start | bytes 24584 | tf_op jit(solution)/shard_map/ppermute | solution.py:317
  59.9 1.2 %collective-permute-start.22 = (f32[2,8,128]{2,1,0:T(8,128)S(1)}, f32[2,8,128]{2,1,0:T(8,128)S(1)}, u32[]{:S(2)}, u32[]{:S(2)}) collective-permute-start(f32[2,8,128]{2,1,0:T(8,128)S(1)} %add_add_fusion), channel_id=1, source_target_pairs={{0,12},{1,13},{2,14},{3,15},{4,8},{5,9},{6,10},{7,11},{8,4},{9,5},... | collective-permute-start | bytes 24584 | tf_op jit(solution)/shard_map/ppermute | solution.py:317
  61.1 2.0 %deliver_1.1 = bf16[32,64,2048]{2,1,0:T(8,128)(2,1)} custom-call(bf16[32,64,2048]{2,1,0:T(8,128)(2,1)S(1)} %get-tuple-element.93.held_ref, bf16[32,64,2048]{2,1,0:T(8,128)(2,1)} %deliver_0.1.refs_0_), custom_call_target="tpu_custom_call", output_to_operand_aliasing={{}: (1, {})} | custom-call | tf_op jit(solution)/shard_map/deliver_1/pallas_call | solution.py:290
  63.2 0.1 collective-permute-done.21
  63.3 2.1 %collective-permute-done.22 = f32[2,8,128]{2,1,0:T(8,128)S(1)} collective-permute-done((f32[2,8,128]{2,1,0:T(8,128)S(1)}, f32[2,8,128]{2,1,0:T(8,128)S(1)}, u32[]{:S(2)}, u32[]{:S(2)}) %collective-permute-start.22) | collective-permute-done | bytes 8224 | tf_op jit(solution)/shard_map/ppermute | solution.py:317
  65.4 0.1 add_reduce_fusion
  65.5 0.5 add_sqrt_fusion
  (23 shorter events, 0.1 us)
Async XLA Ops:
  0.6 13.4 %collective-permute-start = (bf16[8,64,384]{2,1,0:T(8,128)(2,1)}, bf16[8,64,384]{2,1,0:T(8,128)(2,1)S(1)}, u32[]{:S(2)}, u32[]{:S(2)}) collective-permute-start(bf16[8,64,384]{2,1,0:T(8,128)(2,1)} %refs_3_.1), channel_id=1, source_target_pairs={{0,4},{1,5},{2,6},{3,7},{4,12},{5,13},{6,14},{7,15},{8,0},{9,1},{1... | collective-permute-start | bytes 1179656 | tf_op jit(solution)/shard_map/ppermute | solution.py:314
  3.7 10.3 %collective-permute-start.1 = (bf16[8,64,384]{2,1,0:T(8,128)(2,1)}, bf16[8,64,384]{2,1,0:T(8,128)(2,1)S(1)}, u32[]{:S(2)}, u32[]{:S(2)}) collective-permute-start(bf16[8,64,384]{2,1,0:T(8,128)(2,1)} %refs_3_.1), channel_id=1, source_target_pairs={{0,1},{1,0},{2,3},{3,2},{4,5},{5,4},{6,7},{7,6},{8,9},{9,8},{10,11... | collective-permute-start | bytes 1179656 | tf_op jit(solution)/shard_map/ppermute | solution.py:317
  3.7 12.8 %collective-permute-start.4 = (bf16[8,64,384]{2,1,0:T(8,128)(2,1)}, bf16[8,64,384]{2,1,0:T(8,128)(2,1)S(1)}, u32[]{:S(2)}, u32[]{:S(2)}) collective-permute-start(bf16[8,64,384]{2,1,0:T(8,128)(2,1)} %refs_3_.1), channel_id=1, source_target_pairs={{0,2},{1,3},{2,0},{3,1},{4,6},{5,7},{6,4},{7,5},{8,10},{9,11},{10,... | collective-permute-start | bytes 1179656 | tf_op jit(solution)/shard_map/ppermute | solution.py:317
  5.2 0.7 copy-start.3
  5.9 0.7 copy-start.5
  14.0 11.2 %collective-permute-start.2 = (bf16[8,64,384]{2,1,0:T(8,128)(2,1)S(1)}, bf16[8,64,384]{2,1,0:T(8,128)(2,1)S(1)}, u32[]{:S(2)}, u32[]{:S(2)}) collective-permute-start(bf16[8,64,384]{2,1,0:T(8,128)(2,1)S(1)} %collective-permute-done.refs_0_), channel_id=1, source_target_pairs={{0,4},{1,5},{2,6},{3,7},{4,12},{5,13},{6,14},{7,15},{8,0},{9,1},{1... | collective-permute-start | bytes 1179656 | tf_op jit(solution)/shard_map/ppermute | solution.py:314
  15.0 10.3 %collective-permute-start.3 = (bf16[8,64,384]{2,1,0:T(8,128)(2,1)S(1)}, bf16[8,64,384]{2,1,0:T(8,128)(2,1)S(1)}, u32[]{:S(2)}, u32[]{:S(2)}) collective-permute-start(bf16[8,64,384]{2,1,0:T(8,128)(2,1)S(1)} %collective-permute-done.refs_0_), channel_id=1, source_target_pairs={{0,1},{1,0},{2,3},{3,2},{4,5},{5,4},{6,7},{7,6},{8,9},{9,8},{10,11... | collective-permute-start | bytes 1179656 | tf_op jit(solution)/shard_map/ppermute | solution.py:317
  15.0 12.6 %collective-permute-start.8 = (bf16[8,64,384]{2,1,0:T(8,128)(2,1)S(1)}, bf16[8,64,384]{2,1,0:T(8,128)(2,1)S(1)}, u32[]{:S(2)}, u32[]{:S(2)}) collective-permute-start(bf16[8,64,384]{2,1,0:T(8,128)(2,1)S(1)} %collective-permute-done.refs_0_), channel_id=1, source_target_pairs={{0,2},{1,3},{2,0},{3,1},{4,6},{5,7},{6,4},{7,5},{8,10},{9,11},{10,... | collective-permute-start | bytes 1179656 | tf_op jit(solution)/shard_map/ppermute | solution.py:317
  16.5 11.1 %collective-permute-start.9 = (bf16[8,64,384]{2,1,0:T(8,128)(2,1)S(1)}, bf16[8,64,384]{2,1,0:T(8,128)(2,1)S(1)}, u32[]{:S(2)}, u32[]{:S(2)}) collective-permute-start(bf16[8,64,384]{2,1,0:T(8,128)(2,1)S(1)} %collective-permute-done.4.refs_1_), channel_id=1, source_target_pairs={{0,1},{1,0},{2,3},{3,2},{4,5},{5,4},{6,7},{7,6},{8,9},{9,8},{10,11... | collective-permute-start | bytes 1179656 | tf_op jit(solution)/shard_map/ppermute | solution.py:317
  16.7 1.4 %copy-start = (bf16[32,64,384]{2,1,0:T(8,128)(2,1)S(1)}, bf16[32,64,384]{2,1,0:T(8,128)(2,1)}, u32[]{:S(2)}) copy-start(bf16[32,64,384]{2,1,0:T(8,128)(2,1)} %v_ref.9) | copy-start | bytes 4718596
  18.2 1.0 %copy-start.2 = (bf16[8,64,384]{2,1,0:T(8,128)(2,1)S(1)}, bf16[8,64,384]{2,1,0:T(8,128)(2,1)}, u32[]{:S(2)}) copy-start(bf16[8,64,384]{2,1,0:T(8,128)(2,1)} %refs_3_.1) | copy-start | bytes 1179652
  19.1 0.7 copy-start.4
  19.8 7.8 %copy-start.1 = (bf16[32,64,384]{2,1,0:T(8,128)(2,1)S(1)}, bf16[32,64,384]{2,1,0:T(8,128)(2,1)}, u32[]{:S(2)}) copy-start(bf16[32,64,384]{2,1,0:T(8,128)(2,1)} %v_ref.9) | copy-start | bytes 4718596
  25.3 5.5 %collective-permute-start.6 = (bf16[8,64,384]{2,1,0:T(8,128)(2,1)S(1)}, bf16[8,64,384]{2,1,0:T(8,128)(2,1)S(1)}, u32[]{:S(2)}, u32[]{:S(2)}) collective-permute-start(bf16[8,64,384]{2,1,0:T(8,128)(2,1)S(1)} %collective-permute-done.2.refs_0_), channel_id=1, source_target_pairs={{0,1},{1,0},{2,3},{3,2},{4,5},{5,4},{6,7},{7,6},{8,9},{9,8},{10,11... | collective-permute-start | bytes 1179656 | tf_op jit(solution)/shard_map/ppermute | solution.py:317
  25.3 12.4 %collective-permute-start.7 = (bf16[8,64,384]{2,1,0:T(8,128)(2,1)S(1)}, bf16[8,64,384]{2,1,0:T(8,128)(2,1)S(1)}, u32[]{:S(2)}, u32[]{:S(2)}) collective-permute-start(bf16[8,64,384]{2,1,0:T(8,128)(2,1)S(1)} %collective-permute-done.2.refs_0_), channel_id=1, source_target_pairs={{0,4},{1,5},{2,6},{3,7},{4,12},{5,13},{6,14},{7,15},{8,0},{9,1},{1... | collective-permute-start | bytes 1179656 | tf_op jit(solution)/shard_map/ppermute | solution.py:314
  26.3 14.2 %collective-permute-start.5 = (bf16[8,64,384]{2,1,0:T(8,128)(2,1)S(1)}, bf16[8,64,384]{2,1,0:T(8,128)(2,1)S(1)}, u32[]{:S(2)}, u32[]{:S(2)}) collective-permute-start(bf16[8,64,384]{2,1,0:T(8,128)(2,1)S(1)} %collective-permute-done.2.refs_0_), channel_id=1, source_target_pairs={{0,2},{1,3},{2,0},{3,1},{4,6},{5,7},{6,4},{7,5},{8,10},{9,11},{10,... | collective-permute-start | bytes 1179656 | tf_op jit(solution)/shard_map/ppermute | solution.py:317
  27.6 12.9 %collective-permute-start.12 = (bf16[8,64,384]{2,1,0:T(8,128)(2,1)S(1)}, bf16[8,64,384]{2,1,0:T(8,128)(2,1)S(1)}, u32[]{:S(2)}, u32[]{:S(2)}) collective-permute-start(bf16[8,64,384]{2,1,0:T(8,128)(2,1)S(1)} %collective-permute-done.8.refs_1_), channel_id=1, source_target_pairs={{0,1},{1,0},{2,3},{3,2},{4,5},{5,4},{6,7},{7,6},{8,9},{9,8},{10,11... | collective-permute-start | bytes 1179656 | tf_op jit(solution)/shard_map/ppermute | solution.py:317
  37.7 2.9 %collective-permute-start.13 = (bf16[8,64,384]{2,1,0:T(8,128)(2,1)S(1)}, bf16[8,64,384]{2,1,0:T(8,128)(2,1)S(1)}, u32[]{:S(2)}, u32[]{:S(2)}) collective-permute-start(bf16[8,64,384]{2,1,0:T(8,128)(2,1)S(1)} %collective-permute-done.7.refs_0_), channel_id=1, source_target_pairs={{0,1},{1,0},{2,3},{3,2},{4,5},{5,4},{6,7},{7,6},{8,9},{9,8},{10,11... | collective-permute-start | bytes 1179656 | tf_op jit(solution)/shard_map/ppermute | solution.py:317
  37.7 7.7 %collective-permute-start.10 = (bf16[4,64,384]{2,1,0:T(8,128)(2,1)S(1)}, bf16[4,64,384]{2,1,0:T(8,128)(2,1)S(1)}, u32[]{:S(2)}, u32[]{:S(2)}) collective-permute-start(bf16[4,64,384]{2,1,0:T(8,128)(2,1)S(1)} %slice.7), channel_id=1, source_target_pairs={{0,2},{1,3},{2,0},{3,1},{4,6},{5,7},{6,4},{7,5},{8,10},{9,11},{10,... | collective-permute-start | bytes 589832 | tf_op jit(solution)/shard_map/ppermute | solution.py:317
  39.0 7.0 %collective-permute-start.11 = (bf16[4,64,384]{2,1,0:T(8,128)(2,1)S(1)}, bf16[4,64,384]{2,1,0:T(8,128)(2,1)S(1)}, u32[]{:S(2)}, u32[]{:S(2)}) collective-permute-start(bf16[4,64,384]{2,1,0:T(8,128)(2,1)S(1)} %slice.8), channel_id=1, source_target_pairs={{0,8},{1,9},{2,10},{3,11},{4,0},{5,1},{6,2},{7,3},{8,12},{9,13},{1... | collective-permute-start | bytes 589832 | tf_op jit(solution)/shard_map/ppermute | solution.py:314
  46.1 2.3 %collective-permute-start.14 = (bf16[8,64,384]{2,1,0:T(8,128)(2,1)S(1)}, bf16[8,64,384]{2,1,0:T(8,128)(2,1)S(1)}, u32[]{:S(2)}, u32[]{:S(2)}) collective-permute-start(bf16[8,64,384]{2,1,0:T(8,128)(2,1)S(1)} %collective-permute-done.5.refs_1_), channel_id=1, source_target_pairs={{0,1},{1,0},{2,3},{3,2},{4,5},{5,4},{6,7},{7,6},{8,9},{9,8},{10,11... | collective-permute-start | bytes 1179656 | tf_op jit(solution)/shard_map/ppermute | solution.py:317
  46.1 2.3 %collective-permute-start.15 = (bf16[4,64,384]{2,1,0:T(8,128)(2,1)S(1)}, bf16[4,64,384]{2,1,0:T(8,128)(2,1)S(1)}, u32[]{:S(2)}, u32[]{:S(2)}) collective-permute-start(bf16[4,64,384]{2,1,0:T(8,128)(2,1)S(1)} %collective-permute-done.10.refs_0_), channel_id=1, source_target_pairs={{0,1},{1,0},{2,3},{3,2},{4,5},{5,4},{6,7},{7,6},{8,9},{9,8},{10,11... | collective-permute-start | bytes 589832 | tf_op jit(solution)/shard_map/ppermute | solution.py:317
  46.6 1.8 %collective-permute-start.16 = (bf16[4,64,384]{2,1,0:T(8,128)(2,1)S(1)}, bf16[4,64,384]{2,1,0:T(8,128)(2,1)S(1)}, u32[]{:S(2)}, u32[]{:S(2)}) collective-permute-start(bf16[4,64,384]{2,1,0:T(8,128)(2,1)S(1)} %collective-permute-done.11.refs_1_), channel_id=1, source_target_pairs={{0,1},{1,0},{2,3},{3,2},{4,5},{5,4},{6,7},{7,6},{8,9},{9,8},{10,11... | collective-permute-start | bytes 589832 | tf_op jit(solution)/shard_map/ppermute | solution.py:317
  51.4 4.0 %collective-permute-start.17 = (f32[2,8,128]{2,1,0:T(8,128)S(1)}, f32[2,8,128]{2,1,0:T(8,128)S(1)}, u32[]{:S(2)}, u32[]{:S(2)}) collective-permute-start(f32[2,8,128]{2,1,0:T(8,128)S(1)} %get-tuple-element.91), channel_id=1, source_target_pairs={{0,1},{1,0},{2,3},{3,2},{4,5},{5,4},{6,7},{7,6},{8,9},{9,8},{10,11... | collective-permute-start | bytes 24584 | tf_op jit(solution)/shard_map/ppermute | solution.py:317
  52.0 3.7 %collective-permute-start.18 = (f32[2,8,128]{2,1,0:T(8,128)S(1)}, f32[2,8,128]{2,1,0:T(8,128)S(1)}, u32[]{:S(2)}, u32[]{:S(2)}) collective-permute-start(f32[2,8,128]{2,1,0:T(8,128)S(1)} %get-tuple-element.91), channel_id=1, source_target_pairs={{0,2},{1,3},{2,0},{3,1},{4,6},{5,7},{6,4},{7,5},{8,10},{9,11},{10,... | collective-permute-start | bytes 24584 | tf_op jit(solution)/shard_map/ppermute | solution.py:317
  52.9 3.1 %collective-permute-start.19 = (f32[2,8,128]{2,1,0:T(8,128)S(1)}, f32[2,8,128]{2,1,0:T(8,128)S(1)}, u32[]{:S(2)}, u32[]{:S(2)}) collective-permute-start(f32[2,8,128]{2,1,0:T(8,128)S(1)} %get-tuple-element.91), channel_id=1, source_target_pairs={{0,3},{1,2},{2,1},{3,0},{4,7},{5,6},{6,5},{7,4},{8,11},{9,10},{10,... | collective-permute-start | bytes 24584 | tf_op jit(solution)/shard_map/ppermute | solution.py:317
  56.0 7.2 %collective-permute-start.20 = (f32[2,8,128]{2,1,0:T(8,128)S(1)}, f32[2,8,128]{2,1,0:T(8,128)S(1)}, u32[]{:S(2)}, u32[]{:S(2)}) collective-permute-start(f32[2,8,128]{2,1,0:T(8,128)S(1)} %add_add_fusion), channel_id=1, source_target_pairs={{0,4},{1,5},{2,6},{3,7},{4,0},{5,1},{6,2},{7,3},{8,12},{9,13},{10,... | collective-permute-start | bytes 24584 | tf_op jit(solution)/shard_map/ppermute | solution.py:317
  58.7 4.5 %collective-permute-start.21 = (f32[2,8,128]{2,1,0:T(8,128)S(1)}, f32[2,8,128]{2,1,0:T(8,128)S(1)}, u32[]{:S(2)}, u32[]{:S(2)}) collective-permute-start(f32[2,8,128]{2,1,0:T(8,128)S(1)} %add_add_fusion), channel_id=1, source_target_pairs={{0,8},{1,9},{2,10},{3,11},{4,12},{5,13},{6,14},{7,15},{8,0},{9,1},... | collective-permute-start | bytes 24584 | tf_op jit(solution)/shard_map/ppermute | solution.py:317
  59.9 5.4 %collective-permute-start.22 = (f32[2,8,128]{2,1,0:T(8,128)S(1)}, f32[2,8,128]{2,1,0:T(8,128)S(1)}, u32[]{:S(2)}, u32[]{:S(2)}) collective-permute-start(f32[2,8,128]{2,1,0:T(8,128)S(1)} %add_add_fusion), channel_id=1, source_target_pairs={{0,12},{1,13},{2,14},{3,15},{4,8},{5,9},{6,10},{7,11},{8,4},{9,5},... | collective-permute-start | bytes 24584 | tf_op jit(solution)/shard_map/ppermute | solution.py:317

commit v16 on v15

--- a/solution.py
+++ b/solution.py
@@ -27,7 +27,7 @@
 
 def call_of(depth, lag, other_y, other_core):
     if other_y:
-        return depth if other_core and lag >= depth - 2 else lag + other_core
+        return lag + other_core
     return min(lag, depth - 2) if other_core else max(lag - 1, 0)
 
 
@@ -330,7 +330,7 @@
             b.append(swap(a[k], 2))
             a.append(shift_z(a[k], 1))
         else:
-            part = shard_tiles // 2
+            part = 3 * shard_tiles // 8
             c[-1], a[k], back, state = lax.optimization_barrier(
                 (c[-1], a[k], b[0][part:], state)
             )
@@ -348,10 +348,12 @@
         else:
             fresh[k, 0, 1, 0] = c[k]
         state = ladder(k - 1, depth, shard_tiles, integrals, listing, state, fresh)
-    b[-1], last, state = lax.optimization_barrier((b[-1], last, state))
-    first, second = {}, {(k - 1, 1, 1, 0): swap(b[k - 1], 1)}
+    b[-1], last[0], state = lax.optimization_barrier((b[-1], last[0], state))
+    first, second = {(k - 1, 1, 1, 0): swap(b[-1], 1)}, {(k, 1, 1, 0): swap(last[0], 1)}
+    last[part], state = lax.optimization_barrier((last[part], state))
+    second[k, 1, 1, part] = swap(last[part], 1)
     for tile, piece in last.items():
-        first[k, 1, 0, tile], second[k, 1, 1, tile] = piece, swap(piece, 1)
+        first[k, 1, 0, tile] = piece
     for number, fresh in ((k, first), (k + 1, second)):
         state = ladder(number, depth, shard_tiles, integrals, listing, state, fresh)
 

time: 66.1 us -> 66.8 us (1.011)
  waiting for transfers between devices: 16.6 us -> 18.4 us
  Pallas kernels: 23.4 us -> 21.8 us
    ppermute x4, waiting for transfers between devices: 13.9 us -> 16.2 us  [shift_z(): return lax.ppermute(x, 'vir', pairs)]
    pallas_call x5, Pallas kernels: 15.3 us -> 13.8 us  [ladder(): pl.pallas_call(functools.partial(ladder_kernel, call, depth, shard_tiles,...]
  transfers between devices with their start and end apart: 23 -> 23, of which waited for: 8 -> 8; matrix products, arithmetic and copies ran while one was open for 0% -> 0% of each run, Pallas kernels for 31% -> 30%
where the time goes in v16:
time: 66.8 us; the launch traced here: 66.3 us
  Pallas kernels  21.8 us (33%)
  starting transfers between devices  20.3 us (30%)
  waiting for transfers between devices  18.4 us (28%)
  local copies, waits for them, and re-layouts  4.41 us (7%)
  between operations  0.8 us (1%)
    ppermute x4, waiting for transfers between devices, shift_z(): return lax.ppermute(x, 'vir', pairs)  16.2 us
    ppermute x19, starting transfers between devices, swap(): return lax.ppermute(x, 'vir', [(d, d ^ bits) for d in range(devices)])  14 us
    pallas_call x5, Pallas kernels, ladder(): pl.pallas_call(functools.partial(ladder_kernel, call, depth, shard_tiles,...  13.8 us
    ppermute x4, starting transfers between devices, shift_z(): return lax.ppermute(x, 'vir', pairs)  6.3 us
    unnamed x12, local copies, waits for them, and re-layouts  4.37 us
    pallas_call x2, Pallas kernels, deliver(): pl.pallas_call(functools.partial(deliver_kernel, part), out_shape=jax.Sha...  4.04 us
    pallas_call x1, Pallas kernels, prepare(): pl.pallas_call(functools.partial(prepare_kernel, depth, shard_tiles), out...  3.98 us
    ppermute x19, waiting for transfers between devices, swap(): return lax.ppermute(x, 'vir', [(d, d ^ bits) for d in range(devices)])  2.18 us
  transfers between devices with their start and end apart: 23, of which 8 were waited for; matrix products, arithmetic and copies ran while one was open for 0% of the time, Pallas kernels for 30%

profile of v16, /device:TPU:0, one launch (start us, length us, event | category | flops | bytes accessed | tf_op | source)
XLA Modules:
  0.0 66.3 jit_solution(17183771694604375823)
XLA Ops:
  0.6 3.1 %collective-permute-start = (bf16[8,64,384]{2,1,0:T(8,128)(2,1)}, bf16[8,64,384]{2,1,0:T(8,128)(2,1)S(1)}, u32[]{:S(2)}, u32[]{:S(2)}) collective-permute-start(bf16[8,64,384]{2,1,0:T(8,128)(2,1)} %refs_3_.1), channel_id=1, source_target_pairs={{0,4},{1,5},{2,6},{3,7},{4,12},{5,13},{6,14},{7,15},{8,0},{9,1},{1... | collective-permute-start | bytes 1179656 | tf_op jit(solution)/shard_map/ppermute | solution.py:314
  3.7 1.5 %collective-permute-start.4 = (bf16[8,64,384]{2,1,0:T(8,128)(2,1)}, bf16[8,64,384]{2,1,0:T(8,128)(2,1)S(1)}, u32[]{:S(2)}, u32[]{:S(2)}) collective-permute-start(bf16[8,64,384]{2,1,0:T(8,128)(2,1)} %refs_3_.1), channel_id=1, source_target_pairs={{0,2},{1,3},{2,0},{3,1},{4,6},{5,7},{6,4},{7,5},{8,10},{9,11},{10,... | collective-permute-start | bytes 1179656 | tf_op jit(solution)/shard_map/ppermute | solution.py:317
  5.2 0.7 copy-done.3
  5.9 0.7 copy-done.5
  6.5 4.0 %prepare.1 = (bf16[32,64,2048]{2,1,0:T(8,128)(2,1)S(1)}, bf16[132,64,384]{2,1,0:T(8,128)(2,1)S(1)}, f32[2,8,128]{2,1,0:T(8,128)S(1)}, s32[32]{0:T(128)S(1)}, s32...) custom-call(s32[1]{0:T(128)} %bitcast.me_ref, s32[8]{0:T(128)S(1)} %copy-done.3, s32[32]{0:T(128)S(1)} %copy-done.5), custom_call_target="tpu_custom_call" | custom-call | bytes 8388608 | tf_op jit(solution)/shard_map/prepare/pallas_call | solution.py:135
  10.5 3.5 %collective-permute-done.refs_0_ = bf16[8,64,384]{2,1,0:T(8,128)(2,1)S(1)} collective-permute-done((bf16[8,64,384]{2,1,0:T(8,128)(2,1)}, bf16[8,64,384]{2,1,0:T(8,128)(2,1)S(1)}, u32[]{:S(2)}, u32[]{:S(2)}) %collective-permute-start) | collective-permute-done | bytes 393248 | tf_op jit(solution)/shard_map/ppermute | solution.py:314
  14.0 0.9 %collective-permute-start.2 = (bf16[8,64,384]{2,1,0:T(8,128)(2,1)S(1)}, bf16[8,64,384]{2,1,0:T(8,128)(2,1)S(1)}, u32[]{:S(2)}, u32[]{:S(2)}) collective-permute-start(bf16[8,64,384]{2,1,0:T(8,128)(2,1)S(1)} %collective-permute-done.refs_0_), channel_id=1, source_target_pairs={{0,4},{1,5},{2,6},{3,7},{4,12},{5,13},{6,14},{7,15},{8,0},{9,1},{1... | collective-permute-start | bytes 1179656 | tf_op jit(solution)/shard_map/ppermute | solution.py:314
  15.0 0.0 collective-permute-start.3
  15.0 1.5 %collective-permute-start.7 = (bf16[8,64,384]{2,1,0:T(8,128)(2,1)S(1)}, bf16[8,64,384]{2,1,0:T(8,128)(2,1)S(1)}, u32[]{:S(2)}, u32[]{:S(2)}) collective-permute-start(bf16[8,64,384]{2,1,0:T(8,128)(2,1)S(1)} %collective-permute-done.refs_0_), channel_id=1, source_target_pairs={{0,2},{1,3},{2,0},{3,1},{4,6},{5,7},{6,4},{7,5},{8,10},{9,11},{10,... | collective-permute-start | bytes 1179656 | tf_op jit(solution)/shard_map/ppermute | solution.py:317
  16.5 0.0 collective-permute-done.4.refs_1_
  16.5 0.2 collective-permute-start.8
  16.7 1.4 %copy-done = bf16[32,64,384]{2,1,0:T(8,128)(2,1)S(1)} copy-done((bf16[32,64,384]{2,1,0:T(8,128)(2,1)S(1)}, bf16[32,64,384]{2,1,0:T(8,128)(2,1)}, u32[]{:S(2)}) %copy-start) | copy-done | bytes 1572888
  18.2 1.0 %copy-done.2 = bf16[8,64,384]{2,1,0:T(8,128)(2,1)S(1)} copy-done((bf16[8,64,384]{2,1,0:T(8,128)(2,1)S(1)}, bf16[8,64,384]{2,1,0:T(8,128)(2,1)}, u32[]{:S(2)}) %copy-start.2) | copy-done | bytes 393240
  19.1 0.7 copy-done.4
  19.8 2.6 %ladder_0.1 = (bf16[32,64,2048]{2,1,0:T(8,128)(2,1)S(1)}, bf16[132,64,384]{2,1,0:T(8,128)(2,1)S(1)}, f32[2,8,128]{2,1,0:T(8,128)S(1)}) custom-call(s32[1]{0:T(128)} %bitcast.me_ref, s32[8]{0:T(128)S(1)} %copy-done.4, s32[32]{0:T(128)S(1)} %get-tuple-element.52.order_ref, ...), custom_call_target="tpu_custom_call", output_to_operand_aliasing={{0}: (9, {}), {1}: (10, {})} | custom-call | flops 402653184 | bytes 2097152 | tf_op jit(solution)/shard_map/ladder_0/pallas_call | solution.py:252
  22.4 2.9 %collective-permute-done.2.refs_0_ = bf16[8,64,384]{2,1,0:T(8,128)(2,1)S(1)} collective-permute-done((bf16[8,64,384]{2,1,0:T(8,128)(2,1)S(1)}, bf16[8,64,384]{2,1,0:T(8,128)(2,1)S(1)}, u32[]{:S(2)}, u32[]{:S(2)}) %collective-permute-start.2) | collective-permute-done | bytes 393248 | tf_op jit(solution)/shard_map/ppermute | solution.py:314
  25.3 0.8 %collective-permute-start.6 = (bf16[8,64,384]{2,1,0:T(8,128)(2,1)S(1)}, bf16[8,64,384]{2,1,0:T(8,128)(2,1)S(1)}, u32[]{:S(2)}, u32[]{:S(2)}) collective-permute-start(bf16[8,64,384]{2,1,0:T(8,128)(2,1)S(1)} %collective-permute-done.2.refs_0_), channel_id=1, source_target_pairs={{0,4},{1,5},{2,6},{3,7},{4,12},{5,13},{6,14},{7,15},{8,0},{9,1},{1... | collective-permute-start | bytes 1179656 | tf_op jit(solution)/shard_map/ppermute | solution.py:314
  26.0 1.3 %collective-permute-start.10 = (bf16[8,64,384]{2,1,0:T(8,128)(2,1)S(1)}, bf16[8,64,384]{2,1,0:T(8,128)(2,1)S(1)}, u32[]{:S(2)}, u32[]{:S(2)}) collective-permute-start(bf16[8,64,384]{2,1,0:T(8,128)(2,1)S(1)} %collective-permute-done.2.refs_0_), channel_id=1, source_target_pairs={{0,2},{1,3},{2,0},{3,1},{4,6},{5,7},{6,4},{7,5},{8,10},{9,11},{10,... | collective-permute-start | bytes 1179656 | tf_op jit(solution)/shard_map/ppermute | solution.py:317
  27.4 0.0 collective-permute-done.7.refs_1_
  27.4 0.0 collective-permute-start.12
  27.4 0.0 collective-permute-done.8.refs_3_
  27.4 2.6 %ladder_1.1 = (bf16[32,64,2048]{2,1,0:T(8,128)(2,1)S(1)}, bf16[132,64,384]{2,1,0:T(8,128)(2,1)S(1)}, f32[2,8,128]{2,1,0:T(8,128)S(1)}) custom-call(s32[1]{0:T(128)} %bitcast.me_ref, s32[8]{0:T(128)S(1)} %copy-done.4, s32[32]{0:T(128)S(1)} %get-tuple-element.52.order_ref, ...), custom_call_target="tpu_custom_call", output_to_operand_aliasing={{0}: (9, {}), {1}: (10, {})} | custom-call | flops 402653184 | bytes 2097152 | tf_op jit(solution)/shard_map/ladder_1/pallas_call | solution.py:252
  30.0 7.7 %collective-permute-done.6.refs_0_ = bf16[8,64,384]{2,1,0:T(8,128)(2,1)S(1)} collective-permute-done((bf16[8,64,384]{2,1,0:T(8,128)(2,1)S(1)}, bf16[8,64,384]{2,1,0:T(8,128)(2,1)S(1)}, u32[]{:S(2)}, u32[]{:S(2)}) %collective-permute-start.6) | collective-permute-done | bytes 393248 | tf_op jit(solution)/shard_map/ppermute | solution.py:314
  37.7 0.0 collective-permute-start.13
  37.7 1.3 %collective-permute-start.11 = (bf16[3,64,384]{2,1,0:T(8,128)(2,1)S(1)}, bf16[3,64,384]{2,1,0:T(8,128)(2,1)S(1)}, u32[]{:S(2)}, u32[]{:S(2)}) collective-permute-start(bf16[3,64,384]{2,1,0:T(8,128)(2,1)S(1)} %slice.7), channel_id=1, source_target_pairs={{0,2},{1,3},{2,0},{3,1},{4,6},{5,7},{6,4},{7,5},{8,10},{9,11},{10,... | collective-permute-start | bytes 442376 | tf_op jit(solution)/shard_map/ppermute | solution.py:317
  39.0 1.5 %collective-permute-start.9 = (bf16[5,64,384]{2,1,0:T(8,128)(2,1)S(1)}, bf16[5,64,384]{2,1,0:T(8,128)(2,1)S(1)}, u32[]{:S(2)}, u32[]{:S(2)}) collective-permute-start(bf16[5,64,384]{2,1,0:T(8,128)(2,1)S(1)} %slice.8), channel_id=1, source_target_pairs={{0,8},{1,9},{2,10},{3,11},{4,0},{5,1},{6,2},{7,3},{8,12},{9,13},{1... | collective-permute-start | bytes 737288 | tf_op jit(solution)/shard_map/ppermute | solution.py:314
  40.5 0.0 collective-permute-done.10.refs_1_
  40.5 0.0 collective-permute-done.12.refs_3_
  40.6 4.3 %ladder_2.1 = (bf16[32,64,2048]{2,1,0:T(8,128)(2,1)S(1)}, bf16[132,64,384]{2,1,0:T(8,128)(2,1)S(1)}, f32[2,8,128]{2,1,0:T(8,128)S(1)}) custom-call(s32[1]{0:T(128)} %bitcast.me_ref, s32[8]{0:T(128)S(1)} %copy-done.4, s32[32]{0:T(128)S(1)} %get-tuple-element.52.order_ref, ...), custom_call_target="tpu_custom_call", output_to_operand_aliasing={{0}: (9, {}), {1}: (10, {})} | custom-call | flops 503316480 | bytes 2621440 | tf_op jit(solution)/shard_map/ladder_2/pallas_call | solution.py:252
  44.9 0.1 collective-permute-start.14
  45.0 2.1 %collective-permute-done.9.refs_1_ = bf16[5,64,384]{2,1,0:T(8,128)(2,1)S(1)} collective-permute-done((bf16[5,64,384]{2,1,0:T(8,128)(2,1)S(1)}, bf16[5,64,384]{2,1,0:T(8,128)(2,1)S(1)}, u32[]{:S(2)}, u32[]{:S(2)}) %collective-permute-start.9) | collective-permute-done | bytes 245792 | tf_op jit(solution)/shard_map/ppermute | solution.py:314
  47.1 0.5 collective-permute-start.15
  47.6 2.5 %ladder_3.1 = (bf16[32,64,2048]{2,1,0:T(8,128)(2,1)S(1)}, bf16[132,64,384]{2,1,0:T(8,128)(2,1)S(1)}, f32[2,8,128]{2,1,0:T(8,128)S(1)}) custom-call(s32[1]{0:T(128)} %bitcast.me_ref, s32[8]{0:T(128)S(1)} %copy-done.4, s32[32]{0:T(128)S(1)} %get-tuple-element.52.order_ref, ...), custom_call_target="tpu_custom_call", output_to_operand_aliasing={{0}: (9, {}), {1}: (10, {})} | custom-call | flops 201326592 | bytes 1048576 | tf_op jit(solution)/shard_map/ladder_3/pallas_call | solution.py:252
  50.2 1.8 %ladder_4.1 = (bf16[32,64,2048]{2,1,0:T(8,128)(2,1)S(1)}, bf16[132,64,384]{2,1,0:T(8,128)(2,1)S(1)}, f32[2,8,128]{2,1,0:T(8,128)S(1)}) custom-call(s32[1]{0:T(128)} %bitcast.me_ref, s32[8]{0:T(128)S(1)} %copy-done.4, s32[32]{0:T(128)S(1)} %get-tuple-element.52.order_ref, ...), custom_call_target="tpu_custom_call", output_to_operand_aliasing={{0}: (9, {}), {1}: (10, {})} | custom-call | flops 100663296 | bytes 524288 | tf_op jit(solution)/shard_map/ladder_4/pallas_call | solution.py:252
  52.0 0.6 collective-permute-start.17
  52.6 0.8 %collective-permute-start.18 = (f32[2,8,128]{2,1,0:T(8,128)S(1)}, f32[2,8,128]{2,1,0:T(8,128)S(1)}, u32[]{:S(2)}, u32[]{:S(2)}) collective-permute-start(f32[2,8,128]{2,1,0:T(8,128)S(1)} %get-tuple-element.97), channel_id=1, source_target_pairs={{0,2},{1,3},{2,0},{3,1},{4,6},{5,7},{6,4},{7,5},{8,10},{9,11},{10,... | collective-permute-start | bytes 24584 | tf_op jit(solution)/shard_map/ppermute | solution.py:317
  53.4 0.6 collective-permute-start.19
  54.0 2.0 %deliver_0.1.refs_0_ = bf16[32,64,2048]{2,1,0:T(8,128)(2,1)} custom-call(bf16[32,64,2048]{2,1,0:T(8,128)(2,1)S(1)} %get-tuple-element.99.held_ref), custom_call_target="tpu_custom_call" | custom-call | tf_op jit(solution)/shard_map/deliver_0/pallas_call | solution.py:290
  56.0 0.2 collective-permute-done.18
  56.2 0.3 collective-permute-done.19
  56.5 3.0 %collective-permute-start.20 = (f32[2,8,128]{2,1,0:T(8,128)S(1)}, f32[2,8,128]{2,1,0:T(8,128)S(1)}, u32[]{:S(2)}, u32[]{:S(2)}) collective-permute-start(f32[2,8,128]{2,1,0:T(8,128)S(1)} %add_add_fusion), channel_id=1, source_target_pairs={{0,4},{1,5},{2,6},{3,7},{4,0},{5,1},{6,2},{7,3},{8,12},{9,13},{10,... | collective-permute-start | bytes 24584 | tf_op jit(solution)/shard_map/ppermute | solution.py:317
  59.5 0.7 %collective-permute-start.21 = (f32[2,8,128]{2,1,0:T(8,128)S(1)}, f32[2,8,128]{2,1,0:T(8,128)S(1)}, u32[]{:S(2)}, u32[]{:S(2)}) collective-permute-start(f32[2,8,128]{2,1,0:T(8,128)S(1)} %add_add_fusion), channel_id=1, source_target_pairs={{0,8},{1,9},{2,10},{3,11},{4,12},{5,13},{6,14},{7,15},{8,0},{9,1},... | collective-permute-start | bytes 24584 | tf_op jit(solution)/shard_map/ppermute | solution.py:317
  60.2 1.7 %collective-permute-start.22 = (f32[2,8,128]{2,1,0:T(8,128)S(1)}, f32[2,8,128]{2,1,0:T(8,128)S(1)}, u32[]{:S(2)}, u32[]{:S(2)}) collective-permute-start(f32[2,8,128]{2,1,0:T(8,128)S(1)} %add_add_fusion), channel_id=1, source_target_pairs={{0,12},{1,13},{2,14},{3,15},{4,8},{5,9},{6,10},{7,11},{8,4},{9,5},... | collective-permute-start | bytes 24584 | tf_op jit(solution)/shard_map/ppermute | solution.py:317
  61.9 2.0 %deliver_1.1 = bf16[32,64,2048]{2,1,0:T(8,128)(2,1)} custom-call(bf16[32,64,2048]{2,1,0:T(8,128)(2,1)S(1)} %get-tuple-element.99.held_ref, bf16[32,64,2048]{2,1,0:T(8,128)(2,1)} %deliver_0.1.refs_0_), custom_call_target="tpu_custom_call", output_to_operand_aliasing={{}: (1, {})} | custom-call | tf_op jit(solution)/shard_map/deliver_1/pallas_call | solution.py:290
  64.0 0.1 collective-permute-done.21
  64.0 1.6 %collective-permute-done.22 = f32[2,8,128]{2,1,0:T(8,128)S(1)} collective-permute-done((f32[2,8,128]{2,1,0:T(8,128)S(1)}, f32[2,8,128]{2,1,0:T(8,128)S(1)}, u32[]{:S(2)}, u32[]{:S(2)}) %collective-permute-start.22) | collective-permute-done | bytes 8224 | tf_op jit(solution)/shard_map/ppermute | solution.py:317
  65.7 0.1 add_reduce_fusion
  65.8 0.5 add_sqrt_fusion
  (23 shorter events, 0.1 us)
Async XLA Ops:
  0.6 13.4 %collective-permute-start = (bf16[8,64,384]{2,1,0:T(8,128)(2,1)}, bf16[8,64,384]{2,1,0:T(8,128)(2,1)S(1)}, u32[]{:S(2)}, u32[]{:S(2)}) collective-permute-start(bf16[8,64,384]{2,1,0:T(8,128)(2,1)} %refs_3_.1), channel_id=1, source_target_pairs={{0,4},{1,5},{2,6},{3,7},{4,12},{5,13},{6,14},{7,15},{8,0},{9,1},{1... | collective-permute-start | bytes 1179656 | tf_op jit(solution)/shard_map/ppermute | solution.py:314
  3.7 10.3 %collective-permute-start.1 = (bf16[8,64,384]{2,1,0:T(8,128)(2,1)}, bf16[8,64,384]{2,1,0:T(8,128)(2,1)S(1)}, u32[]{:S(2)}, u32[]{:S(2)}) collective-permute-start(bf16[8,64,384]{2,1,0:T(8,128)(2,1)} %refs_3_.1), channel_id=1, source_target_pairs={{0,1},{1,0},{2,3},{3,2},{4,5},{5,4},{6,7},{7,6},{8,9},{9,8},{10,11... | collective-permute-start | bytes 1179656 | tf_op jit(solution)/shard_map/ppermute | solution.py:317
  3.7 12.8 %collective-permute-start.4 = (bf16[8,64,384]{2,1,0:T(8,128)(2,1)}, bf16[8,64,384]{2,1,0:T(8,128)(2,1)S(1)}, u32[]{:S(2)}, u32[]{:S(2)}) collective-permute-start(bf16[8,64,384]{2,1,0:T(8,128)(2,1)} %refs_3_.1), channel_id=1, source_target_pairs={{0,2},{1,3},{2,0},{3,1},{4,6},{5,7},{6,4},{7,5},{8,10},{9,11},{10,... | collective-permute-start | bytes 1179656 | tf_op jit(solution)/shard_map/ppermute | solution.py:317
  5.2 0.7 copy-start.3
  5.9 0.7 copy-start.5
  14.0 11.2 %collective-permute-start.2 = (bf16[8,64,384]{2,1,0:T(8,128)(2,1)S(1)}, bf16[8,64,384]{2,1,0:T(8,128)(2,1)S(1)}, u32[]{:S(2)}, u32[]{:S(2)}) collective-permute-start(bf16[8,64,384]{2,1,0:T(8,128)(2,1)S(1)} %collective-permute-done.refs_0_), channel_id=1, source_target_pairs={{0,4},{1,5},{2,6},{3,7},{4,12},{5,13},{6,14},{7,15},{8,0},{9,1},{1... | collective-permute-start | bytes 1179656 | tf_op jit(solution)/shard_map/ppermute | solution.py:314
  15.0 10.3 %collective-permute-start.3 = (bf16[8,64,384]{2,1,0:T(8,128)(2,1)S(1)}, bf16[8,64,384]{2,1,0:T(8,128)(2,1)S(1)}, u32[]{:S(2)}, u32[]{:S(2)}) collective-permute-start(bf16[8,64,384]{2,1,0:T(8,128)(2,1)S(1)} %collective-permute-done.refs_0_), channel_id=1, source_target_pairs={{0,1},{1,0},{2,3},{3,2},{4,5},{5,4},{6,7},{7,6},{8,9},{9,8},{10,11... | collective-permute-start | bytes 1179656 | tf_op jit(solution)/shard_map/ppermute | solution.py:317
  15.0 12.4 %collective-permute-start.7 = (bf16[8,64,384]{2,1,0:T(8,128)(2,1)S(1)}, bf16[8,64,384]{2,1,0:T(8,128)(2,1)S(1)}, u32[]{:S(2)}, u32[]{:S(2)}) collective-permute-start(bf16[8,64,384]{2,1,0:T(8,128)(2,1)S(1)} %collective-permute-done.refs_0_), channel_id=1, source_target_pairs={{0,2},{1,3},{2,0},{3,1},{4,6},{5,7},{6,4},{7,5},{8,10},{9,11},{10,... | collective-permute-start | bytes 1179656 | tf_op jit(solution)/shard_map/ppermute | solution.py:317
  16.5 10.9 %collective-permute-start.8 = (bf16[8,64,384]{2,1,0:T(8,128)(2,1)S(1)}, bf16[8,64,384]{2,1,0:T(8,128)(2,1)S(1)}, u32[]{:S(2)}, u32[]{:S(2)}) collective-permute-start(bf16[8,64,384]{2,1,0:T(8,128)(2,1)S(1)} %collective-permute-done.4.refs_1_), channel_id=1, source_target_pairs={{0,1},{1,0},{2,3},{3,2},{4,5},{5,4},{6,7},{7,6},{8,9},{9,8},{10,11... | collective-permute-start | bytes 1179656 | tf_op jit(solution)/shard_map/ppermute | solution.py:317
  16.7 1.4 %copy-start = (bf16[32,64,384]{2,1,0:T(8,128)(2,1)S(1)}, bf16[32,64,384]{2,1,0:T(8,128)(2,1)}, u32[]{:S(2)}) copy-start(bf16[32,64,384]{2,1,0:T(8,128)(2,1)} %v_ref.9) | copy-start | bytes 4718596
  18.2 1.0 %copy-start.2 = (bf16[8,64,384]{2,1,0:T(8,128)(2,1)S(1)}, bf16[8,64,384]{2,1,0:T(8,128)(2,1)}, u32[]{:S(2)}) copy-start(bf16[8,64,384]{2,1,0:T(8,128)(2,1)} %refs_3_.1) | copy-start | bytes 1179652
  19.1 0.7 copy-start.4
  19.8 7.6 %copy-start.1 = (bf16[32,64,384]{2,1,0:T(8,128)(2,1)S(1)}, bf16[32,64,384]{2,1,0:T(8,128)(2,1)}, u32[]{:S(2)}) copy-start(bf16[32,64,384]{2,1,0:T(8,128)(2,1)} %v_ref.9) | copy-start | bytes 4718596
  25.3 4.8 %collective-permute-start.5 = (bf16[8,64,384]{2,1,0:T(8,128)(2,1)S(1)}, bf16[8,64,384]{2,1,0:T(8,128)(2,1)S(1)}, u32[]{:S(2)}, u32[]{:S(2)}) collective-permute-start(bf16[8,64,384]{2,1,0:T(8,128)(2,1)S(1)} %collective-permute-done.2.refs_0_), channel_id=1, source_target_pairs={{0,1},{1,0},{2,3},{3,2},{4,5},{5,4},{6,7},{7,6},{8,9},{9,8},{10,11... | collective-permute-start | bytes 1179656 | tf_op jit(solution)/shard_map/ppermute | solution.py:317
  25.3 12.4 %collective-permute-start.6 = (bf16[8,64,384]{2,1,0:T(8,128)(2,1)S(1)}, bf16[8,64,384]{2,1,0:T(8,128)(2,1)S(1)}, u32[]{:S(2)}, u32[]{:S(2)}) collective-permute-start(bf16[8,64,384]{2,1,0:T(8,128)(2,1)S(1)} %collective-permute-done.2.refs_0_), channel_id=1, source_target_pairs={{0,4},{1,5},{2,6},{3,7},{4,12},{5,13},{6,14},{7,15},{8,0},{9,1},{1... | collective-permute-start | bytes 1179656 | tf_op jit(solution)/shard_map/ppermute | solution.py:314
  26.0 14.5 %collective-permute-start.10 = (bf16[8,64,384]{2,1,0:T(8,128)(2,1)S(1)}, bf16[8,64,384]{2,1,0:T(8,128)(2,1)S(1)}, u32[]{:S(2)}, u32[]{:S(2)}) collective-permute-start(bf16[8,64,384]{2,1,0:T(8,128)(2,1)S(1)} %collective-permute-done.2.refs_0_), channel_id=1, source_target_pairs={{0,2},{1,3},{2,0},{3,1},{4,6},{5,7},{6,4},{7,5},{8,10},{9,11},{10,... | collective-permute-start | bytes 1179656 | tf_op jit(solution)/shard_map/ppermute | solution.py:317
  27.4 13.2 %collective-permute-start.12 = (bf16[8,64,384]{2,1,0:T(8,128)(2,1)S(1)}, bf16[8,64,384]{2,1,0:T(8,128)(2,1)S(1)}, u32[]{:S(2)}, u32[]{:S(2)}) collective-permute-start(bf16[8,64,384]{2,1,0:T(8,128)(2,1)S(1)} %collective-permute-done.7.refs_1_), channel_id=1, source_target_pairs={{0,1},{1,0},{2,3},{3,2},{4,5},{5,4},{6,7},{7,6},{8,9},{9,8},{10,11... | collective-permute-start | bytes 1179656 | tf_op jit(solution)/shard_map/ppermute | solution.py:317
  37.7 2.9 %collective-permute-start.13 = (bf16[8,64,384]{2,1,0:T(8,128)(2,1)S(1)}, bf16[8,64,384]{2,1,0:T(8,128)(2,1)S(1)}, u32[]{:S(2)}, u32[]{:S(2)}) collective-permute-start(bf16[8,64,384]{2,1,0:T(8,128)(2,1)S(1)} %collective-permute-done.6.refs_0_), channel_id=1, source_target_pairs={{0,1},{1,0},{2,3},{3,2},{4,5},{5,4},{6,7},{7,6},{8,9},{9,8},{10,11... | collective-permute-start | bytes 1179656 | tf_op jit(solution)/shard_map/ppermute | solution.py:317
  37.7 7.2 %collective-permute-start.11 = (bf16[3,64,384]{2,1,0:T(8,128)(2,1)S(1)}, bf16[3,64,384]{2,1,0:T(8,128)(2,1)S(1)}, u32[]{:S(2)}, u32[]{:S(2)}) collective-permute-start(bf16[3,64,384]{2,1,0:T(8,128)(2,1)S(1)} %slice.7), channel_id=1, source_target_pairs={{0,2},{1,3},{2,0},{3,1},{4,6},{5,7},{6,4},{7,5},{8,10},{9,11},{10,... | collective-permute-start | bytes 442376 | tf_op jit(solution)/shard_map/ppermute | solution.py:317
  39.0 8.1 %collective-permute-start.9 = (bf16[5,64,384]{2,1,0:T(8,128)(2,1)S(1)}, bf16[5,64,384]{2,1,0:T(8,128)(2,1)S(1)}, u32[]{:S(2)}, u32[]{:S(2)}) collective-permute-start(bf16[5,64,384]{2,1,0:T(8,128)(2,1)S(1)} %slice.8), channel_id=1, source_target_pairs={{0,8},{1,9},{2,10},{3,11},{4,0},{5,1},{6,2},{7,3},{8,12},{9,13},{1... | collective-permute-start | bytes 737288 | tf_op jit(solution)/shard_map/ppermute | solution.py:314
  44.9 2.7 %collective-permute-start.14 = (bf16[8,64,384]{2,1,0:T(8,128)(2,1)S(1)}, bf16[8,64,384]{2,1,0:T(8,128)(2,1)S(1)}, u32[]{:S(2)}, u32[]{:S(2)}) collective-permute-start(bf16[8,64,384]{2,1,0:T(8,128)(2,1)S(1)} %collective-permute-done.10.refs_1_), channel_id=1, source_target_pairs={{0,1},{1,0},{2,3},{3,2},{4,5},{5,4},{6,7},{7,6},{8,9},{9,8},{10,11... | collective-permute-start | bytes 1179656 | tf_op jit(solution)/shard_map/ppermute | solution.py:317
  47.1 3.0 %collective-permute-start.16 = (bf16[5,64,384]{2,1,0:T(8,128)(2,1)S(1)}, bf16[5,64,384]{2,1,0:T(8,128)(2,1)S(1)}, u32[]{:S(2)}, u32[]{:S(2)}) collective-permute-start(bf16[5,64,384]{2,1,0:T(8,128)(2,1)S(1)} %collective-permute-done.9.refs_1_), channel_id=1, source_target_pairs={{0,1},{1,0},{2,3},{3,2},{4,5},{5,4},{6,7},{7,6},{8,9},{9,8},{10,11... | collective-permute-start | bytes 737288 | tf_op jit(solution)/shard_map/ppermute | solution.py:317
  47.1 3.0 %collective-permute-start.15 = (bf16[3,64,384]{2,1,0:T(8,128)(2,1)S(1)}, bf16[3,64,384]{2,1,0:T(8,128)(2,1)S(1)}, u32[]{:S(2)}, u32[]{:S(2)}) collective-permute-start(bf16[3,64,384]{2,1,0:T(8,128)(2,1)S(1)} %collective-permute-done.11.refs_2_), channel_id=1, source_target_pairs={{0,1},{1,0},{2,3},{3,2},{4,5},{5,4},{6,7},{7,6},{8,9},{9,8},{10,11... | collective-permute-start | bytes 442376 | tf_op jit(solution)/shard_map/ppermute | solution.py:317
  52.0 4.0 %collective-permute-start.17 = (f32[2,8,128]{2,1,0:T(8,128)S(1)}, f32[2,8,128]{2,1,0:T(8,128)S(1)}, u32[]{:S(2)}, u32[]{:S(2)}) collective-permute-start(f32[2,8,128]{2,1,0:T(8,128)S(1)} %get-tuple-element.97), channel_id=1, source_target_pairs={{0,1},{1,0},{2,3},{3,2},{4,5},{5,4},{6,7},{7,6},{8,9},{9,8},{10,11... | collective-permute-start | bytes 24584 | tf_op jit(solution)/shard_map/ppermute | solution.py:317
  52.6 3.7 %collective-permute-start.18 = (f32[2,8,128]{2,1,0:T(8,128)S(1)}, f32[2,8,128]{2,1,0:T(8,128)S(1)}, u32[]{:S(2)}, u32[]{:S(2)}) collective-permute-start(f32[2,8,128]{2,1,0:T(8,128)S(1)} %get-tuple-element.97), channel_id=1, source_target_pairs={{0,2},{1,3},{2,0},{3,1},{4,6},{5,7},{6,4},{7,5},{8,10},{9,11},{10,... | collective-permute-start | bytes 24584 | tf_op jit(solution)/shard_map/ppermute | solution.py:317
  53.4 3.1 %collective-permute-start.19 = (f32[2,8,128]{2,1,0:T(8,128)S(1)}, f32[2,8,128]{2,1,0:T(8,128)S(1)}, u32[]{:S(2)}, u32[]{:S(2)}) collective-permute-start(f32[2,8,128]{2,1,0:T(8,128)S(1)} %get-tuple-element.97), channel_id=1, source_target_pairs={{0,3},{1,2},{2,1},{3,0},{4,7},{5,6},{6,5},{7,4},{8,11},{9,10},{10,... | collective-permute-start | bytes 24584 | tf_op jit(solution)/shard_map/ppermute | solution.py:317
  56.5 7.5 %collective-permute-start.20 = (f32[2,8,128]{2,1,0:T(8,128)S(1)}, f32[2,8,128]{2,1,0:T(8,128)S(1)}, u32[]{:S(2)}, u32[]{:S(2)}) collective-permute-start(f32[2,8,128]{2,1,0:T(8,128)S(1)} %add_add_fusion), channel_id=1, source_target_pairs={{0,4},{1,5},{2,6},{3,7},{4,0},{5,1},{6,2},{7,3},{8,12},{9,13},{10,... | collective-permute-start | bytes 24584 | tf_op jit(solution)/shard_map/ppermute | solution.py:317
  59.5 4.5 %collective-permute-start.21 = (f32[2,8,128]{2,1,0:T(8,128)S(1)}, f32[2,8,128]{2,1,0:T(8,128)S(1)}, u32[]{:S(2)}, u32[]{:S(2)}) collective-permute-start(f32[2,8,128]{2,1,0:T(8,128)S(1)} %add_add_fusion), channel_id=1, source_target_pairs={{0,8},{1,9},{2,10},{3,11},{4,12},{5,13},{6,14},{7,15},{8,0},{9,1},... | collective-permute-start | bytes 24584 | tf_op jit(solution)/shard_map/ppermute | solution.py:317
  60.2 5.4 %collective-permute-start.22 = (f32[2,8,128]{2,1,0:T(8,128)S(1)}, f32[2,8,128]{2,1,0:T(8,128)S(1)}, u32[]{:S(2)}, u32[]{:S(2)}) collective-permute-start(f32[2,8,128]{2,1,0:T(8,128)S(1)} %add_add_fusion), channel_id=1, source_target_pairs={{0,12},{1,13},{2,14},{3,15},{4,8},{5,9},{6,10},{7,11},{8,4},{9,5},... | collective-permute-start | bytes 24584 | tf_op jit(solution)/shard_map/ppermute | solution.py:317

commit v17 on v16

--- a/solution.py
+++ b/solution.py
@@ -34,8 +34,8 @@
 def prepare_kernel(
     depth, shard_tiles,
     me_ref, counts_ref, irrep_ref,
-    res_ref, gathered_ref, stats_ref, order_ref, offset_ref, stop_ref, end_ref, item_ref,
-    next_ref, call_ref,
+    res_ref, gathered_ref, stats_ref, order_ref, offset_ref, stop_ref, end_ref, item_ref, late_ref,
+    next_ref, call_ref, last_ref,
 ):
     own_tiles = irrep_ref.shape[0]
     irreps = counts_ref.shape[0]
@@ -43,6 +43,7 @@
     most = item_ref.shape[0] // calls
     for s in range(irreps):
         stop_ref[s] = 0
+        last_ref[s] = 0
 
     def count(l, carry):
         s = irrep_ref[l]
@@ -86,6 +87,7 @@
             high = offset + jnp.minimum(tiles, j * BATCH + BATCH) - 1
             call = jnp.maximum(call_ref[low // shard_tiles], call_ref[high // shard_tiles])
             word = (j * 256 + s) * 256 + first
+            last_ref[s] = jnp.maximum(last_ref[s], call)
 
             def batch(i, n):
                 item_ref[n] = word + i * BATCH
@@ -107,6 +109,7 @@
 
     def blank(l, carry):
         res_ref[l] = jnp.zeros(res_ref.shape[1:], res_ref.dtype)
+        late_ref[l] = jnp.where(last_ref[irrep_ref[l]] >= depth - 1, 1, 0)
         return carry
 
     lax.fori_loop(0, own_tiles, blank, 0)
@@ -143,12 +146,14 @@
             jax.ShapeDtypeStruct((irreps,), jnp.int32),
             jax.ShapeDtypeStruct((depth + 1,), jnp.int32),
             jax.ShapeDtypeStruct(((depth + 1) * most,), jnp.int32),
+            jax.ShapeDtypeStruct((own_tiles,), jnp.int32),
         ),
         in_specs=[smem] * 3,
-        out_specs=(vmem, vmem, vmem, smem, smem, smem, smem, smem),
+        out_specs=(vmem, vmem, vmem, smem, smem, smem, smem, smem, smem),
         scratch_shapes=[
             pltpu.SMEM((irreps,), jnp.int32),
             pltpu.SMEM((4 * depth,), jnp.int32),
+            pltpu.SMEM((irreps,), jnp.int32),
         ],
         compiler_params=pltpu.CompilerParams(
             vmem_limit_bytes=2 * all_tiles * rows * width + 2 * own_tiles * rows * columns
@@ -275,28 +280,38 @@
     )(*listing, stats, integrals, residual, gathered, *fresh)
 
 
-def deliver_kernel(part, held_ref, *refs):
+def deliver_kernel(part, late_ref, held_ref, *refs):
     out_ref, sem = refs[-2:]
-    tiles = held_ref.shape[0] // 2
-    copy = pltpu.make_async_copy(
-        held_ref.at[pl.ds(part * tiles, tiles)], out_ref.at[pl.ds(part * tiles, tiles)], sem
-    )
-    copy.start()
-    copy.wait()
-
-
-def deliver(held, part, *out):
+
+    def send(l, started):
+        mine = late_ref[l] == part
+
+        @pl.when(mine)
+        def _():
+            pltpu.make_async_copy(held_ref.at[l], out_ref.at[l], sem).start()
+
+        return started + jnp.where(mine, 1, 0)
+
+    def wait(n, carry):
+        pltpu.make_async_copy(held_ref.at[0], out_ref.at[0], sem).wait()
+        return carry
+
+    lax.fori_loop(0, lax.fori_loop(0, held_ref.shape[0], send, 0), wait, 0)
+
+
+def deliver(held, late, part, *out):
     anywhere = pl.BlockSpec(memory_space=pl.ANY)
     return pl.pallas_call(
         functools.partial(deliver_kernel, part),
         out_shape=jax.ShapeDtypeStruct(held.shape, held.dtype),
-        in_specs=[pl.BlockSpec(memory_space=pltpu.VMEM)] + [anywhere] * len(out),
+        in_specs=[pl.BlockSpec(memory_space=pltpu.SMEM), pl.BlockSpec(memory_space=pltpu.VMEM)]
+        + [anywhere] * len(out),
         out_specs=anywhere,
         scratch_shapes=[pltpu.SemaphoreType.DMA],
-        input_output_aliases={1: 0} if out else {},
+        input_output_aliases={2: 0} if out else {},
         compiler_params=pltpu.CompilerParams(vmem_limit_bytes=2 * held.size + 1024 * 1024),
         name=f"deliver_{part}",
-    )(held, *out)
+    )(late, held, *out)
 
 
 def per_device(amplitudes, ij_counts, integrals, ab_irrep):
@@ -316,7 +331,7 @@
     def swap(x, bits):
         return lax.ppermute(x, "vir", [(d, d ^ bits) for d in range(devices)])
 
-    residual, gathered, stats, *listing = prepare(
+    residual, gathered, stats, *listing, late = prepare(
         me, ij_counts, ab_irrep, depth, shard_tiles, rows, width
     )
     listing = (me, ij_counts, *listing)
@@ -348,7 +363,8 @@
         else:
             fresh[k, 0, 1, 0] = c[k]
         state = ladder(k - 1, depth, shard_tiles, integrals, listing, state, fresh)
-    b[-1], last[0], state = lax.optimization_barrier((b[-1], last[0], state))
+    out = deliver(state[0], late, 0)
+    b[-1], last[0], out, state = lax.optimization_barrier((b[-1], last[0], out, state))
     first, second = {(k - 1, 1, 1, 0): swap(b[-1], 1)}, {(k, 1, 1, 0): swap(last[0], 1)}
     last[part], state = lax.optimization_barrier((last[part], state))
     second[k, 1, 1, part] = swap(last[part], 1)
@@ -358,10 +374,9 @@
         state = ladder(number, depth, shard_tiles, integrals, listing, state, fresh)
 
     residual, _, stats = state
-    out = deliver(residual, 0)
     stats = sum([swap(stats, bits) for bits in (1, 2, 3)], stats)
     stats, residual, out = lax.optimization_barrier((stats, residual, out))
-    out = deliver(residual, 1, out)
+    out = deliver(residual, late, 1, out)
     stats = sum([swap(stats, 4 * bits) for bits in range(1, depth)], stats)
     irrep_sums, ab_counts = jnp.sum(stats, axis=2)
     entries = ab_counts * ij_counts.astype(jnp.float32) * float(rows * rows)

time: 66.8 us -> 67.2 us (level)
  waiting for transfers between devices: 18.4 us -> 19.6 us
  starting transfers between devices: 20.3 us -> 19.3 us
    ppermute x19, waiting for transfers between devices: 2.18 us -> 5.09 us  [swap(): return lax.ppermute(x, 'vir', [(d, d ^ bits) for d in range(devices)])]
    ppermute x4, waiting for transfers between devices: 16.2 us -> 14.6 us  [shift_z(): return lax.ppermute(x, 'vir', pairs)]
    pallas_call x2, Pallas kernels: 4.04 us -> 5.08 us  [deliver(): pl.pallas_call(functools.partial(deliver_kernel, part), out_shape=jax.Sha...]
    ppermute x19, starting transfers between devices: 14 us -> 12.9 us  [swap(): return lax.ppermute(x, 'vir', [(d, d ^ bits) for d in range(devices)])]
  transfers between devices with their start and end apart: 23 -> 23, of which waited for: 8 -> 6; matrix products, arithmetic and copies ran while one was open for 0% -> 0% of each run, Pallas kernels for 30% -> 31%
where the time goes in v17:
time: 67.2 us; the launch traced here: 67.1 us
  Pallas kernels  22.4 us (33%)
  waiting for transfers between devices  19.6 us (29%)
  starting transfers between devices  19.3 us (29%)
  local copies, waits for them, and re-layouts  4.41 us (7%)
  between operations  0.81 us (1%)
    ppermute x4, waiting for transfers between devices, shift_z(): return lax.ppermute(x, 'vir', pairs)  14.6 us
    pallas_call x5, Pallas kernels, ladder(): pl.pallas_call(functools.partial(ladder_kernel, call, depth, shard_tiles,...  13.3 us
    ppermute x19, starting transfers between devices, swap(): return lax.ppermute(x, 'vir', [(d, d ^ bits) for d in range(devices)])  12.9 us
    ppermute x4, starting transfers between devices, shift_z(): return lax.ppermute(x, 'vir', pairs)  6.31 us
    ppermute x19, waiting for transfers between devices, swap(): return lax.ppermute(x, 'vir', [(d, d ^ bits) for d in range(devices)])  5.09 us
    pallas_call x2, Pallas kernels, deliver(): pl.pallas_call(functools.partial(deliver_kernel, part), out_shape=jax.Sha...  5.08 us
    unnamed x12, local copies, waits for them, and re-layouts  4.37 us
    pallas_call x1, Pallas kernels, prepare(): pl.pallas_call(functools.partial(prepare_kernel, depth, shard_tiles), out...  3.99 us
  transfers between devices with their start and end apart: 23, of which 6 were waited for; matrix products, arithmetic and copies ran while one was open for 0% of the time, Pallas kernels for 31%

profile of v17, /device:TPU:0, one launch (start us, length us, event | category | flops | bytes accessed | tf_op | source)
XLA Modules:
  0.0 67.1 jit_solution(206857346149302643)
XLA Ops:
  0.6 3.1 %collective-permute-start = (bf16[8,64,384]{2,1,0:T(8,128)(2,1)}, bf16[8,64,384]{2,1,0:T(8,128)(2,1)S(1)}, u32[]{:S(2)}, u32[]{:S(2)}) collective-permute-start(bf16[8,64,384]{2,1,0:T(8,128)(2,1)} %refs_3_.1), channel_id=1, source_target_pairs={{0,4},{1,5},{2,6},{3,7},{4,12},{5,13},{6,14},{7,15},{8,0},{9,1},{1... | collective-permute-start | bytes 1179656 | tf_op jit(solution)/shard_map/ppermute | solution.py:329
  3.7 0.0 collective-permute-start.1
  3.7 1.5 %collective-permute-start.4 = (bf16[8,64,384]{2,1,0:T(8,128)(2,1)}, bf16[8,64,384]{2,1,0:T(8,128)(2,1)S(1)}, u32[]{:S(2)}, u32[]{:S(2)}) collective-permute-start(bf16[8,64,384]{2,1,0:T(8,128)(2,1)} %refs_3_.1), channel_id=1, source_target_pairs={{0,2},{1,3},{2,0},{3,1},{4,6},{5,7},{6,4},{7,5},{8,10},{9,11},{10,... | collective-permute-start | bytes 1179656 | tf_op jit(solution)/shard_map/ppermute | solution.py:332
  5.2 0.7 copy-done.3
  5.9 0.7 copy-done.5
  6.5 4.0 %prepare.1 = (bf16[32,64,2048]{2,1,0:T(8,128)(2,1)S(1)}, bf16[132,64,384]{2,1,0:T(8,128)(2,1)S(1)}, f32[2,8,128]{2,1,0:T(8,128)S(1)}, s32[32]{0:T(128)S(1)}, s32...) custom-call(s32[1]{0:T(128)} %bitcast.me_ref, s32[8]{0:T(128)S(1)} %copy-done.3, ...), custom_call_target="tpu_custom_call" | custom-call | bytes 8388608 | tf_op jit(solution)/shard_map/prepare/pallas_call | solution.py:138
  10.5 3.5 %collective-permute-done.refs_0_ = bf16[8,64,384]{2,1,0:T(8,128)(2,1)S(1)} collective-permute-done((bf16[8,64,384]{2,1,0:T(8,128)(2,1)}, bf16[8,64,384]{2,1,0:T(8,128)(2,1)S(1)}, u32[]{:S(2)}, u32[]{:S(2)}) %collective-permute-start) | collective-permute-done | bytes 393248 | tf_op jit(solution)/shard_map/ppermute | solution.py:329
  14.0 0.0 collective-permute-done.1.refs_2_
  14.0 0.9 %collective-permute-start.2 = (bf16[8,64,384]{2,1,0:T(8,128)(2,1)S(1)}, bf16[8,64,384]{2,1,0:T(8,128)(2,1)S(1)}, u32[]{:S(2)}, u32[]{:S(2)}) collective-permute-start(bf16[8,64,384]{2,1,0:T(8,128)(2,1)S(1)} %collective-permute-done.refs_0_), channel_id=1, source_target_pairs={{0,4},{1,5},{2,6},{3,7},{4,12},{5,13},{6,14},{7,15},{8,0},{9,1},{1... | collective-permute-start | bytes 1179656 | tf_op jit(solution)/shard_map/ppermute | solution.py:329
  15.0 1.5 %collective-permute-start.7 = (bf16[8,64,384]{2,1,0:T(8,128)(2,1)S(1)}, bf16[8,64,384]{2,1,0:T(8,128)(2,1)S(1)}, u32[]{:S(2)}, u32[]{:S(2)}) collective-permute-start(bf16[8,64,384]{2,1,0:T(8,128)(2,1)S(1)} %collective-permute-done.refs_0_), channel_id=1, source_target_pairs={{0,2},{1,3},{2,0},{3,1},{4,6},{5,7},{6,4},{7,5},{8,10},{9,11},{10,... | collective-permute-start | bytes 1179656 | tf_op jit(solution)/shard_map/ppermute | solution.py:332
  16.5 0.0 collective-permute-done.4.refs_1_
  16.5 0.2 collective-permute-start.8
  16.7 1.4 %copy-done = bf16[32,64,384]{2,1,0:T(8,128)(2,1)S(1)} copy-done((bf16[32,64,384]{2,1,0:T(8,128)(2,1)S(1)}, bf16[32,64,384]{2,1,0:T(8,128)(2,1)}, u32[]{:S(2)}) %copy-start) | copy-done | bytes 1572888
  18.2 1.0 %copy-done.2 = bf16[8,64,384]{2,1,0:T(8,128)(2,1)S(1)} copy-done((bf16[8,64,384]{2,1,0:T(8,128)(2,1)S(1)}, bf16[8,64,384]{2,1,0:T(8,128)(2,1)}, u32[]{:S(2)}) %copy-start.2) | copy-done | bytes 393240
  19.1 0.7 copy-done.4
  19.8 2.1 %ladder_0.1 = (bf16[32,64,2048]{2,1,0:T(8,128)(2,1)S(1)}, bf16[132,64,384]{2,1,0:T(8,128)(2,1)S(1)}, f32[2,8,128]{2,1,0:T(8,128)S(1)}) custom-call(s32[1]{0:T(128)} %bitcast.me_ref, s32[8]{0:T(128)S(1)} %copy-done.4, s32[32]{0:T(128)S(1)} %get-tuple-element.55.order_ref, ...), custom_call_target="tpu_custom_call", output_to_operand_aliasing={{0}: (9, {}), {1}: (10, {})} | custom-call | flops 402653184 | bytes 2097152 | tf_op jit(solution)/shard_map/ladder_0/pallas_call | solution.py:257
  21.9 3.4 %collective-permute-done.2.refs_0_ = bf16[8,64,384]{2,1,0:T(8,128)(2,1)S(1)} collective-permute-done((bf16[8,64,384]{2,1,0:T(8,128)(2,1)S(1)}, bf16[8,64,384]{2,1,0:T(8,128)(2,1)S(1)}, u32[]{:S(2)}, u32[]{:S(2)}) %collective-permute-start.2) | collective-permute-done | bytes 393248 | tf_op jit(solution)/shard_map/ppermute | solution.py:329
  25.3 0.0 collective-permute-done.3.refs_2_
  25.3 0.0 collective-permute-start.5
  25.3 0.8 %collective-permute-start.6 = (bf16[8,64,384]{2,1,0:T(8,128)(2,1)S(1)}, bf16[8,64,384]{2,1,0:T(8,128)(2,1)S(1)}, u32[]{:S(2)}, u32[]{:S(2)}) collective-permute-start(bf16[8,64,384]{2,1,0:T(8,128)(2,1)S(1)} %collective-permute-done.2.refs_0_), channel_id=1, source_target_pairs={{0,4},{1,5},{2,6},{3,7},{4,12},{5,13},{6,14},{7,15},{8,0},{9,1},{1... | collective-permute-start | bytes 1179656 | tf_op jit(solution)/shard_map/ppermute | solution.py:329
  26.1 1.3 %collective-permute-start.10 = (bf16[8,64,384]{2,1,0:T(8,128)(2,1)S(1)}, bf16[8,64,384]{2,1,0:T(8,128)(2,1)S(1)}, u32[]{:S(2)}, u32[]{:S(2)}) collective-permute-start(bf16[8,64,384]{2,1,0:T(8,128)(2,1)S(1)} %collective-permute-done.2.refs_0_), channel_id=1, source_target_pairs={{0,2},{1,3},{2,0},{3,1},{4,6},{5,7},{6,4},{7,5},{8,10},{9,11},{10,... | collective-permute-start | bytes 1179656 | tf_op jit(solution)/shard_map/ppermute | solution.py:332
  27.4 0.0 collective-permute-done.7.refs_1_
  27.4 0.0 collective-permute-start.12
  27.4 0.0 collective-permute-done.8.refs_3_
  27.4 2.6 %ladder_1.1 = (bf16[32,64,2048]{2,1,0:T(8,128)(2,1)S(1)}, bf16[132,64,384]{2,1,0:T(8,128)(2,1)S(1)}, f32[2,8,128]{2,1,0:T(8,128)S(1)}) custom-call(s32[1]{0:T(128)} %bitcast.me_ref, s32[8]{0:T(128)S(1)} %copy-done.4, s32[32]{0:T(128)S(1)} %get-tuple-element.55.order_ref, ...), custom_call_target="tpu_custom_call", output_to_operand_aliasing={{0}: (9, {}), {1}: (10, {})} | custom-call | flops 402653184 | bytes 2097152 | tf_op jit(solution)/shard_map/ladder_1/pallas_call | solution.py:257
  30.0 0.0 collective-permute-done.5.refs_2_
  30.0 7.7 %collective-permute-done.6.refs_0_ = bf16[8,64,384]{2,1,0:T(8,128)(2,1)S(1)} collective-permute-done((bf16[8,64,384]{2,1,0:T(8,128)(2,1)S(1)}, bf16[8,64,384]{2,1,0:T(8,128)(2,1)S(1)}, u32[]{:S(2)}, u32[]{:S(2)}) %collective-permute-start.6) | collective-permute-done | bytes 393248 | tf_op jit(solution)/shard_map/ppermute | solution.py:329
  37.7 1.3 %collective-permute-start.11 = (bf16[3,64,384]{2,1,0:T(8,128)(2,1)S(1)}, bf16[3,64,384]{2,1,0:T(8,128)(2,1)S(1)}, u32[]{:S(2)}, u32[]{:S(2)}) collective-permute-start(bf16[3,64,384]{2,1,0:T(8,128)(2,1)S(1)} %slice.7), channel_id=1, source_target_pairs={{0,2},{1,3},{2,0},{3,1},{4,6},{5,7},{6,4},{7,5},{8,10},{9,11},{10,... | collective-permute-start | bytes 442376 | tf_op jit(solution)/shard_map/ppermute | solution.py:332
  39.0 1.5 %collective-permute-start.9 = (bf16[5,64,384]{2,1,0:T(8,128)(2,1)S(1)}, bf16[5,64,384]{2,1,0:T(8,128)(2,1)S(1)}, u32[]{:S(2)}, u32[]{:S(2)}) collective-permute-start(bf16[5,64,384]{2,1,0:T(8,128)(2,1)S(1)} %slice.8), channel_id=1, source_target_pairs={{0,8},{1,9},{2,10},{3,11},{4,0},{5,1},{6,2},{7,3},{8,12},{9,13},{1... | collective-permute-start | bytes 737288 | tf_op jit(solution)/shard_map/ppermute | solution.py:329
  40.6 4.3 %ladder_2.1 = (bf16[32,64,2048]{2,1,0:T(8,128)(2,1)S(1)}, bf16[132,64,384]{2,1,0:T(8,128)(2,1)S(1)}, f32[2,8,128]{2,1,0:T(8,128)S(1)}) custom-call(s32[1]{0:T(128)} %bitcast.me_ref, s32[8]{0:T(128)S(1)} %copy-done.4, s32[32]{0:T(128)S(1)} %get-tuple-element.55.order_ref, ...), custom_call_target="tpu_custom_call", output_to_operand_aliasing={{0}: (9, {}), {1}: (10, {})} | custom-call | flops 503316480 | bytes 2621440 | tf_op jit(solution)/shard_map/ladder_2/pallas_call | solution.py:257
  44.9 2.8 %deliver_0.1.refs_0_ = bf16[32,64,2048]{2,1,0:T(8,128)(2,1)} custom-call(s32[32]{0:T(128)S(1)} %get-tuple-element.54.late_ref, bf16[32,64,2048]{2,1,0:T(8,128)(2,1)S(1)} %get-tuple-element.92.held_ref.res_in_ref), custom_call_target="tpu_custom_call" | custom-call | tf_op jit(solution)/shard_map/deliver_0/pallas_call | solution.py:304
  47.7 0.1 collective-permute-start.14
  47.8 0.5 collective-permute-start.16
  48.3 0.1 collective-permute-start.15
  48.4 1.1 %collective-permute-done.14.refs_0_ = bf16[8,64,384]{2,1,0:T(8,128)(2,1)S(1)} collective-permute-done((bf16[8,64,384]{2,1,0:T(8,128)(2,1)S(1)}, bf16[8,64,384]{2,1,0:T(8,128)(2,1)S(1)}, u32[]{:S(2)}, u32[]{:S(2)}) %collective-permute-start.14) | collective-permute-done | bytes 393248 | tf_op jit(solution)/shard_map/ppermute | solution.py:332
  49.5 2.5 %ladder_3.1 = (bf16[32,64,2048]{2,1,0:T(8,128)(2,1)S(1)}, bf16[132,64,384]{2,1,0:T(8,128)(2,1)S(1)}, f32[2,8,128]{2,1,0:T(8,128)S(1)}) custom-call(s32[1]{0:T(128)} %bitcast.me_ref, s32[8]{0:T(128)S(1)} %copy-done.4, s32[32]{0:T(128)S(1)} %get-tuple-element.55.order_ref, ...), custom_call_target="tpu_custom_call", output_to_operand_aliasing={{0}: (9, {}), {1}: (10, {})} | custom-call | flops 201326592 | bytes 1048576 | tf_op jit(solution)/shard_map/ladder_3/pallas_call | solution.py:257
  52.0 1.8 %ladder_4.1 = (bf16[32,64,2048]{2,1,0:T(8,128)(2,1)S(1)}, bf16[132,64,384]{2,1,0:T(8,128)(2,1)S(1)}, f32[2,8,128]{2,1,0:T(8,128)S(1)}) custom-call(s32[1]{0:T(128)} %bitcast.me_ref, s32[8]{0:T(128)S(1)} %copy-done.4, s32[32]{0:T(128)S(1)} %get-tuple-element.55.order_ref, ...), custom_call_target="tpu_custom_call", output_to_operand_aliasing={{0}: (9, {}), {1}: (10, {})} | custom-call | flops 100663296 | bytes 524288 | tf_op jit(solution)/shard_map/ladder_4/pallas_call | solution.py:257
  53.9 0.2 collective-permute-start.17
  54.1 0.2 collective-permute-start.18
  54.3 1.5 %collective-permute-start.19 = (f32[2,8,128]{2,1,0:T(8,128)S(1)}, f32[2,8,128]{2,1,0:T(8,128)S(1)}, u32[]{:S(2)}, u32[]{:S(2)}) collective-permute-start(f32[2,8,128]{2,1,0:T(8,128)S(1)} %get-tuple-element.100), channel_id=1, source_target_pairs={{0,3},{1,2},{2,1},{3,0},{4,7},{5,6},{6,5},{7,4},{8,11},{9,10},{10,... | collective-permute-start | bytes 24584 | tf_op jit(solution)/shard_map/ppermute | solution.py:332
  55.8 1.9 %collective-permute-done.18 = f32[2,8,128]{2,1,0:T(8,128)S(1)} collective-permute-done((f32[2,8,128]{2,1,0:T(8,128)S(1)}, f32[2,8,128]{2,1,0:T(8,128)S(1)}, u32[]{:S(2)}, u32[]{:S(2)}) %collective-permute-start.18) | collective-permute-done | bytes 8224 | tf_op jit(solution)/shard_map/ppermute | solution.py:332
  57.7 1.3 %collective-permute-start.20 = (f32[2,8,128]{2,1,0:T(8,128)S(1)}, f32[2,8,128]{2,1,0:T(8,128)S(1)}, u32[]{:S(2)}, u32[]{:S(2)}) collective-permute-start(f32[2,8,128]{2,1,0:T(8,128)S(1)} %add_add_fusion), channel_id=1, source_target_pairs={{0,4},{1,5},{2,6},{3,7},{4,0},{5,1},{6,2},{7,3},{8,12},{9,13},{10,... | collective-permute-start | bytes 24584 | tf_op jit(solution)/shard_map/ppermute | solution.py:332
  59.0 2.0 %collective-permute-start.21 = (f32[2,8,128]{2,1,0:T(8,128)S(1)}, f32[2,8,128]{2,1,0:T(8,128)S(1)}, u32[]{:S(2)}, u32[]{:S(2)}) collective-permute-start(f32[2,8,128]{2,1,0:T(8,128)S(1)} %add_add_fusion), channel_id=1, source_target_pairs={{0,8},{1,9},{2,10},{3,11},{4,12},{5,13},{6,14},{7,15},{8,0},{9,1},... | collective-permute-start | bytes 24584 | tf_op jit(solution)/shard_map/ppermute | solution.py:332
  61.0 1.1 %collective-permute-start.22 = (f32[2,8,128]{2,1,0:T(8,128)S(1)}, f32[2,8,128]{2,1,0:T(8,128)S(1)}, u32[]{:S(2)}, u32[]{:S(2)}) collective-permute-start(f32[2,8,128]{2,1,0:T(8,128)S(1)} %add_add_fusion), channel_id=1, source_target_pairs={{0,12},{1,13},{2,14},{3,15},{4,8},{5,9},{6,10},{7,11},{8,4},{9,5},... | collective-permute-start | bytes 24584 | tf_op jit(solution)/shard_map/ppermute | solution.py:332
  62.2 2.3 %deliver_1.1 = bf16[32,64,2048]{2,1,0:T(8,128)(2,1)} custom-call(s32[32]{0:T(128)S(1)} %get-tuple-element.54.late_ref, bf16[32,64,2048]{2,1,0:T(8,128)(2,1)S(1)} %get-tuple-element.103.held_ref, bf16[32,64,2048]{2,1,0:T(8,128)(2,1)} %deliver_0.1.refs_0_), custom_call_target="tpu_custom_call", output_to_operand_aliasing={{}: (2, {})} | custom-call | tf_op jit(solution)/shard_map/deliver_1/pallas_call | solution.py:304
  64.5 2.0 %collective-permute-done.22 = f32[2,8,128]{2,1,0:T(8,128)S(1)} collective-permute-done((f32[2,8,128]{2,1,0:T(8,128)S(1)}, f32[2,8,128]{2,1,0:T(8,128)S(1)}, u32[]{:S(2)}, u32[]{:S(2)}) %collective-permute-start.22) | collective-permute-done | bytes 8224 | tf_op jit(solution)/shard_map/ppermute | solution.py:332
  66.5 0.1 add_reduce_fusion
  66.6 0.5 add_sqrt_fusion
  (23 shorter events, 0.1 us)
Async XLA Ops:
  0.6 13.4 %collective-permute-start = (bf16[8,64,384]{2,1,0:T(8,128)(2,1)}, bf16[8,64,384]{2,1,0:T(8,128)(2,1)S(1)}, u32[]{:S(2)}, u32[]{:S(2)}) collective-permute-start(bf16[8,64,384]{2,1,0:T(8,128)(2,1)} %refs_3_.1), channel_id=1, source_target_pairs={{0,4},{1,5},{2,6},{3,7},{4,12},{5,13},{6,14},{7,15},{8,0},{9,1},{1... | collective-permute-start | bytes 1179656 | tf_op jit(solution)/shard_map/ppermute | solution.py:329
  3.7 10.3 %collective-permute-start.1 = (bf16[8,64,384]{2,1,0:T(8,128)(2,1)}, bf16[8,64,384]{2,1,0:T(8,128)(2,1)S(1)}, u32[]{:S(2)}, u32[]{:S(2)}) collective-permute-start(bf16[8,64,384]{2,1,0:T(8,128)(2,1)} %refs_3_.1), channel_id=1, source_target_pairs={{0,1},{1,0},{2,3},{3,2},{4,5},{5,4},{6,7},{7,6},{8,9},{9,8},{10,11... | collective-permute-start | bytes 1179656 | tf_op jit(solution)/shard_map/ppermute | solution.py:332
  3.7 12.8 %collective-permute-start.4 = (bf16[8,64,384]{2,1,0:T(8,128)(2,1)}, bf16[8,64,384]{2,1,0:T(8,128)(2,1)S(1)}, u32[]{:S(2)}, u32[]{:S(2)}) collective-permute-start(bf16[8,64,384]{2,1,0:T(8,128)(2,1)} %refs_3_.1), channel_id=1, source_target_pairs={{0,2},{1,3},{2,0},{3,1},{4,6},{5,7},{6,4},{7,5},{8,10},{9,11},{10,... | collective-permute-start | bytes 1179656 | tf_op jit(solution)/shard_map/ppermute | solution.py:332
  5.2 0.7 copy-start.3
  5.9 0.7 copy-start.5
  14.0 11.2 %collective-permute-start.2 = (bf16[8,64,384]{2,1,0:T(8,128)(2,1)S(1)}, bf16[8,64,384]{2,1,0:T(8,128)(2,1)S(1)}, u32[]{:S(2)}, u32[]{:S(2)}) collective-permute-start(bf16[8,64,384]{2,1,0:T(8,128)(2,1)S(1)} %collective-permute-done.refs_0_), channel_id=1, source_target_pairs={{0,4},{1,5},{2,6},{3,7},{4,12},{5,13},{6,14},{7,15},{8,0},{9,1},{1... | collective-permute-start | bytes 1179656 | tf_op jit(solution)/shard_map/ppermute | solution.py:329
  15.0 10.3 %collective-permute-start.3 = (bf16[8,64,384]{2,1,0:T(8,128)(2,1)S(1)}, bf16[8,64,384]{2,1,0:T(8,128)(2,1)S(1)}, u32[]{:S(2)}, u32[]{:S(2)}) collective-permute-start(bf16[8,64,384]{2,1,0:T(8,128)(2,1)S(1)} %collective-permute-done.refs_0_), channel_id=1, source_target_pairs={{0,1},{1,0},{2,3},{3,2},{4,5},{5,4},{6,7},{7,6},{8,9},{9,8},{10,11... | collective-permute-start | bytes 1179656 | tf_op jit(solution)/shard_map/ppermute | solution.py:332
  15.0 12.4 %collective-permute-start.7 = (bf16[8,64,384]{2,1,0:T(8,128)(2,1)S(1)}, bf16[8,64,384]{2,1,0:T(8,128)(2,1)S(1)}, u32[]{:S(2)}, u32[]{:S(2)}) collective-permute-start(bf16[8,64,384]{2,1,0:T(8,128)(2,1)S(1)} %collective-permute-done.refs_0_), channel_id=1, source_target_pairs={{0,2},{1,3},{2,0},{3,1},{4,6},{5,7},{6,4},{7,5},{8,10},{9,11},{10,... | collective-permute-start | bytes 1179656 | tf_op jit(solution)/shard_map/ppermute | solution.py:332
  16.5 10.9 %collective-permute-start.8 = (bf16[8,64,384]{2,1,0:T(8,128)(2,1)S(1)}, bf16[8,64,384]{2,1,0:T(8,128)(2,1)S(1)}, u32[]{:S(2)}, u32[]{:S(2)}) collective-permute-start(bf16[8,64,384]{2,1,0:T(8,128)(2,1)S(1)} %collective-permute-done.4.refs_1_), channel_id=1, source_target_pairs={{0,1},{1,0},{2,3},{3,2},{4,5},{5,4},{6,7},{7,6},{8,9},{9,8},{10,11... | collective-permute-start | bytes 1179656 | tf_op jit(solution)/shard_map/ppermute | solution.py:332
  16.7 1.4 %copy-start = (bf16[32,64,384]{2,1,0:T(8,128)(2,1)S(1)}, bf16[32,64,384]{2,1,0:T(8,128)(2,1)}, u32[]{:S(2)}) copy-start(bf16[32,64,384]{2,1,0:T(8,128)(2,1)} %v_ref.9) | copy-start | bytes 4718596
  18.2 1.0 %copy-start.2 = (bf16[8,64,384]{2,1,0:T(8,128)(2,1)S(1)}, bf16[8,64,384]{2,1,0:T(8,128)(2,1)}, u32[]{:S(2)}) copy-start(bf16[8,64,384]{2,1,0:T(8,128)(2,1)} %refs_3_.1) | copy-start | bytes 1179652
  19.1 0.7 copy-start.4
  19.8 7.6 %copy-start.1 = (bf16[32,64,384]{2,1,0:T(8,128)(2,1)S(1)}, bf16[32,64,384]{2,1,0:T(8,128)(2,1)}, u32[]{:S(2)}) copy-start(bf16[32,64,384]{2,1,0:T(8,128)(2,1)} %v_ref.9) | copy-start | bytes 4718596
  25.3 4.8 %collective-permute-start.5 = (bf16[8,64,384]{2,1,0:T(8,128)(2,1)S(1)}, bf16[8,64,384]{2,1,0:T(8,128)(2,1)S(1)}, u32[]{:S(2)}, u32[]{:S(2)}) collective-permute-start(bf16[8,64,384]{2,1,0:T(8,128)(2,1)S(1)} %collective-permute-done.2.refs_0_), channel_id=1, source_target_pairs={{0,1},{1,0},{2,3},{3,2},{4,5},{5,4},{6,7},{7,6},{8,9},{9,8},{10,11... | collective-permute-start | bytes 1179656 | tf_op jit(solution)/shard_map/ppermute | solution.py:332
  25.3 12.4 %collective-permute-start.6 = (bf16[8,64,384]{2,1,0:T(8,128)(2,1)S(1)}, bf16[8,64,384]{2,1,0:T(8,128)(2,1)S(1)}, u32[]{:S(2)}, u32[]{:S(2)}) collective-permute-start(bf16[8,64,384]{2,1,0:T(8,128)(2,1)S(1)} %collective-permute-done.2.refs_0_), channel_id=1, source_target_pairs={{0,4},{1,5},{2,6},{3,7},{4,12},{5,13},{6,14},{7,15},{8,0},{9,1},{1... | collective-permute-start | bytes 1179656 | tf_op jit(solution)/shard_map/ppermute | solution.py:329
  26.1 14.5 %collective-permute-start.10 = (bf16[8,64,384]{2,1,0:T(8,128)(2,1)S(1)}, bf16[8,64,384]{2,1,0:T(8,128)(2,1)S(1)}, u32[]{:S(2)}, u32[]{:S(2)}) collective-permute-start(bf16[8,64,384]{2,1,0:T(8,128)(2,1)S(1)} %collective-permute-done.2.refs_0_), channel_id=1, source_target_pairs={{0,2},{1,3},{2,0},{3,1},{4,6},{5,7},{6,4},{7,5},{8,10},{9,11},{10,... | collective-permute-start | bytes 1179656 | tf_op jit(solution)/shard_map/ppermute | solution.py:332
  27.4 13.2 %collective-permute-start.12 = (bf16[8,64,384]{2,1,0:T(8,128)(2,1)S(1)}, bf16[8,64,384]{2,1,0:T(8,128)(2,1)S(1)}, u32[]{:S(2)}, u32[]{:S(2)}) collective-permute-start(bf16[8,64,384]{2,1,0:T(8,128)(2,1)S(1)} %collective-permute-done.7.refs_1_), channel_id=1, source_target_pairs={{0,1},{1,0},{2,3},{3,2},{4,5},{5,4},{6,7},{7,6},{8,9},{9,8},{10,11... | collective-permute-start | bytes 1179656 | tf_op jit(solution)/shard_map/ppermute | solution.py:332
  37.7 2.9 %collective-permute-start.13 = (bf16[8,64,384]{2,1,0:T(8,128)(2,1)S(1)}, bf16[8,64,384]{2,1,0:T(8,128)(2,1)S(1)}, u32[]{:S(2)}, u32[]{:S(2)}) collective-permute-start(bf16[8,64,384]{2,1,0:T(8,128)(2,1)S(1)} %collective-permute-done.6.refs_0_), channel_id=1, source_target_pairs={{0,1},{1,0},{2,3},{3,2},{4,5},{5,4},{6,7},{7,6},{8,9},{9,8},{10,11... | collective-permute-start | bytes 1179656 | tf_op jit(solution)/shard_map/ppermute | solution.py:332
  37.7 10.0 %collective-permute-start.11 = (bf16[3,64,384]{2,1,0:T(8,128)(2,1)S(1)}, bf16[3,64,384]{2,1,0:T(8,128)(2,1)S(1)}, u32[]{:S(2)}, u32[]{:S(2)}) collective-permute-start(bf16[3,64,384]{2,1,0:T(8,128)(2,1)S(1)} %slice.7), channel_id=1, source_target_pairs={{0,2},{1,3},{2,0},{3,1},{4,6},{5,7},{6,4},{7,5},{8,10},{9,11},{10,... | collective-permute-start | bytes 442376 | tf_op jit(solution)/shard_map/ppermute | solution.py:332
  39.0 8.8 %collective-permute-start.9 = (bf16[5,64,384]{2,1,0:T(8,128)(2,1)S(1)}, bf16[5,64,384]{2,1,0:T(8,128)(2,1)S(1)}, u32[]{:S(2)}, u32[]{:S(2)}) collective-permute-start(bf16[5,64,384]{2,1,0:T(8,128)(2,1)S(1)} %slice.8), channel_id=1, source_target_pairs={{0,8},{1,9},{2,10},{3,11},{4,0},{5,1},{6,2},{7,3},{8,12},{9,13},{1... | collective-permute-start | bytes 737288 | tf_op jit(solution)/shard_map/ppermute | solution.py:329
  47.7 1.8 %collective-permute-start.14 = (bf16[8,64,384]{2,1,0:T(8,128)(2,1)S(1)}, bf16[8,64,384]{2,1,0:T(8,128)(2,1)S(1)}, u32[]{:S(2)}, u32[]{:S(2)}) collective-permute-start(bf16[8,64,384]{2,1,0:T(8,128)(2,1)S(1)} %collective-permute-done.10.refs_1_), channel_id=1, source_target_pairs={{0,1},{1,0},{2,3},{3,2},{4,5},{5,4},{6,7},{7,6},{8,9},{9,8},{10,11... | collective-permute-start | bytes 1179656 | tf_op jit(solution)/shard_map/ppermute | solution.py:332
  47.8 4.2 %collective-permute-start.16 = (bf16[5,64,384]{2,1,0:T(8,128)(2,1)S(1)}, bf16[5,64,384]{2,1,0:T(8,128)(2,1)S(1)}, u32[]{:S(2)}, u32[]{:S(2)}) collective-permute-start(bf16[5,64,384]{2,1,0:T(8,128)(2,1)S(1)} %collective-permute-done.9.refs_1_), channel_id=1, source_target_pairs={{0,1},{1,0},{2,3},{3,2},{4,5},{5,4},{6,7},{7,6},{8,9},{9,8},{10,11... | collective-permute-start | bytes 737288 | tf_op jit(solution)/shard_map/ppermute | solution.py:332
  48.3 3.7 %collective-permute-start.15 = (bf16[3,64,384]{2,1,0:T(8,128)(2,1)S(1)}, bf16[3,64,384]{2,1,0:T(8,128)(2,1)S(1)}, u32[]{:S(2)}, u32[]{:S(2)}) collective-permute-start(bf16[3,64,384]{2,1,0:T(8,128)(2,1)S(1)} %collective-permute-done.11.refs_2_), channel_id=1, source_target_pairs={{0,1},{1,0},{2,3},{3,2},{4,5},{5,4},{6,7},{7,6},{8,9},{9,8},{10,11... | collective-permute-start | bytes 442376 | tf_op jit(solution)/shard_map/ppermute | solution.py:332
  53.9 1.9 %collective-permute-start.17 = (f32[2,8,128]{2,1,0:T(8,128)S(1)}, f32[2,8,128]{2,1,0:T(8,128)S(1)}, u32[]{:S(2)}, u32[]{:S(2)}) collective-permute-start(f32[2,8,128]{2,1,0:T(8,128)S(1)} %get-tuple-element.100), channel_id=1, source_target_pairs={{0,1},{1,0},{2,3},{3,2},{4,5},{5,4},{6,7},{7,6},{8,9},{9,8},{10,11... | collective-permute-start | bytes 24584 | tf_op jit(solution)/shard_map/ppermute | solution.py:332
  54.1 3.7 %collective-permute-start.18 = (f32[2,8,128]{2,1,0:T(8,128)S(1)}, f32[2,8,128]{2,1,0:T(8,128)S(1)}, u32[]{:S(2)}, u32[]{:S(2)}) collective-permute-start(f32[2,8,128]{2,1,0:T(8,128)S(1)} %get-tuple-element.100), channel_id=1, source_target_pairs={{0,2},{1,3},{2,0},{3,1},{4,6},{5,7},{6,4},{7,5},{8,10},{9,11},{10,... | collective-permute-start | bytes 24584 | tf_op jit(solution)/shard_map/ppermute | solution.py:332
  54.3 3.4 %collective-permute-start.19 = (f32[2,8,128]{2,1,0:T(8,128)S(1)}, f32[2,8,128]{2,1,0:T(8,128)S(1)}, u32[]{:S(2)}, u32[]{:S(2)}) collective-permute-start(f32[2,8,128]{2,1,0:T(8,128)S(1)} %get-tuple-element.100), channel_id=1, source_target_pairs={{0,3},{1,2},{2,1},{3,0},{4,7},{5,6},{6,5},{7,4},{8,11},{9,10},{10,... | collective-permute-start | bytes 24584 | tf_op jit(solution)/shard_map/ppermute | solution.py:332
  57.7 6.7 %collective-permute-start.20 = (f32[2,8,128]{2,1,0:T(8,128)S(1)}, f32[2,8,128]{2,1,0:T(8,128)S(1)}, u32[]{:S(2)}, u32[]{:S(2)}) collective-permute-start(f32[2,8,128]{2,1,0:T(8,128)S(1)} %add_add_fusion), channel_id=1, source_target_pairs={{0,4},{1,5},{2,6},{3,7},{4,0},{5,1},{6,2},{7,3},{8,12},{9,13},{10,... | collective-permute-start | bytes 24584 | tf_op jit(solution)/shard_map/ppermute | solution.py:332
  59.0 5.5 %collective-permute-start.21 = (f32[2,8,128]{2,1,0:T(8,128)S(1)}, f32[2,8,128]{2,1,0:T(8,128)S(1)}, u32[]{:S(2)}, u32[]{:S(2)}) collective-permute-start(f32[2,8,128]{2,1,0:T(8,128)S(1)} %add_add_fusion), channel_id=1, source_target_pairs={{0,8},{1,9},{2,10},{3,11},{4,12},{5,13},{6,14},{7,15},{8,0},{9,1},... | collective-permute-start | bytes 24584 | tf_op jit(solution)/shard_map/ppermute | solution.py:332
  61.0 5.4 %collective-permute-start.22 = (f32[2,8,128]{2,1,0:T(8,128)S(1)}, f32[2,8,128]{2,1,0:T(8,128)S(1)}, u32[]{:S(2)}, u32[]{:S(2)}) collective-permute-start(f32[2,8,128]{2,1,0:T(8,128)S(1)} %add_add_fusion), channel_id=1, source_target_pairs={{0,12},{1,13},{2,14},{3,15},{4,8},{5,9},{6,10},{7,11},{8,4},{9,5},... | collective-permute-start | bytes 24584 | tf_op jit(solution)/shard_map/ppermute | solution.py:332

commit v18 on v16

--- a/solution.py
+++ b/solution.py
@@ -277,12 +277,14 @@
 
 def deliver_kernel(part, held_ref, *refs):
     out_ref, sem = refs[-2:]
-    tiles = held_ref.shape[0] // 2
-    copy = pltpu.make_async_copy(
-        held_ref.at[pl.ds(part * tiles, tiles)], out_ref.at[pl.ds(part * tiles, tiles)], sem
-    )
-    copy.start()
-    copy.wait()
+    tiles = held_ref.shape[0] // 2 // sem.shape[0]
+    copies = []
+    for n in range(sem.shape[0]):
+        at = pl.ds((part * sem.shape[0] + n) * tiles, tiles)
+        copies.append(pltpu.make_async_copy(held_ref.at[at], out_ref.at[at], sem.at[n]))
+        copies[-1].start()
+    for copy in copies:
+        copy.wait()
 
 
 def deliver(held, part, *out):
@@ -292,7 +294,7 @@
         out_shape=jax.ShapeDtypeStruct(held.shape, held.dtype),
         in_specs=[pl.BlockSpec(memory_space=pltpu.VMEM)] + [anywhere] * len(out),
         out_specs=anywhere,
-        scratch_shapes=[pltpu.SemaphoreType.DMA],
+        scratch_shapes=[pltpu.SemaphoreType.DMA((8,))],
         input_output_aliases={1: 0} if out else {},
         compiler_params=pltpu.CompilerParams(vmem_limit_bytes=2 * held.size + 1024 * 1024),
         name=f"deliver_{part}",
@@ -330,7 +332,7 @@
             b.append(swap(a[k], 2))
             a.append(shift_z(a[k], 1))
         else:
-            part = 3 * shard_tiles // 8
+            part = shard_tiles // 2
             c[-1], a[k], back, state = lax.optimization_barrier(
                 (c[-1], a[k], b[0][part:], state)
             )
@@ -349,7 +351,9 @@
             fresh[k, 0, 1, 0] = c[k]
         state = ladder(k - 1, depth, shard_tiles, integrals, listing, state, fresh)
     b[-1], last[0], state = lax.optimization_barrier((b[-1], last[0], state))
-    first, second = {(k - 1, 1, 1, 0): swap(b[-1], 1)}, {(k, 1, 1, 0): swap(last[0], 1)}
+    first, second = {}, {(k, 1, 1, 0): swap(last[0], 1)}
+    for tile in (0, part):
+        first[k - 1, 1, 1, tile] = swap(b[-1][tile:tile + part], 1)
     last[part], state = lax.optimization_barrier((last[part], state))
     second[k, 1, 1, part] = swap(last[part], 1)
     for tile, piece in last.items():

time: 66.8 us -> 67.5 us (1.010)
  waiting for transfers between devices: 18.4 us -> 19.2 us
    ppermute x19 -> x20, waiting for transfers between devices: 2.18 us -> 4.86 us  [swap(): return lax.ppermute(x, 'vir', [(d, d ^ bits) for d in range(devices)])]
    ppermute x4, waiting for transfers between devices: 16.2 us -> 14.4 us  [shift_z(): return lax.ppermute(x, 'vir', pairs)]
    ppermute x19 -> x20, starting transfers between devices: 14 us -> 13.4 us  [swap(): return lax.ppermute(x, 'vir', [(d, d ^ bits) for d in range(devices)])]
  transfers between devices with their start and end apart: 23 -> 24, of which waited for: 8 -> 9; matrix products, arithmetic and copies ran while one was open for 0% -> 0% of each run, Pallas kernels for 30% -> 30%
where the time goes in v18:
time: 67.5 us; the launch traced here: 67.3 us
  Pallas kernels  22.2 us (33%)
  starting transfers between devices  20 us (30%)
  waiting for transfers between devices  19.2 us (28%)
  local copies, waits for them, and re-layouts  4.45 us (7%)
  between operations  0.8 us (1%)
    ppermute x4, waiting for transfers between devices, shift_z(): return lax.ppermute(x, 'vir', pairs)  14.4 us
    pallas_call x5, Pallas kernels, ladder(): pl.pallas_call(functools.partial(ladder_kernel, call, depth, shard_tiles,...  14.1 us
    ppermute x20, starting transfers between devices, swap(): return lax.ppermute(x, 'vir', [(d, d ^ bits) for d in range(devices)])  13.4 us
    ppermute x4, starting transfers between devices, shift_z(): return lax.ppermute(x, 'vir', pairs)  6.59 us
    ppermute x20, waiting for transfers between devices, swap(): return lax.ppermute(x, 'vir', [(d, d ^ bits) for d in range(devices)])  4.86 us
    unnamed x12, local copies, waits for them, and re-layouts  4.37 us
    pallas_call x2, Pallas kernels, deliver(): pl.pallas_call(functools.partial(deliver_kernel, part), out_shape=jax.Sha...  4.14 us
    pallas_call x1, Pallas kernels, prepare(): pl.pallas_call(functools.partial(prepare_kernel, depth, shard_tiles), out...  4 us
  transfers between devices with their start and end apart: 24, of which 9 were waited for; matrix products, arithmetic and copies ran while one was open for 0% of the time, Pallas kernels for 30%

profile of v18, /device:TPU:0, one launch (start us, length us, event | category | flops | bytes accessed | tf_op | source)
XLA Modules:
  0.0 67.3 jit_solution(2766270372524757605)
XLA Ops:
  0.6 3.1 %collective-permute-start = (bf16[8,64,384]{2,1,0:T(8,128)(2,1)}, bf16[8,64,384]{2,1,0:T(8,128)(2,1)S(1)}, u32[]{:S(2)}, u32[]{:S(2)}) collective-permute-start(bf16[8,64,384]{2,1,0:T(8,128)(2,1)} %refs_3_.1), channel_id=1, source_target_pairs={{0,4},{1,5},{2,6},{3,7},{4,12},{5,13},{6,14},{7,15},{8,0},{9,1},{1... | collective-permute-start | bytes 1179656 | tf_op jit(solution)/shard_map/ppermute | solution.py:316
  3.7 1.5 %collective-permute-start.4 = (bf16[8,64,384]{2,1,0:T(8,128)(2,1)}, bf16[8,64,384]{2,1,0:T(8,128)(2,1)S(1)}, u32[]{:S(2)}, u32[]{:S(2)}) collective-permute-start(bf16[8,64,384]{2,1,0:T(8,128)(2,1)} %refs_3_.1), channel_id=1, source_target_pairs={{0,2},{1,3},{2,0},{3,1},{4,6},{5,7},{6,4},{7,5},{8,10},{9,11},{10,... | collective-permute-start | bytes 1179656 | tf_op jit(solution)/shard_map/ppermute | solution.py:319
  5.2 0.7 copy-done.3
  5.9 0.7 copy-done.5
  6.5 4.0 %prepare.1 = (bf16[32,64,2048]{2,1,0:T(8,128)(2,1)S(1)}, bf16[132,64,384]{2,1,0:T(8,128)(2,1)S(1)}, f32[2,8,128]{2,1,0:T(8,128)S(1)}, s32[32]{0:T(128)S(1)}, s32...) custom-call(s32[1]{0:T(128)} %bitcast.me_ref, s32[8]{0:T(128)S(1)} %copy-done.3, s32[32]{0:T(128)S(1)} %copy-done.5), custom_call_target="tpu_custom_call" | custom-call | bytes 8388608 | tf_op jit(solution)/shard_map/prepare/pallas_call | solution.py:135
  10.5 3.5 %collective-permute-done.refs_0_ = bf16[8,64,384]{2,1,0:T(8,128)(2,1)S(1)} collective-permute-done((bf16[8,64,384]{2,1,0:T(8,128)(2,1)}, bf16[8,64,384]{2,1,0:T(8,128)(2,1)S(1)}, u32[]{:S(2)}, u32[]{:S(2)}) %collective-permute-start) | collective-permute-done | bytes 393248 | tf_op jit(solution)/shard_map/ppermute | solution.py:316
  14.0 0.9 %collective-permute-start.2 = (bf16[8,64,384]{2,1,0:T(8,128)(2,1)S(1)}, bf16[8,64,384]{2,1,0:T(8,128)(2,1)S(1)}, u32[]{:S(2)}, u32[]{:S(2)}) collective-permute-start(bf16[8,64,384]{2,1,0:T(8,128)(2,1)S(1)} %collective-permute-done.refs_0_), channel_id=1, source_target_pairs={{0,4},{1,5},{2,6},{3,7},{4,12},{5,13},{6,14},{7,15},{8,0},{9,1},{1... | collective-permute-start | bytes 1179656 | tf_op jit(solution)/shard_map/ppermute | solution.py:316
  15.0 0.0 collective-permute-start.3
  15.0 1.5 %collective-permute-start.7 = (bf16[8,64,384]{2,1,0:T(8,128)(2,1)S(1)}, bf16[8,64,384]{2,1,0:T(8,128)(2,1)S(1)}, u32[]{:S(2)}, u32[]{:S(2)}) collective-permute-start(bf16[8,64,384]{2,1,0:T(8,128)(2,1)S(1)} %collective-permute-done.refs_0_), channel_id=1, source_target_pairs={{0,2},{1,3},{2,0},{3,1},{4,6},{5,7},{6,4},{7,5},{8,10},{9,11},{10,... | collective-permute-start | bytes 1179656 | tf_op jit(solution)/shard_map/ppermute | solution.py:319
  16.5 0.0 collective-permute-done.4.refs_1_
  16.5 0.2 collective-permute-start.8
  16.7 1.4 %copy-done = bf16[32,64,384]{2,1,0:T(8,128)(2,1)S(1)} copy-done((bf16[32,64,384]{2,1,0:T(8,128)(2,1)S(1)}, bf16[32,64,384]{2,1,0:T(8,128)(2,1)}, u32[]{:S(2)}) %copy-start) | copy-done | bytes 1572888
  18.2 1.0 %copy-done.2 = bf16[8,64,384]{2,1,0:T(8,128)(2,1)S(1)} copy-done((bf16[8,64,384]{2,1,0:T(8,128)(2,1)S(1)}, bf16[8,64,384]{2,1,0:T(8,128)(2,1)}, u32[]{:S(2)}) %copy-start.2) | copy-done | bytes 393240
  19.1 0.7 copy-done.4
  19.8 2.6 %ladder_0.1 = (bf16[32,64,2048]{2,1,0:T(8,128)(2,1)S(1)}, bf16[132,64,384]{2,1,0:T(8,128)(2,1)S(1)}, f32[2,8,128]{2,1,0:T(8,128)S(1)}) custom-call(s32[1]{0:T(128)} %bitcast.me_ref, s32[8]{0:T(128)S(1)} %copy-done.4, s32[32]{0:T(128)S(1)} %get-tuple-element.52.order_ref, ...), custom_call_target="tpu_custom_call", output_to_operand_aliasing={{0}: (9, {}), {1}: (10, {})} | custom-call | flops 402653184 | bytes 2097152 | tf_op jit(solution)/shard_map/ladder_0/pallas_call | solution.py:252
  22.4 2.9 %collective-permute-done.2.refs_0_ = bf16[8,64,384]{2,1,0:T(8,128)(2,1)S(1)} collective-permute-done((bf16[8,64,384]{2,1,0:T(8,128)(2,1)S(1)}, bf16[8,64,384]{2,1,0:T(8,128)(2,1)S(1)}, u32[]{:S(2)}, u32[]{:S(2)}) %collective-permute-start.2) | collective-permute-done | bytes 393248 | tf_op jit(solution)/shard_map/ppermute | solution.py:316
  25.3 1.1 %collective-permute-start.6 = (bf16[8,64,384]{2,1,0:T(8,128)(2,1)S(1)}, bf16[8,64,384]{2,1,0:T(8,128)(2,1)S(1)}, u32[]{:S(2)}, u32[]{:S(2)}) collective-permute-start(bf16[8,64,384]{2,1,0:T(8,128)(2,1)S(1)} %collective-permute-done.2.refs_0_), channel_id=1, source_target_pairs={{0,4},{1,5},{2,6},{3,7},{4,12},{5,13},{6,14},{7,15},{8,0},{9,1},{1... | collective-permute-start | bytes 1179656 | tf_op jit(solution)/shard_map/ppermute | solution.py:316
  26.3 1.0 %collective-permute-start.10 = (bf16[8,64,384]{2,1,0:T(8,128)(2,1)S(1)}, bf16[8,64,384]{2,1,0:T(8,128)(2,1)S(1)}, u32[]{:S(2)}, u32[]{:S(2)}) collective-permute-start(bf16[8,64,384]{2,1,0:T(8,128)(2,1)S(1)} %collective-permute-done.2.refs_0_), channel_id=1, source_target_pairs={{0,2},{1,3},{2,0},{3,1},{4,6},{5,7},{6,4},{7,5},{8,10},{9,11},{10,... | collective-permute-start | bytes 1179656 | tf_op jit(solution)/shard_map/ppermute | solution.py:319
  27.4 2.6 %ladder_1.1 = (bf16[32,64,2048]{2,1,0:T(8,128)(2,1)S(1)}, bf16[132,64,384]{2,1,0:T(8,128)(2,1)S(1)}, f32[2,8,128]{2,1,0:T(8,128)S(1)}) custom-call(s32[1]{0:T(128)} %bitcast.me_ref, s32[8]{0:T(128)S(1)} %copy-done.4, s32[32]{0:T(128)S(1)} %get-tuple-element.52.order_ref, ...), custom_call_target="tpu_custom_call", output_to_operand_aliasing={{0}: (9, {}), {1}: (10, {})} | custom-call | flops 402653184 | bytes 2097152 | tf_op jit(solution)/shard_map/ladder_1/pallas_call | solution.py:252
  30.0 7.7 %collective-permute-done.6.refs_0_ = bf16[8,64,384]{2,1,0:T(8,128)(2,1)S(1)} collective-permute-done((bf16[8,64,384]{2,1,0:T(8,128)(2,1)S(1)}, bf16[8,64,384]{2,1,0:T(8,128)(2,1)S(1)}, u32[]{:S(2)}, u32[]{:S(2)}) %collective-permute-start.6) | collective-permute-done | bytes 393248 | tf_op jit(solution)/shard_map/ppermute | solution.py:316
  37.7 0.0 collective-permute-start.13
  37.7 1.3 %collective-permute-start.11 = (bf16[4,64,384]{2,1,0:T(8,128)(2,1)S(1)}, bf16[4,64,384]{2,1,0:T(8,128)(2,1)S(1)}, u32[]{:S(2)}, u32[]{:S(2)}) collective-permute-start(bf16[4,64,384]{2,1,0:T(8,128)(2,1)S(1)} %slice.13), channel_id=1, source_target_pairs={{0,2},{1,3},{2,0},{3,1},{4,6},{5,7},{6,4},{7,5},{8,10},{9,11},{10,... | collective-permute-start | bytes 589832 | tf_op jit(solution)/shard_map/ppermute | solution.py:319
  39.0 1.5 %collective-permute-start.9 = (bf16[4,64,384]{2,1,0:T(8,128)(2,1)S(1)}, bf16[4,64,384]{2,1,0:T(8,128)(2,1)S(1)}, u32[]{:S(2)}, u32[]{:S(2)}) collective-permute-start(bf16[4,64,384]{2,1,0:T(8,128)(2,1)S(1)} %slice.16), channel_id=1, source_target_pairs={{0,8},{1,9},{2,10},{3,11},{4,0},{5,1},{6,2},{7,3},{8,12},{9,13},{1... | collective-permute-start | bytes 589832 | tf_op jit(solution)/shard_map/ppermute | solution.py:316
  40.6 0.0 collective-permute-done.10.refs_1_
  40.6 0.0 collective-permute-done.12.refs_3_
  40.6 0.0 collective-permute-done.13.refs_4_
  40.6 4.3 %ladder_2.1 = (bf16[32,64,2048]{2,1,0:T(8,128)(2,1)S(1)}, bf16[132,64,384]{2,1,0:T(8,128)(2,1)S(1)}, f32[2,8,128]{2,1,0:T(8,128)S(1)}) custom-call(s32[1]{0:T(128)} %bitcast.me_ref, s32[8]{0:T(128)S(1)} %copy-done.4, s32[32]{0:T(128)S(1)} %get-tuple-element.52.order_ref, ...), custom_call_target="tpu_custom_call", output_to_operand_aliasing={{0}: (9, {}), {1}: (10, {})} | custom-call | flops 503316480 | bytes 2621440 | tf_op jit(solution)/shard_map/ladder_2/pallas_call | solution.py:252
  44.9 0.2 collective-permute-done.11.refs_3_
  45.1 0.3 collective-permute-start.14
  45.5 0.2 collective-permute-start.15
  45.7 0.3 collective-permute-done.9.refs_2_
  46.1 0.0 collective-permute-start.17
  46.1 0.5 collective-permute-start.16
  46.6 0.1 collective-permute-done.14.refs_0_
  46.6 0.3 collective-permute-done.15.refs_1_
  46.9 2.8 %ladder_3.1 = (bf16[32,64,2048]{2,1,0:T(8,128)(2,1)S(1)}, bf16[132,64,384]{2,1,0:T(8,128)(2,1)S(1)}, f32[2,8,128]{2,1,0:T(8,128)S(1)}) custom-call(s32[1]{0:T(128)} %bitcast.me_ref, s32[8]{0:T(128)S(1)} %copy-done.4, s32[32]{0:T(128)S(1)} %get-tuple-element.52.order_ref, ...), custom_call_target="tpu_custom_call", output_to_operand_aliasing={{0}: (9, {}), {1}: (10, {})} | custom-call | flops 201326592 | bytes 1048576 | tf_op jit(solution)/shard_map/ladder_3/pallas_call | solution.py:252
  49.8 1.8 %ladder_4.1 = (bf16[32,64,2048]{2,1,0:T(8,128)(2,1)S(1)}, bf16[132,64,384]{2,1,0:T(8,128)(2,1)S(1)}, f32[2,8,128]{2,1,0:T(8,128)S(1)}) custom-call(s32[1]{0:T(128)} %bitcast.me_ref, s32[8]{0:T(128)S(1)} %copy-done.4, s32[32]{0:T(128)S(1)} %get-tuple-element.52.order_ref, ...), custom_call_target="tpu_custom_call", output_to_operand_aliasing={{0}: (9, {}), {1}: (10, {})} | custom-call | flops 100663296 | bytes 524288 | tf_op jit(solution)/shard_map/ladder_4/pallas_call | solution.py:252
  51.6 0.3 collective-permute-start.18
  51.9 1.6 %collective-permute-start.19 = (f32[2,8,128]{2,1,0:T(8,128)S(1)}, f32[2,8,128]{2,1,0:T(8,128)S(1)}, u32[]{:S(2)}, u32[]{:S(2)}) collective-permute-start(f32[2,8,128]{2,1,0:T(8,128)S(1)} %get-tuple-element.97), channel_id=1, source_target_pairs={{0,2},{1,3},{2,0},{3,1},{4,6},{5,7},{6,4},{7,5},{8,10},{9,11},{10,... | collective-permute-start | bytes 24584 | tf_op jit(solution)/shard_map/ppermute | solution.py:319
  53.5 0.1 collective-permute-start.20
  53.6 2.1 %deliver_0.1.refs_0_ = bf16[32,64,2048]{2,1,0:T(8,128)(2,1)} custom-call(bf16[32,64,2048]{2,1,0:T(8,128)(2,1)S(1)} %get-tuple-element.99.held_ref), custom_call_target="tpu_custom_call" | custom-call | tf_op jit(solution)/shard_map/deliver_0/pallas_call | solution.py:292
  55.7 0.9 %collective-permute-done.20 = f32[2,8,128]{2,1,0:T(8,128)S(1)} collective-permute-done((f32[2,8,128]{2,1,0:T(8,128)S(1)}, f32[2,8,128]{2,1,0:T(8,128)S(1)}, u32[]{:S(2)}, u32[]{:S(2)}) %collective-permute-start.20) | collective-permute-done | bytes 8224 | tf_op jit(solution)/shard_map/ppermute | solution.py:319
  56.6 2.0 %collective-permute-start.21 = (f32[2,8,128]{2,1,0:T(8,128)S(1)}, f32[2,8,128]{2,1,0:T(8,128)S(1)}, u32[]{:S(2)}, u32[]{:S(2)}) collective-permute-start(f32[2,8,128]{2,1,0:T(8,128)S(1)} %add_add_fusion), channel_id=1, source_target_pairs={{0,4},{1,5},{2,6},{3,7},{4,0},{5,1},{6,2},{7,3},{8,12},{9,13},{10,... | collective-permute-start | bytes 24584 | tf_op jit(solution)/shard_map/ppermute | solution.py:319
  58.6 2.7 %collective-permute-start.22 = (f32[2,8,128]{2,1,0:T(8,128)S(1)}, f32[2,8,128]{2,1,0:T(8,128)S(1)}, u32[]{:S(2)}, u32[]{:S(2)}) collective-permute-start(f32[2,8,128]{2,1,0:T(8,128)S(1)} %add_add_fusion), channel_id=1, source_target_pairs={{0,8},{1,9},{2,10},{3,11},{4,12},{5,13},{6,14},{7,15},{8,0},{9,1},... | collective-permute-start | bytes 24584 | tf_op jit(solution)/shard_map/ppermute | solution.py:319
  61.3 2.1 %deliver_1.1 = bf16[32,64,2048]{2,1,0:T(8,128)(2,1)} custom-call(bf16[32,64,2048]{2,1,0:T(8,128)(2,1)S(1)} %get-tuple-element.99.held_ref, bf16[32,64,2048]{2,1,0:T(8,128)(2,1)} %deliver_0.1.refs_0_), custom_call_target="tpu_custom_call", output_to_operand_aliasing={{}: (1, {})} | custom-call | tf_op jit(solution)/shard_map/deliver_1/pallas_call | solution.py:292
  63.4 3.3 %collective-permute-done.23 = f32[2,8,128]{2,1,0:T(8,128)S(1)} collective-permute-done((f32[2,8,128]{2,1,0:T(8,128)S(1)}, f32[2,8,128]{2,1,0:T(8,128)S(1)}, u32[]{:S(2)}, u32[]{:S(2)}) %collective-permute-start.23) | collective-permute-done | bytes 8224 | tf_op jit(solution)/shard_map/ppermute | solution.py:319
  66.7 0.1 add_reduce_fusion
  66.8 0.5 add_sqrt_fusion
  (26 shorter events, 0.1 us)
Async XLA Ops:
  0.6 13.4 %collective-permute-start = (bf16[8,64,384]{2,1,0:T(8,128)(2,1)}, bf16[8,64,384]{2,1,0:T(8,128)(2,1)S(1)}, u32[]{:S(2)}, u32[]{:S(2)}) collective-permute-start(bf16[8,64,384]{2,1,0:T(8,128)(2,1)} %refs_3_.1), channel_id=1, source_target_pairs={{0,4},{1,5},{2,6},{3,7},{4,12},{5,13},{6,14},{7,15},{8,0},{9,1},{1... | collective-permute-start | bytes 1179656 | tf_op jit(solution)/shard_map/ppermute | solution.py:316
  3.7 10.3 %collective-permute-start.1 = (bf16[8,64,384]{2,1,0:T(8,128)(2,1)}, bf16[8,64,384]{2,1,0:T(8,128)(2,1)S(1)}, u32[]{:S(2)}, u32[]{:S(2)}) collective-permute-start(bf16[8,64,384]{2,1,0:T(8,128)(2,1)} %refs_3_.1), channel_id=1, source_target_pairs={{0,1},{1,0},{2,3},{3,2},{4,5},{5,4},{6,7},{7,6},{8,9},{9,8},{10,11... | collective-permute-start | bytes 1179656 | tf_op jit(solution)/shard_map/ppermute | solution.py:319
  3.7 12.8 %collective-permute-start.4 = (bf16[8,64,384]{2,1,0:T(8,128)(2,1)}, bf16[8,64,384]{2,1,0:T(8,128)(2,1)S(1)}, u32[]{:S(2)}, u32[]{:S(2)}) collective-permute-start(bf16[8,64,384]{2,1,0:T(8,128)(2,1)} %refs_3_.1), channel_id=1, source_target_pairs={{0,2},{1,3},{2,0},{3,1},{4,6},{5,7},{6,4},{7,5},{8,10},{9,11},{10,... | collective-permute-start | bytes 1179656 | tf_op jit(solution)/shard_map/ppermute | solution.py:319
  5.2 0.7 copy-start.3
  5.9 0.7 copy-start.5
  14.0 11.2 %collective-permute-start.2 = (bf16[8,64,384]{2,1,0:T(8,128)(2,1)S(1)}, bf16[8,64,384]{2,1,0:T(8,128)(2,1)S(1)}, u32[]{:S(2)}, u32[]{:S(2)}) collective-permute-start(bf16[8,64,384]{2,1,0:T(8,128)(2,1)S(1)} %collective-permute-done.refs_0_), channel_id=1, source_target_pairs={{0,4},{1,5},{2,6},{3,7},{4,12},{5,13},{6,14},{7,15},{8,0},{9,1},{1... | collective-permute-start | bytes 1179656 | tf_op jit(solution)/shard_map/ppermute | solution.py:316
  15.0 10.3 %collective-permute-start.3 = (bf16[8,64,384]{2,1,0:T(8,128)(2,1)S(1)}, bf16[8,64,384]{2,1,0:T(8,128)(2,1)S(1)}, u32[]{:S(2)}, u32[]{:S(2)}) collective-permute-start(bf16[8,64,384]{2,1,0:T(8,128)(2,1)S(1)} %collective-permute-done.refs_0_), channel_id=1, source_target_pairs={{0,1},{1,0},{2,3},{3,2},{4,5},{5,4},{6,7},{7,6},{8,9},{9,8},{10,11... | collective-permute-start | bytes 1179656 | tf_op jit(solution)/shard_map/ppermute | solution.py:319
  15.0 12.4 %collective-permute-start.7 = (bf16[8,64,384]{2,1,0:T(8,128)(2,1)S(1)}, bf16[8,64,384]{2,1,0:T(8,128)(2,1)S(1)}, u32[]{:S(2)}, u32[]{:S(2)}) collective-permute-start(bf16[8,64,384]{2,1,0:T(8,128)(2,1)S(1)} %collective-permute-done.refs_0_), channel_id=1, source_target_pairs={{0,2},{1,3},{2,0},{3,1},{4,6},{5,7},{6,4},{7,5},{8,10},{9,11},{10,... | collective-permute-start | bytes 1179656 | tf_op jit(solution)/shard_map/ppermute | solution.py:319
  16.5 10.9 %collective-permute-start.8 = (bf16[8,64,384]{2,1,0:T(8,128)(2,1)S(1)}, bf16[8,64,384]{2,1,0:T(8,128)(2,1)S(1)}, u32[]{:S(2)}, u32[]{:S(2)}) collective-permute-start(bf16[8,64,384]{2,1,0:T(8,128)(2,1)S(1)} %collective-permute-done.4.refs_1_), channel_id=1, source_target_pairs={{0,1},{1,0},{2,3},{3,2},{4,5},{5,4},{6,7},{7,6},{8,9},{9,8},{10,11... | collective-permute-start | bytes 1179656 | tf_op jit(solution)/shard_map/ppermute | solution.py:319
  16.7 1.4 %copy-start = (bf16[32,64,384]{2,1,0:T(8,128)(2,1)S(1)}, bf16[32,64,384]{2,1,0:T(8,128)(2,1)}, u32[]{:S(2)}) copy-start(bf16[32,64,384]{2,1,0:T(8,128)(2,1)} %v_ref.9) | copy-start | bytes 4718596
  18.2 1.0 %copy-start.2 = (bf16[8,64,384]{2,1,0:T(8,128)(2,1)S(1)}, bf16[8,64,384]{2,1,0:T(8,128)(2,1)}, u32[]{:S(2)}) copy-start(bf16[8,64,384]{2,1,0:T(8,128)(2,1)} %refs_3_.1) | copy-start | bytes 1179652
  19.1 0.7 copy-start.4
  19.8 7.6 %copy-start.1 = (bf16[32,64,384]{2,1,0:T(8,128)(2,1)S(1)}, bf16[32,64,384]{2,1,0:T(8,128)(2,1)}, u32[]{:S(2)}) copy-start(bf16[32,64,384]{2,1,0:T(8,128)(2,1)} %v_ref.9) | copy-start | bytes 4718596
  25.3 4.8 %collective-permute-start.5 = (bf16[8,64,384]{2,1,0:T(8,128)(2,1)S(1)}, bf16[8,64,384]{2,1,0:T(8,128)(2,1)S(1)}, u32[]{:S(2)}, u32[]{:S(2)}) collective-permute-start(bf16[8,64,384]{2,1,0:T(8,128)(2,1)S(1)} %collective-permute-done.2.refs_0_), channel_id=1, source_target_pairs={{0,1},{1,0},{2,3},{3,2},{4,5},{5,4},{6,7},{7,6},{8,9},{9,8},{10,11... | collective-permute-start | bytes 1179656 | tf_op jit(solution)/shard_map/ppermute | solution.py:319
  25.3 12.4 %collective-permute-start.6 = (bf16[8,64,384]{2,1,0:T(8,128)(2,1)S(1)}, bf16[8,64,384]{2,1,0:T(8,128)(2,1)S(1)}, u32[]{:S(2)}, u32[]{:S(2)}) collective-permute-start(bf16[8,64,384]{2,1,0:T(8,128)(2,1)S(1)} %collective-permute-done.2.refs_0_), channel_id=1, source_target_pairs={{0,4},{1,5},{2,6},{3,7},{4,12},{5,13},{6,14},{7,15},{8,0},{9,1},{1... | collective-permute-start | bytes 1179656 | tf_op jit(solution)/shard_map/ppermute | solution.py:316
  26.3 14.2 %collective-permute-start.10 = (bf16[8,64,384]{2,1,0:T(8,128)(2,1)S(1)}, bf16[8,64,384]{2,1,0:T(8,128)(2,1)S(1)}, u32[]{:S(2)}, u32[]{:S(2)}) collective-permute-start(bf16[8,64,384]{2,1,0:T(8,128)(2,1)S(1)} %collective-permute-done.2.refs_0_), channel_id=1, source_target_pairs={{0,2},{1,3},{2,0},{3,1},{4,6},{5,7},{6,4},{7,5},{8,10},{9,11},{10,... | collective-permute-start | bytes 1179656 | tf_op jit(solution)/shard_map/ppermute | solution.py:319
  27.4 13.2 %collective-permute-start.12 = (bf16[8,64,384]{2,1,0:T(8,128)(2,1)S(1)}, bf16[8,64,384]{2,1,0:T(8,128)(2,1)S(1)}, u32[]{:S(2)}, u32[]{:S(2)}) collective-permute-start(bf16[8,64,384]{2,1,0:T(8,128)(2,1)S(1)} %collective-permute-done.7.refs_1_), channel_id=1, source_target_pairs={{0,1},{1,0},{2,3},{3,2},{4,5},{5,4},{6,7},{7,6},{8,9},{9,8},{10,11... | collective-permute-start | bytes 1179656 | tf_op jit(solution)/shard_map/ppermute | solution.py:319
  37.7 2.9 %collective-permute-start.13 = (bf16[8,64,384]{2,1,0:T(8,128)(2,1)S(1)}, bf16[8,64,384]{2,1,0:T(8,128)(2,1)S(1)}, u32[]{:S(2)}, u32[]{:S(2)}) collective-permute-start(bf16[8,64,384]{2,1,0:T(8,128)(2,1)S(1)} %collective-permute-done.6.refs_0_), channel_id=1, source_target_pairs={{0,1},{1,0},{2,3},{3,2},{4,5},{5,4},{6,7},{7,6},{8,9},{9,8},{10,11... | collective-permute-start | bytes 1179656 | tf_op jit(solution)/shard_map/ppermute | solution.py:319
  37.7 7.4 %collective-permute-start.11 = (bf16[4,64,384]{2,1,0:T(8,128)(2,1)S(1)}, bf16[4,64,384]{2,1,0:T(8,128)(2,1)S(1)}, u32[]{:S(2)}, u32[]{:S(2)}) collective-permute-start(bf16[4,64,384]{2,1,0:T(8,128)(2,1)S(1)} %slice.13), channel_id=1, source_target_pairs={{0,2},{1,3},{2,0},{3,1},{4,6},{5,7},{6,4},{7,5},{8,10},{9,11},{10,... | collective-permute-start | bytes 589832 | tf_op jit(solution)/shard_map/ppermute | solution.py:319
  39.0 7.0 %collective-permute-start.9 = (bf16[4,64,384]{2,1,0:T(8,128)(2,1)S(1)}, bf16[4,64,384]{2,1,0:T(8,128)(2,1)S(1)}, u32[]{:S(2)}, u32[]{:S(2)}) collective-permute-start(bf16[4,64,384]{2,1,0:T(8,128)(2,1)S(1)} %slice.16), channel_id=1, source_target_pairs={{0,8},{1,9},{2,10},{3,11},{4,0},{5,1},{6,2},{7,3},{8,12},{9,13},{1... | collective-permute-start | bytes 589832 | tf_op jit(solution)/shard_map/ppermute | solution.py:316
  45.1 1.5 %collective-permute-start.14 = (bf16[4,64,384]{2,1,0:T(8,128)(2,1)S(1)}, bf16[4,64,384]{2,1,0:T(8,128)(2,1)S(1)}, u32[]{:S(2)}, u32[]{:S(2)}) collective-permute-start(bf16[4,64,384]{2,1,0:T(8,128)(2,1)S(1)} %get-tuple-element.103), channel_id=1, source_target_pairs={{0,1},{1,0},{2,3},{3,2},{4,5},{5,4},{6,7},{7,6},{8,9},{9,8},{10,11... | collective-permute-start | bytes 589832 | tf_op jit(solution)/shard_map/ppermute | solution.py:319
  45.5 1.4 %collective-permute-start.15 = (bf16[4,64,384]{2,1,0:T(8,128)(2,1)S(1)}, bf16[4,64,384]{2,1,0:T(8,128)(2,1)S(1)}, u32[]{:S(2)}, u32[]{:S(2)}) collective-permute-start(bf16[4,64,384]{2,1,0:T(8,128)(2,1)S(1)} %get-tuple-element.102), channel_id=1, source_target_pairs={{0,1},{1,0},{2,3},{3,2},{4,5},{5,4},{6,7},{7,6},{8,9},{9,8},{10,11... | collective-permute-start | bytes 589832 | tf_op jit(solution)/shard_map/ppermute | solution.py:319
  46.1 3.7 %collective-permute-start.17 = (bf16[4,64,384]{2,1,0:T(8,128)(2,1)S(1)}, bf16[4,64,384]{2,1,0:T(8,128)(2,1)S(1)}, u32[]{:S(2)}, u32[]{:S(2)}) collective-permute-start(bf16[4,64,384]{2,1,0:T(8,128)(2,1)S(1)} %collective-permute-done.9.refs_2_), channel_id=1, source_target_pairs={{0,1},{1,0},{2,3},{3,2},{4,5},{5,4},{6,7},{7,6},{8,9},{9,8},{10,11... | collective-permute-start | bytes 589832 | tf_op jit(solution)/shard_map/ppermute | solution.py:319
  46.1 3.7 %collective-permute-start.16 = (bf16[4,64,384]{2,1,0:T(8,128)(2,1)S(1)}, bf16[4,64,384]{2,1,0:T(8,128)(2,1)S(1)}, u32[]{:S(2)}, u32[]{:S(2)}) collective-permute-start(bf16[4,64,384]{2,1,0:T(8,128)(2,1)S(1)} %collective-permute-done.11.refs_3_), channel_id=1, source_target_pairs={{0,1},{1,0},{2,3},{3,2},{4,5},{5,4},{6,7},{7,6},{8,9},{9,8},{10,11... | collective-permute-start | bytes 589832 | tf_op jit(solution)/shard_map/ppermute | solution.py:319
  51.6 4.0 %collective-permute-start.18 = (f32[2,8,128]{2,1,0:T(8,128)S(1)}, f32[2,8,128]{2,1,0:T(8,128)S(1)}, u32[]{:S(2)}, u32[]{:S(2)}) collective-permute-start(f32[2,8,128]{2,1,0:T(8,128)S(1)} %get-tuple-element.97), channel_id=1, source_target_pairs={{0,1},{1,0},{2,3},{3,2},{4,5},{5,4},{6,7},{7,6},{8,9},{9,8},{10,11... | collective-permute-start | bytes 24584 | tf_op jit(solution)/shard_map/ppermute | solution.py:319
  51.9 3.7 %collective-permute-start.19 = (f32[2,8,128]{2,1,0:T(8,128)S(1)}, f32[2,8,128]{2,1,0:T(8,128)S(1)}, u32[]{:S(2)}, u32[]{:S(2)}) collective-permute-start(f32[2,8,128]{2,1,0:T(8,128)S(1)} %get-tuple-element.97), channel_id=1, source_target_pairs={{0,2},{1,3},{2,0},{3,1},{4,6},{5,7},{6,4},{7,5},{8,10},{9,11},{10,... | collective-permute-start | bytes 24584 | tf_op jit(solution)/shard_map/ppermute | solution.py:319
  53.5 3.1 %collective-permute-start.20 = (f32[2,8,128]{2,1,0:T(8,128)S(1)}, f32[2,8,128]{2,1,0:T(8,128)S(1)}, u32[]{:S(2)}, u32[]{:S(2)}) collective-permute-start(f32[2,8,128]{2,1,0:T(8,128)S(1)} %get-tuple-element.97), channel_id=1, source_target_pairs={{0,3},{1,2},{2,1},{3,0},{4,7},{5,6},{6,5},{7,4},{8,11},{9,10},{10,... | collective-permute-start | bytes 24584 | tf_op jit(solution)/shard_map/ppermute | solution.py:319
  56.6 6.8 %collective-permute-start.21 = (f32[2,8,128]{2,1,0:T(8,128)S(1)}, f32[2,8,128]{2,1,0:T(8,128)S(1)}, u32[]{:S(2)}, u32[]{:S(2)}) collective-permute-start(f32[2,8,128]{2,1,0:T(8,128)S(1)} %add_add_fusion), channel_id=1, source_target_pairs={{0,4},{1,5},{2,6},{3,7},{4,0},{5,1},{6,2},{7,3},{8,12},{9,13},{10,... | collective-permute-start | bytes 24584 | tf_op jit(solution)/shard_map/ppermute | solution.py:319
  58.6 4.8 %collective-permute-start.22 = (f32[2,8,128]{2,1,0:T(8,128)S(1)}, f32[2,8,128]{2,1,0:T(8,128)S(1)}, u32[]{:S(2)}, u32[]{:S(2)}) collective-permute-start(f32[2,8,128]{2,1,0:T(8,128)S(1)} %add_add_fusion), channel_id=1, source_target_pairs={{0,8},{1,9},{2,10},{3,11},{4,12},{5,13},{6,14},{7,15},{8,0},{9,1},... | collective-permute-start | bytes 24584 | tf_op jit(solution)/shard_map/ppermute | solution.py:319
  61.3 5.4 %collective-permute-start.23 = (f32[2,8,128]{2,1,0:T(8,128)S(1)}, f32[2,8,128]{2,1,0:T(8,128)S(1)}, u32[]{:S(2)}, u32[]{:S(2)}) collective-permute-start(f32[2,8,128]{2,1,0:T(8,128)S(1)} %add_add_fusion), channel_id=1, source_target_pairs={{0,12},{1,13},{2,14},{3,15},{4,8},{5,9},{6,10},{7,11},{8,4},{9,5},... | collective-permute-start | bytes 24584 | tf_op jit(solution)/shard_map/ppermute | solution.py:319

commit v19 on v16

--- a/solution.py
+++ b/solution.py
@@ -330,7 +330,7 @@
             b.append(swap(a[k], 2))
             a.append(shift_z(a[k], 1))
         else:
-            part = 3 * shard_tiles // 8
+            part = shard_tiles // 2
             c[-1], a[k], back, state = lax.optimization_barrier(
                 (c[-1], a[k], b[0][part:], state)
             )
@@ -349,7 +349,9 @@
             fresh[k, 0, 1, 0] = c[k]
         state = ladder(k - 1, depth, shard_tiles, integrals, listing, state, fresh)
     b[-1], last[0], state = lax.optimization_barrier((b[-1], last[0], state))
-    first, second = {(k - 1, 1, 1, 0): swap(b[-1], 1)}, {(k, 1, 1, 0): swap(last[0], 1)}
+    first, second = {}, {(k, 1, 1, 0): swap(last[0], 1)}
+    for tile in (0, part):
+        first[k - 1, 1, 1, tile] = swap(b[-1][tile:tile + part], 1)
     last[part], state = lax.optimization_barrier((last[part], state))
     second[k, 1, 1, part] = swap(last[part], 1)
     for tile, piece in last.items():
@@ -359,10 +361,10 @@
 
     residual, _, stats = state
     out = deliver(residual, 0)
-    stats = sum([swap(stats, bits) for bits in (1, 2, 3)], stats)
+    stats = sum([swap(stats, bits) for bits in (3, 2, 1)], stats)
     stats, residual, out = lax.optimization_barrier((stats, residual, out))
     out = deliver(residual, 1, out)
-    stats = sum([swap(stats, 4 * bits) for bits in range(1, depth)], stats)
+    stats = sum([swap(stats, 4 * bits) for bits in range(depth - 1, 0, -1)], stats)
     irrep_sums, ab_counts = jnp.sum(stats, axis=2)
     entries = ab_counts * ij_counts.astype(jnp.float32) * float(rows * rows)
     return out, jnp.sqrt(irrep_sums / entries + 1e-06)

time: 66.8 us -> 65 us (0.973)
  waiting for transfers between devices: 18.4 us -> 16.5 us
  Pallas kernels: 21.8 us -> 22.7 us
    ppermute x4, waiting for transfers between devices: 16.2 us -> 14.4 us  [shift_z(): return lax.ppermute(x, 'vir', pairs)]
    pallas_call x5, Pallas kernels: 13.8 us -> 14.6 us  [ladder(): pl.pallas_call(functools.partial(ladder_kernel, call, depth, shard_tiles,...]
    ppermute x19 -> x20, starting transfers between devices: 14 us -> 13.4 us  [swap(): return lax.ppermute(x, 'vir', [(d, d ^ bits) for d in range(devices)])]
    ppermute x19 -> x20, waiting for transfers between devices: 2.18 us -> 2.12 us  [swap(): return lax.ppermute(x, 'vir', [(d, d ^ bits) for d in range(devices)])]
  transfers between devices with their start and end apart: 23 -> 24, of which waited for: 8 -> 9; matrix products, arithmetic and copies ran while one was open for 0% -> 0% of each run, Pallas kernels for 30% -> 32%
where the time goes in v19:
time: 65 us; the launch traced here: 64.8 us
  Pallas kernels  22.7 us (35%)
  starting transfers between devices  19.7 us (30%)
  waiting for transfers between devices  16.5 us (25%)
  local copies, waits for them, and re-layouts  4.45 us (7%)
  between operations  0.79 us (1%)
    pallas_call x5, Pallas kernels, ladder(): pl.pallas_call(functools.partial(ladder_kernel, call, depth, shard_tiles,...  14.6 us
    ppermute x4, waiting for transfers between devices, shift_z(): return lax.ppermute(x, 'vir', pairs)  14.4 us
    ppermute x20, starting transfers between devices, swap(): return lax.ppermute(x, 'vir', [(d, d ^ bits) for d in range(devices)])  13.4 us
    ppermute x4, starting transfers between devices, shift_z(): return lax.ppermute(x, 'vir', pairs)  6.3 us
    unnamed x12, local copies, waits for them, and re-layouts  4.37 us
    pallas_call x2, Pallas kernels, deliver(): pl.pallas_call(functools.partial(deliver_kernel, part), out_shape=jax.Sha...  4.04 us
    pallas_call x1, Pallas kernels, prepare(): pl.pallas_call(functools.partial(prepare_kernel, depth, shard_tiles), out...  4.01 us
    ppermute x20, waiting for transfers between devices, swap(): return lax.ppermute(x, 'vir', [(d, d ^ bits) for d in range(devices)])  2.12 us
  transfers between devices with their start and end apart: 24, of which 9 were waited for; matrix products, arithmetic and copies ran while one was open for 0% of the time, Pallas kernels for 32%

profile of v19, /device:TPU:0, one launch (start us, length us, event | category | flops | bytes accessed | tf_op | source)
XLA Modules:
  0.0 64.8 jit_solution(5609883539834045006)
XLA Ops:
  0.6 3.1 %collective-permute-start = (bf16[8,64,384]{2,1,0:T(8,128)(2,1)}, bf16[8,64,384]{2,1,0:T(8,128)(2,1)S(1)}, u32[]{:S(2)}, u32[]{:S(2)}) collective-permute-start(bf16[8,64,384]{2,1,0:T(8,128)(2,1)} %refs_3_.1), channel_id=1, source_target_pairs={{0,4},{1,5},{2,6},{3,7},{4,12},{5,13},{6,14},{7,15},{8,0},{9,1},{1... | collective-permute-start | bytes 1179656 | tf_op jit(solution)/shard_map/ppermute | solution.py:314
  3.7 0.0 collective-permute-start.1
  3.7 1.5 %collective-permute-start.4 = (bf16[8,64,384]{2,1,0:T(8,128)(2,1)}, bf16[8,64,384]{2,1,0:T(8,128)(2,1)S(1)}, u32[]{:S(2)}, u32[]{:S(2)}) collective-permute-start(bf16[8,64,384]{2,1,0:T(8,128)(2,1)} %refs_3_.1), channel_id=1, source_target_pairs={{0,2},{1,3},{2,0},{3,1},{4,6},{5,7},{6,4},{7,5},{8,10},{9,11},{10,... | collective-permute-start | bytes 1179656 | tf_op jit(solution)/shard_map/ppermute | solution.py:317
  5.2 0.7 %copy-done.3 = s32[8]{0:T(128)S(1)} copy-done((s32[8]{0:T(128)S(1)}, s32[8]{0:T(128)}, u32[]{:S(2)}) %copy-start.3) | copy-done | bytes 56
  5.9 0.7 %copy-done.5 = s32[32]{0:T(128)S(1)} copy-done((s32[32]{0:T(128)S(1)}, s32[32]{0:T(128)}, u32[]{:S(2)}) %copy-start.5) | copy-done | bytes 152
  6.5 4.0 %prepare.1 = (bf16[32,64,2048]{2,1,0:T(8,128)(2,1)S(1)}, bf16[132,64,384]{2,1,0:T(8,128)(2,1)S(1)}, f32[2,8,128]{2,1,0:T(8,128)S(1)}, s32[32]{0:T(128)S(1)}, s32...) custom-call(s32[1]{0:T(128)} %bitcast.me_ref, s32[8]{0:T(128)S(1)} %copy-done.3, s32[32]{0:T(128)S(1)} %copy-done.5), custom_call_target="tpu_custom_call" | custom-call | bytes 8388608 | tf_op jit(solution)/shard_map/prepare/pallas_call | solution.py:135
  10.6 3.5 %collective-permute-done.refs_0_ = bf16[8,64,384]{2,1,0:T(8,128)(2,1)S(1)} collective-permute-done((bf16[8,64,384]{2,1,0:T(8,128)(2,1)}, bf16[8,64,384]{2,1,0:T(8,128)(2,1)S(1)}, u32[]{:S(2)}, u32[]{:S(2)}) %collective-permute-start) | collective-permute-done | bytes 393248 | tf_op jit(solution)/shard_map/ppermute | solution.py:314
  14.0 0.0 collective-permute-done.1.refs_2_
  14.0 0.9 %collective-permute-start.2 = (bf16[8,64,384]{2,1,0:T(8,128)(2,1)S(1)}, bf16[8,64,384]{2,1,0:T(8,128)(2,1)S(1)}, u32[]{:S(2)}, u32[]{:S(2)}) collective-permute-start(bf16[8,64,384]{2,1,0:T(8,128)(2,1)S(1)} %collective-permute-done.refs_0_), channel_id=1, source_target_pairs={{0,4},{1,5},{2,6},{3,7},{4,12},{5,13},{6,14},{7,15},{8,0},{9,1},{1... | collective-permute-start | bytes 1179656 | tf_op jit(solution)/shard_map/ppermute | solution.py:314
  15.0 1.5 %collective-permute-start.7 = (bf16[8,64,384]{2,1,0:T(8,128)(2,1)S(1)}, bf16[8,64,384]{2,1,0:T(8,128)(2,1)S(1)}, u32[]{:S(2)}, u32[]{:S(2)}) collective-permute-start(bf16[8,64,384]{2,1,0:T(8,128)(2,1)S(1)} %collective-permute-done.refs_0_), channel_id=1, source_target_pairs={{0,2},{1,3},{2,0},{3,1},{4,6},{5,7},{6,4},{7,5},{8,10},{9,11},{10,... | collective-permute-start | bytes 1179656 | tf_op jit(solution)/shard_map/ppermute | solution.py:317
  16.5 0.0 collective-permute-done.4.refs_1_
  16.5 0.2 collective-permute-start.8
  16.7 1.4 %copy-done = bf16[32,64,384]{2,1,0:T(8,128)(2,1)S(1)} copy-done((bf16[32,64,384]{2,1,0:T(8,128)(2,1)S(1)}, bf16[32,64,384]{2,1,0:T(8,128)(2,1)}, u32[]{:S(2)}) %copy-start) | copy-done | bytes 1572888
  18.2 1.0 %copy-done.2 = bf16[8,64,384]{2,1,0:T(8,128)(2,1)S(1)} copy-done((bf16[8,64,384]{2,1,0:T(8,128)(2,1)S(1)}, bf16[8,64,384]{2,1,0:T(8,128)(2,1)}, u32[]{:S(2)}) %copy-start.2) | copy-done | bytes 393240
  19.1 0.7 %copy-done.4 = s32[8]{0:T(128)S(1)} copy-done((s32[8]{0:T(128)S(1)}, s32[8]{0:T(128)}, u32[]{:S(2)}) %copy-start.4) | copy-done | bytes 56
  19.8 2.6 %ladder_0.1 = (bf16[32,64,2048]{2,1,0:T(8,128)(2,1)S(1)}, bf16[132,64,384]{2,1,0:T(8,128)(2,1)S(1)}, f32[2,8,128]{2,1,0:T(8,128)S(1)}) custom-call(s32[1]{0:T(128)} %bitcast.me_ref, s32[8]{0:T(128)S(1)} %copy-done.4, s32[32]{0:T(128)S(1)} %get-tuple-element.52.order_ref, ...), custom_call_target="tpu_custom_call", output_to_operand_aliasing={{0}: (9, {}), {1}: (10, {})} | custom-call | flops 402653184 | bytes 2097152 | tf_op jit(solution)/shard_map/ladder_0/pallas_call | solution.py:252
  22.4 2.9 %collective-permute-done.2.refs_0_ = bf16[8,64,384]{2,1,0:T(8,128)(2,1)S(1)} collective-permute-done((bf16[8,64,384]{2,1,0:T(8,128)(2,1)S(1)}, bf16[8,64,384]{2,1,0:T(8,128)(2,1)S(1)}, u32[]{:S(2)}, u32[]{:S(2)}) %collective-permute-start.2) | collective-permute-done | bytes 393248 | tf_op jit(solution)/shard_map/ppermute | solution.py:314
  25.3 0.0 collective-permute-done.3.refs_2_
  25.3 0.0 collective-permute-start.5
  25.3 0.8 %collective-permute-start.6 = (bf16[8,64,384]{2,1,0:T(8,128)(2,1)S(1)}, bf16[8,64,384]{2,1,0:T(8,128)(2,1)S(1)}, u32[]{:S(2)}, u32[]{:S(2)}) collective-permute-start(bf16[8,64,384]{2,1,0:T(8,128)(2,1)S(1)} %collective-permute-done.2.refs_0_), channel_id=1, source_target_pairs={{0,4},{1,5},{2,6},{3,7},{4,12},{5,13},{6,14},{7,15},{8,0},{9,1},{1... | collective-permute-start | bytes 1179656 | tf_op jit(solution)/shard_map/ppermute | solution.py:314
  26.0 1.3 %collective-permute-start.10 = (bf16[8,64,384]{2,1,0:T(8,128)(2,1)S(1)}, bf16[8,64,384]{2,1,0:T(8,128)(2,1)S(1)}, u32[]{:S(2)}, u32[]{:S(2)}) collective-permute-start(bf16[8,64,384]{2,1,0:T(8,128)(2,1)S(1)} %collective-permute-done.2.refs_0_), channel_id=1, source_target_pairs={{0,2},{1,3},{2,0},{3,1},{4,6},{5,7},{6,4},{7,5},{8,10},{9,11},{10,... | collective-permute-start | bytes 1179656 | tf_op jit(solution)/shard_map/ppermute | solution.py:317
  27.4 0.0 collective-permute-done.7.refs_1_
  27.4 2.6 %ladder_1.1 = (bf16[32,64,2048]{2,1,0:T(8,128)(2,1)S(1)}, bf16[132,64,384]{2,1,0:T(8,128)(2,1)S(1)}, f32[2,8,128]{2,1,0:T(8,128)S(1)}) custom-call(s32[1]{0:T(128)} %bitcast.me_ref, s32[8]{0:T(128)S(1)} %copy-done.4, s32[32]{0:T(128)S(1)} %get-tuple-element.52.order_ref, ...), custom_call_target="tpu_custom_call", output_to_operand_aliasing={{0}: (9, {}), {1}: (10, {})} | custom-call | flops 402653184 | bytes 2097152 | tf_op jit(solution)/shard_map/ladder_1/pallas_call | solution.py:252
  30.0 7.7 %collective-permute-done.6.refs_0_ = bf16[8,64,384]{2,1,0:T(8,128)(2,1)S(1)} collective-permute-done((bf16[8,64,384]{2,1,0:T(8,128)(2,1)S(1)}, bf16[8,64,384]{2,1,0:T(8,128)(2,1)S(1)}, u32[]{:S(2)}, u32[]{:S(2)}) %collective-permute-start.6) | collective-permute-done | bytes 393248 | tf_op jit(solution)/shard_map/ppermute | solution.py:314
  37.7 1.3 %collective-permute-start.11 = (bf16[4,64,384]{2,1,0:T(8,128)(2,1)S(1)}, bf16[4,64,384]{2,1,0:T(8,128)(2,1)S(1)}, u32[]{:S(2)}, u32[]{:S(2)}) collective-permute-start(bf16[4,64,384]{2,1,0:T(8,128)(2,1)S(1)} %slice.13), channel_id=1, source_target_pairs={{0,2},{1,3},{2,0},{3,1},{4,6},{5,7},{6,4},{7,5},{8,10},{9,11},{10,... | collective-permute-start | bytes 589832 | tf_op jit(solution)/shard_map/ppermute | solution.py:317
  39.0 1.5 %collective-permute-start.9 = (bf16[4,64,384]{2,1,0:T(8,128)(2,1)S(1)}, bf16[4,64,384]{2,1,0:T(8,128)(2,1)S(1)}, u32[]{:S(2)}, u32[]{:S(2)}) collective-permute-start(bf16[4,64,384]{2,1,0:T(8,128)(2,1)S(1)} %slice.16), channel_id=1, source_target_pairs={{0,8},{1,9},{2,10},{3,11},{4,0},{5,1},{6,2},{7,3},{8,12},{9,13},{1... | collective-permute-start | bytes 589832 | tf_op jit(solution)/shard_map/ppermute | solution.py:314
  40.6 4.3 %ladder_2.1 = (bf16[32,64,2048]{2,1,0:T(8,128)(2,1)S(1)}, bf16[132,64,384]{2,1,0:T(8,128)(2,1)S(1)}, f32[2,8,128]{2,1,0:T(8,128)S(1)}) custom-call(s32[1]{0:T(128)} %bitcast.me_ref, s32[8]{0:T(128)S(1)} %copy-done.4, s32[32]{0:T(128)S(1)} %get-tuple-element.52.order_ref, ...), custom_call_target="tpu_custom_call", output_to_operand_aliasing={{0}: (9, {}), {1}: (10, {})} | custom-call | flops 503316480 | bytes 2621440 | tf_op jit(solution)/shard_map/ladder_2/pallas_call | solution.py:252
  44.9 0.2 collective-permute-done.11.refs_3_
  45.1 0.1 collective-permute-start.14
  45.2 0.5 collective-permute-start.15
  45.7 0.3 collective-permute-done.9.refs_2_
  46.1 0.5 collective-permute-start.16
  46.6 0.1 collective-permute-done.14.refs_0_
  46.6 0.3 collective-permute-done.15.refs_1_
  46.9 3.3 %ladder_3.1 = (bf16[32,64,2048]{2,1,0:T(8,128)(2,1)S(1)}, bf16[132,64,384]{2,1,0:T(8,128)(2,1)S(1)}, f32[2,8,128]{2,1,0:T(8,128)S(1)}) custom-call(s32[1]{0:T(128)} %bitcast.me_ref, s32[8]{0:T(128)S(1)} %copy-done.4, s32[32]{0:T(128)S(1)} %get-tuple-element.52.order_ref, ...), custom_call_target="tpu_custom_call", output_to_operand_aliasing={{0}: (9, {}), {1}: (10, {})} | custom-call | flops 201326592 | bytes 1048576 | tf_op jit(solution)/shard_map/ladder_3/pallas_call | solution.py:252
  50.3 1.8 %ladder_4.1 = (bf16[32,64,2048]{2,1,0:T(8,128)(2,1)S(1)}, bf16[132,64,384]{2,1,0:T(8,128)(2,1)S(1)}, f32[2,8,128]{2,1,0:T(8,128)S(1)}) custom-call(s32[1]{0:T(128)} %bitcast.me_ref, s32[8]{0:T(128)S(1)} %copy-done.4, s32[32]{0:T(128)S(1)} %get-tuple-element.52.order_ref, ...), custom_call_target="tpu_custom_call", output_to_operand_aliasing={{0}: (9, {}), {1}: (10, {})} | custom-call | flops 100663296 | bytes 524288 | tf_op jit(solution)/shard_map/ladder_4/pallas_call | solution.py:252
  52.1 0.6 collective-permute-start.18
  52.8 0.8 %collective-permute-start.19 = (f32[2,8,128]{2,1,0:T(8,128)S(1)}, f32[2,8,128]{2,1,0:T(8,128)S(1)}, u32[]{:S(2)}, u32[]{:S(2)}) collective-permute-start(f32[2,8,128]{2,1,0:T(8,128)S(1)} %get-tuple-element.97), channel_id=1, source_target_pairs={{0,2},{1,3},{2,0},{3,1},{4,6},{5,7},{6,4},{7,5},{8,10},{9,11},{10,... | collective-permute-start | bytes 24584 | tf_op jit(solution)/shard_map/ppermute | solution.py:317
  53.5 0.5 collective-permute-start.20
  54.0 2.0 %deliver_0.1.refs_0_ = bf16[32,64,2048]{2,1,0:T(8,128)(2,1)} custom-call(bf16[32,64,2048]{2,1,0:T(8,128)(2,1)S(1)} %get-tuple-element.99.held_ref), custom_call_target="tpu_custom_call" | custom-call | tf_op jit(solution)/shard_map/deliver_0/pallas_call | solution.py:290
  56.1 0.3 collective-permute-done.19
  56.4 3.2 %collective-permute-start.21 = (f32[2,8,128]{2,1,0:T(8,128)S(1)}, f32[2,8,128]{2,1,0:T(8,128)S(1)}, u32[]{:S(2)}, u32[]{:S(2)}) collective-permute-start(f32[2,8,128]{2,1,0:T(8,128)S(1)} %add_add_fusion), channel_id=1, source_target_pairs={{0,12},{1,13},{2,14},{3,15},{4,8},{5,9},{6,10},{7,11},{8,4},{9,5},... | collective-permute-start | bytes 24584 | tf_op jit(solution)/shard_map/ppermute | solution.py:317
  59.6 0.1 collective-permute-start.22
  59.7 1.2 %collective-permute-start.23 = (f32[2,8,128]{2,1,0:T(8,128)S(1)}, f32[2,8,128]{2,1,0:T(8,128)S(1)}, u32[]{:S(2)}, u32[]{:S(2)}) collective-permute-start(f32[2,8,128]{2,1,0:T(8,128)S(1)} %add_add_fusion), channel_id=1, source_target_pairs={{0,4},{1,5},{2,6},{3,7},{4,0},{5,1},{6,2},{7,3},{8,12},{9,13},{10,... | collective-permute-start | bytes 24584 | tf_op jit(solution)/shard_map/ppermute | solution.py:317
  60.9 2.0 %deliver_1.1 = bf16[32,64,2048]{2,1,0:T(8,128)(2,1)} custom-call(bf16[32,64,2048]{2,1,0:T(8,128)(2,1)S(1)} %get-tuple-element.99.held_ref, bf16[32,64,2048]{2,1,0:T(8,128)(2,1)} %deliver_0.1.refs_0_), custom_call_target="tpu_custom_call", output_to_operand_aliasing={{}: (1, {})} | custom-call | tf_op jit(solution)/shard_map/deliver_1/pallas_call | solution.py:290
  62.9 1.2 %collective-permute-done.22 = f32[2,8,128]{2,1,0:T(8,128)S(1)} collective-permute-done((f32[2,8,128]{2,1,0:T(8,128)S(1)}, f32[2,8,128]{2,1,0:T(8,128)S(1)}, u32[]{:S(2)}, u32[]{:S(2)}) %collective-permute-start.22) | collective-permute-done | bytes 8224 | tf_op jit(solution)/shard_map/ppermute | solution.py:317
  64.1 0.1 add_reduce_fusion
  64.2 0.5 add_sqrt_fusion
  (26 shorter events, 0.1 us)
Async XLA Ops:
  0.6 13.4 %collective-permute-start = (bf16[8,64,384]{2,1,0:T(8,128)(2,1)}, bf16[8,64,384]{2,1,0:T(8,128)(2,1)S(1)}, u32[]{:S(2)}, u32[]{:S(2)}) collective-permute-start(bf16[8,64,384]{2,1,0:T(8,128)(2,1)} %refs_3_.1), channel_id=1, source_target_pairs={{0,4},{1,5},{2,6},{3,7},{4,12},{5,13},{6,14},{7,15},{8,0},{9,1},{1... | collective-permute-start | bytes 1179656 | tf_op jit(solution)/shard_map/ppermute | solution.py:314
  3.7 10.3 %collective-permute-start.1 = (bf16[8,64,384]{2,1,0:T(8,128)(2,1)}, bf16[8,64,384]{2,1,0:T(8,128)(2,1)S(1)}, u32[]{:S(2)}, u32[]{:S(2)}) collective-permute-start(bf16[8,64,384]{2,1,0:T(8,128)(2,1)} %refs_3_.1), channel_id=1, source_target_pairs={{0,1},{1,0},{2,3},{3,2},{4,5},{5,4},{6,7},{7,6},{8,9},{9,8},{10,11... | collective-permute-start | bytes 1179656 | tf_op jit(solution)/shard_map/ppermute | solution.py:317
  3.7 12.8 %collective-permute-start.4 = (bf16[8,64,384]{2,1,0:T(8,128)(2,1)}, bf16[8,64,384]{2,1,0:T(8,128)(2,1)S(1)}, u32[]{:S(2)}, u32[]{:S(2)}) collective-permute-start(bf16[8,64,384]{2,1,0:T(8,128)(2,1)} %refs_3_.1), channel_id=1, source_target_pairs={{0,2},{1,3},{2,0},{3,1},{4,6},{5,7},{6,4},{7,5},{8,10},{9,11},{10,... | collective-permute-start | bytes 1179656 | tf_op jit(solution)/shard_map/ppermute | solution.py:317
  5.2 0.7 %copy-start.3 = (s32[8]{0:T(128)S(1)}, s32[8]{0:T(128)}, u32[]{:S(2)}) copy-start(s32[8]{0:T(128)} %counts_ref.11) | copy-start | bytes 100
  5.9 0.7 %copy-start.5 = (s32[32]{0:T(128)S(1)}, s32[32]{0:T(128)}, u32[]{:S(2)}) copy-start(s32[32]{0:T(128)} %irrep_ref.1) | copy-start | bytes 388
  14.0 11.2 %collective-permute-start.2 = (bf16[8,64,384]{2,1,0:T(8,128)(2,1)S(1)}, bf16[8,64,384]{2,1,0:T(8,128)(2,1)S(1)}, u32[]{:S(2)}, u32[]{:S(2)}) collective-permute-start(bf16[8,64,384]{2,1,0:T(8,128)(2,1)S(1)} %collective-permute-done.refs_0_), channel_id=1, source_target_pairs={{0,4},{1,5},{2,6},{3,7},{4,12},{5,13},{6,14},{7,15},{8,0},{9,1},{1... | collective-permute-start | bytes 1179656 | tf_op jit(solution)/shard_map/ppermute | solution.py:314
  15.0 10.3 %collective-permute-start.3 = (bf16[8,64,384]{2,1,0:T(8,128)(2,1)S(1)}, bf16[8,64,384]{2,1,0:T(8,128)(2,1)S(1)}, u32[]{:S(2)}, u32[]{:S(2)}) collective-permute-start(bf16[8,64,384]{2,1,0:T(8,128)(2,1)S(1)} %collective-permute-done.refs_0_), channel_id=1, source_target_pairs={{0,1},{1,0},{2,3},{3,2},{4,5},{5,4},{6,7},{7,6},{8,9},{9,8},{10,11... | collective-permute-start | bytes 1179656 | tf_op jit(solution)/shard_map/ppermute | solution.py:317
  15.0 12.4 %collective-permute-start.7 = (bf16[8,64,384]{2,1,0:T(8,128)(2,1)S(1)}, bf16[8,64,384]{2,1,0:T(8,128)(2,1)S(1)}, u32[]{:S(2)}, u32[]{:S(2)}) collective-permute-start(bf16[8,64,384]{2,1,0:T(8,128)(2,1)S(1)} %collective-permute-done.refs_0_), channel_id=1, source_target_pairs={{0,2},{1,3},{2,0},{3,1},{4,6},{5,7},{6,4},{7,5},{8,10},{9,11},{10,... | collective-permute-start | bytes 1179656 | tf_op jit(solution)/shard_map/ppermute | solution.py:317
  16.5 10.9 %collective-permute-start.8 = (bf16[8,64,384]{2,1,0:T(8,128)(2,1)S(1)}, bf16[8,64,384]{2,1,0:T(8,128)(2,1)S(1)}, u32[]{:S(2)}, u32[]{:S(2)}) collective-permute-start(bf16[8,64,384]{2,1,0:T(8,128)(2,1)S(1)} %collective-permute-done.4.refs_1_), channel_id=1, source_target_pairs={{0,1},{1,0},{2,3},{3,2},{4,5},{5,4},{6,7},{7,6},{8,9},{9,8},{10,11... | collective-permute-start | bytes 1179656 | tf_op jit(solution)/shard_map/ppermute | solution.py:317
  16.7 1.4 %copy-start = (bf16[32,64,384]{2,1,0:T(8,128)(2,1)S(1)}, bf16[32,64,384]{2,1,0:T(8,128)(2,1)}, u32[]{:S(2)}) copy-start(bf16[32,64,384]{2,1,0:T(8,128)(2,1)} %v_ref.9) | copy-start | bytes 4718596
  18.2 1.0 %copy-start.2 = (bf16[8,64,384]{2,1,0:T(8,128)(2,1)S(1)}, bf16[8,64,384]{2,1,0:T(8,128)(2,1)}, u32[]{:S(2)}) copy-start(bf16[8,64,384]{2,1,0:T(8,128)(2,1)} %refs_3_.1) | copy-start | bytes 1179652
  19.1 0.7 %copy-start.4 = (s32[8]{0:T(128)S(1)}, s32[8]{0:T(128)}, u32[]{:S(2)}) copy-start(s32[8]{0:T(128)} %counts_ref.11) | copy-start | bytes 100
  19.8 7.6 %copy-start.1 = (bf16[32,64,384]{2,1,0:T(8,128)(2,1)S(1)}, bf16[32,64,384]{2,1,0:T(8,128)(2,1)}, u32[]{:S(2)}) copy-start(bf16[32,64,384]{2,1,0:T(8,128)(2,1)} %v_ref.9) | copy-start | bytes 4718596
  25.3 4.8 %collective-permute-start.5 = (bf16[8,64,384]{2,1,0:T(8,128)(2,1)S(1)}, bf16[8,64,384]{2,1,0:T(8,128)(2,1)S(1)}, u32[]{:S(2)}, u32[]{:S(2)}) collective-permute-start(bf16[8,64,384]{2,1,0:T(8,128)(2,1)S(1)} %collective-permute-done.2.refs_0_), channel_id=1, source_target_pairs={{0,1},{1,0},{2,3},{3,2},{4,5},{5,4},{6,7},{7,6},{8,9},{9,8},{10,11... | collective-permute-start | bytes 1179656 | tf_op jit(solution)/shard_map/ppermute | solution.py:317
  25.3 12.4 %collective-permute-start.6 = (bf16[8,64,384]{2,1,0:T(8,128)(2,1)S(1)}, bf16[8,64,384]{2,1,0:T(8,128)(2,1)S(1)}, u32[]{:S(2)}, u32[]{:S(2)}) collective-permute-start(bf16[8,64,384]{2,1,0:T(8,128)(2,1)S(1)} %collective-permute-done.2.refs_0_), channel_id=1, source_target_pairs={{0,4},{1,5},{2,6},{3,7},{4,12},{5,13},{6,14},{7,15},{8,0},{9,1},{1... | collective-permute-start | bytes 1179656 | tf_op jit(solution)/shard_map/ppermute | solution.py:314
  26.0 14.5 %collective-permute-start.10 = (bf16[8,64,384]{2,1,0:T(8,128)(2,1)S(1)}, bf16[8,64,384]{2,1,0:T(8,128)(2,1)S(1)}, u32[]{:S(2)}, u32[]{:S(2)}) collective-permute-start(bf16[8,64,384]{2,1,0:T(8,128)(2,1)S(1)} %collective-permute-done.2.refs_0_), channel_id=1, source_target_pairs={{0,2},{1,3},{2,0},{3,1},{4,6},{5,7},{6,4},{7,5},{8,10},{9,11},{10,... | collective-permute-start | bytes 1179656 | tf_op jit(solution)/shard_map/ppermute | solution.py:317
  27.4 13.2 %collective-permute-start.12 = (bf16[8,64,384]{2,1,0:T(8,128)(2,1)S(1)}, bf16[8,64,384]{2,1,0:T(8,128)(2,1)S(1)}, u32[]{:S(2)}, u32[]{:S(2)}) collective-permute-start(bf16[8,64,384]{2,1,0:T(8,128)(2,1)S(1)} %collective-permute-done.7.refs_1_), channel_id=1, source_target_pairs={{0,1},{1,0},{2,3},{3,2},{4,5},{5,4},{6,7},{7,6},{8,9},{9,8},{10,11... | collective-permute-start | bytes 1179656 | tf_op jit(solution)/shard_map/ppermute | solution.py:317
  37.7 2.9 %collective-permute-start.13 = (bf16[8,64,384]{2,1,0:T(8,128)(2,1)S(1)}, bf16[8,64,384]{2,1,0:T(8,128)(2,1)S(1)}, u32[]{:S(2)}, u32[]{:S(2)}) collective-permute-start(bf16[8,64,384]{2,1,0:T(8,128)(2,1)S(1)} %collective-permute-done.6.refs_0_), channel_id=1, source_target_pairs={{0,1},{1,0},{2,3},{3,2},{4,5},{5,4},{6,7},{7,6},{8,9},{9,8},{10,11... | collective-permute-start | bytes 1179656 | tf_op jit(solution)/shard_map/ppermute | solution.py:317
  37.7 7.4 %collective-permute-start.11 = (bf16[4,64,384]{2,1,0:T(8,128)(2,1)S(1)}, bf16[4,64,384]{2,1,0:T(8,128)(2,1)S(1)}, u32[]{:S(2)}, u32[]{:S(2)}) collective-permute-start(bf16[4,64,384]{2,1,0:T(8,128)(2,1)S(1)} %slice.13), channel_id=1, source_target_pairs={{0,2},{1,3},{2,0},{3,1},{4,6},{5,7},{6,4},{7,5},{8,10},{9,11},{10,... | collective-permute-start | bytes 589832 | tf_op jit(solution)/shard_map/ppermute | solution.py:317
  39.0 7.0 %collective-permute-start.9 = (bf16[4,64,384]{2,1,0:T(8,128)(2,1)S(1)}, bf16[4,64,384]{2,1,0:T(8,128)(2,1)S(1)}, u32[]{:S(2)}, u32[]{:S(2)}) collective-permute-start(bf16[4,64,384]{2,1,0:T(8,128)(2,1)S(1)} %slice.16), channel_id=1, source_target_pairs={{0,8},{1,9},{2,10},{3,11},{4,0},{5,1},{6,2},{7,3},{8,12},{9,13},{1... | collective-permute-start | bytes 589832 | tf_op jit(solution)/shard_map/ppermute | solution.py:314
  45.1 1.5 %collective-permute-start.14 = (bf16[4,64,384]{2,1,0:T(8,128)(2,1)S(1)}, bf16[4,64,384]{2,1,0:T(8,128)(2,1)S(1)}, u32[]{:S(2)}, u32[]{:S(2)}) collective-permute-start(bf16[4,64,384]{2,1,0:T(8,128)(2,1)S(1)} %get-tuple-element.103), channel_id=1, source_target_pairs={{0,1},{1,0},{2,3},{3,2},{4,5},{5,4},{6,7},{7,6},{8,9},{9,8},{10,11... | collective-permute-start | bytes 589832 | tf_op jit(solution)/shard_map/ppermute | solution.py:317
  45.2 1.7 %collective-permute-start.15 = (bf16[4,64,384]{2,1,0:T(8,128)(2,1)S(1)}, bf16[4,64,384]{2,1,0:T(8,128)(2,1)S(1)}, u32[]{:S(2)}, u32[]{:S(2)}) collective-permute-start(bf16[4,64,384]{2,1,0:T(8,128)(2,1)S(1)} %get-tuple-element.102), channel_id=1, source_target_pairs={{0,1},{1,0},{2,3},{3,2},{4,5},{5,4},{6,7},{7,6},{8,9},{9,8},{10,11... | collective-permute-start | bytes 589832 | tf_op jit(solution)/shard_map/ppermute | solution.py:317
  46.1 4.2 %collective-permute-start.17 = (bf16[4,64,384]{2,1,0:T(8,128)(2,1)S(1)}, bf16[4,64,384]{2,1,0:T(8,128)(2,1)S(1)}, u32[]{:S(2)}, u32[]{:S(2)}) collective-permute-start(bf16[4,64,384]{2,1,0:T(8,128)(2,1)S(1)} %collective-permute-done.9.refs_2_), channel_id=1, source_target_pairs={{0,1},{1,0},{2,3},{3,2},{4,5},{5,4},{6,7},{7,6},{8,9},{9,8},{10,11... | collective-permute-start | bytes 589832 | tf_op jit(solution)/shard_map/ppermute | solution.py:317
  46.1 4.2 %collective-permute-start.16 = (bf16[4,64,384]{2,1,0:T(8,128)(2,1)S(1)}, bf16[4,64,384]{2,1,0:T(8,128)(2,1)S(1)}, u32[]{:S(2)}, u32[]{:S(2)}) collective-permute-start(bf16[4,64,384]{2,1,0:T(8,128)(2,1)S(1)} %collective-permute-done.11.refs_3_), channel_id=1, source_target_pairs={{0,1},{1,0},{2,3},{3,2},{4,5},{5,4},{6,7},{7,6},{8,9},{9,8},{10,11... | collective-permute-start | bytes 589832 | tf_op jit(solution)/shard_map/ppermute | solution.py:317
  52.1 4.0 %collective-permute-start.18 = (f32[2,8,128]{2,1,0:T(8,128)S(1)}, f32[2,8,128]{2,1,0:T(8,128)S(1)}, u32[]{:S(2)}, u32[]{:S(2)}) collective-permute-start(f32[2,8,128]{2,1,0:T(8,128)S(1)} %get-tuple-element.97), channel_id=1, source_target_pairs={{0,3},{1,2},{2,1},{3,0},{4,7},{5,6},{6,5},{7,4},{8,11},{9,10},{10,... | collective-permute-start | bytes 24584 | tf_op jit(solution)/shard_map/ppermute | solution.py:317
  52.8 3.7 %collective-permute-start.19 = (f32[2,8,128]{2,1,0:T(8,128)S(1)}, f32[2,8,128]{2,1,0:T(8,128)S(1)}, u32[]{:S(2)}, u32[]{:S(2)}) collective-permute-start(f32[2,8,128]{2,1,0:T(8,128)S(1)} %get-tuple-element.97), channel_id=1, source_target_pairs={{0,2},{1,3},{2,0},{3,1},{4,6},{5,7},{6,4},{7,5},{8,10},{9,11},{10,... | collective-permute-start | bytes 24584 | tf_op jit(solution)/shard_map/ppermute | solution.py:317
  53.5 2.9 %collective-permute-start.20 = (f32[2,8,128]{2,1,0:T(8,128)S(1)}, f32[2,8,128]{2,1,0:T(8,128)S(1)}, u32[]{:S(2)}, u32[]{:S(2)}) collective-permute-start(f32[2,8,128]{2,1,0:T(8,128)S(1)} %get-tuple-element.97), channel_id=1, source_target_pairs={{0,1},{1,0},{2,3},{3,2},{4,5},{5,4},{6,7},{7,6},{8,9},{9,8},{10,11... | collective-permute-start | bytes 24584 | tf_op jit(solution)/shard_map/ppermute | solution.py:317
  56.4 6.5 %collective-permute-start.21 = (f32[2,8,128]{2,1,0:T(8,128)S(1)}, f32[2,8,128]{2,1,0:T(8,128)S(1)}, u32[]{:S(2)}, u32[]{:S(2)}) collective-permute-start(f32[2,8,128]{2,1,0:T(8,128)S(1)} %add_add_fusion), channel_id=1, source_target_pairs={{0,12},{1,13},{2,14},{3,15},{4,8},{5,9},{6,10},{7,11},{8,4},{9,5},... | collective-permute-start | bytes 24584 | tf_op jit(solution)/shard_map/ppermute | solution.py:317
  59.6 4.5 %collective-permute-start.22 = (f32[2,8,128]{2,1,0:T(8,128)S(1)}, f32[2,8,128]{2,1,0:T(8,128)S(1)}, u32[]{:S(2)}, u32[]{:S(2)}) collective-permute-start(f32[2,8,128]{2,1,0:T(8,128)S(1)} %add_add_fusion), channel_id=1, source_target_pairs={{0,8},{1,9},{2,10},{3,11},{4,12},{5,13},{6,14},{7,15},{8,0},{9,1},... | collective-permute-start | bytes 24584 | tf_op jit(solution)/shard_map/ppermute | solution.py:317
  59.7 4.4 %collective-permute-start.23 = (f32[2,8,128]{2,1,0:T(8,128)S(1)}, f32[2,8,128]{2,1,0:T(8,128)S(1)}, u32[]{:S(2)}, u32[]{:S(2)}) collective-permute-start(f32[2,8,128]{2,1,0:T(8,128)S(1)} %add_add_fusion), channel_id=1, source_target_pairs={{0,4},{1,5},{2,6},{3,7},{4,0},{5,1},{6,2},{7,3},{8,12},{9,13},{10,... | collective-permute-start | bytes 24584 | tf_op jit(solution)/shard_map/ppermute | solution.py:317

commit v20 on v19

--- a/solution.py
+++ b/solution.py
@@ -331,8 +331,8 @@
             a.append(shift_z(a[k], 1))
         else:
             part = shard_tiles // 2
-            c[-1], a[k], back, state = lax.optimization_barrier(
-                (c[-1], a[k], b[0][part:], state)
+            a[k], c[-1], back, state = lax.optimization_barrier(
+                (a[k], c[-1], b[0][part:], state)
             )
             last = {part: shift_z(back, -1), 0: swap(a[k][:part], 2)}
         c.append(swap(a[k], 1))
@@ -361,10 +361,10 @@
 
     residual, _, stats = state
     out = deliver(residual, 0)
-    stats = sum([swap(stats, bits) for bits in (3, 2, 1)], stats)
+    stats = sum([swap(stats, 4 * bits) for bits in range(depth - 1, 0, -1)], stats)
     stats, residual, out = lax.optimization_barrier((stats, residual, out))
     out = deliver(residual, 1, out)
-    stats = sum([swap(stats, 4 * bits) for bits in range(depth - 1, 0, -1)], stats)
+    stats = sum([swap(stats, bits) for bits in (3, 2, 1)], stats)
     irrep_sums, ab_counts = jnp.sum(stats, axis=2)
     entries = ab_counts * ij_counts.astype(jnp.float32) * float(rows * rows)
     return out, jnp.sqrt(irrep_sums / entries + 1e-06)

time: 65 us -> 62.6 us (0.963)
  waiting for transfers between devices: 16.5 us -> 14.6 us
    ppermute x4, waiting for transfers between devices: 14.4 us -> 11.8 us  [shift_z(): return lax.ppermute(x, 'vir', pairs)]
    ppermute x20, waiting for transfers between devices: 2.12 us -> 2.84 us  [swap(): return lax.ppermute(x, 'vir', [(d, d ^ bits) for d in range(devices)])]
  transfers between devices with their start and end apart: 24 -> 24, of which waited for: 9 -> 8; matrix products, arithmetic and copies ran while one was open for 0% -> 0% of each run, Pallas kernels for 32% -> 33%
where the time goes in v20:
time: 62.6 us; the launch traced here: 62.2 us
  Pallas kernels  22.1 us (35%)
  starting transfers between devices  19.7 us (31%)
  waiting for transfers between devices  14.6 us (23%)
  local copies, waits for them, and re-layouts  4.45 us (7%)
  between operations  0.79 us (1%)
  other arithmetic  0.63 us (1%)
    pallas_call x5, Pallas kernels, ladder(): pl.pallas_call(functools.partial(ladder_kernel, call, depth, shard_tiles,...  14.1 us
    ppermute x20, starting transfers between devices, swap(): return lax.ppermute(x, 'vir', [(d, d ^ bits) for d in range(devices)])  13.6 us
    ppermute x4, waiting for transfers between devices, shift_z(): return lax.ppermute(x, 'vir', pairs)  11.8 us
    ppermute x4, starting transfers between devices, shift_z(): return lax.ppermute(x, 'vir', pairs)  6.05 us
    unnamed x12, local copies, waits for them, and re-layouts  4.37 us
    pallas_call x2, Pallas kernels, deliver(): pl.pallas_call(functools.partial(deliver_kernel, part), out_shape=jax.Sha...  4.04 us
    pallas_call x1, Pallas kernels, prepare(): pl.pallas_call(functools.partial(prepare_kernel, depth, shard_tiles), out...  3.96 us
    ppermute x20, waiting for transfers between devices, swap(): return lax.ppermute(x, 'vir', [(d, d ^ bits) for d in range(devices)])  2.84 us
  transfers between devices with their start and end apart: 24, of which 8 were waited for; matrix products, arithmetic and copies ran while one was open for 0% of the time, Pallas kernels for 33%

profile of v20, /device:TPU:0, one launch (start us, length us, event | category | flops | bytes accessed | tf_op | source)
XLA Modules:
  0.0 62.2 jit_solution(4124311111392146898)
XLA Ops:
  0.6 3.1 %collective-permute-start = (bf16[8,64,384]{2,1,0:T(8,128)(2,1)}, bf16[8,64,384]{2,1,0:T(8,128)(2,1)S(1)}, u32[]{:S(2)}, u32[]{:S(2)}) collective-permute-start(bf16[8,64,384]{2,1,0:T(8,128)(2,1)} %refs_3_.1), channel_id=1, source_target_pairs={{0,4},{1,5},{2,6},{3,7},{4,12},{5,13},{6,14},{7,15},{8,0},{9,1},{1... | collective-permute-start | bytes 1179656 | tf_op jit(solution)/shard_map/ppermute | solution.py:314
  3.7 0.0 collective-permute-start.1
  3.7 1.5 %collective-permute-start.4 = (bf16[8,64,384]{2,1,0:T(8,128)(2,1)}, bf16[8,64,384]{2,1,0:T(8,128)(2,1)S(1)}, u32[]{:S(2)}, u32[]{:S(2)}) collective-permute-start(bf16[8,64,384]{2,1,0:T(8,128)(2,1)} %refs_3_.1), channel_id=1, source_target_pairs={{0,2},{1,3},{2,0},{3,1},{4,6},{5,7},{6,4},{7,5},{8,10},{9,11},{10,... | collective-permute-start | bytes 1179656 | tf_op jit(solution)/shard_map/ppermute | solution.py:317
  5.2 0.7 %copy-done.3 = s32[8]{0:T(128)S(1)} copy-done((s32[8]{0:T(128)S(1)}, s32[8]{0:T(128)}, u32[]{:S(2)}) %copy-start.3) | copy-done | bytes 56
  5.9 0.7 %copy-done.5 = s32[32]{0:T(128)S(1)} copy-done((s32[32]{0:T(128)S(1)}, s32[32]{0:T(128)}, u32[]{:S(2)}) %copy-start.5) | copy-done | bytes 152
  6.5 4.0 %prepare.1 = (bf16[32,64,2048]{2,1,0:T(8,128)(2,1)S(1)}, bf16[132,64,384]{2,1,0:T(8,128)(2,1)S(1)}, f32[2,8,128]{2,1,0:T(8,128)S(1)}, s32[32]{0:T(128)S(1)}, s32...) custom-call(s32[1]{0:T(128)} %bitcast.me_ref, s32[8]{0:T(128)S(1)} %copy-done.3, s32[32]{0:T(128)S(1)} %copy-done.5), custom_call_target="tpu_custom_call" | custom-call | bytes 8388608 | tf_op jit(solution)/shard_map/prepare/pallas_call | solution.py:135
  10.5 3.5 %collective-permute-done.refs_0_ = bf16[8,64,384]{2,1,0:T(8,128)(2,1)S(1)} collective-permute-done((bf16[8,64,384]{2,1,0:T(8,128)(2,1)}, bf16[8,64,384]{2,1,0:T(8,128)(2,1)S(1)}, u32[]{:S(2)}, u32[]{:S(2)}) %collective-permute-start) | collective-permute-done | bytes 393248 | tf_op jit(solution)/shard_map/ppermute | solution.py:314
  14.0 0.0 collective-permute-done.1.refs_2_
  14.0 0.9 %collective-permute-start.2 = (bf16[8,64,384]{2,1,0:T(8,128)(2,1)S(1)}, bf16[8,64,384]{2,1,0:T(8,128)(2,1)S(1)}, u32[]{:S(2)}, u32[]{:S(2)}) collective-permute-start(bf16[8,64,384]{2,1,0:T(8,128)(2,1)S(1)} %collective-permute-done.refs_0_), channel_id=1, source_target_pairs={{0,4},{1,5},{2,6},{3,7},{4,12},{5,13},{6,14},{7,15},{8,0},{9,1},{1... | collective-permute-start | bytes 1179656 | tf_op jit(solution)/shard_map/ppermute | solution.py:314
  15.0 0.0 collective-permute-start.3
  15.0 1.5 %collective-permute-start.7 = (bf16[8,64,384]{2,1,0:T(8,128)(2,1)S(1)}, bf16[8,64,384]{2,1,0:T(8,128)(2,1)S(1)}, u32[]{:S(2)}, u32[]{:S(2)}) collective-permute-start(bf16[8,64,384]{2,1,0:T(8,128)(2,1)S(1)} %collective-permute-done.refs_0_), channel_id=1, source_target_pairs={{0,2},{1,3},{2,0},{3,1},{4,6},{5,7},{6,4},{7,5},{8,10},{9,11},{10,... | collective-permute-start | bytes 1179656 | tf_op jit(solution)/shard_map/ppermute | solution.py:317
  16.5 0.2 collective-permute-start.8
  16.7 1.4 %copy-done = bf16[32,64,384]{2,1,0:T(8,128)(2,1)S(1)} copy-done((bf16[32,64,384]{2,1,0:T(8,128)(2,1)S(1)}, bf16[32,64,384]{2,1,0:T(8,128)(2,1)}, u32[]{:S(2)}) %copy-start) | copy-done | bytes 1572888
  18.2 1.0 %copy-done.2 = bf16[8,64,384]{2,1,0:T(8,128)(2,1)S(1)} copy-done((bf16[8,64,384]{2,1,0:T(8,128)(2,1)S(1)}, bf16[8,64,384]{2,1,0:T(8,128)(2,1)}, u32[]{:S(2)}) %copy-start.2) | copy-done | bytes 393240
  19.1 0.7 %copy-done.4 = s32[8]{0:T(128)S(1)} copy-done((s32[8]{0:T(128)S(1)}, s32[8]{0:T(128)}, u32[]{:S(2)}) %copy-start.4) | copy-done | bytes 56
  19.8 2.6 %ladder_0.1 = (bf16[32,64,2048]{2,1,0:T(8,128)(2,1)S(1)}, bf16[132,64,384]{2,1,0:T(8,128)(2,1)S(1)}, f32[2,8,128]{2,1,0:T(8,128)S(1)}) custom-call(s32[1]{0:T(128)} %bitcast.me_ref, s32[8]{0:T(128)S(1)} %copy-done.4, s32[32]{0:T(128)S(1)} %get-tuple-element.52.order_ref, ...), custom_call_target="tpu_custom_call", output_to_operand_aliasing={{0}: (9, {}), {1}: (10, {})} | custom-call | flops 402653184 | bytes 2097152 | tf_op jit(solution)/shard_map/ladder_0/pallas_call | solution.py:252
  22.4 2.9 %collective-permute-done.2.refs_0_ = bf16[8,64,384]{2,1,0:T(8,128)(2,1)S(1)} collective-permute-done((bf16[8,64,384]{2,1,0:T(8,128)(2,1)S(1)}, bf16[8,64,384]{2,1,0:T(8,128)(2,1)S(1)}, u32[]{:S(2)}, u32[]{:S(2)}) %collective-permute-start.2) | collective-permute-done | bytes 393248 | tf_op jit(solution)/shard_map/ppermute | solution.py:314
  25.3 0.5 collective-permute-start.5
  25.8 1.6 %collective-permute-start.10 = (bf16[8,64,384]{2,1,0:T(8,128)(2,1)S(1)}, bf16[8,64,384]{2,1,0:T(8,128)(2,1)S(1)}, u32[]{:S(2)}, u32[]{:S(2)}) collective-permute-start(bf16[8,64,384]{2,1,0:T(8,128)(2,1)S(1)} %collective-permute-done.2.refs_0_), channel_id=1, source_target_pairs={{0,2},{1,3},{2,0},{3,1},{4,6},{5,7},{6,4},{7,5},{8,10},{9,11},{10,... | collective-permute-start | bytes 1179656 | tf_op jit(solution)/shard_map/ppermute | solution.py:317
  27.4 0.0 collective-permute-done.7.refs_1_
  27.4 0.2 collective-permute-start.12
  27.6 0.0 collective-permute-done.8.refs_3_
  27.6 2.6 %ladder_1.1 = (bf16[32,64,2048]{2,1,0:T(8,128)(2,1)S(1)}, bf16[132,64,384]{2,1,0:T(8,128)(2,1)S(1)}, f32[2,8,128]{2,1,0:T(8,128)S(1)}) custom-call(s32[1]{0:T(128)} %bitcast.me_ref, s32[8]{0:T(128)S(1)} %copy-done.4, s32[32]{0:T(128)S(1)} %get-tuple-element.52.order_ref, ...), custom_call_target="tpu_custom_call", output_to_operand_aliasing={{0}: (9, {}), {1}: (10, {})} | custom-call | flops 402653184 | bytes 2097152 | tf_op jit(solution)/shard_map/ladder_1/pallas_call | solution.py:252
  30.2 5.3 %collective-permute-done.5.refs_0_ = bf16[8,64,384]{2,1,0:T(8,128)(2,1)S(1)} collective-permute-done((bf16[8,64,384]{2,1,0:T(8,128)(2,1)S(1)}, bf16[8,64,384]{2,1,0:T(8,128)(2,1)S(1)}, u32[]{:S(2)}, u32[]{:S(2)}) %collective-permute-start.5) | collective-permute-done | bytes 393248 | tf_op jit(solution)/shard_map/ppermute | solution.py:314
  35.5 0.0 collective-permute-done.6.refs_2_
  35.6 1.0 %collective-permute-start.11 = (bf16[4,64,384]{2,1,0:T(8,128)(2,1)S(1)}, bf16[4,64,384]{2,1,0:T(8,128)(2,1)S(1)}, u32[]{:S(2)}, u32[]{:S(2)}) collective-permute-start(bf16[4,64,384]{2,1,0:T(8,128)(2,1)S(1)} %slice.13), channel_id=1, source_target_pairs={{0,2},{1,3},{2,0},{3,1},{4,6},{5,7},{6,4},{7,5},{8,10},{9,11},{10,... | collective-permute-start | bytes 589832 | tf_op jit(solution)/shard_map/ppermute | solution.py:317
  36.6 1.5 %collective-permute-start.9 = (bf16[4,64,384]{2,1,0:T(8,128)(2,1)S(1)}, bf16[4,64,384]{2,1,0:T(8,128)(2,1)S(1)}, u32[]{:S(2)}, u32[]{:S(2)}) collective-permute-start(bf16[4,64,384]{2,1,0:T(8,128)(2,1)S(1)} %slice.16), channel_id=1, source_target_pairs={{0,8},{1,9},{2,10},{3,11},{4,0},{5,1},{6,2},{7,3},{8,12},{9,13},{1... | collective-permute-start | bytes 589832 | tf_op jit(solution)/shard_map/ppermute | solution.py:314
  38.1 4.3 %ladder_2.1 = (bf16[32,64,2048]{2,1,0:T(8,128)(2,1)S(1)}, bf16[132,64,384]{2,1,0:T(8,128)(2,1)S(1)}, f32[2,8,128]{2,1,0:T(8,128)S(1)}) custom-call(s32[1]{0:T(128)} %bitcast.me_ref, s32[8]{0:T(128)S(1)} %copy-done.4, s32[32]{0:T(128)S(1)} %get-tuple-element.52.order_ref, ...), custom_call_target="tpu_custom_call", output_to_operand_aliasing={{0}: (9, {}), {1}: (10, {})} | custom-call | flops 503316480 | bytes 2621440 | tf_op jit(solution)/shard_map/ladder_2/pallas_call | solution.py:252
  42.4 0.5 collective-permute-done.11.refs_3_
  43.0 0.1 collective-permute-start.14
  43.1 0.5 collective-permute-start.15
  43.6 0.0 collective-permute-done.9.refs_2_
  43.6 0.1 collective-permute-start.17
  43.6 0.5 collective-permute-start.16
  44.1 0.4 collective-permute-done.14.refs_0_
  44.5 0.3 collective-permute-done.15.refs_1_
  44.8 2.8 %ladder_3.1 = (bf16[32,64,2048]{2,1,0:T(8,128)(2,1)S(1)}, bf16[132,64,384]{2,1,0:T(8,128)(2,1)S(1)}, f32[2,8,128]{2,1,0:T(8,128)S(1)}) custom-call(s32[1]{0:T(128)} %bitcast.me_ref, s32[8]{0:T(128)S(1)} %copy-done.4, s32[32]{0:T(128)S(1)} %get-tuple-element.52.order_ref, ...), custom_call_target="tpu_custom_call", output_to_operand_aliasing={{0}: (9, {}), {1}: (10, {})} | custom-call | flops 201326592 | bytes 1048576 | tf_op jit(solution)/shard_map/ladder_3/pallas_call | solution.py:252
  47.6 1.8 %ladder_4.1 = (bf16[32,64,2048]{2,1,0:T(8,128)(2,1)S(1)}, bf16[132,64,384]{2,1,0:T(8,128)(2,1)S(1)}, f32[2,8,128]{2,1,0:T(8,128)S(1)}) custom-call(s32[1]{0:T(128)} %bitcast.me_ref, s32[8]{0:T(128)S(1)} %copy-done.4, s32[32]{0:T(128)S(1)} %get-tuple-element.52.order_ref, ...), custom_call_target="tpu_custom_call", output_to_operand_aliasing={{0}: (9, {}), {1}: (10, {})} | custom-call | flops 100663296 | bytes 524288 | tf_op jit(solution)/shard_map/ladder_4/pallas_call | solution.py:252
  49.4 3.1 %collective-permute-start.18 = (f32[2,8,128]{2,1,0:T(8,128)S(1)}, f32[2,8,128]{2,1,0:T(8,128)S(1)}, u32[]{:S(2)}, u32[]{:S(2)}) collective-permute-start(f32[2,8,128]{2,1,0:T(8,128)S(1)} %get-tuple-element.97), channel_id=1, source_target_pairs={{0,12},{1,13},{2,14},{3,15},{4,8},{5,9},{6,10},{7,11},{8,4},{9,5},... | collective-permute-start | bytes 24584 | tf_op jit(solution)/shard_map/ppermute | solution.py:317
  52.5 1.5 %collective-permute-start.19 = (f32[2,8,128]{2,1,0:T(8,128)S(1)}, f32[2,8,128]{2,1,0:T(8,128)S(1)}, u32[]{:S(2)}, u32[]{:S(2)}) collective-permute-start(f32[2,8,128]{2,1,0:T(8,128)S(1)} %get-tuple-element.97), channel_id=1, source_target_pairs={{0,8},{1,9},{2,10},{3,11},{4,12},{5,13},{6,14},{7,15},{8,0},{9,1},... | collective-permute-start | bytes 24584 | tf_op jit(solution)/shard_map/ppermute | solution.py:317
  54.0 2.0 %deliver_0.1.refs_0_ = bf16[32,64,2048]{2,1,0:T(8,128)(2,1)} custom-call(bf16[32,64,2048]{2,1,0:T(8,128)(2,1)S(1)} %get-tuple-element.99.held_ref), custom_call_target="tpu_custom_call" | custom-call | tf_op jit(solution)/shard_map/deliver_0/pallas_call | solution.py:290
  56.1 1.0 %collective-permute-done.19 = f32[2,8,128]{2,1,0:T(8,128)S(1)} collective-permute-done((f32[2,8,128]{2,1,0:T(8,128)S(1)}, f32[2,8,128]{2,1,0:T(8,128)S(1)}, u32[]{:S(2)}, u32[]{:S(2)}) %collective-permute-start.19) | collective-permute-done | bytes 8224 | tf_op jit(solution)/shard_map/ppermute | solution.py:317
  57.1 0.6 collective-permute-done.20
  57.7 1.6 %collective-permute-start.22 = (f32[2,8,128]{2,1,0:T(8,128)S(1)}, f32[2,8,128]{2,1,0:T(8,128)S(1)}, u32[]{:S(2)}, u32[]{:S(2)}) collective-permute-start(f32[2,8,128]{2,1,0:T(8,128)S(1)} %add_add_fusion), channel_id=1, source_target_pairs={{0,2},{1,3},{2,0},{3,1},{4,6},{5,7},{6,4},{7,5},{8,10},{9,11},{10,... | collective-permute-start | bytes 24584 | tf_op jit(solution)/shard_map/ppermute | solution.py:317
  59.3 0.3 collective-permute-start.23
  59.6 2.0 %deliver_1.1 = bf16[32,64,2048]{2,1,0:T(8,128)(2,1)} custom-call(bf16[32,64,2048]{2,1,0:T(8,128)(2,1)S(1)} %get-tuple-element.99.held_ref, bf16[32,64,2048]{2,1,0:T(8,128)(2,1)} %deliver_0.1.refs_0_), custom_call_target="tpu_custom_call", output_to_operand_aliasing={{}: (1, {})} | custom-call | tf_op jit(solution)/shard_map/deliver_1/pallas_call | solution.py:290
  61.6 0.1 add_reduce_fusion
  61.7 0.5 add_sqrt_fusion
  (26 shorter events, 0.1 us)
Async XLA Ops:
  0.6 13.4 %collective-permute-start = (bf16[8,64,384]{2,1,0:T(8,128)(2,1)}, bf16[8,64,384]{2,1,0:T(8,128)(2,1)S(1)}, u32[]{:S(2)}, u32[]{:S(2)}) collective-permute-start(bf16[8,64,384]{2,1,0:T(8,128)(2,1)} %refs_3_.1), channel_id=1, source_target_pairs={{0,4},{1,5},{2,6},{3,7},{4,12},{5,13},{6,14},{7,15},{8,0},{9,1},{1... | collective-permute-start | bytes 1179656 | tf_op jit(solution)/shard_map/ppermute | solution.py:314
  3.7 10.3 %collective-permute-start.1 = (bf16[8,64,384]{2,1,0:T(8,128)(2,1)}, bf16[8,64,384]{2,1,0:T(8,128)(2,1)S(1)}, u32[]{:S(2)}, u32[]{:S(2)}) collective-permute-start(bf16[8,64,384]{2,1,0:T(8,128)(2,1)} %refs_3_.1), channel_id=1, source_target_pairs={{0,1},{1,0},{2,3},{3,2},{4,5},{5,4},{6,7},{7,6},{8,9},{9,8},{10,11... | collective-permute-start | bytes 1179656 | tf_op jit(solution)/shard_map/ppermute | solution.py:317
  3.7 12.8 %collective-permute-start.4 = (bf16[8,64,384]{2,1,0:T(8,128)(2,1)}, bf16[8,64,384]{2,1,0:T(8,128)(2,1)S(1)}, u32[]{:S(2)}, u32[]{:S(2)}) collective-permute-start(bf16[8,64,384]{2,1,0:T(8,128)(2,1)} %refs_3_.1), channel_id=1, source_target_pairs={{0,2},{1,3},{2,0},{3,1},{4,6},{5,7},{6,4},{7,5},{8,10},{9,11},{10,... | collective-permute-start | bytes 1179656 | tf_op jit(solution)/shard_map/ppermute | solution.py:317
  5.2 0.7 %copy-start.3 = (s32[8]{0:T(128)S(1)}, s32[8]{0:T(128)}, u32[]{:S(2)}) copy-start(s32[8]{0:T(128)} %counts_ref.11) | copy-start | bytes 100
  5.9 0.7 %copy-start.5 = (s32[32]{0:T(128)S(1)}, s32[32]{0:T(128)}, u32[]{:S(2)}) copy-start(s32[32]{0:T(128)} %irrep_ref.1) | copy-start | bytes 388
  14.0 11.2 %collective-permute-start.2 = (bf16[8,64,384]{2,1,0:T(8,128)(2,1)S(1)}, bf16[8,64,384]{2,1,0:T(8,128)(2,1)S(1)}, u32[]{:S(2)}, u32[]{:S(2)}) collective-permute-start(bf16[8,64,384]{2,1,0:T(8,128)(2,1)S(1)} %collective-permute-done.refs_0_), channel_id=1, source_target_pairs={{0,4},{1,5},{2,6},{3,7},{4,12},{5,13},{6,14},{7,15},{8,0},{9,1},{1... | collective-permute-start | bytes 1179656 | tf_op jit(solution)/shard_map/ppermute | solution.py:314
  15.0 10.3 %collective-permute-start.3 = (bf16[8,64,384]{2,1,0:T(8,128)(2,1)S(1)}, bf16[8,64,384]{2,1,0:T(8,128)(2,1)S(1)}, u32[]{:S(2)}, u32[]{:S(2)}) collective-permute-start(bf16[8,64,384]{2,1,0:T(8,128)(2,1)S(1)} %collective-permute-done.refs_0_), channel_id=1, source_target_pairs={{0,1},{1,0},{2,3},{3,2},{4,5},{5,4},{6,7},{7,6},{8,9},{9,8},{10,11... | collective-permute-start | bytes 1179656 | tf_op jit(solution)/shard_map/ppermute | solution.py:317
  15.0 12.4 %collective-permute-start.7 = (bf16[8,64,384]{2,1,0:T(8,128)(2,1)S(1)}, bf16[8,64,384]{2,1,0:T(8,128)(2,1)S(1)}, u32[]{:S(2)}, u32[]{:S(2)}) collective-permute-start(bf16[8,64,384]{2,1,0:T(8,128)(2,1)S(1)} %collective-permute-done.refs_0_), channel_id=1, source_target_pairs={{0,2},{1,3},{2,0},{3,1},{4,6},{5,7},{6,4},{7,5},{8,10},{9,11},{10,... | collective-permute-start | bytes 1179656 | tf_op jit(solution)/shard_map/ppermute | solution.py:317
  16.5 11.1 %collective-permute-start.8 = (bf16[8,64,384]{2,1,0:T(8,128)(2,1)S(1)}, bf16[8,64,384]{2,1,0:T(8,128)(2,1)S(1)}, u32[]{:S(2)}, u32[]{:S(2)}) collective-permute-start(bf16[8,64,384]{2,1,0:T(8,128)(2,1)S(1)} %collective-permute-done.4.refs_1_), channel_id=1, source_target_pairs={{0,1},{1,0},{2,3},{3,2},{4,5},{5,4},{6,7},{7,6},{8,9},{9,8},{10,11... | collective-permute-start | bytes 1179656 | tf_op jit(solution)/shard_map/ppermute | solution.py:317
  16.7 1.4 %copy-start = (bf16[32,64,384]{2,1,0:T(8,128)(2,1)S(1)}, bf16[32,64,384]{2,1,0:T(8,128)(2,1)}, u32[]{:S(2)}) copy-start(bf16[32,64,384]{2,1,0:T(8,128)(2,1)} %v_ref.9) | copy-start | bytes 4718596
  18.2 1.0 %copy-start.2 = (bf16[8,64,384]{2,1,0:T(8,128)(2,1)S(1)}, bf16[8,64,384]{2,1,0:T(8,128)(2,1)}, u32[]{:S(2)}) copy-start(bf16[8,64,384]{2,1,0:T(8,128)(2,1)} %refs_3_.1) | copy-start | bytes 1179652
  19.1 0.7 %copy-start.4 = (s32[8]{0:T(128)S(1)}, s32[8]{0:T(128)}, u32[]{:S(2)}) copy-start(s32[8]{0:T(128)} %counts_ref.11) | copy-start | bytes 100
  19.8 7.8 %copy-start.1 = (bf16[32,64,384]{2,1,0:T(8,128)(2,1)S(1)}, bf16[32,64,384]{2,1,0:T(8,128)(2,1)}, u32[]{:S(2)}) copy-start(bf16[32,64,384]{2,1,0:T(8,128)(2,1)} %v_ref.9) | copy-start | bytes 4718596
  25.3 10.3 %collective-permute-start.5 = (bf16[8,64,384]{2,1,0:T(8,128)(2,1)S(1)}, bf16[8,64,384]{2,1,0:T(8,128)(2,1)S(1)}, u32[]{:S(2)}, u32[]{:S(2)}) collective-permute-start(bf16[8,64,384]{2,1,0:T(8,128)(2,1)S(1)} %collective-permute-done.2.refs_0_), channel_id=1, source_target_pairs={{0,4},{1,5},{2,6},{3,7},{4,12},{5,13},{6,14},{7,15},{8,0},{9,1},{1... | collective-permute-start | bytes 1179656 | tf_op jit(solution)/shard_map/ppermute | solution.py:314
  25.8 9.8 %collective-permute-start.6 = (bf16[8,64,384]{2,1,0:T(8,128)(2,1)S(1)}, bf16[8,64,384]{2,1,0:T(8,128)(2,1)S(1)}, u32[]{:S(2)}, u32[]{:S(2)}) collective-permute-start(bf16[8,64,384]{2,1,0:T(8,128)(2,1)S(1)} %collective-permute-done.2.refs_0_), channel_id=1, source_target_pairs={{0,1},{1,0},{2,3},{3,2},{4,5},{5,4},{6,7},{7,6},{8,9},{9,8},{10,11... | collective-permute-start | bytes 1179656 | tf_op jit(solution)/shard_map/ppermute | solution.py:317
  25.8 12.3 %collective-permute-start.10 = (bf16[8,64,384]{2,1,0:T(8,128)(2,1)S(1)}, bf16[8,64,384]{2,1,0:T(8,128)(2,1)S(1)}, u32[]{:S(2)}, u32[]{:S(2)}) collective-permute-start(bf16[8,64,384]{2,1,0:T(8,128)(2,1)S(1)} %collective-permute-done.2.refs_0_), channel_id=1, source_target_pairs={{0,2},{1,3},{2,0},{3,1},{4,6},{5,7},{6,4},{7,5},{8,10},{9,11},{10,... | collective-permute-start | bytes 1179656 | tf_op jit(solution)/shard_map/ppermute | solution.py:317
  27.4 10.7 %collective-permute-start.12 = (bf16[8,64,384]{2,1,0:T(8,128)(2,1)S(1)}, bf16[8,64,384]{2,1,0:T(8,128)(2,1)S(1)}, u32[]{:S(2)}, u32[]{:S(2)}) collective-permute-start(bf16[8,64,384]{2,1,0:T(8,128)(2,1)S(1)} %collective-permute-done.7.refs_1_), channel_id=1, source_target_pairs={{0,1},{1,0},{2,3},{3,2},{4,5},{5,4},{6,7},{7,6},{8,9},{9,8},{10,11... | collective-permute-start | bytes 1179656 | tf_op jit(solution)/shard_map/ppermute | solution.py:317
  35.5 2.6 %collective-permute-start.13 = (bf16[8,64,384]{2,1,0:T(8,128)(2,1)S(1)}, bf16[8,64,384]{2,1,0:T(8,128)(2,1)S(1)}, u32[]{:S(2)}, u32[]{:S(2)}) collective-permute-start(bf16[8,64,384]{2,1,0:T(8,128)(2,1)S(1)} %collective-permute-done.5.refs_0_), channel_id=1, source_target_pairs={{0,1},{1,0},{2,3},{3,2},{4,5},{5,4},{6,7},{7,6},{8,9},{9,8},{10,11... | collective-permute-start | bytes 1179656 | tf_op jit(solution)/shard_map/ppermute | solution.py:317
  35.6 7.4 %collective-permute-start.11 = (bf16[4,64,384]{2,1,0:T(8,128)(2,1)S(1)}, bf16[4,64,384]{2,1,0:T(8,128)(2,1)S(1)}, u32[]{:S(2)}, u32[]{:S(2)}) collective-permute-start(bf16[4,64,384]{2,1,0:T(8,128)(2,1)S(1)} %slice.13), channel_id=1, source_target_pairs={{0,2},{1,3},{2,0},{3,1},{4,6},{5,7},{6,4},{7,5},{8,10},{9,11},{10,... | collective-permute-start | bytes 589832 | tf_op jit(solution)/shard_map/ppermute | solution.py:317
  36.6 7.0 %collective-permute-start.9 = (bf16[4,64,384]{2,1,0:T(8,128)(2,1)S(1)}, bf16[4,64,384]{2,1,0:T(8,128)(2,1)S(1)}, u32[]{:S(2)}, u32[]{:S(2)}) collective-permute-start(bf16[4,64,384]{2,1,0:T(8,128)(2,1)S(1)} %slice.16), channel_id=1, source_target_pairs={{0,8},{1,9},{2,10},{3,11},{4,0},{5,1},{6,2},{7,3},{8,12},{9,13},{1... | collective-permute-start | bytes 589832 | tf_op jit(solution)/shard_map/ppermute | solution.py:314
  43.0 1.5 %collective-permute-start.14 = (bf16[4,64,384]{2,1,0:T(8,128)(2,1)S(1)}, bf16[4,64,384]{2,1,0:T(8,128)(2,1)S(1)}, u32[]{:S(2)}, u32[]{:S(2)}) collective-permute-start(bf16[4,64,384]{2,1,0:T(8,128)(2,1)S(1)} %get-tuple-element.103), channel_id=1, source_target_pairs={{0,1},{1,0},{2,3},{3,2},{4,5},{5,4},{6,7},{7,6},{8,9},{9,8},{10,11... | collective-permute-start | bytes 589832 | tf_op jit(solution)/shard_map/ppermute | solution.py:317
  43.1 1.7 %collective-permute-start.15 = (bf16[4,64,384]{2,1,0:T(8,128)(2,1)S(1)}, bf16[4,64,384]{2,1,0:T(8,128)(2,1)S(1)}, u32[]{:S(2)}, u32[]{:S(2)}) collective-permute-start(bf16[4,64,384]{2,1,0:T(8,128)(2,1)S(1)} %get-tuple-element.102), channel_id=1, source_target_pairs={{0,1},{1,0},{2,3},{3,2},{4,5},{5,4},{6,7},{7,6},{8,9},{9,8},{10,11... | collective-permute-start | bytes 589832 | tf_op jit(solution)/shard_map/ppermute | solution.py:317
  43.6 4.0 %collective-permute-start.17 = (bf16[4,64,384]{2,1,0:T(8,128)(2,1)S(1)}, bf16[4,64,384]{2,1,0:T(8,128)(2,1)S(1)}, u32[]{:S(2)}, u32[]{:S(2)}) collective-permute-start(bf16[4,64,384]{2,1,0:T(8,128)(2,1)S(1)} %collective-permute-done.9.refs_2_), channel_id=1, source_target_pairs={{0,1},{1,0},{2,3},{3,2},{4,5},{5,4},{6,7},{7,6},{8,9},{9,8},{10,11... | collective-permute-start | bytes 589832 | tf_op jit(solution)/shard_map/ppermute | solution.py:317
  43.6 4.0 %collective-permute-start.16 = (bf16[4,64,384]{2,1,0:T(8,128)(2,1)S(1)}, bf16[4,64,384]{2,1,0:T(8,128)(2,1)S(1)}, u32[]{:S(2)}, u32[]{:S(2)}) collective-permute-start(bf16[4,64,384]{2,1,0:T(8,128)(2,1)S(1)} %collective-permute-done.11.refs_3_), channel_id=1, source_target_pairs={{0,1},{1,0},{2,3},{3,2},{4,5},{5,4},{6,7},{7,6},{8,9},{9,8},{10,11... | collective-permute-start | bytes 589832 | tf_op jit(solution)/shard_map/ppermute | solution.py:317
  49.4 6.6 %collective-permute-start.18 = (f32[2,8,128]{2,1,0:T(8,128)S(1)}, f32[2,8,128]{2,1,0:T(8,128)S(1)}, u32[]{:S(2)}, u32[]{:S(2)}) collective-permute-start(f32[2,8,128]{2,1,0:T(8,128)S(1)} %get-tuple-element.97), channel_id=1, source_target_pairs={{0,12},{1,13},{2,14},{3,15},{4,8},{5,9},{6,10},{7,11},{8,4},{9,5},... | collective-permute-start | bytes 24584 | tf_op jit(solution)/shard_map/ppermute | solution.py:317
  52.5 4.5 %collective-permute-start.19 = (f32[2,8,128]{2,1,0:T(8,128)S(1)}, f32[2,8,128]{2,1,0:T(8,128)S(1)}, u32[]{:S(2)}, u32[]{:S(2)}) collective-permute-start(f32[2,8,128]{2,1,0:T(8,128)S(1)} %get-tuple-element.97), channel_id=1, source_target_pairs={{0,8},{1,9},{2,10},{3,11},{4,12},{5,13},{6,14},{7,15},{8,0},{9,1},... | collective-permute-start | bytes 24584 | tf_op jit(solution)/shard_map/ppermute | solution.py:317
  54.0 3.7 %collective-permute-start.20 = (f32[2,8,128]{2,1,0:T(8,128)S(1)}, f32[2,8,128]{2,1,0:T(8,128)S(1)}, u32[]{:S(2)}, u32[]{:S(2)}) collective-permute-start(f32[2,8,128]{2,1,0:T(8,128)S(1)} %get-tuple-element.97), channel_id=1, source_target_pairs={{0,4},{1,5},{2,6},{3,7},{4,0},{5,1},{6,2},{7,3},{8,12},{9,13},{10,... | collective-permute-start | bytes 24584 | tf_op jit(solution)/shard_map/ppermute | solution.py:317
  57.7 3.9 %collective-permute-start.21 = (f32[2,8,128]{2,1,0:T(8,128)S(1)}, f32[2,8,128]{2,1,0:T(8,128)S(1)}, u32[]{:S(2)}, u32[]{:S(2)}) collective-permute-start(f32[2,8,128]{2,1,0:T(8,128)S(1)} %add_add_fusion), channel_id=1, source_target_pairs={{0,3},{1,2},{2,1},{3,0},{4,7},{5,6},{6,5},{7,4},{8,11},{9,10},{10,... | collective-permute-start | bytes 24584 | tf_op jit(solution)/shard_map/ppermute | solution.py:317
  57.7 3.9 %collective-permute-start.22 = (f32[2,8,128]{2,1,0:T(8,128)S(1)}, f32[2,8,128]{2,1,0:T(8,128)S(1)}, u32[]{:S(2)}, u32[]{:S(2)}) collective-permute-start(f32[2,8,128]{2,1,0:T(8,128)S(1)} %add_add_fusion), channel_id=1, source_target_pairs={{0,2},{1,3},{2,0},{3,1},{4,6},{5,7},{6,4},{7,5},{8,10},{9,11},{10,... | collective-permute-start | bytes 24584 | tf_op jit(solution)/shard_map/ppermute | solution.py:317
  59.3 2.3 %collective-permute-start.23 = (f32[2,8,128]{2,1,0:T(8,128)S(1)}, f32[2,8,128]{2,1,0:T(8,128)S(1)}, u32[]{:S(2)}, u32[]{:S(2)}) collective-permute-start(f32[2,8,128]{2,1,0:T(8,128)S(1)} %add_add_fusion), channel_id=1, source_target_pairs={{0,1},{1,0},{2,3},{3,2},{4,5},{5,4},{6,7},{7,6},{8,9},{9,8},{10,11... | collective-permute-start | bytes 24584 | tf_op jit(solution)/shard_map/ppermute | solution.py:317

commit v21 on v20

--- a/solution.py
+++ b/solution.py
@@ -325,7 +325,7 @@
     a, b, c, d = [amplitudes], [], [], []
     for k in range(depth):
         if 0 < k < depth - 1:
-            a[k], c[-1], state = lax.optimization_barrier((a[k], c[-1], state))
+            a[k], state = lax.optimization_barrier((a[k], state))
         if k < depth - 1:
             b.append(swap(a[k], 2))
             a.append(shift_z(a[k], 1))

time: 62.6 us -> 63.4 us (1.013)
  starting transfers between devices: 19.7 us -> 20.5 us
  transfers between devices with their start and end apart: 24 -> 24, of which waited for: 8 -> 6; matrix products, arithmetic and copies ran while one was open for 0% -> 0% of each run, Pallas kernels for 33% -> 33%
where the time goes in v21:
time: 63.4 us; the launch traced here: 63.3 us
  Pallas kernels  22.7 us (36%)
  starting transfers between devices  20.5 us (32%)
  waiting for transfers between devices  14.2 us (22%)
  local copies, waits for them, and re-layouts  4.46 us (7%)
  between operations  0.83 us (1%)
    pallas_call x5, Pallas kernels, ladder(): pl.pallas_call(functools.partial(ladder_kernel, call, depth, shard_tiles,...  14.6 us
    ppermute x20, starting transfers between devices, swap(): return lax.ppermute(x, 'vir', [(d, d ^ bits) for d in range(devices)])  14.2 us
    ppermute x4, waiting for transfers between devices, shift_z(): return lax.ppermute(x, 'vir', pairs)  11.9 us
    ppermute x4, starting transfers between devices, shift_z(): return lax.ppermute(x, 'vir', pairs)  6.29 us
    unnamed x12, local copies, waits for them, and re-layouts  4.37 us
    pallas_call x2, Pallas kernels, deliver(): pl.pallas_call(functools.partial(deliver_kernel, part), out_shape=jax.Sha...  4.04 us
    pallas_call x1, Pallas kernels, prepare(): pl.pallas_call(functools.partial(prepare_kernel, depth, shard_tiles), out...  4.01 us
    ppermute x20, waiting for transfers between devices, swap(): return lax.ppermute(x, 'vir', [(d, d ^ bits) for d in range(devices)])  2.33 us
  transfers between devices with their start and end apart: 24, of which 6 were waited for; matrix products, arithmetic and copies ran while one was open for 0% of the time, Pallas kernels for 33%

profile of v21, /device:TPU:0, one launch (start us, length us, event | category | flops | bytes accessed | tf_op | source)
XLA Modules:
  0.0 63.3 jit_solution(693395065876255174)
XLA Ops:
  0.6 3.1 %collective-permute-start = (bf16[8,64,384]{2,1,0:T(8,128)(2,1)}, bf16[8,64,384]{2,1,0:T(8,128)(2,1)S(1)}, u32[]{:S(2)}, u32[]{:S(2)}) collective-permute-start(bf16[8,64,384]{2,1,0:T(8,128)(2,1)} %refs_3_.1), channel_id=1, source_target_pairs={{0,4},{1,5},{2,6},{3,7},{4,12},{5,13},{6,14},{7,15},{8,0},{9,1},{1... | collective-permute-start | bytes 1179656 | tf_op jit(solution)/shard_map/ppermute | solution.py:314
  3.7 1.5 %collective-permute-start.2 = (bf16[8,64,384]{2,1,0:T(8,128)(2,1)}, bf16[8,64,384]{2,1,0:T(8,128)(2,1)S(1)}, u32[]{:S(2)}, u32[]{:S(2)}) collective-permute-start(bf16[8,64,384]{2,1,0:T(8,128)(2,1)} %refs_3_.1), channel_id=1, source_target_pairs={{0,2},{1,3},{2,0},{3,1},{4,6},{5,7},{6,4},{7,5},{8,10},{9,11},{10,... | collective-permute-start | bytes 1179656 | tf_op jit(solution)/shard_map/ppermute | solution.py:317
  5.2 0.7 %copy-done.3 = s32[8]{0:T(128)S(1)} copy-done((s32[8]{0:T(128)S(1)}, s32[8]{0:T(128)}, u32[]{:S(2)}) %copy-start.3) | copy-done | bytes 56
  5.9 0.7 %copy-done.5 = s32[32]{0:T(128)S(1)} copy-done((s32[32]{0:T(128)S(1)}, s32[32]{0:T(128)}, u32[]{:S(2)}) %copy-start.5) | copy-done | bytes 152
  6.5 4.0 %prepare.1 = (bf16[32,64,2048]{2,1,0:T(8,128)(2,1)S(1)}, bf16[132,64,384]{2,1,0:T(8,128)(2,1)S(1)}, f32[2,8,128]{2,1,0:T(8,128)S(1)}, s32[32]{0:T(128)S(1)}, s32...) custom-call(s32[1]{0:T(128)} %bitcast.me_ref, s32[8]{0:T(128)S(1)} %copy-done.3, s32[32]{0:T(128)S(1)} %copy-done.5), custom_call_target="tpu_custom_call" | custom-call | bytes 8388608 | tf_op jit(solution)/shard_map/prepare/pallas_call | solution.py:135
  10.6 3.5 %collective-permute-done.refs_0_ = bf16[8,64,384]{2,1,0:T(8,128)(2,1)S(1)} collective-permute-done((bf16[8,64,384]{2,1,0:T(8,128)(2,1)}, bf16[8,64,384]{2,1,0:T(8,128)(2,1)S(1)}, u32[]{:S(2)}, u32[]{:S(2)}) %collective-permute-start) | collective-permute-done | bytes 393248 | tf_op jit(solution)/shard_map/ppermute | solution.py:314
  14.0 0.9 %collective-permute-start.1 = (bf16[8,64,384]{2,1,0:T(8,128)(2,1)S(1)}, bf16[8,64,384]{2,1,0:T(8,128)(2,1)S(1)}, u32[]{:S(2)}, u32[]{:S(2)}) collective-permute-start(bf16[8,64,384]{2,1,0:T(8,128)(2,1)S(1)} %collective-permute-done.refs_0_), channel_id=1, source_target_pairs={{0,4},{1,5},{2,6},{3,7},{4,12},{5,13},{6,14},{7,15},{8,0},{9,1},{1... | collective-permute-start | bytes 1179656 | tf_op jit(solution)/shard_map/ppermute | solution.py:314
  15.0 1.5 %collective-permute-start.6 = (bf16[8,64,384]{2,1,0:T(8,128)(2,1)S(1)}, bf16[8,64,384]{2,1,0:T(8,128)(2,1)S(1)}, u32[]{:S(2)}, u32[]{:S(2)}) collective-permute-start(bf16[8,64,384]{2,1,0:T(8,128)(2,1)S(1)} %collective-permute-done.refs_0_), channel_id=1, source_target_pairs={{0,2},{1,3},{2,0},{3,1},{4,6},{5,7},{6,4},{7,5},{8,10},{9,11},{10,... | collective-permute-start | bytes 1179656 | tf_op jit(solution)/shard_map/ppermute | solution.py:317
  16.5 0.0 collective-permute-start.7
  16.5 0.0 collective-permute-done.2.refs_1_
  16.5 0.5 collective-permute-start.8
  17.0 1.4 %copy-done = bf16[32,64,384]{2,1,0:T(8,128)(2,1)S(1)} copy-done((bf16[32,64,384]{2,1,0:T(8,128)(2,1)S(1)}, bf16[32,64,384]{2,1,0:T(8,128)(2,1)}, u32[]{:S(2)}) %copy-start) | copy-done | bytes 1572888
  18.4 1.0 %copy-done.2 = bf16[8,64,384]{2,1,0:T(8,128)(2,1)S(1)} copy-done((bf16[8,64,384]{2,1,0:T(8,128)(2,1)S(1)}, bf16[8,64,384]{2,1,0:T(8,128)(2,1)}, u32[]{:S(2)}) %copy-start.2) | copy-done | bytes 393240
  19.4 0.7 %copy-done.4 = s32[8]{0:T(128)S(1)} copy-done((s32[8]{0:T(128)S(1)}, s32[8]{0:T(128)}, u32[]{:S(2)}) %copy-start.4) | copy-done | bytes 56
  20.1 2.1 %ladder_0.1 = (bf16[32,64,2048]{2,1,0:T(8,128)(2,1)S(1)}, bf16[132,64,384]{2,1,0:T(8,128)(2,1)S(1)}, f32[2,8,128]{2,1,0:T(8,128)S(1)}) custom-call(s32[1]{0:T(128)} %bitcast.me_ref, s32[8]{0:T(128)S(1)} %copy-done.4, s32[32]{0:T(128)S(1)} %get-tuple-element.50.order_ref, ...), custom_call_target="tpu_custom_call", output_to_operand_aliasing={{0}: (9, {}), {1}: (10, {})} | custom-call | flops 402653184 | bytes 2097152 | tf_op jit(solution)/shard_map/ladder_0/pallas_call | solution.py:252
  22.2 3.1 %collective-permute-done.1.refs_0_ = bf16[8,64,384]{2,1,0:T(8,128)(2,1)S(1)} collective-permute-done((bf16[8,64,384]{2,1,0:T(8,128)(2,1)S(1)}, bf16[8,64,384]{2,1,0:T(8,128)(2,1)S(1)}, u32[]{:S(2)}, u32[]{:S(2)}) %collective-permute-start.1) | collective-permute-done | bytes 393248 | tf_op jit(solution)/shard_map/ppermute | solution.py:314
  25.2 0.7 %collective-permute-start.4 = (bf16[8,64,384]{2,1,0:T(8,128)(2,1)S(1)}, bf16[8,64,384]{2,1,0:T(8,128)(2,1)S(1)}, u32[]{:S(2)}, u32[]{:S(2)}) collective-permute-start(bf16[8,64,384]{2,1,0:T(8,128)(2,1)S(1)} %collective-permute-done.1.refs_0_), channel_id=1, source_target_pairs={{0,4},{1,5},{2,6},{3,7},{4,12},{5,13},{6,14},{7,15},{8,0},{9,1},{1... | collective-permute-start | bytes 1179656 | tf_op jit(solution)/shard_map/ppermute | solution.py:314
  26.0 0.0 collective-permute-start.5
  26.0 0.0 collective-permute-done.6.refs_1_
  26.0 1.4 %collective-permute-start.10 = (bf16[8,64,384]{2,1,0:T(8,128)(2,1)S(1)}, bf16[8,64,384]{2,1,0:T(8,128)(2,1)S(1)}, u32[]{:S(2)}, u32[]{:S(2)}) collective-permute-start(bf16[8,64,384]{2,1,0:T(8,128)(2,1)S(1)} %collective-permute-done.1.refs_0_), channel_id=1, source_target_pairs={{0,2},{1,3},{2,0},{3,1},{4,6},{5,7},{6,4},{7,5},{8,10},{9,11},{10,... | collective-permute-start | bytes 1179656 | tf_op jit(solution)/shard_map/ppermute | solution.py:317
  27.4 0.0 collective-permute-done.7.refs_2_
  27.4 0.2 collective-permute-start.12
  27.6 0.0 collective-permute-done.8.refs_3_
  27.6 2.6 %ladder_1.1 = (bf16[32,64,2048]{2,1,0:T(8,128)(2,1)S(1)}, bf16[132,64,384]{2,1,0:T(8,128)(2,1)S(1)}, f32[2,8,128]{2,1,0:T(8,128)S(1)}) custom-call(s32[1]{0:T(128)} %bitcast.me_ref, s32[8]{0:T(128)S(1)} %copy-done.4, s32[32]{0:T(128)S(1)} %get-tuple-element.50.order_ref, ...), custom_call_target="tpu_custom_call", output_to_operand_aliasing={{0}: (9, {}), {1}: (10, {})} | custom-call | flops 402653184 | bytes 2097152 | tf_op jit(solution)/shard_map/ladder_1/pallas_call | solution.py:252
  30.2 5.3 %collective-permute-done.4.refs_0_ = bf16[8,64,384]{2,1,0:T(8,128)(2,1)S(1)} collective-permute-done((bf16[8,64,384]{2,1,0:T(8,128)(2,1)S(1)}, bf16[8,64,384]{2,1,0:T(8,128)(2,1)S(1)}, u32[]{:S(2)}, u32[]{:S(2)}) %collective-permute-start.4) | collective-permute-done | bytes 393248 | tf_op jit(solution)/shard_map/ppermute | solution.py:314
  35.6 1.0 %collective-permute-start.11 = (bf16[4,64,384]{2,1,0:T(8,128)(2,1)S(1)}, bf16[4,64,384]{2,1,0:T(8,128)(2,1)S(1)}, u32[]{:S(2)}, u32[]{:S(2)}) collective-permute-start(bf16[4,64,384]{2,1,0:T(8,128)(2,1)S(1)} %slice.13), channel_id=1, source_target_pairs={{0,2},{1,3},{2,0},{3,1},{4,6},{5,7},{6,4},{7,5},{8,10},{9,11},{10,... | collective-permute-start | bytes 589832 | tf_op jit(solution)/shard_map/ppermute | solution.py:317
  36.6 1.5 %collective-permute-start.9 = (bf16[4,64,384]{2,1,0:T(8,128)(2,1)S(1)}, bf16[4,64,384]{2,1,0:T(8,128)(2,1)S(1)}, u32[]{:S(2)}, u32[]{:S(2)}) collective-permute-start(bf16[4,64,384]{2,1,0:T(8,128)(2,1)S(1)} %slice.16), channel_id=1, source_target_pairs={{0,8},{1,9},{2,10},{3,11},{4,0},{5,1},{6,2},{7,3},{8,12},{9,13},{1... | collective-permute-start | bytes 589832 | tf_op jit(solution)/shard_map/ppermute | solution.py:314
  38.1 0.0 collective-permute-done.12.refs_3_
  38.1 0.0 collective-permute-done.13.refs_4_
  38.1 4.8 %ladder_2.1 = (bf16[32,64,2048]{2,1,0:T(8,128)(2,1)S(1)}, bf16[132,64,384]{2,1,0:T(8,128)(2,1)S(1)}, f32[2,8,128]{2,1,0:T(8,128)S(1)}) custom-call(s32[1]{0:T(128)} %bitcast.me_ref, s32[8]{0:T(128)S(1)} %copy-done.4, s32[32]{0:T(128)S(1)} %get-tuple-element.50.order_ref, ...), custom_call_target="tpu_custom_call", output_to_operand_aliasing={{0}: (9, {}), {1}: (10, {})} | custom-call | flops 503316480 | bytes 2621440 | tf_op jit(solution)/shard_map/ladder_2/pallas_call | solution.py:252
  43.0 0.1 collective-permute-start.14
  43.1 0.5 collective-permute-start.15
  43.6 0.0 collective-permute-done.9.refs_2_
  43.6 0.1 collective-permute-start.17
  43.7 0.4 collective-permute-start.16
  44.1 0.4 collective-permute-done.14.refs_0_
  44.5 0.3 collective-permute-done.15.refs_1_
  44.8 3.3 %ladder_3.1 = (bf16[32,64,2048]{2,1,0:T(8,128)(2,1)S(1)}, bf16[132,64,384]{2,1,0:T(8,128)(2,1)S(1)}, f32[2,8,128]{2,1,0:T(8,128)S(1)}) custom-call(s32[1]{0:T(128)} %bitcast.me_ref, s32[8]{0:T(128)S(1)} %copy-done.4, s32[32]{0:T(128)S(1)} %get-tuple-element.50.order_ref, ...), custom_call_target="tpu_custom_call", output_to_operand_aliasing={{0}: (9, {}), {1}: (10, {})} | custom-call | flops 201326592 | bytes 1048576 | tf_op jit(solution)/shard_map/ladder_3/pallas_call | solution.py:252
  48.2 1.8 %ladder_4.1 = (bf16[32,64,2048]{2,1,0:T(8,128)(2,1)S(1)}, bf16[132,64,384]{2,1,0:T(8,128)(2,1)S(1)}, f32[2,8,128]{2,1,0:T(8,128)S(1)}) custom-call(s32[1]{0:T(128)} %bitcast.me_ref, s32[8]{0:T(128)S(1)} %copy-done.4, s32[32]{0:T(128)S(1)} %get-tuple-element.50.order_ref, ...), custom_call_target="tpu_custom_call", output_to_operand_aliasing={{0}: (9, {}), {1}: (10, {})} | custom-call | flops 100663296 | bytes 524288 | tf_op jit(solution)/shard_map/ladder_4/pallas_call | solution.py:252
  50.0 2.0 %collective-permute-start.18 = (f32[2,8,128]{2,1,0:T(8,128)S(1)}, f32[2,8,128]{2,1,0:T(8,128)S(1)}, u32[]{:S(2)}, u32[]{:S(2)}) collective-permute-start(f32[2,8,128]{2,1,0:T(8,128)S(1)} %get-tuple-element.93), channel_id=1, source_target_pairs={{0,12},{1,13},{2,14},{3,15},{4,8},{5,9},{6,10},{7,11},{8,4},{9,5},... | collective-permute-start | bytes 24584 | tf_op jit(solution)/shard_map/ppermute | solution.py:317
  52.0 3.1 %collective-permute-start.19 = (f32[2,8,128]{2,1,0:T(8,128)S(1)}, f32[2,8,128]{2,1,0:T(8,128)S(1)}, u32[]{:S(2)}, u32[]{:S(2)}) collective-permute-start(f32[2,8,128]{2,1,0:T(8,128)S(1)} %get-tuple-element.93), channel_id=1, source_target_pairs={{0,8},{1,9},{2,10},{3,11},{4,12},{5,13},{6,14},{7,15},{8,0},{9,1},... | collective-permute-start | bytes 24584 | tf_op jit(solution)/shard_map/ppermute | solution.py:317
  55.1 2.0 %deliver_0.1.refs_0_ = bf16[32,64,2048]{2,1,0:T(8,128)(2,1)} custom-call(bf16[32,64,2048]{2,1,0:T(8,128)(2,1)S(1)} %get-tuple-element.95.held_ref), custom_call_target="tpu_custom_call" | custom-call | tf_op jit(solution)/shard_map/deliver_0/pallas_call | solution.py:290
  57.1 1.6 %collective-permute-done.20 = f32[2,8,128]{2,1,0:T(8,128)S(1)} collective-permute-done((f32[2,8,128]{2,1,0:T(8,128)S(1)}, f32[2,8,128]{2,1,0:T(8,128)S(1)}, u32[]{:S(2)}, u32[]{:S(2)}) %collective-permute-start.20) | collective-permute-done | bytes 8224 | tf_op jit(solution)/shard_map/ppermute | solution.py:317
  58.7 0.1 collective-permute-start.22
  58.8 1.8 %collective-permute-start.23 = (f32[2,8,128]{2,1,0:T(8,128)S(1)}, f32[2,8,128]{2,1,0:T(8,128)S(1)}, u32[]{:S(2)}, u32[]{:S(2)}) collective-permute-start(f32[2,8,128]{2,1,0:T(8,128)S(1)} %add_add_fusion), channel_id=1, source_target_pairs={{0,1},{1,0},{2,3},{3,2},{4,5},{5,4},{6,7},{7,6},{8,9},{9,8},{10,11... | collective-permute-start | bytes 24584 | tf_op jit(solution)/shard_map/ppermute | solution.py:317
  60.6 2.0 %deliver_1.1 = bf16[32,64,2048]{2,1,0:T(8,128)(2,1)} custom-call(bf16[32,64,2048]{2,1,0:T(8,128)(2,1)S(1)} %get-tuple-element.95.held_ref, bf16[32,64,2048]{2,1,0:T(8,128)(2,1)} %deliver_0.1.refs_0_), custom_call_target="tpu_custom_call", output_to_operand_aliasing={{}: (1, {})} | custom-call | tf_op jit(solution)/shard_map/deliver_1/pallas_call | solution.py:290
  62.7 0.1 add_reduce_fusion
  62.7 0.5 add_sqrt_fusion
  (26 shorter events, 0.1 us)
Async XLA Ops:
  0.6 13.4 %collective-permute-start = (bf16[8,64,384]{2,1,0:T(8,128)(2,1)}, bf16[8,64,384]{2,1,0:T(8,128)(2,1)S(1)}, u32[]{:S(2)}, u32[]{:S(2)}) collective-permute-start(bf16[8,64,384]{2,1,0:T(8,128)(2,1)} %refs_3_.1), channel_id=1, source_target_pairs={{0,4},{1,5},{2,6},{3,7},{4,12},{5,13},{6,14},{7,15},{8,0},{9,1},{1... | collective-permute-start | bytes 1179656 | tf_op jit(solution)/shard_map/ppermute | solution.py:314
  3.7 12.8 %collective-permute-start.2 = (bf16[8,64,384]{2,1,0:T(8,128)(2,1)}, bf16[8,64,384]{2,1,0:T(8,128)(2,1)S(1)}, u32[]{:S(2)}, u32[]{:S(2)}) collective-permute-start(bf16[8,64,384]{2,1,0:T(8,128)(2,1)} %refs_3_.1), channel_id=1, source_target_pairs={{0,2},{1,3},{2,0},{3,1},{4,6},{5,7},{6,4},{7,5},{8,10},{9,11},{10,... | collective-permute-start | bytes 1179656 | tf_op jit(solution)/shard_map/ppermute | solution.py:317
  5.2 11.8 %collective-permute-start.3 = (bf16[8,64,384]{2,1,0:T(8,128)(2,1)}, bf16[8,64,384]{2,1,0:T(8,128)(2,1)S(1)}, u32[]{:S(2)}, u32[]{:S(2)}) collective-permute-start(bf16[8,64,384]{2,1,0:T(8,128)(2,1)} %refs_3_.1), channel_id=1, source_target_pairs={{0,1},{1,0},{2,3},{3,2},{4,5},{5,4},{6,7},{7,6},{8,9},{9,8},{10,11... | collective-permute-start | bytes 1179656 | tf_op jit(solution)/shard_map/ppermute | solution.py:317
  5.2 0.7 %copy-start.3 = (s32[8]{0:T(128)S(1)}, s32[8]{0:T(128)}, u32[]{:S(2)}) copy-start(s32[8]{0:T(128)} %counts_ref.11) | copy-start | bytes 100
  5.9 0.7 %copy-start.5 = (s32[32]{0:T(128)S(1)}, s32[32]{0:T(128)}, u32[]{:S(2)}) copy-start(s32[32]{0:T(128)} %irrep_ref.1) | copy-start | bytes 388
  14.0 11.2 %collective-permute-start.1 = (bf16[8,64,384]{2,1,0:T(8,128)(2,1)S(1)}, bf16[8,64,384]{2,1,0:T(8,128)(2,1)S(1)}, u32[]{:S(2)}, u32[]{:S(2)}) collective-permute-start(bf16[8,64,384]{2,1,0:T(8,128)(2,1)S(1)} %collective-permute-done.refs_0_), channel_id=1, source_target_pairs={{0,4},{1,5},{2,6},{3,7},{4,12},{5,13},{6,14},{7,15},{8,0},{9,1},{1... | collective-permute-start | bytes 1179656 | tf_op jit(solution)/shard_map/ppermute | solution.py:314
  15.0 11.0 %collective-permute-start.6 = (bf16[8,64,384]{2,1,0:T(8,128)(2,1)S(1)}, bf16[8,64,384]{2,1,0:T(8,128)(2,1)S(1)}, u32[]{:S(2)}, u32[]{:S(2)}) collective-permute-start(bf16[8,64,384]{2,1,0:T(8,128)(2,1)S(1)} %collective-permute-done.refs_0_), channel_id=1, source_target_pairs={{0,2},{1,3},{2,0},{3,1},{4,6},{5,7},{6,4},{7,5},{8,10},{9,11},{10,... | collective-permute-start | bytes 1179656 | tf_op jit(solution)/shard_map/ppermute | solution.py:317
  16.5 10.9 %collective-permute-start.7 = (bf16[8,64,384]{2,1,0:T(8,128)(2,1)S(1)}, bf16[8,64,384]{2,1,0:T(8,128)(2,1)S(1)}, u32[]{:S(2)}, u32[]{:S(2)}) collective-permute-start(bf16[8,64,384]{2,1,0:T(8,128)(2,1)S(1)} %collective-permute-done.refs_0_), channel_id=1, source_target_pairs={{0,1},{1,0},{2,3},{3,2},{4,5},{5,4},{6,7},{7,6},{8,9},{9,8},{10,11... | collective-permute-start | bytes 1179656 | tf_op jit(solution)/shard_map/ppermute | solution.py:317
  16.5 11.1 %collective-permute-start.8 = (bf16[8,64,384]{2,1,0:T(8,128)(2,1)S(1)}, bf16[8,64,384]{2,1,0:T(8,128)(2,1)S(1)}, u32[]{:S(2)}, u32[]{:S(2)}) collective-permute-start(bf16[8,64,384]{2,1,0:T(8,128)(2,1)S(1)} %collective-permute-done.2.refs_1_), channel_id=1, source_target_pairs={{0,1},{1,0},{2,3},{3,2},{4,5},{5,4},{6,7},{7,6},{8,9},{9,8},{10,11... | collective-permute-start | bytes 1179656 | tf_op jit(solution)/shard_map/ppermute | solution.py:317
  17.0 1.4 %copy-start = (bf16[32,64,384]{2,1,0:T(8,128)(2,1)S(1)}, bf16[32,64,384]{2,1,0:T(8,128)(2,1)}, u32[]{:S(2)}) copy-start(bf16[32,64,384]{2,1,0:T(8,128)(2,1)} %v_ref.9) | copy-start | bytes 4718596
  18.4 1.0 %copy-start.2 = (bf16[8,64,384]{2,1,0:T(8,128)(2,1)S(1)}, bf16[8,64,384]{2,1,0:T(8,128)(2,1)}, u32[]{:S(2)}) copy-start(bf16[8,64,384]{2,1,0:T(8,128)(2,1)} %refs_3_.1) | copy-start | bytes 1179652
  19.4 0.7 %copy-start.4 = (s32[8]{0:T(128)S(1)}, s32[8]{0:T(128)}, u32[]{:S(2)}) copy-start(s32[8]{0:T(128)} %counts_ref.11) | copy-start | bytes 100
  20.1 7.5 %copy-start.1 = (bf16[32,64,384]{2,1,0:T(8,128)(2,1)S(1)}, bf16[32,64,384]{2,1,0:T(8,128)(2,1)}, u32[]{:S(2)}) copy-start(bf16[32,64,384]{2,1,0:T(8,128)(2,1)} %v_ref.9) | copy-start | bytes 4718596
  25.2 10.3 %collective-permute-start.4 = (bf16[8,64,384]{2,1,0:T(8,128)(2,1)S(1)}, bf16[8,64,384]{2,1,0:T(8,128)(2,1)S(1)}, u32[]{:S(2)}, u32[]{:S(2)}) collective-permute-start(bf16[8,64,384]{2,1,0:T(8,128)(2,1)S(1)} %collective-permute-done.1.refs_0_), channel_id=1, source_target_pairs={{0,4},{1,5},{2,6},{3,7},{4,12},{5,13},{6,14},{7,15},{8,0},{9,1},{1... | collective-permute-start | bytes 1179656 | tf_op jit(solution)/shard_map/ppermute | solution.py:314
  26.0 9.5 %collective-permute-start.5 = (bf16[8,64,384]{2,1,0:T(8,128)(2,1)S(1)}, bf16[8,64,384]{2,1,0:T(8,128)(2,1)S(1)}, u32[]{:S(2)}, u32[]{:S(2)}) collective-permute-start(bf16[8,64,384]{2,1,0:T(8,128)(2,1)S(1)} %collective-permute-done.1.refs_0_), channel_id=1, source_target_pairs={{0,1},{1,0},{2,3},{3,2},{4,5},{5,4},{6,7},{7,6},{8,9},{9,8},{10,11... | collective-permute-start | bytes 1179656 | tf_op jit(solution)/shard_map/ppermute | solution.py:317
  26.0 12.0 %collective-permute-start.10 = (bf16[8,64,384]{2,1,0:T(8,128)(2,1)S(1)}, bf16[8,64,384]{2,1,0:T(8,128)(2,1)S(1)}, u32[]{:S(2)}, u32[]{:S(2)}) collective-permute-start(bf16[8,64,384]{2,1,0:T(8,128)(2,1)S(1)} %collective-permute-done.1.refs_0_), channel_id=1, source_target_pairs={{0,2},{1,3},{2,0},{3,1},{4,6},{5,7},{6,4},{7,5},{8,10},{9,11},{10,... | collective-permute-start | bytes 1179656 | tf_op jit(solution)/shard_map/ppermute | solution.py:317
  27.4 10.7 %collective-permute-start.12 = (bf16[8,64,384]{2,1,0:T(8,128)(2,1)S(1)}, bf16[8,64,384]{2,1,0:T(8,128)(2,1)S(1)}, u32[]{:S(2)}, u32[]{:S(2)}) collective-permute-start(bf16[8,64,384]{2,1,0:T(8,128)(2,1)S(1)} %collective-permute-done.6.refs_1_), channel_id=1, source_target_pairs={{0,1},{1,0},{2,3},{3,2},{4,5},{5,4},{6,7},{7,6},{8,9},{9,8},{10,11... | collective-permute-start | bytes 1179656 | tf_op jit(solution)/shard_map/ppermute | solution.py:317
  35.5 2.6 %collective-permute-start.13 = (bf16[8,64,384]{2,1,0:T(8,128)(2,1)S(1)}, bf16[8,64,384]{2,1,0:T(8,128)(2,1)S(1)}, u32[]{:S(2)}, u32[]{:S(2)}) collective-permute-start(bf16[8,64,384]{2,1,0:T(8,128)(2,1)S(1)} %collective-permute-done.4.refs_0_), channel_id=1, source_target_pairs={{0,1},{1,0},{2,3},{3,2},{4,5},{5,4},{6,7},{7,6},{8,9},{9,8},{10,11... | collective-permute-start | bytes 1179656 | tf_op jit(solution)/shard_map/ppermute | solution.py:317
  35.6 7.4 %collective-permute-start.11 = (bf16[4,64,384]{2,1,0:T(8,128)(2,1)S(1)}, bf16[4,64,384]{2,1,0:T(8,128)(2,1)S(1)}, u32[]{:S(2)}, u32[]{:S(2)}) collective-permute-start(bf16[4,64,384]{2,1,0:T(8,128)(2,1)S(1)} %slice.13), channel_id=1, source_target_pairs={{0,2},{1,3},{2,0},{3,1},{4,6},{5,7},{6,4},{7,5},{8,10},{9,11},{10,... | collective-permute-start | bytes 589832 | tf_op jit(solution)/shard_map/ppermute | solution.py:317
  36.6 7.0 %collective-permute-start.9 = (bf16[4,64,384]{2,1,0:T(8,128)(2,1)S(1)}, bf16[4,64,384]{2,1,0:T(8,128)(2,1)S(1)}, u32[]{:S(2)}, u32[]{:S(2)}) collective-permute-start(bf16[4,64,384]{2,1,0:T(8,128)(2,1)S(1)} %slice.16), channel_id=1, source_target_pairs={{0,8},{1,9},{2,10},{3,11},{4,0},{5,1},{6,2},{7,3},{8,12},{9,13},{1... | collective-permute-start | bytes 589832 | tf_op jit(solution)/shard_map/ppermute | solution.py:314
  43.0 1.5 %collective-permute-start.14 = (bf16[4,64,384]{2,1,0:T(8,128)(2,1)S(1)}, bf16[4,64,384]{2,1,0:T(8,128)(2,1)S(1)}, u32[]{:S(2)}, u32[]{:S(2)}) collective-permute-start(bf16[4,64,384]{2,1,0:T(8,128)(2,1)S(1)} %get-tuple-element.99), channel_id=1, source_target_pairs={{0,1},{1,0},{2,3},{3,2},{4,5},{5,4},{6,7},{7,6},{8,9},{9,8},{10,11... | collective-permute-start | bytes 589832 | tf_op jit(solution)/shard_map/ppermute | solution.py:317
  43.1 1.7 %collective-permute-start.15 = (bf16[4,64,384]{2,1,0:T(8,128)(2,1)S(1)}, bf16[4,64,384]{2,1,0:T(8,128)(2,1)S(1)}, u32[]{:S(2)}, u32[]{:S(2)}) collective-permute-start(bf16[4,64,384]{2,1,0:T(8,128)(2,1)S(1)} %get-tuple-element.98), channel_id=1, source_target_pairs={{0,1},{1,0},{2,3},{3,2},{4,5},{5,4},{6,7},{7,6},{8,9},{9,8},{10,11... | collective-permute-start | bytes 589832 | tf_op jit(solution)/shard_map/ppermute | solution.py:317
  43.6 4.6 %collective-permute-start.17 = (bf16[4,64,384]{2,1,0:T(8,128)(2,1)S(1)}, bf16[4,64,384]{2,1,0:T(8,128)(2,1)S(1)}, u32[]{:S(2)}, u32[]{:S(2)}) collective-permute-start(bf16[4,64,384]{2,1,0:T(8,128)(2,1)S(1)} %collective-permute-done.9.refs_2_), channel_id=1, source_target_pairs={{0,1},{1,0},{2,3},{3,2},{4,5},{5,4},{6,7},{7,6},{8,9},{9,8},{10,11... | collective-permute-start | bytes 589832 | tf_op jit(solution)/shard_map/ppermute | solution.py:317
  43.7 4.5 %collective-permute-start.16 = (bf16[4,64,384]{2,1,0:T(8,128)(2,1)S(1)}, bf16[4,64,384]{2,1,0:T(8,128)(2,1)S(1)}, u32[]{:S(2)}, u32[]{:S(2)}) collective-permute-start(bf16[4,64,384]{2,1,0:T(8,128)(2,1)S(1)} %collective-permute-done.11.refs_3_), channel_id=1, source_target_pairs={{0,1},{1,0},{2,3},{3,2},{4,5},{5,4},{6,7},{7,6},{8,9},{9,8},{10,11... | collective-permute-start | bytes 589832 | tf_op jit(solution)/shard_map/ppermute | solution.py:317
  50.0 7.1 %collective-permute-start.18 = (f32[2,8,128]{2,1,0:T(8,128)S(1)}, f32[2,8,128]{2,1,0:T(8,128)S(1)}, u32[]{:S(2)}, u32[]{:S(2)}) collective-permute-start(f32[2,8,128]{2,1,0:T(8,128)S(1)} %get-tuple-element.93), channel_id=1, source_target_pairs={{0,12},{1,13},{2,14},{3,15},{4,8},{5,9},{6,10},{7,11},{8,4},{9,5},... | collective-permute-start | bytes 24584 | tf_op jit(solution)/shard_map/ppermute | solution.py:317
  52.0 5.1 %collective-permute-start.19 = (f32[2,8,128]{2,1,0:T(8,128)S(1)}, f32[2,8,128]{2,1,0:T(8,128)S(1)}, u32[]{:S(2)}, u32[]{:S(2)}) collective-permute-start(f32[2,8,128]{2,1,0:T(8,128)S(1)} %get-tuple-element.93), channel_id=1, source_target_pairs={{0,8},{1,9},{2,10},{3,11},{4,12},{5,13},{6,14},{7,15},{8,0},{9,1},... | collective-permute-start | bytes 24584 | tf_op jit(solution)/shard_map/ppermute | solution.py:317
  55.1 3.7 %collective-permute-start.20 = (f32[2,8,128]{2,1,0:T(8,128)S(1)}, f32[2,8,128]{2,1,0:T(8,128)S(1)}, u32[]{:S(2)}, u32[]{:S(2)}) collective-permute-start(f32[2,8,128]{2,1,0:T(8,128)S(1)} %get-tuple-element.93), channel_id=1, source_target_pairs={{0,4},{1,5},{2,6},{3,7},{4,0},{5,1},{6,2},{7,3},{8,12},{9,13},{10,... | collective-permute-start | bytes 24584 | tf_op jit(solution)/shard_map/ppermute | solution.py:317
  58.7 3.9 %collective-permute-start.21 = (f32[2,8,128]{2,1,0:T(8,128)S(1)}, f32[2,8,128]{2,1,0:T(8,128)S(1)}, u32[]{:S(2)}, u32[]{:S(2)}) collective-permute-start(f32[2,8,128]{2,1,0:T(8,128)S(1)} %add_add_fusion), channel_id=1, source_target_pairs={{0,3},{1,2},{2,1},{3,0},{4,7},{5,6},{6,5},{7,4},{8,11},{9,10},{10,... | collective-permute-start | bytes 24584 | tf_op jit(solution)/shard_map/ppermute | solution.py:317
  58.7 3.9 %collective-permute-start.22 = (f32[2,8,128]{2,1,0:T(8,128)S(1)}, f32[2,8,128]{2,1,0:T(8,128)S(1)}, u32[]{:S(2)}, u32[]{:S(2)}) collective-permute-start(f32[2,8,128]{2,1,0:T(8,128)S(1)} %add_add_fusion), channel_id=1, source_target_pairs={{0,2},{1,3},{2,0},{3,1},{4,6},{5,7},{6,4},{7,5},{8,10},{9,11},{10,... | collective-permute-start | bytes 24584 | tf_op jit(solution)/shard_map/ppermute | solution.py:317
  58.8 3.8 %collective-permute-start.23 = (f32[2,8,128]{2,1,0:T(8,128)S(1)}, f32[2,8,128]{2,1,0:T(8,128)S(1)}, u32[]{:S(2)}, u32[]{:S(2)}) collective-permute-start(f32[2,8,128]{2,1,0:T(8,128)S(1)} %add_add_fusion), channel_id=1, source_target_pairs={{0,1},{1,0},{2,3},{3,2},{4,5},{5,4},{6,7},{7,6},{8,9},{9,8},{10,11... | collective-permute-start | bytes 24584 | tf_op jit(solution)/shard_map/ppermute | solution.py:317

commit v22 on v21

--- a/solution.py
+++ b/solution.py
@@ -325,7 +325,10 @@
     a, b, c, d = [amplitudes], [], [], []
     for k in range(depth):
         if 0 < k < depth - 1:
-            a[k], state = lax.optimization_barrier((a[k], state))
+            if k == 1:
+                a[k], state = lax.optimization_barrier((a[k], state))
+            else:
+                a[k], c[-1], state = lax.optimization_barrier((a[k], c[-1], state))
         if k < depth - 1:
             b.append(swap(a[k], 2))
             a.append(shift_z(a[k], 1))

time: 63.4 us -> 63 us (level)
  Pallas kernels: 22.7 us -> 24.3 us
  waiting for transfers between devices: 14.2 us -> 12.9 us
  starting transfers between devices: 20.5 us -> 19.6 us
    pallas_call x5, Pallas kernels: 14.6 us -> 16.2 us  [ladder(): pl.pallas_call(functools.partial(ladder_kernel, call, depth, shard_tiles,...]
    ppermute x4, waiting for transfers between devices: 11.9 us -> 10.6 us  [shift_z(): return lax.ppermute(x, 'vir', pairs)]
  transfers between devices with their start and end apart: 24 -> 24, of which waited for: 6 -> 7; matrix products, arithmetic and copies ran while one was open for 0% -> 0% of each run, Pallas kernels for 33% -> 35%
where the time goes in v22:
time: 63 us; the launch traced here: 62.8 us
  Pallas kernels  24.3 us (39%)
  starting transfers between devices  19.6 us (31%)
  waiting for transfers between devices  12.9 us (20%)
  local copies, waits for them, and re-layouts  4.46 us (7%)
  between operations  0.81 us (1%)
  other arithmetic  0.63 us (1%)
    pallas_call x5, Pallas kernels, ladder(): pl.pallas_call(functools.partial(ladder_kernel, call, depth, shard_tiles,...  16.2 us
    ppermute x20, starting transfers between devices, swap(): return lax.ppermute(x, 'vir', [(d, d ^ bits) for d in range(devices)])  13.6 us
    ppermute x4, waiting for transfers between devices, shift_z(): return lax.ppermute(x, 'vir', pairs)  10.6 us
    ppermute x4, starting transfers between devices, shift_z(): return lax.ppermute(x, 'vir', pairs)  6.05 us
    unnamed x12, local copies, waits for them, and re-layouts  4.37 us
    pallas_call x1, Pallas kernels, prepare(): pl.pallas_call(functools.partial(prepare_kernel, depth, shard_tiles), out...  4.1 us
    pallas_call x2, Pallas kernels, deliver(): pl.pallas_call(functools.partial(deliver_kernel, part), out_shape=jax.Sha...  4.04 us
    ppermute x20, waiting for transfers between devices, swap(): return lax.ppermute(x, 'vir', [(d, d ^ bits) for d in range(devices)])  2.34 us
  transfers between devices with their start and end apart: 24, of which 7 were waited for; matrix products, arithmetic and copies ran while one was open for 0% of the time, Pallas kernels for 35%

profile of v22, /device:TPU:0, one launch (start us, length us, event | category | flops | bytes accessed | tf_op | source)
XLA Modules:
  0.0 62.8 jit_solution(13317156245267363714)
XLA Ops:
  0.6 3.1 %collective-permute-start = (bf16[8,64,384]{2,1,0:T(8,128)(2,1)}, bf16[8,64,384]{2,1,0:T(8,128)(2,1)S(1)}, u32[]{:S(2)}, u32[]{:S(2)}) collective-permute-start(bf16[8,64,384]{2,1,0:T(8,128)(2,1)} %refs_3_.1), channel_id=1, source_target_pairs={{0,4},{1,5},{2,6},{3,7},{4,12},{5,13},{6,14},{7,15},{8,0},{9,1},{1... | collective-permute-start | bytes 1179656 | tf_op jit(solution)/shard_map/ppermute | solution.py:314
  3.7 1.5 %collective-permute-start.3 = (bf16[8,64,384]{2,1,0:T(8,128)(2,1)}, bf16[8,64,384]{2,1,0:T(8,128)(2,1)S(1)}, u32[]{:S(2)}, u32[]{:S(2)}) collective-permute-start(bf16[8,64,384]{2,1,0:T(8,128)(2,1)} %refs_3_.1), channel_id=1, source_target_pairs={{0,2},{1,3},{2,0},{3,1},{4,6},{5,7},{6,4},{7,5},{8,10},{9,11},{10,... | collective-permute-start | bytes 1179656 | tf_op jit(solution)/shard_map/ppermute | solution.py:317
  5.2 0.0 collective-permute-start.4
  5.2 0.7 %copy-done.3 = s32[8]{0:T(128)S(1)} copy-done((s32[8]{0:T(128)S(1)}, s32[8]{0:T(128)}, u32[]{:S(2)}) %copy-start.3) | copy-done | bytes 56
  5.9 0.7 %copy-done.5 = s32[32]{0:T(128)S(1)} copy-done((s32[32]{0:T(128)S(1)}, s32[32]{0:T(128)}, u32[]{:S(2)}) %copy-start.5) | copy-done | bytes 152
  6.5 4.1 %prepare.1 = (bf16[32,64,2048]{2,1,0:T(8,128)(2,1)S(1)}, bf16[132,64,384]{2,1,0:T(8,128)(2,1)S(1)}, f32[2,8,128]{2,1,0:T(8,128)S(1)}, s32[32]{0:T(128)S(1)}, s32...) custom-call(s32[1]{0:T(128)} %bitcast.me_ref, s32[8]{0:T(128)S(1)} %copy-done.3, s32[32]{0:T(128)S(1)} %copy-done.5), custom_call_target="tpu_custom_call" | custom-call | bytes 8388608 | tf_op jit(solution)/shard_map/prepare/pallas_call | solution.py:135
  10.7 3.4 %collective-permute-done.refs_0_ = bf16[8,64,384]{2,1,0:T(8,128)(2,1)S(1)} collective-permute-done((bf16[8,64,384]{2,1,0:T(8,128)(2,1)}, bf16[8,64,384]{2,1,0:T(8,128)(2,1)S(1)}, u32[]{:S(2)}, u32[]{:S(2)}) %collective-permute-start) | collective-permute-done | bytes 393248 | tf_op jit(solution)/shard_map/ppermute | solution.py:314
  14.0 0.9 %collective-permute-start.1 = (bf16[8,64,384]{2,1,0:T(8,128)(2,1)S(1)}, bf16[8,64,384]{2,1,0:T(8,128)(2,1)S(1)}, u32[]{:S(2)}, u32[]{:S(2)}) collective-permute-start(bf16[8,64,384]{2,1,0:T(8,128)(2,1)S(1)} %collective-permute-done.refs_0_), channel_id=1, source_target_pairs={{0,4},{1,5},{2,6},{3,7},{4,12},{5,13},{6,14},{7,15},{8,0},{9,1},{1... | collective-permute-start | bytes 1179656 | tf_op jit(solution)/shard_map/ppermute | solution.py:314
  15.0 1.5 %collective-permute-start.7 = (bf16[8,64,384]{2,1,0:T(8,128)(2,1)S(1)}, bf16[8,64,384]{2,1,0:T(8,128)(2,1)S(1)}, u32[]{:S(2)}, u32[]{:S(2)}) collective-permute-start(bf16[8,64,384]{2,1,0:T(8,128)(2,1)S(1)} %collective-permute-done.refs_0_), channel_id=1, source_target_pairs={{0,2},{1,3},{2,0},{3,1},{4,6},{5,7},{6,4},{7,5},{8,10},{9,11},{10,... | collective-permute-start | bytes 1179656 | tf_op jit(solution)/shard_map/ppermute | solution.py:317
  16.5 0.0 collective-permute-done.3.refs_1_
  16.5 0.2 collective-permute-start.8
  16.7 0.0 collective-permute-done.4.refs_2_
  16.7 1.4 %copy-done = bf16[32,64,384]{2,1,0:T(8,128)(2,1)S(1)} copy-done((bf16[32,64,384]{2,1,0:T(8,128)(2,1)S(1)}, bf16[32,64,384]{2,1,0:T(8,128)(2,1)}, u32[]{:S(2)}) %copy-start) | copy-done | bytes 1572888
  18.2 1.0 %copy-done.2 = bf16[8,64,384]{2,1,0:T(8,128)(2,1)S(1)} copy-done((bf16[8,64,384]{2,1,0:T(8,128)(2,1)S(1)}, bf16[8,64,384]{2,1,0:T(8,128)(2,1)}, u32[]{:S(2)}) %copy-start.2) | copy-done | bytes 393240
  19.2 0.7 %copy-done.4 = s32[8]{0:T(128)S(1)} copy-done((s32[8]{0:T(128)S(1)}, s32[8]{0:T(128)}, u32[]{:S(2)}) %copy-start.4) | copy-done | bytes 56
  19.8 2.1 %ladder_0.1 = (bf16[32,64,2048]{2,1,0:T(8,128)(2,1)S(1)}, bf16[132,64,384]{2,1,0:T(8,128)(2,1)S(1)}, f32[2,8,128]{2,1,0:T(8,128)S(1)}) custom-call(s32[1]{0:T(128)} %bitcast.me_ref, s32[8]{0:T(128)S(1)} %copy-done.4, s32[32]{0:T(128)S(1)} %get-tuple-element.51.order_ref, ...), custom_call_target="tpu_custom_call", output_to_operand_aliasing={{0}: (9, {}), {1}: (10, {})} | custom-call | flops 402653184 | bytes 2097152 | tf_op jit(solution)/shard_map/ladder_0/pallas_call | solution.py:252
  21.9 3.4 %collective-permute-done.1.refs_0_ = bf16[8,64,384]{2,1,0:T(8,128)(2,1)S(1)} collective-permute-done((bf16[8,64,384]{2,1,0:T(8,128)(2,1)S(1)}, bf16[8,64,384]{2,1,0:T(8,128)(2,1)S(1)}, u32[]{:S(2)}, u32[]{:S(2)}) %collective-permute-start.1) | collective-permute-done | bytes 393248 | tf_op jit(solution)/shard_map/ppermute | solution.py:314
  25.2 0.5 collective-permute-start.5
  25.8 0.0 collective-permute-start.6
  25.8 1.6 %collective-permute-start.10 = (bf16[8,64,384]{2,1,0:T(8,128)(2,1)S(1)}, bf16[8,64,384]{2,1,0:T(8,128)(2,1)S(1)}, u32[]{:S(2)}, u32[]{:S(2)}) collective-permute-start(bf16[8,64,384]{2,1,0:T(8,128)(2,1)S(1)} %collective-permute-done.1.refs_0_), channel_id=1, source_target_pairs={{0,2},{1,3},{2,0},{3,1},{4,6},{5,7},{6,4},{7,5},{8,10},{9,11},{10,... | collective-permute-start | bytes 1179656 | tf_op jit(solution)/shard_map/ppermute | solution.py:317
  27.4 0.2 collective-permute-start.12
  27.6 0.0 collective-permute-done.8.refs_3_
  27.6 4.1 %ladder_1.1 = (bf16[32,64,2048]{2,1,0:T(8,128)(2,1)S(1)}, bf16[132,64,384]{2,1,0:T(8,128)(2,1)S(1)}, f32[2,8,128]{2,1,0:T(8,128)S(1)}) custom-call(s32[1]{0:T(128)} %bitcast.me_ref, s32[8]{0:T(128)S(1)} %copy-done.4, s32[32]{0:T(128)S(1)} %get-tuple-element.51.order_ref, ...), custom_call_target="tpu_custom_call", output_to_operand_aliasing={{0}: (9, {}), {1}: (10, {})} | custom-call | flops 402653184 | bytes 2097152 | tf_op jit(solution)/shard_map/ladder_1/pallas_call | solution.py:252
  31.7 3.8 %collective-permute-done.5.refs_0_ = bf16[8,64,384]{2,1,0:T(8,128)(2,1)S(1)} collective-permute-done((bf16[8,64,384]{2,1,0:T(8,128)(2,1)S(1)}, bf16[8,64,384]{2,1,0:T(8,128)(2,1)S(1)}, u32[]{:S(2)}, u32[]{:S(2)}) %collective-permute-start.5) | collective-permute-done | bytes 393248 | tf_op jit(solution)/shard_map/ppermute | solution.py:314
  35.6 1.0 %collective-permute-start.11 = (bf16[4,64,384]{2,1,0:T(8,128)(2,1)S(1)}, bf16[4,64,384]{2,1,0:T(8,128)(2,1)S(1)}, u32[]{:S(2)}, u32[]{:S(2)}) collective-permute-start(bf16[4,64,384]{2,1,0:T(8,128)(2,1)S(1)} %slice.13), channel_id=1, source_target_pairs={{0,2},{1,3},{2,0},{3,1},{4,6},{5,7},{6,4},{7,5},{8,10},{9,11},{10,... | collective-permute-start | bytes 589832 | tf_op jit(solution)/shard_map/ppermute | solution.py:317
  36.6 1.5 %collective-permute-start.9 = (bf16[4,64,384]{2,1,0:T(8,128)(2,1)S(1)}, bf16[4,64,384]{2,1,0:T(8,128)(2,1)S(1)}, u32[]{:S(2)}, u32[]{:S(2)}) collective-permute-start(bf16[4,64,384]{2,1,0:T(8,128)(2,1)S(1)} %slice.16), channel_id=1, source_target_pairs={{0,8},{1,9},{2,10},{3,11},{4,0},{5,1},{6,2},{7,3},{8,12},{9,13},{1... | collective-permute-start | bytes 589832 | tf_op jit(solution)/shard_map/ppermute | solution.py:314
  38.1 0.0 collective-permute-done.13.refs_4_
  38.1 4.8 %ladder_2.1 = (bf16[32,64,2048]{2,1,0:T(8,128)(2,1)S(1)}, bf16[132,64,384]{2,1,0:T(8,128)(2,1)S(1)}, f32[2,8,128]{2,1,0:T(8,128)S(1)}) custom-call(s32[1]{0:T(128)} %bitcast.me_ref, s32[8]{0:T(128)S(1)} %copy-done.4, s32[32]{0:T(128)S(1)} %get-tuple-element.51.order_ref, ...), custom_call_target="tpu_custom_call", output_to_operand_aliasing={{0}: (9, {}), {1}: (10, {})} | custom-call | flops 503316480 | bytes 2621440 | tf_op jit(solution)/shard_map/ladder_2/pallas_call | solution.py:252
  43.0 0.1 collective-permute-start.14
  43.1 0.5 collective-permute-start.15
  43.6 0.0 collective-permute-done.9.refs_2_
  43.6 0.1 collective-permute-start.17
  43.7 0.4 collective-permute-start.16
  44.1 0.4 collective-permute-done.14.refs_0_
  44.5 0.3 collective-permute-done.15.refs_1_
  44.8 2.8 %ladder_3.1 = (bf16[32,64,2048]{2,1,0:T(8,128)(2,1)S(1)}, bf16[132,64,384]{2,1,0:T(8,128)(2,1)S(1)}, f32[2,8,128]{2,1,0:T(8,128)S(1)}) custom-call(s32[1]{0:T(128)} %bitcast.me_ref, s32[8]{0:T(128)S(1)} %copy-done.4, s32[32]{0:T(128)S(1)} %get-tuple-element.51.order_ref, ...), custom_call_target="tpu_custom_call", output_to_operand_aliasing={{0}: (9, {}), {1}: (10, {})} | custom-call | flops 201326592 | bytes 1048576 | tf_op jit(solution)/shard_map/ladder_3/pallas_call | solution.py:252
  47.7 0.0 collective-permute-done.16.refs_0_
  47.7 2.3 %ladder_4.1 = (bf16[32,64,2048]{2,1,0:T(8,128)(2,1)S(1)}, bf16[132,64,384]{2,1,0:T(8,128)(2,1)S(1)}, f32[2,8,128]{2,1,0:T(8,128)S(1)}) custom-call(s32[1]{0:T(128)} %bitcast.me_ref, s32[8]{0:T(128)S(1)} %copy-done.4, s32[32]{0:T(128)S(1)} %get-tuple-element.51.order_ref, ...), custom_call_target="tpu_custom_call", output_to_operand_aliasing={{0}: (9, {}), {1}: (10, {})} | custom-call | flops 100663296 | bytes 524288 | tf_op jit(solution)/shard_map/ladder_4/pallas_call | solution.py:252
  50.0 3.6 %collective-permute-start.18 = (f32[2,8,128]{2,1,0:T(8,128)S(1)}, f32[2,8,128]{2,1,0:T(8,128)S(1)}, u32[]{:S(2)}, u32[]{:S(2)}) collective-permute-start(f32[2,8,128]{2,1,0:T(8,128)S(1)} %get-tuple-element.95), channel_id=1, source_target_pairs={{0,12},{1,13},{2,14},{3,15},{4,8},{5,9},{6,10},{7,11},{8,4},{9,5},... | collective-permute-start | bytes 24584 | tf_op jit(solution)/shard_map/ppermute | solution.py:317
  53.5 1.0 %collective-permute-start.19 = (f32[2,8,128]{2,1,0:T(8,128)S(1)}, f32[2,8,128]{2,1,0:T(8,128)S(1)}, u32[]{:S(2)}, u32[]{:S(2)}) collective-permute-start(f32[2,8,128]{2,1,0:T(8,128)S(1)} %get-tuple-element.95), channel_id=1, source_target_pairs={{0,8},{1,9},{2,10},{3,11},{4,12},{5,13},{6,14},{7,15},{8,0},{9,1},... | collective-permute-start | bytes 24584 | tf_op jit(solution)/shard_map/ppermute | solution.py:317
  54.6 2.0 %deliver_0.1.refs_0_ = bf16[32,64,2048]{2,1,0:T(8,128)(2,1)} custom-call(bf16[32,64,2048]{2,1,0:T(8,128)(2,1)S(1)} %get-tuple-element.97.held_ref), custom_call_target="tpu_custom_call" | custom-call | tf_op jit(solution)/shard_map/deliver_0/pallas_call | solution.py:290
  56.6 1.5 %collective-permute-done.19 = f32[2,8,128]{2,1,0:T(8,128)S(1)} collective-permute-done((f32[2,8,128]{2,1,0:T(8,128)S(1)}, f32[2,8,128]{2,1,0:T(8,128)S(1)}, u32[]{:S(2)}, u32[]{:S(2)}) %collective-permute-start.19) | collective-permute-done | bytes 8224 | tf_op jit(solution)/shard_map/ppermute | solution.py:317
  58.1 0.1 collective-permute-done.20
  58.2 1.1 %collective-permute-start.22 = (f32[2,8,128]{2,1,0:T(8,128)S(1)}, f32[2,8,128]{2,1,0:T(8,128)S(1)}, u32[]{:S(2)}, u32[]{:S(2)}) collective-permute-start(f32[2,8,128]{2,1,0:T(8,128)S(1)} %add_add_fusion), channel_id=1, source_target_pairs={{0,2},{1,3},{2,0},{3,1},{4,6},{5,7},{6,4},{7,5},{8,10},{9,11},{10,... | collective-permute-start | bytes 24584 | tf_op jit(solution)/shard_map/ppermute | solution.py:317
  59.3 0.8 %collective-permute-start.23 = (f32[2,8,128]{2,1,0:T(8,128)S(1)}, f32[2,8,128]{2,1,0:T(8,128)S(1)}, u32[]{:S(2)}, u32[]{:S(2)}) collective-permute-start(f32[2,8,128]{2,1,0:T(8,128)S(1)} %add_add_fusion), channel_id=1, source_target_pairs={{0,1},{1,0},{2,3},{3,2},{4,5},{5,4},{6,7},{7,6},{8,9},{9,8},{10,11... | collective-permute-start | bytes 24584 | tf_op jit(solution)/shard_map/ppermute | solution.py:317
  60.1 2.0 %deliver_1.1 = bf16[32,64,2048]{2,1,0:T(8,128)(2,1)} custom-call(bf16[32,64,2048]{2,1,0:T(8,128)(2,1)S(1)} %get-tuple-element.97.held_ref, bf16[32,64,2048]{2,1,0:T(8,128)(2,1)} %deliver_0.1.refs_0_), custom_call_target="tpu_custom_call", output_to_operand_aliasing={{}: (1, {})} | custom-call | tf_op jit(solution)/shard_map/deliver_1/pallas_call | solution.py:290
  62.1 0.1 add_reduce_fusion
  62.2 0.5 add_sqrt_fusion
  (26 shorter events, 0.1 us)
Async XLA Ops:
  0.6 13.4 %collective-permute-start = (bf16[8,64,384]{2,1,0:T(8,128)(2,1)}, bf16[8,64,384]{2,1,0:T(8,128)(2,1)S(1)}, u32[]{:S(2)}, u32[]{:S(2)}) collective-permute-start(bf16[8,64,384]{2,1,0:T(8,128)(2,1)} %refs_3_.1), channel_id=1, source_target_pairs={{0,4},{1,5},{2,6},{3,7},{4,12},{5,13},{6,14},{7,15},{8,0},{9,1},{1... | collective-permute-start | bytes 1179656 | tf_op jit(solution)/shard_map/ppermute | solution.py:314
  3.7 12.8 %collective-permute-start.3 = (bf16[8,64,384]{2,1,0:T(8,128)(2,1)}, bf16[8,64,384]{2,1,0:T(8,128)(2,1)S(1)}, u32[]{:S(2)}, u32[]{:S(2)}) collective-permute-start(bf16[8,64,384]{2,1,0:T(8,128)(2,1)} %refs_3_.1), channel_id=1, source_target_pairs={{0,2},{1,3},{2,0},{3,1},{4,6},{5,7},{6,4},{7,5},{8,10},{9,11},{10,... | collective-permute-start | bytes 1179656 | tf_op jit(solution)/shard_map/ppermute | solution.py:317
  5.2 11.5 %collective-permute-start.4 = (bf16[8,64,384]{2,1,0:T(8,128)(2,1)}, bf16[8,64,384]{2,1,0:T(8,128)(2,1)S(1)}, u32[]{:S(2)}, u32[]{:S(2)}) collective-permute-start(bf16[8,64,384]{2,1,0:T(8,128)(2,1)} %refs_3_.1), channel_id=1, source_target_pairs={{0,1},{1,0},{2,3},{3,2},{4,5},{5,4},{6,7},{7,6},{8,9},{9,8},{10,11... | collective-permute-start | bytes 1179656 | tf_op jit(solution)/shard_map/ppermute | solution.py:317
  5.2 0.7 %copy-start.3 = (s32[8]{0:T(128)S(1)}, s32[8]{0:T(128)}, u32[]{:S(2)}) copy-start(s32[8]{0:T(128)} %counts_ref.11) | copy-start | bytes 100
  5.9 0.7 %copy-start.5 = (s32[32]{0:T(128)S(1)}, s32[32]{0:T(128)}, u32[]{:S(2)}) copy-start(s32[32]{0:T(128)} %irrep_ref.1) | copy-start | bytes 388
  14.0 11.2 %collective-permute-start.1 = (bf16[8,64,384]{2,1,0:T(8,128)(2,1)S(1)}, bf16[8,64,384]{2,1,0:T(8,128)(2,1)S(1)}, u32[]{:S(2)}, u32[]{:S(2)}) collective-permute-start(bf16[8,64,384]{2,1,0:T(8,128)(2,1)S(1)} %collective-permute-done.refs_0_), channel_id=1, source_target_pairs={{0,4},{1,5},{2,6},{3,7},{4,12},{5,13},{6,14},{7,15},{8,0},{9,1},{1... | collective-permute-start | bytes 1179656 | tf_op jit(solution)/shard_map/ppermute | solution.py:314
  15.0 10.3 %collective-permute-start.2 = (bf16[8,64,384]{2,1,0:T(8,128)(2,1)S(1)}, bf16[8,64,384]{2,1,0:T(8,128)(2,1)S(1)}, u32[]{:S(2)}, u32[]{:S(2)}) collective-permute-start(bf16[8,64,384]{2,1,0:T(8,128)(2,1)S(1)} %collective-permute-done.refs_0_), channel_id=1, source_target_pairs={{0,1},{1,0},{2,3},{3,2},{4,5},{5,4},{6,7},{7,6},{8,9},{9,8},{10,11... | collective-permute-start | bytes 1179656 | tf_op jit(solution)/shard_map/ppermute | solution.py:317
  15.0 12.4 %collective-permute-start.7 = (bf16[8,64,384]{2,1,0:T(8,128)(2,1)S(1)}, bf16[8,64,384]{2,1,0:T(8,128)(2,1)S(1)}, u32[]{:S(2)}, u32[]{:S(2)}) collective-permute-start(bf16[8,64,384]{2,1,0:T(8,128)(2,1)S(1)} %collective-permute-done.refs_0_), channel_id=1, source_target_pairs={{0,2},{1,3},{2,0},{3,1},{4,6},{5,7},{6,4},{7,5},{8,10},{9,11},{10,... | collective-permute-start | bytes 1179656 | tf_op jit(solution)/shard_map/ppermute | solution.py:317
  16.5 11.1 %collective-permute-start.8 = (bf16[8,64,384]{2,1,0:T(8,128)(2,1)S(1)}, bf16[8,64,384]{2,1,0:T(8,128)(2,1)S(1)}, u32[]{:S(2)}, u32[]{:S(2)}) collective-permute-start(bf16[8,64,384]{2,1,0:T(8,128)(2,1)S(1)} %collective-permute-done.3.refs_1_), channel_id=1, source_target_pairs={{0,1},{1,0},{2,3},{3,2},{4,5},{5,4},{6,7},{7,6},{8,9},{9,8},{10,11... | collective-permute-start | bytes 1179656 | tf_op jit(solution)/shard_map/ppermute | solution.py:317
  16.7 1.4 %copy-start = (bf16[32,64,384]{2,1,0:T(8,128)(2,1)S(1)}, bf16[32,64,384]{2,1,0:T(8,128)(2,1)}, u32[]{:S(2)}) copy-start(bf16[32,64,384]{2,1,0:T(8,128)(2,1)} %v_ref.9) | copy-start | bytes 4718596
  18.2 1.0 %copy-start.2 = (bf16[8,64,384]{2,1,0:T(8,128)(2,1)S(1)}, bf16[8,64,384]{2,1,0:T(8,128)(2,1)}, u32[]{:S(2)}) copy-start(bf16[8,64,384]{2,1,0:T(8,128)(2,1)} %refs_3_.1) | copy-start | bytes 1179652
  19.1 0.7 %copy-start.4 = (s32[8]{0:T(128)S(1)}, s32[8]{0:T(128)}, u32[]{:S(2)}) copy-start(s32[8]{0:T(128)} %counts_ref.11) | copy-start | bytes 100
  19.8 7.8 %copy-start.1 = (bf16[32,64,384]{2,1,0:T(8,128)(2,1)S(1)}, bf16[32,64,384]{2,1,0:T(8,128)(2,1)}, u32[]{:S(2)}) copy-start(bf16[32,64,384]{2,1,0:T(8,128)(2,1)} %v_ref.9) | copy-start | bytes 4718596
  25.2 10.3 %collective-permute-start.5 = (bf16[8,64,384]{2,1,0:T(8,128)(2,1)S(1)}, bf16[8,64,384]{2,1,0:T(8,128)(2,1)S(1)}, u32[]{:S(2)}, u32[]{:S(2)}) collective-permute-start(bf16[8,64,384]{2,1,0:T(8,128)(2,1)S(1)} %collective-permute-done.1.refs_0_), channel_id=1, source_target_pairs={{0,4},{1,5},{2,6},{3,7},{4,12},{5,13},{6,14},{7,15},{8,0},{9,1},{1... | collective-permute-start | bytes 1179656 | tf_op jit(solution)/shard_map/ppermute | solution.py:314
  25.8 9.8 %collective-permute-start.6 = (bf16[8,64,384]{2,1,0:T(8,128)(2,1)S(1)}, bf16[8,64,384]{2,1,0:T(8,128)(2,1)S(1)}, u32[]{:S(2)}, u32[]{:S(2)}) collective-permute-start(bf16[8,64,384]{2,1,0:T(8,128)(2,1)S(1)} %collective-permute-done.1.refs_0_), channel_id=1, source_target_pairs={{0,1},{1,0},{2,3},{3,2},{4,5},{5,4},{6,7},{7,6},{8,9},{9,8},{10,11... | collective-permute-start | bytes 1179656 | tf_op jit(solution)/shard_map/ppermute | solution.py:317
  25.8 12.3 %collective-permute-start.10 = (bf16[8,64,384]{2,1,0:T(8,128)(2,1)S(1)}, bf16[8,64,384]{2,1,0:T(8,128)(2,1)S(1)}, u32[]{:S(2)}, u32[]{:S(2)}) collective-permute-start(bf16[8,64,384]{2,1,0:T(8,128)(2,1)S(1)} %collective-permute-done.1.refs_0_), channel_id=1, source_target_pairs={{0,2},{1,3},{2,0},{3,1},{4,6},{5,7},{6,4},{7,5},{8,10},{9,11},{10,... | collective-permute-start | bytes 1179656 | tf_op jit(solution)/shard_map/ppermute | solution.py:317
  27.4 10.7 %collective-permute-start.12 = (bf16[8,64,384]{2,1,0:T(8,128)(2,1)S(1)}, bf16[8,64,384]{2,1,0:T(8,128)(2,1)S(1)}, u32[]{:S(2)}, u32[]{:S(2)}) collective-permute-start(bf16[8,64,384]{2,1,0:T(8,128)(2,1)S(1)} %collective-permute-done.7.refs_1_), channel_id=1, source_target_pairs={{0,1},{1,0},{2,3},{3,2},{4,5},{5,4},{6,7},{7,6},{8,9},{9,8},{10,11... | collective-permute-start | bytes 1179656 | tf_op jit(solution)/shard_map/ppermute | solution.py:317
  35.5 2.6 %collective-permute-start.13 = (bf16[8,64,384]{2,1,0:T(8,128)(2,1)S(1)}, bf16[8,64,384]{2,1,0:T(8,128)(2,1)S(1)}, u32[]{:S(2)}, u32[]{:S(2)}) collective-permute-start(bf16[8,64,384]{2,1,0:T(8,128)(2,1)S(1)} %collective-permute-done.5.refs_0_), channel_id=1, source_target_pairs={{0,1},{1,0},{2,3},{3,2},{4,5},{5,4},{6,7},{7,6},{8,9},{9,8},{10,11... | collective-permute-start | bytes 1179656 | tf_op jit(solution)/shard_map/ppermute | solution.py:317
  35.6 7.4 %collective-permute-start.11 = (bf16[4,64,384]{2,1,0:T(8,128)(2,1)S(1)}, bf16[4,64,384]{2,1,0:T(8,128)(2,1)S(1)}, u32[]{:S(2)}, u32[]{:S(2)}) collective-permute-start(bf16[4,64,384]{2,1,0:T(8,128)(2,1)S(1)} %slice.13), channel_id=1, source_target_pairs={{0,2},{1,3},{2,0},{3,1},{4,6},{5,7},{6,4},{7,5},{8,10},{9,11},{10,... | collective-permute-start | bytes 589832 | tf_op jit(solution)/shard_map/ppermute | solution.py:317
  36.6 7.0 %collective-permute-start.9 = (bf16[4,64,384]{2,1,0:T(8,128)(2,1)S(1)}, bf16[4,64,384]{2,1,0:T(8,128)(2,1)S(1)}, u32[]{:S(2)}, u32[]{:S(2)}) collective-permute-start(bf16[4,64,384]{2,1,0:T(8,128)(2,1)S(1)} %slice.16), channel_id=1, source_target_pairs={{0,8},{1,9},{2,10},{3,11},{4,0},{5,1},{6,2},{7,3},{8,12},{9,13},{1... | collective-permute-start | bytes 589832 | tf_op jit(solution)/shard_map/ppermute | solution.py:314
  43.0 1.5 %collective-permute-start.14 = (bf16[4,64,384]{2,1,0:T(8,128)(2,1)S(1)}, bf16[4,64,384]{2,1,0:T(8,128)(2,1)S(1)}, u32[]{:S(2)}, u32[]{:S(2)}) collective-permute-start(bf16[4,64,384]{2,1,0:T(8,128)(2,1)S(1)} %get-tuple-element.101), channel_id=1, source_target_pairs={{0,1},{1,0},{2,3},{3,2},{4,5},{5,4},{6,7},{7,6},{8,9},{9,8},{10,11... | collective-permute-start | bytes 589832 | tf_op jit(solution)/shard_map/ppermute | solution.py:317
  43.1 1.7 %collective-permute-start.15 = (bf16[4,64,384]{2,1,0:T(8,128)(2,1)S(1)}, bf16[4,64,384]{2,1,0:T(8,128)(2,1)S(1)}, u32[]{:S(2)}, u32[]{:S(2)}) collective-permute-start(bf16[4,64,384]{2,1,0:T(8,128)(2,1)S(1)} %get-tuple-element.100), channel_id=1, source_target_pairs={{0,1},{1,0},{2,3},{3,2},{4,5},{5,4},{6,7},{7,6},{8,9},{9,8},{10,11... | collective-permute-start | bytes 589832 | tf_op jit(solution)/shard_map/ppermute | solution.py:317
  43.6 4.0 %collective-permute-start.17 = (bf16[4,64,384]{2,1,0:T(8,128)(2,1)S(1)}, bf16[4,64,384]{2,1,0:T(8,128)(2,1)S(1)}, u32[]{:S(2)}, u32[]{:S(2)}) collective-permute-start(bf16[4,64,384]{2,1,0:T(8,128)(2,1)S(1)} %collective-permute-done.9.refs_2_), channel_id=1, source_target_pairs={{0,1},{1,0},{2,3},{3,2},{4,5},{5,4},{6,7},{7,6},{8,9},{9,8},{10,11... | collective-permute-start | bytes 589832 | tf_op jit(solution)/shard_map/ppermute | solution.py:317
  43.7 4.0 %collective-permute-start.16 = (bf16[4,64,384]{2,1,0:T(8,128)(2,1)S(1)}, bf16[4,64,384]{2,1,0:T(8,128)(2,1)S(1)}, u32[]{:S(2)}, u32[]{:S(2)}) collective-permute-start(bf16[4,64,384]{2,1,0:T(8,128)(2,1)S(1)} %collective-permute-done.11.refs_3_), channel_id=1, source_target_pairs={{0,1},{1,0},{2,3},{3,2},{4,5},{5,4},{6,7},{7,6},{8,9},{9,8},{10,11... | collective-permute-start | bytes 589832 | tf_op jit(solution)/shard_map/ppermute | solution.py:317
  50.0 6.6 %collective-permute-start.18 = (f32[2,8,128]{2,1,0:T(8,128)S(1)}, f32[2,8,128]{2,1,0:T(8,128)S(1)}, u32[]{:S(2)}, u32[]{:S(2)}) collective-permute-start(f32[2,8,128]{2,1,0:T(8,128)S(1)} %get-tuple-element.95), channel_id=1, source_target_pairs={{0,12},{1,13},{2,14},{3,15},{4,8},{5,9},{6,10},{7,11},{8,4},{9,5},... | collective-permute-start | bytes 24584 | tf_op jit(solution)/shard_map/ppermute | solution.py:317
  53.5 4.5 %collective-permute-start.19 = (f32[2,8,128]{2,1,0:T(8,128)S(1)}, f32[2,8,128]{2,1,0:T(8,128)S(1)}, u32[]{:S(2)}, u32[]{:S(2)}) collective-permute-start(f32[2,8,128]{2,1,0:T(8,128)S(1)} %get-tuple-element.95), channel_id=1, source_target_pairs={{0,8},{1,9},{2,10},{3,11},{4,12},{5,13},{6,14},{7,15},{8,0},{9,1},... | collective-permute-start | bytes 24584 | tf_op jit(solution)/shard_map/ppermute | solution.py:317
  54.6 3.7 %collective-permute-start.20 = (f32[2,8,128]{2,1,0:T(8,128)S(1)}, f32[2,8,128]{2,1,0:T(8,128)S(1)}, u32[]{:S(2)}, u32[]{:S(2)}) collective-permute-start(f32[2,8,128]{2,1,0:T(8,128)S(1)} %get-tuple-element.95), channel_id=1, source_target_pairs={{0,4},{1,5},{2,6},{3,7},{4,0},{5,1},{6,2},{7,3},{8,12},{9,13},{10,... | collective-permute-start | bytes 24584 | tf_op jit(solution)/shard_map/ppermute | solution.py:317
  58.2 3.9 %collective-permute-start.21 = (f32[2,8,128]{2,1,0:T(8,128)S(1)}, f32[2,8,128]{2,1,0:T(8,128)S(1)}, u32[]{:S(2)}, u32[]{:S(2)}) collective-permute-start(f32[2,8,128]{2,1,0:T(8,128)S(1)} %add_add_fusion), channel_id=1, source_target_pairs={{0,3},{1,2},{2,1},{3,0},{4,7},{5,6},{6,5},{7,4},{8,11},{9,10},{10,... | collective-permute-start | bytes 24584 | tf_op jit(solution)/shard_map/ppermute | solution.py:317
  58.2 3.9 %collective-permute-start.22 = (f32[2,8,128]{2,1,0:T(8,128)S(1)}, f32[2,8,128]{2,1,0:T(8,128)S(1)}, u32[]{:S(2)}, u32[]{:S(2)}) collective-permute-start(f32[2,8,128]{2,1,0:T(8,128)S(1)} %add_add_fusion), channel_id=1, source_target_pairs={{0,2},{1,3},{2,0},{3,1},{4,6},{5,7},{6,4},{7,5},{8,10},{9,11},{10,... | collective-permute-start | bytes 24584 | tf_op jit(solution)/shard_map/ppermute | solution.py:317
  59.3 2.8 %collective-permute-start.23 = (f32[2,8,128]{2,1,0:T(8,128)S(1)}, f32[2,8,128]{2,1,0:T(8,128)S(1)}, u32[]{:S(2)}, u32[]{:S(2)}) collective-permute-start(f32[2,8,128]{2,1,0:T(8,128)S(1)} %add_add_fusion), channel_id=1, source_target_pairs={{0,1},{1,0},{2,3},{3,2},{4,5},{5,4},{6,7},{7,6},{8,9},{9,8},{10,11... | collective-permute-start | bytes 24584 | tf_op jit(solution)/shard_map/ppermute | solution.py:317
